TPU v7x, 32 devices: a whole 2x2x4 slice. The times are simulated.
32 devices in a mesh: ctx: 4 (over y, x), exp: 8 (over z, core).
Axes of the slice: x: 2, y: 2, z: 4, core: 2. Of those that a mesh axis runs over, the one named last changes fastest.
Arguments:
- out_grad: bfloat16 [8192, 4096], P(('ctx', 'exp')), may hold values from -6 to 6
- gate_in: bfloat16 [8192, 4096], P(('ctx', 'exp')), may hold values from -6 to 6
- conv_in: bfloat16 [8192, 4096], P(('ctx', 'exp')), may hold values from -6 to 6
- scan_grad: bfloat16 [8192, 4096], P(('ctx', 'exp')), may hold values from -6 to 6
- conv_weight: float32 [4, 8192], P(None, ('ctx', 'exp')), may hold values from -3 to 3
- conv_bias: float32 [8192], P(('ctx', 'exp')), may hold values from -3 to 3
- skip_scale: float32 [8192], P(('ctx', 'exp')), may hold values from 0.5 to 1.5
- projection: bfloat16 [8192, 4096], P(('ctx', 'exp')), may hold values from -0.09375 to 0.09375
- resid_grad: bfloat16 [4096, 4096], P(('ctx', 'exp')), may hold values from -6 to 6
- routes: int32 [4096, 2], P(('ctx', 'exp')), may hold values from 0 to 7, as said below
- gate_probs: float32 [4096, 2], P(('ctx', 'exp')), may hold values from 0.05 to 0.95
Outputs:
- expert_rows: bfloat16 [8, 1792, 4096], P('exp', 'ctx')
Inputs may be any that keep to these rules, and one draw needn't show every extreme that they name: `routes`: each row names 2 different experts. In every aligned block of 128 rows (the rows of one device) no expert is named by more than 56 rows, and in each run of 8 consecutive blocks one expert is named by exactly 56 rows of every block.
All inputs are finite; a program needn't handle non-finite values.
Results may differ from a plain program's by a relative error of at most 0.012.
Values may be sent and summed in bfloat16 or wider, within the bound.
No kernel may reach another device: no remote copies, remote signals or barrier semaphores. Data moves between devices by JAX's collectives and lax.ppermute only.
A program may use at most 128 MiB of HBM per device.

v0:
```python
import jax
import jax.numpy as jnp
from jax import lax
from jax.sharding import PartitionSpec as P

EXP_DEV = 1


def conv_grad(out_grad, gate_in, conv_in, scan_grad, conv_weight, conv_bias, skip_scale):
    kernel_taps = conv_weight.shape[0]
    length = conv_in.shape[1]
    gate_value = gate_in.astype(jnp.float32)
    gated = out_grad.astype(jnp.float32) * gate_value * jax.nn.sigmoid(gate_value)
    padded = jnp.pad(conv_in.astype(jnp.float32), ((0, 0), (kernel_taps - 1, 0)))
    pre_act = conv_bias[:, None] + conv_weight[0][:, None] * padded[:, 0:length]
    for tap in range(1, kernel_taps):
        pre_act = pre_act + conv_weight[tap][:, None] * padded[:, tap : tap + length]
    sig_value = jax.nn.sigmoid(pre_act)
    pre_grad = (
        (scan_grad.astype(jnp.float32) + skip_scale[:, None] * gated)
        * sig_value
        * (1.0 + pre_act * (1.0 - sig_value))
    )
    back_pad = jnp.pad(pre_grad, ((0, 0), (0, kernel_taps - 1)))
    input_grad = conv_weight[0][:, None] * back_pad[:, kernel_taps - 1 : kernel_taps - 1 + length]
    for tap in range(1, kernel_taps):
        start_at = kernel_taps - 1 - tap
        input_grad = (
            input_grad + conv_weight[tap][:, None] * back_pad[:, start_at : start_at + length]
        )
    return input_grad.astype(jnp.bfloat16)


def on_device(
    out_grad,
    gate_in,
    conv_in,
    scan_grad,
    conv_weight,
    conv_bias,
    skip_scale,
    projection,
    resid_grad,
    routes,
    gate_probs,
):
    input_grad = conv_grad(
        out_grad, gate_in, conv_in, scan_grad, conv_weight, conv_bias, skip_scale
    )
    ctx_count = lax.axis_size("ctx")
    exp_count = lax.axis_size("exp")
    channels = input_grad.shape[0]
    tok_rows = resid_grad.shape[0]
    features = projection.shape[1]
    blocked = input_grad.reshape(channels, ctx_count, exp_count, tok_rows)
    local_grad = lax.all_to_all(blocked, "exp", split_axis=2, concat_axis=0, tiled=True)
    local_grad = local_grad.reshape(channels * exp_count, ctx_count * tok_rows)
    block_weights = lax.all_gather(projection, "exp", axis=0, tiled=True)
    summed = lax.psum_scatter(
        lax.dot_general(
            local_grad, block_weights, (((0,), (0,)), ((), ())), preferred_element_type=jnp.float32
        ).astype(jnp.bfloat16),
        "ctx",
        scatter_dimension=0,
        tiled=True,
    ).astype(jnp.float32)
    moe_grad = (resid_grad.astype(jnp.float32) + summed).astype(jnp.bfloat16)
    experts = EXP_DEV * exp_count
    route_width = routes.shape[1]
    capacity = max(2, 14 * tok_rows // (4 * experts))
    flat_routes = routes.reshape(-1)
    onehot = (flat_routes[:, None] == jnp.arange(experts, dtype=jnp.int32)[None, :]).astype(
        jnp.int32
    )
    before = jnp.cumsum(onehot, axis=0) - onehot
    rank_in = jnp.sum(before * onehot, axis=1)
    slot_id = (flat_routes * capacity + rank_in).reshape(tok_rows, route_width)
    targets = jnp.arange(experts * capacity, dtype=jnp.int32)
    matches = slot_id[None, :, :] == targets[:, None, None]
    picked = jnp.any(matches, axis=2).astype(jnp.bfloat16)
    slot_scale = jnp.sum(jnp.where(matches, gate_probs[None, :, :], 0.0), axis=(1, 2))
    gathered = jnp.dot(picked, moe_grad, preferred_element_type=jnp.float32)
    outgoing = (
        (slot_scale[:, None] * gathered).astype(jnp.bfloat16).reshape(experts, capacity, features)
    )
    return lax.all_to_all(outgoing, "exp", split_axis=0, concat_axis=1, tiled=True)


def solution(mesh):
    placed = (
        P(("ctx", "exp"), None),
        P(("ctx", "exp"), None),
        P(("ctx", "exp"), None),
        P(("ctx", "exp"), None),
        P(None, ("ctx", "exp")),
        P(("ctx", "exp")),
        P(("ctx", "exp")),
        P(("ctx", "exp"), None),
        P(("ctx", "exp"), None),
        P(("ctx", "exp"), None),
        P(("ctx", "exp"), None),
    )
    return jax.shard_map(
        on_device, mesh=mesh, in_specs=placed, out_specs=P("exp", "ctx", None), check_vma=False
    )
```

profile of v0, /device:TPU:0, one launch (start us, length us, event | category | flops | bytes accessed | tf_op | source)
XLA Modules:
  0.0 370.4 jit_solution(10569236086791409471)
XLA Ops:
  6.5 0.0 all-gather.2.cloned.1.call-start
  6.5 0.7 all-gather.2.cloned.1.call-update
  7.3 0.0 reduce-scatter.2.cloned.1.call-start
  7.3 3.3 copy.54
  10.6 2.3 convert_element_type.48
  12.8 3.3 copy.51
  16.1 0.0 copy-start.2
  16.1 0.0 copy-start.3
  16.1 0.0 copy-start.4
  16.1 4.2 %copy.52 = bf16[256,4096]{0,1:T(8,128)(2,1)} copy(bf16[256,4096]{1,0:T(8,128)(2,1)} %param.11) | data formatting | bytes 4194304 | tf_op args[0]
  20.3 4.3 %copy.53 = bf16[256,4096]{0,1:T(8,128)(2,1)} copy(bf16[256,4096]{1,0:T(8,128)(2,1)} %param.12) | data formatting | bytes 4194304 | tf_op args[1]
  24.6 0.0 copy-done.2
  24.6 0.0 copy-done.3
  24.6 0.0 copy-done.4
  24.6 9.7 %fusion.4 = f32[256,4096]{0,1:T(8,128)S(1)} fusion(bf16[256,4096]{0,1:T(8,128)(2,1)} %copy.53, f32[256,4096]{0,1:T(8,128)} %convert_element_type.48, bf16[256,4096]{0,1:T(8,128)(2,1)} %copy.52, bf16[256,4096]{0,1:T(8,128)(2,1)S(1)} %copy.51, f32[256]{0:T(256)S(1)} %bitcast.36, f32[256]{0:T(256)S(1)} %bitcast.38, f32[256]{0:T(256)S(1)} %bitcast.34, ...), kind=kLoop, calls=%fused_computation.8 | loop fusion | flops 27262976 | bytes 14686208 | tf_op jit(solution)/shard_map/mul | solution.py:20
  34.3 1.9 add_convert_fusion
  36.3 0.1 copy.55
  36.4 111.8 %all_to_all.27 = bf16[256,4,8,128]{0,3,1,2:T(8,128)(2,1)S(1)} all-to-all(bf16[256,4,8,128]{0,3,1,2:T(8,128)(2,1)S(1)} %copy.55), channel_id=1, replica_groups=mesh['ctx'=4,'exp'=8] {'exp'}, dimensions={2} | all-to-all | bytes 4194304 | tf_op jit(solution)/shard_map/all_to_all | solution.py:56
  148.3 1.2 copy.56
  149.5 0.7 copy.57
  150.2 57.2 %all-gather.2.cloned.1.call-done = bf16[2048,4096]{1,0:T(8,128)(2,1)} async-done(((bf16[256,4096]{1,0:T(8,128)(2,1)}), bf16[2048,4096]{1,0:T(8,128)(2,1)}) %all-gather.2.cloned.1.call-update) | async-done | bytes 16777232 | tf_op jit(solution)/shard_map/all_gather | solution.py:58
  207.4 13.7 %convolution_convert_fusion = bf16[512,4096]{1,0:T(8,128)(2,1)} fusion(bf16[2048,512]{0,1:T(8,128)(2,1)S(1)} %bitcast.31, bf16[2048,4096]{1,0:T(8,128)(2,1)} %all-gather.2.cloned.1.call-done), kind=kOutput, calls=%fused_computation.1 | convolution fusion | flops 8592031744 | bytes 23068672 | tf_op jit(solution)/shard_map/dot_general | solution.py:60
  221.1 0.0 copy-start.1
  221.1 0.0 copy-start.5
  221.1 0.0 copy-start
  221.1 0.0 reduce-scatter.2.cloned.1.call-update
  221.2 0.6 copy-done.1
  221.8 0.1 copy.48
  221.9 0.1 eq.42
  222.1 0.1 eq.38
  222.2 0.6 reduce-window.6
  222.8 0.2 slice_reduce_fusion
  223.1 0.1 fusion.13
  223.1 0.1 reduce_sum.21
  223.3 0.1 copy.50
  223.4 0.1 fusion.11
  223.4 0.0 copy-done.5
  223.5 0.1 select_reduce_fusion
  223.6 48.5 %reduce-scatter.2.cloned.1.call-done = bf16[128,4096]{1,0:T(8,128)(2,1)} async-done(((bf16[512,4096]{1,0:T(8,128)(2,1)}), bf16[128,4096]{1,0:T(8,128)(2,1)}) %reduce-scatter.2.cloned.1.call-update) | async-done | bytes 1048592 | tf_op jit(solution)/shard_map/reduce_scatter | solution.py:59
  272.1 0.0 copy-done
  272.1 2.4 multiply_convert_fusion
  274.5 87.2 %all_to_all.28 = bf16[8,56,4096]{2,1,0:T(8,128)(2,1)S(1)} all-to-all(bf16[8,56,4096]{2,1,0:T(8,128)(2,1)S(1)} %bitcast.26), channel_id=1, replica_groups=mesh['ctx'=4,'exp'=8] {'exp'}, dimensions={0} | all-to-all | bytes 7340032 | tf_op jit(solution)/shard_map/all_to_all | solution.py:86
  361.7 1.8 copy.59
  (5 shorter events, 0.1 us)
Async XLA Ops:
  6.5 200.9 %all-gather.2.cloned.1.call-start = ((), (), s32[]{:S(2)}) async-start(), calls=%async_computation.3 | async-start | bytes 18874368 | tf_op jit(solution)/shard_map/all_gather | solution.py:58
  7.3 264.9 %reduce-scatter.2.cloned.1.call-start = ((), (), s32[]{:S(2)}) async-start(), calls=%async_computation.4 | async-start | bytes 5242880 | tf_op jit(solution)/shard_map/reduce_scatter | solution.py:59
  16.1 8.4 %copy-start.2 = (f32[4,256]{1,0:T(4,128)S(1)}, f32[4,256]{1,0:T(4,128)}, u32[]{:S(2)}) copy-start(f32[4,256]{1,0:T(4,128)} %param.15) | copy-start | bytes 12292
  16.1 8.4 %copy-start.3 = (f32[256]{0:T(256)S(1)}, f32[256]{0:T(256)}, u32[]{:S(2)}) copy-start(f32[256]{0:T(256)} %param.16) | copy-start | bytes 3076
  16.1 8.4 %copy-start.4 = (f32[256]{0:T(256)S(1)}, f32[256]{0:T(256)}, u32[]{:S(2)}) copy-start(f32[256]{0:T(256)} %param.17) | copy-start | bytes 3076
  221.1 0.7 copy-start.1
  221.1 2.3 copy-start.5
  221.1 51.0 %copy-start = (bf16[128,4096]{1,0:T(8,128)(2,1)S(1)}, bf16[128,4096]{1,0:T(8,128)(2,1)}, u32[]{:S(2)}) copy-start(bf16[128,4096]{1,0:T(8,128)(2,1)} %param.19) | copy-start | bytes 3145732
Sparse Core Ops, SparseCore 0:
  9.0 198.3 all-gather.1
  221.3 50.8 reduce-scatter.1
where the time goes:
time: 371 us; the launch traced here: 370 us
  blocking collectives  199 us (54%)
  waiting for transfers between devices  106 us (29%)
  local copies, waits for them, and re-layouts  20.3 us (5%)
  matrix products  16.1 us (4%)
  other arithmetic  14.9 us (4%)
  between operations  13.6 us (4%)
    all_to_all x1, blocking collectives, on_device(): lax.all_to_all(blocked, 'exp', split_axis=2, concat_axis=0, tiled=True)  112 us
    all_to_all x1, blocking collectives, on_device(): lax.all_to_all(outgoing, 'exp', split_axis=0, concat_axis=1, tiled=True)  87.2 us
    all_gather x1, waiting for transfers between devices, on_device(): block_weights = lax.all_gather(projection, 'exp', axis=0, tiled=True)  57.2 us
    reduce_scatter x1, waiting for transfers between devices, on_device(): lax.psum_scatter(lax.dot_general(local_grad, block_weights, (((0,), (0,))...  48.5 us
    unnamed x19, local copies, waits for them, and re-layouts  18.3 us
    dot_general x1, matrix products, on_device(): lax.dot_general(local_grad, block_weights, (((0,), (0,)), ((), ())), pref...  13.7 us
    mul x1, other arithmetic, conv_grad(): (scan_grad.astype(jnp.float32) + skip_scale[:, None] * gated) * sig_value  9.73 us
  transfers between devices with their start and end apart: 2, of which 2 were waited for; matrix products, arithmetic and copies ran while one was open for 9% of the time, Pallas kernels for 0%

commit v1 on v0

v1 whole, which is shorter than its diff:
```python
import functools

import jax
import jax.numpy as jnp
from jax import lax
from jax.experimental import pallas as pl
from jax.experimental.pallas import tpu as pltpu
from jax.sharding import PartitionSpec as P

EXP_DEV = 1
FEATURE_CHUNKS = 4
SKEW = 2
VMEM_BYTES = 48 * 1024 * 1024


def sigmoid(value):
    return 0.5 * jnp.tanh(0.5 * value) + 0.5


def conv_kernel(tile, out_grad, gate_in, conv_in, scan_grad, taps, bias, skip, turned, flat):
    channels, length = out_grad.shape
    kernel_taps = taps.shape[1]
    rows_at_once = 16

    def row_group(group, _):
        row_at = pl.multiple_of(group * rows_at_once, rows_at_once)
        rows = pl.ds(row_at, rows_at_once)
        weights = [taps[rows, tap : tap + 1] for tap in range(kernel_taps)]
        bias_value = bias[rows, :]
        skip_value = skip[rows, :]

        def token_tile(step, carry):
            at = pl.multiple_of((length // tile - 1 - step) * tile, tile)
            columns = pl.ds(at, tile)
            gate = gate_in[rows, columns].astype(jnp.float32)
            gated = out_grad[rows, columns].astype(jnp.float32) * gate * sigmoid(gate)
            here = conv_in[rows, columns].astype(jnp.float32)
            before = conv_in[rows, pl.ds(pl.multiple_of(jnp.maximum(at - 128, 0), 128), 128)].astype(jnp.float32)
            before = jnp.where(at > 0, before, 0.0)
            wide = jnp.concatenate([before, here], axis=1)
            pre = bias_value + weights[kernel_taps - 1] * here
            for tap in range(kernel_taps - 1):
                back = kernel_taps - 1 - tap
                pre = pre + weights[tap] * pltpu.roll(wide, back, 1)[:, 128:]
            sig = sigmoid(pre)
            scan = scan_grad[rows, columns].astype(jnp.float32)
            pre_grad = (scan + skip_value * gated) * sig * (1.0 + pre * (1.0 - sig))
            wide_grad = jnp.concatenate([pre_grad, carry], axis=1)
            total = weights[kernel_taps - 1] * pre_grad
            for tap in range(kernel_taps - 1):
                ahead = kernel_taps - 1 - tap
                total = total + weights[tap] * pltpu.roll(wide_grad, tile + 128 - ahead, 1)[:, :tile]
            flat[rows, columns] = total.astype(flat.dtype)
            return pre_grad[:, :128]

        lax.fori_loop(0, length // tile, token_tile, jnp.zeros((rows_at_once, 128), jnp.float32))
        return 0

    lax.fori_loop(0, channels // rows_at_once, row_group, 0)

    def turn(step, _):
        at = pl.multiple_of(step * tile, tile)
        turned[pl.ds(at, tile), :] = flat[:, pl.ds(at, tile)].T
        return 0

    lax.fori_loop(0, length // tile, turn, 0)


def conv_grad(out_grad, gate_in, conv_in, scan_grad, conv_weight, conv_bias, skip_scale):
    channels, length = out_grad.shape
    block = min(128, channels)
    tile = min(512, length)
    whole = pl.BlockSpec((block, length), lambda step: (step, 0))
    return pl.pallas_call(
        functools.partial(conv_kernel, tile),
        grid=(channels // block,),
        in_specs=[whole] * 4
        + [
            pl.BlockSpec((block, conv_weight.shape[0]), lambda step: (step, 0)),
            pl.BlockSpec((block, 1), lambda step: (step, 0)),
            pl.BlockSpec((block, 1), lambda step: (step, 0)),
        ],
        out_specs=pl.BlockSpec((length, block), lambda step: (0, step)),
        out_shape=jax.ShapeDtypeStruct((length, channels), jnp.bfloat16),
        scratch_shapes=[pltpu.VMEM((block, length), jnp.bfloat16)],
        compiler_params=pltpu.CompilerParams(vmem_limit_bytes=VMEM_BYTES),
        cost_estimate=pl.CostEstimate(
            flops=40 * channels * length, bytes_accessed=10 * channels * length, transcendentals=2 * channels * length
        ),
        name="conv_grad",
    )(out_grad, gate_in, conv_in, scan_grad, conv_weight.T, conv_bias[:, None], skip_scale[:, None])


def matmul_kernel(lefts, rights, place, *refs):
    left_refs = refs[:lefts]
    right_refs = refs[lefts : lefts + rights]
    resid = refs[lefts + rights]
    out = refs[lefts + rights + 1]
    per_right = lefts // rights
    depth = left_refs[0].shape[1]
    total = None
    for index, left in enumerate(left_refs):
        right = right_refs[index // per_right]
        part = jnp.dot(
            left[...], right[pl.ds((index % per_right) * depth, depth), :], preferred_element_type=jnp.float32
        )
        total = part if total is None else total + part
    mine = pl.program_id(0) == place[0]
    total = total + jnp.where(mine, resid[...].astype(jnp.float32), 0.0)
    out[...] = total.astype(out.dtype)


def matmul(lefts, rights, resid, place):
    tokens, depth = lefts[0].shape
    wide, width = rights[0].shape
    tile = resid.shape[0]
    flops = 2 * tokens * depth * len(lefts) * width
    moved = 2 * (tokens * depth * len(lefts) + wide * len(rights) * width + tokens * width)
    return pl.pallas_call(
        functools.partial(matmul_kernel, len(lefts), len(rights)),
        grid_spec=pltpu.PrefetchScalarGridSpec(
            num_scalar_prefetch=1,
            grid=(tokens // tile,),
            in_specs=[pl.BlockSpec((tile, depth), lambda step, place: (step, 0))] * len(lefts)
            + [pl.BlockSpec((wide, width), lambda step, place: (0, 0))] * len(rights)
            + [pl.BlockSpec(resid.shape, lambda step, place: (0, 0))],
            out_specs=pl.BlockSpec((tile, width), lambda step, place: (step, 0)),
        ),
        out_shape=jax.ShapeDtypeStruct((tokens, width), jnp.bfloat16),
        compiler_params=pltpu.CompilerParams(vmem_limit_bytes=VMEM_BYTES),
        cost_estimate=pl.CostEstimate(flops=flops, bytes_accessed=moved, transcendentals=0),
        name="partial_product",
    )(place, *lefts, *rights, resid)


def on_device(
    out_grad,
    gate_in,
    conv_in,
    scan_grad,
    conv_weight,
    conv_bias,
    skip_scale,
    projection,
    resid_grad,
    routes,
    gate_probs,
):
    ctx_count = lax.axis_size("ctx")
    exp_count = lax.axis_size("exp")
    chips = exp_count // 2
    ctx_at = lax.axis_index("ctx")
    exp_at = lax.axis_index("exp")
    chip_at = exp_at // 2
    core_at = exp_at % 2
    channels, length = out_grad.shape
    features = projection.shape[1]
    half = features // 2
    width = half // FEATURE_CHUNKS
    tok_rows = resid_grad.shape[0]
    window = tok_rows * exp_count
    tile = 2 * tok_rows

    def to_core(array):
        return lax.ppermute(array, "exp", [(place, place ^ 1) for place in range(exp_count)])

    def to_ctx(array, offset):
        return lax.ppermute(array, "ctx", [(place, place ^ offset) for place in range(ctx_count)])

    def up(array):
        return lax.ppermute(array, "exp", [(place, place + 2) for place in range(exp_count - 2)])

    def down(array):
        return lax.ppermute(array, "exp", [(place + 2, place) for place in range(exp_count - 2)])

    def columns_of(array, core):
        return lax.dynamic_slice_in_dim(array, core * half, half, 1)

    rows_here = columns_of(projection, core_at)
    rows_there = to_core(columns_of(projection, 1 - core_at))
    chip_rows = jnp.concatenate([rows_here, rows_there], axis=0)
    rights = []
    for chunk in range(FEATURE_CHUNKS):
        piece = chip_rows[:, chunk * width : (chunk + 1) * width]
        rights.append([piece] + [to_ctx(piece, offset) for offset in range(1, ctx_count)])

    resid_here = columns_of(resid_grad, core_at)
    resid_there = to_core(columns_of(resid_grad, 1 - core_at))
    resid = jnp.where(
        core_at == 0,
        jnp.concatenate([resid_here, resid_there], axis=0),
        jnp.concatenate([resid_there, resid_here], axis=0),
    )

    packed = jnp.concatenate([routes.T.astype(jnp.float32), gate_probs.T], axis=0)
    packed = lax.all_gather(packed, "exp", axis=0, tiled=False)
    route_width = routes.shape[1]
    all_routes = packed[:, :route_width]
    all_probs = packed[:, route_width:]
    capacity = max(2, 14 * tok_rows // (4 * EXP_DEV * exp_count))
    experts = jnp.stack([exp_at, exp_at ^ 1]).astype(jnp.float32)
    named = all_routes[None] == experts[:, None, None, None]
    hit = jnp.any(named, axis=2)
    prob = jnp.sum(jnp.where(named, all_probs[None], 0.0), axis=2)
    count = hit.astype(jnp.int32)
    rank = jnp.cumsum(count, axis=2) - count
    slot = jnp.where(hit, rank + (jnp.arange(exp_count, dtype=jnp.int32) % 2)[None, :, None] * capacity, -1)
    slot = slot.reshape(2, chips, 1, tile)
    picks = slot == jnp.arange(2 * capacity, dtype=jnp.int32)[None, None, :, None]
    scale = jnp.sum(jnp.where(picks, prob.reshape(2, chips, 1, tile), 0.0), axis=3, keepdims=True)
    picks = picks.astype(jnp.bfloat16)

    turned = conv_grad(out_grad, gate_in, conv_in, scan_grad, conv_weight, conv_bias, skip_scale)
    lefts = []
    for offset in range(ctx_count):
        piece = lax.dynamic_slice_in_dim(turned, (ctx_at ^ offset) * window, window, 0)
        if offset:
            piece = to_ctx(piece, offset)
        lefts += [piece, to_core(piece)]
    if channels < 128:
        lefts = [jnp.concatenate(lefts, axis=1)]
        rights = [[jnp.concatenate(chunk, axis=0)] for chunk in rights]

    place = chip_at.astype(jnp.int32).reshape(1)
    own = []
    for chunk in range(FEATURE_CHUNKS):
        product = matmul(
            lefts, rights[chunk], resid[:, chunk * width : (chunk + 1) * width], place
        )
        own += [product[at * tile : (at + 1) * tile] for at in range(chips)]

    pieces = len(own)
    steps = pieces + SKEW * (chips - 2)

    def pick(options):
        options = [options(place) for place in range(chips)]
        return lax.select_n(chip_at.astype(jnp.int32), *options) if chips > 2 else jnp.where(
            chip_at == 0, options[0], options[1]
        )

    def own_at(index):
        return own[min(max(index, 0), pieces - 1)].astype(jnp.float32)

    ups, downs = [], []

    def received(listing, index):
        index = min(max(index, 0), steps - 1)
        return listing[index].astype(jnp.float32)

    for step in range(steps):
        raising = pick(lambda place: own_at(step - SKEW * place))
        lowering = pick(lambda place: own_at(step - SKEW * (chips - 1 - place)))
        if step >= SKEW:
            raising = raising + ups[step - SKEW].astype(jnp.float32)
            lowering = lowering + downs[step - SKEW].astype(jnp.float32)
        ups.append(up(raising.astype(jnp.bfloat16)))
        downs.append(down(lowering.astype(jnp.bfloat16)))

    rows_own, rows_got = [], []
    for chunk in range(FEATURE_CHUNKS):
        finished = []
        for at in range(chips):
            index = chunk * chips + at
            below = pick(lambda place: received(ups, index + SKEW * (place - 1)))
            above = pick(lambda place: received(downs, index + SKEW * (chips - 2 - place)))
            finished.append((own_at(index) + below + above).astype(jnp.bfloat16))
        grads = jnp.stack(finished)
        rows = jnp.einsum("eist,itf->eisf", picks, grads, preferred_element_type=jnp.float32)
        rows = (rows * scale).astype(jnp.bfloat16).reshape(2, chips * 2 * capacity, width)
        rows_own.append(rows[0])
        rows_got.append(to_core(rows[1]))
    result = jnp.where(
        core_at == 0,
        jnp.concatenate(rows_own + rows_got, axis=1),
        jnp.concatenate(rows_got + rows_own, axis=1),
    )
    return result[None]


def solution(mesh):
    placed = (
        P(("ctx", "exp"), None),
        P(("ctx", "exp"), None),
        P(("ctx", "exp"), None),
        P(("ctx", "exp"), None),
        P(None, ("ctx", "exp")),
        P(("ctx", "exp")),
        P(("ctx", "exp")),
        P(("ctx", "exp"), None),
        P(("ctx", "exp"), None),
        P(("ctx", "exp"), None),
        P(("ctx", "exp"), None),
    )
    return jax.shard_map(
        on_device, mesh=mesh, in_specs=placed, out_specs=P("exp", "ctx", None), check_vma=False
    )
```

time: 371 us -> 327 us (0.88)
  blocking collectives: 199 us -> 13.5 us
  starting transfers between devices: 0.04 us -> 133 us
  Pallas kernels: 0 us -> 54.5 us
  waiting for transfers between devices: 106 us -> 76 us
  other arithmetic: 14.9 us -> 32 us
  matrix products: 16.1 us -> 1.67 us
  between operations: 13.6 us -> 1.3 us
  local copies, waits for them, and re-layouts: 20.3 us -> 12.8 us
    all_to_all x2 -> x0, blocking collectives: 199 us -> none  [the longest x1 112 us: on_device(): lax.all_to_all(blocked, 'exp', split_axis=2, concat_axis=0, tiled=True)]
    ppermute x0 -> x65, starting transfers between devices: none -> 133 us  [the longest x20 85.6 us: up(): lax.ppermute(array, 'exp', [(place, place + 2) for place in range(exp_cou...]
    ppermute x0 -> x65, waiting for transfers between devices: none -> 76 us  [the longest x15 42.9 us: to_ctx(): lax.ppermute(array, 'ctx', [(place, place ^ offset) for place in range(ct...]
    all_gather x1 -> x0, waiting for transfers between devices: 57.2 us -> none  [on_device(): block_weights = lax.all_gather(projection, 'exp', axis=0, tiled=True)]
    pallas_call x0 -> x5, Pallas kernels: none -> 54.5 us  [the longest x1 31.7 us: conv_grad(): pl.pallas_call(functools.partial(conv_kernel, tile), grid=(channels // bl...]
    reduce_scatter x1 -> x0, waiting for transfers between devices: 48.5 us -> none  [on_device(): lax.psum_scatter(lax.dot_general(local_grad, block_weights, (((0,), (0,))...]
    dot_general x2 -> x4, matrix products: 16.1 us -> 1.67 us  [on_device(): jnp.einsum('eist,itf->eisf', picks, grads, preferred_element_type=jnp.flo...]
    all_gather x0 -> x1, blocking collectives: none -> 13.5 us  [on_device(): packed = lax.all_gather(packed, 'exp', axis=0, tiled=False)]
  transfers between devices with their start and end apart: 2 -> 65, of which waited for: 2 -> 21; matrix products, arithmetic and copies ran while one was open for 9% -> 10% of each run, Pallas kernels for 0% -> 17%
where the time goes in v1:
time: 327 us; the launch traced here: 325 us
  starting transfers between devices  133 us (41%)
  waiting for transfers between devices  76 us (23%)
  Pallas kernels  54.5 us (17%)
  other arithmetic  32 us (10%)
  blocking collectives  13.5 us (4%)
  local copies, waits for them, and re-layouts  12.8 us (4%)
    ppermute x20, starting transfers between devices, up(): lax.ppermute(array, 'exp', [(place, place + 2) for place in range(exp_cou...  85.6 us
    ppermute x15, waiting for transfers between devices, to_ctx(): lax.ppermute(array, 'ctx', [(place, place ^ offset) for place in range(ct...  42.9 us
    pallas_call x1, Pallas kernels, conv_grad(): pl.pallas_call(functools.partial(conv_kernel, tile), grid=(channels // bl...  31.7 us
    ppermute x20, starting transfers between devices, down(): lax.ppermute(array, 'exp', [(place + 2, place) for place in range(exp_cou...  26.2 us
    pallas_call x4, Pallas kernels, matmul(): pl.pallas_call(functools.partial(matmul_kernel, len(lefts), len(rights)),...  22.8 us
    ppermute x20, waiting for transfers between devices, down(): lax.ppermute(array, 'exp', [(place + 2, place) for place in range(exp_cou...  22.6 us
    ppermute x15, starting transfers between devices, to_ctx(): lax.ppermute(array, 'ctx', [(place, place ^ offset) for place in range(ct...  20.3 us
    all_gather x1, blocking collectives, on_device(): packed = lax.all_gather(packed, 'exp', axis=0, tiled=False)  13.5 us
  transfers between devices with their start and end apart: 65, of which 21 were waited for; matrix products, arithmetic and copies ran while one was open for 10% of the time, Pallas kernels for 17%

profile of v1, /device:TPU:0, one launch (start us, length us, event | category | flops | bytes accessed | tf_op | source)
XLA Modules:
  0.0 325.2 jit_solution(7843711993385343000)
XLA Ops:
  0.0 3.2 constant_dynamic-slice_fusion.2
  4.1 1.6 copy-done
  5.7 31.7 %conv_grad.1 = bf16[4096,256]{1,0:T(8,128)(2,1)S(1)} custom-call(bf16[256,4096]{1,0:T(8,128)(2,1)S(1)} %copy-done, bf16[256,4096]{1,0:T(8,128)(2,1)} %gate_in.1, bf16[256,4096]{1,0:T(8,128)(2,1)} %conv_in.1, bf16[256,4096]{1,0:T(8,128)(2,1)} %scan_grad.1, f32[256,4]{1,0:T(8,128)S(1)} %bitcast.104, f32[256,1]{1,0:T(8,128)S(1)} %copy.25.bias, ...), custom_call_target="tpu_custom_call" | custom-call | flops 41943040 | bytes 10485760 | tf_op jit(solution)/shard_map/conv_grad/pallas_call | solution.py:74
  37.6 3.5 %collective-permute-start.5 = (bf16[1024,256]{1,0:T(8,128)(2,1)S(1)}, bf16[1024,256]{1,0:T(8,128)(2,1)S(1)}, u32[]{:S(2)}, u32[]{:S(2)}) collective-permute-start(bf16[1024,256]{1,0:T(8,128)(2,1)S(1)} %get-tuple-element.54), channel_id=1, source_target_pairs={{0,24},{8,16},{16,8},{24,0},{1,25},{9,17},{17,9},{25,1},{2,26},{10... | collective-permute-start | bytes 1572872 | tf_op jit(solution)/shard_map/ppermute | solution.py:168
  42.7 11.3 %collective-permute-done.5.refs_6_ = bf16[1024,256]{1,0:T(8,128)(2,1)S(1)} collective-permute-done((bf16[1024,256]{1,0:T(8,128)(2,1)S(1)}, bf16[1024,256]{1,0:T(8,128)(2,1)S(1)}, u32[]{:S(2)}, u32[]{:S(2)}) %collective-permute-start.5) | collective-permute-done | bytes 524320 | tf_op jit(solution)/shard_map/ppermute | solution.py:168
  54.0 11.1 %collective-permute-done.3.refs_4_ = bf16[1024,256]{1,0:T(8,128)(2,1)} collective-permute-done((bf16[1024,256]{1,0:T(8,128)(2,1)S(1)}, bf16[1024,256]{1,0:T(8,128)(2,1)}, u32[]{:S(2)}, u32[]{:S(2)}) %collective-permute-start.3) | collective-permute-done | bytes 524320 | tf_op jit(solution)/shard_map/ppermute | solution.py:168
  67.3 1.7 collective-permute-start.10
  72.4 2.0 maximum_select_fusion
  74.6 1.7 collective-permute-start.16
  76.2 6.9 %collective-permute-done.10.refs_11_ = bf16[512,512]{1,0:T(8,128)(2,1)} collective-permute-done((bf16[512,512]{1,0:T(8,128)(2,1)S(1)}, bf16[512,512]{1,0:T(8,128)(2,1)}, u32[]{:S(2)}, u32[]{:S(2)}) %collective-permute-start.10) | collective-permute-done | bytes 524320 | tf_op jit(solution)/shard_map/ppermute | solution.py:168
  83.1 11.1 %collective-permute-done.9.refs_10_ = bf16[512,512]{1,0:T(8,128)(2,1)} collective-permute-done((bf16[512,512]{1,0:T(8,128)(2,1)S(1)}, bf16[512,512]{1,0:T(8,128)(2,1)}, u32[]{:S(2)}, u32[]{:S(2)}) %collective-permute-start.9) | collective-permute-done | bytes 524320 | tf_op jit(solution)/shard_map/ppermute | solution.py:168
  94.4 5.8 %partial_product.4 = bf16[1024,512]{1,0:T(8,128)(2,1)} custom-call(s32[1]{0:T(128)} %bitcast.place, bf16[1024,256]{1,0:T(8,128)(2,1)S(1)} %get-tuple-element.57.refs_0_, bf16[1024,256]{1,0:T(8,128)(2,1)S(1)} %copy-done.5, bf16[1024,256]{1,0:T(8,128)(2,1)} %collective-permute-done.1.refs_2_, bf16[1024,256]{1,0:T(8,128)(2,1)} %collective-permute-done.2.refs_3_, ...), custom_call_target="tpu_custom_call" | custom-call | flops 2147483648 | bytes 7340032 | tf_op jit(solution)/shard_map/partial_product/pallas_call | solution.py:119
  100.2 1.9 fusion.151
  103.3 1.7 slice.147
  105.0 5.3 %collective-permute-start.12 = (bf16[256,512]{1,0:T(8,128)(2,1)}, bf16[256,512]{1,0:T(8,128)(2,1)}, u32[]{:S(2)}, u32[]{:S(2)}) collective-permute-start(bf16[256,512]{1,0:T(8,128)(2,1)} %slice.147), channel_id=1, source_target_pairs={{0,2},{1,3},{2,4},{3,5},{4,6},{5,7},{8,10},{9,11},{10,12},{11,13},... | collective-permute-start | bytes 786440 | tf_op jit(solution)/shard_map/ppermute | solution.py:171
  113.6 1.5 collective-permute-done.12
  115.1 1.6 fusion.42
  116.7 4.4 %collective-permute-start.13 = (bf16[256,512]{1,0:T(8,128)(2,1)S(1)}, bf16[256,512]{1,0:T(8,128)(2,1)S(1)}, u32[]{:S(2)}, u32[]{:S(2)}) collective-permute-start(bf16[256,512]{1,0:T(8,128)(2,1)S(1)} %get-tuple-element.70), channel_id=1, source_target_pairs={{0,2},{1,3},{2,4},{3,5},{4,6},{5,7},{8,10},{9,11},{10,12},{11,13},... | collective-permute-start | bytes 786440 | tf_op jit(solution)/shard_map/ppermute | solution.py:171
  124.6 5.6 %partial_product.5 = bf16[1024,512]{1,0:T(8,128)(2,1)} custom-call(s32[1]{0:T(128)} %bitcast.place, bf16[1024,256]{1,0:T(8,128)(2,1)S(1)} %get-tuple-element.57.refs_0_, bf16[1024,256]{1,0:T(8,128)(2,1)S(1)} %copy-done.6, bf16[1024,256]{1,0:T(8,128)(2,1)} %collective-permute-done.1.refs_2_, bf16[1024,256]{1,0:T(8,128)(2,1)} %collective-permute-done.2.refs_3_, ...), custom_call_target="tpu_custom_call" | custom-call | flops 2147483648 | bytes 7340032 | tf_op jit(solution)/shard_map/partial_product/pallas_call | solution.py:119
  130.2 2.4 fusion.44
  132.7 3.2 collective-permute-start.21
  136.0 13.5 %all-gather.1 = f32[8,4,128]{2,1,0:T(4,128)S(1)} all-gather(f32[1,4,128]{2,1,0:T(4,128)S(1)} %maximum_bitcast_fusion.8), channel_id=2, replica_groups=mesh['ctx'=4,'exp'=8] {'exp'}, dimensions={0}, use_global_device_ids=true | all-gather | bytes 18432 | tf_op jit(solution)/shard_map/all_gather | solution.py:196
  149.5 3.0 collective-permute-start.17
  155.2 4.6 %collective-permute-start.22 = (bf16[256,512]{1,0:T(8,128)(2,1)S(1)}, bf16[256,512]{1,0:T(8,128)(2,1)S(1)}, u32[]{:S(2)}, u32[]{:S(2)}) collective-permute-start(bf16[256,512]{1,0:T(8,128)(2,1)S(1)} %fusion.28), channel_id=1, source_target_pairs={{0,2},{1,3},{2,4},{3,5},{4,6},{5,7},{8,10},{9,11},{10,12},{11,13},... | collective-permute-start | bytes 786440 | tf_op jit(solution)/shard_map/ppermute | solution.py:171
  159.9 1.8 collective-permute-start.33
  166.0 2.5 fusion.74
  168.4 1.4 collective-permute-start.20
  169.9 5.8 %collective-permute-start.23 = (bf16[256,512]{1,0:T(8,128)(2,1)}, bf16[256,512]{1,0:T(8,128)(2,1)}, u32[]{:S(2)}, u32[]{:S(2)}) collective-permute-start(bf16[256,512]{1,0:T(8,128)(2,1)} %get-tuple-element.46), channel_id=1, source_target_pairs={{0,2},{1,3},{2,4},{3,5},{4,6},{5,7},{8,10},{9,11},{10,12},{11,13},... | collective-permute-start | bytes 786440 | tf_op jit(solution)/shard_map/ppermute | solution.py:171
  176.3 1.6 collective-permute-start.31
  178.7 1.8 collective-permute-start.44
  180.5 4.5 %collective-permute-start.27 = (bf16[256,512]{1,0:T(8,128)(2,1)}, bf16[256,512]{1,0:T(8,128)(2,1)}, u32[]{:S(2)}, u32[]{:S(2)}) collective-permute-start(bf16[256,512]{1,0:T(8,128)(2,1)} %get-tuple-element.44), channel_id=1, source_target_pairs={{0,2},{1,3},{2,4},{3,5},{4,6},{5,7},{8,10},{9,11},{10,12},{11,13},... | collective-permute-start | bytes 786440 | tf_op jit(solution)/shard_map/ppermute | solution.py:171
  185.0 3.2 fusion.76
  189.5 4.6 %collective-permute-start.29 = (bf16[256,512]{1,0:T(8,128)(2,1)}, bf16[256,512]{1,0:T(8,128)(2,1)S(1)}, u32[]{:S(2)}, u32[]{:S(2)}) collective-permute-start(bf16[256,512]{1,0:T(8,128)(2,1)} %get-tuple-element.50), channel_id=1, source_target_pairs={{0,2},{1,3},{2,4},{3,5},{4,6},{5,7},{8,10},{9,11},{10,12},{11,13},... | collective-permute-start | bytes 786440 | tf_op jit(solution)/shard_map/ppermute | solution.py:171
  194.2 1.6 collective-permute-start.43
  197.6 5.9 %partial_product.6 = bf16[1024,512]{1,0:T(8,128)(2,1)} custom-call(s32[1]{0:T(128)} %bitcast.place, bf16[1024,256]{1,0:T(8,128)(2,1)S(1)} %get-tuple-element.57.refs_0_, bf16[1024,256]{1,0:T(8,128)(2,1)S(1)} %copy-done.7, bf16[1024,256]{1,0:T(8,128)(2,1)} %collective-permute-done.1.refs_2_, bf16[1024,256]{1,0:T(8,128)(2,1)} %collective-permute-done.2.refs_3_, ...), custom_call_target="tpu_custom_call" | custom-call | flops 2147483648 | bytes 7340032 | tf_op jit(solution)/shard_map/partial_product/pallas_call | solution.py:119
  204.9 1.6 fusion.86
  206.5 4.6 %collective-permute-start.34 = (bf16[256,512]{1,0:T(8,128)(2,1)S(1)}, bf16[256,512]{1,0:T(8,128)(2,1)S(1)}, u32[]{:S(2)}, u32[]{:S(2)}) collective-permute-start(bf16[256,512]{1,0:T(8,128)(2,1)S(1)} %get-tuple-element.8), channel_id=1, source_target_pairs={{0,2},{1,3},{2,4},{3,5},{4,6},{5,7},{8,10},{9,11},{10,12},{11,13},... | collective-permute-start | bytes 786440 | tf_op jit(solution)/shard_map/ppermute | solution.py:171
  212.6 5.5 %partial_product.7 = bf16[1024,512]{1,0:T(8,128)(2,1)} custom-call(s32[1]{0:T(128)} %bitcast.place, bf16[1024,256]{1,0:T(8,128)(2,1)S(1)} %get-tuple-element.57.refs_0_, bf16[1024,256]{1,0:T(8,128)(2,1)S(1)} %copy-done.7, bf16[1024,256]{1,0:T(8,128)(2,1)} %collective-permute-done.1.refs_2_, bf16[1024,256]{1,0:T(8,128)(2,1)} %collective-permute-done.2.refs_3_, ...), custom_call_target="tpu_custom_call" | custom-call | flops 2147483648 | bytes 7340032 | tf_op jit(solution)/shard_map/partial_product/pallas_call | solution.py:119
  218.2 4.7 %collective-permute-start.36 = (bf16[256,512]{1,0:T(8,128)(2,1)S(1)}, bf16[256,512]{1,0:T(8,128)(2,1)S(1)}, u32[]{:S(2)}, u32[]{:S(2)}) collective-permute-start(bf16[256,512]{1,0:T(8,128)(2,1)S(1)} %get-tuple-element.10), channel_id=1, source_target_pairs={{0,2},{1,3},{2,4},{3,5},{4,6},{5,7},{8,10},{9,11},{10,12},{11,13},... | collective-permute-start | bytes 786440 | tf_op jit(solution)/shard_map/ppermute | solution.py:171
  223.4 1.4 collective-permute-start.37
  224.9 1.6 fusion.171
  226.5 4.7 %collective-permute-start.38 = (bf16[256,512]{1,0:T(8,128)(2,1)S(1)}, bf16[256,512]{1,0:T(8,128)(2,1)S(1)}, u32[]{:S(2)}, u32[]{:S(2)}) collective-permute-start(bf16[256,512]{1,0:T(8,128)(2,1)S(1)} %get-tuple-element.39), channel_id=1, source_target_pairs={{0,2},{1,3},{2,4},{3,5},{4,6},{5,7},{8,10},{9,11},{10,12},{11,13},... | collective-permute-start | bytes 786440 | tf_op jit(solution)/shard_map/ppermute | solution.py:171
  232.8 4.6 %collective-permute-start.40 = (bf16[256,512]{1,0:T(8,128)(2,1)S(1)}, bf16[256,512]{1,0:T(8,128)(2,1)S(1)}, u32[]{:S(2)}, u32[]{:S(2)}) collective-permute-start(bf16[256,512]{1,0:T(8,128)(2,1)S(1)} %get-tuple-element.42), channel_id=1, source_target_pairs={{0,2},{1,3},{2,4},{3,5},{4,6},{5,7},{8,10},{9,11},{10,12},{11,13},... | collective-permute-start | bytes 786440 | tf_op jit(solution)/shard_map/ppermute | solution.py:171
  237.4 1.4 collective-permute-start.41
  240.1 2.0 fusion.172
  242.6 3.5 %collective-permute-start.45 = (bf16[256,512]{1,0:T(8,128)(2,1)S(1)}, bf16[256,512]{1,0:T(8,128)(2,1)S(1)}, u32[]{:S(2)}, u32[]{:S(2)}) collective-permute-start(bf16[256,512]{1,0:T(8,128)(2,1)S(1)} %get-tuple-element.5), channel_id=1, source_target_pairs={{0,2},{1,3},{2,4},{3,5},{4,6},{5,7},{8,10},{9,11},{10,12},{11,13},... | collective-permute-start | bytes 786440 | tf_op jit(solution)/shard_map/ppermute | solution.py:171
  248.0 5.5 %collective-permute-start.47 = (bf16[256,512]{1,0:T(8,128)(2,1)S(1)}, bf16[256,512]{1,0:T(8,128)(2,1)S(1)}, u32[]{:S(2)}, u32[]{:S(2)}) collective-permute-start(bf16[256,512]{1,0:T(8,128)(2,1)S(1)} %get-tuple-element.7), channel_id=1, source_target_pairs={{0,2},{1,3},{2,4},{3,5},{4,6},{5,7},{8,10},{9,11},{10,12},{11,13},... | collective-permute-start | bytes 786440 | tf_op jit(solution)/shard_map/ppermute | solution.py:171
  253.5 1.8 collective-permute-done.46
  255.7 3.9 %collective-permute-start.49 = (bf16[256,512]{1,0:T(8,128)(2,1)S(1)}, bf16[256,512]{1,0:T(8,128)(2,1)S(1)}, u32[]{:S(2)}, u32[]{:S(2)}) collective-permute-start(bf16[256,512]{1,0:T(8,128)(2,1)S(1)} %get-tuple-element.32), channel_id=1, source_target_pairs={{0,2},{1,3},{2,4},{3,5},{4,6},{5,7},{8,10},{9,11},{10,12},{11,13},... | collective-permute-start | bytes 786440 | tf_op jit(solution)/shard_map/ppermute | solution.py:171
  261.2 4.6 %collective-permute-start.51 = (bf16[256,512]{1,0:T(8,128)(2,1)S(1)}, bf16[256,512]{1,0:T(8,128)(2,1)S(1)}, u32[]{:S(2)}, u32[]{:S(2)}) collective-permute-start(bf16[256,512]{1,0:T(8,128)(2,1)S(1)} %fusion.124), channel_id=1, source_target_pairs={{0,2},{1,3},{2,4},{3,5},{4,6},{5,7},{8,10},{9,11},{10,12},{11,13},... | collective-permute-start | bytes 786440 | tf_op jit(solution)/shard_map/ppermute | solution.py:171
  265.7 1.4 fusion.165
  268.9 2.0 collective-permute-done.51
  272.8 5.0 %collective-permute-start.53 = (bf16[256,512]{1,0:T(8,128)(2,1)S(1)}, bf16[256,512]{1,0:T(8,128)(2,1)S(1)}, u32[]{:S(2)}, u32[]{:S(2)}) collective-permute-start(bf16[256,512]{1,0:T(8,128)(2,1)S(1)} %get-tuple-element.27), channel_id=1, source_target_pairs={{0,2},{1,3},{2,4},{3,5},{4,6},{5,7},{8,10},{9,11},{10,12},{11,13},... | collective-permute-start | bytes 786440 | tf_op jit(solution)/shard_map/ppermute | solution.py:171
  277.9 3.9 %collective-permute-start.55 = (bf16[256,512]{1,0:T(8,128)(2,1)S(1)}, bf16[256,512]{1,0:T(8,128)(2,1)S(1)}, u32[]{:S(2)}, u32[]{:S(2)}) collective-permute-start(bf16[256,512]{1,0:T(8,128)(2,1)S(1)} %get-tuple-element.28), channel_id=1, source_target_pairs={{0,2},{1,3},{2,4},{3,5},{4,6},{5,7},{8,10},{9,11},{10,12},{11,13},... | collective-permute-start | bytes 786440 | tf_op jit(solution)/shard_map/ppermute | solution.py:171
  284.7 1.5 fusion.162
  286.3 6.9 %collective-permute-done.54 = bf16[256,512]{1,0:T(8,128)(2,1)S(1)} collective-permute-done((bf16[256,512]{1,0:T(8,128)(2,1)S(1)}, bf16[256,512]{1,0:T(8,128)(2,1)S(1)}, u32[]{:S(2)}, u32[]{:S(2)}) %collective-permute-start.54) | collective-permute-done | bytes 262176 | tf_op jit(solution)/shard_map/ppermute | solution.py:174
  293.1 4.9 %collective-permute-done.56 = bf16[256,512]{1,0:T(8,128)(2,1)S(1)} collective-permute-done((bf16[256,512]{1,0:T(8,128)(2,1)S(1)}, bf16[256,512]{1,0:T(8,128)(2,1)S(1)}, u32[]{:S(2)}, u32[]{:S(2)}) %collective-permute-start.56) | collective-permute-done | bytes 262176 | tf_op jit(solution)/shard_map/ppermute | solution.py:174
  298.3 3.7 %collective-permute-start.57 = (bf16[256,512]{1,0:T(8,128)(2,1)S(1)}, bf16[256,512]{1,0:T(8,128)(2,1)S(1)}, u32[]{:S(2)}, u32[]{:S(2)}) collective-permute-start(bf16[256,512]{1,0:T(8,128)(2,1)S(1)} %get-tuple-element.61), channel_id=1, source_target_pairs={{0,2},{1,3},{2,4},{3,5},{4,6},{5,7},{8,10},{9,11},{10,12},{11,13},... | collective-permute-start | bytes 786440 | tf_op jit(solution)/shard_map/ppermute | solution.py:171
  305.1 1.6 collective-permute-done.57
  306.8 6.4 %collective-permute-done.58 = bf16[256,512]{1,0:T(8,128)(2,1)S(1)} collective-permute-done((bf16[256,512]{1,0:T(8,128)(2,1)S(1)}, bf16[256,512]{1,0:T(8,128)(2,1)S(1)}, u32[]{:S(2)}, u32[]{:S(2)}) %collective-permute-start.58) | collective-permute-done | bytes 262176 | tf_op jit(solution)/shard_map/ppermute | solution.py:174
  313.8 1.6 collective-permute-start.59
  316.5 2.7 collective-permute-done.59
  320.4 1.7 collective-permute-done.64
  322.9 2.2 broadcast_select_fusion
  (229 shorter events, 52.0 us)
Async XLA Ops:
  3.2 62.4 %collective-permute-start.7 = (bf16[256,2048]{1,0:T(8,128)(2,1)}, bf16[256,2048]{1,0:T(8,128)(2,1)}, u32[]{:S(2)}, u32[]{:S(2)}) collective-permute-start(bf16[256,2048]{1,0:T(8,128)(2,1)} %get-tuple-element.52), channel_id=1, source_target_pairs={{0,1},{1,0},{2,3},{3,2},{4,5},{5,4},{6,7},{7,6},{8,9},{9,8},{10,11... | collective-permute-start | bytes 3145736 | tf_op jit(solution)/shard_map/ppermute | solution.py:165
  37.6 16.3 %collective-permute-start.5 = (bf16[1024,256]{1,0:T(8,128)(2,1)S(1)}, bf16[1024,256]{1,0:T(8,128)(2,1)S(1)}, u32[]{:S(2)}, u32[]{:S(2)}) collective-permute-start(bf16[1024,256]{1,0:T(8,128)(2,1)S(1)} %get-tuple-element.54), channel_id=1, source_target_pairs={{0,24},{8,16},{16,8},{24,0},{1,25},{9,17},{17,9},{25,1},{2,26},{10... | collective-permute-start | bytes 1572872 | tf_op jit(solution)/shard_map/ppermute | solution.py:168
  41.1 23.9 %collective-permute-start.3 = (bf16[1024,256]{1,0:T(8,128)(2,1)S(1)}, bf16[1024,256]{1,0:T(8,128)(2,1)}, u32[]{:S(2)}, u32[]{:S(2)}) collective-permute-start(bf16[1024,256]{1,0:T(8,128)(2,1)S(1)} %get-tuple-element.55), channel_id=1, source_target_pairs={{0,16},{8,24},{16,0},{24,8},{1,17},{9,25},{17,1},{25,9},{2,18},{10... | collective-permute-start | bytes 1572872 | tf_op jit(solution)/shard_map/ppermute | solution.py:168
  41.6 23.7 %collective-permute-start.1 = (bf16[1024,256]{1,0:T(8,128)(2,1)S(1)}, bf16[1024,256]{1,0:T(8,128)(2,1)}, u32[]{:S(2)}, u32[]{:S(2)}) collective-permute-start(bf16[1024,256]{1,0:T(8,128)(2,1)S(1)} %get-tuple-element.56), channel_id=1, source_target_pairs={{0,8},{8,0},{16,24},{24,16},{1,9},{9,1},{17,25},{25,17},{2,10},{10... | collective-permute-start | bytes 1572872 | tf_op jit(solution)/shard_map/ppermute | solution.py:168
  42.7 24.6 %collective-permute-start.11 = (bf16[128,2048]{1,0:T(8,128)(2,1)S(1)}, bf16[128,2048]{1,0:T(8,128)(2,1)}, u32[]{:S(2)}, u32[]{:S(2)}) collective-permute-start(bf16[128,2048]{1,0:T(8,128)(2,1)S(1)} %get-tuple-element.73), channel_id=1, source_target_pairs={{0,1},{1,0},{2,3},{3,2},{4,5},{5,4},{6,7},{7,6},{8,9},{9,8},{10,11... | collective-permute-start | bytes 1572872 | tf_op jit(solution)/shard_map/ppermute | solution.py:165
  53.9 15.0 %collective-permute-start = (bf16[1024,256]{1,0:T(8,128)(2,1)S(1)}, bf16[1024,256]{1,0:T(8,128)(2,1)S(1)}, u32[]{:S(2)}, u32[]{:S(2)}) collective-permute-start(bf16[1024,256]{1,0:T(8,128)(2,1)S(1)} %get-tuple-element.57.refs_0_), channel_id=1, source_target_pairs={{0,1},{1,0},{2,3},{3,2},{4,5},{5,4},{6,7},{7,6},{8,9},{9,8},{10,11... | collective-permute-start | bytes 1572872 | tf_op jit(solution)/shard_map/ppermute | solution.py:165
  65.1 6.0 %collective-permute-start.6 = (bf16[1024,256]{1,0:T(8,128)(2,1)S(1)}, bf16[1024,256]{1,0:T(8,128)(2,1)S(1)}, u32[]{:S(2)}, u32[]{:S(2)}) collective-permute-start(bf16[1024,256]{1,0:T(8,128)(2,1)S(1)} %collective-permute-done.5.refs_6_), channel_id=1, source_target_pairs={{0,1},{1,0},{2,3},{3,2},{4,5},{5,4},{6,7},{7,6},{8,9},{9,8},{10,11... | collective-permute-start | bytes 1572872 | tf_op jit(solution)/shard_map/ppermute | solution.py:165
  65.4 9.2 %collective-permute-start.4 = (bf16[1024,256]{1,0:T(8,128)(2,1)}, bf16[1024,256]{1,0:T(8,128)(2,1)}, u32[]{:S(2)}, u32[]{:S(2)}) collective-permute-start(bf16[1024,256]{1,0:T(8,128)(2,1)} %collective-permute-done.3.refs_4_), channel_id=1, source_target_pairs={{0,1},{1,0},{2,3},{3,2},{4,5},{5,4},{6,7},{7,6},{8,9},{9,8},{10,11... | collective-permute-start | bytes 1572872 | tf_op jit(solution)/shard_map/ppermute | solution.py:165
  65.6 10.7 %collective-permute-start.2 = (bf16[1024,256]{1,0:T(8,128)(2,1)}, bf16[1024,256]{1,0:T(8,128)(2,1)}, u32[]{:S(2)}, u32[]{:S(2)}) collective-permute-start(bf16[1024,256]{1,0:T(8,128)(2,1)} %collective-permute-done.1.refs_2_), channel_id=1, source_target_pairs={{0,1},{1,0},{2,3},{3,2},{4,5},{5,4},{6,7},{7,6},{8,9},{9,8},{10,11... | collective-permute-start | bytes 1572872 | tf_op jit(solution)/shard_map/ppermute | solution.py:165
  67.3 15.9 %collective-permute-start.10 = (bf16[512,512]{1,0:T(8,128)(2,1)S(1)}, bf16[512,512]{1,0:T(8,128)(2,1)}, u32[]{:S(2)}, u32[]{:S(2)}) collective-permute-start(bf16[512,512]{1,0:T(8,128)(2,1)S(1)} %get-tuple-element.36.refs_8_), channel_id=1, source_target_pairs={{0,24},{8,16},{16,8},{24,0},{1,25},{9,17},{17,9},{25,1},{2,26},{10... | collective-permute-start | bytes 1572872 | tf_op jit(solution)/shard_map/ppermute | solution.py:168
  69.7 24.6 %collective-permute-start.9 = (bf16[512,512]{1,0:T(8,128)(2,1)S(1)}, bf16[512,512]{1,0:T(8,128)(2,1)}, u32[]{:S(2)}, u32[]{:S(2)}) collective-permute-start(bf16[512,512]{1,0:T(8,128)(2,1)S(1)} %get-tuple-element.36.refs_8_), channel_id=1, source_target_pairs={{0,16},{8,24},{16,0},{24,8},{1,17},{9,25},{17,1},{25,9},{2,18},{10... | collective-permute-start | bytes 1572872 | tf_op jit(solution)/shard_map/ppermute | solution.py:168
  71.9 22.5 %collective-permute-start.8 = (bf16[512,512]{1,0:T(8,128)(2,1)S(1)}, bf16[512,512]{1,0:T(8,128)(2,1)}, u32[]{:S(2)}, u32[]{:S(2)}) collective-permute-start(bf16[512,512]{1,0:T(8,128)(2,1)S(1)} %get-tuple-element.36.refs_8_), channel_id=1, source_target_pairs={{0,8},{8,0},{16,24},{24,16},{1,9},{9,1},{17,25},{25,17},{2,10},{10... | collective-permute-start | bytes 1572872 | tf_op jit(solution)/shard_map/ppermute | solution.py:168
  74.6 46.6 %collective-permute-start.16 = (bf16[512,512]{1,0:T(8,128)(2,1)S(1)}, bf16[512,512]{1,0:T(8,128)(2,1)}, u32[]{:S(2)}, u32[]{:S(2)}) collective-permute-start(bf16[512,512]{1,0:T(8,128)(2,1)S(1)} %get-tuple-element.37.refs_8_), channel_id=1, source_target_pairs={{0,24},{8,16},{16,8},{24,0},{1,25},{9,17},{17,9},{25,1},{2,26},{10... | collective-permute-start | bytes 1572872 | tf_op jit(solution)/shard_map/ppermute | solution.py:168
  102.0 10.3 %collective-permute-start.24 = (bf16[256,512]{1,0:T(8,128)(2,1)}, bf16[256,512]{1,0:T(8,128)(2,1)}, u32[]{:S(2)}, u32[]{:S(2)}) collective-permute-start(bf16[256,512]{1,0:T(8,128)(2,1)} %fusion.151), channel_id=1, source_target_pairs={{2,0},{3,1},{4,2},{5,3},{6,4},{7,5},{10,8},{11,9},{12,10},{13,11},... | collective-permute-start | bytes 786440 | tf_op jit(solution)/shard_map/ppermute | solution.py:174
  105.0 10.2 %collective-permute-start.12 = (bf16[256,512]{1,0:T(8,128)(2,1)}, bf16[256,512]{1,0:T(8,128)(2,1)}, u32[]{:S(2)}, u32[]{:S(2)}) collective-permute-start(bf16[256,512]{1,0:T(8,128)(2,1)} %slice.147), channel_id=1, source_target_pairs={{0,2},{1,3},{2,4},{3,5},{4,6},{5,7},{8,10},{9,11},{10,12},{11,13},... | collective-permute-start | bytes 786440 | tf_op jit(solution)/shard_map/ppermute | solution.py:171
  110.2 13.2 %collective-permute-start.15 = (bf16[512,512]{1,0:T(8,128)(2,1)S(1)}, bf16[512,512]{1,0:T(8,128)(2,1)S(1)}, u32[]{:S(2)}, u32[]{:S(2)}) collective-permute-start(bf16[512,512]{1,0:T(8,128)(2,1)S(1)} %get-tuple-element.37.refs_8_), channel_id=1, source_target_pairs={{0,16},{8,24},{16,0},{24,8},{1,17},{9,25},{17,1},{25,9},{2,18},{10... | collective-permute-start | bytes 1572872 | tf_op jit(solution)/shard_map/ppermute | solution.py:168
  111.6 13.0 %collective-permute-start.14 = (bf16[512,512]{1,0:T(8,128)(2,1)S(1)}, bf16[512,512]{1,0:T(8,128)(2,1)S(1)}, u32[]{:S(2)}, u32[]{:S(2)}) collective-permute-start(bf16[512,512]{1,0:T(8,128)(2,1)S(1)} %get-tuple-element.37.refs_8_), channel_id=1, source_target_pairs={{0,8},{8,0},{16,24},{24,16},{1,9},{9,1},{17,25},{25,17},{2,10},{10... | collective-permute-start | bytes 1572872 | tf_op jit(solution)/shard_map/ppermute | solution.py:168
  112.3 17.9 %collective-permute-start.18 = (bf16[256,512]{1,0:T(8,128)(2,1)}, bf16[256,512]{1,0:T(8,128)(2,1)S(1)}, u32[]{:S(2)}, u32[]{:S(2)}) collective-permute-start(bf16[256,512]{1,0:T(8,128)(2,1)} %slice.147), channel_id=1, source_target_pairs={{2,0},{3,1},{4,2},{5,3},{6,4},{7,5},{10,8},{11,9},{12,10},{13,11},... | collective-permute-start | bytes 786440 | tf_op jit(solution)/shard_map/ppermute | solution.py:174
  116.7 13.5 %collective-permute-start.13 = (bf16[256,512]{1,0:T(8,128)(2,1)S(1)}, bf16[256,512]{1,0:T(8,128)(2,1)S(1)}, u32[]{:S(2)}, u32[]{:S(2)}) collective-permute-start(bf16[256,512]{1,0:T(8,128)(2,1)S(1)} %get-tuple-element.70), channel_id=1, source_target_pairs={{0,2},{1,3},{2,4},{3,5},{4,6},{5,7},{8,10},{9,11},{10,12},{11,13},... | collective-permute-start | bytes 786440 | tf_op jit(solution)/shard_map/ppermute | solution.py:171
  121.1 9.1 %collective-permute-start.25 = (bf16[256,512]{1,0:T(8,128)(2,1)S(1)}, bf16[256,512]{1,0:T(8,128)(2,1)S(1)}, u32[]{:S(2)}, u32[]{:S(2)}) collective-permute-start(bf16[256,512]{1,0:T(8,128)(2,1)S(1)} %get-tuple-element.71), channel_id=1, source_target_pairs={{2,0},{3,1},{4,2},{5,3},{6,4},{7,5},{10,8},{11,9},{12,10},{13,11},... | collective-permute-start | bytes 786440 | tf_op jit(solution)/shard_map/ppermute | solution.py:174
  132.7 21.2 %collective-permute-start.21 = (bf16[256,512]{1,0:T(8,128)(2,1)}, bf16[256,512]{1,0:T(8,128)(2,1)S(1)}, u32[]{:S(2)}, u32[]{:S(2)}) collective-permute-start(bf16[256,512]{1,0:T(8,128)(2,1)} %get-tuple-element.69), channel_id=1, source_target_pairs={{0,2},{1,3},{2,4},{3,5},{4,6},{5,7},{8,10},{9,11},{10,12},{11,13},... | collective-permute-start | bytes 786440 | tf_op jit(solution)/shard_map/ppermute | solution.py:171
  149.5 13.5 %collective-permute-start.17 = (bf16[256,512]{1,0:T(8,128)(2,1)S(1)}, bf16[256,512]{1,0:T(8,128)(2,1)S(1)}, u32[]{:S(2)}, u32[]{:S(2)}) collective-permute-start(bf16[256,512]{1,0:T(8,128)(2,1)S(1)} %get-tuple-element.47), channel_id=1, source_target_pairs={{0,2},{1,3},{2,4},{3,5},{4,6},{5,7},{8,10},{9,11},{10,12},{11,13},... | collective-permute-start | bytes 786440 | tf_op jit(solution)/shard_map/ppermute | solution.py:171
  152.6 11.7 %collective-permute-start.19 = (bf16[256,512]{1,0:T(8,128)(2,1)S(1)}, bf16[256,512]{1,0:T(8,128)(2,1)S(1)}, u32[]{:S(2)}, u32[]{:S(2)}) collective-permute-start(bf16[256,512]{1,0:T(8,128)(2,1)S(1)} %get-tuple-element.68), channel_id=1, source_target_pairs={{2,0},{3,1},{4,2},{5,3},{6,4},{7,5},{10,8},{11,9},{12,10},{13,11},... | collective-permute-start | bytes 786440 | tf_op jit(solution)/shard_map/ppermute | solution.py:174
  155.2 10.0 %collective-permute-start.22 = (bf16[256,512]{1,0:T(8,128)(2,1)S(1)}, bf16[256,512]{1,0:T(8,128)(2,1)S(1)}, u32[]{:S(2)}, u32[]{:S(2)}) collective-permute-start(bf16[256,512]{1,0:T(8,128)(2,1)S(1)} %fusion.28), channel_id=1, source_target_pairs={{0,2},{1,3},{2,4},{3,5},{4,6},{5,7},{8,10},{9,11},{10,12},{11,13},... | collective-permute-start | bytes 786440 | tf_op jit(solution)/shard_map/ppermute | solution.py:171
  159.9 28.2 %collective-permute-start.33 = (bf16[512,512]{1,0:T(8,128)(2,1)S(1)}, bf16[512,512]{1,0:T(8,128)(2,1)}, u32[]{:S(2)}, u32[]{:S(2)}) collective-permute-start(bf16[512,512]{1,0:T(8,128)(2,1)S(1)} %get-tuple-element.38.refs_8_), channel_id=1, source_target_pairs={{0,24},{8,16},{16,8},{24,0},{1,25},{9,17},{17,9},{25,1},{2,26},{10... | collective-permute-start | bytes 1572872 | tf_op jit(solution)/shard_map/ppermute | solution.py:168
  161.7 27.7 %collective-permute-start.32 = (bf16[512,512]{1,0:T(8,128)(2,1)S(1)}, bf16[512,512]{1,0:T(8,128)(2,1)}, u32[]{:S(2)}, u32[]{:S(2)}) collective-permute-start(bf16[512,512]{1,0:T(8,128)(2,1)S(1)} %get-tuple-element.38.refs_8_), channel_id=1, source_target_pairs={{0,16},{8,24},{16,0},{24,8},{1,17},{9,25},{17,1},{25,9},{2,18},{10... | collective-permute-start | bytes 1572872 | tf_op jit(solution)/shard_map/ppermute | solution.py:168
  163.0 13.4 %collective-permute-start.26 = (bf16[256,512]{1,0:T(8,128)(2,1)}, bf16[256,512]{1,0:T(8,128)(2,1)S(1)}, u32[]{:S(2)}, u32[]{:S(2)}) collective-permute-start(bf16[256,512]{1,0:T(8,128)(2,1)} %get-tuple-element.48), channel_id=1, source_target_pairs={{2,0},{3,1},{4,2},{5,3},{6,4},{7,5},{10,8},{11,9},{12,10},{13,11},... | collective-permute-start | bytes 786440 | tf_op jit(solution)/shard_map/ppermute | solution.py:174
  168.4 10.3 %collective-permute-start.20 = (bf16[256,512]{1,0:T(8,128)(2,1)}, bf16[256,512]{1,0:T(8,128)(2,1)}, u32[]{:S(2)}, u32[]{:S(2)}) collective-permute-start(bf16[256,512]{1,0:T(8,128)(2,1)} %get-tuple-element.45), channel_id=1, source_target_pairs={{2,0},{3,1},{4,2},{5,3},{6,4},{7,5},{10,8},{11,9},{12,10},{13,11},... | collective-permute-start | bytes 786440 | tf_op jit(solution)/shard_map/ppermute | solution.py:174
  169.9 10.6 %collective-permute-start.23 = (bf16[256,512]{1,0:T(8,128)(2,1)}, bf16[256,512]{1,0:T(8,128)(2,1)}, u32[]{:S(2)}, u32[]{:S(2)}) collective-permute-start(bf16[256,512]{1,0:T(8,128)(2,1)} %get-tuple-element.46), channel_id=1, source_target_pairs={{0,2},{1,3},{2,4},{3,5},{4,6},{5,7},{8,10},{9,11},{10,12},{11,13},... | collective-permute-start | bytes 786440 | tf_op jit(solution)/shard_map/ppermute | solution.py:171
  176.3 17.8 %collective-permute-start.31 = (bf16[512,512]{1,0:T(8,128)(2,1)S(1)}, bf16[512,512]{1,0:T(8,128)(2,1)}, u32[]{:S(2)}, u32[]{:S(2)}) collective-permute-start(bf16[512,512]{1,0:T(8,128)(2,1)S(1)} %get-tuple-element.38.refs_8_), channel_id=1, source_target_pairs={{0,8},{8,0},{16,24},{24,16},{1,9},{9,1},{17,25},{25,17},{2,10},{10... | collective-permute-start | bytes 1572872 | tf_op jit(solution)/shard_map/ppermute | solution.py:168
  178.7 32.3 %collective-permute-start.44 = (bf16[512,512]{1,0:T(8,128)(2,1)S(1)}, bf16[512,512]{1,0:T(8,128)(2,1)}, u32[]{:S(2)}, u32[]{:S(2)}) collective-permute-start(bf16[512,512]{1,0:T(8,128)(2,1)S(1)} %get-tuple-element.35.refs_8_), channel_id=1, source_target_pairs={{0,24},{8,16},{16,8},{24,0},{1,25},{9,17},{17,9},{25,1},{2,26},{10... | collective-permute-start | bytes 1572872 | tf_op jit(solution)/shard_map/ppermute | solution.py:168
  180.5 15.3 %collective-permute-start.27 = (bf16[256,512]{1,0:T(8,128)(2,1)}, bf16[256,512]{1,0:T(8,128)(2,1)}, u32[]{:S(2)}, u32[]{:S(2)}) collective-permute-start(bf16[256,512]{1,0:T(8,128)(2,1)} %get-tuple-element.44), channel_id=1, source_target_pairs={{0,2},{1,3},{2,4},{3,5},{4,6},{5,7},{8,10},{9,11},{10,12},{11,13},... | collective-permute-start | bytes 786440 | tf_op jit(solution)/shard_map/ppermute | solution.py:171
  188.2 15.4 %collective-permute-start.28 = (bf16[256,512]{1,0:T(8,128)(2,1)}, bf16[256,512]{1,0:T(8,128)(2,1)}, u32[]{:S(2)}, u32[]{:S(2)}) collective-permute-start(bf16[256,512]{1,0:T(8,128)(2,1)} %get-tuple-element.49), channel_id=1, source_target_pairs={{2,0},{3,1},{4,2},{5,3},{6,4},{7,5},{10,8},{11,9},{12,10},{13,11},... | collective-permute-start | bytes 786440 | tf_op jit(solution)/shard_map/ppermute | solution.py:174
  189.5 15.4 %collective-permute-start.29 = (bf16[256,512]{1,0:T(8,128)(2,1)}, bf16[256,512]{1,0:T(8,128)(2,1)S(1)}, u32[]{:S(2)}, u32[]{:S(2)}) collective-permute-start(bf16[256,512]{1,0:T(8,128)(2,1)} %get-tuple-element.50), channel_id=1, source_target_pairs={{0,2},{1,3},{2,4},{3,5},{4,6},{5,7},{8,10},{9,11},{10,12},{11,13},... | collective-permute-start | bytes 786440 | tf_op jit(solution)/shard_map/ppermute | solution.py:171
  194.2 18.4 %collective-permute-start.43 = (bf16[512,512]{1,0:T(8,128)(2,1)S(1)}, bf16[512,512]{1,0:T(8,128)(2,1)S(1)}, u32[]{:S(2)}, u32[]{:S(2)}) collective-permute-start(bf16[512,512]{1,0:T(8,128)(2,1)S(1)} %get-tuple-element.35.refs_8_), channel_id=1, source_target_pairs={{0,16},{8,24},{16,0},{24,8},{1,17},{9,25},{17,1},{25,9},{2,18},{10... | collective-permute-start | bytes 1572872 | tf_op jit(solution)/shard_map/ppermute | solution.py:168
  195.8 16.8 %collective-permute-start.42 = (bf16[512,512]{1,0:T(8,128)(2,1)S(1)}, bf16[512,512]{1,0:T(8,128)(2,1)S(1)}, u32[]{:S(2)}, u32[]{:S(2)}) collective-permute-start(bf16[512,512]{1,0:T(8,128)(2,1)S(1)} %get-tuple-element.35.refs_8_), channel_id=1, source_target_pairs={{0,8},{8,0},{16,24},{24,16},{1,9},{9,1},{17,25},{25,17},{2,10},{10... | collective-permute-start | bytes 1572872 | tf_op jit(solution)/shard_map/ppermute | solution.py:168
  203.5 19.4 %collective-permute-start.30 = (bf16[256,512]{1,0:T(8,128)(2,1)S(1)}, bf16[256,512]{1,0:T(8,128)(2,1)S(1)}, u32[]{:S(2)}, u32[]{:S(2)}) collective-permute-start(bf16[256,512]{1,0:T(8,128)(2,1)S(1)} %copy-done.36), channel_id=1, source_target_pairs={{2,0},{3,1},{4,2},{5,3},{6,4},{7,5},{10,8},{11,9},{12,10},{13,11},... | collective-permute-start | bytes 786440 | tf_op jit(solution)/shard_map/ppermute | solution.py:174
  206.5 16.4 %collective-permute-start.34 = (bf16[256,512]{1,0:T(8,128)(2,1)S(1)}, bf16[256,512]{1,0:T(8,128)(2,1)S(1)}, u32[]{:S(2)}, u32[]{:S(2)}) collective-permute-start(bf16[256,512]{1,0:T(8,128)(2,1)S(1)} %get-tuple-element.8), channel_id=1, source_target_pairs={{0,2},{1,3},{2,4},{3,5},{4,6},{5,7},{8,10},{9,11},{10,12},{11,13},... | collective-permute-start | bytes 786440 | tf_op jit(solution)/shard_map/ppermute | solution.py:171
  211.0 11.9 %collective-permute-start.35 = (bf16[256,512]{1,0:T(8,128)(2,1)S(1)}, bf16[256,512]{1,0:T(8,128)(2,1)S(1)}, u32[]{:S(2)}, u32[]{:S(2)}) collective-permute-start(bf16[256,512]{1,0:T(8,128)(2,1)S(1)} %get-tuple-element.9), channel_id=1, source_target_pairs={{2,0},{3,1},{4,2},{5,3},{6,4},{7,5},{10,8},{11,9},{12,10},{13,11},... | collective-permute-start | bytes 786440 | tf_op jit(solution)/shard_map/ppermute | solution.py:174
  218.2 14.3 %collective-permute-start.36 = (bf16[256,512]{1,0:T(8,128)(2,1)S(1)}, bf16[256,512]{1,0:T(8,128)(2,1)S(1)}, u32[]{:S(2)}, u32[]{:S(2)}) collective-permute-start(bf16[256,512]{1,0:T(8,128)(2,1)S(1)} %get-tuple-element.10), channel_id=1, source_target_pairs={{0,2},{1,3},{2,4},{3,5},{4,6},{5,7},{8,10},{9,11},{10,12},{11,13},... | collective-permute-start | bytes 786440 | tf_op jit(solution)/shard_map/ppermute | solution.py:171
  223.4 9.2 %collective-permute-start.37 = (bf16[256,512]{1,0:T(8,128)(2,1)S(1)}, bf16[256,512]{1,0:T(8,128)(2,1)S(1)}, u32[]{:S(2)}, u32[]{:S(2)}) collective-permute-start(bf16[256,512]{1,0:T(8,128)(2,1)S(1)} %get-tuple-element.40), channel_id=1, source_target_pairs={{2,0},{3,1},{4,2},{5,3},{6,4},{7,5},{10,8},{11,9},{12,10},{13,11},... | collective-permute-start | bytes 786440 | tf_op jit(solution)/shard_map/ppermute | solution.py:174
  226.5 12.4 %collective-permute-start.38 = (bf16[256,512]{1,0:T(8,128)(2,1)S(1)}, bf16[256,512]{1,0:T(8,128)(2,1)S(1)}, u32[]{:S(2)}, u32[]{:S(2)}) collective-permute-start(bf16[256,512]{1,0:T(8,128)(2,1)S(1)} %get-tuple-element.39), channel_id=1, source_target_pairs={{0,2},{1,3},{2,4},{3,5},{4,6},{5,7},{8,10},{9,11},{10,12},{11,13},... | collective-permute-start | bytes 786440 | tf_op jit(solution)/shard_map/ppermute | solution.py:171
  231.2 8.9 %collective-permute-start.39 = (bf16[256,512]{1,0:T(8,128)(2,1)S(1)}, bf16[256,512]{1,0:T(8,128)(2,1)S(1)}, u32[]{:S(2)}, u32[]{:S(2)}) collective-permute-start(bf16[256,512]{1,0:T(8,128)(2,1)S(1)} %get-tuple-element.41), channel_id=1, source_target_pairs={{2,0},{3,1},{4,2},{5,3},{6,4},{7,5},{10,8},{11,9},{12,10},{13,11},... | collective-permute-start | bytes 786440 | tf_op jit(solution)/shard_map/ppermute | solution.py:174
  232.8 9.3 %collective-permute-start.40 = (bf16[256,512]{1,0:T(8,128)(2,1)S(1)}, bf16[256,512]{1,0:T(8,128)(2,1)S(1)}, u32[]{:S(2)}, u32[]{:S(2)}) collective-permute-start(bf16[256,512]{1,0:T(8,128)(2,1)S(1)} %get-tuple-element.42), channel_id=1, source_target_pairs={{0,2},{1,3},{2,4},{3,5},{4,6},{5,7},{8,10},{9,11},{10,12},{11,13},... | collective-permute-start | bytes 786440 | tf_op jit(solution)/shard_map/ppermute | solution.py:171
  237.4 16.1 %collective-permute-start.41 = (bf16[256,512]{1,0:T(8,128)(2,1)S(1)}, bf16[256,512]{1,0:T(8,128)(2,1)S(1)}, u32[]{:S(2)}, u32[]{:S(2)}) collective-permute-start(bf16[256,512]{1,0:T(8,128)(2,1)S(1)} %get-tuple-element.43), channel_id=1, source_target_pairs={{2,0},{3,1},{4,2},{5,3},{6,4},{7,5},{10,8},{11,9},{12,10},{13,11},... | collective-permute-start | bytes 786440 | tf_op jit(solution)/shard_map/ppermute | solution.py:174
  242.6 10.9 %collective-permute-start.45 = (bf16[256,512]{1,0:T(8,128)(2,1)S(1)}, bf16[256,512]{1,0:T(8,128)(2,1)S(1)}, u32[]{:S(2)}, u32[]{:S(2)}) collective-permute-start(bf16[256,512]{1,0:T(8,128)(2,1)S(1)} %get-tuple-element.5), channel_id=1, source_target_pairs={{0,2},{1,3},{2,4},{3,5},{4,6},{5,7},{8,10},{9,11},{10,12},{11,13},... | collective-permute-start | bytes 786440 | tf_op jit(solution)/shard_map/ppermute | solution.py:171
  246.1 9.2 %collective-permute-start.46 = (bf16[256,512]{1,0:T(8,128)(2,1)S(1)}, bf16[256,512]{1,0:T(8,128)(2,1)S(1)}, u32[]{:S(2)}, u32[]{:S(2)}) collective-permute-start(bf16[256,512]{1,0:T(8,128)(2,1)S(1)} %get-tuple-element.6), channel_id=1, source_target_pairs={{2,0},{3,1},{4,2},{5,3},{6,4},{7,5},{10,8},{11,9},{12,10},{13,11},... | collective-permute-start | bytes 786440 | tf_op jit(solution)/shard_map/ppermute | solution.py:174
  247.9 24.9 %collective-permute-start.61 = (bf16[448,512]{1,0:T(8,128)(2,1)S(1)}, bf16[448,512]{1,0:T(8,128)(2,1)S(1)}, u32[]{:S(2)}, u32[]{:S(2)}) collective-permute-start(bf16[448,512]{1,0:T(8,128)(2,1)S(1)} %bitcast.110), channel_id=1, source_target_pairs={{0,1},{1,0},{2,3},{3,2},{4,5},{5,4},{6,7},{7,6},{8,9},{9,8},{10,11... | collective-permute-start | bytes 1376264 | tf_op jit(solution)/shard_map/ppermute | solution.py:165
  248.0 13.0 %collective-permute-start.47 = (bf16[256,512]{1,0:T(8,128)(2,1)S(1)}, bf16[256,512]{1,0:T(8,128)(2,1)S(1)}, u32[]{:S(2)}, u32[]{:S(2)}) collective-permute-start(bf16[256,512]{1,0:T(8,128)(2,1)S(1)} %get-tuple-element.7), channel_id=1, source_target_pairs={{0,2},{1,3},{2,4},{3,5},{4,6},{5,7},{8,10},{9,11},{10,12},{11,13},... | collective-permute-start | bytes 786440 | tf_op jit(solution)/shard_map/ppermute | solution.py:171
  255.7 13.2 %collective-permute-start.49 = (bf16[256,512]{1,0:T(8,128)(2,1)S(1)}, bf16[256,512]{1,0:T(8,128)(2,1)S(1)}, u32[]{:S(2)}, u32[]{:S(2)}) collective-permute-start(bf16[256,512]{1,0:T(8,128)(2,1)S(1)} %get-tuple-element.32), channel_id=1, source_target_pairs={{0,2},{1,3},{2,4},{3,5},{4,6},{5,7},{8,10},{9,11},{10,12},{11,13},... | collective-permute-start | bytes 786440 | tf_op jit(solution)/shard_map/ppermute | solution.py:171
  259.7 9.2 %collective-permute-start.48 = (bf16[256,512]{1,0:T(8,128)(2,1)S(1)}, bf16[256,512]{1,0:T(8,128)(2,1)S(1)}, u32[]{:S(2)}, u32[]{:S(2)}) collective-permute-start(bf16[256,512]{1,0:T(8,128)(2,1)S(1)} %get-tuple-element.33), channel_id=1, source_target_pairs={{2,0},{3,1},{4,2},{5,3},{6,4},{7,5},{10,8},{11,9},{12,10},{13,11},... | collective-permute-start | bytes 786440 | tf_op jit(solution)/shard_map/ppermute | solution.py:174
  261.2 9.7 %collective-permute-start.51 = (bf16[256,512]{1,0:T(8,128)(2,1)S(1)}, bf16[256,512]{1,0:T(8,128)(2,1)S(1)}, u32[]{:S(2)}, u32[]{:S(2)}) collective-permute-start(bf16[256,512]{1,0:T(8,128)(2,1)S(1)} %fusion.124), channel_id=1, source_target_pairs={{0,2},{1,3},{2,4},{3,5},{4,6},{5,7},{8,10},{9,11},{10,12},{11,13},... | collective-permute-start | bytes 786440 | tf_op jit(solution)/shard_map/ppermute | solution.py:171
  267.6 14.2 %collective-permute-start.50 = (bf16[256,512]{1,0:T(8,128)(2,1)S(1)}, bf16[256,512]{1,0:T(8,128)(2,1)S(1)}, u32[]{:S(2)}, u32[]{:S(2)}) collective-permute-start(bf16[256,512]{1,0:T(8,128)(2,1)S(1)} %get-tuple-element.34), channel_id=1, source_target_pairs={{2,0},{3,1},{4,2},{5,3},{6,4},{7,5},{10,8},{11,9},{12,10},{13,11},... | collective-permute-start | bytes 786440 | tf_op jit(solution)/shard_map/ppermute | solution.py:174
  271.3 10.5 %collective-permute-start.52 = (bf16[256,512]{1,0:T(8,128)(2,1)S(1)}, bf16[256,512]{1,0:T(8,128)(2,1)S(1)}, u32[]{:S(2)}, u32[]{:S(2)}) collective-permute-start(bf16[256,512]{1,0:T(8,128)(2,1)S(1)} %get-tuple-element.29), channel_id=1, source_target_pairs={{2,0},{3,1},{4,2},{5,3},{6,4},{7,5},{10,8},{11,9},{12,10},{13,11},... | collective-permute-start | bytes 786440 | tf_op jit(solution)/shard_map/ppermute | solution.py:174
  272.7 47.6 %collective-permute-start.62 = (bf16[448,512]{1,0:T(8,128)(2,1)S(1)}, bf16[448,512]{1,0:T(8,128)(2,1)S(1)}, u32[]{:S(2)}, u32[]{:S(2)}) collective-permute-start(bf16[448,512]{1,0:T(8,128)(2,1)S(1)} %bitcast.109), channel_id=1, source_target_pairs={{0,1},{1,0},{2,3},{3,2},{4,5},{5,4},{6,7},{7,6},{8,9},{9,8},{10,11... | collective-permute-start | bytes 1376264 | tf_op jit(solution)/shard_map/ppermute | solution.py:165
  272.8 13.4 %collective-permute-start.53 = (bf16[256,512]{1,0:T(8,128)(2,1)S(1)}, bf16[256,512]{1,0:T(8,128)(2,1)S(1)}, u32[]{:S(2)}, u32[]{:S(2)}) collective-permute-start(bf16[256,512]{1,0:T(8,128)(2,1)S(1)} %get-tuple-element.27), channel_id=1, source_target_pairs={{0,2},{1,3},{2,4},{3,5},{4,6},{5,7},{8,10},{9,11},{10,12},{11,13},... | collective-permute-start | bytes 786440 | tf_op jit(solution)/shard_map/ppermute | solution.py:171
  277.9 27.2 %collective-permute-start.55 = (bf16[256,512]{1,0:T(8,128)(2,1)S(1)}, bf16[256,512]{1,0:T(8,128)(2,1)S(1)}, u32[]{:S(2)}, u32[]{:S(2)}) collective-permute-start(bf16[256,512]{1,0:T(8,128)(2,1)S(1)} %get-tuple-element.28), channel_id=1, source_target_pairs={{0,2},{1,3},{2,4},{3,5},{4,6},{5,7},{8,10},{9,11},{10,12},{11,13},... | collective-permute-start | bytes 786440 | tf_op jit(solution)/shard_map/ppermute | solution.py:171
  282.1 11.0 %collective-permute-start.54 = (bf16[256,512]{1,0:T(8,128)(2,1)S(1)}, bf16[256,512]{1,0:T(8,128)(2,1)S(1)}, u32[]{:S(2)}, u32[]{:S(2)}) collective-permute-start(bf16[256,512]{1,0:T(8,128)(2,1)S(1)} %get-tuple-element.30), channel_id=1, source_target_pairs={{2,0},{3,1},{4,2},{5,3},{6,4},{7,5},{10,8},{11,9},{12,10},{13,11},... | collective-permute-start | bytes 786440 | tf_op jit(solution)/shard_map/ppermute | solution.py:174
  283.4 14.6 %collective-permute-start.56 = (bf16[256,512]{1,0:T(8,128)(2,1)S(1)}, bf16[256,512]{1,0:T(8,128)(2,1)S(1)}, u32[]{:S(2)}, u32[]{:S(2)}) collective-permute-start(bf16[256,512]{1,0:T(8,128)(2,1)S(1)} %get-tuple-element.31), channel_id=1, source_target_pairs={{2,0},{3,1},{4,2},{5,3},{6,4},{7,5},{10,8},{11,9},{12,10},{13,11},... | collective-permute-start | bytes 786440 | tf_op jit(solution)/shard_map/ppermute | solution.py:174
  298.3 8.4 %collective-permute-start.57 = (bf16[256,512]{1,0:T(8,128)(2,1)S(1)}, bf16[256,512]{1,0:T(8,128)(2,1)S(1)}, u32[]{:S(2)}, u32[]{:S(2)}) collective-permute-start(bf16[256,512]{1,0:T(8,128)(2,1)S(1)} %get-tuple-element.61), channel_id=1, source_target_pairs={{0,2},{1,3},{2,4},{3,5},{4,6},{5,7},{8,10},{9,11},{10,12},{11,13},... | collective-permute-start | bytes 786440 | tf_op jit(solution)/shard_map/ppermute | solution.py:171
  302.0 11.1 %collective-permute-start.58 = (bf16[256,512]{1,0:T(8,128)(2,1)S(1)}, bf16[256,512]{1,0:T(8,128)(2,1)S(1)}, u32[]{:S(2)}, u32[]{:S(2)}) collective-permute-start(bf16[256,512]{1,0:T(8,128)(2,1)S(1)} %get-tuple-element.63), channel_id=1, source_target_pairs={{2,0},{3,1},{4,2},{5,3},{6,4},{7,5},{10,8},{11,9},{12,10},{13,11},... | collective-permute-start | bytes 786440 | tf_op jit(solution)/shard_map/ppermute | solution.py:174
  303.8 12.7 %collective-permute-start.60 = (bf16[256,512]{1,0:T(8,128)(2,1)S(1)}, bf16[256,512]{1,0:T(8,128)(2,1)S(1)}, u32[]{:S(2)}, u32[]{:S(2)}) collective-permute-start(bf16[256,512]{1,0:T(8,128)(2,1)S(1)} %get-tuple-element.62), channel_id=1, source_target_pairs={{2,0},{3,1},{4,2},{5,3},{6,4},{7,5},{10,8},{11,9},{12,10},{13,11},... | collective-permute-start | bytes 786440 | tf_op jit(solution)/shard_map/ppermute | solution.py:174
  313.8 5.5 %collective-permute-start.59 = (bf16[256,512]{1,0:T(8,128)(2,1)S(1)}, bf16[256,512]{1,0:T(8,128)(2,1)S(1)}, u32[]{:S(2)}, u32[]{:S(2)}) collective-permute-start(bf16[256,512]{1,0:T(8,128)(2,1)S(1)} %get-tuple-element.60), channel_id=1, source_target_pairs={{0,2},{1,3},{2,4},{3,5},{4,6},{5,7},{8,10},{9,11},{10,12},{11,13},... | collective-permute-start | bytes 786440 | tf_op jit(solution)/shard_map/ppermute | solution.py:171
  315.9 4.5 %collective-permute-start.63 = (bf16[448,512]{1,0:T(8,128)(2,1)S(1)}, bf16[448,512]{1,0:T(8,128)(2,1)S(1)}, u32[]{:S(2)}, u32[]{:S(2)}) collective-permute-start(bf16[448,512]{1,0:T(8,128)(2,1)S(1)} %bitcast.111), channel_id=1, source_target_pairs={{0,1},{1,0},{2,3},{3,2},{4,5},{5,4},{6,7},{7,6},{8,9},{9,8},{10,11... | collective-permute-start | bytes 1376264 | tf_op jit(solution)/shard_map/ppermute | solution.py:165
  (43 other events, 432.1 us)

commit v2 on v1

v2 whole, which is shorter than its diff:
```python
import functools

import jax
import jax.numpy as jnp
from jax import lax
from jax.experimental import pallas as pl
from jax.experimental.pallas import tpu as pltpu
from jax.sharding import PartitionSpec as P

EXP_DEV = 1
PIECES = 8
DELAY = 3
VMEM_BYTES = 48 * 1024 * 1024


def conv_kernel(tile, out_grad, gate_in, conv_in, scan_grad, taps, bias, skip, turned, flat):
    channels, length = out_grad.shape
    kernel_taps = taps.shape[1]
    rows_at_once = 16

    def row_group(group, _):
        row_at = pl.multiple_of(group * rows_at_once, rows_at_once)
        rows = pl.ds(row_at, rows_at_once)

        def spread(column):
            return jnp.concatenate([jnp.broadcast_to(column, (rows_at_once, 128))] * (tile // 128), axis=1)

        weights = [spread(taps[rows, tap : tap + 1]) for tap in range(kernel_taps)]
        bias_half = spread(bias[rows, :])
        skip_value = spread(skip[rows, :])
        after = jnp.zeros((rows_at_once, 128), jnp.float32)
        for at in range(length - tile, -1, -tile):
            columns = pl.ds(at, tile)
            gate = 0.5 * gate_in[rows, columns].astype(jnp.float32)
            gated = out_grad[rows, columns].astype(jnp.float32) * (gate + gate * jnp.tanh(gate))
            here = conv_in[rows, columns].astype(jnp.float32)
            if at:
                before = conv_in[rows, pl.ds(at - 128, 128)].astype(jnp.float32)
            else:
                before = jnp.zeros((rows_at_once, 128), jnp.float32)
            wide = jnp.concatenate([before, here], axis=1)
            half = bias_half + weights[kernel_taps - 1] * here
            for tap in range(kernel_taps - 1):
                back = kernel_taps - 1 - tap
                half = half + weights[tap] * pltpu.roll(wide, back, 1)[:, 128:]
            turn = jnp.tanh(half)
            scan = scan_grad[rows, columns].astype(jnp.float32)
            grad = (scan + skip_value * gated) * (1.0 + turn + half * (1.0 - turn * turn))
            wide_grad = jnp.concatenate([grad, after], axis=1)
            total = weights[kernel_taps - 1] * grad
            for tap in range(kernel_taps - 1):
                ahead = kernel_taps - 1 - tap
                total = total + weights[tap] * pltpu.roll(wide_grad, tile + 128 - ahead, 1)[:, :tile]
            flat[rows, columns] = total.astype(flat.dtype)
            after = grad[:, :128]
        return 0

    lax.fori_loop(0, channels // rows_at_once, row_group, 0)
    for at in range(0, length, tile):
        turned[pl.ds(at, tile), :] = flat[:, pl.ds(at, tile)].T


def conv_grad(out_grad, gate_in, conv_in, scan_grad, conv_weight, conv_bias, skip_scale):
    channels, length = out_grad.shape
    block = min(128, channels)
    tile = min(512, length)
    whole = pl.BlockSpec((block, length), lambda step: (step, 0))
    return pl.pallas_call(
        functools.partial(conv_kernel, tile),
        grid=(channels // block,),
        in_specs=[whole] * 4
        + [
            pl.BlockSpec((block, conv_weight.shape[0]), lambda step: (step, 0)),
            pl.BlockSpec((block, 1), lambda step: (step, 0)),
            pl.BlockSpec((block, 1), lambda step: (step, 0)),
        ],
        out_specs=pl.BlockSpec((length, block), lambda step: (0, step)),
        out_shape=jax.ShapeDtypeStruct((length, channels), jnp.bfloat16),
        scratch_shapes=[pltpu.VMEM((block, length), jnp.bfloat16)],
        compiler_params=pltpu.CompilerParams(vmem_limit_bytes=VMEM_BYTES),
        cost_estimate=pl.CostEstimate(
            flops=40 * channels * length, bytes_accessed=10 * channels * length, transcendentals=2 * channels * length
        ),
        name="conv_grad",
    )(out_grad, gate_in, conv_in, scan_grad, 0.5 * conv_weight.T, 0.5 * conv_bias[:, None], skip_scale[:, None])


def matmul_kernel(lefts, rights, place, *refs):
    left_refs = refs[:lefts]
    right_refs = refs[lefts : lefts + rights]
    resid = refs[lefts + rights]
    out = refs[lefts + rights + 1]
    left = jnp.concatenate([ref[...] for ref in left_refs], axis=1)
    right = jnp.concatenate([ref[...] for ref in right_refs], axis=0)
    total = jnp.dot(left, right, preferred_element_type=jnp.float32)
    mine = pl.program_id(0) == place[0]
    total = total + jnp.where(mine, resid[...].astype(jnp.float32), 0.0)
    out[...] = total.astype(out.dtype)


def matmul(lefts, rights, resid, place):
    tokens, depth = lefts[0].shape
    wide, width = rights[0].shape
    tile = resid.shape[0]
    flops = 2 * tokens * depth * len(lefts) * width
    moved = 2 * (tokens * depth * len(lefts) + wide * len(rights) * width + tokens * width)
    return pl.pallas_call(
        functools.partial(matmul_kernel, len(lefts), len(rights)),
        grid_spec=pltpu.PrefetchScalarGridSpec(
            num_scalar_prefetch=1,
            grid=(tokens // tile,),
            in_specs=[pl.BlockSpec((tile, depth), lambda step, place: (step, 0))] * len(lefts)
            + [pl.BlockSpec((wide, width), lambda step, place: (0, 0))] * len(rights)
            + [pl.BlockSpec(resid.shape, lambda step, place: (0, 0))],
            out_specs=pl.BlockSpec((tile, width), lambda step, place: (step, 0)),
        ),
        out_shape=jax.ShapeDtypeStruct((tokens, width), jnp.bfloat16),
        compiler_params=pltpu.CompilerParams(vmem_limit_bytes=VMEM_BYTES),
        cost_estimate=pl.CostEstimate(flops=flops, bytes_accessed=moved, transcendentals=0),
        name="partial_product",
    )(place, *lefts, *rights, resid)


def on_device(
    out_grad,
    gate_in,
    conv_in,
    scan_grad,
    conv_weight,
    conv_bias,
    skip_scale,
    projection,
    resid_grad,
    routes,
    gate_probs,
):
    ctx_count = lax.axis_size("ctx")
    exp_count = lax.axis_size("exp")
    chips = exp_count // 2
    ctx_at = lax.axis_index("ctx")
    exp_at = lax.axis_index("exp")
    chip_at = exp_at // 2
    core_at = exp_at % 2
    channels, length = out_grad.shape
    features = projection.shape[1]
    half = features // 2
    width = half // PIECES
    groups = [1, 1] + [2] * ((PIECES - 2) // 2)
    tok_rows = resid_grad.shape[0]
    window = tok_rows * exp_count
    tile = 2 * tok_rows

    def to_core(array):
        return lax.ppermute(array, "exp", [(place, place ^ 1) for place in range(exp_count)])

    def to_ctx(array, offset):
        return lax.ppermute(array, "ctx", [(place, place ^ offset) for place in range(ctx_count)])

    def swap_chips(array, low, inward=True, outward=True):
        pairs = set()
        for core in (0, 1):
            for near, far in ((low, low + 1), (chips - 1 - low, chips - 2 - low)):
                if inward:
                    pairs.add((2 * near + core, 2 * far + core))
                if outward:
                    pairs.add((2 * far + core, 2 * near + core))
        return lax.ppermute(array, "exp", sorted(pairs))

    def columns_of(array, core):
        return lax.dynamic_slice_in_dim(array, core * half, half, 1)

    rows_here = columns_of(projection, core_at)
    rows_there = to_core(columns_of(projection, 1 - core_at))
    chip_rows = jnp.concatenate([rows_here, rows_there], axis=0)
    rights = []
    at = 0
    for group in groups:
        piece = chip_rows[:, at : at + group * width]
        rights.append([piece] + [to_ctx(piece, offset) for offset in range(1, ctx_count)])
        at += group * width

    resid_here = columns_of(resid_grad, core_at)
    resid_there = to_core(columns_of(resid_grad, 1 - core_at))
    resid = jnp.where(
        core_at == 0,
        jnp.concatenate([resid_here, resid_there], axis=0),
        jnp.concatenate([resid_there, resid_here], axis=0),
    )

    turned = conv_grad(out_grad, gate_in, conv_in, scan_grad, conv_weight, conv_bias, skip_scale)
    turned, rights[0] = lax.optimization_barrier((turned, rights[0]))
    lefts = []
    for offset in range(ctx_count):
        piece = lax.dynamic_slice_in_dim(turned, (ctx_at ^ offset) * window, window, 0)
        if offset:
            piece = to_ctx(piece, offset)
        lefts += [piece, to_core(piece)]
    packed = jnp.concatenate([routes.T.astype(jnp.float32), gate_probs.T], axis=0)
    packed, lefts[0] = lax.optimization_barrier((packed, lefts[0]))
    routed = lax.all_gather(packed, "exp", axis=0, tiled=False)
    routed, lefts = lax.optimization_barrier((routed, lefts))
    if channels < 128:
        lefts = [jnp.concatenate(lefts, axis=1)]
        rights = [[jnp.concatenate(chunk, axis=0)] for chunk in rights]

    route_width = routes.shape[1]
    all_routes = routed[:, :route_width]
    all_probs = routed[:, route_width:]
    capacity = max(2, 14 * tok_rows // (4 * EXP_DEV * exp_count))
    experts = jnp.stack([exp_at, exp_at ^ 1]).astype(jnp.float32)
    named = all_routes[None] == experts[:, None, None, None]
    hit = jnp.any(named, axis=2)
    prob = jnp.sum(jnp.where(named, all_probs[None], 0.0), axis=2)
    count = hit.astype(jnp.int32)
    rank = jnp.cumsum(count, axis=2) - count
    slot = jnp.where(hit, rank + (jnp.arange(exp_count, dtype=jnp.int32) % 2)[None, :, None] * capacity, -1)
    slot = slot.reshape(2, chips, 1, tile)
    picks = slot == jnp.arange(2 * capacity, dtype=jnp.int32)[None, None, :, None]
    scale = jnp.sum(jnp.where(picks, prob.reshape(2, chips, 1, tile), 0.0), axis=3, keepdims=True)
    picks = picks.astype(jnp.bfloat16)

    place = chip_at.astype(jnp.int32).reshape(1)
    own = []
    at = 0
    for group, right in zip(groups, rights):
        product = matmul(lefts, right, resid[:, at : at + group * width], place)
        own += [product[:, part * width : (part + 1) * width] for part in range(group)]
        at += group * width

    middle = chips // 2
    distance = jnp.minimum(chip_at, chips - 1 - chip_at)
    rows_own, rows_got = [], []

    def add(one, other):
        return (one.astype(jnp.float32) + other.astype(jnp.float32)).astype(jnp.bfloat16)

    def finish(grads):
        rows = jnp.einsum("eist,itf->eisf", picks, grads.reshape(chips, tile, width), preferred_element_type=jnp.float32)
        rows = (rows * scale).astype(jnp.bfloat16).reshape(2, chips * 2 * capacity, width)
        rows_own.append(rows[0])
        rows_got.append(to_core(rows[1]))

    hops = middle - 1
    sums = [list(own)] + [[None] * PIECES for _ in range(hops)]
    ready = [[None] * PIECES for _ in range(hops + 1)]
    lag = DELAY - 1
    last = PIECES + lag * hops + DELAY * hops
    for step in range(last + 1):
        for hop in range(hops):
            inward = step - lag * hop
            outward = inward - DELAY - 2 * lag * (hops - 1 - hop)
            send_in = 0 <= inward < PIECES
            send_out = 0 <= outward < PIECES
            if not (send_in or send_out):
                continue
            if send_in and send_out:
                payload = jnp.where(distance == hop, sums[hop][inward], ready[hop + 1][outward])
            else:
                payload = sums[hop][inward] if send_in else ready[hop + 1][outward]
            got = swap_chips(payload, hop, send_in, send_out)
            if send_in:
                sums[hop + 1][inward] = add(sums[hop][inward], got)
                if hop == hops - 1:
                    crossed = swap_chips(sums[hop + 1][inward], middle - 1)
                    ready[hops][inward] = add(sums[hop + 1][inward], crossed)
            if send_out:
                ready[hop][outward] = jnp.where(distance == hop, got, ready[hop + 1][outward])
                if hop == 0:
                    finish(ready[0][outward])
    result = jnp.where(
        core_at == 0,
        jnp.concatenate(rows_own + rows_got, axis=1),
        jnp.concatenate(rows_got + rows_own, axis=1),
    )
    return result[None]


def solution(mesh):
    placed = (
        P(("ctx", "exp"), None),
        P(("ctx", "exp"), None),
        P(("ctx", "exp"), None),
        P(("ctx", "exp"), None),
        P(None, ("ctx", "exp")),
        P(("ctx", "exp")),
        P(("ctx", "exp")),
        P(("ctx", "exp"), None),
        P(("ctx", "exp"), None),
        P(("ctx", "exp"), None),
        P(("ctx", "exp"), None),
    )
    return jax.shard_map(
        on_device, mesh=mesh, in_specs=placed, out_specs=P("exp", "ctx", None), check_vma=False
    )
```

time: 327 us -> 287 us (0.88)
  starting transfers between devices: 133 us -> 84.8 us
  waiting for transfers between devices: 76 us -> 108 us
  Pallas kernels: 54.5 us -> 38.5 us
  other arithmetic: 32 us -> 18.6 us
  local copies, waits for them, and re-layouts: 12.8 us -> 20.1 us
    ppermute x40 -> x19, starting transfers between devices: 112 us -> 59.3 us  [swap_chips(): return lax.ppermute(array, 'exp', sorted(pairs))]
    ppermute x40 -> x19, waiting for transfers between devices: 31.4 us -> 73 us  [swap_chips(): return lax.ppermute(array, 'exp', sorted(pairs))]
    pallas_call x1, Pallas kernels: 31.7 us -> 16.9 us  [conv_grad(): pl.pallas_call(functools.partial(conv_kernel, tile), grid=(channels // bl...]
    convert_element_type x15 -> x8, other arithmetic: 17.1 us -> 3.54 us  [add(): (one.astype(jnp.float32) + other.astype(jnp.float32)).astype(jnp.bfloat16)]
    ppermute x15 -> x18, waiting for transfers between devices: 42.9 us -> 32.1 us  [to_ctx(): lax.ppermute(array, 'ctx', [(place, place ^ offset) for place in range(ct...]
    another operation x7 -> x0, other arithmetic: 8.19 us -> none  [on_device(): grads = jnp.stack(finished)]
    unnamed x97 -> x90, local copies, waits for them, and re-layouts: 6.03 us -> 9.66 us
    ppermute x15 -> x18, starting transfers between devices: 20.3 us -> 23.1 us  [to_ctx(): lax.ppermute(array, 'ctx', [(place, place ^ offset) for place in range(ct...]
  transfers between devices with their start and end apart: 65 -> 51, of which waited for: 21 -> 17; matrix products, arithmetic and copies ran while one was open for 10% -> 9% of each run, Pallas kernels for 17% -> 13%
where the time goes in v2:
time: 287 us; the launch traced here: 286 us
  waiting for transfers between devices  108 us (38%)
  starting transfers between devices  84.8 us (30%)
  Pallas kernels  38.5 us (13%)
  local copies, waits for them, and re-layouts  20.1 us (7%)
  other arithmetic  18.6 us (6%)
  blocking collectives  13 us (5%)
    ppermute x19, waiting for transfers between devices, swap_chips(): return lax.ppermute(array, 'exp', sorted(pairs))  73 us
    ppermute x19, starting transfers between devices, swap_chips(): return lax.ppermute(array, 'exp', sorted(pairs))  59.3 us
    ppermute x18, waiting for transfers between devices, to_ctx(): lax.ppermute(array, 'ctx', [(place, place ^ offset) for place in range(ct...  32.1 us
    ppermute x18, starting transfers between devices, to_ctx(): lax.ppermute(array, 'ctx', [(place, place ^ offset) for place in range(ct...  23.1 us
    pallas_call x5, Pallas kernels, matmul(): pl.pallas_call(functools.partial(matmul_kernel, len(lefts), len(rights)),...  21.6 us
    pallas_call x1, Pallas kernels, conv_grad(): pl.pallas_call(functools.partial(conv_kernel, tile), grid=(channels // bl...  16.9 us
    all_gather x1, blocking collectives, on_device(): routed = lax.all_gather(packed, 'exp', axis=0, tiled=False)  13 us
    unnamed x90, local copies, waits for them, and re-layouts  9.66 us
  transfers between devices with their start and end apart: 51, of which 17 were waited for; matrix products, arithmetic and copies ran while one was open for 9% of the time, Pallas kernels for 13%

profile of v2, /device:TPU:0, one launch (start us, length us, event | category | flops | bytes accessed | tf_op | source)
XLA Modules:
  0.0 286.2 jit_solution(3643327999276084183)
XLA Ops:
  0.0 3.3 %constant_dynamic-slice_fusion.7 = (bf16[256,2048]{1,0:T(8,128)(2,1)}, bf16[256,2048]{1,0:T(8,128)(2,1)}) fusion(bf16[256,4096]{1,0:T(8,128)(2,1)} %param.18, s32[]{:T(128)S(6)} %select_n.140, s32[]{:T(128)S(6)} %select_n.141), kind=kLoop, calls=%fused_computation.128 | loop fusion | bytes 4194312 | tf_op jit(solution)/shard_map/dynamic_slice | solution.py:170
  3.8 1.1 constant_dynamic-slice_fusion.1
  5.0 1.2 collective-permute-done
  6.3 1.0 copy-done.21
  7.2 1.1 fusion.26
  8.4 3.9 %collective-permute-start.3 = (bf16[512,256]{1,0:T(8,128)(2,1)S(1)}, bf16[512,256]{1,0:T(8,128)(2,1)S(1)}, u32[]{:S(2)}, u32[]{:S(2)}) collective-permute-start(bf16[512,256]{1,0:T(8,128)(2,1)S(1)} %get-tuple-element.32.refs_8_), channel_id=1, source_target_pairs={{0,24},{8,16},{16,8},{24,0},{1,25},{9,17},{17,9},{25,1},{2,26},{10... | collective-permute-start | bytes 786440 | tf_op jit(solution)/shard_map/ppermute | solution.py:157
  13.2 16.9 %conv_grad.1 = bf16[4096,256]{1,0:T(8,128)(2,1)S(1)} custom-call(bf16[256,4096]{1,0:T(8,128)(2,1)S(1)} %copy-done.8, bf16[256,4096]{1,0:T(8,128)(2,1)} %gate_in.1, bf16[256,4096]{1,0:T(8,128)(2,1)} %conv_in.1, bf16[256,4096]{1,0:T(8,128)(2,1)} %scan_grad.1, f32[256,4]{1,0:T(8,128)S(1)} %bitcast.151, f32[256,1]{1,0:T(8,128)S(1)} %copy.36.bias, ...), custom_call_target="tpu_custom_call" | custom-call | flops 41943040 | bytes 10485760 | tf_op jit(solution)/shard_map/conv_grad/pallas_call | solution.py:68
  30.2 1.2 constant_dynamic-slice_fusion.2
  31.4 2.8 collective-permute-start.9
  35.8 11.7 %collective-permute-done.9.refs_6_ = bf16[1024,256]{1,0:T(8,128)(2,1)S(1)} collective-permute-done((bf16[1024,256]{1,0:T(8,128)(2,1)}, bf16[1024,256]{1,0:T(8,128)(2,1)S(1)}, u32[]{:S(2)}, u32[]{:S(2)}) %collective-permute-start.9) | collective-permute-done | bytes 524320 | tf_op jit(solution)/shard_map/ppermute | solution.py:157
  47.5 9.7 %collective-permute-done.7.refs_4_ = bf16[1024,256]{1,0:T(8,128)(2,1)S(1)} collective-permute-done((bf16[1024,256]{1,0:T(8,128)(2,1)}, bf16[1024,256]{1,0:T(8,128)(2,1)S(1)}, u32[]{:S(2)}, u32[]{:S(2)}) %collective-permute-start.7) | collective-permute-done | bytes 524320 | tf_op jit(solution)/shard_map/ppermute | solution.py:157
  57.7 1.9 maximum_select_fusion
  59.7 1.0 fusion.32
  60.7 1.7 collective-permute-start.23
  62.4 13.0 %all-gather.1 = f32[8,4,128]{2,1,0:T(4,128)S(1)} all-gather(f32[1,4,128]{2,1,0:T(4,128)S(1)} %bitcast.177), channel_id=2, replica_groups=mesh['ctx'=4,'exp'=8] {'exp'}, dimensions={0}, use_global_device_ids=true | all-gather | bytes 18432 | tf_op jit(solution)/shard_map/all_gather | solution.py:200
  75.5 1.2 collective-permute-start.22
  77.3 4.0 %partial_product.6 = bf16[1024,256]{1,0:T(8,128)(2,1)} custom-call(s32[1]{0:T(128)} %bitcast.place, bf16[1024,256]{1,0:T(8,128)(2,1)S(1)} %get-tuple-element.24.refs_0_, bf16[1024,256]{1,0:T(8,128)(2,1)S(1)} %collective-permute-done.4.refs_1_, bf16[1024,256]{1,0:T(8,128)(2,1)S(1)} %collective-permute-done.5.refs_2_, ...), custom_call_target="tpu_custom_call" | custom-call | flops 1073741824 | bytes 5767168 | tf_op jit(solution)/shard_map/partial_product/pallas_call | solution.py:107
  81.3 4.3 %collective-permute-start.15 = (bf16[1024,256]{1,0:T(8,128)(2,1)}, bf16[1024,256]{1,0:T(8,128)(2,1)}, u32[]{:S(2)}, u32[]{:S(2)}) collective-permute-start(bf16[1024,256]{1,0:T(8,128)(2,1)} %partial_product.6), channel_id=1, source_target_pairs={{0,2},{1,3},{6,4},{7,5},{8,10},{9,11},{14,12},{15,13},{16,18},{17,... | collective-permute-start | bytes 1572872 | tf_op jit(solution)/shard_map/ppermute | solution.py:167
  85.6 1.2 pad_maximum_fusion
  86.8 1.7 collective-permute-start.13
  91.0 1.2 reduce_window_sum.13
  92.2 1.3 reduce_window_sum.14
  94.8 1.2 collective-permute-start.12
  96.1 1.5 collective-permute-start.11
  97.6 2.1 add_convert_fusion.15
  99.8 1.5 collective-permute-start.16
  102.0 1.6 collective-permute-start.20
  103.6 1.0 copy-done.1
  104.6 1.0 copy-done.4
  105.6 2.9 %partial_product.8 = bf16[1024,256]{1,0:T(8,128)(2,1)S(1)} custom-call(s32[1]{0:T(128)} %bitcast.place, bf16[1024,256]{1,0:T(8,128)(2,1)S(1)} %get-tuple-element.24.refs_0_, bf16[1024,256]{1,0:T(8,128)(2,1)S(1)} %collective-permute-done.4.refs_1_, bf16[1024,256]{1,0:T(8,128)(2,1)S(1)} %collective-permute-done.5.refs_2_, bf16[1024,256]{1,0:T(8,128)(2,1)S(1)} %copy-done.4, ...), custom_call_target="tpu_custom_call" | custom-call | flops 1073741824 | bytes 5767168 | tf_op jit(solution)/shard_map/partial_product/pallas_call | solution.py:107
  108.6 0.8 copy-done.6
  109.9 4.2 %collective-permute-done.12.refs_10_ = bf16[512,512]{1,0:T(8,128)(2,1)} collective-permute-done((bf16[512,512]{1,0:T(8,128)(2,1)}, bf16[512,512]{1,0:T(8,128)(2,1)}, u32[]{:S(2)}, u32[]{:S(2)}) %collective-permute-start.12) | collective-permute-done | bytes 524320 | tf_op jit(solution)/shard_map/ppermute | solution.py:157
  114.2 1.5 collective-permute-start.18
  115.7 1.3 collective-permute-start.24
  117.0 1.0 copy-done.2
  118.0 1.0 copy-done.5
  119.1 0.9 copy-done.17
  120.0 5.2 %partial_product.5 = bf16[1024,512]{1,0:T(8,128)(2,1)} custom-call(s32[1]{0:T(128)} %bitcast.place, bf16[1024,256]{1,0:T(8,128)(2,1)S(1)} %get-tuple-element.24.refs_0_, bf16[1024,256]{1,0:T(8,128)(2,1)S(1)} %collective-permute-done.4.refs_1_, bf16[1024,256]{1,0:T(8,128)(2,1)S(1)} %collective-permute-done.5.refs_2_, bf16[1024,256]{1,0:T(8,128)(2,1)S(1)} %copy-done.5, ...), custom_call_target="tpu_custom_call" | custom-call | flops 2147483648 | bytes 7340032 | tf_op jit(solution)/shard_map/partial_product/pallas_call | solution.py:107
  125.3 1.7 fusion.33
  127.0 1.3 collective-permute-start.27
  128.6 6.2 %collective-permute-done.19.refs_10_ = bf16[512,512]{1,0:T(8,128)(2,1)S(1)} collective-permute-done((bf16[512,512]{1,0:T(8,128)(2,1)}, bf16[512,512]{1,0:T(8,128)(2,1)S(1)}, u32[]{:S(2)}, u32[]{:S(2)}) %collective-permute-start.19) | collective-permute-done | bytes 524320 | tf_op jit(solution)/shard_map/ppermute | solution.py:157
  134.9 1.7 collective-permute-start.32
  136.6 1.2 collective-permute-start.31
  137.8 4.8 %partial_product.7 = bf16[1024,512]{1,0:T(8,128)(2,1)} custom-call(s32[1]{0:T(128)} %bitcast.place, bf16[1024,256]{1,0:T(8,128)(2,1)S(1)} %get-tuple-element.24.refs_0_, bf16[1024,256]{1,0:T(8,128)(2,1)S(1)} %collective-permute-done.4.refs_1_, bf16[1024,256]{1,0:T(8,128)(2,1)S(1)} %collective-permute-done.5.refs_2_, bf16[1024,256]{1,0:T(8,128)(2,1)S(1)} %copy-done.5, ...), custom_call_target="tpu_custom_call" | custom-call | flops 2147483648 | bytes 7340032 | tf_op jit(solution)/shard_map/partial_product/pallas_call | solution.py:107
  144.0 6.7 %collective-permute-done.17 = bf16[1024,256]{1,0:T(8,128)(2,1)S(1)} collective-permute-done((bf16[1024,256]{1,0:T(8,128)(2,1)S(1)}, bf16[1024,256]{1,0:T(8,128)(2,1)S(1)}, u32[]{:S(2)}, u32[]{:S(2)}) %collective-permute-start.17) | collective-permute-done | bytes 524320 | tf_op jit(solution)/shard_map/ppermute | solution.py:167
  151.7 1.4 broadcast_select_fusion.12
  153.8 14.9 %collective-permute-start.29 = (bf16[1024,256]{1,0:T(8,128)(2,1)S(1)}, bf16[1024,256]{1,0:T(8,128)(2,1)S(1)}, u32[]{:S(2)}, u32[]{:S(2)}) collective-permute-start(bf16[1024,256]{1,0:T(8,128)(2,1)S(1)} %get-tuple-element.59), channel_id=1, source_target_pairs={{0,2},{1,3},{2,0},{3,1},{4,6},{5,7},{6,4},{7,5},{8,10},{9,11},{10,... | collective-permute-start | bytes 1572872 | tf_op jit(solution)/shard_map/ppermute | solution.py:167
  168.9 0.8 copy-done.32
  169.7 4.6 %partial_product.9 = bf16[1024,512]{1,0:T(8,128)(2,1)} custom-call(s32[1]{0:T(128)} %bitcast.place, bf16[1024,256]{1,0:T(8,128)(2,1)S(1)} %get-tuple-element.24.refs_0_, bf16[1024,256]{1,0:T(8,128)(2,1)S(1)} %collective-permute-done.4.refs_1_, bf16[1024,256]{1,0:T(8,128)(2,1)S(1)} %collective-permute-done.5.refs_2_, bf16[1024,256]{1,0:T(8,128)(2,1)S(1)} %copy-done.5, ...), custom_call_target="tpu_custom_call" | custom-call | flops 2147483648 | bytes 7340032 | tf_op jit(solution)/shard_map/partial_product/pallas_call | solution.py:107
  175.0 2.4 collective-permute-start.26
  177.4 2.0 collective-permute-done.29
  179.9 10.3 %collective-permute-done.26 = bf16[1024,256]{1,0:T(8,128)(2,1)S(1)} collective-permute-done((bf16[1024,256]{1,0:T(8,128)(2,1)S(1)}, bf16[1024,256]{1,0:T(8,128)(2,1)S(1)}, u32[]{:S(2)}, u32[]{:S(2)}) %collective-permute-start.26) | collective-permute-done | bytes 524320 | tf_op jit(solution)/shard_map/ppermute | solution.py:167
  191.0 1.0 collective-permute-start.37
  193.8 1.3 collective-permute-start.38
  195.6 24.4 %collective-permute-start.36 = (bf16[1024,256]{1,0:T(8,128)(2,1)S(1)}, bf16[1024,256]{1,0:T(8,128)(2,1)S(1)}, u32[]{:S(2)}, u32[]{:S(2)}) collective-permute-start(bf16[1024,256]{1,0:T(8,128)(2,1)S(1)} %get-tuple-element.52), channel_id=1, source_target_pairs={{0,2},{1,3},{2,0},{3,1},{4,6},{5,7},{6,4},{7,5},{8,10},{9,11},{10,... | collective-permute-start | bytes 1572872 | tf_op jit(solution)/shard_map/ppermute | solution.py:167
  220.1 1.1 collective-permute-done.38
  221.7 11.2 %collective-permute-done.36 = bf16[1024,256]{1,0:T(8,128)(2,1)S(1)} collective-permute-done((bf16[1024,256]{1,0:T(8,128)(2,1)S(1)}, bf16[1024,256]{1,0:T(8,128)(2,1)S(1)}, u32[]{:S(2)}, u32[]{:S(2)}) %collective-permute-start.36) | collective-permute-done | bytes 524320 | tf_op jit(solution)/shard_map/ppermute | solution.py:167
  233.5 9.4 %collective-permute-done.34 = bf16[1024,256]{1,0:T(8,128)(2,1)S(1)} collective-permute-done((bf16[1024,256]{1,0:T(8,128)(2,1)S(1)}, bf16[1024,256]{1,0:T(8,128)(2,1)S(1)}, u32[]{:S(2)}, u32[]{:S(2)}) %collective-permute-start.34) | collective-permute-done | bytes 524320 | tf_op jit(solution)/shard_map/ppermute | solution.py:167
  245.3 1.3 collective-permute-start.42
  246.8 1.3 collective-permute-start.40
  248.2 22.8 %collective-permute-done.42 = bf16[1024,256]{1,0:T(8,128)(2,1)S(1)} collective-permute-done((bf16[1024,256]{1,0:T(8,128)(2,1)S(1)}, bf16[1024,256]{1,0:T(8,128)(2,1)S(1)}, u32[]{:S(2)}, u32[]{:S(2)}) %collective-permute-start.42) | collective-permute-done | bytes 524320 | tf_op jit(solution)/shard_map/ppermute | solution.py:167
  271.0 9.5 %collective-permute-done.40 = bf16[1024,256]{1,0:T(8,128)(2,1)S(1)} collective-permute-done((bf16[1024,256]{1,0:T(8,128)(2,1)S(1)}, bf16[1024,256]{1,0:T(8,128)(2,1)S(1)}, u32[]{:S(2)}, u32[]{:S(2)}) %collective-permute-start.40) | collective-permute-done | bytes 524320 | tf_op jit(solution)/shard_map/ppermute | solution.py:167
  282.0 0.9 collective-permute-done.49
  284.0 2.2 broadcast_select_fusion
  (203 shorter events, 23.2 us)
Async XLA Ops:
  0.0 13.0 %copy-start.28 = (f32[256]{0:T(256)S(1)}, f32[256]{0:T(256)}, u32[]{:S(2)}) copy-start(f32[256]{0:T(256)} %param.17) | copy-start | bytes 3076
  0.0 13.2 %copy-start.8 = (bf16[256,4096]{1,0:T(8,128)(2,1)S(1)}, bf16[256,4096]{1,0:T(8,128)(2,1)}, u32[]{:S(2)}) copy-start(bf16[256,4096]{1,0:T(8,128)(2,1)} %out_grad.1) | copy-start | bytes 6291460
  3.3 3.0 %collective-permute-start = (bf16[256,2048]{1,0:T(8,128)(2,1)}, bf16[256,2048]{1,0:T(8,128)(2,1)S(1)}, u32[]{:S(2)}, u32[]{:S(2)}) collective-permute-start(bf16[256,2048]{1,0:T(8,128)(2,1)} %get-tuple-element.47), channel_id=1, source_target_pairs={{0,1},{1,0},{2,3},{3,2},{4,5},{5,4},{6,7},{7,6},{8,9},{9,8},{10,11... | collective-permute-start | bytes 3145736 | tf_op jit(solution)/shard_map/ppermute | solution.py:154
  4.8 52.9 %collective-permute-start.14 = (bf16[128,2048]{1,0:T(8,128)(2,1)}, bf16[128,2048]{1,0:T(8,128)(2,1)}, u32[]{:S(2)}, u32[]{:S(2)}) collective-permute-start(bf16[128,2048]{1,0:T(8,128)(2,1)} %get-tuple-element.66), channel_id=1, source_target_pairs={{0,1},{1,0},{2,3},{3,2},{4,5},{5,4},{6,7},{7,6},{8,9},{9,8},{10,11... | collective-permute-start | bytes 1572872 | tf_op jit(solution)/shard_map/ppermute | solution.py:154
  8.4 21.8 %copy-start.9 = (bf16[512,256]{1,0:T(8,128)(2,1)}, bf16[512,256]{1,0:T(8,128)(2,1)S(1)}, u32[]{:S(2)}) copy-start(bf16[512,256]{1,0:T(8,128)(2,1)S(1)} %get-tuple-element.32.refs_8_) | copy-start | bytes 786436
  8.4 21.8 %collective-permute-start.3 = (bf16[512,256]{1,0:T(8,128)(2,1)S(1)}, bf16[512,256]{1,0:T(8,128)(2,1)S(1)}, u32[]{:S(2)}, u32[]{:S(2)}) collective-permute-start(bf16[512,256]{1,0:T(8,128)(2,1)S(1)} %get-tuple-element.32.refs_8_), channel_id=1, source_target_pairs={{0,24},{8,16},{16,8},{24,0},{1,25},{9,17},{17,9},{25,1},{2,26},{10... | collective-permute-start | bytes 786440 | tf_op jit(solution)/shard_map/ppermute | solution.py:157
  12.3 18.0 %collective-permute-start.2 = (bf16[512,256]{1,0:T(8,128)(2,1)S(1)}, bf16[512,256]{1,0:T(8,128)(2,1)}, u32[]{:S(2)}, u32[]{:S(2)}) collective-permute-start(bf16[512,256]{1,0:T(8,128)(2,1)S(1)} %get-tuple-element.32.refs_8_), channel_id=1, source_target_pairs={{0,16},{8,24},{16,0},{24,8},{1,17},{9,25},{17,1},{25,9},{2,18},{10... | collective-permute-start | bytes 786440 | tf_op jit(solution)/shard_map/ppermute | solution.py:157
  12.8 17.5 %collective-permute-start.1 = (bf16[512,256]{1,0:T(8,128)(2,1)S(1)}, bf16[512,256]{1,0:T(8,128)(2,1)}, u32[]{:S(2)}, u32[]{:S(2)}) collective-permute-start(bf16[512,256]{1,0:T(8,128)(2,1)S(1)} %get-tuple-element.32.refs_8_), channel_id=1, source_target_pairs={{0,8},{8,0},{16,24},{24,16},{1,9},{9,1},{17,25},{25,17},{2,10},{10... | collective-permute-start | bytes 786440 | tf_op jit(solution)/shard_map/ppermute | solution.py:157
  31.4 16.0 %collective-permute-start.9 = (bf16[1024,256]{1,0:T(8,128)(2,1)}, bf16[1024,256]{1,0:T(8,128)(2,1)S(1)}, u32[]{:S(2)}, u32[]{:S(2)}) collective-permute-start(bf16[1024,256]{1,0:T(8,128)(2,1)} %get-tuple-element.42), channel_id=1, source_target_pairs={{0,24},{8,16},{16,8},{24,0},{1,25},{9,17},{17,9},{25,1},{2,26},{10... | collective-permute-start | bytes 1572872 | tf_op jit(solution)/shard_map/ppermute | solution.py:157
  34.3 22.9 %collective-permute-start.7 = (bf16[1024,256]{1,0:T(8,128)(2,1)}, bf16[1024,256]{1,0:T(8,128)(2,1)S(1)}, u32[]{:S(2)}, u32[]{:S(2)}) collective-permute-start(bf16[1024,256]{1,0:T(8,128)(2,1)} %get-tuple-element.43), channel_id=1, source_target_pairs={{0,16},{8,24},{16,0},{24,8},{1,17},{9,25},{17,1},{25,9},{2,18},{10... | collective-permute-start | bytes 1572872 | tf_op jit(solution)/shard_map/ppermute | solution.py:157
  34.8 22.6 %collective-permute-start.5 = (bf16[1024,256]{1,0:T(8,128)(2,1)}, bf16[1024,256]{1,0:T(8,128)(2,1)S(1)}, u32[]{:S(2)}, u32[]{:S(2)}) collective-permute-start(bf16[1024,256]{1,0:T(8,128)(2,1)} %get-tuple-element.44), channel_id=1, source_target_pairs={{0,8},{8,0},{16,24},{24,16},{1,9},{9,1},{17,25},{25,17},{2,10},{10... | collective-permute-start | bytes 1572872 | tf_op jit(solution)/shard_map/ppermute | solution.py:157
  35.0 42.2 %copy-start.10 = (bf16[512,256]{1,0:T(8,128)(2,1)S(1)}, bf16[512,256]{1,0:T(8,128)(2,1)}, u32[]{:S(2)}) copy-start(bf16[512,256]{1,0:T(8,128)(2,1)} %copy-done.9) | copy-start | bytes 786436
  35.7 53.4 %copy-start.27 = (f32[2]{0:T(128)}, f32[2]{0:T(128)S(1)}, u32[]{:S(2)}) copy-start(f32[2]{0:T(128)S(1)} %add_convert_fusion.16) | copy-start | bytes 28
  35.7 39.8 %collective-permute-start.4 = (bf16[1024,256]{1,0:T(8,128)(2,1)S(1)}, bf16[1024,256]{1,0:T(8,128)(2,1)S(1)}, u32[]{:S(2)}, u32[]{:S(2)}) collective-permute-start(bf16[1024,256]{1,0:T(8,128)(2,1)S(1)} %get-tuple-element.24.refs_0_), channel_id=1, source_target_pairs={{0,1},{1,0},{2,3},{3,2},{4,5},{5,4},{6,7},{7,6},{8,9},{9,8},{10,11... | collective-permute-start | bytes 1572872 | tf_op jit(solution)/shard_map/ppermute | solution.py:154
  47.4 29.8 %copy-start.14 = (bf16[512,256]{1,0:T(8,128)(2,1)S(1)}, bf16[512,256]{1,0:T(8,128)(2,1)}, u32[]{:S(2)}) copy-start(bf16[512,256]{1,0:T(8,128)(2,1)} %copy-done.13) | copy-start | bytes 786436
  47.4 29.2 %collective-permute-start.10 = (bf16[1024,256]{1,0:T(8,128)(2,1)S(1)}, bf16[1024,256]{1,0:T(8,128)(2,1)S(1)}, u32[]{:S(2)}, u32[]{:S(2)}) collective-permute-start(bf16[1024,256]{1,0:T(8,128)(2,1)S(1)} %collective-permute-done.9.refs_6_), channel_id=1, source_target_pairs={{0,1},{1,0},{2,3},{3,2},{4,5},{5,4},{6,7},{7,6},{8,9},{9,8},{10,11... | collective-permute-start | bytes 1572872 | tf_op jit(solution)/shard_map/ppermute | solution.py:154
  57.2 20.0 %collective-permute-start.8 = (bf16[1024,256]{1,0:T(8,128)(2,1)S(1)}, bf16[1024,256]{1,0:T(8,128)(2,1)S(1)}, u32[]{:S(2)}, u32[]{:S(2)}) collective-permute-start(bf16[1024,256]{1,0:T(8,128)(2,1)S(1)} %collective-permute-done.7.refs_4_), channel_id=1, source_target_pairs={{0,1},{1,0},{2,3},{3,2},{4,5},{5,4},{6,7},{7,6},{8,9},{9,8},{10,11... | collective-permute-start | bytes 1572872 | tf_op jit(solution)/shard_map/ppermute | solution.py:154
  57.4 19.8 %collective-permute-start.6 = (bf16[1024,256]{1,0:T(8,128)(2,1)S(1)}, bf16[1024,256]{1,0:T(8,128)(2,1)S(1)}, u32[]{:S(2)}, u32[]{:S(2)}) collective-permute-start(bf16[1024,256]{1,0:T(8,128)(2,1)S(1)} %collective-permute-done.5.refs_2_), channel_id=1, source_target_pairs={{0,1},{1,0},{2,3},{3,2},{4,5},{5,4},{6,7},{7,6},{8,9},{9,8},{10,11... | collective-permute-start | bytes 1572872 | tf_op jit(solution)/shard_map/ppermute | solution.py:154
  59.7 25.9 %copy-start.18 = (bf16[256,2048]{1,0:T(8,128)(2,1)S(1)}, bf16[256,2048]{1,0:T(8,128)(2,1)}, u32[]{:S(2)}) copy-start(bf16[256,2048]{1,0:T(8,128)(2,1)} %get-tuple-element.46) | copy-start | bytes 3145732
  59.7 25.9 %copy-start.22 = (bf16[256,2048]{1,0:T(8,128)(2,1)S(1)}, bf16[256,2048]{1,0:T(8,128)(2,1)}, u32[]{:S(2)}) copy-start(bf16[256,2048]{1,0:T(8,128)(2,1)} %copy-done.21) | copy-start | bytes 3145732
  60.7 34.2 %collective-permute-start.23 = (bf16[512,256]{1,0:T(8,128)(2,1)S(1)}, bf16[512,256]{1,0:T(8,128)(2,1)}, u32[]{:S(2)}, u32[]{:S(2)}) collective-permute-start(bf16[512,256]{1,0:T(8,128)(2,1)S(1)} %get-tuple-element.40.refs_8_), channel_id=1, source_target_pairs={{0,24},{8,16},{16,8},{24,0},{1,25},{9,17},{17,9},{25,1},{2,26},{10... | collective-permute-start | bytes 786440 | tf_op jit(solution)/shard_map/ppermute | solution.py:157
  75.5 24.3 %collective-permute-start.22 = (bf16[512,256]{1,0:T(8,128)(2,1)S(1)}, bf16[512,256]{1,0:T(8,128)(2,1)}, u32[]{:S(2)}, u32[]{:S(2)}) collective-permute-start(bf16[512,256]{1,0:T(8,128)(2,1)S(1)} %get-tuple-element.40.refs_8_), channel_id=1, source_target_pairs={{0,16},{8,24},{16,0},{24,8},{1,17},{9,25},{17,1},{25,9},{2,18},{10... | collective-permute-start | bytes 786440 | tf_op jit(solution)/shard_map/ppermute | solution.py:157
  76.7 25.3 %collective-permute-start.21 = (bf16[512,256]{1,0:T(8,128)(2,1)S(1)}, bf16[512,256]{1,0:T(8,128)(2,1)}, u32[]{:S(2)}, u32[]{:S(2)}) collective-permute-start(bf16[512,256]{1,0:T(8,128)(2,1)S(1)} %get-tuple-element.40.refs_8_), channel_id=1, source_target_pairs={{0,8},{8,0},{16,24},{24,16},{1,9},{9,1},{17,25},{25,17},{2,10},{10... | collective-permute-start | bytes 786440 | tf_op jit(solution)/shard_map/ppermute | solution.py:157
  81.3 14.9 %collective-permute-start.15 = (bf16[1024,256]{1,0:T(8,128)(2,1)}, bf16[1024,256]{1,0:T(8,128)(2,1)}, u32[]{:S(2)}, u32[]{:S(2)}) collective-permute-start(bf16[1024,256]{1,0:T(8,128)(2,1)} %partial_product.6), channel_id=1, source_target_pairs={{0,2},{1,3},{6,4},{7,5},{8,10},{9,11},{14,12},{15,13},{16,18},{17,... | collective-permute-start | bytes 1572872 | tf_op jit(solution)/shard_map/ppermute | solution.py:167
  86.8 22.6 %collective-permute-start.13 = (bf16[512,512]{1,0:T(8,128)(2,1)}, bf16[512,512]{1,0:T(8,128)(2,1)}, u32[]{:S(2)}, u32[]{:S(2)}) collective-permute-start(bf16[512,512]{1,0:T(8,128)(2,1)} %get-tuple-element.38.refs_8_), channel_id=1, source_target_pairs={{0,24},{8,16},{16,8},{24,0},{1,25},{9,17},{17,9},{25,1},{2,26},{10... | collective-permute-start | bytes 1572872 | tf_op jit(solution)/shard_map/ppermute | solution.py:157
  94.8 19.3 %collective-permute-start.12 = (bf16[512,512]{1,0:T(8,128)(2,1)}, bf16[512,512]{1,0:T(8,128)(2,1)}, u32[]{:S(2)}, u32[]{:S(2)}) collective-permute-start(bf16[512,512]{1,0:T(8,128)(2,1)} %get-tuple-element.38.refs_8_), channel_id=1, source_target_pairs={{0,16},{8,24},{16,0},{24,8},{1,17},{9,25},{17,1},{25,9},{2,18},{10... | collective-permute-start | bytes 1572872 | tf_op jit(solution)/shard_map/ppermute | solution.py:157
  96.1 19.5 %collective-permute-start.11 = (bf16[512,512]{1,0:T(8,128)(2,1)}, bf16[512,512]{1,0:T(8,128)(2,1)}, u32[]{:S(2)}, u32[]{:S(2)}) collective-permute-start(bf16[512,512]{1,0:T(8,128)(2,1)} %get-tuple-element.38.refs_8_), channel_id=1, source_target_pairs={{0,8},{8,0},{16,24},{24,16},{1,9},{9,1},{17,25},{25,17},{2,10},{10... | collective-permute-start | bytes 1572872 | tf_op jit(solution)/shard_map/ppermute | solution.py:157
  99.8 25.5 %collective-permute-start.16 = (bf16[1024,256]{1,0:T(8,128)(2,1)}, bf16[1024,256]{1,0:T(8,128)(2,1)}, u32[]{:S(2)}, u32[]{:S(2)}) collective-permute-start(bf16[1024,256]{1,0:T(8,128)(2,1)} %add_convert_fusion.15), channel_id=1, source_target_pairs={{2,4},{3,5},{4,2},{5,3},{10,12},{11,13},{12,10},{13,11},{18,20},{1... | collective-permute-start | bytes 1572872 | tf_op jit(solution)/shard_map/ppermute | solution.py:167
  102.0 26.3 %collective-permute-start.20 = (bf16[512,512]{1,0:T(8,128)(2,1)}, bf16[512,512]{1,0:T(8,128)(2,1)}, u32[]{:S(2)}, u32[]{:S(2)}) collective-permute-start(bf16[512,512]{1,0:T(8,128)(2,1)} %get-tuple-element.39.refs_8_), channel_id=1, source_target_pairs={{0,24},{8,16},{16,8},{24,0},{1,25},{9,17},{17,9},{25,1},{2,26},{10... | collective-permute-start | bytes 1572872 | tf_op jit(solution)/shard_map/ppermute | solution.py:157
  109.4 25.5 %collective-permute-start.19 = (bf16[512,512]{1,0:T(8,128)(2,1)}, bf16[512,512]{1,0:T(8,128)(2,1)S(1)}, u32[]{:S(2)}, u32[]{:S(2)}) collective-permute-start(bf16[512,512]{1,0:T(8,128)(2,1)} %get-tuple-element.39.refs_8_), channel_id=1, source_target_pairs={{0,16},{8,24},{16,0},{24,8},{1,17},{9,25},{17,1},{25,9},{2,18},{10... | collective-permute-start | bytes 1572872 | tf_op jit(solution)/shard_map/ppermute | solution.py:157
  114.2 22.4 %collective-permute-start.18 = (bf16[512,512]{1,0:T(8,128)(2,1)}, bf16[512,512]{1,0:T(8,128)(2,1)S(1)}, u32[]{:S(2)}, u32[]{:S(2)}) collective-permute-start(bf16[512,512]{1,0:T(8,128)(2,1)} %get-tuple-element.39.refs_8_), channel_id=1, source_target_pairs={{0,8},{8,0},{16,24},{24,16},{1,9},{9,1},{17,25},{25,17},{2,10},{10... | collective-permute-start | bytes 1572872 | tf_op jit(solution)/shard_map/ppermute | solution.py:157
  115.7 26.9 %collective-permute-start.24 = (bf16[1024,256]{1,0:T(8,128)(2,1)}, bf16[1024,256]{1,0:T(8,128)(2,1)S(1)}, u32[]{:S(2)}, u32[]{:S(2)}) collective-permute-start(bf16[1024,256]{1,0:T(8,128)(2,1)} %copy-done.6), channel_id=1, source_target_pairs={{0,2},{1,3},{6,4},{7,5},{8,10},{9,11},{14,12},{15,13},{16,18},{17,... | collective-permute-start | bytes 1572872 | tf_op jit(solution)/shard_map/ppermute | solution.py:167
  120.0 14.8 %copy-start.11 = (bf16[512,512]{1,0:T(8,128)(2,1)S(1)}, bf16[512,512]{1,0:T(8,128)(2,1)}, u32[]{:S(2)}) copy-start(bf16[512,512]{1,0:T(8,128)(2,1)} %get-tuple-element.37.refs_8_) | copy-start | bytes 1572868
  120.0 17.8 %copy-start.12 = (bf16[512,512]{1,0:T(8,128)(2,1)S(1)}, bf16[512,512]{1,0:T(8,128)(2,1)}, u32[]{:S(2)}) copy-start(bf16[512,512]{1,0:T(8,128)(2,1)} %get-tuple-element.39.refs_8_) | copy-start | bytes 1572868
  120.0 17.8 %copy-start.16 = (bf16[256,512]{1,0:T(8,128)(2,1)S(1)}, bf16[256,512]{1,0:T(8,128)(2,1)}, u32[]{:S(2)}) copy-start(bf16[256,512]{1,0:T(8,128)(2,1)} %get-tuple-element.57.refs_12_) | copy-start | bytes 786436
  127.0 16.3 %collective-permute-start.27 = (bf16[1024,256]{1,0:T(8,128)(2,1)S(1)}, bf16[1024,256]{1,0:T(8,128)(2,1)S(1)}, u32[]{:S(2)}, u32[]{:S(2)}) collective-permute-start(bf16[1024,256]{1,0:T(8,128)(2,1)S(1)} %get-tuple-element.61), channel_id=1, source_target_pairs={{0,2},{1,3},{6,4},{7,5},{8,10},{9,11},{14,12},{15,13},{16,18},{17,... | collective-permute-start | bytes 1572872 | tf_op jit(solution)/shard_map/ppermute | solution.py:167
  128.3 22.4 %collective-permute-start.17 = (bf16[1024,256]{1,0:T(8,128)(2,1)S(1)}, bf16[1024,256]{1,0:T(8,128)(2,1)S(1)}, u32[]{:S(2)}, u32[]{:S(2)}) collective-permute-start(bf16[1024,256]{1,0:T(8,128)(2,1)S(1)} %get-tuple-element.62), channel_id=1, source_target_pairs={{0,2},{1,3},{2,0},{3,1},{4,6},{5,7},{6,4},{7,5},{8,10},{9,11},{10,... | collective-permute-start | bytes 1572872 | tf_op jit(solution)/shard_map/ppermute | solution.py:167
  134.9 34.0 %collective-permute-start.32 = (bf16[512,512]{1,0:T(8,128)(2,1)S(1)}, bf16[512,512]{1,0:T(8,128)(2,1)S(1)}, u32[]{:S(2)}, u32[]{:S(2)}) collective-permute-start(bf16[512,512]{1,0:T(8,128)(2,1)S(1)} %copy-done.11), channel_id=1, source_target_pairs={{0,24},{8,16},{16,8},{24,0},{1,25},{9,17},{17,9},{25,1},{2,26},{10... | collective-permute-start | bytes 1572872 | tf_op jit(solution)/shard_map/ppermute | solution.py:157
  136.6 32.3 %collective-permute-start.31 = (bf16[512,512]{1,0:T(8,128)(2,1)S(1)}, bf16[512,512]{1,0:T(8,128)(2,1)S(1)}, u32[]{:S(2)}, u32[]{:S(2)}) collective-permute-start(bf16[512,512]{1,0:T(8,128)(2,1)S(1)} %copy-done.11), channel_id=1, source_target_pairs={{0,16},{8,24},{16,0},{24,8},{1,17},{9,25},{17,1},{25,9},{2,18},{10... | collective-permute-start | bytes 1572872 | tf_op jit(solution)/shard_map/ppermute | solution.py:157
  137.8 12.9 %copy-start.23 = (bf16[1024,512]{1,0:T(8,128)(2,1)S(1)}, bf16[1024,512]{1,0:T(8,128)(2,1)}, u32[]{:S(2)}) copy-start(bf16[1024,512]{1,0:T(8,128)(2,1)} %partial_product.5) | copy-start | bytes 3145732
  142.6 26.3 %collective-permute-start.30 = (bf16[512,512]{1,0:T(8,128)(2,1)S(1)}, bf16[512,512]{1,0:T(8,128)(2,1)S(1)}, u32[]{:S(2)}, u32[]{:S(2)}) collective-permute-start(bf16[512,512]{1,0:T(8,128)(2,1)S(1)} %copy-done.11), channel_id=1, source_target_pairs={{0,8},{8,0},{16,24},{24,16},{1,9},{9,1},{17,25},{25,17},{2,10},{10... | collective-permute-start | bytes 1572872 | tf_op jit(solution)/shard_map/ppermute | solution.py:157
  143.3 10.1 %collective-permute-start.25 = (bf16[1024,256]{1,0:T(8,128)(2,1)S(1)}, bf16[1024,256]{1,0:T(8,128)(2,1)S(1)}, u32[]{:S(2)}, u32[]{:S(2)}) collective-permute-start(bf16[1024,256]{1,0:T(8,128)(2,1)S(1)} %add_convert_fusion.13), channel_id=1, source_target_pairs={{2,4},{3,5},{4,2},{5,3},{10,12},{11,13},{12,10},{13,11},{18,20},{1... | collective-permute-start | bytes 1572872 | tf_op jit(solution)/shard_map/ppermute | solution.py:167
  151.0 2.4 collective-permute-start.28
  153.1 16.6 %copy-start.15 = (bf16[256,512]{1,0:T(8,128)(2,1)S(1)}, bf16[256,512]{1,0:T(8,128)(2,1)}, u32[]{:S(2)}) copy-start(bf16[256,512]{1,0:T(8,128)(2,1)} %get-tuple-element.56.refs_12_) | copy-start | bytes 786436
  153.8 25.6 %collective-permute-start.29 = (bf16[1024,256]{1,0:T(8,128)(2,1)S(1)}, bf16[1024,256]{1,0:T(8,128)(2,1)S(1)}, u32[]{:S(2)}, u32[]{:S(2)}) collective-permute-start(bf16[1024,256]{1,0:T(8,128)(2,1)S(1)} %get-tuple-element.59), channel_id=1, source_target_pairs={{0,2},{1,3},{2,0},{3,1},{4,6},{5,7},{6,4},{7,5},{8,10},{9,11},{10,... | collective-permute-start | bytes 1572872 | tf_op jit(solution)/shard_map/ppermute | solution.py:167
  168.8 6.2 %collective-permute-start.43 = (bf16[448,256]{1,0:T(8,128)(2,1)S(1)}, bf16[448,256]{1,0:T(8,128)(2,1)S(1)}, u32[]{:S(2)}, u32[]{:S(2)}) collective-permute-start(bf16[448,256]{1,0:T(8,128)(2,1)S(1)} %bitcast.170), channel_id=1, source_target_pairs={{0,1},{1,0},{2,3},{3,2},{4,5},{5,4},{6,7},{7,6},{8,9},{9,8},{10,11... | collective-permute-start | bytes 688136 | tf_op jit(solution)/shard_map/ppermute | solution.py:154
  174.3 20.9 %collective-permute-start.33 = (bf16[1024,256]{1,0:T(8,128)(2,1)S(1)}, bf16[1024,256]{1,0:T(8,128)(2,1)S(1)}, u32[]{:S(2)}, u32[]{:S(2)}) collective-permute-start(bf16[1024,256]{1,0:T(8,128)(2,1)S(1)} %get-tuple-element.54), channel_id=1, source_target_pairs={{2,4},{3,5},{4,2},{5,3},{10,12},{11,13},{12,10},{13,11},{18,20},{1... | collective-permute-start | bytes 1572872 | tf_op jit(solution)/shard_map/ppermute | solution.py:167
  175.0 15.2 %collective-permute-start.26 = (bf16[1024,256]{1,0:T(8,128)(2,1)S(1)}, bf16[1024,256]{1,0:T(8,128)(2,1)S(1)}, u32[]{:S(2)}, u32[]{:S(2)}) collective-permute-start(bf16[1024,256]{1,0:T(8,128)(2,1)S(1)} %get-tuple-element.60), channel_id=1, source_target_pairs={{0,2},{1,3},{2,0},{3,1},{4,6},{5,7},{6,4},{7,5},{8,10},{9,11},{10,... | collective-permute-start | bytes 1572872 | tf_op jit(solution)/shard_map/ppermute | solution.py:167
  191.0 2.6 collective-permute-start.37
  192.1 1.6 collective-permute-start.44
  192.2 2.9 %collective-permute-start.45 = (bf16[448,256]{1,0:T(8,128)(2,1)S(1)}, bf16[448,256]{1,0:T(8,128)(2,1)S(1)}, u32[]{:S(2)}, u32[]{:S(2)}) collective-permute-start(bf16[448,256]{1,0:T(8,128)(2,1)S(1)} %bitcast.171), channel_id=1, source_target_pairs={{0,1},{1,0},{2,3},{3,2},{4,5},{5,4},{6,7},{7,6},{8,9},{9,8},{10,11... | collective-permute-start | bytes 688136 | tf_op jit(solution)/shard_map/ppermute | solution.py:154
  192.7 2.4 collective-permute-start.35
  193.8 27.4 %collective-permute-start.38 = (bf16[1024,256]{1,0:T(8,128)(2,1)S(1)}, bf16[1024,256]{1,0:T(8,128)(2,1)S(1)}, u32[]{:S(2)}, u32[]{:S(2)}) collective-permute-start(bf16[1024,256]{1,0:T(8,128)(2,1)S(1)} %add_convert_fusion.4), channel_id=1, source_target_pairs={{2,0},{3,1},{4,6},{5,7},{10,8},{11,9},{12,14},{13,15},{18,16},{19,... | collective-permute-start | bytes 1572872 | tf_op jit(solution)/shard_map/ppermute | solution.py:167
  195.6 37.3 %collective-permute-start.36 = (bf16[1024,256]{1,0:T(8,128)(2,1)S(1)}, bf16[1024,256]{1,0:T(8,128)(2,1)S(1)}, u32[]{:S(2)}, u32[]{:S(2)}) collective-permute-start(bf16[1024,256]{1,0:T(8,128)(2,1)S(1)} %get-tuple-element.52), channel_id=1, source_target_pairs={{0,2},{1,3},{2,0},{3,1},{4,6},{5,7},{6,4},{7,5},{8,10},{9,11},{10,... | collective-permute-start | bytes 1572872 | tf_op jit(solution)/shard_map/ppermute | solution.py:167
  220.0 22.8 %collective-permute-start.34 = (bf16[1024,256]{1,0:T(8,128)(2,1)S(1)}, bf16[1024,256]{1,0:T(8,128)(2,1)S(1)}, u32[]{:S(2)}, u32[]{:S(2)}) collective-permute-start(bf16[1024,256]{1,0:T(8,128)(2,1)S(1)} %get-tuple-element.53), channel_id=1, source_target_pairs={{0,2},{1,3},{2,0},{3,1},{4,6},{5,7},{6,4},{7,5},{8,10},{9,11},{10,... | collective-permute-start | bytes 1572872 | tf_op jit(solution)/shard_map/ppermute | solution.py:167
  221.6 26.5 %collective-permute-start.48 = (bf16[448,256]{1,0:T(8,128)(2,1)S(1)}, bf16[448,256]{1,0:T(8,128)(2,1)S(1)}, u32[]{:S(2)}, u32[]{:S(2)}) collective-permute-start(bf16[448,256]{1,0:T(8,128)(2,1)S(1)} %bitcast.168), channel_id=1, source_target_pairs={{0,1},{1,0},{2,3},{3,2},{4,5},{5,4},{6,7},{7,6},{8,9},{9,8},{10,11... | collective-permute-start | bytes 688136 | tf_op jit(solution)/shard_map/ppermute | solution.py:154
  233.4 14.7 %collective-permute-start.47 = (bf16[448,256]{1,0:T(8,128)(2,1)S(1)}, bf16[448,256]{1,0:T(8,128)(2,1)S(1)}, u32[]{:S(2)}, u32[]{:S(2)}) collective-permute-start(bf16[448,256]{1,0:T(8,128)(2,1)S(1)} %bitcast.169), channel_id=1, source_target_pairs={{0,1},{1,0},{2,3},{3,2},{4,5},{5,4},{6,7},{7,6},{8,9},{9,8},{10,11... | collective-permute-start | bytes 688136 | tf_op jit(solution)/shard_map/ppermute | solution.py:154
  243.1 2.0 collective-permute-start.41
  243.8 2.8 collective-permute-start.39
  245.1 3.0 %collective-permute-start.46 = (bf16[448,256]{1,0:T(8,128)(2,1)S(1)}, bf16[448,256]{1,0:T(8,128)(2,1)S(1)}, u32[]{:S(2)}, u32[]{:S(2)}) collective-permute-start(bf16[448,256]{1,0:T(8,128)(2,1)S(1)} %bitcast.172), channel_id=1, source_target_pairs={{0,1},{1,0},{2,3},{3,2},{4,5},{5,4},{6,7},{7,6},{8,9},{9,8},{10,11... | collective-permute-start | bytes 688136 | tf_op jit(solution)/shard_map/ppermute | solution.py:154
  245.3 25.7 %collective-permute-start.42 = (bf16[1024,256]{1,0:T(8,128)(2,1)S(1)}, bf16[1024,256]{1,0:T(8,128)(2,1)S(1)}, u32[]{:S(2)}, u32[]{:S(2)}) collective-permute-start(bf16[1024,256]{1,0:T(8,128)(2,1)S(1)} %add_convert_fusion), channel_id=1, source_target_pairs={{2,0},{3,1},{4,6},{5,7},{10,8},{11,9},{12,14},{13,15},{18,16},{19,... | collective-permute-start | bytes 1572872 | tf_op jit(solution)/shard_map/ppermute | solution.py:167
  246.8 33.8 %collective-permute-start.40 = (bf16[1024,256]{1,0:T(8,128)(2,1)S(1)}, bf16[1024,256]{1,0:T(8,128)(2,1)S(1)}, u32[]{:S(2)}, u32[]{:S(2)}) collective-permute-start(bf16[1024,256]{1,0:T(8,128)(2,1)S(1)} %add_convert_fusion.2), channel_id=1, source_target_pairs={{2,0},{3,1},{4,6},{5,7},{10,8},{11,9},{12,14},{13,15},{18,16},{19,... | collective-permute-start | bytes 1572872 | tf_op jit(solution)/shard_map/ppermute | solution.py:167
  281.3 1.6 collective-permute-start.49
  281.5 1.8 collective-permute-start.50
  (20 other events, 86.0 us)

commit v3 on v2

--- a/solution.py
+++ b/solution.py
@@ -8,7 +8,8 @@
 from jax.sharding import PartitionSpec as P
 
 EXP_DEV = 1
-PIECES = 8
+GROUPS = ((1,), (1, 2), (2, 2), (2, 2), (2, 1, 1))
+UNITS = sum(map(sum, GROUPS))
 DELAY = 3
 VMEM_BYTES = 48 * 1024 * 1024
 
@@ -60,45 +61,44 @@
         turned[pl.ds(at, tile), :] = flat[:, pl.ds(at, tile)].T
 
 
-def conv_grad(out_grad, gate_in, conv_in, scan_grad, conv_weight, conv_bias, skip_scale):
+def conv_grad(part, parts, out_grad, gate_in, conv_in, scan_grad, taps_half, bias_half, skip):
     channels, length = out_grad.shape
-    block = min(128, channels)
+    block = channels // parts
     tile = min(512, length)
-    whole = pl.BlockSpec((block, length), lambda step: (step, 0))
+    whole = pl.BlockSpec((block, length), lambda step: (part, 0))
+    column = pl.BlockSpec((block, 1), lambda step: (part, 0))
     return pl.pallas_call(
         functools.partial(conv_kernel, tile),
-        grid=(channels // block,),
-        in_specs=[whole] * 4
-        + [
-            pl.BlockSpec((block, conv_weight.shape[0]), lambda step: (step, 0)),
-            pl.BlockSpec((block, 1), lambda step: (step, 0)),
-            pl.BlockSpec((block, 1), lambda step: (step, 0)),
-        ],
-        out_specs=pl.BlockSpec((length, block), lambda step: (0, step)),
-        out_shape=jax.ShapeDtypeStruct((length, channels), jnp.bfloat16),
+        grid=(1,),
+        in_specs=[whole] * 4 + [pl.BlockSpec((block, taps_half.shape[1]), lambda step: (part, 0)), column, column],
+        out_specs=pl.BlockSpec((length, block), lambda step: (0, 0)),
+        out_shape=jax.ShapeDtypeStruct((length, block), jnp.bfloat16),
         scratch_shapes=[pltpu.VMEM((block, length), jnp.bfloat16)],
         compiler_params=pltpu.CompilerParams(vmem_limit_bytes=VMEM_BYTES),
         cost_estimate=pl.CostEstimate(
-            flops=40 * channels * length, bytes_accessed=10 * channels * length, transcendentals=2 * channels * length
+            flops=40 * block * length, bytes_accessed=10 * block * length, transcendentals=2 * block * length
         ),
         name="conv_grad",
-    )(out_grad, gate_in, conv_in, scan_grad, 0.5 * conv_weight.T, 0.5 * conv_bias[:, None], skip_scale[:, None])
+    )(out_grad, gate_in, conv_in, scan_grad, taps_half, bias_half, skip)
 
 
 def matmul_kernel(lefts, rights, place, *refs):
     left_refs = refs[:lefts]
     right_refs = refs[lefts : lefts + rights]
     resid = refs[lefts + rights]
-    out = refs[lefts + rights + 1]
+    outs = refs[lefts + rights + 1 :]
     left = jnp.concatenate([ref[...] for ref in left_refs], axis=1)
     right = jnp.concatenate([ref[...] for ref in right_refs], axis=0)
     total = jnp.dot(left, right, preferred_element_type=jnp.float32)
     mine = pl.program_id(0) == place[0]
     total = total + jnp.where(mine, resid[...].astype(jnp.float32), 0.0)
-    out[...] = total.astype(out.dtype)
-
-
-def matmul(lefts, rights, resid, place):
+    at = 0
+    for out in outs:
+        out[...] = total[:, at : at + out.shape[1]].astype(out.dtype)
+        at += out.shape[1]
+
+
+def matmul(lefts, rights, resid, place, widths):
     tokens, depth = lefts[0].shape
     wide, width = rights[0].shape
     tile = resid.shape[0]
@@ -112,9 +112,9 @@
             in_specs=[pl.BlockSpec((tile, depth), lambda step, place: (step, 0))] * len(lefts)
             + [pl.BlockSpec((wide, width), lambda step, place: (0, 0))] * len(rights)
             + [pl.BlockSpec(resid.shape, lambda step, place: (0, 0))],
-            out_specs=pl.BlockSpec((tile, width), lambda step, place: (step, 0)),
+            out_specs=[pl.BlockSpec((tile, part), lambda step, place: (step, 0)) for part in widths],
         ),
-        out_shape=jax.ShapeDtypeStruct((tokens, width), jnp.bfloat16),
+        out_shape=[jax.ShapeDtypeStruct((tokens, part), jnp.bfloat16) for part in widths],
         compiler_params=pltpu.CompilerParams(vmem_limit_bytes=VMEM_BYTES),
         cost_estimate=pl.CostEstimate(flops=flops, bytes_accessed=moved, transcendentals=0),
         name="partial_product",
@@ -144,8 +144,9 @@
     channels, length = out_grad.shape
     features = projection.shape[1]
     half = features // 2
-    width = half // PIECES
-    groups = [1, 1] + [2] * ((PIECES - 2) // 2)
+    unit = half // UNITS
+    widths = [[unit * part for part in group] for group in GROUPS]
+    starts = [sum(map(sum, widths[:at])) for at in range(len(widths))]
     tok_rows = resid_grad.shape[0]
     window = tok_rows * exp_count
     tile = 2 * tok_rows
@@ -166,42 +167,47 @@
                     pairs.add((2 * far + core, 2 * near + core))
         return lax.ppermute(array, "exp", sorted(pairs))
 
-    def columns_of(array, core):
-        return lax.dynamic_slice_in_dim(array, core * half, half, 1)
-
-    rows_here = columns_of(projection, core_at)
-    rows_there = to_core(columns_of(projection, 1 - core_at))
-    chip_rows = jnp.concatenate([rows_here, rows_there], axis=0)
-    rights = []
-    at = 0
-    for group in groups:
-        piece = chip_rows[:, at : at + group * width]
-        rights.append([piece] + [to_ctx(piece, offset) for offset in range(1, ctx_count)])
-        at += group * width
-
-    resid_here = columns_of(resid_grad, core_at)
-    resid_there = to_core(columns_of(resid_grad, 1 - core_at))
+    def columns_of(array, core, at, width):
+        return lax.dynamic_slice_in_dim(array, core * half + at, width, 1)
+
+    def both_cores(array, at, width):
+        here = columns_of(array, core_at, at, width)
+        return here, to_core(columns_of(array, 1 - core_at, at, width))
+
+    def spread(piece):
+        return [piece] + [to_ctx(piece, offset) for offset in range(1, ctx_count)]
+
+    first = sum(widths[0])
+    rights = [spread(jnp.concatenate(both_cores(projection, 0, first), axis=0))]
+
+    parts = 2 if channels % 256 == 0 else 1
+    conv_args = [0.5 * conv_weight.T, 0.5 * conv_bias[:, None], skip_scale[:, None]]
+    lefts = []
+    routed = None
+    packed = jnp.concatenate([routes.T.astype(jnp.float32), gate_probs.T], axis=0)
+    for part in range(parts):
+        if part == parts - 1:
+            scan_grad, rights[0] = lax.optimization_barrier((scan_grad, rights[0]))
+        turned = conv_grad(part, parts, out_grad, gate_in, conv_in, scan_grad, *conv_args)
+        mine = [lax.dynamic_slice_in_dim(turned, (ctx_at ^ offset) * window, window, 0) for offset in range(ctx_count)]
+        mine = mine[:1] + [to_ctx(mine[offset], offset) for offset in range(1, ctx_count)]
+        if part == parts - 1:
+            packed, projection, resid_grad, turned = lax.optimization_barrier((packed, projection, resid_grad, turned))
+            routed = lax.all_gather(packed, "exp", axis=0, tiled=False)
+            routed, mine[0] = lax.optimization_barrier((routed, mine[0]))
+        for piece in mine:
+            lefts.append((piece, to_core(piece)))
+
+    rest_here, rest_there = both_cores(projection, first, half - first)
+    for group, at in list(zip(widths, starts))[1:]:
+        cut = slice(at - first, at - first + sum(group))
+        rights.append(spread(jnp.concatenate([rest_here[:, cut], rest_there[:, cut]], axis=0)))
+    resid_here, resid_there = both_cores(resid_grad, 0, half)
     resid = jnp.where(
         core_at == 0,
         jnp.concatenate([resid_here, resid_there], axis=0),
         jnp.concatenate([resid_there, resid_here], axis=0),
     )
-
-    turned = conv_grad(out_grad, gate_in, conv_in, scan_grad, conv_weight, conv_bias, skip_scale)
-    turned, rights[0] = lax.optimization_barrier((turned, rights[0]))
-    lefts = []
-    for offset in range(ctx_count):
-        piece = lax.dynamic_slice_in_dim(turned, (ctx_at ^ offset) * window, window, 0)
-        if offset:
-            piece = to_ctx(piece, offset)
-        lefts += [piece, to_core(piece)]
-    packed = jnp.concatenate([routes.T.astype(jnp.float32), gate_probs.T], axis=0)
-    packed, lefts[0] = lax.optimization_barrier((packed, lefts[0]))
-    routed = lax.all_gather(packed, "exp", axis=0, tiled=False)
-    routed, lefts = lax.optimization_barrier((routed, lefts))
-    if channels < 128:
-        lefts = [jnp.concatenate(lefts, axis=1)]
-        rights = [[jnp.concatenate(chunk, axis=0)] for chunk in rights]
 
     route_width = routes.shape[1]
     all_routes = routed[:, :route_width]
@@ -218,14 +224,22 @@
     picks = slot == jnp.arange(2 * capacity, dtype=jnp.int32)[None, None, :, None]
     scale = jnp.sum(jnp.where(picks, prob.reshape(2, chips, 1, tile), 0.0), axis=3, keepdims=True)
     picks = picks.astype(jnp.bfloat16)
-
+    picks, scale, lefts = lax.optimization_barrier((picks, scale, lefts))
+
+    lefts = [
+        lefts[part * ctx_count + offset][core]
+        for offset in range(ctx_count)
+        for core in (0, 1)
+        for part in range(parts)
+    ]
+    if channels < 128:
+        lefts = [jnp.concatenate(lefts, axis=1)]
+        rights = [[jnp.concatenate(chunk, axis=0)] for chunk in rights]
     place = chip_at.astype(jnp.int32).reshape(1)
     own = []
-    at = 0
-    for group, right in zip(groups, rights):
-        product = matmul(lefts, right, resid[:, at : at + group * width], place)
-        own += [product[:, part * width : (part + 1) * width] for part in range(group)]
-        at += group * width
+    for group, at, right in zip(widths, starts, rights):
+        own += matmul(lefts, right, resid[:, at : at + sum(group)], place, group)
+    pieces = len(own)
 
     middle = chips // 2
     distance = jnp.minimum(chip_at, chips - 1 - chip_at)
@@ -235,36 +249,41 @@
         return (one.astype(jnp.float32) + other.astype(jnp.float32)).astype(jnp.bfloat16)
 
     def finish(grads):
+        width = grads.shape[1]
         rows = jnp.einsum("eist,itf->eisf", picks, grads.reshape(chips, tile, width), preferred_element_type=jnp.float32)
         rows = (rows * scale).astype(jnp.bfloat16).reshape(2, chips * 2 * capacity, width)
         rows_own.append(rows[0])
         rows_got.append(to_core(rows[1]))
 
     hops = middle - 1
-    sums = [list(own)] + [[None] * PIECES for _ in range(hops)]
-    ready = [[None] * PIECES for _ in range(hops + 1)]
+    sums = [list(own)] + [[None] * pieces for _ in range(hops)]
+    ready = [[None] * pieces for _ in range(hops + 1)]
     lag = DELAY - 1
-    last = PIECES + lag * hops + DELAY * hops
+    last = pieces + lag * hops + DELAY * hops
     for step in range(last + 1):
         for hop in range(hops):
             inward = step - lag * hop
             outward = inward - DELAY - 2 * lag * (hops - 1 - hop)
-            send_in = 0 <= inward < PIECES
-            send_out = 0 <= outward < PIECES
-            if not (send_in or send_out):
-                continue
-            if send_in and send_out:
-                payload = jnp.where(distance == hop, sums[hop][inward], ready[hop + 1][outward])
+            send_in = 0 <= inward < pieces
+            send_out = 0 <= outward < pieces
+            if send_in and 0 <= inward - 2:
+                sums[hop][inward], sums[hop + 1][inward - 2] = lax.optimization_barrier(
+                    (sums[hop][inward], sums[hop + 1][inward - 2])
+                )
+            rising = sums[hop][inward] if send_in else None
+            falling = ready[hop + 1][outward] if send_out else None
+            if send_in and send_out and rising.shape == falling.shape:
+                got_in = got_out = swap_chips(jnp.where(distance == hop, rising, falling), hop)
             else:
-                payload = sums[hop][inward] if send_in else ready[hop + 1][outward]
-            got = swap_chips(payload, hop, send_in, send_out)
+                got_in = swap_chips(rising, hop, True, False) if send_in else None
+                got_out = swap_chips(falling, hop, False, True) if send_out else None
             if send_in:
-                sums[hop + 1][inward] = add(sums[hop][inward], got)
+                sums[hop + 1][inward] = add(rising, got_in)
                 if hop == hops - 1:
                     crossed = swap_chips(sums[hop + 1][inward], middle - 1)
                     ready[hops][inward] = add(sums[hop + 1][inward], crossed)
             if send_out:
-                ready[hop][outward] = jnp.where(distance == hop, got, ready[hop + 1][outward])
+                ready[hop][outward] = jnp.where(distance == hop, got_out, falling)
                 if hop == 0:
                     finish(ready[0][outward])
     result = jnp.where(

time: 287 us -> 348 us (1.21)
  waiting for transfers between devices: 108 us -> 142 us
  starting transfers between devices: 84.8 us -> 107 us
  local copies, waits for them, and re-layouts: 20.1 us -> 25.3 us
  other arithmetic: 18.6 us -> 13.9 us
    ppermute x19 -> x27, waiting for transfers between devices: 73 us -> 90.2 us  [swap_chips(): return lax.ppermute(array, 'exp', sorted(pairs))]
    ppermute x18 -> x21, waiting for transfers between devices: 32.1 us -> 48.9 us  [to_ctx(): lax.ppermute(array, 'ctx', [(place, place ^ offset) for place in range(ct...]
    ppermute x19 -> x27, starting transfers between devices: 59.3 us -> 73.4 us  [swap_chips(): return lax.ppermute(array, 'exp', sorted(pairs))]
    ppermute x18 -> x21, starting transfers between devices: 23.1 us -> 28.9 us  [to_ctx(): lax.ppermute(array, 'ctx', [(place, place ^ offset) for place in range(ct...]
    slice x2 -> x7, local copies, waits for them, and re-layouts: 1.01 us -> 5.36 us  [the longest x2 2.21 us: on_device(): rest_here[:, cut]]
    pallas_call x1 -> x2, Pallas kernels: 16.9 us -> 17.8 us  [conv_grad(): pl.pallas_call(functools.partial(conv_kernel, tile), grid=(1,), in_specs=...]
    unnamed x90 -> x86, local copies, waits for them, and re-layouts: 9.66 us -> 10 us
  transfers between devices with their start and end apart: 51 -> 69, of which waited for: 17 -> 27; matrix products, arithmetic and copies ran while one was open for 9% -> 8% of each run, Pallas kernels for 13% -> 12%
where the time goes in v3:
time: 348 us; the launch traced here: 346 us
  waiting for transfers between devices  142 us (41%)
  starting transfers between devices  107 us (31%)
  Pallas kernels  40 us (11%)
  local copies, waits for them, and re-layouts  25.3 us (7%)
  other arithmetic  13.9 us (4%)
  blocking collectives  13.3 us (4%)
    ppermute x27, waiting for transfers between devices, swap_chips(): return lax.ppermute(array, 'exp', sorted(pairs))  90.2 us
    ppermute x27, starting transfers between devices, swap_chips(): return lax.ppermute(array, 'exp', sorted(pairs))  73.4 us
    ppermute x21, waiting for transfers between devices, to_ctx(): lax.ppermute(array, 'ctx', [(place, place ^ offset) for place in range(ct...  48.9 us
    ppermute x21, starting transfers between devices, to_ctx(): lax.ppermute(array, 'ctx', [(place, place ^ offset) for place in range(ct...  28.9 us
    pallas_call x5, Pallas kernels, matmul(): pl.pallas_call(functools.partial(matmul_kernel, len(lefts), len(rights)),...  22.2 us
    pallas_call x2, Pallas kernels, conv_grad(): pl.pallas_call(functools.partial(conv_kernel, tile), grid=(1,), in_specs=...  17.8 us
    all_gather x1, blocking collectives, on_device(): routed = lax.all_gather(packed, 'exp', axis=0, tiled=False)  13.3 us
    unnamed x86, local copies, waits for them, and re-layouts  10 us
  transfers between devices with their start and end apart: 69, of which 27 were waited for; matrix products, arithmetic and copies ran while one was open for 8% of the time, Pallas kernels for 12%

profile of v3, /device:TPU:0, one launch (start us, length us, event | category | flops | bytes accessed | tf_op | source)
XLA Modules:
  0.0 345.6 jit_solution(10976501794320092604)
XLA Ops:
  3.9 1.6 copy-done
  5.5 1.6 copy-done.2
  7.1 8.9 %conv_grad.3 = bf16[4096,128]{1,0:T(8,128)(2,1)S(1)} custom-call(bf16[256,4096]{1,0:T(8,128)(2,1)S(1)} %copy-done, bf16[256,4096]{1,0:T(8,128)(2,1)S(1)} %copy-done.2, bf16[256,4096]{1,0:T(8,128)(2,1)} %conv_in.3, bf16[256,4096]{1,0:T(8,128)(2,1)} %scan_grad.2, f32[256,4]{1,0:T(8,128)S(1)} %bitcast.197, f32[256,1]{1,0:T(8,128)S(1)} %copy.42.bias, ...), custom_call_target="tpu_custom_call" | custom-call | flops 20971520 | bytes 5242880 | tf_op jit(solution)/shard_map/conv_grad/pallas_call | solution.py:70
  16.9 3.5 %collective-permute-start.9 = (bf16[1024,128]{1,0:T(8,128)(2,1)}, bf16[1024,128]{1,0:T(8,128)(2,1)S(1)}, u32[]{:S(2)}, u32[]{:S(2)}) collective-permute-start(bf16[1024,128]{1,0:T(8,128)(2,1)} %get-tuple-element.109), channel_id=1, source_target_pairs={{0,24},{8,16},{16,8},{24,0},{1,25},{9,17},{17,9},{25,1},{2,26},{10... | collective-permute-start | bytes 786440 | tf_op jit(solution)/shard_map/ppermute | solution.py:158
  21.7 1.5 collective-permute-start.3
  23.2 2.0 collective-permute-start.1
  25.2 5.4 %collective-permute-done.3.refs_19_ = bf16[512,128]{1,0:T(8,128)(2,1)S(1)} collective-permute-done((bf16[512,128]{1,0:T(8,128)(2,1)}, bf16[512,128]{1,0:T(8,128)(2,1)S(1)}, u32[]{:S(2)}, u32[]{:S(2)}) %collective-permute-start.3) | collective-permute-done | bytes 131104 | tf_op jit(solution)/shard_map/ppermute | solution.py:158
  31.3 1.9 collective-permute-start.5
  33.2 5.7 %collective-permute-done.2.refs_18_ = bf16[512,128]{1,0:T(8,128)(2,1)} collective-permute-done((bf16[512,128]{1,0:T(8,128)(2,1)}, bf16[512,128]{1,0:T(8,128)(2,1)}, u32[]{:S(2)}, u32[]{:S(2)}) %collective-permute-start.2) | collective-permute-done | bytes 131104 | tf_op jit(solution)/shard_map/ppermute | solution.py:158
  38.9 1.6 copy-done.3
  40.5 8.9 %conv_grad.2 = bf16[4096,128]{1,0:T(8,128)(2,1)S(1)} custom-call(bf16[256,4096]{1,0:T(8,128)(2,1)S(1)} %copy-done.1, bf16[256,4096]{1,0:T(8,128)(2,1)S(1)} %copy-done.3, bf16[256,4096]{1,0:T(8,128)(2,1)} %conv_in.3, bf16[256,4096]{1,0:T(8,128)(2,1)} %scan_grad.2, f32[256,4]{1,0:T(8,128)S(1)} %bitcast.198, f32[256,1]{1,0:T(8,128)S(1)} %copy.42.bias, ...), custom_call_target="tpu_custom_call" | custom-call | flops 20971520 | bytes 5242880 | tf_op jit(solution)/shard_map/conv_grad/pallas_call | solution.py:70
  49.5 13.3 %all-gather.1 = f32[8,4,128]{2,1,0:T(4,128)S(1)} all-gather(f32[1,4,128]{2,1,0:T(4,128)S(1)} %bitcast.230), channel_id=2, replica_groups=mesh['ctx'=4,'exp'=8] {'exp'}, dimensions={0}, use_global_device_ids=true | all-gather | bytes 18432 | tf_op jit(solution)/shard_map/all_gather | solution.py:196
  63.9 2.3 constant_dynamic-slice_fusion.6
  66.2 1.8 collective-permute-start.16
  70.8 5.6 %collective-permute-done.16.refs_13_ = bf16[1024,128]{1,0:T(8,128)(2,1)S(1)} collective-permute-done((bf16[1024,128]{1,0:T(8,128)(2,1)S(1)}, bf16[1024,128]{1,0:T(8,128)(2,1)S(1)}, u32[]{:S(2)}, u32[]{:S(2)}) %collective-permute-start.16) | collective-permute-done | bytes 262176 | tf_op jit(solution)/shard_map/ppermute | solution.py:158
  76.3 1.4 fusion.21
  77.7 1.3 broadcast_in_dim.47
  79.7 2.2 constant_dynamic-slice_fusion.3
  83.8 1.9 maximum_select_fusion
  86.7 4.1 %partial_product.5 = bf16[1024,128]{1,0:T(8,128)(2,1)} custom-call(s32[1]{0:T(128)} %bitcast.place, bf16[1024,128]{1,0:T(8,128)(2,1)S(1)} %get-tuple-element.54.refs_0_, bf16[1024,128]{1,0:T(8,128)(2,1)S(1)} %get-tuple-element.55.refs_1_, bf16[1024,128]{1,0:T(8,128)(2,1)} %collective-permute-done.4.refs_2_, ...), custom_call_target="tpu_custom_call" | custom-call | flops 536870912 | bytes 4980736 | tf_op jit(solution)/shard_map/partial_product/pallas_call | solution.py:107
  91.5 4.2 %collective-permute-start.19 = (bf16[1024,128]{1,0:T(8,128)(2,1)}, bf16[1024,128]{1,0:T(8,128)(2,1)}, u32[]{:S(2)}, u32[]{:S(2)}) collective-permute-start(bf16[1024,128]{1,0:T(8,128)(2,1)} %partial_product.5), channel_id=1, source_target_pairs={{0,2},{1,3},{6,4},{7,5},{8,10},{9,11},{14,12},{15,13},{16,18},{17,... | collective-permute-start | bytes 786440 | tf_op jit(solution)/shard_map/ppermute | solution.py:168
  98.8 2.2 collective-permute-done.19
  104.1 1.8 collective-permute-start.25
  107.7 1.3 collective-permute-start.21
  110.2 1.8 collective-permute-start.31
  112.1 8.2 %collective-permute-done.21 = bf16[1024,128]{1,0:T(8,128)(2,1)S(1)} collective-permute-done((bf16[1024,128]{1,0:T(8,128)(2,1)S(1)}, bf16[1024,128]{1,0:T(8,128)(2,1)S(1)}, u32[]{:S(2)}, u32[]{:S(2)}) %collective-permute-start.21) | collective-permute-done | bytes 262176 | tf_op jit(solution)/shard_map/ppermute | solution.py:168
  120.2 1.5 collective-permute-start.30
  122.9 2.7 collective-permute-done.24.refs_18_
  125.6 1.7 collective-permute-start.34
  127.5 4.8 %partial_product.6 = (bf16[1024,128]{1,0:T(8,128)(2,1)S(1)}, bf16[1024,256]{1,0:T(8,128)(2,1)}) custom-call(s32[1]{0:T(128)} %bitcast.place, bf16[1024,128]{1,0:T(8,128)(2,1)S(1)} %get-tuple-element.54.refs_0_, bf16[1024,128]{1,0:T(8,128)(2,1)S(1)} %get-tuple-element.55.refs_1_, bf16[1024,128]{1,0:T(8,128)(2,1)} %collective-permute-done.4.refs_2_, ...), custom_call_target="tpu_custom_call" | custom-call | flops 1610612736 | bytes 6553600 | tf_op jit(solution)/shard_map/partial_product/pallas_call | solution.py:107
  132.3 5.6 %collective-permute-start.26 = (bf16[1024,128]{1,0:T(8,128)(2,1)S(1)}, bf16[1024,128]{1,0:T(8,128)(2,1)S(1)}, u32[]{:S(2)}, u32[]{:S(2)}) collective-permute-start(bf16[1024,128]{1,0:T(8,128)(2,1)S(1)} %get-tuple-element.78), channel_id=1, source_target_pairs={{0,2},{1,3},{6,4},{7,5},{8,10},{9,11},{14,12},{15,13},{16,18},{17,... | collective-permute-start | bytes 786440 | tf_op jit(solution)/shard_map/ppermute | solution.py:168
  138.0 1.3 collective-permute-start.33
  139.3 8.8 %collective-permute-done.30.refs_18_ = bf16[512,512]{1,0:T(8,128)(2,1)S(1)} collective-permute-done((bf16[512,512]{1,0:T(8,128)(2,1)S(1)}, bf16[512,512]{1,0:T(8,128)(2,1)S(1)}, u32[]{:S(2)}, u32[]{:S(2)}) %collective-permute-start.30) | collective-permute-done | bytes 524320 | tf_op jit(solution)/shard_map/ppermute | solution.py:158
  148.1 1.5 collective-permute-start.32
  149.7 1.6 collective-permute-start.44
  151.2 8.2 %collective-permute-done.34.refs_19_ = bf16[512,512]{1,0:T(8,128)(2,1)S(1)} collective-permute-done((bf16[512,512]{1,0:T(8,128)(2,1)S(1)}, bf16[512,512]{1,0:T(8,128)(2,1)S(1)}, u32[]{:S(2)}, u32[]{:S(2)}) %collective-permute-start.34) | collective-permute-done | bytes 524320 | tf_op jit(solution)/shard_map/ppermute | solution.py:158
  159.4 1.5 collective-permute-start.43
  163.5 4.5 %partial_product.7 = (bf16[1024,256]{1,0:T(8,128)(2,1)S(1)}, bf16[1024,256]{1,0:T(8,128)(2,1)S(1)}) custom-call(s32[1]{0:T(128)} %bitcast.place, bf16[1024,128]{1,0:T(8,128)(2,1)S(1)} %get-tuple-element.54.refs_0_, bf16[1024,128]{1,0:T(8,128)(2,1)S(1)} %get-tuple-element.55.refs_1_, bf16[1024,128]{1,0:T(8,128)(2,1)} %collective-permute-done.4.refs_2_, ...), custom_call_target="tpu_custom_call" | custom-call | flops 2147483648 | bytes 7340032 | tf_op jit(solution)/shard_map/partial_product/pallas_call | solution.py:107
  168.1 2.4 collective-permute-done.33.refs_18_
  170.5 5.6 %collective-permute-start.36 = (bf16[1024,256]{1,0:T(8,128)(2,1)S(1)}, bf16[1024,256]{1,0:T(8,128)(2,1)S(1)}, u32[]{:S(2)}, u32[]{:S(2)}) collective-permute-start(bf16[1024,256]{1,0:T(8,128)(2,1)S(1)} %copy-done.17), channel_id=1, source_target_pairs={{0,2},{1,3},{6,4},{7,5},{8,10},{9,11},{14,12},{15,13},{16,18},{17,... | collective-permute-start | bytes 1572872 | tf_op jit(solution)/shard_map/ppermute | solution.py:168
  176.9 4.4 %partial_product.8 = (bf16[1024,256]{1,0:T(8,128)(2,1)S(1)}, bf16[1024,256]{1,0:T(8,128)(2,1)S(1)}) custom-call(s32[1]{0:T(128)} %bitcast.place, bf16[1024,128]{1,0:T(8,128)(2,1)S(1)} %get-tuple-element.54.refs_0_, bf16[1024,128]{1,0:T(8,128)(2,1)S(1)} %get-tuple-element.55.refs_1_, bf16[1024,128]{1,0:T(8,128)(2,1)} %collective-permute-done.4.refs_2_, ...), custom_call_target="tpu_custom_call" | custom-call | flops 2147483648 | bytes 7340032 | tf_op jit(solution)/shard_map/partial_product/pallas_call | solution.py:107
  181.9 9.4 %collective-permute-done.43.refs_18_ = bf16[512,512]{1,0:T(8,128)(2,1)} collective-permute-done((bf16[512,512]{1,0:T(8,128)(2,1)S(1)}, bf16[512,512]{1,0:T(8,128)(2,1)}, u32[]{:S(2)}, u32[]{:S(2)}) %collective-permute-start.43) | collective-permute-done | bytes 524320 | tf_op jit(solution)/shard_map/ppermute | solution.py:158
  191.5 4.4 %partial_product.9 = (bf16[1024,256]{1,0:T(8,128)(2,1)S(1)}, bf16[1024,128]{1,0:T(8,128)(2,1)S(1)}, bf16[1024,128]{1,0:T(8,128)(2,1)S(1)}) custom-call(s32[1]{0:T(128)} %bitcast.place, bf16[1024,128]{1,0:T(8,128)(2,1)S(1)} %get-tuple-element.54.refs_0_, bf16[1024,128]{1,0:T(8,128)(2,1)S(1)} %get-tuple-element.55.refs_1_, ...), custom_call_target="tpu_custom_call" | custom-call | flops 2147483648 | bytes 7340032 | tf_op jit(solution)/shard_map/partial_product/pallas_call | solution.py:107
  195.9 5.7 %collective-permute-start.35 = (bf16[1024,256]{1,0:T(8,128)(2,1)S(1)}, bf16[1024,256]{1,0:T(8,128)(2,1)S(1)}, u32[]{:S(2)}, u32[]{:S(2)}) collective-permute-start(bf16[1024,256]{1,0:T(8,128)(2,1)S(1)} %get-tuple-element.81), channel_id=1, source_target_pairs={{0,2},{1,3},{6,4},{7,5},{8,10},{9,11},{14,12},{15,13},{16,18},{17,... | collective-permute-start | bytes 1572872 | tf_op jit(solution)/shard_map/ppermute | solution.py:168
  203.8 7.7 %collective-permute-start.39 = (bf16[1024,256]{1,0:T(8,128)(2,1)S(1)}, bf16[1024,256]{1,0:T(8,128)(2,1)S(1)}, u32[]{:S(2)}, u32[]{:S(2)}) collective-permute-start(bf16[1024,256]{1,0:T(8,128)(2,1)S(1)} %get-tuple-element.87), channel_id=1, source_target_pairs={{0,2},{1,3},{6,4},{7,5},{8,10},{9,11},{14,12},{15,13},{16,18},{17,... | collective-permute-start | bytes 1572872 | tf_op jit(solution)/shard_map/ppermute | solution.py:168
  212.0 1.9 collective-permute-done.35
  215.0 7.8 %collective-permute-start.38 = (bf16[1024,256]{1,0:T(8,128)(2,1)S(1)}, bf16[1024,256]{1,0:T(8,128)(2,1)S(1)}, u32[]{:S(2)}, u32[]{:S(2)}) collective-permute-start(bf16[1024,256]{1,0:T(8,128)(2,1)S(1)} %broadcast_select_fusion.9), channel_id=1, source_target_pairs={{0,2},{1,3},{2,0},{3,1},{4,6},{5,7},{6,4},{7,5},{8,10},{9,11},{10,... | collective-permute-start | bytes 1572872 | tf_op jit(solution)/shard_map/ppermute | solution.py:168
  222.8 2.3 collective-permute-done.39
  226.1 7.9 %collective-permute-start.41 = (bf16[1024,256]{1,0:T(8,128)(2,1)S(1)}, bf16[1024,256]{1,0:T(8,128)(2,1)S(1)}, u32[]{:S(2)}, u32[]{:S(2)}) collective-permute-start(bf16[1024,256]{1,0:T(8,128)(2,1)S(1)} %broadcast_select_fusion.7), channel_id=1, source_target_pairs={{0,2},{1,3},{2,0},{3,1},{4,6},{5,7},{6,4},{7,5},{8,10},{9,11},{10,... | collective-permute-start | bytes 1572872 | tf_op jit(solution)/shard_map/ppermute | solution.py:168
  234.0 2.3 collective-permute-done.38
  238.4 7.9 %collective-permute-done.41 = bf16[1024,256]{1,0:T(8,128)(2,1)S(1)} collective-permute-done((bf16[1024,256]{1,0:T(8,128)(2,1)S(1)}, bf16[1024,256]{1,0:T(8,128)(2,1)S(1)}, u32[]{:S(2)}, u32[]{:S(2)}) %collective-permute-start.41) | collective-permute-done | bytes 524320 | tf_op jit(solution)/shard_map/ppermute | solution.py:168
  247.8 7.3 %collective-permute-start.53 = (bf16[1024,128]{1,0:T(8,128)(2,1)S(1)}, bf16[1024,128]{1,0:T(8,128)(2,1)S(1)}, u32[]{:S(2)}, u32[]{:S(2)}) collective-permute-start(bf16[1024,128]{1,0:T(8,128)(2,1)S(1)} %get-tuple-element.92), channel_id=1, source_target_pairs={{0,2},{1,3},{6,4},{7,5},{8,10},{9,11},{14,12},{15,13},{16,18},{17,... | collective-permute-start | bytes 786440 | tf_op jit(solution)/shard_map/ppermute | solution.py:168
  256.7 4.4 %collective-permute-done.53 = bf16[1024,128]{1,0:T(8,128)(2,1)S(1)} collective-permute-done((bf16[1024,128]{1,0:T(8,128)(2,1)S(1)}, bf16[1024,128]{1,0:T(8,128)(2,1)S(1)}, u32[]{:S(2)}, u32[]{:S(2)}) %collective-permute-start.53) | collective-permute-done | bytes 262176 | tf_op jit(solution)/shard_map/ppermute | solution.py:168
  262.0 1.3 collective-permute-start.50
  264.7 7.4 %collective-permute-done.48 = bf16[1024,256]{1,0:T(8,128)(2,1)S(1)} collective-permute-done((bf16[1024,256]{1,0:T(8,128)(2,1)S(1)}, bf16[1024,256]{1,0:T(8,128)(2,1)S(1)}, u32[]{:S(2)}, u32[]{:S(2)}) %collective-permute-start.48) | collective-permute-done | bytes 524320 | tf_op jit(solution)/shard_map/ppermute | solution.py:168
  272.8 2.6 collective-permute-start.46
  275.4 13.5 %collective-permute-done.55 = bf16[1024,128]{1,0:T(8,128)(2,1)S(1)} collective-permute-done((bf16[1024,128]{1,0:T(8,128)(2,1)S(1)}, bf16[1024,128]{1,0:T(8,128)(2,1)S(1)}, u32[]{:S(2)}, u32[]{:S(2)}) %collective-permute-start.55) | collective-permute-done | bytes 262176 | tf_op jit(solution)/shard_map/ppermute | solution.py:168
  290.3 8.8 %collective-permute-done.46 = bf16[1024,256]{1,0:T(8,128)(2,1)S(1)} collective-permute-done((bf16[1024,256]{1,0:T(8,128)(2,1)S(1)}, bf16[1024,256]{1,0:T(8,128)(2,1)S(1)}, u32[]{:S(2)}, u32[]{:S(2)}) %collective-permute-start.46) | collective-permute-done | bytes 524320 | tf_op jit(solution)/shard_map/ppermute | solution.py:168
  299.9 3.0 collective-permute-start.56
  303.5 4.1 %collective-permute-done.56 = bf16[1024,128]{1,0:T(8,128)(2,1)S(1)} collective-permute-done((bf16[1024,128]{1,0:T(8,128)(2,1)S(1)}, bf16[1024,128]{1,0:T(8,128)(2,1)S(1)}, u32[]{:S(2)}, u32[]{:S(2)}) %collective-permute-start.56) | collective-permute-done | bytes 262176 | tf_op jit(solution)/shard_map/ppermute | solution.py:168
  307.7 1.4 collective-permute-done.63
  312.7 17.7 %collective-permute-done.58 = bf16[1024,128]{1,0:T(8,128)(2,1)S(1)} collective-permute-done((bf16[1024,128]{1,0:T(8,128)(2,1)S(1)}, bf16[1024,128]{1,0:T(8,128)(2,1)S(1)}, u32[]{:S(2)}, u32[]{:S(2)}) %collective-permute-start.58) | collective-permute-done | bytes 262176 | tf_op jit(solution)/shard_map/ppermute | solution.py:168
  330.7 9.5 %collective-permute-done.52 = bf16[1024,256]{1,0:T(8,128)(2,1)S(1)} collective-permute-done((bf16[1024,256]{1,0:T(8,128)(2,1)S(1)}, bf16[1024,256]{1,0:T(8,128)(2,1)S(1)}, u32[]{:S(2)}, u32[]{:S(2)}) %collective-permute-start.52) | collective-permute-done | bytes 524320 | tf_op jit(solution)/shard_map/ppermute | solution.py:168
  343.4 2.2 broadcast_select_fusion
  (262 shorter events, 51.8 us)
Async XLA Ops:
  0.9 20.1 %collective-permute-start = (bf16[256,128]{1,0:T(8,128)(2,1)S(1)}, bf16[256,128]{1,0:T(8,128)(2,1)S(1)}, u32[]{:S(2)}, u32[]{:S(2)}) collective-permute-start(bf16[256,128]{1,0:T(8,128)(2,1)S(1)} %get-tuple-element.99), channel_id=1, source_target_pairs={{0,1},{1,0},{2,3},{3,2},{4,5},{5,4},{6,7},{7,6},{8,9},{9,8},{10,11... | collective-permute-start | bytes 196616 | tf_op jit(solution)/shard_map/ppermute | solution.py:155
  16.9 49.2 %collective-permute-start.9 = (bf16[1024,128]{1,0:T(8,128)(2,1)}, bf16[1024,128]{1,0:T(8,128)(2,1)S(1)}, u32[]{:S(2)}, u32[]{:S(2)}) collective-permute-start(bf16[1024,128]{1,0:T(8,128)(2,1)} %get-tuple-element.109), channel_id=1, source_target_pairs={{0,24},{8,16},{16,8},{24,0},{1,25},{9,17},{17,9},{25,1},{2,26},{10... | collective-permute-start | bytes 786440 | tf_op jit(solution)/shard_map/ppermute | solution.py:158
  20.4 47.6 %collective-permute-start.7 = (bf16[1024,128]{1,0:T(8,128)(2,1)}, bf16[1024,128]{1,0:T(8,128)(2,1)S(1)}, u32[]{:S(2)}, u32[]{:S(2)}) collective-permute-start(bf16[1024,128]{1,0:T(8,128)(2,1)} %get-tuple-element.110), channel_id=1, source_target_pairs={{0,16},{8,24},{16,0},{24,8},{1,17},{9,25},{17,1},{25,9},{2,18},{10... | collective-permute-start | bytes 786440 | tf_op jit(solution)/shard_map/ppermute | solution.py:158
  21.7 9.0 %collective-permute-start.3 = (bf16[512,128]{1,0:T(8,128)(2,1)}, bf16[512,128]{1,0:T(8,128)(2,1)S(1)}, u32[]{:S(2)}, u32[]{:S(2)}) collective-permute-start(bf16[512,128]{1,0:T(8,128)(2,1)} %pad_maximum_fusion.4.refs_16_), channel_id=1, source_target_pairs={{0,24},{8,16},{16,8},{24,0},{1,25},{9,17},{17,9},{25,1},{2,26},{10... | collective-permute-start | bytes 393224 | tf_op jit(solution)/shard_map/ppermute | solution.py:158
  23.2 15.7 %collective-permute-start.2 = (bf16[512,128]{1,0:T(8,128)(2,1)}, bf16[512,128]{1,0:T(8,128)(2,1)}, u32[]{:S(2)}, u32[]{:S(2)}) collective-permute-start(bf16[512,128]{1,0:T(8,128)(2,1)} %pad_maximum_fusion.4.refs_16_), channel_id=1, source_target_pairs={{0,16},{8,24},{16,0},{24,8},{1,17},{9,25},{17,1},{25,9},{2,18},{10... | collective-permute-start | bytes 393224 | tf_op jit(solution)/shard_map/ppermute | solution.py:158
  23.2 15.7 %collective-permute-start.1 = (bf16[512,128]{1,0:T(8,128)(2,1)}, bf16[512,128]{1,0:T(8,128)(2,1)}, u32[]{:S(2)}, u32[]{:S(2)}) collective-permute-start(bf16[512,128]{1,0:T(8,128)(2,1)} %pad_maximum_fusion.4.refs_16_), channel_id=1, source_target_pairs={{0,8},{8,0},{16,24},{24,16},{1,9},{9,1},{17,25},{25,17},{2,10},{10... | collective-permute-start | bytes 393224 | tf_op jit(solution)/shard_map/ppermute | solution.py:158
  31.3 37.7 %collective-permute-start.5 = (bf16[1024,128]{1,0:T(8,128)(2,1)}, bf16[1024,128]{1,0:T(8,128)(2,1)S(1)}, u32[]{:S(2)}, u32[]{:S(2)}) collective-permute-start(bf16[1024,128]{1,0:T(8,128)(2,1)} %get-tuple-element.111), channel_id=1, source_target_pairs={{0,8},{8,0},{16,24},{24,16},{1,9},{9,1},{17,25},{25,17},{2,10},{10... | collective-permute-start | bytes 786440 | tf_op jit(solution)/shard_map/ppermute | solution.py:158
  38.9 31.3 %collective-permute-start.4 = (bf16[1024,128]{1,0:T(8,128)(2,1)S(1)}, bf16[1024,128]{1,0:T(8,128)(2,1)}, u32[]{:S(2)}, u32[]{:S(2)}) collective-permute-start(bf16[1024,128]{1,0:T(8,128)(2,1)S(1)} %get-tuple-element.54.refs_0_), channel_id=1, source_target_pairs={{0,1},{1,0},{2,3},{3,2},{4,5},{5,4},{6,7},{7,6},{8,9},{9,8},{10,11... | collective-permute-start | bytes 786440 | tf_op jit(solution)/shard_map/ppermute | solution.py:155
  63.5 7.3 %collective-permute-start.11 = (bf16[1024,128]{1,0:T(8,128)(2,1)S(1)}, bf16[1024,128]{1,0:T(8,128)(2,1)S(1)}, u32[]{:S(2)}, u32[]{:S(2)}) collective-permute-start(bf16[1024,128]{1,0:T(8,128)(2,1)S(1)} %get-tuple-element.55.refs_1_), channel_id=1, source_target_pairs={{0,1},{1,0},{2,3},{3,2},{4,5},{5,4},{6,7},{7,6},{8,9},{9,8},{10,11... | collective-permute-start | bytes 786440 | tf_op jit(solution)/shard_map/ppermute | solution.py:155
  66.2 10.2 %collective-permute-start.16 = (bf16[1024,128]{1,0:T(8,128)(2,1)S(1)}, bf16[1024,128]{1,0:T(8,128)(2,1)S(1)}, u32[]{:S(2)}, u32[]{:S(2)}) collective-permute-start(bf16[1024,128]{1,0:T(8,128)(2,1)S(1)} %get-tuple-element.105), channel_id=1, source_target_pairs={{0,24},{8,16},{16,8},{24,0},{1,25},{9,17},{17,9},{25,1},{2,26},{10... | collective-permute-start | bytes 786440 | tf_op jit(solution)/shard_map/ppermute | solution.py:158
  68.0 15.3 %collective-permute-start.18 = (bf16[128,2048]{1,0:T(8,128)(2,1)}, bf16[128,2048]{1,0:T(8,128)(2,1)}, u32[]{:S(2)}, u32[]{:S(2)}) collective-permute-start(bf16[128,2048]{1,0:T(8,128)(2,1)} %get-tuple-element.104), channel_id=1, source_target_pairs={{0,1},{1,0},{2,3},{3,2},{4,5},{5,4},{6,7},{7,6},{8,9},{9,8},{10,11... | collective-permute-start | bytes 1572872 | tf_op jit(solution)/shard_map/ppermute | solution.py:155
  69.0 12.9 %collective-permute-start.14 = (bf16[1024,128]{1,0:T(8,128)(2,1)S(1)}, bf16[1024,128]{1,0:T(8,128)(2,1)S(1)}, u32[]{:S(2)}, u32[]{:S(2)}) collective-permute-start(bf16[1024,128]{1,0:T(8,128)(2,1)S(1)} %get-tuple-element.106), channel_id=1, source_target_pairs={{0,16},{8,24},{16,0},{24,8},{1,17},{9,25},{17,1},{25,9},{2,18},{10... | collective-permute-start | bytes 786440 | tf_op jit(solution)/shard_map/ppermute | solution.py:158
  70.2 12.2 %collective-permute-start.12 = (bf16[1024,128]{1,0:T(8,128)(2,1)S(1)}, bf16[1024,128]{1,0:T(8,128)(2,1)S(1)}, u32[]{:S(2)}, u32[]{:S(2)}) collective-permute-start(bf16[1024,128]{1,0:T(8,128)(2,1)S(1)} %get-tuple-element.107), channel_id=1, source_target_pairs={{0,8},{8,0},{16,24},{24,16},{1,9},{9,1},{17,25},{25,17},{2,10},{10... | collective-permute-start | bytes 786440 | tf_op jit(solution)/shard_map/ppermute | solution.py:158
  70.8 11.8 %collective-permute-start.10 = (bf16[1024,128]{1,0:T(8,128)(2,1)S(1)}, bf16[1024,128]{1,0:T(8,128)(2,1)S(1)}, u32[]{:S(2)}, u32[]{:S(2)}) collective-permute-start(bf16[1024,128]{1,0:T(8,128)(2,1)S(1)} %collective-permute-done.9.refs_12_), channel_id=1, source_target_pairs={{0,1},{1,0},{2,3},{3,2},{4,5},{5,4},{6,7},{7,6},{8,9},{9,8},{10,11... | collective-permute-start | bytes 786440 | tf_op jit(solution)/shard_map/ppermute | solution.py:155
  76.3 6.6 %collective-permute-start.8 = (bf16[1024,128]{1,0:T(8,128)(2,1)S(1)}, bf16[1024,128]{1,0:T(8,128)(2,1)S(1)}, u32[]{:S(2)}, u32[]{:S(2)}) collective-permute-start(bf16[1024,128]{1,0:T(8,128)(2,1)S(1)} %collective-permute-done.7.refs_8_), channel_id=1, source_target_pairs={{0,1},{1,0},{2,3},{3,2},{4,5},{5,4},{6,7},{7,6},{8,9},{9,8},{10,11... | collective-permute-start | bytes 786440 | tf_op jit(solution)/shard_map/ppermute | solution.py:155
  81.9 3.8 %collective-permute-start.6 = (bf16[1024,128]{1,0:T(8,128)(2,1)S(1)}, bf16[1024,128]{1,0:T(8,128)(2,1)S(1)}, u32[]{:S(2)}, u32[]{:S(2)}) collective-permute-start(bf16[1024,128]{1,0:T(8,128)(2,1)S(1)} %collective-permute-done.5.refs_4_), channel_id=1, source_target_pairs={{0,1},{1,0},{2,3},{3,2},{4,5},{5,4},{6,7},{7,6},{8,9},{9,8},{10,11... | collective-permute-start | bytes 786440 | tf_op jit(solution)/shard_map/ppermute | solution.py:155
  82.4 3.3 collective-permute-start.17
  82.5 3.3 collective-permute-start.15
  83.0 2.8 collective-permute-start.13
  83.3 19.8 %collective-permute-start.22 = (bf16[256,1920]{1,0:T(8,128)(2,1)}, bf16[256,1920]{1,0:T(8,128)(2,1)}, u32[]{:S(2)}, u32[]{:S(2)}) collective-permute-start(bf16[256,1920]{1,0:T(8,128)(2,1)} %constant_dynamic-slice_fusion.3), channel_id=1, source_target_pairs={{0,1},{1,0},{2,3},{3,2},{4,5},{5,4},{6,7},{7,6},{8,9},{9,8},{10,11... | collective-permute-start | bytes 2949128 | tf_op jit(solution)/shard_map/ppermute | solution.py:155
  91.5 9.6 %collective-permute-start.19 = (bf16[1024,128]{1,0:T(8,128)(2,1)}, bf16[1024,128]{1,0:T(8,128)(2,1)}, u32[]{:S(2)}, u32[]{:S(2)}) collective-permute-start(bf16[1024,128]{1,0:T(8,128)(2,1)} %partial_product.5), channel_id=1, source_target_pairs={{0,2},{1,3},{6,4},{7,5},{8,10},{9,11},{14,12},{15,13},{16,18},{17,... | collective-permute-start | bytes 786440 | tf_op jit(solution)/shard_map/ppermute | solution.py:168
  102.2 5.5 %collective-permute-start.20 = (bf16[1024,128]{1,0:T(8,128)(2,1)S(1)}, bf16[1024,128]{1,0:T(8,128)(2,1)S(1)}, u32[]{:S(2)}, u32[]{:S(2)}) collective-permute-start(bf16[1024,128]{1,0:T(8,128)(2,1)S(1)} %add_convert_fusion.19), channel_id=1, source_target_pairs={{2,4},{3,5},{4,2},{5,3},{10,12},{11,13},{12,10},{13,11},{18,20},{1... | collective-permute-start | bytes 786440 | tf_op jit(solution)/shard_map/ppermute | solution.py:168
  104.1 18.0 %collective-permute-start.25 = (bf16[512,384]{1,0:T(8,128)(2,1)S(1)}, bf16[512,384]{1,0:T(8,128)(2,1)S(1)}, u32[]{:S(2)}, u32[]{:S(2)}) collective-permute-start(bf16[512,384]{1,0:T(8,128)(2,1)S(1)} %pad_maximum_fusion.3.refs_16_), channel_id=1, source_target_pairs={{0,24},{8,16},{16,8},{24,0},{1,25},{9,17},{17,9},{25,1},{2,26},{10... | collective-permute-start | bytes 1179656 | tf_op jit(solution)/shard_map/ppermute | solution.py:158
  105.9 19.8 %collective-permute-start.24 = (bf16[512,384]{1,0:T(8,128)(2,1)S(1)}, bf16[512,384]{1,0:T(8,128)(2,1)S(1)}, u32[]{:S(2)}, u32[]{:S(2)}) collective-permute-start(bf16[512,384]{1,0:T(8,128)(2,1)S(1)} %pad_maximum_fusion.3.refs_16_), channel_id=1, source_target_pairs={{0,16},{8,24},{16,0},{24,8},{1,17},{9,25},{17,1},{25,9},{2,18},{10... | collective-permute-start | bytes 1179656 | tf_op jit(solution)/shard_map/ppermute | solution.py:158
  107.1 20.2 %collective-permute-start.23 = (bf16[512,384]{1,0:T(8,128)(2,1)S(1)}, bf16[512,384]{1,0:T(8,128)(2,1)S(1)}, u32[]{:S(2)}, u32[]{:S(2)}) collective-permute-start(bf16[512,384]{1,0:T(8,128)(2,1)S(1)} %pad_maximum_fusion.3.refs_16_), channel_id=1, source_target_pairs={{0,8},{8,0},{16,24},{24,16},{1,9},{9,1},{17,25},{25,17},{2,10},{10... | collective-permute-start | bytes 1179656 | tf_op jit(solution)/shard_map/ppermute | solution.py:158
  107.7 12.5 %collective-permute-start.21 = (bf16[1024,128]{1,0:T(8,128)(2,1)S(1)}, bf16[1024,128]{1,0:T(8,128)(2,1)S(1)}, u32[]{:S(2)}, u32[]{:S(2)}) collective-permute-start(bf16[1024,128]{1,0:T(8,128)(2,1)S(1)} %add_convert_fusion.18), channel_id=1, source_target_pairs={{2,0},{3,1},{4,6},{5,7},{10,8},{11,9},{12,14},{13,15},{18,16},{19,... | collective-permute-start | bytes 786440 | tf_op jit(solution)/shard_map/ppermute | solution.py:168
  110.2 27.7 %collective-permute-start.31 = (bf16[512,512]{1,0:T(8,128)(2,1)S(1)}, bf16[512,512]{1,0:T(8,128)(2,1)S(1)}, u32[]{:S(2)}, u32[]{:S(2)}) collective-permute-start(bf16[512,512]{1,0:T(8,128)(2,1)S(1)} %pad_maximum_fusion.refs_16_), channel_id=1, source_target_pairs={{0,24},{8,16},{16,8},{24,0},{1,25},{9,17},{17,9},{25,1},{2,26},{10... | collective-permute-start | bytes 1572872 | tf_op jit(solution)/shard_map/ppermute | solution.py:158
  120.2 27.9 %collective-permute-start.30 = (bf16[512,512]{1,0:T(8,128)(2,1)S(1)}, bf16[512,512]{1,0:T(8,128)(2,1)S(1)}, u32[]{:S(2)}, u32[]{:S(2)}) collective-permute-start(bf16[512,512]{1,0:T(8,128)(2,1)S(1)} %pad_maximum_fusion.refs_16_), channel_id=1, source_target_pairs={{0,16},{8,24},{16,0},{24,8},{1,17},{9,25},{17,1},{25,9},{2,18},{10... | collective-permute-start | bytes 1572872 | tf_op jit(solution)/shard_map/ppermute | solution.py:158
  122.1 27.5 %collective-permute-start.29 = (bf16[512,512]{1,0:T(8,128)(2,1)S(1)}, bf16[512,512]{1,0:T(8,128)(2,1)S(1)}, u32[]{:S(2)}, u32[]{:S(2)}) collective-permute-start(bf16[512,512]{1,0:T(8,128)(2,1)S(1)} %pad_maximum_fusion.refs_16_), channel_id=1, source_target_pairs={{0,8},{8,0},{16,24},{24,16},{1,9},{9,1},{17,25},{25,17},{2,10},{10... | collective-permute-start | bytes 1572872 | tf_op jit(solution)/shard_map/ppermute | solution.py:158
  125.6 33.7 %collective-permute-start.34 = (bf16[512,512]{1,0:T(8,128)(2,1)S(1)}, bf16[512,512]{1,0:T(8,128)(2,1)S(1)}, u32[]{:S(2)}, u32[]{:S(2)}) collective-permute-start(bf16[512,512]{1,0:T(8,128)(2,1)S(1)} %pad_maximum_fusion.1.refs_16_), channel_id=1, source_target_pairs={{0,24},{8,16},{16,8},{24,0},{1,25},{9,17},{17,9},{25,1},{2,26},{10... | collective-permute-start | bytes 1572872 | tf_op jit(solution)/shard_map/ppermute | solution.py:158
  127.4 4.9 %collective-permute-start.59 = (bf16[448,128]{1,0:T(8,128)(2,1)S(1)}, bf16[448,128]{1,0:T(8,128)(2,1)S(1)}, u32[]{:S(2)}, u32[]{:S(2)}) collective-permute-start(bf16[448,128]{1,0:T(8,128)(2,1)S(1)} %bitcast.227), channel_id=1, source_target_pairs={{0,1},{1,0},{2,3},{3,2},{4,5},{5,4},{6,7},{7,6},{8,9},{9,8},{10,11... | collective-permute-start | bytes 344072 | tf_op jit(solution)/shard_map/ppermute | solution.py:155
  132.3 28.6 %collective-permute-start.26 = (bf16[1024,128]{1,0:T(8,128)(2,1)S(1)}, bf16[1024,128]{1,0:T(8,128)(2,1)S(1)}, u32[]{:S(2)}, u32[]{:S(2)}) collective-permute-start(bf16[1024,128]{1,0:T(8,128)(2,1)S(1)} %get-tuple-element.78), channel_id=1, source_target_pairs={{0,2},{1,3},{6,4},{7,5},{8,10},{9,11},{14,12},{15,13},{16,18},{17,... | collective-permute-start | bytes 786440 | tf_op jit(solution)/shard_map/ppermute | solution.py:168
  138.0 32.5 %collective-permute-start.33 = (bf16[512,512]{1,0:T(8,128)(2,1)S(1)}, bf16[512,512]{1,0:T(8,128)(2,1)S(1)}, u32[]{:S(2)}, u32[]{:S(2)}) collective-permute-start(bf16[512,512]{1,0:T(8,128)(2,1)S(1)} %pad_maximum_fusion.1.refs_16_), channel_id=1, source_target_pairs={{0,16},{8,24},{16,0},{24,8},{1,17},{9,25},{17,1},{25,9},{2,18},{10... | collective-permute-start | bytes 1572872 | tf_op jit(solution)/shard_map/ppermute | solution.py:158
  148.1 28.1 %collective-permute-start.32 = (bf16[512,512]{1,0:T(8,128)(2,1)S(1)}, bf16[512,512]{1,0:T(8,128)(2,1)}, u32[]{:S(2)}, u32[]{:S(2)}) collective-permute-start(bf16[512,512]{1,0:T(8,128)(2,1)S(1)} %pad_maximum_fusion.1.refs_16_), channel_id=1, source_target_pairs={{0,8},{8,0},{16,24},{24,16},{1,9},{9,1},{17,25},{25,17},{2,10},{10... | collective-permute-start | bytes 1572872 | tf_op jit(solution)/shard_map/ppermute | solution.py:158
  149.7 32.2 %collective-permute-start.44 = (bf16[512,512]{1,0:T(8,128)(2,1)S(1)}, bf16[512,512]{1,0:T(8,128)(2,1)S(1)}, u32[]{:S(2)}, u32[]{:S(2)}) collective-permute-start(bf16[512,512]{1,0:T(8,128)(2,1)S(1)} %pad_maximum_fusion.2.refs_16_), channel_id=1, source_target_pairs={{0,24},{8,16},{16,8},{24,0},{1,25},{9,17},{17,9},{25,1},{2,26},{10... | collective-permute-start | bytes 1572872 | tf_op jit(solution)/shard_map/ppermute | solution.py:158
  159.4 31.9 %collective-permute-start.43 = (bf16[512,512]{1,0:T(8,128)(2,1)S(1)}, bf16[512,512]{1,0:T(8,128)(2,1)}, u32[]{:S(2)}, u32[]{:S(2)}) collective-permute-start(bf16[512,512]{1,0:T(8,128)(2,1)S(1)} %pad_maximum_fusion.2.refs_16_), channel_id=1, source_target_pairs={{0,16},{8,24},{16,0},{24,8},{1,17},{9,25},{17,1},{25,9},{2,18},{10... | collective-permute-start | bytes 1572872 | tf_op jit(solution)/shard_map/ppermute | solution.py:158
  160.9 30.6 %collective-permute-start.42 = (bf16[512,512]{1,0:T(8,128)(2,1)S(1)}, bf16[512,512]{1,0:T(8,128)(2,1)}, u32[]{:S(2)}, u32[]{:S(2)}) collective-permute-start(bf16[512,512]{1,0:T(8,128)(2,1)S(1)} %pad_maximum_fusion.2.refs_16_), channel_id=1, source_target_pairs={{0,8},{8,0},{16,24},{24,16},{1,9},{9,1},{17,25},{25,17},{2,10},{10... | collective-permute-start | bytes 1572872 | tf_op jit(solution)/shard_map/ppermute | solution.py:158
  170.5 32.4 %collective-permute-start.36 = (bf16[1024,256]{1,0:T(8,128)(2,1)S(1)}, bf16[1024,256]{1,0:T(8,128)(2,1)S(1)}, u32[]{:S(2)}, u32[]{:S(2)}) collective-permute-start(bf16[1024,256]{1,0:T(8,128)(2,1)S(1)} %copy-done.17), channel_id=1, source_target_pairs={{0,2},{1,3},{6,4},{7,5},{8,10},{9,11},{14,12},{15,13},{16,18},{17,... | collective-permute-start | bytes 1572872 | tf_op jit(solution)/shard_map/ppermute | solution.py:168
  176.2 25.4 %collective-permute-start.27 = (bf16[1024,128]{1,0:T(8,128)(2,1)S(1)}, bf16[1024,128]{1,0:T(8,128)(2,1)S(1)}, u32[]{:S(2)}, u32[]{:S(2)}) collective-permute-start(bf16[1024,128]{1,0:T(8,128)(2,1)S(1)} %add_convert_fusion.17), channel_id=1, source_target_pairs={{2,4},{3,5},{4,2},{5,3},{10,12},{11,13},{12,10},{13,11},{18,20},{1... | collective-permute-start | bytes 786440 | tf_op jit(solution)/shard_map/ppermute | solution.py:168
  195.9 18.0 %collective-permute-start.35 = (bf16[1024,256]{1,0:T(8,128)(2,1)S(1)}, bf16[1024,256]{1,0:T(8,128)(2,1)S(1)}, u32[]{:S(2)}, u32[]{:S(2)}) collective-permute-start(bf16[1024,256]{1,0:T(8,128)(2,1)S(1)} %get-tuple-element.81), channel_id=1, source_target_pairs={{0,2},{1,3},{6,4},{7,5},{8,10},{9,11},{14,12},{15,13},{16,18},{17,... | collective-permute-start | bytes 1572872 | tf_op jit(solution)/shard_map/ppermute | solution.py:168
  201.7 9.9 %collective-permute-start.28 = (bf16[1024,128]{1,0:T(8,128)(2,1)S(1)}, bf16[1024,128]{1,0:T(8,128)(2,1)S(1)}, u32[]{:S(2)}, u32[]{:S(2)}) collective-permute-start(bf16[1024,128]{1,0:T(8,128)(2,1)S(1)} %add_convert_fusion.16), channel_id=1, source_target_pairs={{2,0},{3,1},{4,6},{5,7},{10,8},{11,9},{12,14},{13,15},{18,16},{19,... | collective-permute-start | bytes 786440 | tf_op jit(solution)/shard_map/ppermute | solution.py:168
  203.1 11.6 %collective-permute-start.37 = (bf16[1024,256]{1,0:T(8,128)(2,1)S(1)}, bf16[1024,256]{1,0:T(8,128)(2,1)S(1)}, u32[]{:S(2)}, u32[]{:S(2)}) collective-permute-start(bf16[1024,256]{1,0:T(8,128)(2,1)S(1)} %add_convert_fusion.10), channel_id=1, source_target_pairs={{2,4},{3,5},{4,2},{5,3},{10,12},{11,13},{12,10},{13,11},{18,20},{1... | collective-permute-start | bytes 1572872 | tf_op jit(solution)/shard_map/ppermute | solution.py:168
  203.8 21.3 %collective-permute-start.39 = (bf16[1024,256]{1,0:T(8,128)(2,1)S(1)}, bf16[1024,256]{1,0:T(8,128)(2,1)S(1)}, u32[]{:S(2)}, u32[]{:S(2)}) collective-permute-start(bf16[1024,256]{1,0:T(8,128)(2,1)S(1)} %get-tuple-element.87), channel_id=1, source_target_pairs={{0,2},{1,3},{6,4},{7,5},{8,10},{9,11},{14,12},{15,13},{16,18},{17,... | collective-permute-start | bytes 1572872 | tf_op jit(solution)/shard_map/ppermute | solution.py:168
  211.9 2.8 collective-permute-start.60
  214.0 11.9 %collective-permute-start.40 = (bf16[1024,256]{1,0:T(8,128)(2,1)S(1)}, bf16[1024,256]{1,0:T(8,128)(2,1)S(1)}, u32[]{:S(2)}, u32[]{:S(2)}) collective-permute-start(bf16[1024,256]{1,0:T(8,128)(2,1)S(1)} %add_convert_fusion.11), channel_id=1, source_target_pairs={{2,4},{3,5},{4,2},{5,3},{10,12},{11,13},{12,10},{13,11},{18,20},{1... | collective-permute-start | bytes 1572872 | tf_op jit(solution)/shard_map/ppermute | solution.py:168
  215.0 21.4 %collective-permute-start.38 = (bf16[1024,256]{1,0:T(8,128)(2,1)S(1)}, bf16[1024,256]{1,0:T(8,128)(2,1)S(1)}, u32[]{:S(2)}, u32[]{:S(2)}) collective-permute-start(bf16[1024,256]{1,0:T(8,128)(2,1)S(1)} %broadcast_select_fusion.9), channel_id=1, source_target_pairs={{0,2},{1,3},{2,0},{3,1},{4,6},{5,7},{6,4},{7,5},{8,10},{9,11},{10,... | collective-permute-start | bytes 1572872 | tf_op jit(solution)/shard_map/ppermute | solution.py:168
  225.2 39.5 %collective-permute-start.45 = (bf16[1024,256]{1,0:T(8,128)(2,1)S(1)}, bf16[1024,256]{1,0:T(8,128)(2,1)S(1)}, u32[]{:S(2)}, u32[]{:S(2)}) collective-permute-start(bf16[1024,256]{1,0:T(8,128)(2,1)S(1)} %add_convert_fusion.8), channel_id=1, source_target_pairs={{2,4},{3,5},{4,2},{5,3},{10,12},{11,13},{12,10},{13,11},{18,20},{1... | collective-permute-start | bytes 1572872 | tf_op jit(solution)/shard_map/ppermute | solution.py:168
  226.1 20.2 %collective-permute-start.41 = (bf16[1024,256]{1,0:T(8,128)(2,1)S(1)}, bf16[1024,256]{1,0:T(8,128)(2,1)S(1)}, u32[]{:S(2)}, u32[]{:S(2)}) collective-permute-start(bf16[1024,256]{1,0:T(8,128)(2,1)S(1)} %broadcast_select_fusion.7), channel_id=1, source_target_pairs={{0,2},{1,3},{2,0},{3,1},{4,6},{5,7},{6,4},{7,5},{8,10},{9,11},{10,... | collective-permute-start | bytes 1572872 | tf_op jit(solution)/shard_map/ppermute | solution.py:168
  237.1 18.1 %collective-permute-start.47 = (bf16[1024,256]{1,0:T(8,128)(2,1)S(1)}, bf16[1024,256]{1,0:T(8,128)(2,1)S(1)}, u32[]{:S(2)}, u32[]{:S(2)}) collective-permute-start(bf16[1024,256]{1,0:T(8,128)(2,1)S(1)} %add_convert_fusion.6), channel_id=1, source_target_pairs={{2,4},{3,5},{4,2},{5,3},{10,12},{11,13},{12,10},{13,11},{18,20},{1... | collective-permute-start | bytes 1572872 | tf_op jit(solution)/shard_map/ppermute | solution.py:168
  246.9 8.3 %collective-permute-start.62 = (bf16[448,256]{1,0:T(8,128)(2,1)S(1)}, bf16[448,256]{1,0:T(8,128)(2,1)S(1)}, u32[]{:S(2)}, u32[]{:S(2)}) collective-permute-start(bf16[448,256]{1,0:T(8,128)(2,1)S(1)} %bitcast.221), channel_id=1, source_target_pairs={{0,1},{1,0},{2,3},{3,2},{4,5},{5,4},{6,7},{7,6},{8,9},{9,8},{10,11... | collective-permute-start | bytes 688136 | tf_op jit(solution)/shard_map/ppermute | solution.py:155
  247.1 14.7 %collective-permute-start.49 = (bf16[1024,256]{1,0:T(8,128)(2,1)S(1)}, bf16[1024,256]{1,0:T(8,128)(2,1)S(1)}, u32[]{:S(2)}, u32[]{:S(2)}) collective-permute-start(bf16[1024,256]{1,0:T(8,128)(2,1)S(1)} %add_convert_fusion.3), channel_id=1, source_target_pairs={{2,4},{3,5},{4,2},{5,3},{10,12},{11,13},{12,10},{13,11},{18,20},{1... | collective-permute-start | bytes 1572872 | tf_op jit(solution)/shard_map/ppermute | solution.py:168
  247.8 13.3 %collective-permute-start.53 = (bf16[1024,128]{1,0:T(8,128)(2,1)S(1)}, bf16[1024,128]{1,0:T(8,128)(2,1)S(1)}, u32[]{:S(2)}, u32[]{:S(2)}) collective-permute-start(bf16[1024,128]{1,0:T(8,128)(2,1)S(1)} %get-tuple-element.92), channel_id=1, source_target_pairs={{0,2},{1,3},{6,4},{7,5},{8,10},{9,11},{14,12},{15,13},{16,18},{17,... | collective-permute-start | bytes 786440 | tf_op jit(solution)/shard_map/ppermute | solution.py:168
  255.4 16.7 %collective-permute-start.48 = (bf16[1024,256]{1,0:T(8,128)(2,1)S(1)}, bf16[1024,256]{1,0:T(8,128)(2,1)S(1)}, u32[]{:S(2)}, u32[]{:S(2)}) collective-permute-start(bf16[1024,256]{1,0:T(8,128)(2,1)S(1)} %add_convert_fusion.4), channel_id=1, source_target_pairs={{2,0},{3,1},{4,6},{5,7},{10,8},{11,9},{12,14},{13,15},{18,16},{19,... | collective-permute-start | bytes 1572872 | tf_op jit(solution)/shard_map/ppermute | solution.py:168
  261.2 2.1 collective-permute-start.54
  262.0 27.4 %collective-permute-start.50 = (bf16[1024,256]{1,0:T(8,128)(2,1)S(1)}, bf16[1024,256]{1,0:T(8,128)(2,1)S(1)}, u32[]{:S(2)}, u32[]{:S(2)}) collective-permute-start(bf16[1024,256]{1,0:T(8,128)(2,1)S(1)} %add_convert_fusion.2), channel_id=1, source_target_pairs={{2,0},{3,1},{4,6},{5,7},{10,8},{11,9},{12,14},{13,15},{18,16},{19,... | collective-permute-start | bytes 1572872 | tf_op jit(solution)/shard_map/ppermute | solution.py:168
  263.4 25.5 %collective-permute-start.55 = (bf16[1024,128]{1,0:T(8,128)(2,1)S(1)}, bf16[1024,128]{1,0:T(8,128)(2,1)S(1)}, u32[]{:S(2)}, u32[]{:S(2)}) collective-permute-start(bf16[1024,128]{1,0:T(8,128)(2,1)S(1)} %add_convert_fusion.14), channel_id=1, source_target_pairs={{2,0},{3,1},{4,6},{5,7},{10,8},{11,9},{12,14},{13,15},{18,16},{19,... | collective-permute-start | bytes 786440 | tf_op jit(solution)/shard_map/ppermute | solution.py:168
  272.8 37.1 %collective-permute-start.64 = (bf16[448,256]{1,0:T(8,128)(2,1)S(1)}, bf16[448,256]{1,0:T(8,128)(2,1)S(1)}, u32[]{:S(2)}, u32[]{:S(2)}) collective-permute-start(bf16[448,256]{1,0:T(8,128)(2,1)S(1)} %bitcast.219), channel_id=1, source_target_pairs={{0,1},{1,0},{2,3},{3,2},{4,5},{5,4},{6,7},{7,6},{8,9},{9,8},{10,11... | collective-permute-start | bytes 688136 | tf_op jit(solution)/shard_map/ppermute | solution.py:155
  272.8 26.3 %collective-permute-start.46 = (bf16[1024,256]{1,0:T(8,128)(2,1)S(1)}, bf16[1024,256]{1,0:T(8,128)(2,1)S(1)}, u32[]{:S(2)}, u32[]{:S(2)}) collective-permute-start(bf16[1024,256]{1,0:T(8,128)(2,1)S(1)} %get-tuple-element.159), channel_id=1, source_target_pairs={{0,2},{1,3},{2,0},{3,1},{4,6},{5,7},{6,4},{7,5},{8,10},{9,11},{10,... | collective-permute-start | bytes 1572872 | tf_op jit(solution)/shard_map/ppermute | solution.py:168
  289.3 52.9 %collective-permute-start.67 = (bf16[448,128]{1,0:T(8,128)(2,1)S(1)}, bf16[448,128]{1,0:T(8,128)(2,1)S(1)}, u32[]{:S(2)}, u32[]{:S(2)}) collective-permute-start(bf16[448,128]{1,0:T(8,128)(2,1)S(1)} %bitcast.225), channel_id=1, source_target_pairs={{0,1},{1,0},{2,3},{3,2},{4,5},{5,4},{6,7},{7,6},{8,9},{9,8},{10,11... | collective-permute-start | bytes 344072 | tf_op jit(solution)/shard_map/ppermute | solution.py:155
  289.8 22.9 %collective-permute-start.65 = (bf16[448,256]{1,0:T(8,128)(2,1)S(1)}, bf16[448,256]{1,0:T(8,128)(2,1)S(1)}, u32[]{:S(2)}, u32[]{:S(2)}) collective-permute-start(bf16[448,256]{1,0:T(8,128)(2,1)S(1)} %bitcast.220), channel_id=1, source_target_pairs={{0,1},{1,0},{2,3},{3,2},{4,5},{5,4},{6,7},{7,6},{8,9},{9,8},{10,11... | collective-permute-start | bytes 688136 | tf_op jit(solution)/shard_map/ppermute | solution.py:155
  299.2 12.0 %collective-permute-start.51 = (bf16[1024,256]{1,0:T(8,128)(2,1)S(1)}, bf16[1024,256]{1,0:T(8,128)(2,1)S(1)}, u32[]{:S(2)}, u32[]{:S(2)}) collective-permute-start(bf16[1024,256]{1,0:T(8,128)(2,1)S(1)} %add_convert_fusion.1), channel_id=1, source_target_pairs={{2,4},{3,5},{4,2},{5,3},{10,12},{11,13},{12,10},{13,11},{18,20},{1... | collective-permute-start | bytes 1572872 | tf_op jit(solution)/shard_map/ppermute | solution.py:168
  299.9 7.7 %collective-permute-start.56 = (bf16[1024,128]{1,0:T(8,128)(2,1)S(1)}, bf16[1024,128]{1,0:T(8,128)(2,1)S(1)}, u32[]{:S(2)}, u32[]{:S(2)}) collective-permute-start(bf16[1024,128]{1,0:T(8,128)(2,1)S(1)} %get-tuple-element.94), channel_id=1, source_target_pairs={{0,2},{1,3},{6,4},{7,5},{8,10},{9,11},{14,12},{15,13},{16,18},{17,... | collective-permute-start | bytes 786440 | tf_op jit(solution)/shard_map/ppermute | solution.py:168
  309.9 20.4 %collective-permute-start.58 = (bf16[1024,128]{1,0:T(8,128)(2,1)S(1)}, bf16[1024,128]{1,0:T(8,128)(2,1)S(1)}, u32[]{:S(2)}, u32[]{:S(2)}) collective-permute-start(bf16[1024,128]{1,0:T(8,128)(2,1)S(1)} %add_convert_fusion.12), channel_id=1, source_target_pairs={{2,0},{3,1},{4,6},{5,7},{10,8},{11,9},{12,14},{13,15},{18,16},{19,... | collective-permute-start | bytes 786440 | tf_op jit(solution)/shard_map/ppermute | solution.py:168
  311.4 28.8 %collective-permute-start.52 = (bf16[1024,256]{1,0:T(8,128)(2,1)S(1)}, bf16[1024,256]{1,0:T(8,128)(2,1)S(1)}, u32[]{:S(2)}, u32[]{:S(2)}) collective-permute-start(bf16[1024,256]{1,0:T(8,128)(2,1)S(1)} %add_convert_fusion), channel_id=1, source_target_pairs={{2,0},{3,1},{4,6},{5,7},{10,8},{11,9},{12,14},{13,15},{18,16},{19,... | collective-permute-start | bytes 1572872 | tf_op jit(solution)/shard_map/ppermute | solution.py:168
  (33 other events, 355.6 us)

commit v4 on v3

--- a/solution.py
+++ b/solution.py
@@ -8,10 +8,10 @@
 from jax.sharding import PartitionSpec as P
 
 EXP_DEV = 1
-GROUPS = ((1,), (1, 2), (2, 2), (2, 2), (2, 1, 1))
+GROUPS = ((1,), (1,), (1, 1), (1, 1), (1, 1))
 UNITS = sum(map(sum, GROUPS))
 DELAY = 3
-VMEM_BYTES = 48 * 1024 * 1024
+VMEM_BYTES = 60 * 1024 * 1024
 
 
 def conv_kernel(tile, out_grad, gate_in, conv_in, scan_grad, taps, bias, skip, turned, flat):
@@ -61,22 +61,22 @@
         turned[pl.ds(at, tile), :] = flat[:, pl.ds(at, tile)].T
 
 
-def conv_grad(part, parts, out_grad, gate_in, conv_in, scan_grad, taps_half, bias_half, skip):
+def conv_grad(out_grad, gate_in, conv_in, scan_grad, taps_half, bias_half, skip):
     channels, length = out_grad.shape
-    block = channels // parts
+    block = min(128, channels)
     tile = min(512, length)
-    whole = pl.BlockSpec((block, length), lambda step: (part, 0))
-    column = pl.BlockSpec((block, 1), lambda step: (part, 0))
+    whole = pl.BlockSpec((block, length), lambda step: (step, 0))
+    column = pl.BlockSpec((block, 1), lambda step: (step, 0))
     return pl.pallas_call(
         functools.partial(conv_kernel, tile),
-        grid=(1,),
-        in_specs=[whole] * 4 + [pl.BlockSpec((block, taps_half.shape[1]), lambda step: (part, 0)), column, column],
-        out_specs=pl.BlockSpec((length, block), lambda step: (0, 0)),
-        out_shape=jax.ShapeDtypeStruct((length, block), jnp.bfloat16),
+        grid=(channels // block,),
+        in_specs=[whole] * 4 + [pl.BlockSpec((block, taps_half.shape[1]), lambda step: (step, 0)), column, column],
+        out_specs=pl.BlockSpec((length, block), lambda step: (0, step)),
+        out_shape=jax.ShapeDtypeStruct((length, channels), jnp.bfloat16),
         scratch_shapes=[pltpu.VMEM((block, length), jnp.bfloat16)],
         compiler_params=pltpu.CompilerParams(vmem_limit_bytes=VMEM_BYTES),
         cost_estimate=pl.CostEstimate(
-            flops=40 * block * length, bytes_accessed=10 * block * length, transcendentals=2 * block * length
+            flops=40 * channels * length, bytes_accessed=10 * channels * length, transcendentals=2 * channels * length
         ),
         name="conv_grad",
     )(out_grad, gate_in, conv_in, scan_grad, taps_half, bias_half, skip)
@@ -180,23 +180,33 @@
     first = sum(widths[0])
     rights = [spread(jnp.concatenate(both_cores(projection, 0, first), axis=0))]
 
-    parts = 2 if channels % 256 == 0 else 1
-    conv_args = [0.5 * conv_weight.T, 0.5 * conv_bias[:, None], skip_scale[:, None]]
+    turned = conv_grad(
+        out_grad,
+        gate_in,
+        conv_in,
+        scan_grad,
+        0.5 * conv_weight.T,
+        0.5 * conv_bias[:, None],
+        skip_scale[:, None],
+    )
+    turned, rights[0], projection, resid_grad, routes = lax.optimization_barrier(
+        (turned, rights[0], projection, resid_grad, routes)
+    )
     lefts = []
-    routed = None
-    packed = jnp.concatenate([routes.T.astype(jnp.float32), gate_probs.T], axis=0)
-    for part in range(parts):
-        if part == parts - 1:
-            scan_grad, rights[0] = lax.optimization_barrier((scan_grad, rights[0]))
-        turned = conv_grad(part, parts, out_grad, gate_in, conv_in, scan_grad, *conv_args)
-        mine = [lax.dynamic_slice_in_dim(turned, (ctx_at ^ offset) * window, window, 0) for offset in range(ctx_count)]
-        mine = mine[:1] + [to_ctx(mine[offset], offset) for offset in range(1, ctx_count)]
-        if part == parts - 1:
-            packed, projection, resid_grad, turned = lax.optimization_barrier((packed, projection, resid_grad, turned))
-            routed = lax.all_gather(packed, "exp", axis=0, tiled=False)
-            routed, mine[0] = lax.optimization_barrier((routed, mine[0]))
-        for piece in mine:
-            lefts.append((piece, to_core(piece)))
+    for offset in range(ctx_count):
+        piece = lax.dynamic_slice_in_dim(turned, (ctx_at ^ offset) * window, window, 0)
+        if offset:
+            piece = to_ctx(piece, offset)
+        lefts += [piece, to_core(piece)]
+
+    routed = jnp.concatenate([routes.T.astype(jnp.float32), gate_probs.T], axis=0)[None]
+    offset = 1
+    while offset < exp_count:
+        other = lax.ppermute(routed, "exp", [(place, place ^ offset) for place in range(exp_count)])
+        routed = jnp.concatenate([routed, other], axis=0)
+        offset *= 2
+    order = (jnp.arange(exp_count)[:, None] ^ exp_at) == jnp.arange(exp_count)[None, :]
+    routed = jnp.sum(jnp.where(order[:, :, None, None], routed[None], 0.0), axis=1)
 
     rest_here, rest_there = both_cores(projection, first, half - first)
     for group, at in list(zip(widths, starts))[1:]:
@@ -226,20 +236,11 @@
     picks = picks.astype(jnp.bfloat16)
     picks, scale, lefts = lax.optimization_barrier((picks, scale, lefts))
 
-    lefts = [
-        lefts[part * ctx_count + offset][core]
-        for offset in range(ctx_count)
-        for core in (0, 1)
-        for part in range(parts)
-    ]
     if channels < 128:
         lefts = [jnp.concatenate(lefts, axis=1)]
         rights = [[jnp.concatenate(chunk, axis=0)] for chunk in rights]
     place = chip_at.astype(jnp.int32).reshape(1)
-    own = []
-    for group, at, right in zip(widths, starts, rights):
-        own += matmul(lefts, right, resid[:, at : at + sum(group)], place, group)
-    pieces = len(own)
+    pieces = sum(map(len, GROUPS))
 
     middle = chips // 2
     distance = jnp.minimum(chip_at, chips - 1 - chip_at)
@@ -256,34 +257,44 @@
         rows_got.append(to_core(rows[1]))
 
     hops = middle - 1
-    sums = [list(own)] + [[None] * pieces for _ in range(hops)]
+    sums = [[None] * pieces for _ in range(hops + 1)]
     ready = [[None] * pieces for _ in range(hops + 1)]
     lag = DELAY - 1
     last = pieces + lag * hops + DELAY * hops
+    group_at = 0
+    first_of = [sum(map(len, GROUPS[:at])) for at in range(len(GROUPS))]
     for step in range(last + 1):
+        if group_at < len(GROUPS) and first_of[group_at] == step:
+            if step >= 2:
+                sums[1][step - 2], place = lax.optimization_barrier((sums[1][step - 2], place))
+            group, at = widths[group_at], starts[group_at]
+            products = matmul(lefts, rights[group_at], resid[:, at : at + sum(group)], place, group)
+            sums[0][step : step + len(group)] = products
+            group_at += 1
         for hop in range(hops):
             inward = step - lag * hop
             outward = inward - DELAY - 2 * lag * (hops - 1 - hop)
             send_in = 0 <= inward < pieces
             send_out = 0 <= outward < pieces
+            if not (send_in or send_out):
+                continue
             if send_in and 0 <= inward - 2:
                 sums[hop][inward], sums[hop + 1][inward - 2] = lax.optimization_barrier(
                     (sums[hop][inward], sums[hop + 1][inward - 2])
                 )
             rising = sums[hop][inward] if send_in else None
             falling = ready[hop + 1][outward] if send_out else None
-            if send_in and send_out and rising.shape == falling.shape:
-                got_in = got_out = swap_chips(jnp.where(distance == hop, rising, falling), hop)
+            if send_in and send_out:
+                got = swap_chips(jnp.where(distance == hop, rising, falling), hop)
             else:
-                got_in = swap_chips(rising, hop, True, False) if send_in else None
-                got_out = swap_chips(falling, hop, False, True) if send_out else None
+                got = swap_chips(rising if send_in else falling, hop, send_in, send_out)
             if send_in:
-                sums[hop + 1][inward] = add(rising, got_in)
+                sums[hop + 1][inward] = add(rising, got)
                 if hop == hops - 1:
                     crossed = swap_chips(sums[hop + 1][inward], middle - 1)
                     ready[hops][inward] = add(sums[hop + 1][inward], crossed)
             if send_out:
-                ready[hop][outward] = jnp.where(distance == hop, got_out, falling)
+                ready[hop][outward] = jnp.where(distance == hop, got, falling)
                 if hop == 0:
                     finish(ready[0][outward])
     result = jnp.where(

time: 348 us -> 248 us (0.71)
  starting transfers between devices: 107 us -> 57 us
  waiting for transfers between devices: 142 us -> 95.3 us
  blocking collectives: 13.3 us -> 0 us
  other arithmetic: 13.9 us -> 22.9 us
  Pallas kernels: 40 us -> 47.8 us
  local copies, waits for them, and re-layouts: 25.3 us -> 20.1 us
    ppermute x27 -> x19, starting transfers between devices: 73.4 us -> 29.1 us  [swap_chips(): return lax.ppermute(array, 'exp', sorted(pairs))]
    ppermute x27 -> x19, waiting for transfers between devices: 90.2 us -> 64.6 us  [swap_chips(): return lax.ppermute(array, 'exp', sorted(pairs))]
    ppermute x21 -> x18, waiting for transfers between devices: 48.9 us -> 25.3 us  [to_ctx(): lax.ppermute(array, 'ctx', [(place, place ^ offset) for place in range(ct...]
    all_gather x1 -> x0, blocking collectives: 13.3 us -> none  [on_device(): routed = lax.all_gather(packed, 'exp', axis=0, tiled=False)]
    pallas_call x5, Pallas kernels: 22.2 us -> 29.8 us  [matmul(): pl.pallas_call(functools.partial(matmul_kernel, len(lefts), len(rights)),...]
    select_n x12 -> x13, other arithmetic: 1.56 us -> 9.1 us  [the longest x5 4.71 us: on_device(): got = swap_chips(jnp.where(distance == hop, rising, falling), hop)]
    ppermute x21 -> x18, starting transfers between devices: 28.9 us -> 21.9 us  [to_ctx(): lax.ppermute(array, 'ctx', [(place, place ^ offset) for place in range(ct...]
    unnamed x86 -> x82, local copies, waits for them, and re-layouts: 10 us -> 3.62 us
  transfers between devices with their start and end apart: 69 -> 55, of which waited for: 27 -> 18; matrix products, arithmetic and copies ran while one was open for 8% -> 16% of each run, Pallas kernels for 12% -> 19%
where the time goes in v4:
time: 248 us; the launch traced here: 246 us
  waiting for transfers between devices  95.3 us (38%)
  starting transfers between devices  57 us (23%)
  Pallas kernels  47.8 us (19%)
  other arithmetic  22.9 us (9%)
  local copies, waits for them, and re-layouts  20.1 us (8%)
    ppermute x19, waiting for transfers between devices, swap_chips(): return lax.ppermute(array, 'exp', sorted(pairs))  64.6 us
    pallas_call x5, Pallas kernels, matmul(): pl.pallas_call(functools.partial(matmul_kernel, len(lefts), len(rights)),...  29.8 us
    ppermute x19, starting transfers between devices, swap_chips(): return lax.ppermute(array, 'exp', sorted(pairs))  29.1 us
    ppermute x18, waiting for transfers between devices, to_ctx(): lax.ppermute(array, 'ctx', [(place, place ^ offset) for place in range(ct...  25.3 us
    ppermute x18, starting transfers between devices, to_ctx(): lax.ppermute(array, 'ctx', [(place, place ^ offset) for place in range(ct...  21.9 us
    pallas_call x1, Pallas kernels, conv_grad(): pl.pallas_call(functools.partial(conv_kernel, tile), grid=(channels // bl...  18 us
  transfers between devices with their start and end apart: 55, of which 18 were waited for; matrix products, arithmetic and copies ran while one was open for 16% of the time, Pallas kernels for 19%

profile of v4, /device:TPU:0, one launch (start us, length us, event | category | flops | bytes accessed | tf_op | source)
XLA Modules:
  0.0 246.4 jit_solution(4601843128554837324)
XLA Ops:
  0.0 1.0 constant_dynamic-slice_fusion.12
  3.0 3.5 %collective-permute-start.3 = (bf16[512,256]{1,0:T(8,128)(2,1)S(1)}, bf16[512,256]{1,0:T(8,128)(2,1)S(1)}, u32[]{:S(2)}, u32[]{:S(2)}) collective-permute-start(bf16[512,256]{1,0:T(8,128)(2,1)S(1)} %pad_maximum_fusion.3.refs_8_), channel_id=1, source_target_pairs={{0,24},{8,16},{16,8},{24,0},{1,25},{9,17},{17,9},{25,1},{2,26},{10... | collective-permute-start | bytes 786440 | tf_op jit(solution)/shard_map/ppermute | solution.py:158
  8.8 1.5 copy.32.skip
  10.3 18.0 %conv_grad.1 = bf16[4096,256]{1,0:T(8,128)(2,1)} custom-call(bf16[256,4096]{1,0:T(8,128)(2,1)} %out_grad.1, bf16[256,4096]{1,0:T(8,128)(2,1)} %gate_in.1, bf16[256,4096]{1,0:T(8,128)(2,1)} %conv_in.1, bf16[256,4096]{1,0:T(8,128)(2,1)} %scan_grad.1, f32[256,4]{1,0:T(8,128)} %bitcast.178, f32[256,1]{1,0:T(8,128)} %copy.31.bias, f32[256,1]{1,0:T(8,128)} %copy.32.skip), custom_call_target="tpu_custom_call" | custom-call | flops 41943040 | bytes 10485760 | tf_op jit(solution)/shard_map/conv_grad/pallas_call | solution.py:70
  28.5 2.6 %constant_dynamic-slice_fusion.3 = bf16[256,1792]{1,0:T(8,128)(2,1)} fusion(bf16[256,4096]{1,0:T(8,128)(2,1)} %param.18, s32[]{:T(128)S(6)} %select_n.164), kind=kLoop, calls=%fused_computation.108 | loop fusion | bytes 1835012 | tf_op jit(solution)/shard_map/dynamic_slice | solution.py:171
  31.3 0.9 constant_dynamic-slice_fusion.6
  32.2 1.2 constant_dynamic-slice_fusion.7
  33.4 2.8 %collective-permute-start.12 = (bf16[1024,256]{1,0:T(8,128)(2,1)}, bf16[1024,256]{1,0:T(8,128)(2,1)S(1)}, u32[]{:S(2)}, u32[]{:S(2)}) collective-permute-start(bf16[1024,256]{1,0:T(8,128)(2,1)} %get-tuple-element.68), channel_id=1, source_target_pairs={{0,24},{8,16},{16,8},{24,0},{1,25},{9,17},{17,9},{25,1},{2,26},{10... | collective-permute-start | bytes 1572872 | tf_op jit(solution)/shard_map/ppermute | solution.py:158
  36.8 1.6 collective-permute-start.5
  38.3 1.2 constant_dynamic-slice_fusion.4
  40.4 2.6 %collective-permute-start.6 = (f32[4,4,128]{2,1,0:T(4,128)S(1)}, f32[4,4,128]{2,1,0:T(4,128)S(1)}, u32[]{:S(2)}, u32[]{:S(2)}) collective-permute-start(f32[4,4,128]{2,1,0:T(4,128)S(1)} %pad_maximum_fusion.6), channel_id=1, source_target_pairs={{0,4},{1,5},{2,6},{3,7},{4,0},{5,1},{6,2},{7,3},{8,12},{9,13},{10,... | collective-permute-start | bytes 24584 | tf_op jit(solution)/shard_map/ppermute | solution.py:205
  43.0 0.9 constant_dynamic-slice_fusion.1
  44.0 1.0 collective-permute-done.6
  46.6 2.8 %collective-permute-done.12.refs_6_ = bf16[1024,256]{1,0:T(8,128)(2,1)S(1)} collective-permute-done((bf16[1024,256]{1,0:T(8,128)(2,1)}, bf16[1024,256]{1,0:T(8,128)(2,1)S(1)}, u32[]{:S(2)}, u32[]{:S(2)}) %collective-permute-start.12) | collective-permute-done | bytes 524320 | tf_op jit(solution)/shard_map/ppermute | solution.py:158
  49.4 10.8 %collective-permute-done.10.refs_4_ = bf16[1024,256]{1,0:T(8,128)(2,1)S(1)} collective-permute-done((bf16[1024,256]{1,0:T(8,128)(2,1)}, bf16[1024,256]{1,0:T(8,128)(2,1)S(1)}, u32[]{:S(2)}, u32[]{:S(2)}) %collective-permute-start.10) | collective-permute-done | bytes 524320 | tf_op jit(solution)/shard_map/ppermute | solution.py:158
  60.7 1.6 maximum_select_fusion
  63.0 1.0 fusion.22
  64.0 0.9 slice.145
  65.0 1.9 collective-permute-start.22
  66.9 1.3 collective-permute-start.21
  70.6 5.3 %partial_product.5 = bf16[1024,256]{1,0:T(8,128)(2,1)} custom-call(s32[1]{0:T(128)} %bitcast.place, bf16[1024,256]{1,0:T(8,128)(2,1)} %copy-done.1, bf16[1024,256]{1,0:T(8,128)(2,1)} %copy-done.4, bf16[1024,256]{1,0:T(8,128)(2,1)} %collective-permute-done.8.refs_2_, bf16[1024,256]{1,0:T(8,128)(2,1)} %copy-done.7, bf16[1024,256]{1,0:T(8,128)(2,1)} %copy-done.3, ...), custom_call_target="tpu_custom_call" | custom-call | flops 1073741824 | bytes 5767168 | tf_op jit(solution)/shard_map/partial_product/pallas_call | solution.py:107
  75.9 4.3 %collective-permute-start.15 = (bf16[1024,256]{1,0:T(8,128)(2,1)}, bf16[1024,256]{1,0:T(8,128)(2,1)}, u32[]{:S(2)}, u32[]{:S(2)}) collective-permute-start(bf16[1024,256]{1,0:T(8,128)(2,1)} %partial_product.5), channel_id=1, source_target_pairs={{0,2},{1,3},{6,4},{7,5},{8,10},{9,11},{14,12},{15,13},{16,18},{17,... | collective-permute-start | bytes 1572872 | tf_op jit(solution)/shard_map/ppermute | solution.py:168
  80.2 1.2 fusion.24
  82.2 1.5 collective-permute-start.19
  83.7 1.2 collective-permute-start.18
  87.3 5.2 %partial_product.7 = bf16[1024,256]{1,0:T(8,128)(2,1)} custom-call(s32[1]{0:T(128)} %bitcast.place, bf16[1024,256]{1,0:T(8,128)(2,1)} %copy-done.1, bf16[1024,256]{1,0:T(8,128)(2,1)} %copy-done.4, bf16[1024,256]{1,0:T(8,128)(2,1)} %collective-permute-done.8.refs_2_, bf16[1024,256]{1,0:T(8,128)(2,1)} %copy-done.7, bf16[1024,256]{1,0:T(8,128)(2,1)} %copy-done.3, ...), custom_call_target="tpu_custom_call" | custom-call | flops 1073741824 | bytes 5767168 | tf_op jit(solution)/shard_map/partial_product/pallas_call | solution.py:107
  92.5 1.3 collective-permute-start.23
  93.8 1.2 add_convert_fusion.15
  96.6 1.7 collective-permute-done.19.refs_11_
  98.3 1.5 collective-permute-start.29
  99.8 9.7 %collective-permute-done.18.refs_10_ = bf16[512,512]{1,0:T(8,128)(2,1)} collective-permute-done((bf16[512,512]{1,0:T(8,128)(2,1)}, bf16[512,512]{1,0:T(8,128)(2,1)}, u32[]{:S(2)}, u32[]{:S(2)}) %collective-permute-start.18) | collective-permute-done | bytes 524320 | tf_op jit(solution)/shard_map/ppermute | solution.py:158
  109.5 1.2 collective-permute-start.28
  111.5 6.5 %partial_product.6 = (bf16[1024,256]{1,0:T(8,128)(2,1)}, bf16[1024,256]{1,0:T(8,128)(2,1)}) custom-call(s32[1]{0:T(128)} %bitcast.place, bf16[1024,256]{1,0:T(8,128)(2,1)} %copy-done.1, bf16[1024,256]{1,0:T(8,128)(2,1)} %copy-done.4, bf16[1024,256]{1,0:T(8,128)(2,1)} %collective-permute-done.8.refs_2_, bf16[1024,256]{1,0:T(8,128)(2,1)} %copy-done.7, ...), custom_call_target="tpu_custom_call" | custom-call | flops 2147483648 | bytes 7340032 | tf_op jit(solution)/shard_map/partial_product/pallas_call | solution.py:107
  118.0 1.5 collective-permute-start.26
  120.3 2.1 broadcast_select_fusion.13
  122.4 8.3 %collective-permute-done.26 = bf16[1024,256]{1,0:T(8,128)(2,1)S(1)} collective-permute-done((bf16[1024,256]{1,0:T(8,128)(2,1)}, bf16[1024,256]{1,0:T(8,128)(2,1)S(1)}, u32[]{:S(2)}, u32[]{:S(2)}) %collective-permute-start.26) | collective-permute-done | bytes 524320 | tf_op jit(solution)/shard_map/ppermute | solution.py:168
  130.7 2.4 collective-permute-start.25
  133.2 1.5 collective-permute-start.36
  134.7 1.2 collective-permute-start.35
  136.8 6.4 %partial_product.8 = (bf16[1024,256]{1,0:T(8,128)(2,1)}, bf16[1024,256]{1,0:T(8,128)(2,1)}) custom-call(s32[1]{0:T(128)} %bitcast.place, bf16[1024,256]{1,0:T(8,128)(2,1)} %copy-done.1, bf16[1024,256]{1,0:T(8,128)(2,1)} %copy-done.4, bf16[1024,256]{1,0:T(8,128)(2,1)} %collective-permute-done.8.refs_2_, bf16[1024,256]{1,0:T(8,128)(2,1)} %copy-done.7, ...), custom_call_target="tpu_custom_call" | custom-call | flops 2147483648 | bytes 7340032 | tf_op jit(solution)/shard_map/partial_product/pallas_call | solution.py:107
  144.1 1.2 broadcast_select_fusion.11
  145.3 1.8 collective-permute-start.31
  147.2 1.2 broadcast_select_fusion.12
  148.4 1.2 add_convert_fusion.10
  151.3 1.0 broadcast_select_fusion.9
  152.4 4.5 %collective-permute-done.31 = bf16[1024,256]{1,0:T(8,128)(2,1)S(1)} collective-permute-done((bf16[1024,256]{1,0:T(8,128)(2,1)S(1)}, bf16[1024,256]{1,0:T(8,128)(2,1)S(1)}, u32[]{:S(2)}, u32[]{:S(2)}) %collective-permute-start.31) | collective-permute-done | bytes 524320 | tf_op jit(solution)/shard_map/ppermute | solution.py:168
  156.9 1.2 broadcast_select_fusion.10
  159.4 4.7 %collective-permute-start.33 = (bf16[1024,256]{1,0:T(8,128)(2,1)}, bf16[1024,256]{1,0:T(8,128)(2,1)}, u32[]{:S(2)}, u32[]{:S(2)}) collective-permute-start(bf16[1024,256]{1,0:T(8,128)(2,1)} %broadcast_select_fusion.9), channel_id=1, source_target_pairs={{0,2},{1,3},{2,0},{3,1},{4,6},{5,7},{6,4},{7,5},{8,10},{9,11},{10,... | collective-permute-start | bytes 1572872 | tf_op jit(solution)/shard_map/ppermute | solution.py:168
  165.0 6.4 %partial_product.9 = (bf16[1024,256]{1,0:T(8,128)(2,1)}, bf16[1024,256]{1,0:T(8,128)(2,1)}) custom-call(s32[1]{0:T(128)} %bitcast.place, bf16[1024,256]{1,0:T(8,128)(2,1)} %copy-done.1, bf16[1024,256]{1,0:T(8,128)(2,1)} %copy-done.4, bf16[1024,256]{1,0:T(8,128)(2,1)} %collective-permute-done.8.refs_2_, bf16[1024,256]{1,0:T(8,128)(2,1)} %copy-done.7, ...), custom_call_target="tpu_custom_call" | custom-call | flops 2147483648 | bytes 7340032 | tf_op jit(solution)/shard_map/partial_product/pallas_call | solution.py:107
  171.7 1.4 collective-permute-done.48
  173.2 3.8 %collective-permute-done.33 = bf16[1024,256]{1,0:T(8,128)(2,1)} collective-permute-done((bf16[1024,256]{1,0:T(8,128)(2,1)}, bf16[1024,256]{1,0:T(8,128)(2,1)}, u32[]{:S(2)}, u32[]{:S(2)}) %collective-permute-start.33) | collective-permute-done | bytes 524320 | tf_op jit(solution)/shard_map/ppermute | solution.py:168
  177.0 1.4 broadcast_select_fusion.8
  178.8 1.2 add_convert_fusion.6
  180.9 3.3 %collective-permute-start.38 = (bf16[1024,256]{1,0:T(8,128)(2,1)S(1)}, bf16[1024,256]{1,0:T(8,128)(2,1)S(1)}, u32[]{:S(2)}, u32[]{:S(2)}) collective-permute-start(bf16[1024,256]{1,0:T(8,128)(2,1)S(1)} %broadcast_select_fusion.7), channel_id=1, source_target_pairs={{0,2},{1,3},{2,0},{3,1},{4,6},{5,7},{6,4},{7,5},{8,10},{9,11},{10,... | collective-permute-start | bytes 1572872 | tf_op jit(solution)/shard_map/ppermute | solution.py:168
  184.7 1.3 collective-permute-start.42
  186.0 10.9 %collective-permute-done.38 = bf16[1024,256]{1,0:T(8,128)(2,1)S(1)} collective-permute-done((bf16[1024,256]{1,0:T(8,128)(2,1)S(1)}, bf16[1024,256]{1,0:T(8,128)(2,1)S(1)}, u32[]{:S(2)}, u32[]{:S(2)}) %collective-permute-start.38) | collective-permute-done | bytes 524320 | tf_op jit(solution)/shard_map/ppermute | solution.py:168
  198.4 9.8 %collective-permute-done.40 = bf16[1024,256]{1,0:T(8,128)(2,1)S(1)} collective-permute-done((bf16[1024,256]{1,0:T(8,128)(2,1)S(1)}, bf16[1024,256]{1,0:T(8,128)(2,1)S(1)}, u32[]{:S(2)}, u32[]{:S(2)}) %collective-permute-start.40) | collective-permute-done | bytes 524320 | tf_op jit(solution)/shard_map/ppermute | solution.py:168
  210.4 1.3 collective-permute-start.44
  211.7 7.7 %collective-permute-done.42 = bf16[1024,256]{1,0:T(8,128)(2,1)S(1)} collective-permute-done((bf16[1024,256]{1,0:T(8,128)(2,1)S(1)}, bf16[1024,256]{1,0:T(8,128)(2,1)S(1)}, u32[]{:S(2)}, u32[]{:S(2)}) %collective-permute-start.42) | collective-permute-done | bytes 524320 | tf_op jit(solution)/shard_map/ppermute | solution.py:168
  220.0 1.3 collective-permute-start.46
  221.4 9.5 %collective-permute-done.44 = bf16[1024,256]{1,0:T(8,128)(2,1)S(1)} collective-permute-done((bf16[1024,256]{1,0:T(8,128)(2,1)S(1)}, bf16[1024,256]{1,0:T(8,128)(2,1)S(1)}, u32[]{:S(2)}, u32[]{:S(2)}) %collective-permute-start.44) | collective-permute-done | bytes 524320 | tf_op jit(solution)/shard_map/ppermute | solution.py:168
  231.4 10.1 %collective-permute-done.46 = bf16[1024,256]{1,0:T(8,128)(2,1)S(1)} collective-permute-done((bf16[1024,256]{1,0:T(8,128)(2,1)S(1)}, bf16[1024,256]{1,0:T(8,128)(2,1)S(1)}, u32[]{:S(2)}, u32[]{:S(2)}) %collective-permute-start.46) | collective-permute-done | bytes 524320 | tf_op jit(solution)/shard_map/ppermute | solution.py:168
  242.0 1.4 collective-permute-done.54
  244.2 2.2 broadcast_select_fusion
  (224 shorter events, 31.4 us)
Async XLA Ops:
  1.0 2.0 collective-permute-start
  3.0 25.3 %copy-start.17 = (bf16[512,256]{1,0:T(8,128)(2,1)}, bf16[512,256]{1,0:T(8,128)(2,1)S(1)}, u32[]{:S(2)}) copy-start(bf16[512,256]{1,0:T(8,128)(2,1)S(1)} %pad_maximum_fusion.3.refs_8_) | copy-start | bytes 786436
  3.0 25.4 %collective-permute-start.3 = (bf16[512,256]{1,0:T(8,128)(2,1)S(1)}, bf16[512,256]{1,0:T(8,128)(2,1)S(1)}, u32[]{:S(2)}, u32[]{:S(2)}) collective-permute-start(bf16[512,256]{1,0:T(8,128)(2,1)S(1)} %pad_maximum_fusion.3.refs_8_), channel_id=1, source_target_pairs={{0,24},{8,16},{16,8},{24,0},{1,25},{9,17},{17,9},{25,1},{2,26},{10... | collective-permute-start | bytes 786440 | tf_op jit(solution)/shard_map/ppermute | solution.py:158
  6.5 21.8 %collective-permute-start.2 = (bf16[512,256]{1,0:T(8,128)(2,1)S(1)}, bf16[512,256]{1,0:T(8,128)(2,1)S(1)}, u32[]{:S(2)}, u32[]{:S(2)}) collective-permute-start(bf16[512,256]{1,0:T(8,128)(2,1)S(1)} %pad_maximum_fusion.3.refs_8_), channel_id=1, source_target_pairs={{0,16},{8,24},{16,0},{24,8},{1,17},{9,25},{17,1},{25,9},{2,18},{10... | collective-permute-start | bytes 786440 | tf_op jit(solution)/shard_map/ppermute | solution.py:158
  7.0 21.4 %collective-permute-start.1 = (bf16[512,256]{1,0:T(8,128)(2,1)S(1)}, bf16[512,256]{1,0:T(8,128)(2,1)S(1)}, u32[]{:S(2)}, u32[]{:S(2)}) collective-permute-start(bf16[512,256]{1,0:T(8,128)(2,1)S(1)} %pad_maximum_fusion.3.refs_8_), channel_id=1, source_target_pairs={{0,8},{8,0},{16,24},{24,16},{1,9},{9,1},{17,25},{25,17},{2,10},{10... | collective-permute-start | bytes 786440 | tf_op jit(solution)/shard_map/ppermute | solution.py:158
  10.3 18.1 %copy-start.27 = (s32[128,2]{0,1:T(2,128)S(1)}, s32[128,2]{0,1:T(2,128)}, u32[]{:S(2)}) copy-start(s32[128,2]{0,1:T(2,128)} %param.20) | copy-start | bytes 3076
  10.3 18.1 %copy-start.28 = (f32[128,2]{0,1:T(2,128)S(1)}, f32[128,2]{0,1:T(2,128)}, u32[]{:S(2)}) copy-start(f32[128,2]{0,1:T(2,128)} %param.21) | copy-start | bytes 3076
  10.3 21.0 %copy-start.19 = (bf16[128,4096]{1,0:T(8,128)(2,1)S(1)}, bf16[128,4096]{1,0:T(8,128)(2,1)}, u32[]{:S(2)}) copy-start(bf16[128,4096]{1,0:T(8,128)(2,1)} %param.19) | copy-start | bytes 3145732
  28.5 8.3 %collective-permute-start.4 = (f32[1,4,128]{2,1,0:T(4,128)S(1)}, f32[1,4,128]{2,1,0:T(4,128)S(1)}, u32[]{:S(2)}, u32[]{:S(2)}) collective-permute-start(f32[1,4,128]{2,1,0:T(4,128)S(1)} %maximum_bitcast_fusion), channel_id=1, source_target_pairs={{0,1},{1,0},{2,3},{3,2},{4,5},{5,4},{6,7},{7,6},{8,9},{9,8},{10,11... | collective-permute-start | bytes 6152 | tf_op jit(solution)/shard_map/ppermute | solution.py:205
  31.1 32.9 %collective-permute-start.16 = (bf16[256,1792]{1,0:T(8,128)(2,1)}, bf16[256,1792]{1,0:T(8,128)(2,1)}, u32[]{:S(2)}, u32[]{:S(2)}) collective-permute-start(bf16[256,1792]{1,0:T(8,128)(2,1)} %constant_dynamic-slice_fusion.3), channel_id=1, source_target_pairs={{0,1},{1,0},{2,3},{3,2},{4,5},{5,4},{6,7},{7,6},{8,9},{9,8},{10,11... | collective-permute-start | bytes 2752520 | tf_op jit(solution)/shard_map/ppermute | solution.py:155
  33.4 31.5 %copy-start.1 = (bf16[1024,256]{1,0:T(8,128)(2,1)}, bf16[1024,256]{1,0:T(8,128)(2,1)S(1)}, u32[]{:S(2)}) copy-start(bf16[1024,256]{1,0:T(8,128)(2,1)S(1)} %get-tuple-element.37.refs_0_) | copy-start | bytes 1572868
  33.4 15.9 %collective-permute-start.12 = (bf16[1024,256]{1,0:T(8,128)(2,1)}, bf16[1024,256]{1,0:T(8,128)(2,1)S(1)}, u32[]{:S(2)}, u32[]{:S(2)}) collective-permute-start(bf16[1024,256]{1,0:T(8,128)(2,1)} %get-tuple-element.68), channel_id=1, source_target_pairs={{0,24},{8,16},{16,8},{24,0},{1,25},{9,17},{17,9},{25,1},{2,26},{10... | collective-permute-start | bytes 1572872 | tf_op jit(solution)/shard_map/ppermute | solution.py:158
  36.2 24.0 %collective-permute-start.10 = (bf16[1024,256]{1,0:T(8,128)(2,1)}, bf16[1024,256]{1,0:T(8,128)(2,1)S(1)}, u32[]{:S(2)}, u32[]{:S(2)}) collective-permute-start(bf16[1024,256]{1,0:T(8,128)(2,1)} %get-tuple-element.69), channel_id=1, source_target_pairs={{0,16},{8,24},{16,0},{24,8},{1,17},{9,25},{17,1},{25,9},{2,18},{10... | collective-permute-start | bytes 1572872 | tf_op jit(solution)/shard_map/ppermute | solution.py:158
  36.8 3.6 %collective-permute-start.5 = (f32[2,4,128]{2,1,0:T(4,128)S(1)}, f32[2,4,128]{2,1,0:T(4,128)S(1)}, u32[]{:S(2)}, u32[]{:S(2)}) collective-permute-start(f32[2,4,128]{2,1,0:T(4,128)S(1)} %pad_maximum_fusion.7), channel_id=1, source_target_pairs={{0,2},{1,3},{2,0},{3,1},{4,6},{5,7},{6,4},{7,5},{8,10},{9,11},{10,... | collective-permute-start | bytes 12296 | tf_op jit(solution)/shard_map/ppermute | solution.py:205
  40.4 4.5 %collective-permute-start.6 = (f32[4,4,128]{2,1,0:T(4,128)S(1)}, f32[4,4,128]{2,1,0:T(4,128)S(1)}, u32[]{:S(2)}, u32[]{:S(2)}) collective-permute-start(f32[4,4,128]{2,1,0:T(4,128)S(1)} %pad_maximum_fusion.6), channel_id=1, source_target_pairs={{0,4},{1,5},{2,6},{3,7},{4,0},{5,1},{6,2},{7,3},{8,12},{9,13},{10,... | collective-permute-start | bytes 24584 | tf_op jit(solution)/shard_map/ppermute | solution.py:205
  43.9 2.6 %collective-permute-start.14 = (bf16[128,2048]{1,0:T(8,128)(2,1)}, bf16[128,2048]{1,0:T(8,128)(2,1)}, u32[]{:S(2)}, u32[]{:S(2)}) collective-permute-start(bf16[128,2048]{1,0:T(8,128)(2,1)} %get-tuple-element.80), channel_id=1, source_target_pairs={{0,1},{1,0},{2,3},{3,2},{4,5},{5,4},{6,7},{7,6},{8,9},{9,8},{10,11... | collective-permute-start | bytes 1572872 | tf_op jit(solution)/shard_map/ppermute | solution.py:155
  44.9 15.7 %collective-permute-start.8 = (bf16[1024,256]{1,0:T(8,128)(2,1)}, bf16[1024,256]{1,0:T(8,128)(2,1)}, u32[]{:S(2)}, u32[]{:S(2)}) collective-permute-start(bf16[1024,256]{1,0:T(8,128)(2,1)} %get-tuple-element.70), channel_id=1, source_target_pairs={{0,8},{8,0},{16,24},{24,16},{1,9},{9,1},{17,25},{25,17},{2,10},{10... | collective-permute-start | bytes 1572872 | tf_op jit(solution)/shard_map/ppermute | solution.py:158
  46.5 20.3 %collective-permute-start.7 = (bf16[1024,256]{1,0:T(8,128)(2,1)S(1)}, bf16[1024,256]{1,0:T(8,128)(2,1)S(1)}, u32[]{:S(2)}, u32[]{:S(2)}) collective-permute-start(bf16[1024,256]{1,0:T(8,128)(2,1)S(1)} %get-tuple-element.37.refs_0_), channel_id=1, source_target_pairs={{0,1},{1,0},{2,3},{3,2},{4,5},{5,4},{6,7},{7,6},{8,9},{9,8},{10,11... | collective-permute-start | bytes 1572872 | tf_op jit(solution)/shard_map/ppermute | solution.py:155
  49.4 21.2 %copy-start.2 = (bf16[1024,256]{1,0:T(8,128)(2,1)}, bf16[1024,256]{1,0:T(8,128)(2,1)S(1)}, u32[]{:S(2)}) copy-start(bf16[1024,256]{1,0:T(8,128)(2,1)S(1)} %collective-permute-done.12.refs_6_) | copy-start | bytes 1572868
  49.4 18.8 %collective-permute-start.13 = (bf16[1024,256]{1,0:T(8,128)(2,1)S(1)}, bf16[1024,256]{1,0:T(8,128)(2,1)S(1)}, u32[]{:S(2)}, u32[]{:S(2)}) collective-permute-start(bf16[1024,256]{1,0:T(8,128)(2,1)S(1)} %collective-permute-done.12.refs_6_), channel_id=1, source_target_pairs={{0,1},{1,0},{2,3},{3,2},{4,5},{5,4},{6,7},{7,6},{8,9},{9,8},{10,11... | collective-permute-start | bytes 1572872 | tf_op jit(solution)/shard_map/ppermute | solution.py:155
  60.2 8.3 %collective-permute-start.11 = (bf16[1024,256]{1,0:T(8,128)(2,1)S(1)}, bf16[1024,256]{1,0:T(8,128)(2,1)S(1)}, u32[]{:S(2)}, u32[]{:S(2)}) collective-permute-start(bf16[1024,256]{1,0:T(8,128)(2,1)S(1)} %collective-permute-done.10.refs_4_), channel_id=1, source_target_pairs={{0,1},{1,0},{2,3},{3,2},{4,5},{5,4},{6,7},{7,6},{8,9},{9,8},{10,11... | collective-permute-start | bytes 1572872 | tf_op jit(solution)/shard_map/ppermute | solution.py:155
  60.6 8.4 %collective-permute-start.9 = (bf16[1024,256]{1,0:T(8,128)(2,1)}, bf16[1024,256]{1,0:T(8,128)(2,1)S(1)}, u32[]{:S(2)}, u32[]{:S(2)}) collective-permute-start(bf16[1024,256]{1,0:T(8,128)(2,1)} %collective-permute-done.8.refs_2_), channel_id=1, source_target_pairs={{0,1},{1,0},{2,3},{3,2},{4,5},{5,4},{6,7},{7,6},{8,9},{9,8},{10,11... | collective-permute-start | bytes 1572872 | tf_op jit(solution)/shard_map/ppermute | solution.py:155
  65.0 21.6 %copy-start.18 = (bf16[512,256]{1,0:T(8,128)(2,1)}, bf16[512,256]{1,0:T(8,128)(2,1)S(1)}, u32[]{:S(2)}) copy-start(bf16[512,256]{1,0:T(8,128)(2,1)S(1)} %pad_maximum_fusion.4.refs_8_) | copy-start | bytes 786436
  65.0 18.7 %collective-permute-start.22 = (bf16[512,256]{1,0:T(8,128)(2,1)S(1)}, bf16[512,256]{1,0:T(8,128)(2,1)}, u32[]{:S(2)}, u32[]{:S(2)}) collective-permute-start(bf16[512,256]{1,0:T(8,128)(2,1)S(1)} %pad_maximum_fusion.4.refs_8_), channel_id=1, source_target_pairs={{0,24},{8,16},{16,8},{24,0},{1,25},{9,17},{17,9},{25,1},{2,26},{10... | collective-permute-start | bytes 786440 | tf_op jit(solution)/shard_map/ppermute | solution.py:158
  66.9 18.0 %collective-permute-start.21 = (bf16[512,256]{1,0:T(8,128)(2,1)S(1)}, bf16[512,256]{1,0:T(8,128)(2,1)S(1)}, u32[]{:S(2)}, u32[]{:S(2)}) collective-permute-start(bf16[512,256]{1,0:T(8,128)(2,1)S(1)} %pad_maximum_fusion.4.refs_8_), channel_id=1, source_target_pairs={{0,16},{8,24},{16,0},{24,8},{1,17},{9,25},{17,1},{25,9},{2,18},{10... | collective-permute-start | bytes 786440 | tf_op jit(solution)/shard_map/ppermute | solution.py:158
  68.2 18.4 %collective-permute-start.20 = (bf16[512,256]{1,0:T(8,128)(2,1)S(1)}, bf16[512,256]{1,0:T(8,128)(2,1)S(1)}, u32[]{:S(2)}, u32[]{:S(2)}) collective-permute-start(bf16[512,256]{1,0:T(8,128)(2,1)S(1)} %pad_maximum_fusion.4.refs_8_), channel_id=1, source_target_pairs={{0,8},{8,0},{16,24},{24,16},{1,9},{9,1},{17,25},{25,17},{2,10},{10... | collective-permute-start | bytes 786440 | tf_op jit(solution)/shard_map/ppermute | solution.py:158
  75.9 17.9 %collective-permute-start.15 = (bf16[1024,256]{1,0:T(8,128)(2,1)}, bf16[1024,256]{1,0:T(8,128)(2,1)}, u32[]{:S(2)}, u32[]{:S(2)}) collective-permute-start(bf16[1024,256]{1,0:T(8,128)(2,1)} %partial_product.5), channel_id=1, source_target_pairs={{0,2},{1,3},{6,4},{7,5},{8,10},{9,11},{14,12},{15,13},{16,18},{17,... | collective-permute-start | bytes 1572872 | tf_op jit(solution)/shard_map/ppermute | solution.py:168
  82.2 16.1 %collective-permute-start.19 = (bf16[512,512]{1,0:T(8,128)(2,1)}, bf16[512,512]{1,0:T(8,128)(2,1)}, u32[]{:S(2)}, u32[]{:S(2)}) collective-permute-start(bf16[512,512]{1,0:T(8,128)(2,1)} %pad_maximum_fusion.refs_8_), channel_id=1, source_target_pairs={{0,24},{8,16},{16,8},{24,0},{1,25},{9,17},{17,9},{25,1},{2,26},{10... | collective-permute-start | bytes 1572872 | tf_op jit(solution)/shard_map/ppermute | solution.py:158
  83.7 25.8 %collective-permute-start.18 = (bf16[512,512]{1,0:T(8,128)(2,1)}, bf16[512,512]{1,0:T(8,128)(2,1)}, u32[]{:S(2)}, u32[]{:S(2)}) collective-permute-start(bf16[512,512]{1,0:T(8,128)(2,1)} %pad_maximum_fusion.refs_8_), channel_id=1, source_target_pairs={{0,16},{8,24},{16,0},{24,8},{1,17},{9,25},{17,1},{25,9},{2,18},{10... | collective-permute-start | bytes 1572872 | tf_op jit(solution)/shard_map/ppermute | solution.py:158
  84.9 25.8 %collective-permute-start.17 = (bf16[512,512]{1,0:T(8,128)(2,1)}, bf16[512,512]{1,0:T(8,128)(2,1)}, u32[]{:S(2)}, u32[]{:S(2)}) collective-permute-start(bf16[512,512]{1,0:T(8,128)(2,1)} %pad_maximum_fusion.refs_8_), channel_id=1, source_target_pairs={{0,8},{8,0},{16,24},{24,16},{1,9},{9,1},{17,25},{25,17},{2,10},{10... | collective-permute-start | bytes 1572872 | tf_op jit(solution)/shard_map/ppermute | solution.py:158
  92.5 25.5 %collective-permute-start.23 = (bf16[1024,256]{1,0:T(8,128)(2,1)}, bf16[1024,256]{1,0:T(8,128)(2,1)S(1)}, u32[]{:S(2)}, u32[]{:S(2)}) collective-permute-start(bf16[1024,256]{1,0:T(8,128)(2,1)} %partial_product.7), channel_id=1, source_target_pairs={{0,2},{1,3},{6,4},{7,5},{8,10},{9,11},{14,12},{15,13},{16,18},{17,... | collective-permute-start | bytes 1572872 | tf_op jit(solution)/shard_map/ppermute | solution.py:168
  95.0 24.6 %collective-permute-start.24 = (bf16[1024,256]{1,0:T(8,128)(2,1)S(1)}, bf16[1024,256]{1,0:T(8,128)(2,1)S(1)}, u32[]{:S(2)}, u32[]{:S(2)}) collective-permute-start(bf16[1024,256]{1,0:T(8,128)(2,1)S(1)} %add_convert_fusion.15), channel_id=1, source_target_pairs={{2,4},{3,5},{4,2},{5,3},{10,12},{11,13},{12,10},{13,11},{18,20},{1... | collective-permute-start | bytes 1572872 | tf_op jit(solution)/shard_map/ppermute | solution.py:168
  98.3 34.9 %collective-permute-start.29 = (bf16[512,512]{1,0:T(8,128)(2,1)}, bf16[512,512]{1,0:T(8,128)(2,1)}, u32[]{:S(2)}, u32[]{:S(2)}) collective-permute-start(bf16[512,512]{1,0:T(8,128)(2,1)} %pad_maximum_fusion.1.refs_8_), channel_id=1, source_target_pairs={{0,24},{8,16},{16,8},{24,0},{1,25},{9,17},{17,9},{25,1},{2,26},{10... | collective-permute-start | bytes 1572872 | tf_op jit(solution)/shard_map/ppermute | solution.py:158
  109.5 25.3 %collective-permute-start.28 = (bf16[512,512]{1,0:T(8,128)(2,1)}, bf16[512,512]{1,0:T(8,128)(2,1)}, u32[]{:S(2)}, u32[]{:S(2)}) collective-permute-start(bf16[512,512]{1,0:T(8,128)(2,1)} %pad_maximum_fusion.1.refs_8_), channel_id=1, source_target_pairs={{0,16},{8,24},{16,0},{24,8},{1,17},{9,25},{17,1},{25,9},{2,18},{10... | collective-permute-start | bytes 1572872 | tf_op jit(solution)/shard_map/ppermute | solution.py:158
  110.7 25.3 %collective-permute-start.27 = (bf16[512,512]{1,0:T(8,128)(2,1)}, bf16[512,512]{1,0:T(8,128)(2,1)}, u32[]{:S(2)}, u32[]{:S(2)}) collective-permute-start(bf16[512,512]{1,0:T(8,128)(2,1)} %pad_maximum_fusion.1.refs_8_), channel_id=1, source_target_pairs={{0,8},{8,0},{16,24},{24,16},{1,9},{9,1},{17,25},{25,17},{2,10},{10... | collective-permute-start | bytes 1572872 | tf_op jit(solution)/shard_map/ppermute | solution.py:158
  118.0 15.1 %copy-start.21 = (bf16[1024,256]{1,0:T(8,128)(2,1)S(1)}, bf16[1024,256]{1,0:T(8,128)(2,1)}, u32[]{:S(2)}) copy-start(bf16[1024,256]{1,0:T(8,128)(2,1)} %get-tuple-element.56) | copy-start | bytes 1572868
  118.0 12.7 %collective-permute-start.26 = (bf16[1024,256]{1,0:T(8,128)(2,1)}, bf16[1024,256]{1,0:T(8,128)(2,1)S(1)}, u32[]{:S(2)}, u32[]{:S(2)}) collective-permute-start(bf16[1024,256]{1,0:T(8,128)(2,1)} %get-tuple-element.56), channel_id=1, source_target_pairs={{0,2},{1,3},{6,4},{7,5},{8,10},{9,11},{14,12},{15,13},{16,18},{17,... | collective-permute-start | bytes 1572872 | tf_op jit(solution)/shard_map/ppermute | solution.py:168
  119.6 23.6 %collective-permute-start.30 = (bf16[1024,256]{1,0:T(8,128)(2,1)S(1)}, bf16[1024,256]{1,0:T(8,128)(2,1)S(1)}, u32[]{:S(2)}, u32[]{:S(2)}) collective-permute-start(bf16[1024,256]{1,0:T(8,128)(2,1)S(1)} %add_convert_fusion.14), channel_id=1, source_target_pairs={{2,4},{3,5},{4,2},{5,3},{10,12},{11,13},{12,10},{13,11},{18,20},{1... | collective-permute-start | bytes 1572872 | tf_op jit(solution)/shard_map/ppermute | solution.py:168
  130.7 14.6 %collective-permute-start.25 = (bf16[1024,256]{1,0:T(8,128)(2,1)}, bf16[1024,256]{1,0:T(8,128)(2,1)}, u32[]{:S(2)}, u32[]{:S(2)}) collective-permute-start(bf16[1024,256]{1,0:T(8,128)(2,1)} %broadcast_select_fusion.13), channel_id=1, source_target_pairs={{0,2},{1,3},{2,0},{3,1},{4,6},{5,7},{6,4},{7,5},{8,10},{9,11},{10,... | collective-permute-start | bytes 1572872 | tf_op jit(solution)/shard_map/ppermute | solution.py:168
  133.2 26.2 %collective-permute-start.36 = (bf16[512,512]{1,0:T(8,128)(2,1)}, bf16[512,512]{1,0:T(8,128)(2,1)}, u32[]{:S(2)}, u32[]{:S(2)}) collective-permute-start(bf16[512,512]{1,0:T(8,128)(2,1)} %pad_maximum_fusion.2.refs_8_), channel_id=1, source_target_pairs={{0,24},{8,16},{16,8},{24,0},{1,25},{9,17},{17,9},{25,1},{2,26},{10... | collective-permute-start | bytes 1572872 | tf_op jit(solution)/shard_map/ppermute | solution.py:158
  134.7 29.3 %collective-permute-start.35 = (bf16[512,512]{1,0:T(8,128)(2,1)}, bf16[512,512]{1,0:T(8,128)(2,1)}, u32[]{:S(2)}, u32[]{:S(2)}) collective-permute-start(bf16[512,512]{1,0:T(8,128)(2,1)} %pad_maximum_fusion.2.refs_8_), channel_id=1, source_target_pairs={{0,16},{8,24},{16,0},{24,8},{1,17},{9,25},{17,1},{25,9},{2,18},{10... | collective-permute-start | bytes 1572872 | tf_op jit(solution)/shard_map/ppermute | solution.py:158
  136.0 29.0 %collective-permute-start.34 = (bf16[512,512]{1,0:T(8,128)(2,1)}, bf16[512,512]{1,0:T(8,128)(2,1)}, u32[]{:S(2)}, u32[]{:S(2)}) collective-permute-start(bf16[512,512]{1,0:T(8,128)(2,1)} %pad_maximum_fusion.2.refs_8_), channel_id=1, source_target_pairs={{0,8},{8,0},{16,24},{24,16},{1,9},{9,1},{17,25},{25,17},{2,10},{10... | collective-permute-start | bytes 1572872 | tf_op jit(solution)/shard_map/ppermute | solution.py:158
  143.3 7.4 %collective-permute-start.32 = (bf16[1024,256]{1,0:T(8,128)(2,1)S(1)}, bf16[1024,256]{1,0:T(8,128)(2,1)S(1)}, u32[]{:S(2)}, u32[]{:S(2)}) collective-permute-start(bf16[1024,256]{1,0:T(8,128)(2,1)S(1)} %add_convert_fusion.12), channel_id=1, source_target_pairs={{2,4},{3,5},{4,2},{5,3},{10,12},{11,13},{12,10},{13,11},{18,20},{1... | collective-permute-start | bytes 1572872 | tf_op jit(solution)/shard_map/ppermute | solution.py:168
  145.3 11.5 %collective-permute-start.31 = (bf16[1024,256]{1,0:T(8,128)(2,1)S(1)}, bf16[1024,256]{1,0:T(8,128)(2,1)S(1)}, u32[]{:S(2)}, u32[]{:S(2)}) collective-permute-start(bf16[1024,256]{1,0:T(8,128)(2,1)S(1)} %broadcast_select_fusion.11), channel_id=1, source_target_pairs={{0,2},{1,3},{2,0},{3,1},{4,6},{5,7},{6,4},{7,5},{8,10},{9,11},{10,... | collective-permute-start | bytes 1572872 | tf_op jit(solution)/shard_map/ppermute | solution.py:168
  150.6 30.0 %collective-permute-start.37 = (bf16[1024,256]{1,0:T(8,128)(2,1)S(1)}, bf16[1024,256]{1,0:T(8,128)(2,1)S(1)}, u32[]{:S(2)}, u32[]{:S(2)}) collective-permute-start(bf16[1024,256]{1,0:T(8,128)(2,1)S(1)} %add_convert_fusion.10), channel_id=1, source_target_pairs={{2,4},{3,5},{4,2},{5,3},{10,12},{11,13},{12,10},{13,11},{18,20},{1... | collective-permute-start | bytes 1572872 | tf_op jit(solution)/shard_map/ppermute | solution.py:168
  156.9 14.8 %collective-permute-start.47 = (bf16[448,256]{1,0:T(8,128)(2,1)}, bf16[448,256]{1,0:T(8,128)(2,1)S(1)}, u32[]{:S(2)}, u32[]{:S(2)}) collective-permute-start(bf16[448,256]{1,0:T(8,128)(2,1)} %bitcast.51), channel_id=1, source_target_pairs={{0,1},{1,0},{2,3},{3,2},{4,5},{5,4},{6,7},{7,6},{8,9},{9,8},{10,11... | collective-permute-start | bytes 688136 | tf_op jit(solution)/shard_map/ppermute | solution.py:155
  159.4 17.6 %collective-permute-start.33 = (bf16[1024,256]{1,0:T(8,128)(2,1)}, bf16[1024,256]{1,0:T(8,128)(2,1)}, u32[]{:S(2)}, u32[]{:S(2)}) collective-permute-start(bf16[1024,256]{1,0:T(8,128)(2,1)} %broadcast_select_fusion.9), channel_id=1, source_target_pairs={{0,2},{1,3},{2,0},{3,1},{4,6},{5,7},{6,4},{7,5},{8,10},{9,11},{10,... | collective-permute-start | bytes 1572872 | tf_op jit(solution)/shard_map/ppermute | solution.py:168
  164.1 20.1 %collective-permute-start.39 = (bf16[1024,256]{1,0:T(8,128)(2,1)S(1)}, bf16[1024,256]{1,0:T(8,128)(2,1)S(1)}, u32[]{:S(2)}, u32[]{:S(2)}) collective-permute-start(bf16[1024,256]{1,0:T(8,128)(2,1)S(1)} %add_convert_fusion.8), channel_id=1, source_target_pairs={{2,4},{3,5},{4,2},{5,3},{10,12},{11,13},{12,10},{13,11},{18,20},{1... | collective-permute-start | bytes 1572872 | tf_op jit(solution)/shard_map/ppermute | solution.py:168
  171.4 1.8 collective-permute-start.48
  178.7 5.8 %collective-permute-start.49 = (bf16[448,256]{1,0:T(8,128)(2,1)S(1)}, bf16[448,256]{1,0:T(8,128)(2,1)S(1)}, u32[]{:S(2)}, u32[]{:S(2)}) collective-permute-start(bf16[448,256]{1,0:T(8,128)(2,1)S(1)} %bitcast.181), channel_id=1, source_target_pairs={{0,1},{1,0},{2,3},{3,2},{4,5},{5,4},{6,7},{7,6},{8,9},{9,8},{10,11... | collective-permute-start | bytes 688136 | tf_op jit(solution)/shard_map/ppermute | solution.py:155
  180.0 4.6 %collective-permute-start.41 = (bf16[1024,256]{1,0:T(8,128)(2,1)S(1)}, bf16[1024,256]{1,0:T(8,128)(2,1)S(1)}, u32[]{:S(2)}, u32[]{:S(2)}) collective-permute-start(bf16[1024,256]{1,0:T(8,128)(2,1)S(1)} %add_convert_fusion.6), channel_id=1, source_target_pairs={{2,4},{3,5},{4,2},{5,3},{10,12},{11,13},{12,10},{13,11},{18,20},{1... | collective-permute-start | bytes 1572872 | tf_op jit(solution)/shard_map/ppermute | solution.py:168
  180.9 16.0 %collective-permute-start.38 = (bf16[1024,256]{1,0:T(8,128)(2,1)S(1)}, bf16[1024,256]{1,0:T(8,128)(2,1)S(1)}, u32[]{:S(2)}, u32[]{:S(2)}) collective-permute-start(bf16[1024,256]{1,0:T(8,128)(2,1)S(1)} %broadcast_select_fusion.7), channel_id=1, source_target_pairs={{0,2},{1,3},{2,0},{3,1},{4,6},{5,7},{6,4},{7,5},{8,10},{9,11},{10,... | collective-permute-start | bytes 1572872 | tf_op jit(solution)/shard_map/ppermute | solution.py:168
  184.4 23.7 %collective-permute-start.40 = (bf16[1024,256]{1,0:T(8,128)(2,1)S(1)}, bf16[1024,256]{1,0:T(8,128)(2,1)S(1)}, u32[]{:S(2)}, u32[]{:S(2)}) collective-permute-start(bf16[1024,256]{1,0:T(8,128)(2,1)S(1)} %broadcast_select_fusion.5), channel_id=1, source_target_pairs={{0,2},{1,3},{2,0},{3,1},{4,6},{5,7},{6,4},{7,5},{8,10},{9,11},{10,... | collective-permute-start | bytes 1572872 | tf_op jit(solution)/shard_map/ppermute | solution.py:168
  184.7 34.7 %collective-permute-start.42 = (bf16[1024,256]{1,0:T(8,128)(2,1)S(1)}, bf16[1024,256]{1,0:T(8,128)(2,1)S(1)}, u32[]{:S(2)}, u32[]{:S(2)}) collective-permute-start(bf16[1024,256]{1,0:T(8,128)(2,1)S(1)} %add_convert_fusion.4), channel_id=1, source_target_pairs={{2,0},{3,1},{4,6},{5,7},{10,8},{11,9},{12,14},{13,15},{18,16},{19,... | collective-permute-start | bytes 1572872 | tf_op jit(solution)/shard_map/ppermute | solution.py:168
  197.4 12.2 %collective-permute-start.50 = (bf16[448,256]{1,0:T(8,128)(2,1)S(1)}, bf16[448,256]{1,0:T(8,128)(2,1)S(1)}, u32[]{:S(2)}, u32[]{:S(2)}) collective-permute-start(bf16[448,256]{1,0:T(8,128)(2,1)S(1)} %bitcast.180), channel_id=1, source_target_pairs={{0,1},{1,0},{2,3},{3,2},{4,5},{5,4},{6,7},{7,6},{8,9},{9,8},{10,11... | collective-permute-start | bytes 688136 | tf_op jit(solution)/shard_map/ppermute | solution.py:155
  197.7 12.6 %collective-permute-start.43 = (bf16[1024,256]{1,0:T(8,128)(2,1)S(1)}, bf16[1024,256]{1,0:T(8,128)(2,1)S(1)}, u32[]{:S(2)}, u32[]{:S(2)}) collective-permute-start(bf16[1024,256]{1,0:T(8,128)(2,1)S(1)} %add_convert_fusion.3), channel_id=1, source_target_pairs={{2,4},{3,5},{4,2},{5,3},{10,12},{11,13},{12,10},{13,11},{18,20},{1... | collective-permute-start | bytes 1572872 | tf_op jit(solution)/shard_map/ppermute | solution.py:168
  208.7 1.6 collective-permute-start.51
  208.9 11.0 %collective-permute-start.45 = (bf16[1024,256]{1,0:T(8,128)(2,1)S(1)}, bf16[1024,256]{1,0:T(8,128)(2,1)S(1)}, u32[]{:S(2)}, u32[]{:S(2)}) collective-permute-start(bf16[1024,256]{1,0:T(8,128)(2,1)S(1)} %add_convert_fusion.1), channel_id=1, source_target_pairs={{2,4},{3,5},{4,2},{5,3},{10,12},{11,13},{12,10},{13,11},{18,20},{1... | collective-permute-start | bytes 1572872 | tf_op jit(solution)/shard_map/ppermute | solution.py:168
  210.4 20.5 %collective-permute-start.44 = (bf16[1024,256]{1,0:T(8,128)(2,1)S(1)}, bf16[1024,256]{1,0:T(8,128)(2,1)S(1)}, u32[]{:S(2)}, u32[]{:S(2)}) collective-permute-start(bf16[1024,256]{1,0:T(8,128)(2,1)S(1)} %add_convert_fusion.2), channel_id=1, source_target_pairs={{2,0},{3,1},{4,6},{5,7},{10,8},{11,9},{12,14},{13,15},{18,16},{19,... | collective-permute-start | bytes 1572872 | tf_op jit(solution)/shard_map/ppermute | solution.py:168
  219.8 1.6 collective-permute-start.52
  220.0 21.4 %collective-permute-start.46 = (bf16[1024,256]{1,0:T(8,128)(2,1)S(1)}, bf16[1024,256]{1,0:T(8,128)(2,1)S(1)}, u32[]{:S(2)}, u32[]{:S(2)}) collective-permute-start(bf16[1024,256]{1,0:T(8,128)(2,1)S(1)} %add_convert_fusion), channel_id=1, source_target_pairs={{2,0},{3,1},{4,6},{5,7},{10,8},{11,9},{12,14},{13,15},{18,16},{19,... | collective-permute-start | bytes 1572872 | tf_op jit(solution)/shard_map/ppermute | solution.py:168
  230.9 12.6 %copy-start.20 = (bf16[1,4,112,256]{3,2,0,1:T(8,128)(2,1)S(1)}, bf16[1,4,112,256]{3,2,0,1:T(8,128)(2,1)}, u32[]{:S(2)}) copy-start(bf16[1,4,112,256]{3,2,0,1:T(8,128)(2,1)} %get-tuple-element.97) | copy-start | bytes 688132
  231.3 10.7 %collective-permute-start.53 = (bf16[448,256]{1,0:T(8,128)(2,1)S(1)}, bf16[448,256]{1,0:T(8,128)(2,1)S(1)}, u32[]{:S(2)}, u32[]{:S(2)}) collective-permute-start(bf16[448,256]{1,0:T(8,128)(2,1)S(1)} %bitcast.182), channel_id=1, source_target_pairs={{0,1},{1,0},{2,3},{3,2},{4,5},{5,4},{6,7},{7,6},{8,9},{9,8},{10,11... | collective-permute-start | bytes 688136 | tf_op jit(solution)/shard_map/ppermute | solution.py:155
  241.9 1.6 collective-permute-start.54
  (20 other events, 116.2 us)

commit v5 on v4

--- a/solution.py
+++ b/solution.py
@@ -8,27 +8,34 @@
 from jax.sharding import PartitionSpec as P
 
 EXP_DEV = 1
-GROUPS = ((1,), (1,), (1, 1), (1, 1), (1, 1))
+GROUPS = ((1, 1), (1, 1), (1, 1), (1, 1))
 UNITS = sum(map(sum, GROUPS))
 DELAY = 3
 VMEM_BYTES = 60 * 1024 * 1024
 
 
-def conv_kernel(tile, out_grad, gate_in, conv_in, scan_grad, taps, bias, skip, turned, flat):
+def conv_kernel(tile, at_ctx, out_grad, gate_in, conv_in, scan_grad, taps, bias, skip, *refs):
+    turned, flat, columns_of = refs[:-2], refs[-2], refs[-1]
     channels, length = out_grad.shape
-    kernel_taps = taps.shape[1]
+    window = length // len(turned)
+    kernel_taps = taps.shape[0]
     rows_at_once = 16
+    settings = jnp.concatenate(
+        [0.5 * taps[...], 0.5 * bias[...], skip[...], jnp.zeros((8 - kernel_taps - 2, channels), jnp.float32)], axis=0
+    )
+    columns_of[...] = settings.T
 
     def row_group(group, _):
         row_at = pl.multiple_of(group * rows_at_once, rows_at_once)
         rows = pl.ds(row_at, rows_at_once)
 
-        def spread(column):
-            return jnp.concatenate([jnp.broadcast_to(column, (rows_at_once, 128))] * (tile // 128), axis=1)
-
-        weights = [spread(taps[rows, tap : tap + 1]) for tap in range(kernel_taps)]
-        bias_half = spread(bias[rows, :])
-        skip_value = spread(skip[rows, :])
+        def spread(index):
+            column = jnp.broadcast_to(columns_of[rows, index : index + 1], (rows_at_once, 128))
+            return jnp.concatenate([column] * (tile // 128), axis=1)
+
+        weights = [spread(tap) for tap in range(kernel_taps)]
+        bias_half = spread(kernel_taps)
+        skip_value = spread(kernel_taps + 1)
         after = jnp.zeros((rows_at_once, 128), jnp.float32)
         for at in range(length - tile, -1, -tile):
             columns = pl.ds(at, tile)
@@ -57,29 +64,36 @@
         return 0
 
     lax.fori_loop(0, channels // rows_at_once, row_group, 0)
-    for at in range(0, length, tile):
-        turned[pl.ds(at, tile), :] = flat[:, pl.ds(at, tile)].T
-
-
-def conv_grad(out_grad, gate_in, conv_in, scan_grad, taps_half, bias_half, skip):
+    for offset, out in enumerate(turned):
+        from_at = (at_ctx[0] ^ offset) * window
+        for at in range(0, window, tile):
+            out[pl.ds(at, tile), :] = flat[:, pl.ds(pl.multiple_of(from_at + at, tile), tile)].T
+
+
+def conv_grad(at_ctx, ctx_count, out_grad, gate_in, conv_in, scan_grad, conv_weight, conv_bias, skip_scale):
     channels, length = out_grad.shape
     block = min(128, channels)
-    tile = min(512, length)
-    whole = pl.BlockSpec((block, length), lambda step: (step, 0))
-    column = pl.BlockSpec((block, 1), lambda step: (step, 0))
+    window = length // ctx_count
+    tile = min(512, window)
+    whole = pl.BlockSpec((block, length), lambda step, at_ctx: (step, 0))
+    row = pl.BlockSpec((1, block), lambda step, at_ctx: (0, step))
     return pl.pallas_call(
         functools.partial(conv_kernel, tile),
-        grid=(channels // block,),
-        in_specs=[whole] * 4 + [pl.BlockSpec((block, taps_half.shape[1]), lambda step: (step, 0)), column, column],
-        out_specs=pl.BlockSpec((length, block), lambda step: (0, step)),
-        out_shape=jax.ShapeDtypeStruct((length, channels), jnp.bfloat16),
-        scratch_shapes=[pltpu.VMEM((block, length), jnp.bfloat16)],
+        grid_spec=pltpu.PrefetchScalarGridSpec(
+            num_scalar_prefetch=1,
+            grid=(channels // block,),
+            in_specs=[whole] * 4
+            + [pl.BlockSpec((conv_weight.shape[0], block), lambda step, at_ctx: (0, step)), row, row],
+            out_specs=[pl.BlockSpec((window, block), lambda step, at_ctx: (0, step))] * ctx_count,
+            scratch_shapes=[pltpu.VMEM((block, length), jnp.bfloat16), pltpu.VMEM((block, 8), jnp.float32)],
+        ),
+        out_shape=[jax.ShapeDtypeStruct((window, channels), jnp.bfloat16)] * ctx_count,
         compiler_params=pltpu.CompilerParams(vmem_limit_bytes=VMEM_BYTES),
         cost_estimate=pl.CostEstimate(
             flops=40 * channels * length, bytes_accessed=10 * channels * length, transcendentals=2 * channels * length
         ),
         name="conv_grad",
-    )(out_grad, gate_in, conv_in, scan_grad, taps_half, bias_half, skip)
+    )(at_ctx, out_grad, gate_in, conv_in, scan_grad, conv_weight, conv_bias[None], skip_scale[None])
 
 
 def matmul_kernel(lefts, rights, place, *refs):
@@ -100,17 +114,17 @@
 
 def matmul(lefts, rights, resid, place, widths):
     tokens, depth = lefts[0].shape
-    wide, width = rights[0].shape
+    width = rights[0].shape[1]
     tile = resid.shape[0]
     flops = 2 * tokens * depth * len(lefts) * width
-    moved = 2 * (tokens * depth * len(lefts) + wide * len(rights) * width + tokens * width)
+    moved = 2 * (tokens * depth * len(lefts) + depth * len(lefts) * width + tokens * width)
     return pl.pallas_call(
         functools.partial(matmul_kernel, len(lefts), len(rights)),
         grid_spec=pltpu.PrefetchScalarGridSpec(
             num_scalar_prefetch=1,
             grid=(tokens // tile,),
             in_specs=[pl.BlockSpec((tile, depth), lambda step, place: (step, 0))] * len(lefts)
-            + [pl.BlockSpec((wide, width), lambda step, place: (0, 0))] * len(rights)
+            + [pl.BlockSpec(right.shape, lambda step, place: (0, 0)) for right in rights]
             + [pl.BlockSpec(resid.shape, lambda step, place: (0, 0))],
             out_specs=[pl.BlockSpec((tile, part), lambda step, place: (step, 0)) for part in widths],
         ),
@@ -174,6 +188,12 @@
         here = columns_of(array, core_at, at, width)
         return here, to_core(columns_of(array, 1 - core_at, at, width))
 
+    def spread_twice(piece, late):
+        near = [to_ctx(piece, 1), to_ctx(piece, 2)]
+        cut = piece.shape[0] // 2
+        low, high, _ = lax.optimization_barrier((near[1][:cut], near[0][cut:], late))
+        return [piece, near[0], near[1], to_ctx(low, 1), to_ctx(high, 2)]
+
     def spread(piece):
         return [piece] + [to_ctx(piece, offset) for offset in range(1, ctx_count)]
 
@@ -181,23 +201,22 @@
     rights = [spread(jnp.concatenate(both_cores(projection, 0, first), axis=0))]
 
     turned = conv_grad(
+        ctx_at.astype(jnp.int32).reshape(1),
+        ctx_count,
         out_grad,
         gate_in,
         conv_in,
         scan_grad,
-        0.5 * conv_weight.T,
-        0.5 * conv_bias[:, None],
-        skip_scale[:, None],
-    )
-    turned, rights[0], projection, resid_grad, routes = lax.optimization_barrier(
-        (turned, rights[0], projection, resid_grad, routes)
-    )
-    lefts = []
-    for offset in range(ctx_count):
-        piece = lax.dynamic_slice_in_dim(turned, (ctx_at ^ offset) * window, window, 0)
-        if offset:
-            piece = to_ctx(piece, offset)
+        conv_weight,
+        conv_bias,
+        skip_scale,
+    )
+    turned, rights[0] = lax.optimization_barrier((turned, rights[0]))
+    lefts = [turned[0], to_core(turned[0])]
+    for offset in range(1, ctx_count):
+        piece = to_ctx(turned[offset], offset)
         lefts += [piece, to_core(piece)]
+    lefts[1], projection, resid_grad, routes = lax.optimization_barrier((lefts[1], projection, resid_grad, routes))
 
     routed = jnp.concatenate([routes.T.astype(jnp.float32), gate_probs.T], axis=0)[None]
     offset = 1
@@ -209,9 +228,10 @@
     routed = jnp.sum(jnp.where(order[:, :, None, None], routed[None], 0.0), axis=1)
 
     rest_here, rest_there = both_cores(projection, first, half - first)
+    rest = []
     for group, at in list(zip(widths, starts))[1:]:
         cut = slice(at - first, at - first + sum(group))
-        rights.append(spread(jnp.concatenate([rest_here[:, cut], rest_there[:, cut]], axis=0)))
+        rest.append(jnp.concatenate([rest_here[:, cut], rest_there[:, cut]], axis=0))
     resid_here, resid_there = both_cores(resid_grad, 0, half)
     resid = jnp.where(
         core_at == 0,
@@ -238,13 +258,12 @@
 
     if channels < 128:
         lefts = [jnp.concatenate(lefts, axis=1)]
-        rights = [[jnp.concatenate(chunk, axis=0)] for chunk in rights]
     place = chip_at.astype(jnp.int32).reshape(1)
     pieces = sum(map(len, GROUPS))
 
     middle = chips // 2
     distance = jnp.minimum(chip_at, chips - 1 - chip_at)
-    rows_own, rows_got = [], []
+    rows_own, rows_got, waiting = [], [], []
 
     def add(one, other):
         return (one.astype(jnp.float32) + other.astype(jnp.float32)).astype(jnp.bfloat16)
@@ -254,7 +273,10 @@
         rows = jnp.einsum("eist,itf->eisf", picks, grads.reshape(chips, tile, width), preferred_element_type=jnp.float32)
         rows = (rows * scale).astype(jnp.bfloat16).reshape(2, chips * 2 * capacity, width)
         rows_own.append(rows[0])
-        rows_got.append(to_core(rows[1]))
+        waiting.append(rows[1])
+        if len(waiting) == 2 or len(rows_own) == pieces:
+            rows_got.append(to_core(jnp.concatenate(waiting, axis=1)))
+            waiting.clear()
 
     hops = middle - 1
     sums = [[None] * pieces for _ in range(hops + 1)]
@@ -265,10 +287,19 @@
     first_of = [sum(map(len, GROUPS[:at])) for at in range(len(GROUPS))]
     for step in range(last + 1):
         if group_at < len(GROUPS) and first_of[group_at] == step:
-            if step >= 2:
+            group, at = widths[group_at], starts[group_at]
+            if group_at:
                 sums[1][step - 2], place = lax.optimization_barrier((sums[1][step - 2], place))
-            group, at = widths[group_at], starts[group_at]
-            products = matmul(lefts, rights[group_at], resid[:, at : at + sum(group)], place, group)
+                piece = rest[group_at - 1]
+                if ctx_count == 4:
+                    late = sums[1][step - 4] if step >= 4 else lefts[0]
+                    rights.append(spread_twice(piece, late))
+                else:
+                    rights.append(spread(piece))
+            right = rights[group_at]
+            if channels < 128:
+                right = [jnp.concatenate(right, axis=0)]
+            products = matmul(lefts, right, resid[:, at : at + sum(group)], place, group)
             sums[0][step : step + len(group)] = products
             group_at += 1
         for hop in range(hops):

time: 248 us -> 252 us (1.016)
  waiting for transfers between devices: 95.3 us -> 102 us
  starting transfers between devices: 57 us -> 63.4 us
  local copies, waits for them, and re-layouts: 20.1 us -> 16.4 us
  Pallas kernels: 47.8 us -> 44.2 us
    ppermute x19, starting transfers between devices: 29.1 us -> 37.5 us  [swap_chips(): return lax.ppermute(array, 'exp', sorted(pairs))]
    ppermute x18, waiting for transfers between devices: 25.3 us -> 29.7 us  [to_ctx(): lax.ppermute(array, 'ctx', [(place, place ^ offset) for place in range(ct...]
    slice x10 -> x15, local copies, waits for them, and re-layouts: 3.44 us -> 7.78 us  [the longest x3 3.4 us: spread_twice(): near[1][:cut]]
    pallas_call x5 -> x4, Pallas kernels: 29.8 us -> 25.9 us  [matmul(): pl.pallas_call(functools.partial(matmul_kernel, len(lefts), len(rights)),...]
    ppermute x19, waiting for transfers between devices: 64.6 us -> 68.2 us  [swap_chips(): return lax.ppermute(array, 'exp', sorted(pairs))]
  transfers between devices with their start and end apart: 55 -> 51, of which waited for: 18 -> 23; matrix products, arithmetic and copies ran while one was open for 16% -> 14% of each run, Pallas kernels for 19% -> 18%
where the time goes in v5:
time: 252 us; the launch traced here: 251 us
  waiting for transfers between devices  102 us (40%)
  starting transfers between devices  63.4 us (25%)
  Pallas kernels  44.2 us (18%)
  other arithmetic  21 us (8%)
  local copies, waits for them, and re-layouts  16.4 us (7%)
    ppermute x19, waiting for transfers between devices, swap_chips(): return lax.ppermute(array, 'exp', sorted(pairs))  68.2 us
    ppermute x19, starting transfers between devices, swap_chips(): return lax.ppermute(array, 'exp', sorted(pairs))  37.5 us
    ppermute x18, waiting for transfers between devices, to_ctx(): lax.ppermute(array, 'ctx', [(place, place ^ offset) for place in range(ct...  29.7 us
    pallas_call x4, Pallas kernels, matmul(): pl.pallas_call(functools.partial(matmul_kernel, len(lefts), len(rights)),...  25.9 us
    ppermute x18, starting transfers between devices, to_ctx(): lax.ppermute(array, 'ctx', [(place, place ^ offset) for place in range(ct...  19.6 us
    pallas_call x1, Pallas kernels, conv_grad(): pl.pallas_call(functools.partial(conv_kernel, tile), grid_spec=pltpu.Pref...  18.2 us
    select_n x8, other arithmetic, on_device(): ready[hop][outward] = jnp.where(distance == hop, got, falling)  5.29 us
    select_n x5, other arithmetic, on_device(): got = swap_chips(jnp.where(distance == hop, rising, falling), hop)  5.24 us
  transfers between devices with their start and end apart: 51, of which 23 were waited for; matrix products, arithmetic and copies ran while one was open for 14% of the time, Pallas kernels for 18%

profile of v5, /device:TPU:0, one launch (start us, length us, event | category | flops | bytes accessed | tf_op | source)
XLA Modules:
  0.0 250.5 jit_solution(14552866392669974387)
XLA Ops:
  0.0 1.1 constant_dynamic-slice_fusion.7
  1.6 1.2 collective-permute-done
  2.8 3.9 %collective-permute-start.3 = (bf16[512,512]{1,0:T(8,128)(2,1)S(1)}, bf16[512,512]{1,0:T(8,128)(2,1)}, u32[]{:S(2)}, u32[]{:S(2)}) collective-permute-start(bf16[512,512]{1,0:T(8,128)(2,1)S(1)} %pad_maximum_fusion.refs_8_), channel_id=1, source_target_pairs={{0,24},{8,16},{16,8},{24,0},{1,25},{9,17},{17,9},{25,1},{2,26},{10... | collective-permute-start | bytes 1572872 | tf_op jit(solution)/shard_map/ppermute | solution.py:172
  7.3 18.2 %conv_grad.1 = (bf16[1024,256]{1,0:T(8,128)(2,1)}, bf16[1024,256]{1,0:T(8,128)(2,1)}, bf16[1024,256]{1,0:T(8,128)(2,1)}, bf16[1024,256]{1,0:T(8,128)(2,1)}) custom-call(s32[1]{0:T(128)} %bitcast.1.at_ctx, bf16[256,4096]{1,0:T(8,128)(2,1)} %out_grad.1, bf16[256,4096]{1,0:T(8,128)(2,1)} %gate_in.1, bf16[256,4096]{1,0:T(8,128)(2,1)} %conv_in.1, ...), custom_call_target="tpu_custom_call" | custom-call | flops 41943040 | bytes 10485760 | tf_op jit(solution)/shard_map/conv_grad/pallas_call | solution.py:80
  25.6 4.7 %collective-permute-done.2.refs_10_ = bf16[512,512]{1,0:T(8,128)(2,1)} collective-permute-done((bf16[512,512]{1,0:T(8,128)(2,1)S(1)}, bf16[512,512]{1,0:T(8,128)(2,1)}, u32[]{:S(2)}, u32[]{:S(2)}) %collective-permute-start.2) | collective-permute-done | bytes 524320 | tf_op jit(solution)/shard_map/ppermute | solution.py:172
  30.8 1.5 collective-permute-start.8
  32.9 1.4 collective-permute-start.12
  35.8 1.6 collective-permute-start.6
  37.5 2.1 constant_dynamic-slice_fusion.5
  39.6 2.7 %collective-permute-start.7 = (f32[4,4,128]{2,1,0:T(4,128)S(1)}, f32[4,4,128]{2,1,0:T(4,128)S(1)}, u32[]{:S(2)}, u32[]{:S(2)}) collective-permute-start(f32[4,4,128]{2,1,0:T(4,128)S(1)} %pad_maximum_fusion.9), channel_id=1, source_target_pairs={{0,4},{1,5},{2,6},{3,7},{4,0},{5,1},{6,2},{7,3},{8,12},{9,13},{10,... | collective-permute-start | bytes 24584 | tf_op jit(solution)/shard_map/ppermute | solution.py:224
  43.1 2.7 %collective-permute-done.8.refs_2_ = bf16[1024,256]{1,0:T(8,128)(2,1)} collective-permute-done((bf16[1024,256]{1,0:T(8,128)(2,1)}, bf16[1024,256]{1,0:T(8,128)(2,1)}, u32[]{:S(2)}, u32[]{:S(2)}) %collective-permute-start.8) | collective-permute-done | bytes 524320 | tf_op jit(solution)/shard_map/ppermute | solution.py:172
  45.8 12.1 %collective-permute-done.10.refs_4_ = bf16[1024,256]{1,0:T(8,128)(2,1)} collective-permute-done((bf16[1024,256]{1,0:T(8,128)(2,1)}, bf16[1024,256]{1,0:T(8,128)(2,1)}, u32[]{:S(2)}, u32[]{:S(2)}) %collective-permute-start.10) | collective-permute-done | bytes 524320 | tf_op jit(solution)/shard_map/ppermute | solution.py:172
  61.8 1.0 fusion.22
  62.8 6.5 %partial_product.4 = (bf16[1024,256]{1,0:T(8,128)(2,1)}, bf16[1024,256]{1,0:T(8,128)(2,1)}) custom-call(s32[1]{0:T(128)} %bitcast.place, bf16[1024,256]{1,0:T(8,128)(2,1)} %get-tuple-element.61.refs_0_, bf16[1024,256]{1,0:T(8,128)(2,1)} %copy-done.20, bf16[1024,256]{1,0:T(8,128)(2,1)} %collective-permute-done.8.refs_2_, bf16[1024,256]{1,0:T(8,128)(2,1)} %copy-done.21, ...), custom_call_target="tpu_custom_call" | custom-call | flops 2147483648 | bytes 7340032 | tf_op jit(solution)/shard_map/partial_product/pallas_call | solution.py:121
  69.3 3.6 %collective-permute-start.15 = (bf16[1024,256]{1,0:T(8,128)(2,1)}, bf16[1024,256]{1,0:T(8,128)(2,1)S(1)}, u32[]{:S(2)}, u32[]{:S(2)}) collective-permute-start(bf16[1024,256]{1,0:T(8,128)(2,1)} %get-tuple-element.74), channel_id=1, source_target_pairs={{0,2},{1,3},{6,4},{7,5},{8,10},{9,11},{14,12},{15,13},{16,18},{17,... | collective-permute-start | bytes 1572872 | tf_op jit(solution)/shard_map/ppermute | solution.py:182
  73.0 1.2 fusion.23
  75.0 1.2 collective-permute-start.17
  76.2 1.3 collective-permute-start.21
  77.5 8.0 %collective-permute-done.15 = bf16[1024,256]{1,0:T(8,128)(2,1)S(1)} collective-permute-done((bf16[1024,256]{1,0:T(8,128)(2,1)}, bf16[1024,256]{1,0:T(8,128)(2,1)S(1)}, u32[]{:S(2)}, u32[]{:S(2)}) %collective-permute-start.15) | collective-permute-done | bytes 524320 | tf_op jit(solution)/shard_map/ppermute | solution.py:182
  85.5 1.2 add_convert_fusion.15
  89.7 1.1 collective-permute-start.20
  91.6 1.0 collective-permute-start.26
  93.4 2.9 %collective-permute-done.19.refs_11_ = bf16[256,512]{1,0:T(8,128)(2,1)} collective-permute-done((bf16[256,512]{1,0:T(8,128)(2,1)}, bf16[256,512]{1,0:T(8,128)(2,1)}, u32[]{:S(2)}, u32[]{:S(2)}) %collective-permute-start.19) | collective-permute-done | bytes 262176 | tf_op jit(solution)/shard_map/ppermute | solution.py:172
  96.9 2.2 collective-permute-done.20.refs_12_
  99.1 1.1 collective-permute-start.34
  100.1 6.5 %partial_product.5 = (bf16[1024,256]{1,0:T(8,128)(2,1)}, bf16[1024,256]{1,0:T(8,128)(2,1)}) custom-call(s32[1]{0:T(128)} %bitcast.place, bf16[1024,256]{1,0:T(8,128)(2,1)} %get-tuple-element.61.refs_0_, bf16[1024,256]{1,0:T(8,128)(2,1)} %copy-done.20, bf16[1024,256]{1,0:T(8,128)(2,1)} %collective-permute-done.8.refs_2_, bf16[1024,256]{1,0:T(8,128)(2,1)} %copy-done.21, ...), custom_call_target="tpu_custom_call" | custom-call | flops 2147483648 | bytes 7340032 | tf_op jit(solution)/shard_map/partial_product/pallas_call | solution.py:121
  106.6 1.1 collective-permute-start.33
  107.7 6.3 %collective-permute-start.24 = (bf16[1024,256]{1,0:T(8,128)(2,1)}, bf16[1024,256]{1,0:T(8,128)(2,1)S(1)}, u32[]{:S(2)}, u32[]{:S(2)}) collective-permute-start(bf16[1024,256]{1,0:T(8,128)(2,1)} %get-tuple-element.84), channel_id=1, source_target_pairs={{0,2},{1,3},{6,4},{7,5},{8,10},{9,11},{14,12},{15,13},{16,18},{17,... | collective-permute-start | bytes 1572872 | tf_op jit(solution)/shard_map/ppermute | solution.py:182
  114.2 1.2 broadcast_select_fusion.13
  115.5 1.0 slice.161
  116.5 1.4 collective-permute-start.29
  118.0 1.0 slice.162
  119.3 1.1 collective-permute-start.27
  120.3 1.7 slice.167
  123.6 1.5 collective-permute-done.24
  125.1 1.2 collective-permute-start.35
  126.4 1.4 collective-permute-done.27.refs_11_
  128.6 2.6 %collective-permute-done.28.refs_12_ = bf16[256,512]{1,0:T(8,128)(2,1)S(1)} collective-permute-done((bf16[256,512]{1,0:T(8,128)(2,1)S(1)}, bf16[256,512]{1,0:T(8,128)(2,1)S(1)}, u32[]{:S(2)}, u32[]{:S(2)}) %collective-permute-start.28) | collective-permute-done | bytes 262176 | tf_op jit(solution)/shard_map/ppermute | solution.py:172
  131.9 6.4 %partial_product.6 = (bf16[1024,256]{1,0:T(8,128)(2,1)}, bf16[1024,256]{1,0:T(8,128)(2,1)}) custom-call(s32[1]{0:T(128)} %bitcast.place, bf16[1024,256]{1,0:T(8,128)(2,1)} %get-tuple-element.61.refs_0_, bf16[1024,256]{1,0:T(8,128)(2,1)} %copy-done.20, bf16[1024,256]{1,0:T(8,128)(2,1)} %collective-permute-done.8.refs_2_, bf16[1024,256]{1,0:T(8,128)(2,1)} %copy-done.21, ...), custom_call_target="tpu_custom_call" | custom-call | flops 2147483648 | bytes 7340032 | tf_op jit(solution)/shard_map/partial_product/pallas_call | solution.py:121
  138.3 1.3 add_convert_fusion.10
  139.7 1.6 collective-permute-start.37
  141.3 1.4 broadcast_select_fusion.11
  142.7 6.9 %collective-permute-start.30 = (bf16[1024,256]{1,0:T(8,128)(2,1)S(1)}, bf16[1024,256]{1,0:T(8,128)(2,1)S(1)}, u32[]{:S(2)}, u32[]{:S(2)}) collective-permute-start(bf16[1024,256]{1,0:T(8,128)(2,1)S(1)} %broadcast_select_fusion.11), channel_id=1, source_target_pairs={{0,2},{1,3},{2,0},{3,1},{4,6},{5,7},{6,4},{7,5},{8,10},{9,11},{10,... | collective-permute-start | bytes 1572872 | tf_op jit(solution)/shard_map/ppermute | solution.py:182
  149.6 1.2 broadcast_select_fusion.12
  152.6 1.0 broadcast_select_fusion.9
  153.6 6.9 %collective-permute-done.30 = bf16[1024,256]{1,0:T(8,128)(2,1)S(1)} collective-permute-done((bf16[1024,256]{1,0:T(8,128)(2,1)S(1)}, bf16[1024,256]{1,0:T(8,128)(2,1)S(1)}, u32[]{:S(2)}, u32[]{:S(2)}) %collective-permute-start.30) | collective-permute-done | bytes 524320 | tf_op jit(solution)/shard_map/ppermute | solution.py:182
  160.6 1.2 broadcast_select_fusion.10
  163.7 6.6 %partial_product.7 = (bf16[1024,256]{1,0:T(8,128)(2,1)}, bf16[1024,256]{1,0:T(8,128)(2,1)}) custom-call(s32[1]{0:T(128)} %bitcast.place, bf16[1024,256]{1,0:T(8,128)(2,1)} %get-tuple-element.61.refs_0_, bf16[1024,256]{1,0:T(8,128)(2,1)} %copy-done.20, bf16[1024,256]{1,0:T(8,128)(2,1)} %collective-permute-done.8.refs_2_, bf16[1024,256]{1,0:T(8,128)(2,1)} %copy-done.21, ...), custom_call_target="tpu_custom_call" | custom-call | flops 2147483648 | bytes 7340032 | tf_op jit(solution)/shard_map/partial_product/pallas_call | solution.py:121
  170.4 1.4 broadcast_select_fusion.7
  171.8 3.3 %collective-permute-start.38 = (bf16[1024,256]{1,0:T(8,128)(2,1)S(1)}, bf16[1024,256]{1,0:T(8,128)(2,1)S(1)}, u32[]{:S(2)}, u32[]{:S(2)}) collective-permute-start(bf16[1024,256]{1,0:T(8,128)(2,1)S(1)} %broadcast_select_fusion.7), channel_id=1, source_target_pairs={{0,2},{1,3},{2,0},{3,1},{4,6},{5,7},{6,4},{7,5},{8,10},{9,11},{10,... | collective-permute-start | bytes 1572872 | tf_op jit(solution)/shard_map/ppermute | solution.py:182
  175.8 1.2 add_convert_fusion.6
  177.9 1.2 broadcast_select_fusion.8
  179.5 8.2 %collective-permute-done.38 = bf16[1024,256]{1,0:T(8,128)(2,1)S(1)} collective-permute-done((bf16[1024,256]{1,0:T(8,128)(2,1)S(1)}, bf16[1024,256]{1,0:T(8,128)(2,1)S(1)}, u32[]{:S(2)}, u32[]{:S(2)}) %collective-permute-start.38) | collective-permute-done | bytes 524320 | tf_op jit(solution)/shard_map/ppermute | solution.py:182
  187.7 1.2 broadcast_select_fusion.6
  190.6 4.6 %collective-permute-start.40 = (bf16[1024,256]{1,0:T(8,128)(2,1)S(1)}, bf16[1024,256]{1,0:T(8,128)(2,1)S(1)}, u32[]{:S(2)}, u32[]{:S(2)}) collective-permute-start(bf16[1024,256]{1,0:T(8,128)(2,1)S(1)} %broadcast_select_fusion.5), channel_id=1, source_target_pairs={{0,2},{1,3},{2,0},{3,1},{4,6},{5,7},{6,4},{7,5},{8,10},{9,11},{10,... | collective-permute-start | bytes 1572872 | tf_op jit(solution)/shard_map/ppermute | solution.py:182
  195.4 1.3 collective-permute-start.42
  196.8 1.3 collective-permute-start.44
  198.1 9.8 %collective-permute-done.40 = bf16[1024,256]{1,0:T(8,128)(2,1)S(1)} collective-permute-done((bf16[1024,256]{1,0:T(8,128)(2,1)S(1)}, bf16[1024,256]{1,0:T(8,128)(2,1)S(1)}, u32[]{:S(2)}, u32[]{:S(2)}) %collective-permute-start.40) | collective-permute-done | bytes 524320 | tf_op jit(solution)/shard_map/ppermute | solution.py:182
  209.3 9.8 %collective-permute-done.42 = bf16[1024,256]{1,0:T(8,128)(2,1)S(1)} collective-permute-done((bf16[1024,256]{1,0:T(8,128)(2,1)S(1)}, bf16[1024,256]{1,0:T(8,128)(2,1)S(1)}, u32[]{:S(2)}, u32[]{:S(2)}) %collective-permute-start.42) | collective-permute-done | bytes 524320 | tf_op jit(solution)/shard_map/ppermute | solution.py:182
  219.5 10.3 %collective-permute-done.44 = bf16[1024,256]{1,0:T(8,128)(2,1)S(1)} collective-permute-done((bf16[1024,256]{1,0:T(8,128)(2,1)S(1)}, bf16[1024,256]{1,0:T(8,128)(2,1)S(1)}, u32[]{:S(2)}, u32[]{:S(2)}) %collective-permute-start.44) | collective-permute-done | bytes 524320 | tf_op jit(solution)/shard_map/ppermute | solution.py:182
  230.3 1.3 collective-permute-start.46
  231.8 13.8 %collective-permute-done.46 = bf16[1024,256]{1,0:T(8,128)(2,1)S(1)} collective-permute-done((bf16[1024,256]{1,0:T(8,128)(2,1)S(1)}, bf16[1024,256]{1,0:T(8,128)(2,1)S(1)}, u32[]{:S(2)}, u32[]{:S(2)}) %collective-permute-start.46) | collective-permute-done | bytes 524320 | tf_op jit(solution)/shard_map/ppermute | solution.py:182
  246.5 1.4 collective-permute-done.50
  248.3 2.2 broadcast_select_fusion
  (205 shorter events, 29.5 us)
Async XLA Ops:
  1.1 1.7 collective-permute-start
  2.8 22.8 %copy-start.13 = (bf16[512,512]{1,0:T(8,128)(2,1)}, bf16[512,512]{1,0:T(8,128)(2,1)S(1)}, u32[]{:S(2)}) copy-start(bf16[512,512]{1,0:T(8,128)(2,1)S(1)} %pad_maximum_fusion.refs_8_) | copy-start | bytes 1572868
  2.8 22.8 %collective-permute-start.3 = (bf16[512,512]{1,0:T(8,128)(2,1)S(1)}, bf16[512,512]{1,0:T(8,128)(2,1)}, u32[]{:S(2)}, u32[]{:S(2)}) collective-permute-start(bf16[512,512]{1,0:T(8,128)(2,1)S(1)} %pad_maximum_fusion.refs_8_), channel_id=1, source_target_pairs={{0,24},{8,16},{16,8},{24,0},{1,25},{9,17},{17,9},{25,1},{2,26},{10... | collective-permute-start | bytes 1572872 | tf_op jit(solution)/shard_map/ppermute | solution.py:172
  6.7 23.6 %collective-permute-start.2 = (bf16[512,512]{1,0:T(8,128)(2,1)S(1)}, bf16[512,512]{1,0:T(8,128)(2,1)}, u32[]{:S(2)}, u32[]{:S(2)}) collective-permute-start(bf16[512,512]{1,0:T(8,128)(2,1)S(1)} %pad_maximum_fusion.refs_8_), channel_id=1, source_target_pairs={{0,16},{8,24},{16,0},{24,8},{1,17},{9,25},{17,1},{25,9},{2,18},{10... | collective-permute-start | bytes 1572872 | tf_op jit(solution)/shard_map/ppermute | solution.py:172
  7.2 23.4 %collective-permute-start.1 = (bf16[512,512]{1,0:T(8,128)(2,1)S(1)}, bf16[512,512]{1,0:T(8,128)(2,1)}, u32[]{:S(2)}, u32[]{:S(2)}) collective-permute-start(bf16[512,512]{1,0:T(8,128)(2,1)S(1)} %pad_maximum_fusion.refs_8_), channel_id=1, source_target_pairs={{0,8},{8,0},{16,24},{24,16},{1,9},{9,1},{17,25},{25,17},{2,10},{10... | collective-permute-start | bytes 1572872 | tf_op jit(solution)/shard_map/ppermute | solution.py:172
  7.3 26.9 %copy-start.18 = (s32[128,2]{0,1:T(2,128)S(1)}, s32[128,2]{0,1:T(2,128)}, u32[]{:S(2)}) copy-start(s32[128,2]{0,1:T(2,128)} %param.20) | copy-start | bytes 3076
  7.3 27.0 %copy-start.19 = (f32[128,2]{0,1:T(2,128)S(1)}, f32[128,2]{0,1:T(2,128)}, u32[]{:S(2)}) copy-start(f32[128,2]{0,1:T(2,128)} %param.21) | copy-start | bytes 3076
  7.3 27.1 %copy-start.6 = (bf16[256,4096]{1,0:T(8,128)(2,1)S(1)}, bf16[256,4096]{1,0:T(8,128)(2,1)}, u32[]{:S(2)}) copy-start(bf16[256,4096]{1,0:T(8,128)(2,1)} %param.18) | copy-start | bytes 6291460
  30.5 3.7 %collective-permute-start.4 = (bf16[1024,256]{1,0:T(8,128)(2,1)}, bf16[1024,256]{1,0:T(8,128)(2,1)S(1)}, u32[]{:S(2)}, u32[]{:S(2)}) collective-permute-start(bf16[1024,256]{1,0:T(8,128)(2,1)} %get-tuple-element.61.refs_0_), channel_id=1, source_target_pairs={{0,1},{1,0},{2,3},{3,2},{4,5},{5,4},{6,7},{7,6},{8,9},{9,8},{10,11... | collective-permute-start | bytes 1572872 | tf_op jit(solution)/shard_map/ppermute | solution.py:169
  30.8 15.0 %collective-permute-start.8 = (bf16[1024,256]{1,0:T(8,128)(2,1)}, bf16[1024,256]{1,0:T(8,128)(2,1)}, u32[]{:S(2)}, u32[]{:S(2)}) collective-permute-start(bf16[1024,256]{1,0:T(8,128)(2,1)} %get-tuple-element.58), channel_id=1, source_target_pairs={{0,8},{8,0},{16,24},{24,16},{1,9},{9,1},{17,25},{25,17},{2,10},{10... | collective-permute-start | bytes 1572872 | tf_op jit(solution)/shard_map/ppermute | solution.py:172
  32.3 25.6 %collective-permute-start.10 = (bf16[1024,256]{1,0:T(8,128)(2,1)}, bf16[1024,256]{1,0:T(8,128)(2,1)}, u32[]{:S(2)}, u32[]{:S(2)}) collective-permute-start(bf16[1024,256]{1,0:T(8,128)(2,1)} %get-tuple-element.59), channel_id=1, source_target_pairs={{0,16},{8,24},{16,0},{24,8},{1,17},{9,25},{17,1},{25,9},{2,18},{10... | collective-permute-start | bytes 1572872 | tf_op jit(solution)/shard_map/ppermute | solution.py:172
  32.9 25.0 %collective-permute-start.12 = (bf16[1024,256]{1,0:T(8,128)(2,1)}, bf16[1024,256]{1,0:T(8,128)(2,1)}, u32[]{:S(2)}, u32[]{:S(2)}) collective-permute-start(bf16[1024,256]{1,0:T(8,128)(2,1)} %get-tuple-element.60), channel_id=1, source_target_pairs={{0,24},{8,16},{16,8},{24,0},{1,25},{9,17},{17,9},{25,1},{2,26},{10... | collective-permute-start | bytes 1572872 | tf_op jit(solution)/shard_map/ppermute | solution.py:172
  34.3 1.5 collective-permute-start.5
  35.3 37.6 %collective-permute-start.16 = (bf16[256,1536]{1,0:T(8,128)(2,1)}, bf16[256,1536]{1,0:T(8,128)(2,1)}, u32[]{:S(2)}, u32[]{:S(2)}) collective-permute-start(bf16[256,1536]{1,0:T(8,128)(2,1)} %constant_dynamic-slice_fusion.2), channel_id=1, source_target_pairs={{0,1},{1,0},{2,3},{3,2},{4,5},{5,4},{6,7},{7,6},{8,9},{9,8},{10,11... | collective-permute-start | bytes 2359304 | tf_op jit(solution)/shard_map/ppermute | solution.py:169
  35.8 3.8 %collective-permute-start.6 = (f32[2,4,128]{2,1,0:T(4,128)S(1)}, f32[2,4,128]{2,1,0:T(4,128)S(1)}, u32[]{:S(2)}, u32[]{:S(2)}) collective-permute-start(f32[2,4,128]{2,1,0:T(4,128)S(1)} %pad_maximum_fusion.10), channel_id=1, source_target_pairs={{0,2},{1,3},{2,0},{3,1},{4,6},{5,7},{6,4},{7,5},{8,10},{9,11},{10,... | collective-permute-start | bytes 12296 | tf_op jit(solution)/shard_map/ppermute | solution.py:224
  39.6 18.8 %collective-permute-start.7 = (f32[4,4,128]{2,1,0:T(4,128)S(1)}, f32[4,4,128]{2,1,0:T(4,128)S(1)}, u32[]{:S(2)}, u32[]{:S(2)}) collective-permute-start(f32[4,4,128]{2,1,0:T(4,128)S(1)} %pad_maximum_fusion.9), channel_id=1, source_target_pairs={{0,4},{1,5},{2,6},{3,7},{4,0},{5,1},{6,2},{7,3},{8,12},{9,13},{10,... | collective-permute-start | bytes 24584 | tf_op jit(solution)/shard_map/ppermute | solution.py:224
  45.8 15.7 %collective-permute-start.14 = (bf16[128,2048]{1,0:T(8,128)(2,1)}, bf16[128,2048]{1,0:T(8,128)(2,1)S(1)}, u32[]{:S(2)}, u32[]{:S(2)}) collective-permute-start(bf16[128,2048]{1,0:T(8,128)(2,1)} %get-tuple-element.107), channel_id=1, source_target_pairs={{0,1},{1,0},{2,3},{3,2},{4,5},{5,4},{6,7},{7,6},{8,9},{9,8},{10,11... | collective-permute-start | bytes 1572872 | tf_op jit(solution)/shard_map/ppermute | solution.py:169
  57.9 2.1 collective-permute-start.9
  57.9 2.9 %collective-permute-start.11 = (bf16[1024,256]{1,0:T(8,128)(2,1)}, bf16[1024,256]{1,0:T(8,128)(2,1)S(1)}, u32[]{:S(2)}, u32[]{:S(2)}) collective-permute-start(bf16[1024,256]{1,0:T(8,128)(2,1)} %collective-permute-done.10.refs_4_), channel_id=1, source_target_pairs={{0,1},{1,0},{2,3},{3,2},{4,5},{5,4},{6,7},{7,6},{8,9},{9,8},{10,11... | collective-permute-start | bytes 1572872 | tf_op jit(solution)/shard_map/ppermute | solution.py:169
  58.4 3.1 %collective-permute-start.13 = (bf16[1024,256]{1,0:T(8,128)(2,1)}, bf16[1024,256]{1,0:T(8,128)(2,1)S(1)}, u32[]{:S(2)}, u32[]{:S(2)}) collective-permute-start(bf16[1024,256]{1,0:T(8,128)(2,1)} %collective-permute-done.12.refs_6_), channel_id=1, source_target_pairs={{0,1},{1,0},{2,3},{3,2},{4,5},{5,4},{6,7},{7,6},{8,9},{9,8},{10,11... | collective-permute-start | bytes 1572872 | tf_op jit(solution)/shard_map/ppermute | solution.py:169
  62.8 11.3 %copy-start.8 = (bf16[256,512]{1,0:T(8,128)(2,1)S(1)}, bf16[256,512]{1,0:T(8,128)(2,1)}, u32[]{:S(2)}) copy-start(bf16[256,512]{1,0:T(8,128)(2,1)} %get-tuple-element.99) | copy-start | bytes 786436
  69.3 21.5 %copy-start.7 = (bf16[256,512]{1,0:T(8,128)(2,1)S(1)}, bf16[256,512]{1,0:T(8,128)(2,1)}, u32[]{:S(2)}) copy-start(bf16[256,512]{1,0:T(8,128)(2,1)} %get-tuple-element.98) | copy-start | bytes 786436
  69.3 16.2 %collective-permute-start.15 = (bf16[1024,256]{1,0:T(8,128)(2,1)}, bf16[1024,256]{1,0:T(8,128)(2,1)S(1)}, u32[]{:S(2)}, u32[]{:S(2)}) collective-permute-start(bf16[1024,256]{1,0:T(8,128)(2,1)} %get-tuple-element.74), channel_id=1, source_target_pairs={{0,2},{1,3},{6,4},{7,5},{8,10},{9,11},{14,12},{15,13},{16,18},{17,... | collective-permute-start | bytes 1572872 | tf_op jit(solution)/shard_map/ppermute | solution.py:182
  74.2 12.5 %copy-start.14 = (bf16[512,512]{1,0:T(8,128)(2,1)}, bf16[512,512]{1,0:T(8,128)(2,1)S(1)}, u32[]{:S(2)}) copy-start(bf16[512,512]{1,0:T(8,128)(2,1)S(1)} %pad_maximum_fusion.1.refs_8_) | copy-start | bytes 1572868
  74.2 13.8 %collective-permute-start.18 = (bf16[512,512]{1,0:T(8,128)(2,1)S(1)}, bf16[512,512]{1,0:T(8,128)(2,1)S(1)}, u32[]{:S(2)}, u32[]{:S(2)}) collective-permute-start(bf16[512,512]{1,0:T(8,128)(2,1)S(1)} %pad_maximum_fusion.1.refs_8_), channel_id=1, source_target_pairs={{0,16},{8,24},{16,0},{24,8},{1,17},{9,25},{17,1},{25,9},{2,18},{10... | collective-permute-start | bytes 1572872 | tf_op jit(solution)/shard_map/ppermute | solution.py:172
  75.0 13.7 %collective-permute-start.17 = (bf16[512,512]{1,0:T(8,128)(2,1)S(1)}, bf16[512,512]{1,0:T(8,128)(2,1)S(1)}, u32[]{:S(2)}, u32[]{:S(2)}) collective-permute-start(bf16[512,512]{1,0:T(8,128)(2,1)S(1)} %pad_maximum_fusion.1.refs_8_), channel_id=1, source_target_pairs={{0,8},{8,0},{16,24},{24,16},{1,9},{9,1},{17,25},{25,17},{2,10},{10... | collective-permute-start | bytes 1572872 | tf_op jit(solution)/shard_map/ppermute | solution.py:172
  76.2 30.4 %collective-permute-start.21 = (bf16[1024,256]{1,0:T(8,128)(2,1)}, bf16[1024,256]{1,0:T(8,128)(2,1)S(1)}, u32[]{:S(2)}, u32[]{:S(2)}) collective-permute-start(bf16[1024,256]{1,0:T(8,128)(2,1)} %get-tuple-element.80), channel_id=1, source_target_pairs={{0,2},{1,3},{6,4},{7,5},{8,10},{9,11},{14,12},{15,13},{16,18},{17,... | collective-permute-start | bytes 1572872 | tf_op jit(solution)/shard_map/ppermute | solution.py:182
  86.7 21.0 %collective-permute-start.22 = (bf16[1024,256]{1,0:T(8,128)(2,1)S(1)}, bf16[1024,256]{1,0:T(8,128)(2,1)S(1)}, u32[]{:S(2)}, u32[]{:S(2)}) collective-permute-start(bf16[1024,256]{1,0:T(8,128)(2,1)S(1)} %add_convert_fusion.15), channel_id=1, source_target_pairs={{2,4},{3,5},{4,2},{5,3},{10,12},{11,13},{12,10},{13,11},{18,20},{1... | collective-permute-start | bytes 1572872 | tf_op jit(solution)/shard_map/ppermute | solution.py:182
  88.8 7.5 %collective-permute-start.19 = (bf16[256,512]{1,0:T(8,128)(2,1)}, bf16[256,512]{1,0:T(8,128)(2,1)}, u32[]{:S(2)}, u32[]{:S(2)}) collective-permute-start(bf16[256,512]{1,0:T(8,128)(2,1)} %slice.156), channel_id=1, source_target_pairs={{0,8},{8,0},{16,24},{24,16},{1,9},{9,1},{17,25},{25,17},{2,10},{10... | collective-permute-start | bytes 786440 | tf_op jit(solution)/shard_map/ppermute | solution.py:172
  89.7 9.3 %collective-permute-start.20 = (bf16[256,512]{1,0:T(8,128)(2,1)S(1)}, bf16[256,512]{1,0:T(8,128)(2,1)}, u32[]{:S(2)}, u32[]{:S(2)}) collective-permute-start(bf16[256,512]{1,0:T(8,128)(2,1)S(1)} %slice.157), channel_id=1, source_target_pairs={{0,16},{8,24},{16,0},{24,8},{1,17},{9,25},{17,1},{25,9},{2,18},{10... | collective-permute-start | bytes 786440 | tf_op jit(solution)/shard_map/ppermute | solution.py:172
  91.6 23.8 %collective-permute-start.26 = (bf16[512,512]{1,0:T(8,128)(2,1)}, bf16[512,512]{1,0:T(8,128)(2,1)}, u32[]{:S(2)}, u32[]{:S(2)}) collective-permute-start(bf16[512,512]{1,0:T(8,128)(2,1)} %pad_maximum_fusion.2.refs_8_), channel_id=1, source_target_pairs={{0,16},{8,24},{16,0},{24,8},{1,17},{9,25},{17,1},{25,9},{2,18},{10... | collective-permute-start | bytes 1572872 | tf_op jit(solution)/shard_map/ppermute | solution.py:172
  96.3 20.2 %collective-permute-start.25 = (bf16[512,512]{1,0:T(8,128)(2,1)}, bf16[512,512]{1,0:T(8,128)(2,1)}, u32[]{:S(2)}, u32[]{:S(2)}) collective-permute-start(bf16[512,512]{1,0:T(8,128)(2,1)} %pad_maximum_fusion.2.refs_8_), channel_id=1, source_target_pairs={{0,8},{8,0},{16,24},{24,16},{1,9},{9,1},{17,25},{25,17},{2,10},{10... | collective-permute-start | bytes 1572872 | tf_op jit(solution)/shard_map/ppermute | solution.py:172
  99.1 20.2 %collective-permute-start.34 = (bf16[512,512]{1,0:T(8,128)(2,1)}, bf16[512,512]{1,0:T(8,128)(2,1)}, u32[]{:S(2)}, u32[]{:S(2)}) collective-permute-start(bf16[512,512]{1,0:T(8,128)(2,1)} %pad_maximum_fusion.3.refs_8_), channel_id=1, source_target_pairs={{0,16},{8,24},{16,0},{24,8},{1,17},{9,25},{17,1},{25,9},{2,18},{10... | collective-permute-start | bytes 1572872 | tf_op jit(solution)/shard_map/ppermute | solution.py:172
  100.1 13.9 %copy-start.11 = (bf16[1024,256]{1,0:T(8,128)(2,1)S(1)}, bf16[1024,256]{1,0:T(8,128)(2,1)}, u32[]{:S(2)}) copy-start(bf16[1024,256]{1,0:T(8,128)(2,1)} %get-tuple-element.80) | copy-start | bytes 1572868
  106.6 19.7 %copy-start.12 = (bf16[1024,256]{1,0:T(8,128)(2,1)S(1)}, bf16[1024,256]{1,0:T(8,128)(2,1)}, u32[]{:S(2)}) copy-start(bf16[1024,256]{1,0:T(8,128)(2,1)} %get-tuple-element.84) | copy-start | bytes 1572868
  106.6 15.4 %collective-permute-start.33 = (bf16[512,512]{1,0:T(8,128)(2,1)}, bf16[512,512]{1,0:T(8,128)(2,1)S(1)}, u32[]{:S(2)}, u32[]{:S(2)}) collective-permute-start(bf16[512,512]{1,0:T(8,128)(2,1)} %pad_maximum_fusion.3.refs_8_), channel_id=1, source_target_pairs={{0,8},{8,0},{16,24},{24,16},{1,9},{9,1},{17,25},{25,17},{2,10},{10... | collective-permute-start | bytes 1572872 | tf_op jit(solution)/shard_map/ppermute | solution.py:172
  107.7 17.4 %collective-permute-start.24 = (bf16[1024,256]{1,0:T(8,128)(2,1)}, bf16[1024,256]{1,0:T(8,128)(2,1)S(1)}, u32[]{:S(2)}, u32[]{:S(2)}) collective-permute-start(bf16[1024,256]{1,0:T(8,128)(2,1)} %get-tuple-element.84), channel_id=1, source_target_pairs={{0,2},{1,3},{6,4},{7,5},{8,10},{9,11},{14,12},{15,13},{16,18},{17,... | collective-permute-start | bytes 1572872 | tf_op jit(solution)/shard_map/ppermute | solution.py:182
  115.5 22.9 %collective-permute-start.23 = (bf16[1024,256]{1,0:T(8,128)(2,1)S(1)}, bf16[1024,256]{1,0:T(8,128)(2,1)}, u32[]{:S(2)}, u32[]{:S(2)}) collective-permute-start(bf16[1024,256]{1,0:T(8,128)(2,1)S(1)} %broadcast_select_fusion.13), channel_id=1, source_target_pairs={{0,2},{1,3},{2,0},{3,1},{4,6},{5,7},{6,4},{7,5},{8,10},{9,11},{10,... | collective-permute-start | bytes 1572872 | tf_op jit(solution)/shard_map/ppermute | solution.py:182
  116.5 24.8 %collective-permute-start.29 = (bf16[1024,256]{1,0:T(8,128)(2,1)S(1)}, bf16[1024,256]{1,0:T(8,128)(2,1)}, u32[]{:S(2)}, u32[]{:S(2)}) collective-permute-start(bf16[1024,256]{1,0:T(8,128)(2,1)S(1)} %add_convert_fusion.14), channel_id=1, source_target_pairs={{2,4},{3,5},{4,2},{5,3},{10,12},{11,13},{12,10},{13,11},{18,20},{1... | collective-permute-start | bytes 1572872 | tf_op jit(solution)/shard_map/ppermute | solution.py:182
  119.3 8.5 %collective-permute-start.27 = (bf16[256,512]{1,0:T(8,128)(2,1)S(1)}, bf16[256,512]{1,0:T(8,128)(2,1)S(1)}, u32[]{:S(2)}, u32[]{:S(2)}) collective-permute-start(bf16[256,512]{1,0:T(8,128)(2,1)S(1)} %slice.161), channel_id=1, source_target_pairs={{0,8},{8,0},{16,24},{24,16},{1,9},{9,1},{17,25},{25,17},{2,10},{10... | collective-permute-start | bytes 786440 | tf_op jit(solution)/shard_map/ppermute | solution.py:172
  122.0 9.2 %collective-permute-start.28 = (bf16[256,512]{1,0:T(8,128)(2,1)S(1)}, bf16[256,512]{1,0:T(8,128)(2,1)S(1)}, u32[]{:S(2)}, u32[]{:S(2)}) collective-permute-start(bf16[256,512]{1,0:T(8,128)(2,1)S(1)} %slice.162), channel_id=1, source_target_pairs={{0,16},{8,24},{16,0},{24,8},{1,17},{9,25},{17,1},{25,9},{2,18},{10... | collective-permute-start | bytes 786440 | tf_op jit(solution)/shard_map/ppermute | solution.py:172
  125.1 38.6 %collective-permute-start.35 = (bf16[256,512]{1,0:T(8,128)(2,1)}, bf16[256,512]{1,0:T(8,128)(2,1)}, u32[]{:S(2)}, u32[]{:S(2)}) collective-permute-start(bf16[256,512]{1,0:T(8,128)(2,1)} %slice.167), channel_id=1, source_target_pairs={{0,8},{8,0},{16,24},{24,16},{1,9},{9,1},{17,25},{25,17},{2,10},{10... | collective-permute-start | bytes 786440 | tf_op jit(solution)/shard_map/ppermute | solution.py:172
  127.8 35.9 %collective-permute-start.36 = (bf16[256,512]{1,0:T(8,128)(2,1)}, bf16[256,512]{1,0:T(8,128)(2,1)}, u32[]{:S(2)}, u32[]{:S(2)}) collective-permute-start(bf16[256,512]{1,0:T(8,128)(2,1)} %slice.168), channel_id=1, source_target_pairs={{0,16},{8,24},{16,0},{24,8},{1,17},{9,25},{17,1},{25,9},{2,18},{10... | collective-permute-start | bytes 786440 | tf_op jit(solution)/shard_map/ppermute | solution.py:172
  131.2 21.4 %collective-permute-start.31 = (bf16[1024,256]{1,0:T(8,128)(2,1)S(1)}, bf16[1024,256]{1,0:T(8,128)(2,1)S(1)}, u32[]{:S(2)}, u32[]{:S(2)}) collective-permute-start(bf16[1024,256]{1,0:T(8,128)(2,1)S(1)} %add_convert_fusion.12), channel_id=1, source_target_pairs={{2,4},{3,5},{4,2},{5,3},{10,12},{11,13},{12,10},{13,11},{18,20},{1... | collective-permute-start | bytes 1572872 | tf_op jit(solution)/shard_map/ppermute | solution.py:182
  139.7 12.9 %copy-start.2 = (bf16[1024,256]{1,0:T(8,128)(2,1)S(1)}, bf16[1024,256]{1,0:T(8,128)(2,1)}, u32[]{:S(2)}) copy-start(bf16[1024,256]{1,0:T(8,128)(2,1)} %get-tuple-element.90) | copy-start | bytes 1572868
  139.7 30.8 %collective-permute-start.37 = (bf16[1024,256]{1,0:T(8,128)(2,1)S(1)}, bf16[1024,256]{1,0:T(8,128)(2,1)}, u32[]{:S(2)}, u32[]{:S(2)}) collective-permute-start(bf16[1024,256]{1,0:T(8,128)(2,1)S(1)} %add_convert_fusion.10), channel_id=1, source_target_pairs={{2,4},{3,5},{4,2},{5,3},{10,12},{11,13},{12,10},{13,11},{18,20},{1... | collective-permute-start | bytes 1572872 | tf_op jit(solution)/shard_map/ppermute | solution.py:182
  142.7 17.8 %collective-permute-start.30 = (bf16[1024,256]{1,0:T(8,128)(2,1)S(1)}, bf16[1024,256]{1,0:T(8,128)(2,1)S(1)}, u32[]{:S(2)}, u32[]{:S(2)}) collective-permute-start(bf16[1024,256]{1,0:T(8,128)(2,1)S(1)} %broadcast_select_fusion.11), channel_id=1, source_target_pairs={{0,2},{1,3},{2,0},{3,1},{4,6},{5,7},{6,4},{7,5},{8,10},{9,11},{10,... | collective-permute-start | bytes 1572872 | tf_op jit(solution)/shard_map/ppermute | solution.py:182
  150.9 10.9 %copy-start.5 = (bf16[1024,256]{1,0:T(8,128)(2,1)S(1)}, bf16[1024,256]{1,0:T(8,128)(2,1)}, u32[]{:S(2)}) copy-start(bf16[1024,256]{1,0:T(8,128)(2,1)} %get-tuple-element.88) | copy-start | bytes 1572868
  153.6 22.2 %collective-permute-start.32 = (bf16[1024,256]{1,0:T(8,128)(2,1)}, bf16[1024,256]{1,0:T(8,128)(2,1)}, u32[]{:S(2)}, u32[]{:S(2)}) collective-permute-start(bf16[1024,256]{1,0:T(8,128)(2,1)} %broadcast_select_fusion.9), channel_id=1, source_target_pairs={{0,2},{1,3},{2,0},{3,1},{4,6},{5,7},{6,4},{7,5},{8,10},{9,11},{10,... | collective-permute-start | bytes 1572872 | tf_op jit(solution)/shard_map/ppermute | solution.py:182
  162.2 28.1 %collective-permute-start.39 = (bf16[1024,256]{1,0:T(8,128)(2,1)S(1)}, bf16[1024,256]{1,0:T(8,128)(2,1)S(1)}, u32[]{:S(2)}, u32[]{:S(2)}) collective-permute-start(bf16[1024,256]{1,0:T(8,128)(2,1)S(1)} %add_convert_fusion.8), channel_id=1, source_target_pairs={{2,4},{3,5},{4,2},{5,3},{10,12},{11,13},{12,10},{13,11},{18,20},{1... | collective-permute-start | bytes 1572872 | tf_op jit(solution)/shard_map/ppermute | solution.py:182
  170.4 75.8 %collective-permute-start.47 = (bf16[448,512]{1,0:T(8,128)(2,1)S(1)}, bf16[448,512]{1,0:T(8,128)(2,1)S(1)}, u32[]{:S(2)}, u32[]{:S(2)}) collective-permute-start(bf16[448,512]{1,0:T(8,128)(2,1)S(1)} %pad_maximum_fusion.4), channel_id=1, source_target_pairs={{0,1},{1,0},{2,3},{3,2},{4,5},{5,4},{6,7},{7,6},{8,9},{9,8},{10,11... | collective-permute-start | bytes 1376264 | tf_op jit(solution)/shard_map/ppermute | solution.py:169
  171.8 15.8 %collective-permute-start.38 = (bf16[1024,256]{1,0:T(8,128)(2,1)S(1)}, bf16[1024,256]{1,0:T(8,128)(2,1)S(1)}, u32[]{:S(2)}, u32[]{:S(2)}) collective-permute-start(bf16[1024,256]{1,0:T(8,128)(2,1)S(1)} %broadcast_select_fusion.7), channel_id=1, source_target_pairs={{0,2},{1,3},{2,0},{3,1},{4,6},{5,7},{6,4},{7,5},{8,10},{9,11},{10,... | collective-permute-start | bytes 1572872 | tf_op jit(solution)/shard_map/ppermute | solution.py:182
  177.0 18.3 %collective-permute-start.41 = (bf16[1024,256]{1,0:T(8,128)(2,1)S(1)}, bf16[1024,256]{1,0:T(8,128)(2,1)S(1)}, u32[]{:S(2)}, u32[]{:S(2)}) collective-permute-start(bf16[1024,256]{1,0:T(8,128)(2,1)S(1)} %add_convert_fusion.6), channel_id=1, source_target_pairs={{2,4},{3,5},{4,2},{5,3},{10,12},{11,13},{12,10},{13,11},{18,20},{1... | collective-permute-start | bytes 1572872 | tf_op jit(solution)/shard_map/ppermute | solution.py:182
  179.1 10.3 %copy-start.4 = (bf16[1024,256]{1,0:T(8,128)(2,1)S(1)}, bf16[1024,256]{1,0:T(8,128)(2,1)}, u32[]{:S(2)}) copy-start(bf16[1024,256]{1,0:T(8,128)(2,1)} %get-tuple-element.94) | copy-start | bytes 1572868
  179.5 10.9 %copy-start.1 = (bf16[1024,256]{1,0:T(8,128)(2,1)S(1)}, bf16[1024,256]{1,0:T(8,128)(2,1)}, u32[]{:S(2)}) copy-start(bf16[1024,256]{1,0:T(8,128)(2,1)} %get-tuple-element.96) | copy-start | bytes 1572868
  189.3 57.0 %collective-permute-start.48 = (bf16[448,512]{1,0:T(8,128)(2,1)S(1)}, bf16[448,512]{1,0:T(8,128)(2,1)S(1)}, u32[]{:S(2)}, u32[]{:S(2)}) collective-permute-start(bf16[448,512]{1,0:T(8,128)(2,1)S(1)} %pad_maximum_fusion.5), channel_id=1, source_target_pairs={{0,1},{1,0},{2,3},{3,2},{4,5},{5,4},{6,7},{7,6},{8,9},{9,8},{10,11... | collective-permute-start | bytes 1376264 | tf_op jit(solution)/shard_map/ppermute | solution.py:169
  189.5 7.2 %collective-permute-start.43 = (bf16[1024,256]{1,0:T(8,128)(2,1)S(1)}, bf16[1024,256]{1,0:T(8,128)(2,1)S(1)}, u32[]{:S(2)}, u32[]{:S(2)}) collective-permute-start(bf16[1024,256]{1,0:T(8,128)(2,1)S(1)} %add_convert_fusion.3), channel_id=1, source_target_pairs={{2,4},{3,5},{4,2},{5,3},{10,12},{11,13},{12,10},{13,11},{18,20},{1... | collective-permute-start | bytes 1572872 | tf_op jit(solution)/shard_map/ppermute | solution.py:182
  190.6 17.3 %collective-permute-start.40 = (bf16[1024,256]{1,0:T(8,128)(2,1)S(1)}, bf16[1024,256]{1,0:T(8,128)(2,1)S(1)}, u32[]{:S(2)}, u32[]{:S(2)}) collective-permute-start(bf16[1024,256]{1,0:T(8,128)(2,1)S(1)} %broadcast_select_fusion.5), channel_id=1, source_target_pairs={{0,2},{1,3},{2,0},{3,1},{4,6},{5,7},{6,4},{7,5},{8,10},{9,11},{10,... | collective-permute-start | bytes 1572872 | tf_op jit(solution)/shard_map/ppermute | solution.py:182
  195.4 23.7 %collective-permute-start.42 = (bf16[1024,256]{1,0:T(8,128)(2,1)S(1)}, bf16[1024,256]{1,0:T(8,128)(2,1)S(1)}, u32[]{:S(2)}, u32[]{:S(2)}) collective-permute-start(bf16[1024,256]{1,0:T(8,128)(2,1)S(1)} %add_convert_fusion.4), channel_id=1, source_target_pairs={{2,0},{3,1},{4,6},{5,7},{10,8},{11,9},{12,14},{13,15},{18,16},{19,... | collective-permute-start | bytes 1572872 | tf_op jit(solution)/shard_map/ppermute | solution.py:182
  196.8 33.0 %collective-permute-start.44 = (bf16[1024,256]{1,0:T(8,128)(2,1)S(1)}, bf16[1024,256]{1,0:T(8,128)(2,1)S(1)}, u32[]{:S(2)}, u32[]{:S(2)}) collective-permute-start(bf16[1024,256]{1,0:T(8,128)(2,1)S(1)} %add_convert_fusion.2), channel_id=1, source_target_pairs={{2,0},{3,1},{4,6},{5,7},{10,8},{11,9},{12,14},{13,15},{18,16},{19,... | collective-permute-start | bytes 1572872 | tf_op jit(solution)/shard_map/ppermute | solution.py:182
  208.0 22.1 %collective-permute-start.45 = (bf16[1024,256]{1,0:T(8,128)(2,1)S(1)}, bf16[1024,256]{1,0:T(8,128)(2,1)S(1)}, u32[]{:S(2)}, u32[]{:S(2)}) collective-permute-start(bf16[1024,256]{1,0:T(8,128)(2,1)S(1)} %add_convert_fusion.1), channel_id=1, source_target_pairs={{2,4},{3,5},{4,2},{5,3},{10,12},{11,13},{12,10},{13,11},{18,20},{1... | collective-permute-start | bytes 1572872 | tf_op jit(solution)/shard_map/ppermute | solution.py:182
  230.3 15.3 %collective-permute-start.46 = (bf16[1024,256]{1,0:T(8,128)(2,1)S(1)}, bf16[1024,256]{1,0:T(8,128)(2,1)S(1)}, u32[]{:S(2)}, u32[]{:S(2)}) collective-permute-start(bf16[1024,256]{1,0:T(8,128)(2,1)S(1)} %add_convert_fusion), channel_id=1, source_target_pairs={{2,0},{3,1},{4,6},{5,7},{10,8},{11,9},{12,14},{13,15},{18,16},{19,... | collective-permute-start | bytes 1572872 | tf_op jit(solution)/shard_map/ppermute | solution.py:182
  231.7 14.7 %collective-permute-start.49 = (bf16[448,512]{1,0:T(8,128)(2,1)S(1)}, bf16[448,512]{1,0:T(8,128)(2,1)S(1)}, u32[]{:S(2)}, u32[]{:S(2)}) collective-permute-start(bf16[448,512]{1,0:T(8,128)(2,1)S(1)} %pad_maximum_fusion.6), channel_id=1, source_target_pairs={{0,1},{1,0},{2,3},{3,2},{4,5},{5,4},{6,7},{7,6},{8,9},{9,8},{10,11... | collective-permute-start | bytes 1376264 | tf_op jit(solution)/shard_map/ppermute | solution.py:169
  246.1 1.9 collective-permute-start.50
  (13 other events, 48.6 us)

commit v6 on v5

--- a/solution.py
+++ b/solution.py
@@ -11,6 +11,7 @@
 GROUPS = ((1, 1), (1, 1), (1, 1), (1, 1))
 UNITS = sum(map(sum, GROUPS))
 DELAY = 3
+SWAPS = (6, 8)
 VMEM_BYTES = 60 * 1024 * 1024
 
 
@@ -188,11 +189,13 @@
         here = columns_of(array, core_at, at, width)
         return here, to_core(columns_of(array, 1 - core_at, at, width))
 
-    def spread_twice(piece, late):
-        near = [to_ctx(piece, 1), to_ctx(piece, 2)]
-        cut = piece.shape[0] // 2
-        low, high, _ = lax.optimization_barrier((near[1][:cut], near[0][cut:], late))
-        return [piece, near[0], near[1], to_ctx(low, 1), to_ctx(high, 2)]
+    def spread_near(piece):
+        return [piece, to_ctx(piece, 1), to_ctx(piece, 2)]
+
+    def spread_on(near):
+        cut = near[0].shape[0] // 2
+        low, high = chain(near[2][:cut], near[1][cut:])
+        return near + [to_ctx(low, 1), to_ctx(high, 2)]
 
     def spread(piece):
         return [piece] + [to_ctx(piece, offset) for offset in range(1, ctx_count)]
@@ -256,10 +259,26 @@
     picks = picks.astype(jnp.bfloat16)
     picks, scale, lefts = lax.optimization_barrier((picks, scale, lefts))
 
+    lefts, picks, scale, resid, rest = lax.optimization_barrier((lefts, picks, scale, resid, rest))
     if channels < 128:
         lefts = [jnp.concatenate(lefts, axis=1)]
     place = chip_at.astype(jnp.int32).reshape(1)
     pieces = sum(map(len, GROUPS))
+    token = [place]
+
+    def chain(*arrays):
+        *arrays, token[0] = lax.optimization_barrier((*arrays, token[0]))
+        token[0] = arrays[0]
+        return arrays
+
+    def products(group_at, right):
+        group, at = widths[group_at], starts[group_at]
+        if channels < 128:
+            right = [jnp.concatenate(right, axis=0)]
+        right = chain(*right)
+        found = matmul(lefts, right, resid[:, at : at + sum(group)], place, group)
+        token[0] = found[0]
+        return found
 
     middle = chips // 2
     distance = jnp.minimum(chip_at, chips - 1 - chip_at)
@@ -274,60 +293,64 @@
         rows = (rows * scale).astype(jnp.bfloat16).reshape(2, chips * 2 * capacity, width)
         rows_own.append(rows[0])
         waiting.append(rows[1])
-        if len(waiting) == 2 or len(rows_own) == pieces:
+        if len(rows_own) in SWAPS:
             rows_got.append(to_core(jnp.concatenate(waiting, axis=1)))
             waiting.clear()
 
+    square = ctx_count == 4
     hops = middle - 1
+    lag = DELAY - 1
     sums = [[None] * pieces for _ in range(hops + 1)]
     ready = [[None] * pieces for _ in range(hops + 1)]
-    lag = DELAY - 1
-    last = pieces + lag * hops + DELAY * hops
-    group_at = 0
+    outer, across = {}, {}
     first_of = [sum(map(len, GROUPS[:at])) for at in range(len(GROUPS))]
-    for step in range(last + 1):
-        if group_at < len(GROUPS) and first_of[group_at] == step:
-            group, at = widths[group_at], starts[group_at]
-            if group_at:
-                sums[1][step - 2], place = lax.optimization_barrier((sums[1][step - 2], place))
-                piece = rest[group_at - 1]
-                if ctx_count == 4:
-                    late = sums[1][step - 4] if step >= 4 else lefts[0]
-                    rights.append(spread_twice(piece, late))
-                else:
-                    rights.append(spread(piece))
-            right = rights[group_at]
-            if channels < 128:
-                right = [jnp.concatenate(right, axis=0)]
-            products = matmul(lefts, right, resid[:, at : at + sum(group)], place, group)
-            sums[0][step : step + len(group)] = products
-            group_at += 1
+    sums[0][: len(GROUPS[0])] = products(0, rights[0])
+    rights.append(spread(rest[0]))
+    near = None
+    for step in range(pieces + 2 * lag * hops + DELAY + 1):
+        for hop in range(hops):
+            if (step - 2, hop) not in outer:
+                continue
+            got, inward, outward = outer[step - 2, hop]
+            if inward is not None:
+                own, got = chain(sums[hop][inward], got)
+                sums[hop + 1][inward] = token[0] = add(own, got)
+                if hop == hops - 1:
+                    across[step] = (swap_chips(token[0], middle - 1), inward)
+            if outward is not None:
+                ready[hop][outward] = jnp.where(distance == hop, got, ready[hop + 1][outward])
+                if hop == 0:
+                    finish(ready[0][outward])
+        if step - 1 in across:
+            got, index = across[step - 1]
+            own, got = chain(sums[hops][index], got)
+            ready[hops][index] = add(own, got)
+        if step and step in first_of:
+            group_at = first_of.index(step)
+            if near is not None:
+                rights.append(near)
+            sums[0][step : step + len(GROUPS[group_at])] = products(group_at, rights[group_at])
+            near = None
+            if group_at + 1 < len(GROUPS):
+                (piece,) = chain(rest[group_at])
+                near = spread_near(piece) if square else spread(piece)
         for hop in range(hops):
             inward = step - lag * hop
             outward = inward - DELAY - 2 * lag * (hops - 1 - hop)
-            send_in = 0 <= inward < pieces
-            send_out = 0 <= outward < pieces
-            if not (send_in or send_out):
+            inward = inward if 0 <= inward < pieces else None
+            outward = outward if 0 <= outward < pieces else None
+            if inward is not None and outward is not None:
+                payload = jnp.where(distance == hop, sums[hop][inward], ready[hop + 1][outward])
+            elif inward is not None:
+                payload = sums[hop][inward]
+            elif outward is not None:
+                payload = ready[hop + 1][outward]
+            else:
                 continue
-            if send_in and 0 <= inward - 2:
-                sums[hop][inward], sums[hop + 1][inward - 2] = lax.optimization_barrier(
-                    (sums[hop][inward], sums[hop + 1][inward - 2])
-                )
-            rising = sums[hop][inward] if send_in else None
-            falling = ready[hop + 1][outward] if send_out else None
-            if send_in and send_out:
-                got = swap_chips(jnp.where(distance == hop, rising, falling), hop)
-            else:
-                got = swap_chips(rising if send_in else falling, hop, send_in, send_out)
-            if send_in:
-                sums[hop + 1][inward] = add(rising, got)
-                if hop == hops - 1:
-                    crossed = swap_chips(sums[hop + 1][inward], middle - 1)
-                    ready[hops][inward] = add(sums[hop + 1][inward], crossed)
-            if send_out:
-                ready[hop][outward] = jnp.where(distance == hop, got, falling)
-                if hop == 0:
-                    finish(ready[0][outward])
+            (payload,) = chain(payload)
+            outer[step, hop] = (swap_chips(payload, hop, inward is not None, outward is not None), inward, outward)
+        if square and near is not None and step % 2:
+            near = spread_on(near)
     result = jnp.where(
         core_at == 0,
         jnp.concatenate(rows_own + rows_got, axis=1),

time: 252 us -> 231 us (0.917)
  starting transfers between devices: 63.4 us -> 51.6 us
  waiting for transfers between devices: 102 us -> 96.5 us
    ppermute x19, waiting for transfers between devices: 68.2 us -> 46.4 us  [swap_chips(): return lax.ppermute(array, 'exp', sorted(pairs))]
    ppermute x18 -> x17, waiting for transfers between devices: 29.7 us -> 46.3 us  [to_ctx(): lax.ppermute(array, 'ctx', [(place, place ^ offset) for place in range(ct...]
    ppermute x19, starting transfers between devices: 37.5 us -> 26.2 us  [swap_chips(): return lax.ppermute(array, 'exp', sorted(pairs))]
    slice x7 -> x5, local copies, waits for them, and re-layouts: 6.14 us -> 1.17 us  [the longest x1 1.1 us: products(): found = matmul(lefts, right, resid[:, at:at + sum(group)], place, group)]
    unnamed x73 -> x90, local copies, waits for them, and re-layouts: 2.39 us -> 6.31 us
    ppermute x18 -> x17, starting transfers between devices: 19.6 us -> 19.4 us  [to_ctx(): lax.ppermute(array, 'ctx', [(place, place ^ offset) for place in range(ct...]
  transfers between devices with their start and end apart: 51 -> 48, of which waited for: 23 -> 23; matrix products, arithmetic and copies ran while one was open for 14% -> 11% of each run, Pallas kernels for 18% -> 16%
where the time goes in v6:
time: 231 us; the launch traced here: 230 us
  waiting for transfers between devices  96.5 us (42%)
  starting transfers between devices  51.6 us (22%)
  Pallas kernels  44.1 us (19%)
  other arithmetic  20.1 us (9%)
  local copies, waits for them, and re-layouts  14 us (6%)
  matrix products  2.35 us (1%)
    ppermute x19, waiting for transfers between devices, swap_chips(): return lax.ppermute(array, 'exp', sorted(pairs))  46.4 us
    ppermute x17, waiting for transfers between devices, to_ctx(): lax.ppermute(array, 'ctx', [(place, place ^ offset) for place in range(ct...  46.3 us
    ppermute x19, starting transfers between devices, swap_chips(): return lax.ppermute(array, 'exp', sorted(pairs))  26.2 us
    pallas_call x4, Pallas kernels, matmul(): pl.pallas_call(functools.partial(matmul_kernel, len(lefts), len(rights)),...  25.8 us
    ppermute x17, starting transfers between devices, to_ctx(): lax.ppermute(array, 'ctx', [(place, place ^ offset) for place in range(ct...  19.4 us
    pallas_call x1, Pallas kernels, conv_grad(): pl.pallas_call(functools.partial(conv_kernel, tile), grid_spec=pltpu.Pref...  18.3 us
    select_n x5, other arithmetic, on_device(): jnp.where(distance == hop, sums[hop][inward], ready[hop + 1][outward])  7.13 us
    unnamed x90, local copies, waits for them, and re-layouts  6.31 us
  transfers between devices with their start and end apart: 48, of which 23 were waited for; matrix products, arithmetic and copies ran while one was open for 11% of the time, Pallas kernels for 16%

profile of v6, /device:TPU:0, one launch (start us, length us, event | category | flops | bytes accessed | tf_op | source)
XLA Modules:
  0.0 229.7 jit_solution(2953734643064078512)
XLA Ops:
  0.0 1.1 constant_dynamic-slice_fusion.7
  1.6 1.2 collective-permute-done
  2.8 3.9 %collective-permute-start.3 = (bf16[512,512]{1,0:T(8,128)(2,1)S(1)}, bf16[512,512]{1,0:T(8,128)(2,1)}, u32[]{:S(2)}, u32[]{:S(2)}) collective-permute-start(bf16[512,512]{1,0:T(8,128)(2,1)S(1)} %pad_maximum_fusion.refs_8_), channel_id=1, source_target_pairs={{0,24},{8,16},{16,8},{24,0},{1,25},{9,17},{17,9},{25,1},{2,26},{10... | collective-permute-start | bytes 1572872 | tf_op jit(solution)/shard_map/ppermute | solution.py:173
  7.3 18.3 %conv_grad.1 = (bf16[1024,256]{1,0:T(8,128)(2,1)}, bf16[1024,256]{1,0:T(8,128)(2,1)}, bf16[1024,256]{1,0:T(8,128)(2,1)}, bf16[1024,256]{1,0:T(8,128)(2,1)}) custom-call(s32[1]{0:T(128)} %bitcast.1.at_ctx, bf16[256,4096]{1,0:T(8,128)(2,1)} %out_grad.1, bf16[256,4096]{1,0:T(8,128)(2,1)} %gate_in.1, bf16[256,4096]{1,0:T(8,128)(2,1)} %conv_in.1, ...), custom_call_target="tpu_custom_call" | custom-call | flops 41943040 | bytes 10485760 | tf_op jit(solution)/shard_map/conv_grad/pallas_call | solution.py:81
  25.6 4.6 %collective-permute-done.2.refs_10_ = bf16[512,512]{1,0:T(8,128)(2,1)} collective-permute-done((bf16[512,512]{1,0:T(8,128)(2,1)S(1)}, bf16[512,512]{1,0:T(8,128)(2,1)}, u32[]{:S(2)}, u32[]{:S(2)}) %collective-permute-start.2) | collective-permute-done | bytes 524320 | tf_op jit(solution)/shard_map/ppermute | solution.py:173
  30.8 1.5 collective-permute-start.8
  32.9 1.4 collective-permute-start.12
  34.4 1.0 constant_dynamic-slice_fusion.2
  35.8 1.6 collective-permute-start.6
  37.5 2.1 constant_dynamic-slice_fusion.5
  39.6 2.7 %collective-permute-start.7 = (f32[4,4,128]{2,1,0:T(4,128)S(1)}, f32[4,4,128]{2,1,0:T(4,128)S(1)}, u32[]{:S(2)}, u32[]{:S(2)}) collective-permute-start(f32[4,4,128]{2,1,0:T(4,128)S(1)} %pad_maximum_fusion.6), channel_id=1, source_target_pairs={{0,4},{1,5},{2,6},{3,7},{4,0},{5,1},{6,2},{7,3},{8,12},{9,13},{10,... | collective-permute-start | bytes 24584 | tf_op jit(solution)/shard_map/ppermute | solution.py:227
  42.2 0.9 constant_dynamic-slice_fusion.3
  43.1 2.7 %collective-permute-done.8.refs_2_ = bf16[1024,256]{1,0:T(8,128)(2,1)} collective-permute-done((bf16[1024,256]{1,0:T(8,128)(2,1)}, bf16[1024,256]{1,0:T(8,128)(2,1)}, u32[]{:S(2)}, u32[]{:S(2)}) %collective-permute-start.8) | collective-permute-done | bytes 524320 | tf_op jit(solution)/shard_map/ppermute | solution.py:173
  45.8 12.1 %collective-permute-done.10.refs_4_ = bf16[1024,256]{1,0:T(8,128)(2,1)} collective-permute-done((bf16[1024,256]{1,0:T(8,128)(2,1)}, bf16[1024,256]{1,0:T(8,128)(2,1)}, u32[]{:S(2)}, u32[]{:S(2)}) %collective-permute-start.10) | collective-permute-done | bytes 524320 | tf_op jit(solution)/shard_map/ppermute | solution.py:173
  59.5 0.8 select_reduce_fusion
  61.9 1.2 fusion.23
  63.1 0.8 pad_maximum_fusion.3.refs_8_
  63.9 0.9 pad_maximum_fusion.1
  64.8 1.1 fusion.22
  65.9 6.4 %partial_product.4 = (bf16[1024,256]{1,0:T(8,128)(2,1)}, bf16[1024,256]{1,0:T(8,128)(2,1)}) custom-call(s32[1]{0:T(128)} %bitcast.place, bf16[1024,256]{1,0:T(8,128)(2,1)} %get-tuple-element.142.refs_0_, bf16[1024,256]{1,0:T(8,128)(2,1)} %copy-done.27, bf16[1024,256]{1,0:T(8,128)(2,1)} %collective-permute-done.8.refs_2_, bf16[1024,256]{1,0:T(8,128)(2,1)} %copy-done.28, ...), custom_call_target="tpu_custom_call" | custom-call | flops 2147483648 | bytes 7340032 | tf_op jit(solution)/shard_map/partial_product/pallas_call | solution.py:122
  72.3 3.5 %collective-permute-start.19 = (bf16[1024,256]{1,0:T(8,128)(2,1)}, bf16[1024,256]{1,0:T(8,128)(2,1)S(1)}, u32[]{:S(2)}, u32[]{:S(2)}) collective-permute-start(bf16[1024,256]{1,0:T(8,128)(2,1)} %get-tuple-element.164), channel_id=1, source_target_pairs={{0,2},{1,3},{6,4},{7,5},{8,10},{9,11},{14,12},{15,13},{16,18},{17,... | collective-permute-start | bytes 1572872 | tf_op jit(solution)/shard_map/ppermute | solution.py:183
  75.8 1.5 collective-permute-start.18
  77.3 2.1 collective-permute-start.16
  79.4 1.3 collective-permute-start.21
  80.7 7.7 %collective-permute-done.19 = bf16[1024,256]{1,0:T(8,128)(2,1)S(1)} collective-permute-done((bf16[1024,256]{1,0:T(8,128)(2,1)}, bf16[1024,256]{1,0:T(8,128)(2,1)S(1)}, u32[]{:S(2)}, u32[]{:S(2)}) %collective-permute-start.19) | collective-permute-done | bytes 524320 | tf_op jit(solution)/shard_map/ppermute | solution.py:183
  88.4 1.2 add_convert_fusion.15
  90.3 1.5 collective-permute-done.18.refs_11_
  91.7 10.1 %collective-permute-done.17.refs_10_ = bf16[512,512]{1,0:T(8,128)(2,1)} collective-permute-done((bf16[512,512]{1,0:T(8,128)(2,1)S(1)}, bf16[512,512]{1,0:T(8,128)(2,1)}, u32[]{:S(2)}, u32[]{:S(2)}) %collective-permute-start.17) | collective-permute-done | bytes 524320 | tf_op jit(solution)/shard_map/ppermute | solution.py:173
  101.8 6.5 %partial_product.5 = (bf16[1024,256]{1,0:T(8,128)(2,1)}, bf16[1024,256]{1,0:T(8,128)(2,1)}) custom-call(s32[1]{0:T(128)} %bitcast.place, bf16[1024,256]{1,0:T(8,128)(2,1)} %get-tuple-element.142.refs_0_, bf16[1024,256]{1,0:T(8,128)(2,1)} %copy-done.27, bf16[1024,256]{1,0:T(8,128)(2,1)} %collective-permute-done.8.refs_2_, bf16[1024,256]{1,0:T(8,128)(2,1)} %copy-done.28, ...), custom_call_target="tpu_custom_call" | custom-call | flops 2147483648 | bytes 7340032 | tf_op jit(solution)/shard_map/partial_product/pallas_call | solution.py:122
  109.0 1.4 collective-permute-start.23
  110.3 1.6 collective-permute-start.28
  112.8 2.3 broadcast_select_fusion.13
  115.0 0.9 collective-permute-start.22
  116.0 6.5 %collective-permute-done.24.refs_10_ = bf16[512,512]{1,0:T(8,128)(2,1)S(1)} collective-permute-done((bf16[512,512]{1,0:T(8,128)(2,1)}, bf16[512,512]{1,0:T(8,128)(2,1)S(1)}, u32[]{:S(2)}, u32[]{:S(2)}) %collective-permute-start.24) | collective-permute-done | bytes 524320 | tf_op jit(solution)/shard_map/ppermute | solution.py:173
  122.5 1.7 collective-permute-start.25
  126.0 5.1 %collective-permute-done.26.refs_12_ = bf16[256,512]{1,0:T(8,128)(2,1)S(1)} collective-permute-done((bf16[256,512]{1,0:T(8,128)(2,1)S(1)}, bf16[256,512]{1,0:T(8,128)(2,1)S(1)}, u32[]{:S(2)}, u32[]{:S(2)}) %collective-permute-start.26) | collective-permute-done | bytes 262176 | tf_op jit(solution)/shard_map/ppermute | solution.py:173
  132.5 6.5 %partial_product.6 = (bf16[1024,256]{1,0:T(8,128)(2,1)}, bf16[1024,256]{1,0:T(8,128)(2,1)}) custom-call(s32[1]{0:T(128)} %bitcast.place, bf16[1024,256]{1,0:T(8,128)(2,1)} %get-tuple-element.142.refs_0_, bf16[1024,256]{1,0:T(8,128)(2,1)} %copy-done.27, bf16[1024,256]{1,0:T(8,128)(2,1)} %collective-permute-done.8.refs_2_, bf16[1024,256]{1,0:T(8,128)(2,1)} %copy-done.28, ...), custom_call_target="tpu_custom_call" | custom-call | flops 2147483648 | bytes 7340032 | tf_op jit(solution)/shard_map/partial_product/pallas_call | solution.py:122
  139.8 1.4 collective-permute-start.30
  141.2 1.2 broadcast_select_fusion.12
  142.4 1.2 collective-permute-start.29
  143.6 1.2 add_convert_fusion.10
  145.5 1.2 broadcast_select_fusion.11
  146.8 1.0 broadcast_select_fusion.10
  147.8 2.6 %collective-permute-start.33 = (bf16[1024,256]{1,0:T(8,128)(2,1)}, bf16[1024,256]{1,0:T(8,128)(2,1)S(1)}, u32[]{:S(2)}, u32[]{:S(2)}) collective-permute-start(bf16[1024,256]{1,0:T(8,128)(2,1)} %broadcast_select_fusion.10), channel_id=1, source_target_pairs={{0,2},{1,3},{2,0},{3,1},{4,6},{5,7},{6,4},{7,5},{8,10},{9,11},{10,... | collective-permute-start | bytes 1572872 | tf_op jit(solution)/shard_map/ppermute | solution.py:183
  151.6 0.8 copy-done.19
  153.0 4.3 %collective-permute-done.29 = bf16[1024,256]{1,0:T(8,128)(2,1)S(1)} collective-permute-done((bf16[1024,256]{1,0:T(8,128)(2,1)S(1)}, bf16[1024,256]{1,0:T(8,128)(2,1)S(1)}, u32[]{:S(2)}, u32[]{:S(2)}) %collective-permute-start.29) | collective-permute-done | bytes 524320 | tf_op jit(solution)/shard_map/ppermute | solution.py:183
  158.7 1.5 collective-permute-start.38
  161.0 3.4 %collective-permute-done.35.refs_12_ = bf16[256,512]{1,0:T(8,128)(2,1)S(1)} collective-permute-done((bf16[256,512]{1,0:T(8,128)(2,1)S(1)}, bf16[256,512]{1,0:T(8,128)(2,1)S(1)}, u32[]{:S(2)}, u32[]{:S(2)}) %collective-permute-start.35) | collective-permute-done | bytes 262176 | tf_op jit(solution)/shard_map/ppermute | solution.py:173
  165.8 6.4 %partial_product.7 = (bf16[1024,256]{1,0:T(8,128)(2,1)}, bf16[1024,256]{1,0:T(8,128)(2,1)}) custom-call(s32[1]{0:T(128)} %bitcast.place, bf16[1024,256]{1,0:T(8,128)(2,1)} %get-tuple-element.142.refs_0_, bf16[1024,256]{1,0:T(8,128)(2,1)} %copy-done.27, bf16[1024,256]{1,0:T(8,128)(2,1)} %collective-permute-done.8.refs_2_, bf16[1024,256]{1,0:T(8,128)(2,1)} %copy-done.28, ...), custom_call_target="tpu_custom_call" | custom-call | flops 2147483648 | bytes 7340032 | tf_op jit(solution)/shard_map/partial_product/pallas_call | solution.py:122
  172.3 1.4 broadcast_select_fusion.8
  174.5 1.0 collective-permute-start.40
  175.9 1.2 broadcast_select_fusion.6
  177.1 4.4 %collective-permute-start.39 = (bf16[1024,256]{1,0:T(8,128)(2,1)S(1)}, bf16[1024,256]{1,0:T(8,128)(2,1)S(1)}, u32[]{:S(2)}, u32[]{:S(2)}) collective-permute-start(bf16[1024,256]{1,0:T(8,128)(2,1)S(1)} %broadcast_select_fusion.6), channel_id=1, source_target_pairs={{0,2},{1,3},{2,0},{3,1},{4,6},{5,7},{6,4},{7,5},{8,10},{9,11},{10,... | collective-permute-start | bytes 1572872 | tf_op jit(solution)/shard_map/ppermute | solution.py:183
  181.5 7.1 %collective-permute-done.37 = bf16[1024,256]{1,0:T(8,128)(2,1)S(1)} collective-permute-done((bf16[1024,256]{1,0:T(8,128)(2,1)S(1)}, bf16[1024,256]{1,0:T(8,128)(2,1)S(1)}, u32[]{:S(2)}, u32[]{:S(2)}) %collective-permute-start.37) | collective-permute-done | bytes 524320 | tf_op jit(solution)/shard_map/ppermute | solution.py:183
  190.1 1.3 collective-permute-start.41
  191.5 8.4 %collective-permute-done.39 = bf16[1024,256]{1,0:T(8,128)(2,1)S(1)} collective-permute-done((bf16[1024,256]{1,0:T(8,128)(2,1)S(1)}, bf16[1024,256]{1,0:T(8,128)(2,1)S(1)}, u32[]{:S(2)}, u32[]{:S(2)}) %collective-permute-start.39) | collective-permute-done | bytes 524320 | tf_op jit(solution)/shard_map/ppermute | solution.py:183
  199.8 1.2 broadcast_select_fusion.4
  202.5 1.3 collective-permute-start.43
  203.8 2.8 %collective-permute-done.41 = bf16[1024,256]{1,0:T(8,128)(2,1)S(1)} collective-permute-done((bf16[1024,256]{1,0:T(8,128)(2,1)S(1)}, bf16[1024,256]{1,0:T(8,128)(2,1)S(1)}, u32[]{:S(2)}, u32[]{:S(2)}) %collective-permute-start.41) | collective-permute-done | bytes 524320 | tf_op jit(solution)/shard_map/ppermute | solution.py:183
  207.3 1.3 collective-permute-start.45
  208.6 6.2 %collective-permute-done.43 = bf16[1024,256]{1,0:T(8,128)(2,1)S(1)} collective-permute-done((bf16[1024,256]{1,0:T(8,128)(2,1)S(1)}, bf16[1024,256]{1,0:T(8,128)(2,1)S(1)}, u32[]{:S(2)}, u32[]{:S(2)}) %collective-permute-start.43) | collective-permute-done | bytes 524320 | tf_op jit(solution)/shard_map/ppermute | solution.py:183
  215.2 9.6 %collective-permute-done.45 = bf16[1024,256]{1,0:T(8,128)(2,1)S(1)} collective-permute-done((bf16[1024,256]{1,0:T(8,128)(2,1)S(1)}, bf16[1024,256]{1,0:T(8,128)(2,1)S(1)}, u32[]{:S(2)}, u32[]{:S(2)}) %collective-permute-start.45) | collective-permute-done | bytes 524320 | tf_op jit(solution)/shard_map/ppermute | solution.py:183
  225.7 1.4 collective-permute-done.47
  227.5 2.2 broadcast_select_fusion
  (211 shorter events, 24.4 us)
Async XLA Ops:
  1.1 1.7 collective-permute-start
  2.8 22.8 %copy-start.16 = (bf16[512,512]{1,0:T(8,128)(2,1)}, bf16[512,512]{1,0:T(8,128)(2,1)S(1)}, u32[]{:S(2)}) copy-start(bf16[512,512]{1,0:T(8,128)(2,1)S(1)} %pad_maximum_fusion.refs_8_) | copy-start | bytes 1572868
  2.8 22.8 %collective-permute-start.3 = (bf16[512,512]{1,0:T(8,128)(2,1)S(1)}, bf16[512,512]{1,0:T(8,128)(2,1)}, u32[]{:S(2)}, u32[]{:S(2)}) collective-permute-start(bf16[512,512]{1,0:T(8,128)(2,1)S(1)} %pad_maximum_fusion.refs_8_), channel_id=1, source_target_pairs={{0,24},{8,16},{16,8},{24,0},{1,25},{9,17},{17,9},{25,1},{2,26},{10... | collective-permute-start | bytes 1572872 | tf_op jit(solution)/shard_map/ppermute | solution.py:173
  6.7 23.6 %collective-permute-start.2 = (bf16[512,512]{1,0:T(8,128)(2,1)S(1)}, bf16[512,512]{1,0:T(8,128)(2,1)}, u32[]{:S(2)}, u32[]{:S(2)}) collective-permute-start(bf16[512,512]{1,0:T(8,128)(2,1)S(1)} %pad_maximum_fusion.refs_8_), channel_id=1, source_target_pairs={{0,16},{8,24},{16,0},{24,8},{1,17},{9,25},{17,1},{25,9},{2,18},{10... | collective-permute-start | bytes 1572872 | tf_op jit(solution)/shard_map/ppermute | solution.py:173
  7.2 23.4 %collective-permute-start.1 = (bf16[512,512]{1,0:T(8,128)(2,1)S(1)}, bf16[512,512]{1,0:T(8,128)(2,1)}, u32[]{:S(2)}, u32[]{:S(2)}) collective-permute-start(bf16[512,512]{1,0:T(8,128)(2,1)S(1)} %pad_maximum_fusion.refs_8_), channel_id=1, source_target_pairs={{0,8},{8,0},{16,24},{24,16},{1,9},{9,1},{17,25},{25,17},{2,10},{10... | collective-permute-start | bytes 1572872 | tf_op jit(solution)/shard_map/ppermute | solution.py:173
  7.3 26.9 %copy-start.25 = (s32[128,2]{0,1:T(2,128)S(1)}, s32[128,2]{0,1:T(2,128)}, u32[]{:S(2)}) copy-start(s32[128,2]{0,1:T(2,128)} %param.20) | copy-start | bytes 3076
  7.3 27.0 %copy-start.26 = (f32[128,2]{0,1:T(2,128)S(1)}, f32[128,2]{0,1:T(2,128)}, u32[]{:S(2)}) copy-start(f32[128,2]{0,1:T(2,128)} %param.21) | copy-start | bytes 3076
  7.3 27.1 %copy-start.11 = (bf16[256,4096]{1,0:T(8,128)(2,1)S(1)}, bf16[256,4096]{1,0:T(8,128)(2,1)}, u32[]{:S(2)}) copy-start(bf16[256,4096]{1,0:T(8,128)(2,1)} %param.18) | copy-start | bytes 6291460
  30.5 3.7 %collective-permute-start.4 = (bf16[1024,256]{1,0:T(8,128)(2,1)}, bf16[1024,256]{1,0:T(8,128)(2,1)S(1)}, u32[]{:S(2)}, u32[]{:S(2)}) collective-permute-start(bf16[1024,256]{1,0:T(8,128)(2,1)} %get-tuple-element.142.refs_0_), channel_id=1, source_target_pairs={{0,1},{1,0},{2,3},{3,2},{4,5},{5,4},{6,7},{7,6},{8,9},{9,8},{10,11... | collective-permute-start | bytes 1572872 | tf_op jit(solution)/shard_map/ppermute | solution.py:170
  30.8 15.0 %collective-permute-start.8 = (bf16[1024,256]{1,0:T(8,128)(2,1)}, bf16[1024,256]{1,0:T(8,128)(2,1)}, u32[]{:S(2)}, u32[]{:S(2)}) collective-permute-start(bf16[1024,256]{1,0:T(8,128)(2,1)} %get-tuple-element.127), channel_id=1, source_target_pairs={{0,8},{8,0},{16,24},{24,16},{1,9},{9,1},{17,25},{25,17},{2,10},{10... | collective-permute-start | bytes 1572872 | tf_op jit(solution)/shard_map/ppermute | solution.py:173
  32.3 25.6 %collective-permute-start.10 = (bf16[1024,256]{1,0:T(8,128)(2,1)}, bf16[1024,256]{1,0:T(8,128)(2,1)}, u32[]{:S(2)}, u32[]{:S(2)}) collective-permute-start(bf16[1024,256]{1,0:T(8,128)(2,1)} %get-tuple-element.128), channel_id=1, source_target_pairs={{0,16},{8,24},{16,0},{24,8},{1,17},{9,25},{17,1},{25,9},{2,18},{10... | collective-permute-start | bytes 1572872 | tf_op jit(solution)/shard_map/ppermute | solution.py:173
  32.9 25.0 %collective-permute-start.12 = (bf16[1024,256]{1,0:T(8,128)(2,1)}, bf16[1024,256]{1,0:T(8,128)(2,1)}, u32[]{:S(2)}, u32[]{:S(2)}) collective-permute-start(bf16[1024,256]{1,0:T(8,128)(2,1)} %get-tuple-element.129), channel_id=1, source_target_pairs={{0,24},{8,16},{16,8},{24,0},{1,25},{9,17},{17,9},{25,1},{2,26},{10... | collective-permute-start | bytes 1572872 | tf_op jit(solution)/shard_map/ppermute | solution.py:173
  34.3 1.5 collective-permute-start.5
  35.3 26.6 %collective-permute-start.15 = (bf16[256,1536]{1,0:T(8,128)(2,1)}, bf16[256,1536]{1,0:T(8,128)(2,1)}, u32[]{:S(2)}, u32[]{:S(2)}) collective-permute-start(bf16[256,1536]{1,0:T(8,128)(2,1)} %constant_dynamic-slice_fusion.2), channel_id=1, source_target_pairs={{0,1},{1,0},{2,3},{3,2},{4,5},{5,4},{6,7},{7,6},{8,9},{9,8},{10,11... | collective-permute-start | bytes 2359304 | tf_op jit(solution)/shard_map/ppermute | solution.py:170
  35.8 3.7 %collective-permute-start.6 = (f32[2,4,128]{2,1,0:T(4,128)S(1)}, f32[2,4,128]{2,1,0:T(4,128)S(1)}, u32[]{:S(2)}, u32[]{:S(2)}) collective-permute-start(f32[2,4,128]{2,1,0:T(4,128)S(1)} %pad_maximum_fusion.7), channel_id=1, source_target_pairs={{0,2},{1,3},{2,0},{3,1},{4,6},{5,7},{6,4},{7,5},{8,10},{9,11},{10,... | collective-permute-start | bytes 12296 | tf_op jit(solution)/shard_map/ppermute | solution.py:227
  39.6 18.8 %collective-permute-start.7 = (f32[4,4,128]{2,1,0:T(4,128)S(1)}, f32[4,4,128]{2,1,0:T(4,128)S(1)}, u32[]{:S(2)}, u32[]{:S(2)}) collective-permute-start(f32[4,4,128]{2,1,0:T(4,128)S(1)} %pad_maximum_fusion.6), channel_id=1, source_target_pairs={{0,4},{1,5},{2,6},{3,7},{4,0},{5,1},{6,2},{7,3},{8,12},{9,13},{10,... | collective-permute-start | bytes 24584 | tf_op jit(solution)/shard_map/ppermute | solution.py:227
  43.1 20.8 %copy-start.12 = (bf16[256,512]{1,0:T(8,128)(2,1)S(1)}, bf16[256,512]{1,0:T(8,128)(2,1)}, u32[]{:S(2)}) copy-start(bf16[256,512]{1,0:T(8,128)(2,1)} %get-tuple-element.236) | copy-start | bytes 786436
  43.1 20.8 %copy-start.13 = (bf16[256,512]{1,0:T(8,128)(2,1)S(1)}, bf16[256,512]{1,0:T(8,128)(2,1)}, u32[]{:S(2)}) copy-start(bf16[256,512]{1,0:T(8,128)(2,1)} %get-tuple-element.237) | copy-start | bytes 786436
  45.8 15.8 %collective-permute-start.14 = (bf16[128,2048]{1,0:T(8,128)(2,1)}, bf16[128,2048]{1,0:T(8,128)(2,1)S(1)}, u32[]{:S(2)}, u32[]{:S(2)}) collective-permute-start(bf16[128,2048]{1,0:T(8,128)(2,1)} %get-tuple-element.247), channel_id=1, source_target_pairs={{0,1},{1,0},{2,3},{3,2},{4,5},{5,4},{6,7},{7,6},{8,9},{9,8},{10,11... | collective-permute-start | bytes 1572872 | tf_op jit(solution)/shard_map/ppermute | solution.py:170
  57.9 2.8 %collective-permute-start.9 = (bf16[1024,256]{1,0:T(8,128)(2,1)}, bf16[1024,256]{1,0:T(8,128)(2,1)S(1)}, u32[]{:S(2)}, u32[]{:S(2)}) collective-permute-start(bf16[1024,256]{1,0:T(8,128)(2,1)} %collective-permute-done.8.refs_2_), channel_id=1, source_target_pairs={{0,1},{1,0},{2,3},{3,2},{4,5},{5,4},{6,7},{7,6},{8,9},{9,8},{10,11... | collective-permute-start | bytes 1572872 | tf_op jit(solution)/shard_map/ppermute | solution.py:170
  57.9 3.0 %collective-permute-start.11 = (bf16[1024,256]{1,0:T(8,128)(2,1)}, bf16[1024,256]{1,0:T(8,128)(2,1)}, u32[]{:S(2)}, u32[]{:S(2)}) collective-permute-start(bf16[1024,256]{1,0:T(8,128)(2,1)} %collective-permute-done.10.refs_4_), channel_id=1, source_target_pairs={{0,1},{1,0},{2,3},{3,2},{4,5},{5,4},{6,7},{7,6},{8,9},{9,8},{10,11... | collective-permute-start | bytes 1572872 | tf_op jit(solution)/shard_map/ppermute | solution.py:170
  58.4 3.2 %collective-permute-start.13 = (bf16[1024,256]{1,0:T(8,128)(2,1)}, bf16[1024,256]{1,0:T(8,128)(2,1)}, u32[]{:S(2)}, u32[]{:S(2)}) collective-permute-start(bf16[1024,256]{1,0:T(8,128)(2,1)} %collective-permute-done.12.refs_6_), channel_id=1, source_target_pairs={{0,1},{1,0},{2,3},{3,2},{4,5},{5,4},{6,7},{7,6},{8,9},{9,8},{10,11... | collective-permute-start | bytes 1572872 | tf_op jit(solution)/shard_map/ppermute | solution.py:170
  64.8 12.5 %copy-start.17 = (bf16[512,512]{1,0:T(8,128)(2,1)}, bf16[512,512]{1,0:T(8,128)(2,1)S(1)}, u32[]{:S(2)}) copy-start(bf16[512,512]{1,0:T(8,128)(2,1)S(1)} %get-tuple-element.166.refs_8_) | copy-start | bytes 1572868
  72.3 16.1 %collective-permute-start.19 = (bf16[1024,256]{1,0:T(8,128)(2,1)}, bf16[1024,256]{1,0:T(8,128)(2,1)S(1)}, u32[]{:S(2)}, u32[]{:S(2)}) collective-permute-start(bf16[1024,256]{1,0:T(8,128)(2,1)} %get-tuple-element.164), channel_id=1, source_target_pairs={{0,2},{1,3},{6,4},{7,5},{8,10},{9,11},{14,12},{15,13},{16,18},{17,... | collective-permute-start | bytes 1572872 | tf_op jit(solution)/shard_map/ppermute | solution.py:183
  75.8 15.9 %collective-permute-start.18 = (bf16[512,512]{1,0:T(8,128)(2,1)S(1)}, bf16[512,512]{1,0:T(8,128)(2,1)}, u32[]{:S(2)}, u32[]{:S(2)}) collective-permute-start(bf16[512,512]{1,0:T(8,128)(2,1)S(1)} %get-tuple-element.166.refs_8_), channel_id=1, source_target_pairs={{0,24},{8,16},{16,8},{24,0},{1,25},{9,17},{17,9},{25,1},{2,26},{10... | collective-permute-start | bytes 1572872 | tf_op jit(solution)/shard_map/ppermute | solution.py:173
  77.3 24.5 %collective-permute-start.17 = (bf16[512,512]{1,0:T(8,128)(2,1)S(1)}, bf16[512,512]{1,0:T(8,128)(2,1)}, u32[]{:S(2)}, u32[]{:S(2)}) collective-permute-start(bf16[512,512]{1,0:T(8,128)(2,1)S(1)} %get-tuple-element.166.refs_8_), channel_id=1, source_target_pairs={{0,16},{8,24},{16,0},{24,8},{1,17},{9,25},{17,1},{25,9},{2,18},{10... | collective-permute-start | bytes 1572872 | tf_op jit(solution)/shard_map/ppermute | solution.py:173
  77.3 24.5 %collective-permute-start.16 = (bf16[512,512]{1,0:T(8,128)(2,1)S(1)}, bf16[512,512]{1,0:T(8,128)(2,1)}, u32[]{:S(2)}, u32[]{:S(2)}) collective-permute-start(bf16[512,512]{1,0:T(8,128)(2,1)S(1)} %get-tuple-element.166.refs_8_), channel_id=1, source_target_pairs={{0,8},{8,0},{16,24},{24,16},{1,9},{9,1},{17,25},{25,17},{2,10},{10... | collective-permute-start | bytes 1572872 | tf_op jit(solution)/shard_map/ppermute | solution.py:173
  79.4 32.5 %collective-permute-start.21 = (bf16[1024,256]{1,0:T(8,128)(2,1)}, bf16[1024,256]{1,0:T(8,128)(2,1)S(1)}, u32[]{:S(2)}, u32[]{:S(2)}) collective-permute-start(bf16[1024,256]{1,0:T(8,128)(2,1)} %get-tuple-element.175), channel_id=1, source_target_pairs={{0,2},{1,3},{6,4},{7,5},{8,10},{9,11},{14,12},{15,13},{16,18},{17,... | collective-permute-start | bytes 1572872 | tf_op jit(solution)/shard_map/ppermute | solution.py:183
  89.5 23.2 %collective-permute-start.20 = (bf16[1024,256]{1,0:T(8,128)(2,1)S(1)}, bf16[1024,256]{1,0:T(8,128)(2,1)S(1)}, u32[]{:S(2)}, u32[]{:S(2)}) collective-permute-start(bf16[1024,256]{1,0:T(8,128)(2,1)S(1)} %add_convert_fusion.15), channel_id=1, source_target_pairs={{2,4},{3,5},{4,2},{5,3},{10,12},{11,13},{12,10},{13,11},{18,20},{1... | collective-permute-start | bytes 1572872 | tf_op jit(solution)/shard_map/ppermute | solution.py:183
  101.8 10.1 %copy-start.14 = (bf16[1024,256]{1,0:T(8,128)(2,1)S(1)}, bf16[1024,256]{1,0:T(8,128)(2,1)}, u32[]{:S(2)}) copy-start(bf16[1024,256]{1,0:T(8,128)(2,1)} %get-tuple-element.175) | copy-start | bytes 1572868
  108.3 16.9 %copy-start.15 = (bf16[1024,256]{1,0:T(8,128)(2,1)S(1)}, bf16[1024,256]{1,0:T(8,128)(2,1)}, u32[]{:S(2)}) copy-start(bf16[1024,256]{1,0:T(8,128)(2,1)} %get-tuple-element.182) | copy-start | bytes 1572868
  108.3 14.1 %collective-permute-start.24 = (bf16[512,512]{1,0:T(8,128)(2,1)}, bf16[512,512]{1,0:T(8,128)(2,1)S(1)}, u32[]{:S(2)}, u32[]{:S(2)}) collective-permute-start(bf16[512,512]{1,0:T(8,128)(2,1)} %get-tuple-element.185.refs_8_), channel_id=1, source_target_pairs={{0,16},{8,24},{16,0},{24,8},{1,17},{9,25},{17,1},{25,9},{2,18},{10... | collective-permute-start | bytes 1572872 | tf_op jit(solution)/shard_map/ppermute | solution.py:173
  109.0 13.5 %collective-permute-start.23 = (bf16[512,512]{1,0:T(8,128)(2,1)}, bf16[512,512]{1,0:T(8,128)(2,1)S(1)}, u32[]{:S(2)}, u32[]{:S(2)}) collective-permute-start(bf16[512,512]{1,0:T(8,128)(2,1)} %get-tuple-element.185.refs_8_), channel_id=1, source_target_pairs={{0,8},{8,0},{16,24},{24,16},{1,9},{9,1},{17,25},{25,17},{2,10},{10... | collective-permute-start | bytes 1572872 | tf_op jit(solution)/shard_map/ppermute | solution.py:173
  110.3 14.2 %collective-permute-start.28 = (bf16[1024,256]{1,0:T(8,128)(2,1)}, bf16[1024,256]{1,0:T(8,128)(2,1)S(1)}, u32[]{:S(2)}, u32[]{:S(2)}) collective-permute-start(bf16[1024,256]{1,0:T(8,128)(2,1)} %get-tuple-element.182), channel_id=1, source_target_pairs={{0,2},{1,3},{6,4},{7,5},{8,10},{9,11},{14,12},{15,13},{16,18},{17,... | collective-permute-start | bytes 1572872 | tf_op jit(solution)/shard_map/ppermute | solution.py:183
  112.1 13.9 %collective-permute-start.27 = (bf16[1024,256]{1,0:T(8,128)(2,1)S(1)}, bf16[1024,256]{1,0:T(8,128)(2,1)S(1)}, u32[]{:S(2)}, u32[]{:S(2)}) collective-permute-start(bf16[1024,256]{1,0:T(8,128)(2,1)S(1)} %add_convert_fusion.14), channel_id=1, source_target_pairs={{2,4},{3,5},{4,2},{5,3},{10,12},{11,13},{12,10},{13,11},{18,20},{1... | collective-permute-start | bytes 1572872 | tf_op jit(solution)/shard_map/ppermute | solution.py:183
  112.8 26.2 %copy-start.3 = (bf16[1024,256]{1,0:T(8,128)(2,1)}, bf16[1024,256]{1,0:T(8,128)(2,1)S(1)}, u32[]{:S(2)}) copy-start(bf16[1024,256]{1,0:T(8,128)(2,1)S(1)} %collective-permute-done.20) | copy-start | bytes 1572868
  115.0 28.6 %collective-permute-start.22 = (bf16[1024,256]{1,0:T(8,128)(2,1)}, bf16[1024,256]{1,0:T(8,128)(2,1)}, u32[]{:S(2)}, u32[]{:S(2)}) collective-permute-start(bf16[1024,256]{1,0:T(8,128)(2,1)} %broadcast_select_fusion.13), channel_id=1, source_target_pairs={{0,2},{1,3},{2,0},{3,1},{4,6},{5,7},{6,4},{7,5},{8,10},{9,11},{10,... | collective-permute-start | bytes 1572872 | tf_op jit(solution)/shard_map/ppermute | solution.py:183
  122.5 8.6 %collective-permute-start.25 = (bf16[256,512]{1,0:T(8,128)(2,1)S(1)}, bf16[256,512]{1,0:T(8,128)(2,1)S(1)}, u32[]{:S(2)}, u32[]{:S(2)}) collective-permute-start(bf16[256,512]{1,0:T(8,128)(2,1)S(1)} %slice.149), channel_id=1, source_target_pairs={{0,8},{8,0},{16,24},{24,16},{1,9},{9,1},{17,25},{25,17},{2,10},{10... | collective-permute-start | bytes 786440 | tf_op jit(solution)/shard_map/ppermute | solution.py:173
  124.5 6.5 %collective-permute-start.26 = (bf16[256,512]{1,0:T(8,128)(2,1)S(1)}, bf16[256,512]{1,0:T(8,128)(2,1)S(1)}, u32[]{:S(2)}, u32[]{:S(2)}) collective-permute-start(bf16[256,512]{1,0:T(8,128)(2,1)S(1)} %slice.150), channel_id=1, source_target_pairs={{0,16},{8,24},{16,0},{24,8},{1,17},{9,25},{17,1},{25,9},{2,18},{10... | collective-permute-start | bytes 786440 | tf_op jit(solution)/shard_map/ppermute | solution.py:173
  125.3 21.5 %collective-permute-start.32 = (bf16[1024,256]{1,0:T(8,128)(2,1)S(1)}, bf16[1024,256]{1,0:T(8,128)(2,1)S(1)}, u32[]{:S(2)}, u32[]{:S(2)}) collective-permute-start(bf16[1024,256]{1,0:T(8,128)(2,1)S(1)} %add_convert_fusion.12), channel_id=1, source_target_pairs={{2,4},{3,5},{4,2},{5,3},{10,12},{11,13},{12,10},{13,11},{18,20},{1... | collective-permute-start | bytes 1572872 | tf_op jit(solution)/shard_map/ppermute | solution.py:183
  126.0 15.2 %copy-start.5 = (bf16[1024,256]{1,0:T(8,128)(2,1)}, bf16[1024,256]{1,0:T(8,128)(2,1)S(1)}, u32[]{:S(2)}) copy-start(bf16[1024,256]{1,0:T(8,128)(2,1)S(1)} %collective-permute-done.27) | copy-start | bytes 1572868
  132.5 11.2 %copy-start.7 = (bf16[1024,256]{1,0:T(8,128)(2,1)S(1)}, bf16[1024,256]{1,0:T(8,128)(2,1)}, u32[]{:S(2)}) copy-start(bf16[1024,256]{1,0:T(8,128)(2,1)} %get-tuple-element.199) | copy-start | bytes 1572868
  139.0 11.5 %copy-start.18 = (f32[2,4,112]{2,0,1:T(2,128)S(1)}, f32[2,4,112]{2,0,1:T(2,128)}, u32[]{:S(2)}) copy-start(f32[2,4,112]{2,0,1:T(2,128)} %select_reduce_fusion) | copy-start | bytes 10756
  139.0 12.5 %collective-permute-start.31 = (bf16[512,512]{1,0:T(8,128)(2,1)}, bf16[512,512]{1,0:T(8,128)(2,1)S(1)}, u32[]{:S(2)}, u32[]{:S(2)}) collective-permute-start(bf16[512,512]{1,0:T(8,128)(2,1)} %pad_maximum_fusion.3.refs_8_), channel_id=1, source_target_pairs={{0,8},{8,0},{16,24},{24,16},{1,9},{9,1},{17,25},{25,17},{2,10},{10... | collective-permute-start | bytes 1572872 | tf_op jit(solution)/shard_map/ppermute | solution.py:173
  139.8 12.6 %collective-permute-start.30 = (bf16[512,512]{1,0:T(8,128)(2,1)}, bf16[512,512]{1,0:T(8,128)(2,1)S(1)}, u32[]{:S(2)}, u32[]{:S(2)}) collective-permute-start(bf16[512,512]{1,0:T(8,128)(2,1)} %pad_maximum_fusion.3.refs_8_), channel_id=1, source_target_pairs={{0,16},{8,24},{16,0},{24,8},{1,17},{9,25},{17,1},{25,9},{2,18},{10... | collective-permute-start | bytes 1572872 | tf_op jit(solution)/shard_map/ppermute | solution.py:173
  142.4 14.9 %collective-permute-start.29 = (bf16[1024,256]{1,0:T(8,128)(2,1)S(1)}, bf16[1024,256]{1,0:T(8,128)(2,1)S(1)}, u32[]{:S(2)}, u32[]{:S(2)}) collective-permute-start(bf16[1024,256]{1,0:T(8,128)(2,1)S(1)} %broadcast_select_fusion.12), channel_id=1, source_target_pairs={{0,2},{1,3},{2,0},{3,1},{4,6},{5,7},{6,4},{7,5},{8,10},{9,11},{10,... | collective-permute-start | bytes 1572872 | tf_op jit(solution)/shard_map/ppermute | solution.py:183
  144.8 16.2 %collective-permute-start.36 = (bf16[1024,256]{1,0:T(8,128)(2,1)S(1)}, bf16[1024,256]{1,0:T(8,128)(2,1)S(1)}, u32[]{:S(2)}, u32[]{:S(2)}) collective-permute-start(bf16[1024,256]{1,0:T(8,128)(2,1)S(1)} %add_convert_fusion.10), channel_id=1, source_target_pairs={{2,4},{3,5},{4,2},{5,3},{10,12},{11,13},{12,10},{13,11},{18,20},{1... | collective-permute-start | bytes 1572872 | tf_op jit(solution)/shard_map/ppermute | solution.py:183
  146.8 10.6 %copy-start.6 = (bf16[1024,256]{1,0:T(8,128)(2,1)S(1)}, bf16[1024,256]{1,0:T(8,128)(2,1)}, u32[]{:S(2)}) copy-start(bf16[1024,256]{1,0:T(8,128)(2,1)} %copy-done.5) | copy-start | bytes 1572868
  147.8 9.7 %copy-start.9 = (bf16[1024,256]{1,0:T(8,128)(2,1)S(1)}, bf16[1024,256]{1,0:T(8,128)(2,1)}, u32[]{:S(2)}) copy-start(bf16[1024,256]{1,0:T(8,128)(2,1)} %get-tuple-element.206) | copy-start | bytes 1572868
  147.8 25.9 %collective-permute-start.33 = (bf16[1024,256]{1,0:T(8,128)(2,1)}, bf16[1024,256]{1,0:T(8,128)(2,1)S(1)}, u32[]{:S(2)}, u32[]{:S(2)}) collective-permute-start(bf16[1024,256]{1,0:T(8,128)(2,1)} %broadcast_select_fusion.10), channel_id=1, source_target_pairs={{0,2},{1,3},{2,0},{3,1},{4,6},{5,7},{6,4},{7,5},{8,10},{9,11},{10,... | collective-permute-start | bytes 1572872 | tf_op jit(solution)/shard_map/ppermute | solution.py:183
  152.4 12.0 %collective-permute-start.34 = (bf16[256,512]{1,0:T(8,128)(2,1)S(1)}, bf16[256,512]{1,0:T(8,128)(2,1)S(1)}, u32[]{:S(2)}, u32[]{:S(2)}) collective-permute-start(bf16[256,512]{1,0:T(8,128)(2,1)S(1)} %slice.152), channel_id=1, source_target_pairs={{0,8},{8,0},{16,24},{24,16},{1,9},{9,1},{17,25},{25,17},{2,10},{10... | collective-permute-start | bytes 786440 | tf_op jit(solution)/shard_map/ppermute | solution.py:173
  158.0 6.4 %collective-permute-start.35 = (bf16[256,512]{1,0:T(8,128)(2,1)S(1)}, bf16[256,512]{1,0:T(8,128)(2,1)S(1)}, u32[]{:S(2)}, u32[]{:S(2)}) collective-permute-start(bf16[256,512]{1,0:T(8,128)(2,1)S(1)} %slice.153), channel_id=1, source_target_pairs={{0,16},{8,24},{16,0},{24,8},{1,17},{9,25},{17,1},{25,9},{2,18},{10... | collective-permute-start | bytes 786440 | tf_op jit(solution)/shard_map/ppermute | solution.py:173
  158.7 17.1 %collective-permute-start.38 = (bf16[1024,256]{1,0:T(8,128)(2,1)S(1)}, bf16[1024,256]{1,0:T(8,128)(2,1)}, u32[]{:S(2)}, u32[]{:S(2)}) collective-permute-start(bf16[1024,256]{1,0:T(8,128)(2,1)S(1)} %add_convert_fusion.8), channel_id=1, source_target_pairs={{2,4},{3,5},{4,2},{5,3},{10,12},{11,13},{12,10},{13,11},{18,20},{1... | collective-permute-start | bytes 1572872 | tf_op jit(solution)/shard_map/ppermute | solution.py:183
  173.7 14.9 %collective-permute-start.37 = (bf16[1024,256]{1,0:T(8,128)(2,1)S(1)}, bf16[1024,256]{1,0:T(8,128)(2,1)S(1)}, u32[]{:S(2)}, u32[]{:S(2)}) collective-permute-start(bf16[1024,256]{1,0:T(8,128)(2,1)S(1)} %broadcast_select_fusion.8), channel_id=1, source_target_pairs={{0,2},{1,3},{2,0},{3,1},{4,6},{5,7},{6,4},{7,5},{8,10},{9,11},{10,... | collective-permute-start | bytes 1572872 | tf_op jit(solution)/shard_map/ppermute | solution.py:183
  174.0 14.6 %copy-start.10 = (bf16[1024,256]{1,0:T(8,128)(2,1)S(1)}, bf16[1024,256]{1,0:T(8,128)(2,1)}, u32[]{:S(2)}) copy-start(bf16[1024,256]{1,0:T(8,128)(2,1)} %get-tuple-element.223) | copy-start | bytes 1572868
  174.5 15.2 %collective-permute-start.40 = (bf16[1024,256]{1,0:T(8,128)(2,1)S(1)}, bf16[1024,256]{1,0:T(8,128)(2,1)S(1)}, u32[]{:S(2)}, u32[]{:S(2)}) collective-permute-start(bf16[1024,256]{1,0:T(8,128)(2,1)S(1)} %add_convert_fusion.6), channel_id=1, source_target_pairs={{2,4},{3,5},{4,2},{5,3},{10,12},{11,13},{12,10},{13,11},{18,20},{1... | collective-permute-start | bytes 1572872 | tf_op jit(solution)/shard_map/ppermute | solution.py:183
  177.1 22.7 %collective-permute-start.39 = (bf16[1024,256]{1,0:T(8,128)(2,1)S(1)}, bf16[1024,256]{1,0:T(8,128)(2,1)S(1)}, u32[]{:S(2)}, u32[]{:S(2)}) collective-permute-start(bf16[1024,256]{1,0:T(8,128)(2,1)S(1)} %broadcast_select_fusion.6), channel_id=1, source_target_pairs={{0,2},{1,3},{2,0},{3,1},{4,6},{5,7},{6,4},{7,5},{8,10},{9,11},{10,... | collective-permute-start | bytes 1572872 | tf_op jit(solution)/shard_map/ppermute | solution.py:183
  188.7 13.6 %collective-permute-start.42 = (bf16[1024,256]{1,0:T(8,128)(2,1)S(1)}, bf16[1024,256]{1,0:T(8,128)(2,1)S(1)}, u32[]{:S(2)}, u32[]{:S(2)}) collective-permute-start(bf16[1024,256]{1,0:T(8,128)(2,1)S(1)} %add_convert_fusion.4), channel_id=1, source_target_pairs={{2,4},{3,5},{4,2},{5,3},{10,12},{11,13},{12,10},{13,11},{18,20},{1... | collective-permute-start | bytes 1572872 | tf_op jit(solution)/shard_map/ppermute | solution.py:183
  190.1 16.5 %collective-permute-start.41 = (bf16[1024,256]{1,0:T(8,128)(2,1)S(1)}, bf16[1024,256]{1,0:T(8,128)(2,1)S(1)}, u32[]{:S(2)}, u32[]{:S(2)}) collective-permute-start(bf16[1024,256]{1,0:T(8,128)(2,1)S(1)} %add_convert_fusion.3), channel_id=1, source_target_pairs={{2,0},{3,1},{4,6},{5,7},{10,8},{11,9},{12,14},{13,15},{18,16},{19,... | collective-permute-start | bytes 1572872 | tf_op jit(solution)/shard_map/ppermute | solution.py:183
  201.6 5.6 %collective-permute-start.44 = (bf16[1024,256]{1,0:T(8,128)(2,1)S(1)}, bf16[1024,256]{1,0:T(8,128)(2,1)S(1)}, u32[]{:S(2)}, u32[]{:S(2)}) collective-permute-start(bf16[1024,256]{1,0:T(8,128)(2,1)S(1)} %add_convert_fusion.2), channel_id=1, source_target_pairs={{2,4},{3,5},{4,2},{5,3},{10,12},{11,13},{12,10},{13,11},{18,20},{1... | collective-permute-start | bytes 1572872 | tf_op jit(solution)/shard_map/ppermute | solution.py:183
  202.5 12.3 %collective-permute-start.43 = (bf16[1024,256]{1,0:T(8,128)(2,1)S(1)}, bf16[1024,256]{1,0:T(8,128)(2,1)S(1)}, u32[]{:S(2)}, u32[]{:S(2)}) collective-permute-start(bf16[1024,256]{1,0:T(8,128)(2,1)S(1)} %add_convert_fusion.1), channel_id=1, source_target_pairs={{2,0},{3,1},{4,6},{5,7},{10,8},{11,9},{12,14},{13,15},{18,16},{19,... | collective-permute-start | bytes 1572872 | tf_op jit(solution)/shard_map/ppermute | solution.py:183
  207.0 18.3 %collective-permute-start.46 = (bf16[448,1536]{1,0:T(8,128)(2,1)S(1)}, bf16[448,1536]{1,0:T(8,128)(2,1)S(1)}, u32[]{:S(2)}, u32[]{:S(2)}) collective-permute-start(bf16[448,1536]{1,0:T(8,128)(2,1)S(1)} %constant_dynamic-update-slice_fusion), channel_id=1, source_target_pairs={{0,1},{1,0},{2,3},{3,2},{4,5},{5,4},{6,7},{7,6},{8,9},{9,8},{10,11... | collective-permute-start | bytes 4128776 | tf_op jit(solution)/shard_map/ppermute | solution.py:170
  207.3 17.5 %collective-permute-start.45 = (bf16[1024,256]{1,0:T(8,128)(2,1)S(1)}, bf16[1024,256]{1,0:T(8,128)(2,1)S(1)}, u32[]{:S(2)}, u32[]{:S(2)}) collective-permute-start(bf16[1024,256]{1,0:T(8,128)(2,1)S(1)} %add_convert_fusion), channel_id=1, source_target_pairs={{2,0},{3,1},{4,6},{5,7},{10,8},{11,9},{12,14},{13,15},{18,16},{19,... | collective-permute-start | bytes 1572872 | tf_op jit(solution)/shard_map/ppermute | solution.py:183
  225.2 1.9 collective-permute-start.47
  (17 other events, 60.1 us)

commit v7 on v6

--- a/solution.py
+++ b/solution.py
@@ -12,7 +12,8 @@
 UNITS = sum(map(sum, GROUPS))
 DELAY = 3
 SWAPS = (6, 8)
-VMEM_BYTES = 60 * 1024 * 1024
+CONV_VMEM = 44 * 1024 * 1024
+PRODUCT_VMEM = 22 * 1024 * 1024
 
 
 def conv_kernel(tile, at_ctx, out_grad, gate_in, conv_in, scan_grad, taps, bias, skip, *refs):
@@ -89,7 +90,7 @@
             scratch_shapes=[pltpu.VMEM((block, length), jnp.bfloat16), pltpu.VMEM((block, 8), jnp.float32)],
         ),
         out_shape=[jax.ShapeDtypeStruct((window, channels), jnp.bfloat16)] * ctx_count,
-        compiler_params=pltpu.CompilerParams(vmem_limit_bytes=VMEM_BYTES),
+        compiler_params=pltpu.CompilerParams(vmem_limit_bytes=CONV_VMEM),
         cost_estimate=pl.CostEstimate(
             flops=40 * channels * length, bytes_accessed=10 * channels * length, transcendentals=2 * channels * length
         ),
@@ -105,8 +106,13 @@
     left = jnp.concatenate([ref[...] for ref in left_refs], axis=1)
     right = jnp.concatenate([ref[...] for ref in right_refs], axis=0)
     total = jnp.dot(left, right, preferred_element_type=jnp.float32)
-    mine = pl.program_id(0) == place[0]
-    total = total + jnp.where(mine, resid[...].astype(jnp.float32), 0.0)
+    many = left.shape[0] // resid.shape[0]
+    parts = []
+    for part in range(many):
+        mine = pl.program_id(0) * many + part == place[0]
+        rows = total[part * resid.shape[0] : (part + 1) * resid.shape[0]]
+        parts.append(rows + jnp.where(mine, resid[...].astype(jnp.float32), 0.0))
+    total = jnp.concatenate(parts, axis=0)
     at = 0
     for out in outs:
         out[...] = total[:, at : at + out.shape[1]].astype(out.dtype)
@@ -116,7 +122,7 @@
 def matmul(lefts, rights, resid, place, widths):
     tokens, depth = lefts[0].shape
     width = rights[0].shape[1]
-    tile = resid.shape[0]
+    tile = 2 * resid.shape[0]
     flops = 2 * tokens * depth * len(lefts) * width
     moved = 2 * (tokens * depth * len(lefts) + depth * len(lefts) * width + tokens * width)
     return pl.pallas_call(
@@ -130,7 +136,7 @@
             out_specs=[pl.BlockSpec((tile, part), lambda step, place: (step, 0)) for part in widths],
         ),
         out_shape=[jax.ShapeDtypeStruct((tokens, part), jnp.bfloat16) for part in widths],
-        compiler_params=pltpu.CompilerParams(vmem_limit_bytes=VMEM_BYTES),
+        compiler_params=pltpu.CompilerParams(vmem_limit_bytes=PRODUCT_VMEM),
         cost_estimate=pl.CostEstimate(flops=flops, bytes_accessed=moved, transcendentals=0),
         name="partial_product",
     )(place, *lefts, *rights, resid)
@@ -216,9 +222,7 @@
     )
     turned, rights[0] = lax.optimization_barrier((turned, rights[0]))
     lefts = [turned[0], to_core(turned[0])]
-    for offset in range(1, ctx_count):
-        piece = to_ctx(turned[offset], offset)
-        lefts += [piece, to_core(piece)]
+    received = [to_ctx(turned[offset], offset) for offset in range(1, ctx_count)]
     lefts[1], projection, resid_grad, routes = lax.optimization_barrier((lefts[1], projection, resid_grad, routes))
 
     routed = jnp.concatenate([routes.T.astype(jnp.float32), gate_probs.T], axis=0)[None]
@@ -235,6 +239,10 @@
     for group, at in list(zip(widths, starts))[1:]:
         cut = slice(at - first, at - first + sum(group))
         rest.append(jnp.concatenate([rest_here[:, cut], rest_there[:, cut]], axis=0))
+    received[-2], rest = lax.optimization_barrier((received[-2], rest))
+    rights.append(spread(rest[0]))
+    for piece in received:
+        lefts += [piece, to_core(piece)]
     resid_here, resid_there = both_cores(resid_grad, 0, half)
     resid = jnp.where(
         core_at == 0,
@@ -305,7 +313,6 @@
     outer, across = {}, {}
     first_of = [sum(map(len, GROUPS[:at])) for at in range(len(GROUPS))]
     sums[0][: len(GROUPS[0])] = products(0, rights[0])
-    rights.append(spread(rest[0]))
     near = None
     for step in range(pieces + 2 * lag * hops + DELAY + 1):
         for hop in range(hops):
@@ -325,15 +332,17 @@
             got, index = across[step - 1]
             own, got = chain(sums[hops][index], got)
             ready[hops][index] = add(own, got)
+        if square and near is not None and step % 2:
+            near = spread_on(near)
         if step and step in first_of:
             group_at = first_of.index(step)
             if near is not None:
                 rights.append(near)
-            sums[0][step : step + len(GROUPS[group_at])] = products(group_at, rights[group_at])
             near = None
             if group_at + 1 < len(GROUPS):
-                (piece,) = chain(rest[group_at])
+                piece, *rights[group_at] = chain(rest[group_at], *rights[group_at])
                 near = spread_near(piece) if square else spread(piece)
+            sums[0][step : step + len(GROUPS[group_at])] = products(group_at, rights[group_at])
         for hop in range(hops):
             inward = step - lag * hop
             outward = inward - DELAY - 2 * lag * (hops - 1 - hop)
@@ -349,8 +358,6 @@
                 continue
             (payload,) = chain(payload)
             outer[step, hop] = (swap_chips(payload, hop, inward is not None, outward is not None), inward, outward)
-        if square and near is not None and step % 2:
-            near = spread_on(near)
     result = jnp.where(
         core_at == 0,
         jnp.concatenate(rows_own + rows_got, axis=1),

time: 231 us -> 228 us (0.987)
  local copies, waits for them, and re-layouts: 14 us -> 33.3 us
  waiting for transfers between devices: 96.5 us -> 78.2 us
  starting transfers between devices: 51.6 us -> 64.4 us
  Pallas kernels: 44.1 us -> 31.8 us
  other arithmetic: 20.1 us -> 15.1 us
    ppermute x17, waiting for transfers between devices: 46.3 us -> 23 us  [to_ctx(): lax.ppermute(array, 'ctx', [(place, place ^ offset) for place in range(ct...]
    unnamed x90 -> x100, local copies, waits for them, and re-layouts: 6.31 us -> 22.8 us
    ppermute x19, starting transfers between devices: 26.2 us -> 38 us  [swap_chips(): return lax.ppermute(array, 'exp', sorted(pairs))]
    pallas_call x4, Pallas kernels: 25.8 us -> 15.2 us  [matmul(): pl.pallas_call(functools.partial(matmul_kernel, len(lefts), len(rights)),...]
    ppermute x19, waiting for transfers between devices: 46.4 us -> 52.7 us  [swap_chips(): return lax.ppermute(array, 'exp', sorted(pairs))]
    select_n x5, other arithmetic: 7.13 us -> 2.16 us  [on_device(): jnp.where(distance == hop, sums[hop][inward], ready[hop + 1][outward])]
  transfers between devices with their start and end apart: 48 -> 48, of which waited for: 23 -> 14; matrix products, arithmetic and copies ran while one was open for 11% -> 11% of each run, Pallas kernels for 16% -> 12%
where the time goes in v7:
time: 228 us; the launch traced here: 226 us
  waiting for transfers between devices  78.2 us (34%)
  starting transfers between devices  64.4 us (28%)
  local copies, waits for them, and re-layouts  33.3 us (15%)
  Pallas kernels  31.8 us (14%)
  other arithmetic  15.1 us (7%)
  matrix products  2.34 us (1%)
    ppermute x19, waiting for transfers between devices, swap_chips(): return lax.ppermute(array, 'exp', sorted(pairs))  52.7 us
    ppermute x19, starting transfers between devices, swap_chips(): return lax.ppermute(array, 'exp', sorted(pairs))  38 us
    ppermute x17, waiting for transfers between devices, to_ctx(): lax.ppermute(array, 'ctx', [(place, place ^ offset) for place in range(ct...  23 us
    unnamed x100, local copies, waits for them, and re-layouts  22.8 us
    ppermute x17, starting transfers between devices, to_ctx(): lax.ppermute(array, 'ctx', [(place, place ^ offset) for place in range(ct...  19.9 us
    pallas_call x1, Pallas kernels, conv_grad(): pl.pallas_call(functools.partial(conv_kernel, tile), grid_spec=pltpu.Pref...  16.6 us
    pallas_call x4, Pallas kernels, matmul(): pl.pallas_call(functools.partial(matmul_kernel, len(lefts), len(rights)),...  15.2 us
    dynamic_slice x3, local copies, waits for them, and re-layouts, columns_of(): return lax.dynamic_slice_in_dim(array, core * half + at, width, 1)  5.58 us
  transfers between devices with their start and end apart: 48, of which 14 were waited for; matrix products, arithmetic and copies ran while one was open for 11% of the time, Pallas kernels for 12%

profile of v7, /device:TPU:0, one launch (start us, length us, event | category | flops | bytes accessed | tf_op | source)
XLA Modules:
  0.0 226.3 jit_solution(11268134410897635707)
XLA Ops:
  0.0 1.1 constant_dynamic-slice_fusion.7
  1.6 1.2 collective-permute-done
  2.8 3.9 %collective-permute-start.3 = (bf16[512,512]{1,0:T(8,128)(2,1)S(1)}, bf16[512,512]{1,0:T(8,128)(2,1)S(1)}, u32[]{:S(2)}, u32[]{:S(2)}) collective-permute-start(bf16[512,512]{1,0:T(8,128)(2,1)S(1)} %pad_maximum_fusion.refs_8_), channel_id=1, source_target_pairs={{0,24},{8,16},{16,8},{24,0},{1,25},{9,17},{17,9},{25,1},{2,26},{10... | collective-permute-start | bytes 1572872 | tf_op jit(solution)/shard_map/ppermute | solution.py:179
  7.3 1.6 copy-done
  8.9 1.6 copy-done.1
  10.5 1.6 copy-done.2
  14.1 16.6 %conv_grad.1 = (bf16[1024,256]{1,0:T(8,128)(2,1)S(1)}, bf16[1024,256]{1,0:T(8,128)(2,1)S(1)}, bf16[1024,256]{1,0:T(8,128)(2,1)S(1)}, bf16[1024,256]{1,0:T(8,128)(2,1)S(1)}) custom-call(s32[1]{0:T(128)} %bitcast.1.at_ctx, bf16[256,4096]{1,0:T(8,128)(2,1)S(1)} %copy-done, bf16[256,4096]{1,0:T(8,128)(2,1)S(1)} %copy-done.1, bf16[256,4096]{1,0:T(8,128)(2,1)S(1)} %copy-done.2, ...), custom_call_target="tpu_custom_call" | custom-call | flops 41943040 | bytes 10485760 | tf_op jit(solution)/shard_map/conv_grad/pallas_call | solution.py:82
  34.3 1.9 collective-permute-start.8
  36.2 1.5 collective-permute-start.10
  37.9 2.2 constant_dynamic-slice_fusion.4
  40.5 2.0 collective-permute-start.6
  42.4 2.4 %constant_dynamic-slice_fusion.3 = (bf16[128,2048]{1,0:T(8,128)(2,1)}, bf16[128,2048]{1,0:T(8,128)(2,1)}) fusion(bf16[128,4096]{1,0:T(8,128)(2,1)} %param.19, s32[]{:T(128)S(6)} %select_n.138, s32[]{:T(128)S(6)} %select_n.139), kind=kLoop, calls=%fused_computation.109 | loop fusion | bytes 2097160 | tf_op jit(solution)/shard_map/dynamic_slice | solution.py:192
  44.8 2.7 %collective-permute-start.7 = (f32[4,4,128]{2,1,0:T(4,128)S(1)}, f32[4,4,128]{2,1,0:T(4,128)S(1)}, u32[]{:S(2)}, u32[]{:S(2)}) collective-permute-start(f32[4,4,128]{2,1,0:T(4,128)S(1)} %pad_maximum_fusion.6), channel_id=1, source_target_pairs={{0,4},{1,5},{2,6},{3,7},{4,0},{5,1},{6,2},{7,3},{8,12},{9,13},{10,... | collective-permute-start | bytes 24584 | tf_op jit(solution)/shard_map/ppermute | solution.py:231
  47.5 2.0 constant_dynamic-slice_fusion.5
  49.5 12.2 %collective-permute-done.13.refs_6_ = bf16[1024,256]{1,0:T(8,128)(2,1)} collective-permute-done((bf16[1024,256]{1,0:T(8,128)(2,1)}, bf16[1024,256]{1,0:T(8,128)(2,1)}, u32[]{:S(2)}, u32[]{:S(2)}) %collective-permute-start.13) | collective-permute-done | bytes 524320 | tf_op jit(solution)/shard_map/ppermute | solution.py:179
  63.1 1.2 fusion.23
  64.5 1.2 pad_maximum_fusion.1
  67.0 1.6 maximum_select_fusion
  68.8 1.1 copy-done.15
  69.8 3.7 %partial_product.4 = (bf16[1024,256]{1,0:T(8,128)(2,1)S(1)}, bf16[1024,256]{1,0:T(8,128)(2,1)S(1)}) custom-call(s32[1]{0:T(128)} %bitcast.place, bf16[1024,256]{1,0:T(8,128)(2,1)S(1)} %copy-done.9, bf16[1024,256]{1,0:T(8,128)(2,1)S(1)} %copy-done.12, bf16[1024,256]{1,0:T(8,128)(2,1)S(1)} %copy-done.15, bf16[1024,256]{1,0:T(8,128)(2,1)} %collective-permute-done.9.refs_3_, ...), custom_call_target="tpu_custom_call" | custom-call | flops 2147483648 | bytes 7340032 | tf_op jit(solution)/shard_map/partial_product/pallas_call | solution.py:128
  73.6 3.5 %collective-permute-start.19 = (bf16[1024,256]{1,0:T(8,128)(2,1)S(1)}, bf16[1024,256]{1,0:T(8,128)(2,1)S(1)}, u32[]{:S(2)}, u32[]{:S(2)}) collective-permute-start(bf16[1024,256]{1,0:T(8,128)(2,1)S(1)} %get-tuple-element.180), channel_id=1, source_target_pairs={{0,2},{1,3},{6,4},{7,5},{8,10},{9,11},{14,12},{15,13},{16,18},{17,... | collective-permute-start | bytes 1572872 | tf_op jit(solution)/shard_map/ppermute | solution.py:189
  77.1 1.5 collective-permute-start.18
  78.6 1.4 collective-permute-start.17
  80.7 2.1 collective-permute-start.21
  82.7 6.5 %collective-permute-done.19 = bf16[1024,256]{1,0:T(8,128)(2,1)S(1)} collective-permute-done((bf16[1024,256]{1,0:T(8,128)(2,1)S(1)}, bf16[1024,256]{1,0:T(8,128)(2,1)S(1)}, u32[]{:S(2)}, u32[]{:S(2)}) %collective-permute-start.19) | collective-permute-done | bytes 524320 | tf_op jit(solution)/shard_map/ppermute | solution.py:189
  90.2 1.5 collective-permute-start.20
  91.7 1.1 collective-permute-done.18.refs_11_
  93.7 9.6 %collective-permute-done.17.refs_10_ = bf16[512,512]{1,0:T(8,128)(2,1)S(1)} collective-permute-done((bf16[512,512]{1,0:T(8,128)(2,1)S(1)}, bf16[512,512]{1,0:T(8,128)(2,1)S(1)}, u32[]{:S(2)}, u32[]{:S(2)}) %collective-permute-start.17) | collective-permute-done | bytes 524320 | tf_op jit(solution)/shard_map/ppermute | solution.py:179
  105.8 1.2 collective-permute-start.22
  107.0 1.0 copy-done.10
  108.0 1.0 copy-done.13
  109.1 1.0 copy-done.16
  110.1 1.0 copy-done.18
  111.1 1.0 copy-done.29
  112.2 1.0 copy-done.31
  113.2 1.0 copy-done.33
  114.3 3.7 %partial_product.5 = (bf16[1024,256]{1,0:T(8,128)(2,1)S(1)}, bf16[1024,256]{1,0:T(8,128)(2,1)S(1)}) custom-call(s32[1]{0:T(128)} %bitcast.place, bf16[1024,256]{1,0:T(8,128)(2,1)S(1)} %copy-done.10, bf16[1024,256]{1,0:T(8,128)(2,1)S(1)} %copy-done.13, bf16[1024,256]{1,0:T(8,128)(2,1)S(1)} %copy-done.16, bf16[1024,256]{1,0:T(8,128)(2,1)} %collective-permute-done.9.refs_3_, ...), custom_call_target="tpu_custom_call" | custom-call | flops 2147483648 | bytes 7340032 | tf_op jit(solution)/shard_map/partial_product/pallas_call | solution.py:128
  118.0 1.6 collective-permute-start.28
  119.6 1.2 add_convert_fusion.14
  121.5 1.1 slice.149
  123.6 1.2 collective-permute-start.25
  124.8 1.4 broadcast_select_fusion.13
  126.2 2.2 collective-permute-start.24
  128.4 3.5 %collective-permute-done.28 = bf16[1024,256]{1,0:T(8,128)(2,1)S(1)} collective-permute-done((bf16[1024,256]{1,0:T(8,128)(2,1)S(1)}, bf16[1024,256]{1,0:T(8,128)(2,1)S(1)}, u32[]{:S(2)}, u32[]{:S(2)}) %collective-permute-start.28) | collective-permute-done | bytes 524320 | tf_op jit(solution)/shard_map/ppermute | solution.py:189
  133.4 1.5 collective-permute-start.31
  135.9 4.0 %partial_product.6 = (bf16[1024,256]{1,0:T(8,128)(2,1)S(1)}, bf16[1024,256]{1,0:T(8,128)(2,1)S(1)}) custom-call(s32[1]{0:T(128)} %bitcast.place, bf16[1024,256]{1,0:T(8,128)(2,1)S(1)} %copy-done.10, bf16[1024,256]{1,0:T(8,128)(2,1)S(1)} %copy-done.13, bf16[1024,256]{1,0:T(8,128)(2,1)S(1)} %copy-done.16, bf16[1024,256]{1,0:T(8,128)(2,1)} %collective-permute-done.9.refs_3_, ...), custom_call_target="tpu_custom_call" | custom-call | flops 2147483648 | bytes 7340032 | tf_op jit(solution)/shard_map/partial_product/pallas_call | solution.py:128
  140.1 5.3 %collective-permute-start.29 = (bf16[1024,256]{1,0:T(8,128)(2,1)S(1)}, bf16[1024,256]{1,0:T(8,128)(2,1)S(1)}, u32[]{:S(2)}, u32[]{:S(2)}) collective-permute-start(bf16[1024,256]{1,0:T(8,128)(2,1)S(1)} %broadcast_select_fusion.12), channel_id=1, source_target_pairs={{0,2},{1,3},{2,0},{3,1},{4,6},{5,7},{6,4},{7,5},{8,10},{9,11},{10,... | collective-permute-start | bytes 1572872 | tf_op jit(solution)/shard_map/ppermute | solution.py:189
  145.5 1.4 broadcast_select_fusion.11
  149.0 1.5 collective-permute-start.34
  150.5 2.1 collective-permute-start.33
  152.6 4.6 %collective-permute-done.29 = bf16[1024,256]{1,0:T(8,128)(2,1)S(1)} collective-permute-done((bf16[1024,256]{1,0:T(8,128)(2,1)S(1)}, bf16[1024,256]{1,0:T(8,128)(2,1)S(1)}, u32[]{:S(2)}, u32[]{:S(2)}) %collective-permute-start.29) | collective-permute-done | bytes 524320 | tf_op jit(solution)/shard_map/ppermute | solution.py:189
  158.8 3.8 %partial_product.7 = (bf16[1024,256]{1,0:T(8,128)(2,1)S(1)}, bf16[1024,256]{1,0:T(8,128)(2,1)S(1)}) custom-call(s32[1]{0:T(128)} %bitcast.place, bf16[1024,256]{1,0:T(8,128)(2,1)S(1)} %copy-done.10, bf16[1024,256]{1,0:T(8,128)(2,1)S(1)} %copy-done.13, bf16[1024,256]{1,0:T(8,128)(2,1)S(1)} %copy-done.16, bf16[1024,256]{1,0:T(8,128)(2,1)} %collective-permute-done.9.refs_3_, ...), custom_call_target="tpu_custom_call" | custom-call | flops 2147483648 | bytes 7340032 | tf_op jit(solution)/shard_map/partial_product/pallas_call | solution.py:128
  162.8 5.4 %collective-permute-start.37 = (bf16[1024,256]{1,0:T(8,128)(2,1)S(1)}, bf16[1024,256]{1,0:T(8,128)(2,1)S(1)}, u32[]{:S(2)}, u32[]{:S(2)}) collective-permute-start(bf16[1024,256]{1,0:T(8,128)(2,1)S(1)} %broadcast_select_fusion.8), channel_id=1, source_target_pairs={{0,2},{1,3},{2,0},{3,1},{4,6},{5,7},{6,4},{7,5},{8,10},{9,11},{10,... | collective-permute-start | bytes 1572872 | tf_op jit(solution)/shard_map/ppermute | solution.py:189
  170.0 5.4 %collective-permute-start.39 = (bf16[1024,256]{1,0:T(8,128)(2,1)S(1)}, bf16[1024,256]{1,0:T(8,128)(2,1)S(1)}, u32[]{:S(2)}, u32[]{:S(2)}) collective-permute-start(bf16[1024,256]{1,0:T(8,128)(2,1)S(1)} %broadcast_select_fusion.6), channel_id=1, source_target_pairs={{0,2},{1,3},{2,0},{3,1},{4,6},{5,7},{6,4},{7,5},{8,10},{9,11},{10,... | collective-permute-start | bytes 1572872 | tf_op jit(solution)/shard_map/ppermute | solution.py:189
  175.5 5.5 %collective-permute-done.37 = bf16[1024,256]{1,0:T(8,128)(2,1)S(1)} collective-permute-done((bf16[1024,256]{1,0:T(8,128)(2,1)S(1)}, bf16[1024,256]{1,0:T(8,128)(2,1)S(1)}, u32[]{:S(2)}, u32[]{:S(2)}) %collective-permute-start.37) | collective-permute-done | bytes 524320 | tf_op jit(solution)/shard_map/ppermute | solution.py:189
  182.6 1.3 collective-permute-start.41
  183.9 8.4 %collective-permute-done.39 = bf16[1024,256]{1,0:T(8,128)(2,1)S(1)} collective-permute-done((bf16[1024,256]{1,0:T(8,128)(2,1)S(1)}, bf16[1024,256]{1,0:T(8,128)(2,1)S(1)}, u32[]{:S(2)}, u32[]{:S(2)}) %collective-permute-start.39) | collective-permute-done | bytes 524320 | tf_op jit(solution)/shard_map/ppermute | solution.py:189
  193.8 1.3 collective-permute-start.43
  195.3 8.2 %collective-permute-done.41 = bf16[1024,256]{1,0:T(8,128)(2,1)S(1)} collective-permute-done((bf16[1024,256]{1,0:T(8,128)(2,1)S(1)}, bf16[1024,256]{1,0:T(8,128)(2,1)S(1)}, u32[]{:S(2)}, u32[]{:S(2)}) %collective-permute-start.41) | collective-permute-done | bytes 524320 | tf_op jit(solution)/shard_map/ppermute | solution.py:189
  203.8 1.3 collective-permute-start.45
  205.3 9.4 %collective-permute-done.43 = bf16[1024,256]{1,0:T(8,128)(2,1)S(1)} collective-permute-done((bf16[1024,256]{1,0:T(8,128)(2,1)S(1)}, bf16[1024,256]{1,0:T(8,128)(2,1)S(1)}, u32[]{:S(2)}, u32[]{:S(2)}) %collective-permute-start.43) | collective-permute-done | bytes 524320 | tf_op jit(solution)/shard_map/ppermute | solution.py:189
  215.1 6.3 %collective-permute-done.45 = bf16[1024,256]{1,0:T(8,128)(2,1)S(1)} collective-permute-done((bf16[1024,256]{1,0:T(8,128)(2,1)S(1)}, bf16[1024,256]{1,0:T(8,128)(2,1)S(1)}, u32[]{:S(2)}, u32[]{:S(2)}) %collective-permute-start.45) | collective-permute-done | bytes 524320 | tf_op jit(solution)/shard_map/ppermute | solution.py:189
  222.3 1.4 collective-permute-done.47
  224.1 2.2 broadcast_select_fusion
  (221 shorter events, 30.2 us)
Async XLA Ops:
  1.1 1.7 collective-permute-start
  2.8 30.3 %collective-permute-start.3 = (bf16[512,512]{1,0:T(8,128)(2,1)S(1)}, bf16[512,512]{1,0:T(8,128)(2,1)S(1)}, u32[]{:S(2)}, u32[]{:S(2)}) collective-permute-start(bf16[512,512]{1,0:T(8,128)(2,1)S(1)} %pad_maximum_fusion.refs_8_), channel_id=1, source_target_pairs={{0,24},{8,16},{16,8},{24,0},{1,25},{9,17},{17,9},{25,1},{2,26},{10... | collective-permute-start | bytes 1572872 | tf_op jit(solution)/shard_map/ppermute | solution.py:179
  6.7 27.3 %collective-permute-start.2 = (bf16[512,512]{1,0:T(8,128)(2,1)S(1)}, bf16[512,512]{1,0:T(8,128)(2,1)S(1)}, u32[]{:S(2)}, u32[]{:S(2)}) collective-permute-start(bf16[512,512]{1,0:T(8,128)(2,1)S(1)} %pad_maximum_fusion.refs_8_), channel_id=1, source_target_pairs={{0,16},{8,24},{16,0},{24,8},{1,17},{9,25},{17,1},{25,9},{2,18},{10... | collective-permute-start | bytes 1572872 | tf_op jit(solution)/shard_map/ppermute | solution.py:179
  7.2 26.8 %collective-permute-start.1 = (bf16[512,512]{1,0:T(8,128)(2,1)S(1)}, bf16[512,512]{1,0:T(8,128)(2,1)S(1)}, u32[]{:S(2)}, u32[]{:S(2)}) collective-permute-start(bf16[512,512]{1,0:T(8,128)(2,1)S(1)} %pad_maximum_fusion.refs_8_), channel_id=1, source_target_pairs={{0,8},{8,0},{16,24},{24,16},{1,9},{9,1},{17,25},{25,17},{2,10},{10... | collective-permute-start | bytes 1572872 | tf_op jit(solution)/shard_map/ppermute | solution.py:179
  14.1 23.7 %copy-start.36 = (s32[128,2]{0,1:T(2,128)S(1)}, s32[128,2]{0,1:T(2,128)}, u32[]{:S(2)}) copy-start(s32[128,2]{0,1:T(2,128)} %param.20) | copy-start | bytes 3076
  14.1 23.7 %copy-start.37 = (f32[128,2]{0,1:T(2,128)S(1)}, f32[128,2]{0,1:T(2,128)}, u32[]{:S(2)}) copy-start(f32[128,2]{0,1:T(2,128)} %param.21) | copy-start | bytes 3076
  33.1 31.4 %copy-start.8 = (bf16[1024,256]{1,0:T(8,128)(2,1)}, bf16[1024,256]{1,0:T(8,128)(2,1)S(1)}, u32[]{:S(2)}) copy-start(bf16[1024,256]{1,0:T(8,128)(2,1)S(1)} %get-tuple-element.158.refs_0_) | copy-start | bytes 1572868
  34.0 30.5 %copy-start.21 = (bf16[512,512]{1,0:T(8,128)(2,1)}, bf16[512,512]{1,0:T(8,128)(2,1)S(1)}, u32[]{:S(2)}) copy-start(bf16[512,512]{1,0:T(8,128)(2,1)S(1)} %collective-permute-done.2.refs_10_) | copy-start | bytes 1572868
  34.0 30.5 %copy-start.23 = (bf16[512,512]{1,0:T(8,128)(2,1)}, bf16[512,512]{1,0:T(8,128)(2,1)S(1)}, u32[]{:S(2)}) copy-start(bf16[512,512]{1,0:T(8,128)(2,1)S(1)} %collective-permute-done.1.refs_9_) | copy-start | bytes 1572868
  34.0 3.8 %collective-permute-start.4 = (bf16[1024,256]{1,0:T(8,128)(2,1)S(1)}, bf16[1024,256]{1,0:T(8,128)(2,1)S(1)}, u32[]{:S(2)}, u32[]{:S(2)}) collective-permute-start(bf16[1024,256]{1,0:T(8,128)(2,1)S(1)} %get-tuple-element.158.refs_0_), channel_id=1, source_target_pairs={{0,1},{1,0},{2,3},{3,2},{4,5},{5,4},{6,7},{7,6},{8,9},{9,8},{10,11... | collective-permute-start | bytes 1572872 | tf_op jit(solution)/shard_map/ppermute | solution.py:176
  34.3 15.2 %collective-permute-start.8 = (bf16[1024,256]{1,0:T(8,128)(2,1)}, bf16[1024,256]{1,0:T(8,128)(2,1)S(1)}, u32[]{:S(2)}, u32[]{:S(2)}) collective-permute-start(bf16[1024,256]{1,0:T(8,128)(2,1)} %copy-done.27), channel_id=1, source_target_pairs={{0,8},{8,0},{16,24},{24,16},{1,9},{9,1},{17,25},{25,17},{2,10},{10... | collective-permute-start | bytes 1572872 | tf_op jit(solution)/shard_map/ppermute | solution.py:179
  36.2 29.6 %collective-permute-start.10 = (bf16[1024,256]{1,0:T(8,128)(2,1)}, bf16[1024,256]{1,0:T(8,128)(2,1)}, u32[]{:S(2)}, u32[]{:S(2)}) collective-permute-start(bf16[1024,256]{1,0:T(8,128)(2,1)} %copy-done.25), channel_id=1, source_target_pairs={{0,16},{8,24},{16,0},{24,8},{1,17},{9,25},{17,1},{25,9},{2,18},{10... | collective-permute-start | bytes 1572872 | tf_op jit(solution)/shard_map/ppermute | solution.py:179
  37.7 23.9 %collective-permute-start.13 = (bf16[1024,256]{1,0:T(8,128)(2,1)}, bf16[1024,256]{1,0:T(8,128)(2,1)}, u32[]{:S(2)}, u32[]{:S(2)}) collective-permute-start(bf16[1024,256]{1,0:T(8,128)(2,1)} %copy-done.26), channel_id=1, source_target_pairs={{0,24},{8,16},{16,8},{24,0},{1,25},{9,17},{17,9},{25,1},{2,26},{10... | collective-permute-start | bytes 1572872 | tf_op jit(solution)/shard_map/ppermute | solution.py:179
  37.8 26.6 %copy-start.11 = (bf16[1024,256]{1,0:T(8,128)(2,1)}, bf16[1024,256]{1,0:T(8,128)(2,1)S(1)}, u32[]{:S(2)}) copy-start(bf16[1024,256]{1,0:T(8,128)(2,1)S(1)} %collective-permute-done.4.refs_1_) | copy-start | bytes 1572868
  37.8 2.6 %collective-permute-start.5 = (f32[1,4,128]{2,1,0:T(4,128)S(1)}, f32[1,4,128]{2,1,0:T(4,128)S(1)}, u32[]{:S(2)}, u32[]{:S(2)}) collective-permute-start(f32[1,4,128]{2,1,0:T(4,128)S(1)} %maximum_bitcast_fusion), channel_id=1, source_target_pairs={{0,1},{1,0},{2,3},{3,2},{4,5},{5,4},{6,7},{7,6},{8,9},{9,8},{10,11... | collective-permute-start | bytes 6152 | tf_op jit(solution)/shard_map/ppermute | solution.py:231
  40.1 23.1 %collective-permute-start.11 = (bf16[256,1536]{1,0:T(8,128)(2,1)}, bf16[256,1536]{1,0:T(8,128)(2,1)}, u32[]{:S(2)}, u32[]{:S(2)}) collective-permute-start(bf16[256,1536]{1,0:T(8,128)(2,1)} %constant_dynamic-slice_fusion.4), channel_id=1, source_target_pairs={{0,1},{1,0},{2,3},{3,2},{4,5},{5,4},{6,7},{7,6},{8,9},{9,8},{10,11... | collective-permute-start | bytes 2359304 | tf_op jit(solution)/shard_map/ppermute | solution.py:176
  40.5 4.3 %collective-permute-start.6 = (f32[2,4,128]{2,1,0:T(4,128)S(1)}, f32[2,4,128]{2,1,0:T(4,128)S(1)}, u32[]{:S(2)}, u32[]{:S(2)}) collective-permute-start(f32[2,4,128]{2,1,0:T(4,128)S(1)} %pad_maximum_fusion.7), channel_id=1, source_target_pairs={{0,2},{1,3},{2,0},{3,1},{4,6},{5,7},{6,4},{7,5},{8,10},{9,11},{10,... | collective-permute-start | bytes 12296 | tf_op jit(solution)/shard_map/ppermute | solution.py:231
  44.8 16.8 %collective-permute-start.7 = (f32[4,4,128]{2,1,0:T(4,128)S(1)}, f32[4,4,128]{2,1,0:T(4,128)S(1)}, u32[]{:S(2)}, u32[]{:S(2)}) collective-permute-start(f32[4,4,128]{2,1,0:T(4,128)S(1)} %pad_maximum_fusion.6), channel_id=1, source_target_pairs={{0,4},{1,5},{2,6},{3,7},{4,0},{5,1},{6,2},{7,3},{8,12},{9,13},{10,... | collective-permute-start | bytes 24584 | tf_op jit(solution)/shard_map/ppermute | solution.py:231
  49.4 19.1 %copy-start.14 = (bf16[1024,256]{1,0:T(8,128)(2,1)}, bf16[1024,256]{1,0:T(8,128)(2,1)S(1)}, u32[]{:S(2)}) copy-start(bf16[1024,256]{1,0:T(8,128)(2,1)S(1)} %collective-permute-done.8.refs_2_) | copy-start | bytes 1572868
  49.4 17.5 %collective-permute-start.15 = (bf16[128,2048]{1,0:T(8,128)(2,1)}, bf16[128,2048]{1,0:T(8,128)(2,1)}, u32[]{:S(2)}, u32[]{:S(2)}) collective-permute-start(bf16[128,2048]{1,0:T(8,128)(2,1)} %get-tuple-element.271), channel_id=1, source_target_pairs={{0,1},{1,0},{2,3},{3,2},{4,5},{5,4},{6,7},{7,6},{8,9},{9,8},{10,11... | collective-permute-start | bytes 1572872 | tf_op jit(solution)/shard_map/ppermute | solution.py:176
  61.6 6.9 %collective-permute-start.9 = (bf16[1024,256]{1,0:T(8,128)(2,1)S(1)}, bf16[1024,256]{1,0:T(8,128)(2,1)}, u32[]{:S(2)}, u32[]{:S(2)}) collective-permute-start(bf16[1024,256]{1,0:T(8,128)(2,1)S(1)} %collective-permute-done.8.refs_2_), channel_id=1, source_target_pairs={{0,1},{1,0},{2,3},{3,2},{4,5},{5,4},{6,7},{7,6},{8,9},{9,8},{10,11... | collective-permute-start | bytes 1572872 | tf_op jit(solution)/shard_map/ppermute | solution.py:176
  61.6 6.9 %collective-permute-start.14 = (bf16[1024,256]{1,0:T(8,128)(2,1)}, bf16[1024,256]{1,0:T(8,128)(2,1)}, u32[]{:S(2)}, u32[]{:S(2)}) collective-permute-start(bf16[1024,256]{1,0:T(8,128)(2,1)} %collective-permute-done.13.refs_6_), channel_id=1, source_target_pairs={{0,1},{1,0},{2,3},{3,2},{4,5},{5,4},{6,7},{7,6},{8,9},{9,8},{10,11... | collective-permute-start | bytes 1572872 | tf_op jit(solution)/shard_map/ppermute | solution.py:176
  63.1 3.9 %copy-start.35 = (bf16[128,2048]{1,0:T(8,128)(2,1)S(1)}, bf16[128,2048]{1,0:T(8,128)(2,1)}, u32[]{:S(2)}) copy-start(bf16[128,2048]{1,0:T(8,128)(2,1)} %get-tuple-element.270) | copy-start | bytes 1572868
  64.4 4.3 %copy-start.12 = (bf16[1024,256]{1,0:T(8,128)(2,1)S(1)}, bf16[1024,256]{1,0:T(8,128)(2,1)}, u32[]{:S(2)}) copy-start(bf16[1024,256]{1,0:T(8,128)(2,1)} %copy-done.11) | copy-start | bytes 1572868
  64.4 4.3 %copy-start.20 = (bf16[512,512]{1,0:T(8,128)(2,1)S(1)}, bf16[512,512]{1,0:T(8,128)(2,1)}, u32[]{:S(2)}) copy-start(bf16[512,512]{1,0:T(8,128)(2,1)} %copy-done.19) | copy-start | bytes 1572868
  64.5 4.3 %copy-start.9 = (bf16[1024,256]{1,0:T(8,128)(2,1)S(1)}, bf16[1024,256]{1,0:T(8,128)(2,1)}, u32[]{:S(2)}) copy-start(bf16[1024,256]{1,0:T(8,128)(2,1)} %copy-done.8) | copy-start | bytes 1572868
  64.5 4.3 %copy-start.22 = (bf16[512,512]{1,0:T(8,128)(2,1)S(1)}, bf16[512,512]{1,0:T(8,128)(2,1)}, u32[]{:S(2)}) copy-start(bf16[512,512]{1,0:T(8,128)(2,1)} %copy-done.21) | copy-start | bytes 1572868
  64.5 4.3 %copy-start.24 = (bf16[512,512]{1,0:T(8,128)(2,1)S(1)}, bf16[512,512]{1,0:T(8,128)(2,1)}, u32[]{:S(2)}) copy-start(bf16[512,512]{1,0:T(8,128)(2,1)} %copy-done.23) | copy-start | bytes 1572868
  65.8 2.8 %collective-permute-start.12 = (bf16[1024,256]{1,0:T(8,128)(2,1)}, bf16[1024,256]{1,0:T(8,128)(2,1)S(1)}, u32[]{:S(2)}, u32[]{:S(2)}) collective-permute-start(bf16[1024,256]{1,0:T(8,128)(2,1)} %collective-permute-done.10.refs_4_), channel_id=1, source_target_pairs={{0,1},{1,0},{2,3},{3,2},{4,5},{5,4},{6,7},{7,6},{8,9},{9,8},{10,11... | collective-permute-start | bytes 1572872 | tf_op jit(solution)/shard_map/ppermute | solution.py:176
  68.6 5.0 %copy-start.17 = (bf16[1024,256]{1,0:T(8,128)(2,1)}, bf16[1024,256]{1,0:T(8,128)(2,1)S(1)}, u32[]{:S(2)}) copy-start(bf16[1024,256]{1,0:T(8,128)(2,1)S(1)} %collective-permute-done.12.refs_5_) | copy-start | bytes 1572868
  73.6 15.7 %collective-permute-start.19 = (bf16[1024,256]{1,0:T(8,128)(2,1)S(1)}, bf16[1024,256]{1,0:T(8,128)(2,1)S(1)}, u32[]{:S(2)}, u32[]{:S(2)}) collective-permute-start(bf16[1024,256]{1,0:T(8,128)(2,1)S(1)} %get-tuple-element.180), channel_id=1, source_target_pairs={{0,2},{1,3},{6,4},{7,5},{8,10},{9,11},{14,12},{15,13},{16,18},{17,... | collective-permute-start | bytes 1572872 | tf_op jit(solution)/shard_map/ppermute | solution.py:189
  77.1 15.8 %collective-permute-start.18 = (bf16[512,512]{1,0:T(8,128)(2,1)S(1)}, bf16[512,512]{1,0:T(8,128)(2,1)S(1)}, u32[]{:S(2)}, u32[]{:S(2)}) collective-permute-start(bf16[512,512]{1,0:T(8,128)(2,1)S(1)} %get-tuple-element.187.refs_8_), channel_id=1, source_target_pairs={{0,24},{8,16},{16,8},{24,0},{1,25},{9,17},{17,9},{25,1},{2,26},{10... | collective-permute-start | bytes 1572872 | tf_op jit(solution)/shard_map/ppermute | solution.py:179
  78.6 24.7 %collective-permute-start.17 = (bf16[512,512]{1,0:T(8,128)(2,1)S(1)}, bf16[512,512]{1,0:T(8,128)(2,1)S(1)}, u32[]{:S(2)}, u32[]{:S(2)}) collective-permute-start(bf16[512,512]{1,0:T(8,128)(2,1)S(1)} %get-tuple-element.187.refs_8_), channel_id=1, source_target_pairs={{0,16},{8,24},{16,0},{24,8},{1,17},{9,25},{17,1},{25,9},{2,18},{10... | collective-permute-start | bytes 1572872 | tf_op jit(solution)/shard_map/ppermute | solution.py:179
  80.0 24.2 %collective-permute-start.16 = (bf16[512,512]{1,0:T(8,128)(2,1)S(1)}, bf16[512,512]{1,0:T(8,128)(2,1)S(1)}, u32[]{:S(2)}, u32[]{:S(2)}) collective-permute-start(bf16[512,512]{1,0:T(8,128)(2,1)S(1)} %get-tuple-element.187.refs_8_), channel_id=1, source_target_pairs={{0,8},{8,0},{16,24},{24,16},{1,9},{9,1},{17,25},{25,17},{2,10},{10... | collective-permute-start | bytes 1572872 | tf_op jit(solution)/shard_map/ppermute | solution.py:179
  80.7 38.9 %collective-permute-start.21 = (bf16[1024,256]{1,0:T(8,128)(2,1)S(1)}, bf16[1024,256]{1,0:T(8,128)(2,1)}, u32[]{:S(2)}, u32[]{:S(2)}) collective-permute-start(bf16[1024,256]{1,0:T(8,128)(2,1)S(1)} %get-tuple-element.194), channel_id=1, source_target_pairs={{0,2},{1,3},{6,4},{7,5},{8,10},{9,11},{14,12},{15,13},{16,18},{17,... | collective-permute-start | bytes 1572872 | tf_op jit(solution)/shard_map/ppermute | solution.py:189
  90.2 31.3 %collective-permute-start.20 = (bf16[1024,256]{1,0:T(8,128)(2,1)}, bf16[1024,256]{1,0:T(8,128)(2,1)}, u32[]{:S(2)}, u32[]{:S(2)}) collective-permute-start(bf16[1024,256]{1,0:T(8,128)(2,1)} %add_convert_fusion.15), channel_id=1, source_target_pairs={{2,4},{3,5},{4,2},{5,3},{10,12},{11,13},{12,10},{13,11},{18,20},{1... | collective-permute-start | bytes 1572872 | tf_op jit(solution)/shard_map/ppermute | solution.py:189
  105.0 16.5 %collective-permute-start.23 = (bf16[512,512]{1,0:T(8,128)(2,1)S(1)}, bf16[512,512]{1,0:T(8,128)(2,1)S(1)}, u32[]{:S(2)}, u32[]{:S(2)}) collective-permute-start(bf16[512,512]{1,0:T(8,128)(2,1)S(1)} %get-tuple-element.211.refs_8_), channel_id=1, source_target_pairs={{0,8},{8,0},{16,24},{24,16},{1,9},{9,1},{17,25},{25,17},{2,10},{10... | collective-permute-start | bytes 1572872 | tf_op jit(solution)/shard_map/ppermute | solution.py:179
  105.8 15.8 %collective-permute-start.22 = (bf16[512,512]{1,0:T(8,128)(2,1)S(1)}, bf16[512,512]{1,0:T(8,128)(2,1)}, u32[]{:S(2)}, u32[]{:S(2)}) collective-permute-start(bf16[512,512]{1,0:T(8,128)(2,1)S(1)} %get-tuple-element.211.refs_8_), channel_id=1, source_target_pairs={{0,16},{8,24},{16,0},{24,8},{1,17},{9,25},{17,1},{25,9},{2,18},{10... | collective-permute-start | bytes 1572872 | tf_op jit(solution)/shard_map/ppermute | solution.py:179
  118.0 13.9 %collective-permute-start.28 = (bf16[1024,256]{1,0:T(8,128)(2,1)S(1)}, bf16[1024,256]{1,0:T(8,128)(2,1)S(1)}, u32[]{:S(2)}, u32[]{:S(2)}) collective-permute-start(bf16[1024,256]{1,0:T(8,128)(2,1)S(1)} %get-tuple-element.202), channel_id=1, source_target_pairs={{0,2},{1,3},{6,4},{7,5},{8,10},{9,11},{14,12},{15,13},{16,18},{17,... | collective-permute-start | bytes 1572872 | tf_op jit(solution)/shard_map/ppermute | solution.py:189
  120.8 12.0 %collective-permute-start.27 = (bf16[1024,256]{1,0:T(8,128)(2,1)S(1)}, bf16[1024,256]{1,0:T(8,128)(2,1)S(1)}, u32[]{:S(2)}, u32[]{:S(2)}) collective-permute-start(bf16[1024,256]{1,0:T(8,128)(2,1)S(1)} %add_convert_fusion.14), channel_id=1, source_target_pairs={{2,4},{3,5},{4,2},{5,3},{10,12},{11,13},{12,10},{13,11},{18,20},{1... | collective-permute-start | bytes 1572872 | tf_op jit(solution)/shard_map/ppermute | solution.py:189
  121.5 11.3 %copy-start.3 = (bf16[512,512]{1,0:T(8,128)(2,1)}, bf16[512,512]{1,0:T(8,128)(2,1)S(1)}, u32[]{:S(2)}) copy-start(bf16[512,512]{1,0:T(8,128)(2,1)S(1)} %collective-permute-done.23.refs_9_) | copy-start | bytes 1572868
  122.7 10.1 %collective-permute-start.26 = (bf16[256,512]{1,0:T(8,128)(2,1)S(1)}, bf16[256,512]{1,0:T(8,128)(2,1)S(1)}, u32[]{:S(2)}, u32[]{:S(2)}) collective-permute-start(bf16[256,512]{1,0:T(8,128)(2,1)S(1)} %slice.150), channel_id=1, source_target_pairs={{0,16},{8,24},{16,0},{24,8},{1,17},{9,25},{17,1},{25,9},{2,18},{10... | collective-permute-start | bytes 786440 | tf_op jit(solution)/shard_map/ppermute | solution.py:179
  123.6 9.2 %collective-permute-start.25 = (bf16[256,512]{1,0:T(8,128)(2,1)S(1)}, bf16[256,512]{1,0:T(8,128)(2,1)S(1)}, u32[]{:S(2)}, u32[]{:S(2)}) collective-permute-start(bf16[256,512]{1,0:T(8,128)(2,1)S(1)} %slice.149), channel_id=1, source_target_pairs={{0,8},{8,0},{16,24},{24,16},{1,9},{9,1},{17,25},{25,17},{2,10},{10... | collective-permute-start | bytes 786440 | tf_op jit(solution)/shard_map/ppermute | solution.py:179
  126.2 19.3 %collective-permute-start.24 = (bf16[1024,256]{1,0:T(8,128)(2,1)S(1)}, bf16[1024,256]{1,0:T(8,128)(2,1)S(1)}, u32[]{:S(2)}, u32[]{:S(2)}) collective-permute-start(bf16[1024,256]{1,0:T(8,128)(2,1)S(1)} %broadcast_select_fusion.13), channel_id=1, source_target_pairs={{0,2},{1,3},{2,0},{3,1},{4,6},{5,7},{6,4},{7,5},{8,10},{9,11},{10,... | collective-permute-start | bytes 1572872 | tf_op jit(solution)/shard_map/ppermute | solution.py:189
  132.0 16.0 %collective-permute-start.30 = (bf16[1024,256]{1,0:T(8,128)(2,1)S(1)}, bf16[1024,256]{1,0:T(8,128)(2,1)S(1)}, u32[]{:S(2)}, u32[]{:S(2)}) collective-permute-start(bf16[1024,256]{1,0:T(8,128)(2,1)S(1)} %add_convert_fusion.12), channel_id=1, source_target_pairs={{2,4},{3,5},{4,2},{5,3},{10,12},{11,13},{12,10},{13,11},{18,20},{1... | collective-permute-start | bytes 1572872 | tf_op jit(solution)/shard_map/ppermute | solution.py:189
  132.8 15.6 %collective-permute-start.32 = (bf16[512,512]{1,0:T(8,128)(2,1)S(1)}, bf16[512,512]{1,0:T(8,128)(2,1)S(1)}, u32[]{:S(2)}, u32[]{:S(2)}) collective-permute-start(bf16[512,512]{1,0:T(8,128)(2,1)S(1)} %pad_maximum_fusion.3.refs_8_), channel_id=1, source_target_pairs={{0,8},{8,0},{16,24},{24,16},{1,9},{9,1},{17,25},{25,17},{2,10},{10... | collective-permute-start | bytes 1572872 | tf_op jit(solution)/shard_map/ppermute | solution.py:179
  133.4 15.0 %collective-permute-start.31 = (bf16[512,512]{1,0:T(8,128)(2,1)S(1)}, bf16[512,512]{1,0:T(8,128)(2,1)S(1)}, u32[]{:S(2)}, u32[]{:S(2)}) collective-permute-start(bf16[512,512]{1,0:T(8,128)(2,1)S(1)} %pad_maximum_fusion.3.refs_8_), channel_id=1, source_target_pairs={{0,16},{8,24},{16,0},{24,8},{1,17},{9,25},{17,1},{25,9},{2,18},{10... | collective-permute-start | bytes 1572872 | tf_op jit(solution)/shard_map/ppermute | solution.py:179
  139.9 6.9 %copy-start.34 = (bf16[2,4,112,256]{3,2,0,1:T(8,128)(2,1)S(1)}, bf16[2,4,112,256]{3,2,0,1:T(8,128)(2,1)}, u32[]{:S(2)}) copy-start(bf16[2,4,112,256]{3,2,0,1:T(8,128)(2,1)} %fusion.16) | copy-start | bytes 1376260
  140.1 17.1 %collective-permute-start.29 = (bf16[1024,256]{1,0:T(8,128)(2,1)S(1)}, bf16[1024,256]{1,0:T(8,128)(2,1)S(1)}, u32[]{:S(2)}, u32[]{:S(2)}) collective-permute-start(bf16[1024,256]{1,0:T(8,128)(2,1)S(1)} %broadcast_select_fusion.12), channel_id=1, source_target_pairs={{0,2},{1,3},{2,0},{3,1},{4,6},{5,7},{6,4},{7,5},{8,10},{9,11},{10,... | collective-permute-start | bytes 1572872 | tf_op jit(solution)/shard_map/ppermute | solution.py:189
  147.4 11.4 %collective-permute-start.36 = (bf16[1024,256]{1,0:T(8,128)(2,1)S(1)}, bf16[1024,256]{1,0:T(8,128)(2,1)S(1)}, u32[]{:S(2)}, u32[]{:S(2)}) collective-permute-start(bf16[1024,256]{1,0:T(8,128)(2,1)S(1)} %add_convert_fusion.10), channel_id=1, source_target_pairs={{2,4},{3,5},{4,2},{5,3},{10,12},{11,13},{12,10},{13,11},{18,20},{1... | collective-permute-start | bytes 1572872 | tf_op jit(solution)/shard_map/ppermute | solution.py:189
  148.4 10.4 %collective-permute-start.35 = (bf16[256,512]{1,0:T(8,128)(2,1)S(1)}, bf16[256,512]{1,0:T(8,128)(2,1)S(1)}, u32[]{:S(2)}, u32[]{:S(2)}) collective-permute-start(bf16[256,512]{1,0:T(8,128)(2,1)S(1)} %slice.153), channel_id=1, source_target_pairs={{0,16},{8,24},{16,0},{24,8},{1,17},{9,25},{17,1},{25,9},{2,18},{10... | collective-permute-start | bytes 786440 | tf_op jit(solution)/shard_map/ppermute | solution.py:179
  149.0 9.9 %collective-permute-start.34 = (bf16[256,512]{1,0:T(8,128)(2,1)S(1)}, bf16[256,512]{1,0:T(8,128)(2,1)S(1)}, u32[]{:S(2)}, u32[]{:S(2)}) collective-permute-start(bf16[256,512]{1,0:T(8,128)(2,1)S(1)} %slice.152), channel_id=1, source_target_pairs={{0,8},{8,0},{16,24},{24,16},{1,9},{9,1},{17,25},{25,17},{2,10},{10... | collective-permute-start | bytes 786440 | tf_op jit(solution)/shard_map/ppermute | solution.py:179
  150.5 18.0 %collective-permute-start.33 = (bf16[1024,256]{1,0:T(8,128)(2,1)S(1)}, bf16[1024,256]{1,0:T(8,128)(2,1)S(1)}, u32[]{:S(2)}, u32[]{:S(2)}) collective-permute-start(bf16[1024,256]{1,0:T(8,128)(2,1)S(1)} %broadcast_select_fusion.10), channel_id=1, source_target_pairs={{0,2},{1,3},{2,0},{3,1},{4,6},{5,7},{6,4},{7,5},{8,10},{9,11},{10,... | collective-permute-start | bytes 1572872 | tf_op jit(solution)/shard_map/ppermute | solution.py:189
  157.9 11.6 %collective-permute-start.38 = (bf16[1024,256]{1,0:T(8,128)(2,1)S(1)}, bf16[1024,256]{1,0:T(8,128)(2,1)S(1)}, u32[]{:S(2)}, u32[]{:S(2)}) collective-permute-start(bf16[1024,256]{1,0:T(8,128)(2,1)S(1)} %add_convert_fusion.8), channel_id=1, source_target_pairs={{2,4},{3,5},{4,2},{5,3},{10,12},{11,13},{12,10},{13,11},{18,20},{1... | collective-permute-start | bytes 1572872 | tf_op jit(solution)/shard_map/ppermute | solution.py:189
  162.8 18.2 %collective-permute-start.37 = (bf16[1024,256]{1,0:T(8,128)(2,1)S(1)}, bf16[1024,256]{1,0:T(8,128)(2,1)S(1)}, u32[]{:S(2)}, u32[]{:S(2)}) collective-permute-start(bf16[1024,256]{1,0:T(8,128)(2,1)S(1)} %broadcast_select_fusion.8), channel_id=1, source_target_pairs={{0,2},{1,3},{2,0},{3,1},{4,6},{5,7},{6,4},{7,5},{8,10},{9,11},{10,... | collective-permute-start | bytes 1572872 | tf_op jit(solution)/shard_map/ppermute | solution.py:189
  168.6 13.9 %collective-permute-start.40 = (bf16[1024,256]{1,0:T(8,128)(2,1)S(1)}, bf16[1024,256]{1,0:T(8,128)(2,1)S(1)}, u32[]{:S(2)}, u32[]{:S(2)}) collective-permute-start(bf16[1024,256]{1,0:T(8,128)(2,1)S(1)} %add_convert_fusion.6), channel_id=1, source_target_pairs={{2,4},{3,5},{4,2},{5,3},{10,12},{11,13},{12,10},{13,11},{18,20},{1... | collective-permute-start | bytes 1572872 | tf_op jit(solution)/shard_map/ppermute | solution.py:189
  170.0 22.3 %collective-permute-start.39 = (bf16[1024,256]{1,0:T(8,128)(2,1)S(1)}, bf16[1024,256]{1,0:T(8,128)(2,1)S(1)}, u32[]{:S(2)}, u32[]{:S(2)}) collective-permute-start(bf16[1024,256]{1,0:T(8,128)(2,1)S(1)} %broadcast_select_fusion.6), channel_id=1, source_target_pairs={{0,2},{1,3},{2,0},{3,1},{4,6},{5,7},{6,4},{7,5},{8,10},{9,11},{10,... | collective-permute-start | bytes 1572872 | tf_op jit(solution)/shard_map/ppermute | solution.py:189
  181.7 12.0 %collective-permute-start.42 = (bf16[1024,256]{1,0:T(8,128)(2,1)S(1)}, bf16[1024,256]{1,0:T(8,128)(2,1)S(1)}, u32[]{:S(2)}, u32[]{:S(2)}) collective-permute-start(bf16[1024,256]{1,0:T(8,128)(2,1)S(1)} %add_convert_fusion.4), channel_id=1, source_target_pairs={{2,4},{3,5},{4,2},{5,3},{10,12},{11,13},{12,10},{13,11},{18,20},{1... | collective-permute-start | bytes 1572872 | tf_op jit(solution)/shard_map/ppermute | solution.py:189
  182.6 20.9 %collective-permute-start.41 = (bf16[1024,256]{1,0:T(8,128)(2,1)S(1)}, bf16[1024,256]{1,0:T(8,128)(2,1)S(1)}, u32[]{:S(2)}, u32[]{:S(2)}) collective-permute-start(bf16[1024,256]{1,0:T(8,128)(2,1)S(1)} %add_convert_fusion.3), channel_id=1, source_target_pairs={{2,0},{3,1},{4,6},{5,7},{10,8},{11,9},{12,14},{13,15},{18,16},{19,... | collective-permute-start | bytes 1572872 | tf_op jit(solution)/shard_map/ppermute | solution.py:189
  192.9 2.3 collective-permute-start.44
  193.8 20.9 %collective-permute-start.43 = (bf16[1024,256]{1,0:T(8,128)(2,1)S(1)}, bf16[1024,256]{1,0:T(8,128)(2,1)S(1)}, u32[]{:S(2)}, u32[]{:S(2)}) collective-permute-start(bf16[1024,256]{1,0:T(8,128)(2,1)S(1)} %add_convert_fusion.1), channel_id=1, source_target_pairs={{2,0},{3,1},{4,6},{5,7},{10,8},{11,9},{12,14},{13,15},{18,16},{19,... | collective-permute-start | bytes 1572872 | tf_op jit(solution)/shard_map/ppermute | solution.py:189
  203.8 17.6 %collective-permute-start.45 = (bf16[1024,256]{1,0:T(8,128)(2,1)S(1)}, bf16[1024,256]{1,0:T(8,128)(2,1)S(1)}, u32[]{:S(2)}, u32[]{:S(2)}) collective-permute-start(bf16[1024,256]{1,0:T(8,128)(2,1)S(1)} %add_convert_fusion), channel_id=1, source_target_pairs={{2,0},{3,1},{4,6},{5,7},{10,8},{11,9},{12,14},{13,15},{18,16},{19,... | collective-permute-start | bytes 1572872 | tf_op jit(solution)/shard_map/ppermute | solution.py:189
  205.2 16.7 %collective-permute-start.46 = (bf16[448,1536]{1,0:T(8,128)(2,1)S(1)}, bf16[448,1536]{1,0:T(8,128)(2,1)S(1)}, u32[]{:S(2)}, u32[]{:S(2)}) collective-permute-start(bf16[448,1536]{1,0:T(8,128)(2,1)S(1)} %constant_dynamic-update-slice_fusion), channel_id=1, source_target_pairs={{0,1},{1,0},{2,3},{3,2},{4,5},{5,4},{6,7},{7,6},{8,9},{9,8},{10,11... | collective-permute-start | bytes 4128776 | tf_op jit(solution)/shard_map/ppermute | solution.py:176
  221.8 1.9 collective-permute-start.47
  (22 other events, 21.9 us)

commit v8 on v7

--- a/solution.py
+++ b/solution.py
@@ -8,68 +8,76 @@
 from jax.sharding import PartitionSpec as P
 
 EXP_DEV = 1
-GROUPS = ((1, 1), (1, 1), (1, 1), (1, 1))
+GROUPS = ((1,), (1,), (1, 1), (1, 1), (1, 1))
+FIRST_PHASE = {1: 2, 2: 3, 4: 4}
+SECOND_PHASE = {2: 2, 3: 3, 5: 4}
 UNITS = sum(map(sum, GROUPS))
 DELAY = 3
 SWAPS = (6, 8)
-CONV_VMEM = 44 * 1024 * 1024
-PRODUCT_VMEM = 22 * 1024 * 1024
+VMEM_BYTES = 60 * 1024 * 1024
 
 
 def conv_kernel(tile, at_ctx, out_grad, gate_in, conv_in, scan_grad, taps, bias, skip, *refs):
     turned, flat, columns_of = refs[:-2], refs[-2], refs[-1]
     channels, length = out_grad.shape
     window = length // len(turned)
-    kernel_taps = taps.shape[0]
     rows_at_once = 16
+    groups = channels // rows_at_once
+    chunk = window // groups
     settings = jnp.concatenate(
-        [0.5 * taps[...], 0.5 * bias[...], skip[...], jnp.zeros((8 - kernel_taps - 2, channels), jnp.float32)], axis=0
+        [0.5 * taps[...], 0.5 * bias[...], skip[...], jnp.zeros((2, channels), jnp.float32)], axis=0
     )
     columns_of[...] = settings.T
 
-    def row_group(group, _):
-        row_at = pl.multiple_of(group * rows_at_once, rows_at_once)
-        rows = pl.ds(row_at, rows_at_once)
-
-        def spread(index):
-            column = jnp.broadcast_to(columns_of[rows, index : index + 1], (rows_at_once, 128))
-            return jnp.concatenate([column] * (tile // 128), axis=1)
-
-        weights = [spread(tap) for tap in range(kernel_taps)]
-        bias_half = spread(kernel_taps)
-        skip_value = spread(kernel_taps + 1)
-        after = jnp.zeros((rows_at_once, 128), jnp.float32)
-        for at in range(length - tile, -1, -tile):
-            columns = pl.ds(at, tile)
-            gate = 0.5 * gate_in[rows, columns].astype(jnp.float32)
-            gated = out_grad[rows, columns].astype(jnp.float32) * (gate + gate * jnp.tanh(gate))
-            here = conv_in[rows, columns].astype(jnp.float32)
-            if at:
-                before = conv_in[rows, pl.ds(at - 128, 128)].astype(jnp.float32)
-            else:
-                before = jnp.zeros((rows_at_once, 128), jnp.float32)
-            wide = jnp.concatenate([before, here], axis=1)
-            half = bias_half + weights[kernel_taps - 1] * here
-            for tap in range(kernel_taps - 1):
-                back = kernel_taps - 1 - tap
-                half = half + weights[tap] * pltpu.roll(wide, back, 1)[:, 128:]
-            turn = jnp.tanh(half)
-            scan = scan_grad[rows, columns].astype(jnp.float32)
-            grad = (scan + skip_value * gated) * (1.0 + turn + half * (1.0 - turn * turn))
-            wide_grad = jnp.concatenate([grad, after], axis=1)
-            total = weights[kernel_taps - 1] * grad
-            for tap in range(kernel_taps - 1):
-                ahead = kernel_taps - 1 - tap
-                total = total + weights[tap] * pltpu.roll(wide_grad, tile + 128 - ahead, 1)[:, :tile]
-            flat[rows, columns] = total.astype(flat.dtype)
-            after = grad[:, :128]
-        return 0
-
-    lax.fori_loop(0, channels // rows_at_once, row_group, 0)
-    for offset, out in enumerate(turned):
+    def turn(offset, at):
+        at = pl.multiple_of(at, chunk)
+        turned[offset][pl.ds(at, chunk), :] = flat[offset % 2, :, pl.ds(at, chunk)].T
+
+    for offset in range(len(turned)):
         from_at = (at_ctx[0] ^ offset) * window
-        for at in range(0, window, tile):
-            out[pl.ds(at, tile), :] = flat[:, pl.ds(pl.multiple_of(from_at + at, tile), tile)].T
+
+        def row_group(group, _):
+            if offset:
+                turn(offset - 1, group * chunk)
+            rows = pl.ds(pl.multiple_of(group * rows_at_once, rows_at_once), rows_at_once)
+            setting = [jnp.broadcast_to(columns_of[rows, at : at + 1], (rows_at_once, 128)) for at in range(6)]
+
+            def spread(index, width):
+                return jnp.concatenate([setting[index]] * (width // 128), axis=1)
+
+            def columns(ref, at, width):
+                return ref[rows, pl.ds(pl.multiple_of(at, 128), width)].astype(jnp.float32)
+
+            def grad_of(at, width):
+                gate = 0.5 * columns(gate_in, at, width)
+                gated = columns(out_grad, at, width) * (gate + gate * jnp.tanh(gate))
+                here = columns(conv_in, at, width)
+                before = jnp.where(at > 0, columns(conv_in, jnp.maximum(at - 128, 0), 128), 0.0)
+                wide = jnp.concatenate([before, here], axis=1)
+                one_back = pltpu.roll(wide, 1, 1)
+                older = spread(1, width + 128) * wide + spread(0, width + 128) * one_back
+                half = spread(4, width) + spread(3, width) * here + spread(2, width) * one_back[:, 128:]
+                half = half + pltpu.roll(older, 2, 1)[:, 128:]
+                turn_value = jnp.tanh(half)
+                slope = 1.0 + turn_value + half * (1.0 - turn_value * turn_value)
+                return (columns(scan_grad, at, width) + spread(5, width) * gated) * slope
+
+            end = from_at + window
+            after = grad_of(jnp.minimum(end, length - 128), 128)
+            after = jnp.where(end < length, after, 0.0)
+            for at in range(window - tile, -1, -tile):
+                grad = grad_of(from_at + at, tile)
+                wide = jnp.concatenate([grad, after], axis=1)
+                one_on = pltpu.roll(wide, tile + 127, 1)
+                later = spread(1, tile + 128) * wide + spread(0, tile + 128) * one_on
+                total = spread(3, tile) * grad + spread(2, tile) * one_on[:, :tile]
+                total = total + pltpu.roll(later, tile + 126, 1)[:, :tile]
+                flat[offset % 2, rows, pl.ds(at, tile)] = total.astype(flat.dtype)
+                after = grad[:, :128]
+            return 0
+
+        lax.fori_loop(0, groups, row_group, 0)
+    lax.fori_loop(0, groups, lambda group, _: (turn(len(turned) - 1, group * chunk), 0)[1], 0)
 
 
 def conv_grad(at_ctx, ctx_count, out_grad, gate_in, conv_in, scan_grad, conv_weight, conv_bias, skip_scale):
@@ -87,10 +95,10 @@
             in_specs=[whole] * 4
             + [pl.BlockSpec((conv_weight.shape[0], block), lambda step, at_ctx: (0, step)), row, row],
             out_specs=[pl.BlockSpec((window, block), lambda step, at_ctx: (0, step))] * ctx_count,
-            scratch_shapes=[pltpu.VMEM((block, length), jnp.bfloat16), pltpu.VMEM((block, 8), jnp.float32)],
+            scratch_shapes=[pltpu.VMEM((2, block, window), jnp.bfloat16), pltpu.VMEM((block, 8), jnp.float32)],
         ),
         out_shape=[jax.ShapeDtypeStruct((window, channels), jnp.bfloat16)] * ctx_count,
-        compiler_params=pltpu.CompilerParams(vmem_limit_bytes=CONV_VMEM),
+        compiler_params=pltpu.CompilerParams(vmem_limit_bytes=VMEM_BYTES),
         cost_estimate=pl.CostEstimate(
             flops=40 * channels * length, bytes_accessed=10 * channels * length, transcendentals=2 * channels * length
         ),
@@ -136,7 +144,7 @@
             out_specs=[pl.BlockSpec((tile, part), lambda step, place: (step, 0)) for part in widths],
         ),
         out_shape=[jax.ShapeDtypeStruct((tokens, part), jnp.bfloat16) for part in widths],
-        compiler_params=pltpu.CompilerParams(vmem_limit_bytes=PRODUCT_VMEM),
+        compiler_params=pltpu.CompilerParams(vmem_limit_bytes=VMEM_BYTES),
         cost_estimate=pl.CostEstimate(flops=flops, bytes_accessed=moved, transcendentals=0),
         name="partial_product",
     )(place, *lefts, *rights, resid)
@@ -313,7 +321,7 @@
     outer, across = {}, {}
     first_of = [sum(map(len, GROUPS[:at])) for at in range(len(GROUPS))]
     sums[0][: len(GROUPS[0])] = products(0, rights[0])
-    near = None
+    rights += [None] * (len(GROUPS) - len(rights))
     for step in range(pieces + 2 * lag * hops + DELAY + 1):
         for hop in range(hops):
             if (step - 2, hop) not in outer:
@@ -332,16 +340,14 @@
             got, index = across[step - 1]
             own, got = chain(sums[hops][index], got)
             ready[hops][index] = add(own, got)
-        if square and near is not None and step % 2:
-            near = spread_on(near)
-        if step and step in first_of:
-            group_at = first_of.index(step)
-            if near is not None:
-                rights.append(near)
-            near = None
-            if group_at + 1 < len(GROUPS):
-                piece, *rights[group_at] = chain(rest[group_at], *rights[group_at])
-                near = spread_near(piece) if square else spread(piece)
+        if step in SECOND_PHASE and square:
+            rights[SECOND_PHASE[step]] = spread_on(rights[SECOND_PHASE[step]])
+        group_at = first_of.index(step) if step and step in first_of else None
+        if step in FIRST_PHASE:
+            coming = FIRST_PHASE[step]
+            piece, *rights[group_at] = chain(rest[coming - 1], *rights[group_at])
+            rights[coming] = spread_near(piece) if square else spread(piece)
+        if group_at:
             sums[0][step : step + len(GROUPS[group_at])] = products(group_at, rights[group_at])
         for hop in range(hops):
             inward = step - lag * hop

time: 228 us -> 238 us (1.044)
  Pallas kernels: 31.8 us -> 54.2 us
  local copies, waits for them, and re-layouts: 33.3 us -> 20.8 us
  other arithmetic: 15.1 us -> 22.6 us
  starting transfers between devices: 64.4 us -> 58 us
    unnamed x100 -> x92, local copies, waits for them, and re-layouts: 22.8 us -> 4.78 us
    ppermute x19, waiting for transfers between devices: 52.7 us -> 38.7 us  [swap_chips(): return lax.ppermute(array, 'exp', sorted(pairs))]
    ppermute x17 -> x21, waiting for transfers between devices: 23 us -> 36.1 us  [to_ctx(): lax.ppermute(array, 'ctx', [(place, place ^ offset) for place in range(ct...]
    pallas_call x1, Pallas kernels: 16.6 us -> 28 us  [conv_grad(): pl.pallas_call(functools.partial(conv_kernel, tile), grid_spec=pltpu.Pref...]
    pallas_call x4 -> x5, Pallas kernels: 15.2 us -> 26.3 us  [matmul(): pl.pallas_call(functools.partial(matmul_kernel, len(lefts), len(rights)),...]
    ppermute x19, starting transfers between devices: 38 us -> 27.5 us  [swap_chips(): return lax.ppermute(array, 'exp', sorted(pairs))]
    select_n x5, other arithmetic: 2.16 us -> 7.12 us  [on_device(): jnp.where(distance == hop, sums[hop][inward], ready[hop + 1][outward])]
    slice x4 -> x6, local copies, waits for them, and re-layouts: 1.18 us -> 5.58 us  [spread_on(): low, high = chain(near[2][:cut], near[1][cut:])]
  transfers between devices with their start and end apart: 48 -> 52, of which waited for: 14 -> 17; matrix products, arithmetic and copies ran while one was open for 11% -> 16% of each run, Pallas kernels for 12% -> 21%
where the time goes in v8:
time: 238 us; the launch traced here: 237 us
  waiting for transfers between devices  77.8 us (33%)
  starting transfers between devices  58 us (24%)
  Pallas kernels  54.2 us (23%)
  other arithmetic  22.6 us (9%)
  local copies, waits for them, and re-layouts  20.8 us (9%)
    ppermute x19, waiting for transfers between devices, swap_chips(): return lax.ppermute(array, 'exp', sorted(pairs))  38.7 us
    ppermute x21, waiting for transfers between devices, to_ctx(): lax.ppermute(array, 'ctx', [(place, place ^ offset) for place in range(ct...  36.1 us
    pallas_call x1, Pallas kernels, conv_grad(): pl.pallas_call(functools.partial(conv_kernel, tile), grid_spec=pltpu.Pref...  28 us
    ppermute x19, starting transfers between devices, swap_chips(): return lax.ppermute(array, 'exp', sorted(pairs))  27.5 us
    pallas_call x5, Pallas kernels, matmul(): pl.pallas_call(functools.partial(matmul_kernel, len(lefts), len(rights)),...  26.3 us
    ppermute x21, starting transfers between devices, to_ctx(): lax.ppermute(array, 'ctx', [(place, place ^ offset) for place in range(ct...  23.8 us
    select_n x5, other arithmetic, on_device(): jnp.where(distance == hop, sums[hop][inward], ready[hop + 1][outward])  7.12 us
    slice x6, local copies, waits for them, and re-layouts, spread_on(): low, high = chain(near[2][:cut], near[1][cut:])  5.58 us
  transfers between devices with their start and end apart: 52, of which 17 were waited for; matrix products, arithmetic and copies ran while one was open for 16% of the time, Pallas kernels for 21%

profile of v8, /device:TPU:0, one launch (start us, length us, event | category | flops | bytes accessed | tf_op | source)
XLA Modules:
  0.0 236.9 jit_solution(11709464524584330959)
XLA Ops:
  0.0 1.0 constant_dynamic-slice_fusion.8
  1.5 1.0 collective-permute-done
  2.5 3.9 %collective-permute-start.3 = (bf16[512,256]{1,0:T(8,128)(2,1)S(1)}, bf16[512,256]{1,0:T(8,128)(2,1)S(1)}, u32[]{:S(2)}, u32[]{:S(2)}) collective-permute-start(bf16[512,256]{1,0:T(8,128)(2,1)S(1)} %pad_maximum_fusion.4.refs_8_), channel_id=1, source_target_pairs={{0,24},{8,16},{16,8},{24,0},{1,25},{9,17},{17,9},{25,1},{2,26},{10... | collective-permute-start | bytes 786440 | tf_op jit(solution)/shard_map/ppermute | solution.py:187
  7.0 28.0 %conv_grad.1 = (bf16[1024,256]{1,0:T(8,128)(2,1)}, bf16[1024,256]{1,0:T(8,128)(2,1)}, bf16[1024,256]{1,0:T(8,128)(2,1)}, bf16[1024,256]{1,0:T(8,128)(2,1)}) custom-call(s32[1]{0:T(128)} %bitcast.1.at_ctx, bf16[256,4096]{1,0:T(8,128)(2,1)} %out_grad.1, bf16[256,4096]{1,0:T(8,128)(2,1)} %gate_in.1, bf16[256,4096]{1,0:T(8,128)(2,1)} %conv_in.1, ...), custom_call_target="tpu_custom_call" | custom-call | flops 41943040 | bytes 10485760 | tf_op jit(solution)/shard_map/conv_grad/pallas_call | solution.py:90
  36.1 1.9 collective-permute-start.8
  38.0 1.5 collective-permute-start.10
  39.7 2.2 constant_dynamic-slice_fusion.5
  43.3 2.0 collective-permute-start.6
  45.2 1.2 constant_dynamic-slice_fusion.6
  46.9 3.0 %collective-permute-start.7 = (f32[4,4,128]{2,1,0:T(4,128)S(1)}, f32[4,4,128]{2,1,0:T(4,128)S(1)}, u32[]{:S(2)}, u32[]{:S(2)}) collective-permute-start(f32[4,4,128]{2,1,0:T(4,128)S(1)} %pad_maximum_fusion.7), channel_id=1, source_target_pairs={{0,4},{1,5},{2,6},{3,7},{4,0},{5,1},{6,2},{7,3},{8,12},{9,13},{10,... | collective-permute-start | bytes 24584 | tf_op jit(solution)/shard_map/ppermute | solution.py:239
  51.1 12.3 %collective-permute-done.13.refs_6_ = bf16[1024,256]{1,0:T(8,128)(2,1)} collective-permute-done((bf16[1024,256]{1,0:T(8,128)(2,1)}, bf16[1024,256]{1,0:T(8,128)(2,1)}, u32[]{:S(2)}, u32[]{:S(2)}) %collective-permute-start.13) | collective-permute-done | bytes 524320 | tf_op jit(solution)/shard_map/ppermute | solution.py:187
  65.9 1.2 fusion.24
  67.9 1.1 pad_maximum_fusion
  69.4 1.6 maximum_select_fusion
  71.9 4.3 %partial_product.5 = bf16[1024,256]{1,0:T(8,128)(2,1)} custom-call(s32[1]{0:T(128)} %bitcast.place, bf16[1024,256]{1,0:T(8,128)(2,1)} %get-tuple-element.172.refs_0_, bf16[1024,256]{1,0:T(8,128)(2,1)} %copy-done.1, bf16[1024,256]{1,0:T(8,128)(2,1)} %copy-done.2, bf16[1024,256]{1,0:T(8,128)(2,1)} %collective-permute-done.9.refs_3_, ...), custom_call_target="tpu_custom_call" | custom-call | flops 1073741824 | bytes 5767168 | tf_op jit(solution)/shard_map/partial_product/pallas_call | solution.py:136
  76.2 3.6 %collective-permute-start.21 = (bf16[1024,256]{1,0:T(8,128)(2,1)}, bf16[1024,256]{1,0:T(8,128)(2,1)S(1)}, u32[]{:S(2)}, u32[]{:S(2)}) collective-permute-start(bf16[1024,256]{1,0:T(8,128)(2,1)} %partial_product.5), channel_id=1, source_target_pairs={{0,2},{1,3},{6,4},{7,5},{8,10},{9,11},{14,12},{15,13},{16,18},{17,... | collective-permute-start | bytes 1572872 | tf_op jit(solution)/shard_map/ppermute | solution.py:197
  79.8 1.5 collective-permute-start.18
  81.3 1.4 collective-permute-start.17
  83.4 6.6 %collective-permute-done.18.refs_11_ = bf16[512,256]{1,0:T(8,128)(2,1)S(1)} collective-permute-done((bf16[512,256]{1,0:T(8,128)(2,1)S(1)}, bf16[512,256]{1,0:T(8,128)(2,1)S(1)}, u32[]{:S(2)}, u32[]{:S(2)}) %collective-permute-start.18) | collective-permute-done | bytes 262176 | tf_op jit(solution)/shard_map/ppermute | solution.py:187
  90.0 4.9 %collective-permute-done.17.refs_10_ = bf16[512,256]{1,0:T(8,128)(2,1)S(1)} collective-permute-done((bf16[512,256]{1,0:T(8,128)(2,1)S(1)}, bf16[512,256]{1,0:T(8,128)(2,1)S(1)}, u32[]{:S(2)}, u32[]{:S(2)}) %collective-permute-start.17) | collective-permute-done | bytes 262176 | tf_op jit(solution)/shard_map/ppermute | solution.py:187
  95.5 1.5 collective-permute-start.19
  96.9 4.3 %partial_product.6 = bf16[1024,256]{1,0:T(8,128)(2,1)} custom-call(s32[1]{0:T(128)} %bitcast.place, bf16[1024,256]{1,0:T(8,128)(2,1)} %get-tuple-element.172.refs_0_, bf16[1024,256]{1,0:T(8,128)(2,1)} %copy-done.1, bf16[1024,256]{1,0:T(8,128)(2,1)} %copy-done.2, bf16[1024,256]{1,0:T(8,128)(2,1)} %collective-permute-done.9.refs_3_, ...), custom_call_target="tpu_custom_call" | custom-call | flops 1073741824 | bytes 5767168 | tf_op jit(solution)/shard_map/partial_product/pallas_call | solution.py:136
  101.3 1.6 collective-permute-start.25
  103.0 6.1 %collective-permute-done.20.refs_10_ = bf16[512,512]{1,0:T(8,128)(2,1)} collective-permute-done((bf16[512,512]{1,0:T(8,128)(2,1)}, bf16[512,512]{1,0:T(8,128)(2,1)}, u32[]{:S(2)}, u32[]{:S(2)}) %collective-permute-start.20) | collective-permute-done | bytes 524320 | tf_op jit(solution)/shard_map/ppermute | solution.py:187
  109.1 1.0 slice.170
  110.1 1.7 slice.171
  112.5 1.2 collective-permute-start.22
  115.4 4.1 %collective-permute-done.23.refs_12_ = bf16[256,512]{1,0:T(8,128)(2,1)} collective-permute-done((bf16[256,512]{1,0:T(8,128)(2,1)}, bf16[256,512]{1,0:T(8,128)(2,1)}, u32[]{:S(2)}, u32[]{:S(2)}) %collective-permute-start.23) | collective-permute-done | bytes 262176 | tf_op jit(solution)/shard_map/ppermute | solution.py:187
  119.5 1.5 collective-permute-start.27
  121.5 5.9 %partial_product.7 = (bf16[1024,256]{1,0:T(8,128)(2,1)}, bf16[1024,256]{1,0:T(8,128)(2,1)}) custom-call(s32[1]{0:T(128)} %bitcast.place, bf16[1024,256]{1,0:T(8,128)(2,1)} %get-tuple-element.172.refs_0_, bf16[1024,256]{1,0:T(8,128)(2,1)} %copy-done.1, bf16[1024,256]{1,0:T(8,128)(2,1)} %copy-done.2, bf16[1024,256]{1,0:T(8,128)(2,1)} %collective-permute-done.9.refs_3_, ...), custom_call_target="tpu_custom_call" | custom-call | flops 2147483648 | bytes 7340032 | tf_op jit(solution)/shard_map/partial_product/pallas_call | solution.py:136
  127.4 1.8 collective-permute-start.32
  130.0 2.2 broadcast_select_fusion.13
  133.8 1.3 collective-permute-start.30
  136.5 5.3 %collective-permute-done.32 = bf16[1024,256]{1,0:T(8,128)(2,1)S(1)} collective-permute-done((bf16[1024,256]{1,0:T(8,128)(2,1)}, bf16[1024,256]{1,0:T(8,128)(2,1)S(1)}, u32[]{:S(2)}, u32[]{:S(2)}) %collective-permute-start.32) | collective-permute-done | bytes 524320 | tf_op jit(solution)/shard_map/ppermute | solution.py:197
  143.5 1.6 collective-permute-start.36
  145.6 5.9 %partial_product.8 = (bf16[1024,256]{1,0:T(8,128)(2,1)}, bf16[1024,256]{1,0:T(8,128)(2,1)}) custom-call(s32[1]{0:T(128)} %bitcast.place, bf16[1024,256]{1,0:T(8,128)(2,1)} %get-tuple-element.172.refs_0_, bf16[1024,256]{1,0:T(8,128)(2,1)} %copy-done.1, bf16[1024,256]{1,0:T(8,128)(2,1)} %copy-done.2, bf16[1024,256]{1,0:T(8,128)(2,1)} %collective-permute-done.9.refs_3_, ...), custom_call_target="tpu_custom_call" | custom-call | flops 2147483648 | bytes 7340032 | tf_op jit(solution)/shard_map/partial_product/pallas_call | solution.py:136
  151.4 1.3 broadcast_select_fusion.12
  152.8 4.1 %collective-permute-start.33 = (bf16[1024,256]{1,0:T(8,128)(2,1)S(1)}, bf16[1024,256]{1,0:T(8,128)(2,1)S(1)}, u32[]{:S(2)}, u32[]{:S(2)}) collective-permute-start(bf16[1024,256]{1,0:T(8,128)(2,1)S(1)} %broadcast_select_fusion.12), channel_id=1, source_target_pairs={{0,2},{1,3},{2,0},{3,1},{4,6},{5,7},{6,4},{7,5},{8,10},{9,11},{10,... | collective-permute-start | bytes 1572872 | tf_op jit(solution)/shard_map/ppermute | solution.py:197
  156.9 1.4 broadcast_select_fusion.11
  158.6 1.2 add_convert_fusion.10
  161.4 1.0 broadcast_select_fusion.10
  162.4 1.0 slice.176
  163.4 1.0 slice.175
  164.4 1.6 collective-permute-start.39
  166.5 1.6 collective-permute-start.37
  168.7 1.5 collective-permute-start.42
  171.0 1.3 collective-permute-done.38.refs_11_
  173.1 5.8 %partial_product.9 = (bf16[1024,256]{1,0:T(8,128)(2,1)}, bf16[1024,256]{1,0:T(8,128)(2,1)}) custom-call(s32[1]{0:T(128)} %bitcast.place, bf16[1024,256]{1,0:T(8,128)(2,1)} %get-tuple-element.172.refs_0_, bf16[1024,256]{1,0:T(8,128)(2,1)} %copy-done.1, bf16[1024,256]{1,0:T(8,128)(2,1)} %copy-done.2, bf16[1024,256]{1,0:T(8,128)(2,1)} %collective-permute-done.9.refs_3_, ...), custom_call_target="tpu_custom_call" | custom-call | flops 2147483648 | bytes 7340032 | tf_op jit(solution)/shard_map/partial_product/pallas_call | solution.py:136
  178.9 1.3 broadcast_select_fusion.8
  180.2 3.7 %collective-permute-start.41 = (bf16[1024,256]{1,0:T(8,128)(2,1)S(1)}, bf16[1024,256]{1,0:T(8,128)(2,1)S(1)}, u32[]{:S(2)}, u32[]{:S(2)}) collective-permute-start(bf16[1024,256]{1,0:T(8,128)(2,1)S(1)} %broadcast_select_fusion.8), channel_id=1, source_target_pairs={{0,2},{1,3},{2,0},{3,1},{4,6},{5,7},{6,4},{7,5},{8,10},{9,11},{10,... | collective-permute-start | bytes 1572872 | tf_op jit(solution)/shard_map/ppermute | solution.py:197
  183.9 1.2 add_convert_fusion.6
  185.9 1.7 broadcast_select_fusion.7
  187.6 1.3 broadcast_select_fusion.6
  189.4 5.7 %collective-permute-done.41 = bf16[1024,256]{1,0:T(8,128)(2,1)S(1)} collective-permute-done((bf16[1024,256]{1,0:T(8,128)(2,1)S(1)}, bf16[1024,256]{1,0:T(8,128)(2,1)S(1)}, u32[]{:S(2)}, u32[]{:S(2)}) %collective-permute-start.41) | collective-permute-done | bytes 524320 | tf_op jit(solution)/shard_map/ppermute | solution.py:197
  196.7 1.3 collective-permute-start.45
  198.0 8.4 %collective-permute-done.43 = bf16[1024,256]{1,0:T(8,128)(2,1)S(1)} collective-permute-done((bf16[1024,256]{1,0:T(8,128)(2,1)S(1)}, bf16[1024,256]{1,0:T(8,128)(2,1)S(1)}, u32[]{:S(2)}, u32[]{:S(2)}) %collective-permute-start.43) | collective-permute-done | bytes 524320 | tf_op jit(solution)/shard_map/ppermute | solution.py:197
  206.4 1.2 broadcast_select_fusion.4
  209.0 1.3 collective-permute-start.47
  210.4 7.2 %collective-permute-done.45 = bf16[1024,256]{1,0:T(8,128)(2,1)S(1)} collective-permute-done((bf16[1024,256]{1,0:T(8,128)(2,1)S(1)}, bf16[1024,256]{1,0:T(8,128)(2,1)S(1)}, u32[]{:S(2)}, u32[]{:S(2)}) %collective-permute-start.45) | collective-permute-done | bytes 524320 | tf_op jit(solution)/shard_map/ppermute | solution.py:197
  218.0 1.3 collective-permute-start.49
  219.4 7.0 %collective-permute-done.47 = bf16[1024,256]{1,0:T(8,128)(2,1)S(1)} collective-permute-done((bf16[1024,256]{1,0:T(8,128)(2,1)S(1)}, bf16[1024,256]{1,0:T(8,128)(2,1)S(1)}, u32[]{:S(2)}, u32[]{:S(2)}) %collective-permute-start.47) | collective-permute-done | bytes 524320 | tf_op jit(solution)/shard_map/ppermute | solution.py:197
  226.8 5.2 %collective-permute-done.49 = bf16[1024,256]{1,0:T(8,128)(2,1)S(1)} collective-permute-done((bf16[1024,256]{1,0:T(8,128)(2,1)S(1)}, bf16[1024,256]{1,0:T(8,128)(2,1)S(1)}, u32[]{:S(2)}, u32[]{:S(2)}) %collective-permute-start.49) | collective-permute-done | bytes 524320 | tf_op jit(solution)/shard_map/ppermute | solution.py:197
  232.9 1.4 collective-permute-done.51
  234.7 2.2 broadcast_select_fusion
  (228 shorter events, 30.9 us)
Async XLA Ops:
  1.0 1.5 collective-permute-start
  2.5 32.5 %copy-start.15 = (bf16[512,256]{1,0:T(8,128)(2,1)}, bf16[512,256]{1,0:T(8,128)(2,1)S(1)}, u32[]{:S(2)}) copy-start(bf16[512,256]{1,0:T(8,128)(2,1)S(1)} %pad_maximum_fusion.4.refs_8_) | copy-start | bytes 786436
  2.5 32.5 %collective-permute-start.3 = (bf16[512,256]{1,0:T(8,128)(2,1)S(1)}, bf16[512,256]{1,0:T(8,128)(2,1)S(1)}, u32[]{:S(2)}, u32[]{:S(2)}) collective-permute-start(bf16[512,256]{1,0:T(8,128)(2,1)S(1)} %pad_maximum_fusion.4.refs_8_), channel_id=1, source_target_pairs={{0,24},{8,16},{16,8},{24,0},{1,25},{9,17},{17,9},{25,1},{2,26},{10... | collective-permute-start | bytes 786440 | tf_op jit(solution)/shard_map/ppermute | solution.py:187
  6.4 28.7 %collective-permute-start.2 = (bf16[512,256]{1,0:T(8,128)(2,1)S(1)}, bf16[512,256]{1,0:T(8,128)(2,1)S(1)}, u32[]{:S(2)}, u32[]{:S(2)}) collective-permute-start(bf16[512,256]{1,0:T(8,128)(2,1)S(1)} %pad_maximum_fusion.4.refs_8_), channel_id=1, source_target_pairs={{0,16},{8,24},{16,0},{24,8},{1,17},{9,25},{17,1},{25,9},{2,18},{10... | collective-permute-start | bytes 786440 | tf_op jit(solution)/shard_map/ppermute | solution.py:187
  6.9 28.2 %collective-permute-start.1 = (bf16[512,256]{1,0:T(8,128)(2,1)S(1)}, bf16[512,256]{1,0:T(8,128)(2,1)S(1)}, u32[]{:S(2)}, u32[]{:S(2)}) collective-permute-start(bf16[512,256]{1,0:T(8,128)(2,1)S(1)} %pad_maximum_fusion.4.refs_8_), channel_id=1, source_target_pairs={{0,8},{8,0},{16,24},{24,16},{1,9},{9,1},{17,25},{25,17},{2,10},{10... | collective-permute-start | bytes 786440 | tf_op jit(solution)/shard_map/ppermute | solution.py:187
  7.0 32.5 %copy-start.28 = (s32[128,2]{0,1:T(2,128)S(1)}, s32[128,2]{0,1:T(2,128)}, u32[]{:S(2)}) copy-start(s32[128,2]{0,1:T(2,128)} %param.20) | copy-start | bytes 3076
  7.0 32.5 %copy-start.29 = (f32[128,2]{0,1:T(2,128)S(1)}, f32[128,2]{0,1:T(2,128)}, u32[]{:S(2)}) copy-start(f32[128,2]{0,1:T(2,128)} %param.21) | copy-start | bytes 3076
  7.0 35.3 %copy-start.17 = (bf16[128,4096]{1,0:T(8,128)(2,1)S(1)}, bf16[128,4096]{1,0:T(8,128)(2,1)}, u32[]{:S(2)}) copy-start(bf16[128,4096]{1,0:T(8,128)(2,1)} %param.19) | copy-start | bytes 3145732
  35.8 3.7 %collective-permute-start.4 = (bf16[1024,256]{1,0:T(8,128)(2,1)}, bf16[1024,256]{1,0:T(8,128)(2,1)S(1)}, u32[]{:S(2)}, u32[]{:S(2)}) collective-permute-start(bf16[1024,256]{1,0:T(8,128)(2,1)} %get-tuple-element.172.refs_0_), channel_id=1, source_target_pairs={{0,1},{1,0},{2,3},{3,2},{4,5},{5,4},{6,7},{7,6},{8,9},{9,8},{10,11... | collective-permute-start | bytes 1572872 | tf_op jit(solution)/shard_map/ppermute | solution.py:184
  36.1 15.0 %collective-permute-start.8 = (bf16[1024,256]{1,0:T(8,128)(2,1)}, bf16[1024,256]{1,0:T(8,128)(2,1)S(1)}, u32[]{:S(2)}, u32[]{:S(2)}) collective-permute-start(bf16[1024,256]{1,0:T(8,128)(2,1)} %get-tuple-element.152), channel_id=1, source_target_pairs={{0,8},{8,0},{16,24},{24,16},{1,9},{9,1},{17,25},{25,17},{2,10},{10... | collective-permute-start | bytes 1572872 | tf_op jit(solution)/shard_map/ppermute | solution.py:187
  38.0 31.0 %collective-permute-start.10 = (bf16[1024,256]{1,0:T(8,128)(2,1)}, bf16[1024,256]{1,0:T(8,128)(2,1)S(1)}, u32[]{:S(2)}, u32[]{:S(2)}) collective-permute-start(bf16[1024,256]{1,0:T(8,128)(2,1)} %get-tuple-element.153), channel_id=1, source_target_pairs={{0,16},{8,24},{16,0},{24,8},{1,17},{9,25},{17,1},{25,9},{2,18},{10... | collective-permute-start | bytes 1572872 | tf_op jit(solution)/shard_map/ppermute | solution.py:187
  39.5 23.9 %collective-permute-start.13 = (bf16[1024,256]{1,0:T(8,128)(2,1)}, bf16[1024,256]{1,0:T(8,128)(2,1)}, u32[]{:S(2)}, u32[]{:S(2)}) collective-permute-start(bf16[1024,256]{1,0:T(8,128)(2,1)} %get-tuple-element.156), channel_id=1, source_target_pairs={{0,24},{8,16},{16,8},{24,0},{1,25},{9,17},{17,9},{25,1},{2,26},{10... | collective-permute-start | bytes 1572872 | tf_op jit(solution)/shard_map/ppermute | solution.py:187
  39.6 27.5 %copy-start.1 = (bf16[1024,256]{1,0:T(8,128)(2,1)}, bf16[1024,256]{1,0:T(8,128)(2,1)S(1)}, u32[]{:S(2)}) copy-start(bf16[1024,256]{1,0:T(8,128)(2,1)S(1)} %collective-permute-done.4.refs_1_) | copy-start | bytes 1572868
  39.6 3.7 %collective-permute-start.5 = (f32[1,4,128]{2,1,0:T(4,128)S(1)}, f32[1,4,128]{2,1,0:T(4,128)S(1)}, u32[]{:S(2)}, u32[]{:S(2)}) collective-permute-start(f32[1,4,128]{2,1,0:T(4,128)S(1)} %maximum_bitcast_fusion), channel_id=1, source_target_pairs={{0,1},{1,0},{2,3},{3,2},{4,5},{5,4},{6,7},{7,6},{8,9},{9,8},{10,11... | collective-permute-start | bytes 6152 | tf_op jit(solution)/shard_map/ppermute | solution.py:239
  41.9 23.0 %collective-permute-start.11 = (bf16[256,1792]{1,0:T(8,128)(2,1)}, bf16[256,1792]{1,0:T(8,128)(2,1)}, u32[]{:S(2)}, u32[]{:S(2)}) collective-permute-start(bf16[256,1792]{1,0:T(8,128)(2,1)} %constant_dynamic-slice_fusion.5), channel_id=1, source_target_pairs={{0,1},{1,0},{2,3},{3,2},{4,5},{5,4},{6,7},{7,6},{8,9},{9,8},{10,11... | collective-permute-start | bytes 2752520 | tf_op jit(solution)/shard_map/ppermute | solution.py:184
  43.3 3.6 %collective-permute-start.6 = (f32[2,4,128]{2,1,0:T(4,128)S(1)}, f32[2,4,128]{2,1,0:T(4,128)S(1)}, u32[]{:S(2)}, u32[]{:S(2)}) collective-permute-start(f32[2,4,128]{2,1,0:T(4,128)S(1)} %pad_maximum_fusion.8), channel_id=1, source_target_pairs={{0,2},{1,3},{2,0},{3,1},{4,6},{5,7},{6,4},{7,5},{8,10},{9,11},{10,... | collective-permute-start | bytes 12296 | tf_op jit(solution)/shard_map/ppermute | solution.py:239
  46.9 16.5 %collective-permute-start.7 = (f32[4,4,128]{2,1,0:T(4,128)S(1)}, f32[4,4,128]{2,1,0:T(4,128)S(1)}, u32[]{:S(2)}, u32[]{:S(2)}) collective-permute-start(f32[4,4,128]{2,1,0:T(4,128)S(1)} %pad_maximum_fusion.7), channel_id=1, source_target_pairs={{0,4},{1,5},{2,6},{3,7},{4,0},{5,1},{6,2},{7,3},{8,12},{9,13},{10,... | collective-permute-start | bytes 24584 | tf_op jit(solution)/shard_map/ppermute | solution.py:239
  51.1 19.9 %copy-start.2 = (bf16[1024,256]{1,0:T(8,128)(2,1)}, bf16[1024,256]{1,0:T(8,128)(2,1)S(1)}, u32[]{:S(2)}) copy-start(bf16[1024,256]{1,0:T(8,128)(2,1)S(1)} %collective-permute-done.8.refs_2_) | copy-start | bytes 1572868
  51.1 18.3 %collective-permute-start.15 = (bf16[128,2048]{1,0:T(8,128)(2,1)}, bf16[128,2048]{1,0:T(8,128)(2,1)}, u32[]{:S(2)}, u32[]{:S(2)}) collective-permute-start(bf16[128,2048]{1,0:T(8,128)(2,1)} %get-tuple-element.298), channel_id=1, source_target_pairs={{0,1},{1,0},{2,3},{3,2},{4,5},{5,4},{6,7},{7,6},{8,9},{9,8},{10,11... | collective-permute-start | bytes 1572872 | tf_op jit(solution)/shard_map/ppermute | solution.py:184
  63.4 7.5 %collective-permute-start.9 = (bf16[1024,256]{1,0:T(8,128)(2,1)S(1)}, bf16[1024,256]{1,0:T(8,128)(2,1)}, u32[]{:S(2)}, u32[]{:S(2)}) collective-permute-start(bf16[1024,256]{1,0:T(8,128)(2,1)S(1)} %collective-permute-done.8.refs_2_), channel_id=1, source_target_pairs={{0,1},{1,0},{2,3},{3,2},{4,5},{5,4},{6,7},{7,6},{8,9},{9,8},{10,11... | collective-permute-start | bytes 1572872 | tf_op jit(solution)/shard_map/ppermute | solution.py:184
  63.4 7.5 %collective-permute-start.14 = (bf16[1024,256]{1,0:T(8,128)(2,1)}, bf16[1024,256]{1,0:T(8,128)(2,1)}, u32[]{:S(2)}, u32[]{:S(2)}) collective-permute-start(bf16[1024,256]{1,0:T(8,128)(2,1)} %collective-permute-done.13.refs_6_), channel_id=1, source_target_pairs={{0,1},{1,0},{2,3},{3,2},{4,5},{5,4},{6,7},{7,6},{8,9},{9,8},{10,11... | collective-permute-start | bytes 1572872 | tf_op jit(solution)/shard_map/ppermute | solution.py:184
  67.9 14.8 %copy-start.16 = (bf16[512,256]{1,0:T(8,128)(2,1)}, bf16[512,256]{1,0:T(8,128)(2,1)S(1)}, u32[]{:S(2)}) copy-start(bf16[512,256]{1,0:T(8,128)(2,1)S(1)} %pad_maximum_fusion.5.refs_8_) | copy-start | bytes 786436
  69.0 2.0 collective-permute-start.12
  76.2 26.6 %copy-start.14 = (bf16[1024,256]{1,0:T(8,128)(2,1)S(1)}, bf16[1024,256]{1,0:T(8,128)(2,1)}, u32[]{:S(2)}) copy-start(bf16[1024,256]{1,0:T(8,128)(2,1)} %partial_product.5) | copy-start | bytes 1572868
  76.2 26.6 %collective-permute-start.21 = (bf16[1024,256]{1,0:T(8,128)(2,1)}, bf16[1024,256]{1,0:T(8,128)(2,1)S(1)}, u32[]{:S(2)}, u32[]{:S(2)}) collective-permute-start(bf16[1024,256]{1,0:T(8,128)(2,1)} %partial_product.5), channel_id=1, source_target_pairs={{0,2},{1,3},{6,4},{7,5},{8,10},{9,11},{14,12},{15,13},{16,18},{17,... | collective-permute-start | bytes 1572872 | tf_op jit(solution)/shard_map/ppermute | solution.py:197
  79.8 10.1 %collective-permute-start.18 = (bf16[512,256]{1,0:T(8,128)(2,1)S(1)}, bf16[512,256]{1,0:T(8,128)(2,1)S(1)}, u32[]{:S(2)}, u32[]{:S(2)}) collective-permute-start(bf16[512,256]{1,0:T(8,128)(2,1)S(1)} %pad_maximum_fusion.5.refs_8_), channel_id=1, source_target_pairs={{0,24},{8,16},{16,8},{24,0},{1,25},{9,17},{17,9},{25,1},{2,26},{10... | collective-permute-start | bytes 786440 | tf_op jit(solution)/shard_map/ppermute | solution.py:187
  81.3 13.5 %collective-permute-start.17 = (bf16[512,256]{1,0:T(8,128)(2,1)S(1)}, bf16[512,256]{1,0:T(8,128)(2,1)S(1)}, u32[]{:S(2)}, u32[]{:S(2)}) collective-permute-start(bf16[512,256]{1,0:T(8,128)(2,1)S(1)} %pad_maximum_fusion.5.refs_8_), channel_id=1, source_target_pairs={{0,16},{8,24},{16,0},{24,8},{1,17},{9,25},{17,1},{25,9},{2,18},{10... | collective-permute-start | bytes 786440 | tf_op jit(solution)/shard_map/ppermute | solution.py:187
  82.8 12.1 %collective-permute-start.16 = (bf16[512,256]{1,0:T(8,128)(2,1)S(1)}, bf16[512,256]{1,0:T(8,128)(2,1)S(1)}, u32[]{:S(2)}, u32[]{:S(2)}) collective-permute-start(bf16[512,256]{1,0:T(8,128)(2,1)S(1)} %pad_maximum_fusion.5.refs_8_), channel_id=1, source_target_pairs={{0,8},{8,0},{16,24},{24,16},{1,9},{9,1},{17,25},{25,17},{2,10},{10... | collective-permute-start | bytes 786440 | tf_op jit(solution)/shard_map/ppermute | solution.py:187
  94.9 14.2 %collective-permute-start.20 = (bf16[512,512]{1,0:T(8,128)(2,1)}, bf16[512,512]{1,0:T(8,128)(2,1)}, u32[]{:S(2)}, u32[]{:S(2)}) collective-permute-start(bf16[512,512]{1,0:T(8,128)(2,1)} %get-tuple-element.212.refs_8_), channel_id=1, source_target_pairs={{0,16},{8,24},{16,0},{24,8},{1,17},{9,25},{17,1},{25,9},{2,18},{10... | collective-permute-start | bytes 1572872 | tf_op jit(solution)/shard_map/ppermute | solution.py:187
  95.5 14.6 %collective-permute-start.19 = (bf16[512,512]{1,0:T(8,128)(2,1)}, bf16[512,512]{1,0:T(8,128)(2,1)}, u32[]{:S(2)}, u32[]{:S(2)}) collective-permute-start(bf16[512,512]{1,0:T(8,128)(2,1)} %get-tuple-element.212.refs_8_), channel_id=1, source_target_pairs={{0,8},{8,0},{16,24},{24,16},{1,9},{9,1},{17,25},{25,17},{2,10},{10... | collective-permute-start | bytes 1572872 | tf_op jit(solution)/shard_map/ppermute | solution.py:187
  101.3 27.9 %collective-permute-start.25 = (bf16[1024,256]{1,0:T(8,128)(2,1)}, bf16[1024,256]{1,0:T(8,128)(2,1)S(1)}, u32[]{:S(2)}, u32[]{:S(2)}) collective-permute-start(bf16[1024,256]{1,0:T(8,128)(2,1)} %partial_product.6), channel_id=1, source_target_pairs={{0,2},{1,3},{6,4},{7,5},{8,10},{9,11},{14,12},{15,13},{16,18},{17,... | collective-permute-start | bytes 1572872 | tf_op jit(solution)/shard_map/ppermute | solution.py:197
  111.8 7.7 %collective-permute-start.23 = (bf16[256,512]{1,0:T(8,128)(2,1)}, bf16[256,512]{1,0:T(8,128)(2,1)}, u32[]{:S(2)}, u32[]{:S(2)}) collective-permute-start(bf16[256,512]{1,0:T(8,128)(2,1)} %slice.171), channel_id=1, source_target_pairs={{0,16},{8,24},{16,0},{24,8},{1,17},{9,25},{17,1},{25,9},{2,18},{10... | collective-permute-start | bytes 786440 | tf_op jit(solution)/shard_map/ppermute | solution.py:187
  112.5 6.9 %collective-permute-start.22 = (bf16[256,512]{1,0:T(8,128)(2,1)S(1)}, bf16[256,512]{1,0:T(8,128)(2,1)}, u32[]{:S(2)}, u32[]{:S(2)}) collective-permute-start(bf16[256,512]{1,0:T(8,128)(2,1)S(1)} %slice.170), channel_id=1, source_target_pairs={{0,8},{8,0},{16,24},{24,16},{1,9},{9,1},{17,25},{25,17},{2,10},{10... | collective-permute-start | bytes 786440 | tf_op jit(solution)/shard_map/ppermute | solution.py:187
  113.8 16.3 %collective-permute-start.24 = (bf16[1024,256]{1,0:T(8,128)(2,1)S(1)}, bf16[1024,256]{1,0:T(8,128)(2,1)S(1)}, u32[]{:S(2)}, u32[]{:S(2)}) collective-permute-start(bf16[1024,256]{1,0:T(8,128)(2,1)S(1)} %add_convert_fusion.15), channel_id=1, source_target_pairs={{2,4},{3,5},{4,2},{5,3},{10,12},{11,13},{12,10},{13,11},{18,20},{1... | collective-permute-start | bytes 1572872 | tf_op jit(solution)/shard_map/ppermute | solution.py:197
  119.5 12.8 %collective-permute-start.27 = (bf16[512,512]{1,0:T(8,128)(2,1)}, bf16[512,512]{1,0:T(8,128)(2,1)S(1)}, u32[]{:S(2)}, u32[]{:S(2)}) collective-permute-start(bf16[512,512]{1,0:T(8,128)(2,1)} %get-tuple-element.237.refs_8_), channel_id=1, source_target_pairs={{0,8},{8,0},{16,24},{24,16},{1,9},{9,1},{17,25},{25,17},{2,10},{10... | collective-permute-start | bytes 1572872 | tf_op jit(solution)/shard_map/ppermute | solution.py:187
  121.0 11.8 %collective-permute-start.26 = (bf16[512,512]{1,0:T(8,128)(2,1)}, bf16[512,512]{1,0:T(8,128)(2,1)}, u32[]{:S(2)}, u32[]{:S(2)}) collective-permute-start(bf16[512,512]{1,0:T(8,128)(2,1)} %get-tuple-element.237.refs_8_), channel_id=1, source_target_pairs={{0,16},{8,24},{16,0},{24,8},{1,17},{9,25},{17,1},{25,9},{2,18},{10... | collective-permute-start | bytes 1572872 | tf_op jit(solution)/shard_map/ppermute | solution.py:187
  127.4 14.4 %copy-start.18 = (bf16[1024,256]{1,0:T(8,128)(2,1)S(1)}, bf16[1024,256]{1,0:T(8,128)(2,1)}, u32[]{:S(2)}) copy-start(bf16[1024,256]{1,0:T(8,128)(2,1)} %get-tuple-element.228) | copy-start | bytes 1572868
  127.4 14.4 %collective-permute-start.32 = (bf16[1024,256]{1,0:T(8,128)(2,1)}, bf16[1024,256]{1,0:T(8,128)(2,1)S(1)}, u32[]{:S(2)}, u32[]{:S(2)}) collective-permute-start(bf16[1024,256]{1,0:T(8,128)(2,1)} %get-tuple-element.228), channel_id=1, source_target_pairs={{0,2},{1,3},{6,4},{7,5},{8,10},{9,11},{14,12},{15,13},{16,18},{17,... | collective-permute-start | bytes 1572872 | tf_op jit(solution)/shard_map/ppermute | solution.py:197
  129.3 13.3 %collective-permute-start.31 = (bf16[1024,256]{1,0:T(8,128)(2,1)S(1)}, bf16[1024,256]{1,0:T(8,128)(2,1)S(1)}, u32[]{:S(2)}, u32[]{:S(2)}) collective-permute-start(bf16[1024,256]{1,0:T(8,128)(2,1)S(1)} %add_convert_fusion.14), channel_id=1, source_target_pairs={{2,4},{3,5},{4,2},{5,3},{10,12},{11,13},{12,10},{13,11},{18,20},{1... | collective-permute-start | bytes 1572872 | tf_op jit(solution)/shard_map/ppermute | solution.py:197
  130.0 11.8 %copy-start.8 = (bf16[1024,256]{1,0:T(8,128)(2,1)}, bf16[1024,256]{1,0:T(8,128)(2,1)S(1)}, u32[]{:S(2)}) copy-start(bf16[1024,256]{1,0:T(8,128)(2,1)S(1)} %collective-permute-done.24) | copy-start | bytes 1572868
  133.8 8.9 %collective-permute-start.30 = (bf16[256,512]{1,0:T(8,128)(2,1)S(1)}, bf16[256,512]{1,0:T(8,128)(2,1)S(1)}, u32[]{:S(2)}, u32[]{:S(2)}) collective-permute-start(bf16[256,512]{1,0:T(8,128)(2,1)S(1)} %slice.173), channel_id=1, source_target_pairs={{0,16},{8,24},{16,0},{24,8},{1,17},{9,25},{17,1},{25,9},{2,18},{10... | collective-permute-start | bytes 786440 | tf_op jit(solution)/shard_map/ppermute | solution.py:187
  135.0 7.6 %collective-permute-start.29 = (bf16[256,512]{1,0:T(8,128)(2,1)S(1)}, bf16[256,512]{1,0:T(8,128)(2,1)S(1)}, u32[]{:S(2)}, u32[]{:S(2)}) collective-permute-start(bf16[256,512]{1,0:T(8,128)(2,1)S(1)} %slice.172), channel_id=1, source_target_pairs={{0,8},{8,0},{16,24},{24,16},{1,9},{9,1},{17,25},{25,17},{2,10},{10... | collective-permute-start | bytes 786440 | tf_op jit(solution)/shard_map/ppermute | solution.py:187
  135.9 21.0 %collective-permute-start.28 = (bf16[1024,256]{1,0:T(8,128)(2,1)}, bf16[1024,256]{1,0:T(8,128)(2,1)}, u32[]{:S(2)}, u32[]{:S(2)}) collective-permute-start(bf16[1024,256]{1,0:T(8,128)(2,1)} %broadcast_select_fusion.13), channel_id=1, source_target_pairs={{0,2},{1,3},{2,0},{3,1},{4,6},{5,7},{6,4},{7,5},{8,10},{9,11},{10,... | collective-permute-start | bytes 1572872 | tf_op jit(solution)/shard_map/ppermute | solution.py:197
  141.9 18.7 %collective-permute-start.34 = (bf16[1024,256]{1,0:T(8,128)(2,1)S(1)}, bf16[1024,256]{1,0:T(8,128)(2,1)S(1)}, u32[]{:S(2)}, u32[]{:S(2)}) collective-permute-start(bf16[1024,256]{1,0:T(8,128)(2,1)S(1)} %add_convert_fusion.12), channel_id=1, source_target_pairs={{2,4},{3,5},{4,2},{5,3},{10,12},{11,13},{12,10},{13,11},{18,20},{1... | collective-permute-start | bytes 1572872 | tf_op jit(solution)/shard_map/ppermute | solution.py:197
  142.7 8.8 %copy-start.6 = (bf16[1024,256]{1,0:T(8,128)(2,1)}, bf16[1024,256]{1,0:T(8,128)(2,1)S(1)}, u32[]{:S(2)}) copy-start(bf16[1024,256]{1,0:T(8,128)(2,1)S(1)} %collective-permute-done.31) | copy-start | bytes 1572868
  143.5 18.9 %collective-permute-start.36 = (bf16[512,512]{1,0:T(8,128)(2,1)}, bf16[512,512]{1,0:T(8,128)(2,1)}, u32[]{:S(2)}, u32[]{:S(2)}) collective-permute-start(bf16[512,512]{1,0:T(8,128)(2,1)} %pad_maximum_fusion.2.refs_8_), channel_id=1, source_target_pairs={{0,8},{8,0},{16,24},{24,16},{1,9},{9,1},{17,25},{25,17},{2,10},{10... | collective-permute-start | bytes 1572872 | tf_op jit(solution)/shard_map/ppermute | solution.py:187
  145.1 18.4 %collective-permute-start.35 = (bf16[512,512]{1,0:T(8,128)(2,1)}, bf16[512,512]{1,0:T(8,128)(2,1)}, u32[]{:S(2)}, u32[]{:S(2)}) collective-permute-start(bf16[512,512]{1,0:T(8,128)(2,1)} %pad_maximum_fusion.2.refs_8_), channel_id=1, source_target_pairs={{0,16},{8,24},{16,0},{24,8},{1,17},{9,25},{17,1},{25,9},{2,18},{10... | collective-permute-start | bytes 1572872 | tf_op jit(solution)/shard_map/ppermute | solution.py:187
  152.8 15.3 %collective-permute-start.33 = (bf16[1024,256]{1,0:T(8,128)(2,1)S(1)}, bf16[1024,256]{1,0:T(8,128)(2,1)S(1)}, u32[]{:S(2)}, u32[]{:S(2)}) collective-permute-start(bf16[1024,256]{1,0:T(8,128)(2,1)S(1)} %broadcast_select_fusion.12), channel_id=1, source_target_pairs={{0,2},{1,3},{2,0},{3,1},{4,6},{5,7},{6,4},{7,5},{8,10},{9,11},{10,... | collective-permute-start | bytes 1572872 | tf_op jit(solution)/shard_map/ppermute | solution.py:197
  158.3 9.8 %copy-start.7 = (bf16[1024,256]{1,0:T(8,128)(2,1)S(1)}, bf16[1024,256]{1,0:T(8,128)(2,1)}, u32[]{:S(2)}) copy-start(bf16[1024,256]{1,0:T(8,128)(2,1)} %copy-done.6) | copy-start | bytes 1572868
  159.8 11.2 %collective-permute-start.40 = (bf16[1024,256]{1,0:T(8,128)(2,1)S(1)}, bf16[1024,256]{1,0:T(8,128)(2,1)S(1)}, u32[]{:S(2)}, u32[]{:S(2)}) collective-permute-start(bf16[1024,256]{1,0:T(8,128)(2,1)S(1)} %add_convert_fusion.10), channel_id=1, source_target_pairs={{2,4},{3,5},{4,2},{5,3},{10,12},{11,13},{12,10},{13,11},{18,20},{1... | collective-permute-start | bytes 1572872 | tf_op jit(solution)/shard_map/ppermute | solution.py:197
  164.4 6.6 %collective-permute-start.39 = (bf16[256,512]{1,0:T(8,128)(2,1)S(1)}, bf16[256,512]{1,0:T(8,128)(2,1)S(1)}, u32[]{:S(2)}, u32[]{:S(2)}) collective-permute-start(bf16[256,512]{1,0:T(8,128)(2,1)S(1)} %slice.176), channel_id=1, source_target_pairs={{0,16},{8,24},{16,0},{24,8},{1,17},{9,25},{17,1},{25,9},{2,18},{10... | collective-permute-start | bytes 786440 | tf_op jit(solution)/shard_map/ppermute | solution.py:187
  166.0 6.4 %collective-permute-start.38 = (bf16[256,512]{1,0:T(8,128)(2,1)S(1)}, bf16[256,512]{1,0:T(8,128)(2,1)S(1)}, u32[]{:S(2)}, u32[]{:S(2)}) collective-permute-start(bf16[256,512]{1,0:T(8,128)(2,1)S(1)} %slice.175), channel_id=1, source_target_pairs={{0,8},{8,0},{16,24},{24,16},{1,9},{9,1},{17,25},{25,17},{2,10},{10... | collective-permute-start | bytes 786440 | tf_op jit(solution)/shard_map/ppermute | solution.py:187
  166.5 17.4 %collective-permute-start.37 = (bf16[1024,256]{1,0:T(8,128)(2,1)}, bf16[1024,256]{1,0:T(8,128)(2,1)}, u32[]{:S(2)}, u32[]{:S(2)}) collective-permute-start(bf16[1024,256]{1,0:T(8,128)(2,1)} %broadcast_select_fusion.10), channel_id=1, source_target_pairs={{0,2},{1,3},{2,0},{3,1},{4,6},{5,7},{6,4},{7,5},{8,10},{9,11},{10,... | collective-permute-start | bytes 1572872 | tf_op jit(solution)/shard_map/ppermute | solution.py:197
  168.7 18.9 %collective-permute-start.42 = (bf16[1024,256]{1,0:T(8,128)(2,1)S(1)}, bf16[1024,256]{1,0:T(8,128)(2,1)}, u32[]{:S(2)}, u32[]{:S(2)}) collective-permute-start(bf16[1024,256]{1,0:T(8,128)(2,1)S(1)} %add_convert_fusion.8), channel_id=1, source_target_pairs={{2,4},{3,5},{4,2},{5,3},{10,12},{11,13},{12,10},{13,11},{18,20},{1... | collective-permute-start | bytes 1572872 | tf_op jit(solution)/shard_map/ppermute | solution.py:197
  180.2 14.9 %collective-permute-start.41 = (bf16[1024,256]{1,0:T(8,128)(2,1)S(1)}, bf16[1024,256]{1,0:T(8,128)(2,1)S(1)}, u32[]{:S(2)}, u32[]{:S(2)}) collective-permute-start(bf16[1024,256]{1,0:T(8,128)(2,1)S(1)} %broadcast_select_fusion.8), channel_id=1, source_target_pairs={{0,2},{1,3},{2,0},{3,1},{4,6},{5,7},{6,4},{7,5},{8,10},{9,11},{10,... | collective-permute-start | bytes 1572872 | tf_op jit(solution)/shard_map/ppermute | solution.py:197
  185.1 11.5 %collective-permute-start.44 = (bf16[1024,256]{1,0:T(8,128)(2,1)S(1)}, bf16[1024,256]{1,0:T(8,128)(2,1)S(1)}, u32[]{:S(2)}, u32[]{:S(2)}) collective-permute-start(bf16[1024,256]{1,0:T(8,128)(2,1)S(1)} %add_convert_fusion.6), channel_id=1, source_target_pairs={{2,4},{3,5},{4,2},{5,3},{10,12},{11,13},{12,10},{13,11},{18,20},{1... | collective-permute-start | bytes 1572872 | tf_op jit(solution)/shard_map/ppermute | solution.py:197
  189.2 17.2 %collective-permute-start.43 = (bf16[1024,256]{1,0:T(8,128)(2,1)S(1)}, bf16[1024,256]{1,0:T(8,128)(2,1)S(1)}, u32[]{:S(2)}, u32[]{:S(2)}) collective-permute-start(bf16[1024,256]{1,0:T(8,128)(2,1)S(1)} %broadcast_select_fusion.6), channel_id=1, source_target_pairs={{0,2},{1,3},{2,0},{3,1},{4,6},{5,7},{6,4},{7,5},{8,10},{9,11},{10,... | collective-permute-start | bytes 1572872 | tf_op jit(solution)/shard_map/ppermute | solution.py:197
  195.8 13.0 %collective-permute-start.46 = (bf16[1024,256]{1,0:T(8,128)(2,1)S(1)}, bf16[1024,256]{1,0:T(8,128)(2,1)S(1)}, u32[]{:S(2)}, u32[]{:S(2)}) collective-permute-start(bf16[1024,256]{1,0:T(8,128)(2,1)S(1)} %add_convert_fusion.4), channel_id=1, source_target_pairs={{2,4},{3,5},{4,2},{5,3},{10,12},{11,13},{12,10},{13,11},{18,20},{1... | collective-permute-start | bytes 1572872 | tf_op jit(solution)/shard_map/ppermute | solution.py:197
  196.7 20.9 %collective-permute-start.45 = (bf16[1024,256]{1,0:T(8,128)(2,1)S(1)}, bf16[1024,256]{1,0:T(8,128)(2,1)S(1)}, u32[]{:S(2)}, u32[]{:S(2)}) collective-permute-start(bf16[1024,256]{1,0:T(8,128)(2,1)S(1)} %add_convert_fusion.3), channel_id=1, source_target_pairs={{2,0},{3,1},{4,6},{5,7},{10,8},{11,9},{12,14},{13,15},{18,16},{19,... | collective-permute-start | bytes 1572872 | tf_op jit(solution)/shard_map/ppermute | solution.py:197
  208.0 2.2 collective-permute-start.48
  209.0 17.4 %collective-permute-start.47 = (bf16[1024,256]{1,0:T(8,128)(2,1)S(1)}, bf16[1024,256]{1,0:T(8,128)(2,1)S(1)}, u32[]{:S(2)}, u32[]{:S(2)}) collective-permute-start(bf16[1024,256]{1,0:T(8,128)(2,1)S(1)} %add_convert_fusion.1), channel_id=1, source_target_pairs={{2,0},{3,1},{4,6},{5,7},{10,8},{11,9},{12,14},{13,15},{18,16},{19,... | collective-permute-start | bytes 1572872 | tf_op jit(solution)/shard_map/ppermute | solution.py:197
  218.0 14.1 %collective-permute-start.49 = (bf16[1024,256]{1,0:T(8,128)(2,1)S(1)}, bf16[1024,256]{1,0:T(8,128)(2,1)S(1)}, u32[]{:S(2)}, u32[]{:S(2)}) collective-permute-start(bf16[1024,256]{1,0:T(8,128)(2,1)S(1)} %add_convert_fusion), channel_id=1, source_target_pairs={{2,0},{3,1},{4,6},{5,7},{10,8},{11,9},{12,14},{13,15},{18,16},{19,... | collective-permute-start | bytes 1572872 | tf_op jit(solution)/shard_map/ppermute | solution.py:197
  219.3 13.2 %collective-permute-start.50 = (bf16[448,1536]{1,0:T(8,128)(2,1)S(1)}, bf16[448,1536]{1,0:T(8,128)(2,1)S(1)}, u32[]{:S(2)}, u32[]{:S(2)}) collective-permute-start(bf16[448,1536]{1,0:T(8,128)(2,1)S(1)} %constant_dynamic-update-slice_fusion), channel_id=1, source_target_pairs={{0,1},{1,0},{2,3},{3,2},{4,5},{5,4},{6,7},{7,6},{8,9},{9,8},{10,11... | collective-permute-start | bytes 4128776 | tf_op jit(solution)/shard_map/ppermute | solution.py:184
  232.5 1.9 collective-permute-start.51
  (22 other events, 98.4 us)

commit v9 on v7

--- a/solution.py
+++ b/solution.py
@@ -8,12 +8,13 @@
 from jax.sharding import PartitionSpec as P
 
 EXP_DEV = 1
-GROUPS = ((1, 1), (1, 1), (1, 1), (1, 1))
+GROUPS = ((1,), (1,), (1, 1), (1, 1), (1, 1))
+FIRST_PHASE = {2: 3, 4: 4}
+SECOND_PHASE = {3: 3, 5: 4}
 UNITS = sum(map(sum, GROUPS))
 DELAY = 3
 SWAPS = (6, 8)
-CONV_VMEM = 44 * 1024 * 1024
-PRODUCT_VMEM = 22 * 1024 * 1024
+VMEM_BYTES = 60 * 1024 * 1024
 
 
 def conv_kernel(tile, at_ctx, out_grad, gate_in, conv_in, scan_grad, taps, bias, skip, *refs):
@@ -31,11 +32,12 @@
         row_at = pl.multiple_of(group * rows_at_once, rows_at_once)
         rows = pl.ds(row_at, rows_at_once)
 
-        def spread(index):
+        def spread(index, width=tile):
             column = jnp.broadcast_to(columns_of[rows, index : index + 1], (rows_at_once, 128))
-            return jnp.concatenate([column] * (tile // 128), axis=1)
+            return jnp.concatenate([column] * (width // 128), axis=1)
 
         weights = [spread(tap) for tap in range(kernel_taps)]
+        wider = [spread(tap, tile + 128) for tap in (0, 1)]
         bias_half = spread(kernel_taps)
         skip_value = spread(kernel_taps + 1)
         after = jnp.zeros((rows_at_once, 128), jnp.float32)
@@ -49,18 +51,18 @@
             else:
                 before = jnp.zeros((rows_at_once, 128), jnp.float32)
             wide = jnp.concatenate([before, here], axis=1)
-            half = bias_half + weights[kernel_taps - 1] * here
-            for tap in range(kernel_taps - 1):
-                back = kernel_taps - 1 - tap
-                half = half + weights[tap] * pltpu.roll(wide, back, 1)[:, 128:]
+            one_back = pltpu.roll(wide, 1, 1)
+            older = wider[1] * wide + wider[0] * one_back
+            half = bias_half + weights[3] * here + weights[2] * one_back[:, 128:]
+            half = half + pltpu.roll(older, 2, 1)[:, 128:]
             turn = jnp.tanh(half)
             scan = scan_grad[rows, columns].astype(jnp.float32)
             grad = (scan + skip_value * gated) * (1.0 + turn + half * (1.0 - turn * turn))
             wide_grad = jnp.concatenate([grad, after], axis=1)
-            total = weights[kernel_taps - 1] * grad
-            for tap in range(kernel_taps - 1):
-                ahead = kernel_taps - 1 - tap
-                total = total + weights[tap] * pltpu.roll(wide_grad, tile + 128 - ahead, 1)[:, :tile]
+            one_on = pltpu.roll(wide_grad, tile + 127, 1)
+            later = wider[1] * wide_grad + wider[0] * one_on
+            total = weights[3] * grad + weights[2] * one_on[:, :tile]
+            total = total + pltpu.roll(later, tile + 126, 1)[:, :tile]
             flat[rows, columns] = total.astype(flat.dtype)
             after = grad[:, :128]
         return 0
@@ -90,7 +92,7 @@
             scratch_shapes=[pltpu.VMEM((block, length), jnp.bfloat16), pltpu.VMEM((block, 8), jnp.float32)],
         ),
         out_shape=[jax.ShapeDtypeStruct((window, channels), jnp.bfloat16)] * ctx_count,
-        compiler_params=pltpu.CompilerParams(vmem_limit_bytes=CONV_VMEM),
+        compiler_params=pltpu.CompilerParams(vmem_limit_bytes=VMEM_BYTES),
         cost_estimate=pl.CostEstimate(
             flops=40 * channels * length, bytes_accessed=10 * channels * length, transcendentals=2 * channels * length
         ),
@@ -136,7 +138,7 @@
             out_specs=[pl.BlockSpec((tile, part), lambda step, place: (step, 0)) for part in widths],
         ),
         out_shape=[jax.ShapeDtypeStruct((tokens, part), jnp.bfloat16) for part in widths],
-        compiler_params=pltpu.CompilerParams(vmem_limit_bytes=PRODUCT_VMEM),
+        compiler_params=pltpu.CompilerParams(vmem_limit_bytes=VMEM_BYTES),
         cost_estimate=pl.CostEstimate(flops=flops, bytes_accessed=moved, transcendentals=0),
         name="partial_product",
     )(place, *lefts, *rights, resid)
@@ -239,10 +241,6 @@
     for group, at in list(zip(widths, starts))[1:]:
         cut = slice(at - first, at - first + sum(group))
         rest.append(jnp.concatenate([rest_here[:, cut], rest_there[:, cut]], axis=0))
-    received[-2], rest = lax.optimization_barrier((received[-2], rest))
-    rights.append(spread(rest[0]))
-    for piece in received:
-        lefts += [piece, to_core(piece)]
     resid_here, resid_there = both_cores(resid_grad, 0, half)
     resid = jnp.where(
         core_at == 0,
@@ -265,9 +263,14 @@
     picks = slot == jnp.arange(2 * capacity, dtype=jnp.int32)[None, None, :, None]
     scale = jnp.sum(jnp.where(picks, prob.reshape(2, chips, 1, tile), 0.0), axis=3, keepdims=True)
     picks = picks.astype(jnp.bfloat16)
-    picks, scale, lefts = lax.optimization_barrier((picks, scale, lefts))
-
-    lefts, picks, scale, resid, rest = lax.optimization_barrier((lefts, picks, scale, resid, rest))
+
+    rights.append(spread(rest[0]))
+    received, rest, rights[1], resid, picks, scale = lax.optimization_barrier(
+        (received, rest, rights[1], resid, picks, scale)
+    )
+    for piece in received:
+        lefts += [piece, to_core(piece)]
+
     if channels < 128:
         lefts = [jnp.concatenate(lefts, axis=1)]
     place = chip_at.astype(jnp.int32).reshape(1)
@@ -312,8 +315,10 @@
     ready = [[None] * pieces for _ in range(hops + 1)]
     outer, across = {}, {}
     first_of = [sum(map(len, GROUPS[:at])) for at in range(len(GROUPS))]
+    lefts, rest[1] = lax.optimization_barrier((lefts, rest[1]))
+    rights.append(spread_near(rest[1]) if square else spread(rest[1]))
     sums[0][: len(GROUPS[0])] = products(0, rights[0])
-    near = None
+    rights += [None] * (len(GROUPS) - len(rights))
     for step in range(pieces + 2 * lag * hops + DELAY + 1):
         for hop in range(hops):
             if (step - 2, hop) not in outer:
@@ -332,16 +337,14 @@
             got, index = across[step - 1]
             own, got = chain(sums[hops][index], got)
             ready[hops][index] = add(own, got)
-        if square and near is not None and step % 2:
-            near = spread_on(near)
-        if step and step in first_of:
-            group_at = first_of.index(step)
-            if near is not None:
-                rights.append(near)
-            near = None
-            if group_at + 1 < len(GROUPS):
-                piece, *rights[group_at] = chain(rest[group_at], *rights[group_at])
-                near = spread_near(piece) if square else spread(piece)
+        if step in SECOND_PHASE and square:
+            rights[SECOND_PHASE[step]] = spread_on(rights[SECOND_PHASE[step]])
+        group_at = first_of.index(step) if step and step in first_of else None
+        if step in FIRST_PHASE:
+            coming = FIRST_PHASE[step]
+            piece, *rights[group_at] = chain(rest[coming - 1], *rights[group_at])
+            rights[coming] = spread_near(piece) if square else spread(piece)
+        if group_at:
             sums[0][step : step + len(GROUPS[group_at])] = products(group_at, rights[group_at])
         for hop in range(hops):
             inward = step - lag * hop
@@ -358,6 +361,8 @@
                 continue
             (payload,) = chain(payload)
             outer[step, hop] = (swap_chips(payload, hop, inward is not None, outward is not None), inward, outward)
+        if step == 1 and square:
+            rights[2] = spread_on(rights[2])
     result = jnp.where(
         core_at == 0,
         jnp.concatenate(rows_own + rows_got, axis=1),

time: 228 us -> 213 us (0.934)
  waiting for transfers between devices: 78.2 us -> 63.3 us
  local copies, waits for them, and re-layouts: 33.3 us -> 22 us
  other arithmetic: 15.1 us -> 23.4 us
  Pallas kernels: 31.8 us -> 39.1 us
  starting transfers between devices: 64.4 us -> 60.6 us
    unnamed x100 -> x122, local copies, waits for them, and re-layouts: 22.8 us -> 6.72 us
    pallas_call x4 -> x5, Pallas kernels: 15.2 us -> 26.3 us  [matmul(): pl.pallas_call(functools.partial(matmul_kernel, len(lefts), len(rights)),...]
    ppermute x17 -> x21, waiting for transfers between devices: 23 us -> 12.5 us  [to_ctx(): lax.ppermute(array, 'ctx', [(place, place ^ offset) for place in range(ct...]
    ppermute x19, starting transfers between devices: 38 us -> 29.8 us  [swap_chips(): return lax.ppermute(array, 'exp', sorted(pairs))]
    ppermute x19, waiting for transfers between devices: 52.7 us -> 45.3 us  [swap_chips(): return lax.ppermute(array, 'exp', sorted(pairs))]
    ppermute x17 -> x21, starting transfers between devices: 19.9 us -> 24.4 us  [to_ctx(): lax.ppermute(array, 'ctx', [(place, place ^ offset) for place in range(ct...]
    select_n x5, other arithmetic: 2.16 us -> 6.04 us  [on_device(): jnp.where(distance == hop, sums[hop][inward], ready[hop + 1][outward])]
    pallas_call x1, Pallas kernels: 16.6 us -> 12.8 us  [conv_grad(): pl.pallas_call(functools.partial(conv_kernel, tile), grid_spec=pltpu.Pref...]
  transfers between devices with their start and end apart: 48 -> 52, of which waited for: 14 -> 20; matrix products, arithmetic and copies ran while one was open for 11% -> 19% of each run, Pallas kernels for 12% -> 18%
where the time goes in v9:
time: 213 us; the launch traced here: 212 us
  waiting for transfers between devices  63.3 us (30%)
  starting transfers between devices  60.6 us (28%)
  Pallas kernels  39.1 us (18%)
  other arithmetic  23.4 us (11%)
  local copies, waits for them, and re-layouts  22 us (10%)
  matrix products  2.35 us (1%)
    ppermute x19, waiting for transfers between devices, swap_chips(): return lax.ppermute(array, 'exp', sorted(pairs))  45.3 us
    ppermute x19, starting transfers between devices, swap_chips(): return lax.ppermute(array, 'exp', sorted(pairs))  29.8 us
    pallas_call x5, Pallas kernels, matmul(): pl.pallas_call(functools.partial(matmul_kernel, len(lefts), len(rights)),...  26.3 us
    ppermute x21, starting transfers between devices, to_ctx(): lax.ppermute(array, 'ctx', [(place, place ^ offset) for place in range(ct...  24.4 us
    pallas_call x1, Pallas kernels, conv_grad(): pl.pallas_call(functools.partial(conv_kernel, tile), grid_spec=pltpu.Pref...  12.8 us
    ppermute x21, waiting for transfers between devices, to_ctx(): lax.ppermute(array, 'ctx', [(place, place ^ offset) for place in range(ct...  12.5 us
    unnamed x122, local copies, waits for them, and re-layouts  6.72 us
    select_n x5, other arithmetic, on_device(): jnp.where(distance == hop, sums[hop][inward], ready[hop + 1][outward])  6.04 us
  transfers between devices with their start and end apart: 52, of which 20 were waited for; matrix products, arithmetic and copies ran while one was open for 19% of the time, Pallas kernels for 18%

profile of v9, /device:TPU:0, one launch (start us, length us, event | category | flops | bytes accessed | tf_op | source)
XLA Modules:
  0.0 212.1 jit_solution(12618800472019918113)
XLA Ops:
  0.0 1.0 constant_dynamic-slice_fusion.8
  1.5 1.0 collective-permute-done
  2.5 3.9 %collective-permute-start.3 = (bf16[512,256]{1,0:T(8,128)(2,1)S(1)}, bf16[512,256]{1,0:T(8,128)(2,1)S(1)}, u32[]{:S(2)}, u32[]{:S(2)}) collective-permute-start(bf16[512,256]{1,0:T(8,128)(2,1)S(1)} %pad_maximum_fusion.4.refs_8_), channel_id=1, source_target_pairs={{0,24},{8,16},{16,8},{24,0},{1,25},{9,17},{17,9},{25,1},{2,26},{10... | collective-permute-start | bytes 786440 | tf_op jit(solution)/shard_map/ppermute | solution.py:181
  7.0 12.8 %conv_grad.1 = (bf16[1024,256]{1,0:T(8,128)(2,1)}, bf16[1024,256]{1,0:T(8,128)(2,1)}, bf16[1024,256]{1,0:T(8,128)(2,1)}, bf16[1024,256]{1,0:T(8,128)(2,1)}) custom-call(s32[1]{0:T(128)} %bitcast.1.at_ctx, bf16[256,4096]{1,0:T(8,128)(2,1)} %out_grad.1, bf16[256,4096]{1,0:T(8,128)(2,1)} %gate_in.1, bf16[256,4096]{1,0:T(8,128)(2,1)} %conv_in.1, ...), custom_call_target="tpu_custom_call" | custom-call | flops 41943040 | bytes 10485760 | tf_op jit(solution)/shard_map/conv_grad/pallas_call | solution.py:84
  20.8 1.9 collective-permute-start.5
  22.7 1.5 collective-permute-start.6
  24.4 2.2 %constant_dynamic-slice_fusion.5 = bf16[256,1792]{1,0:T(8,128)(2,1)} fusion(bf16[256,4096]{1,0:T(8,128)(2,1)} %param.18, s32[]{:T(128)S(6)} %select_n.141), kind=kLoop, calls=%fused_computation.106 | loop fusion | bytes 1835012 | tf_op jit(solution)/shard_map/dynamic_slice | solution.py:194
  27.1 1.1 constant_dynamic-slice_fusion.4
  28.2 2.0 collective-permute-start.14
  30.2 2.0 constant_dynamic-slice_fusion.6
  32.3 2.7 %collective-permute-start.15 = (f32[4,4,128]{2,1,0:T(4,128)S(1)}, f32[4,4,128]{2,1,0:T(4,128)S(1)}, u32[]{:S(2)}, u32[]{:S(2)}) collective-permute-start(f32[4,4,128]{2,1,0:T(4,128)S(1)} %pad_maximum_fusion.7), channel_id=1, source_target_pairs={{0,4},{1,5},{2,6},{3,7},{4,0},{5,1},{6,2},{7,3},{8,12},{9,13},{10,... | collective-permute-start | bytes 24584 | tf_op jit(solution)/shard_map/ppermute | solution.py:233
  35.9 1.0 collective-permute-done.15
  39.8 2.0 maximum_select_fusion
  42.9 2.5 %collective-permute-start.11 = (bf16[512,256]{1,0:T(8,128)(2,1)S(1)}, bf16[512,256]{1,0:T(8,128)(2,1)S(1)}, u32[]{:S(2)}, u32[]{:S(2)}) collective-permute-start(bf16[512,256]{1,0:T(8,128)(2,1)S(1)} %pad_maximum_fusion.5.refs_8_), channel_id=1, source_target_pairs={{0,24},{8,16},{16,8},{24,0},{1,25},{9,17},{17,9},{25,1},{2,26},{10... | collective-permute-start | bytes 786440 | tf_op jit(solution)/shard_map/ppermute | solution.py:181
  45.9 1.2 fusion.24
  48.5 1.0 pad_maximum_fusion
  49.5 3.5 %collective-permute-done.6.refs_4_ = bf16[1024,256]{1,0:T(8,128)(2,1)S(1)} collective-permute-done((bf16[1024,256]{1,0:T(8,128)(2,1)}, bf16[1024,256]{1,0:T(8,128)(2,1)S(1)}, u32[]{:S(2)}, u32[]{:S(2)}) %collective-permute-start.6) | collective-permute-done | bytes 524320 | tf_op jit(solution)/shard_map/ppermute | solution.py:181
  53.6 5.2 %collective-permute-done.10.refs_10_ = bf16[512,256]{1,0:T(8,128)(2,1)S(1)} collective-permute-done((bf16[512,256]{1,0:T(8,128)(2,1)S(1)}, bf16[512,256]{1,0:T(8,128)(2,1)S(1)}, u32[]{:S(2)}, u32[]{:S(2)}) %collective-permute-start.10) | collective-permute-done | bytes 262176 | tf_op jit(solution)/shard_map/ppermute | solution.py:181
  62.7 1.5 collective-permute-start.20
  64.8 4.3 %partial_product.5 = bf16[1024,256]{1,0:T(8,128)(2,1)} custom-call(s32[1]{0:T(128)} %bitcast.place, bf16[1024,256]{1,0:T(8,128)(2,1)} %get-tuple-element.149.refs_0_, bf16[1024,256]{1,0:T(8,128)(2,1)} %copy-done.1, bf16[1024,256]{1,0:T(8,128)(2,1)} %copy-done.2, bf16[1024,256]{1,0:T(8,128)(2,1)} %copy-done.4, bf16[1024,256]{1,0:T(8,128)(2,1)} %copy-done.3, ...), custom_call_target="tpu_custom_call" | custom-call | flops 1073741824 | bytes 5767168 | tf_op jit(solution)/shard_map/partial_product/pallas_call | solution.py:130
  69.1 3.6 %collective-permute-start.23 = (bf16[1024,256]{1,0:T(8,128)(2,1)}, bf16[1024,256]{1,0:T(8,128)(2,1)S(1)}, u32[]{:S(2)}, u32[]{:S(2)}) collective-permute-start(bf16[1024,256]{1,0:T(8,128)(2,1)} %partial_product.5), channel_id=1, source_target_pairs={{0,2},{1,3},{6,4},{7,5},{8,10},{9,11},{14,12},{15,13},{16,18},{17,... | collective-permute-start | bytes 1572872 | tf_op jit(solution)/shard_map/ppermute | solution.py:191
  72.7 4.3 %partial_product.6 = bf16[1024,256]{1,0:T(8,128)(2,1)} custom-call(s32[1]{0:T(128)} %bitcast.place, bf16[1024,256]{1,0:T(8,128)(2,1)} %get-tuple-element.149.refs_0_, bf16[1024,256]{1,0:T(8,128)(2,1)} %copy-done.1, bf16[1024,256]{1,0:T(8,128)(2,1)} %copy-done.2, bf16[1024,256]{1,0:T(8,128)(2,1)} %copy-done.4, bf16[1024,256]{1,0:T(8,128)(2,1)} %copy-done.3, ...), custom_call_target="tpu_custom_call" | custom-call | flops 1073741824 | bytes 5767168 | tf_op jit(solution)/shard_map/partial_product/pallas_call | solution.py:130
  77.0 2.1 collective-permute-start.25
  79.2 1.0 slice.170
  80.1 1.0 slice.171
  81.1 1.6 collective-permute-start.21
  82.7 2.7 %collective-permute-done.23 = bf16[1024,256]{1,0:T(8,128)(2,1)S(1)} collective-permute-done((bf16[1024,256]{1,0:T(8,128)(2,1)}, bf16[1024,256]{1,0:T(8,128)(2,1)S(1)}, u32[]{:S(2)}, u32[]{:S(2)}) %collective-permute-start.23) | collective-permute-done | bytes 524320 | tf_op jit(solution)/shard_map/ppermute | solution.py:191
  86.2 1.2 collective-permute-start.22
  87.4 1.2 add_convert_fusion.15
  90.2 2.3 %collective-permute-done.22.refs_12_ = bf16[256,512]{1,0:T(8,128)(2,1)S(1)} collective-permute-done((bf16[256,512]{1,0:T(8,128)(2,1)S(1)}, bf16[256,512]{1,0:T(8,128)(2,1)S(1)}, u32[]{:S(2)}, u32[]{:S(2)}) %collective-permute-start.22) | collective-permute-done | bytes 262176 | tf_op jit(solution)/shard_map/ppermute | solution.py:181
  92.6 2.1 %collective-permute-start.27 = (bf16[512,512]{1,0:T(8,128)(2,1)}, bf16[512,512]{1,0:T(8,128)(2,1)S(1)}, u32[]{:S(2)}, u32[]{:S(2)}) collective-permute-start(bf16[512,512]{1,0:T(8,128)(2,1)} %get-tuple-element.213.refs_8_), channel_id=1, source_target_pairs={{0,8},{8,0},{16,24},{24,16},{1,9},{9,1},{17,25},{25,17},{2,10},{10... | collective-permute-start | bytes 1572872 | tf_op jit(solution)/shard_map/ppermute | solution.py:181
  94.8 5.9 %partial_product.7 = (bf16[1024,256]{1,0:T(8,128)(2,1)}, bf16[1024,256]{1,0:T(8,128)(2,1)}) custom-call(s32[1]{0:T(128)} %bitcast.place, bf16[1024,256]{1,0:T(8,128)(2,1)} %get-tuple-element.149.refs_0_, bf16[1024,256]{1,0:T(8,128)(2,1)} %copy-done.1, bf16[1024,256]{1,0:T(8,128)(2,1)} %copy-done.2, bf16[1024,256]{1,0:T(8,128)(2,1)} %copy-done.4, ...), custom_call_target="tpu_custom_call" | custom-call | flops 2147483648 | bytes 7340032 | tf_op jit(solution)/shard_map/partial_product/pallas_call | solution.py:130
  100.7 5.1 %collective-permute-start.32 = (bf16[1024,256]{1,0:T(8,128)(2,1)}, bf16[1024,256]{1,0:T(8,128)(2,1)S(1)}, u32[]{:S(2)}, u32[]{:S(2)}) collective-permute-start(bf16[1024,256]{1,0:T(8,128)(2,1)} %get-tuple-element.204), channel_id=1, source_target_pairs={{0,2},{1,3},{6,4},{7,5},{8,10},{9,11},{14,12},{15,13},{16,18},{17,... | collective-permute-start | bytes 1572872 | tf_op jit(solution)/shard_map/ppermute | solution.py:191
  105.8 1.2 add_convert_fusion.14
  107.7 2.2 %broadcast_select_fusion.13 = bf16[1024,256]{1,0:T(8,128)(2,1)} fusion(bf16[1024,256]{1,0:T(8,128)(2,1)} %get-tuple-element.225, pred[]{:T(512)S(6)} %eq.31, bf16[1024,256]{1,0:T(8,128)(2,1)S(1)} %collective-permute-done.24, bf16[1024,256]{1,0:T(8,128)(2,1)S(1)} %add_convert_fusion.15), kind=kLoop, calls=%fused_computation.62 | loop fusion | flops 1310720 | bytes 2097153 | tf_op jit(solution)/shard_map/jit(_where)/select_n | solution.py:355
  110.8 1.0 collective-permute-start.29
  112.3 6.2 %collective-permute-done.32 = bf16[1024,256]{1,0:T(8,128)(2,1)S(1)} collective-permute-done((bf16[1024,256]{1,0:T(8,128)(2,1)}, bf16[1024,256]{1,0:T(8,128)(2,1)S(1)}, u32[]{:S(2)}, u32[]{:S(2)}) %collective-permute-start.32) | collective-permute-done | bytes 524320 | tf_op jit(solution)/shard_map/ppermute | solution.py:191
  120.0 1.0 collective-permute-start.36
  121.8 5.9 %partial_product.8 = (bf16[1024,256]{1,0:T(8,128)(2,1)}, bf16[1024,256]{1,0:T(8,128)(2,1)}) custom-call(s32[1]{0:T(128)} %bitcast.place, bf16[1024,256]{1,0:T(8,128)(2,1)} %get-tuple-element.149.refs_0_, bf16[1024,256]{1,0:T(8,128)(2,1)} %copy-done.1, bf16[1024,256]{1,0:T(8,128)(2,1)} %copy-done.2, bf16[1024,256]{1,0:T(8,128)(2,1)} %copy-done.4, ...), custom_call_target="tpu_custom_call" | custom-call | flops 2147483648 | bytes 7340032 | tf_op jit(solution)/shard_map/partial_product/pallas_call | solution.py:130
  127.8 1.3 broadcast_select_fusion.12
  129.1 2.9 %collective-permute-start.33 = (bf16[1024,256]{1,0:T(8,128)(2,1)S(1)}, bf16[1024,256]{1,0:T(8,128)(2,1)S(1)}, u32[]{:S(2)}, u32[]{:S(2)}) collective-permute-start(bf16[1024,256]{1,0:T(8,128)(2,1)S(1)} %broadcast_select_fusion.12), channel_id=1, source_target_pairs={{0,2},{1,3},{2,0},{3,1},{4,6},{5,7},{6,4},{7,5},{8,10},{9,11},{10,... | collective-permute-start | bytes 1572872 | tf_op jit(solution)/shard_map/ppermute | solution.py:191
  132.0 1.2 broadcast_select_fusion.11
  133.6 1.2 add_convert_fusion.10
  136.4 1.0 broadcast_select_fusion.10
  138.4 1.0 slice.175
  139.4 1.4 collective-permute-start.39
  141.6 1.6 collective-permute-start.37
  143.2 1.5 collective-permute-done.33
  148.4 5.9 %partial_product.9 = (bf16[1024,256]{1,0:T(8,128)(2,1)}, bf16[1024,256]{1,0:T(8,128)(2,1)}) custom-call(s32[1]{0:T(128)} %bitcast.place, bf16[1024,256]{1,0:T(8,128)(2,1)} %get-tuple-element.149.refs_0_, bf16[1024,256]{1,0:T(8,128)(2,1)} %copy-done.1, bf16[1024,256]{1,0:T(8,128)(2,1)} %copy-done.2, bf16[1024,256]{1,0:T(8,128)(2,1)} %copy-done.4, ...), custom_call_target="tpu_custom_call" | custom-call | flops 2147483648 | bytes 7340032 | tf_op jit(solution)/shard_map/partial_product/pallas_call | solution.py:130
  154.3 1.3 broadcast_select_fusion.8
  155.6 2.6 %collective-permute-start.41 = (bf16[1024,256]{1,0:T(8,128)(2,1)S(1)}, bf16[1024,256]{1,0:T(8,128)(2,1)S(1)}, u32[]{:S(2)}, u32[]{:S(2)}) collective-permute-start(bf16[1024,256]{1,0:T(8,128)(2,1)S(1)} %broadcast_select_fusion.8), channel_id=1, source_target_pairs={{0,2},{1,3},{2,0},{3,1},{4,6},{5,7},{6,4},{7,5},{8,10},{9,11},{10,... | collective-permute-start | bytes 1572872 | tf_op jit(solution)/shard_map/ppermute | solution.py:191
  158.2 1.2 add_convert_fusion.6
  160.2 1.7 broadcast_select_fusion.7
  162.4 1.5 collective-permute-start.43
  164.0 6.1 %collective-permute-done.41 = bf16[1024,256]{1,0:T(8,128)(2,1)S(1)} collective-permute-done((bf16[1024,256]{1,0:T(8,128)(2,1)S(1)}, bf16[1024,256]{1,0:T(8,128)(2,1)S(1)}, u32[]{:S(2)}, u32[]{:S(2)}) %collective-permute-start.41) | collective-permute-done | bytes 524320 | tf_op jit(solution)/shard_map/ppermute | solution.py:191
  171.7 1.3 collective-permute-start.45
  173.0 8.3 %collective-permute-done.43 = bf16[1024,256]{1,0:T(8,128)(2,1)S(1)} collective-permute-done((bf16[1024,256]{1,0:T(8,128)(2,1)S(1)}, bf16[1024,256]{1,0:T(8,128)(2,1)S(1)}, u32[]{:S(2)}, u32[]{:S(2)}) %collective-permute-start.43) | collective-permute-done | bytes 524320 | tf_op jit(solution)/shard_map/ppermute | solution.py:191
  183.0 1.3 collective-permute-start.47
  184.4 8.2 %collective-permute-done.45 = bf16[1024,256]{1,0:T(8,128)(2,1)S(1)} collective-permute-done((bf16[1024,256]{1,0:T(8,128)(2,1)S(1)}, bf16[1024,256]{1,0:T(8,128)(2,1)S(1)}, u32[]{:S(2)}, u32[]{:S(2)}) %collective-permute-start.45) | collective-permute-done | bytes 524320 | tf_op jit(solution)/shard_map/ppermute | solution.py:191
  193.0 1.3 collective-permute-start.49
  194.5 7.1 %collective-permute-done.47 = bf16[1024,256]{1,0:T(8,128)(2,1)S(1)} collective-permute-done((bf16[1024,256]{1,0:T(8,128)(2,1)S(1)}, bf16[1024,256]{1,0:T(8,128)(2,1)S(1)}, u32[]{:S(2)}, u32[]{:S(2)}) %collective-permute-start.47) | collective-permute-done | bytes 524320 | tf_op jit(solution)/shard_map/ppermute | solution.py:191
  201.9 5.2 %collective-permute-done.49 = bf16[1024,256]{1,0:T(8,128)(2,1)S(1)} collective-permute-done((bf16[1024,256]{1,0:T(8,128)(2,1)S(1)}, bf16[1024,256]{1,0:T(8,128)(2,1)S(1)}, u32[]{:S(2)}, u32[]{:S(2)}) %collective-permute-start.49) | collective-permute-done | bytes 524320 | tf_op jit(solution)/shard_map/ppermute | solution.py:191
  208.1 1.4 collective-permute-done.51
  209.8 2.2 %broadcast_select_fusion = bf16[1,448,4096]{2,1,0:T(8,128)(2,1)} fusion(bf16[1,448,4096]{2,1,0:T(8,128)(2,1)S(1)} %get-tuple-element.279, bf16[1,448,4096]{2,1,0:T(8,128)(2,1)S(1)} %constant_dynamic-update-slice_fusion.14, pred[]{:T(512)S(6)} %eq.30), kind=kLoop, calls=%fused_computation | loop fusion | flops 1835008 | bytes 11010049 | tf_op jit(solution)/shard_map/jit(_where)/select_n | solution.py:366
  (258 shorter events, 35.0 us)
Async XLA Ops:
  1.0 1.5 collective-permute-start
  2.5 17.3 %copy-start.20 = (bf16[512,256]{1,0:T(8,128)(2,1)}, bf16[512,256]{1,0:T(8,128)(2,1)S(1)}, u32[]{:S(2)}) copy-start(bf16[512,256]{1,0:T(8,128)(2,1)S(1)} %pad_maximum_fusion.4.refs_8_) | copy-start | bytes 786436
  2.5 17.3 %collective-permute-start.3 = (bf16[512,256]{1,0:T(8,128)(2,1)S(1)}, bf16[512,256]{1,0:T(8,128)(2,1)S(1)}, u32[]{:S(2)}, u32[]{:S(2)}) collective-permute-start(bf16[512,256]{1,0:T(8,128)(2,1)S(1)} %pad_maximum_fusion.4.refs_8_), channel_id=1, source_target_pairs={{0,24},{8,16},{16,8},{24,0},{1,25},{9,17},{17,9},{25,1},{2,26},{10... | collective-permute-start | bytes 786440 | tf_op jit(solution)/shard_map/ppermute | solution.py:181
  6.4 13.5 %collective-permute-start.2 = (bf16[512,256]{1,0:T(8,128)(2,1)S(1)}, bf16[512,256]{1,0:T(8,128)(2,1)S(1)}, u32[]{:S(2)}, u32[]{:S(2)}) collective-permute-start(bf16[512,256]{1,0:T(8,128)(2,1)S(1)} %pad_maximum_fusion.4.refs_8_), channel_id=1, source_target_pairs={{0,16},{8,24},{16,0},{24,8},{1,17},{9,25},{17,1},{25,9},{2,18},{10... | collective-permute-start | bytes 786440 | tf_op jit(solution)/shard_map/ppermute | solution.py:181
  6.9 13.0 %collective-permute-start.1 = (bf16[512,256]{1,0:T(8,128)(2,1)S(1)}, bf16[512,256]{1,0:T(8,128)(2,1)S(1)}, u32[]{:S(2)}, u32[]{:S(2)}) collective-permute-start(bf16[512,256]{1,0:T(8,128)(2,1)S(1)} %pad_maximum_fusion.4.refs_8_), channel_id=1, source_target_pairs={{0,8},{8,0},{16,24},{24,16},{1,9},{9,1},{17,25},{25,17},{2,10},{10... | collective-permute-start | bytes 786440 | tf_op jit(solution)/shard_map/ppermute | solution.py:181
  7.0 17.3 %copy-start.41 = (s32[128,2]{0,1:T(2,128)S(1)}, s32[128,2]{0,1:T(2,128)}, u32[]{:S(2)}) copy-start(s32[128,2]{0,1:T(2,128)} %param.20) | copy-start | bytes 3076
  7.0 17.3 %copy-start.42 = (f32[128,2]{0,1:T(2,128)S(1)}, f32[128,2]{0,1:T(2,128)}, u32[]{:S(2)}) copy-start(f32[128,2]{0,1:T(2,128)} %param.21) | copy-start | bytes 3076
  7.0 20.0 %copy-start.23 = (bf16[128,4096]{1,0:T(8,128)(2,1)S(1)}, bf16[128,4096]{1,0:T(8,128)(2,1)}, u32[]{:S(2)}) copy-start(bf16[128,4096]{1,0:T(8,128)(2,1)} %param.19) | copy-start | bytes 3145732
  19.9 18.0 %copy-start.31 = (bf16[512,256]{1,0:T(8,128)(2,1)}, bf16[512,256]{1,0:T(8,128)(2,1)S(1)}, u32[]{:S(2)}) copy-start(bf16[512,256]{1,0:T(8,128)(2,1)S(1)} %collective-permute-done.3.refs_11_) | copy-start | bytes 786436
  19.9 4.4 %collective-permute-start.4 = (bf16[1024,256]{1,0:T(8,128)(2,1)}, bf16[1024,256]{1,0:T(8,128)(2,1)S(1)}, u32[]{:S(2)}, u32[]{:S(2)}) collective-permute-start(bf16[1024,256]{1,0:T(8,128)(2,1)} %get-tuple-element.149.refs_0_), channel_id=1, source_target_pairs={{0,1},{1,0},{2,3},{3,2},{4,5},{5,4},{6,7},{7,6},{8,9},{9,8},{10,11... | collective-permute-start | bytes 1572872 | tf_op jit(solution)/shard_map/ppermute | solution.py:178
  20.8 26.2 %collective-permute-start.5 = (bf16[1024,256]{1,0:T(8,128)(2,1)}, bf16[1024,256]{1,0:T(8,128)(2,1)S(1)}, u32[]{:S(2)}, u32[]{:S(2)}) collective-permute-start(bf16[1024,256]{1,0:T(8,128)(2,1)} %get-tuple-element.139), channel_id=1, source_target_pairs={{0,8},{8,0},{16,24},{24,16},{1,9},{9,1},{17,25},{25,17},{2,10},{10... | collective-permute-start | bytes 1572872 | tf_op jit(solution)/shard_map/ppermute | solution.py:181
  22.7 30.4 %collective-permute-start.6 = (bf16[1024,256]{1,0:T(8,128)(2,1)}, bf16[1024,256]{1,0:T(8,128)(2,1)S(1)}, u32[]{:S(2)}, u32[]{:S(2)}) collective-permute-start(bf16[1024,256]{1,0:T(8,128)(2,1)} %get-tuple-element.140), channel_id=1, source_target_pairs={{0,16},{8,24},{16,0},{24,8},{1,17},{9,25},{17,1},{25,9},{2,18},{10... | collective-permute-start | bytes 1572872 | tf_op jit(solution)/shard_map/ppermute | solution.py:181
  24.2 28.9 %collective-permute-start.7 = (bf16[1024,256]{1,0:T(8,128)(2,1)}, bf16[1024,256]{1,0:T(8,128)(2,1)}, u32[]{:S(2)}, u32[]{:S(2)}) collective-permute-start(bf16[1024,256]{1,0:T(8,128)(2,1)} %get-tuple-element.141), channel_id=1, source_target_pairs={{0,24},{8,16},{16,8},{24,0},{1,25},{9,17},{17,9},{25,1},{2,26},{10... | collective-permute-start | bytes 1572872 | tf_op jit(solution)/shard_map/ppermute | solution.py:181
  24.3 17.6 %copy-start.1 = (bf16[1024,256]{1,0:T(8,128)(2,1)}, bf16[1024,256]{1,0:T(8,128)(2,1)S(1)}, u32[]{:S(2)}) copy-start(bf16[1024,256]{1,0:T(8,128)(2,1)S(1)} %collective-permute-done.4.refs_1_) | copy-start | bytes 1572868
  24.4 3.8 %collective-permute-start.13 = (f32[1,4,128]{2,1,0:T(4,128)S(1)}, f32[1,4,128]{2,1,0:T(4,128)S(1)}, u32[]{:S(2)}, u32[]{:S(2)}) collective-permute-start(f32[1,4,128]{2,1,0:T(4,128)S(1)} %maximum_bitcast_fusion), channel_id=1, source_target_pairs={{0,1},{1,0},{2,3},{3,2},{4,5},{5,4},{6,7},{7,6},{8,9},{9,8},{10,11... | collective-permute-start | bytes 6152 | tf_op jit(solution)/shard_map/ppermute | solution.py:233
  26.7 15.2 %collective-permute-start.8 = (bf16[256,1792]{1,0:T(8,128)(2,1)}, bf16[256,1792]{1,0:T(8,128)(2,1)}, u32[]{:S(2)}, u32[]{:S(2)}) collective-permute-start(bf16[256,1792]{1,0:T(8,128)(2,1)} %constant_dynamic-slice_fusion.5), channel_id=1, source_target_pairs={{0,1},{1,0},{2,3},{3,2},{4,5},{5,4},{6,7},{7,6},{8,9},{9,8},{10,11... | collective-permute-start | bytes 2752520 | tf_op jit(solution)/shard_map/ppermute | solution.py:178
  28.2 4.1 %collective-permute-start.14 = (f32[2,4,128]{2,1,0:T(4,128)S(1)}, f32[2,4,128]{2,1,0:T(4,128)S(1)}, u32[]{:S(2)}, u32[]{:S(2)}) collective-permute-start(f32[2,4,128]{2,1,0:T(4,128)S(1)} %pad_maximum_fusion.8), channel_id=1, source_target_pairs={{0,2},{1,3},{2,0},{3,1},{4,6},{5,7},{6,4},{7,5},{8,10},{9,11},{10,... | collective-permute-start | bytes 12296 | tf_op jit(solution)/shard_map/ppermute | solution.py:233
  32.3 4.6 %collective-permute-start.15 = (f32[4,4,128]{2,1,0:T(4,128)S(1)}, f32[4,4,128]{2,1,0:T(4,128)S(1)}, u32[]{:S(2)}, u32[]{:S(2)}) collective-permute-start(f32[4,4,128]{2,1,0:T(4,128)S(1)} %pad_maximum_fusion.7), channel_id=1, source_target_pairs={{0,4},{1,5},{2,6},{3,7},{4,0},{5,1},{6,2},{7,3},{8,12},{9,13},{10,... | collective-permute-start | bytes 24584 | tf_op jit(solution)/shard_map/ppermute | solution.py:233
  36.9 2.1 %collective-permute-start.12 = (bf16[128,2048]{1,0:T(8,128)(2,1)}, bf16[128,2048]{1,0:T(8,128)(2,1)S(1)}, u32[]{:S(2)}, u32[]{:S(2)}) collective-permute-start(bf16[128,2048]{1,0:T(8,128)(2,1)} %get-tuple-element.274), channel_id=1, source_target_pairs={{0,1},{1,0},{2,3},{3,2},{4,5},{5,4},{6,7},{7,6},{8,9},{9,8},{10,11... | collective-permute-start | bytes 1572872 | tf_op jit(solution)/shard_map/ppermute | solution.py:178
  42.8 26.2 %copy-start.21 = (bf16[512,256]{1,0:T(8,128)(2,1)}, bf16[512,256]{1,0:T(8,128)(2,1)S(1)}, u32[]{:S(2)}) copy-start(bf16[512,256]{1,0:T(8,128)(2,1)S(1)} %pad_maximum_fusion.5.refs_8_) | copy-start | bytes 786436
  42.9 10.8 %collective-permute-start.11 = (bf16[512,256]{1,0:T(8,128)(2,1)S(1)}, bf16[512,256]{1,0:T(8,128)(2,1)S(1)}, u32[]{:S(2)}, u32[]{:S(2)}) collective-permute-start(bf16[512,256]{1,0:T(8,128)(2,1)S(1)} %pad_maximum_fusion.5.refs_8_), channel_id=1, source_target_pairs={{0,24},{8,16},{16,8},{24,0},{1,25},{9,17},{17,9},{25,1},{2,26},{10... | collective-permute-start | bytes 786440 | tf_op jit(solution)/shard_map/ppermute | solution.py:181
  45.4 13.5 %collective-permute-start.10 = (bf16[512,256]{1,0:T(8,128)(2,1)S(1)}, bf16[512,256]{1,0:T(8,128)(2,1)S(1)}, u32[]{:S(2)}, u32[]{:S(2)}) collective-permute-start(bf16[512,256]{1,0:T(8,128)(2,1)S(1)} %pad_maximum_fusion.5.refs_8_), channel_id=1, source_target_pairs={{0,16},{8,24},{16,0},{24,8},{1,17},{9,25},{17,1},{25,9},{2,18},{10... | collective-permute-start | bytes 786440 | tf_op jit(solution)/shard_map/ppermute | solution.py:181
  47.1 17.7 %copy-start.2 = (bf16[1024,256]{1,0:T(8,128)(2,1)}, bf16[1024,256]{1,0:T(8,128)(2,1)S(1)}, u32[]{:S(2)}) copy-start(bf16[1024,256]{1,0:T(8,128)(2,1)S(1)} %collective-permute-done.5.refs_2_) | copy-start | bytes 1572868
  47.1 11.8 %collective-permute-start.9 = (bf16[512,256]{1,0:T(8,128)(2,1)S(1)}, bf16[512,256]{1,0:T(8,128)(2,1)S(1)}, u32[]{:S(2)}, u32[]{:S(2)}) collective-permute-start(bf16[512,256]{1,0:T(8,128)(2,1)S(1)} %pad_maximum_fusion.5.refs_8_), channel_id=1, source_target_pairs={{0,8},{8,0},{16,24},{24,16},{1,9},{9,1},{17,25},{25,17},{2,10},{10... | collective-permute-start | bytes 786440 | tf_op jit(solution)/shard_map/ppermute | solution.py:181
  58.9 2.0 collective-permute-start.16
  59.6 2.1 %collective-permute-start.17 = (bf16[1024,256]{1,0:T(8,128)(2,1)S(1)}, bf16[1024,256]{1,0:T(8,128)(2,1)}, u32[]{:S(2)}, u32[]{:S(2)}) collective-permute-start(bf16[1024,256]{1,0:T(8,128)(2,1)S(1)} %collective-permute-done.6.refs_4_), channel_id=1, source_target_pairs={{0,1},{1,0},{2,3},{3,2},{4,5},{5,4},{6,7},{7,6},{8,9},{9,8},{10,11... | collective-permute-start | bytes 1572872 | tf_op jit(solution)/shard_map/ppermute | solution.py:178
  59.7 3.0 %collective-permute-start.18 = (bf16[1024,256]{1,0:T(8,128)(2,1)}, bf16[1024,256]{1,0:T(8,128)(2,1)}, u32[]{:S(2)}, u32[]{:S(2)}) collective-permute-start(bf16[1024,256]{1,0:T(8,128)(2,1)} %collective-permute-done.7.refs_6_), channel_id=1, source_target_pairs={{0,1},{1,0},{2,3},{3,2},{4,5},{5,4},{6,7},{7,6},{8,9},{9,8},{10,11... | collective-permute-start | bytes 1572872 | tf_op jit(solution)/shard_map/ppermute | solution.py:178
  62.7 16.5 %collective-permute-start.20 = (bf16[512,512]{1,0:T(8,128)(2,1)}, bf16[512,512]{1,0:T(8,128)(2,1)}, u32[]{:S(2)}, u32[]{:S(2)}) collective-permute-start(bf16[512,512]{1,0:T(8,128)(2,1)} %get-tuple-element.188.refs_8_), channel_id=1, source_target_pairs={{0,16},{8,24},{16,0},{24,8},{1,17},{9,25},{17,1},{25,9},{2,18},{10... | collective-permute-start | bytes 1572872 | tf_op jit(solution)/shard_map/ppermute | solution.py:181
  64.2 15.9 %collective-permute-start.19 = (bf16[512,512]{1,0:T(8,128)(2,1)}, bf16[512,512]{1,0:T(8,128)(2,1)}, u32[]{:S(2)}, u32[]{:S(2)}) collective-permute-start(bf16[512,512]{1,0:T(8,128)(2,1)} %get-tuple-element.188.refs_8_), channel_id=1, source_target_pairs={{0,8},{8,0},{16,24},{24,16},{1,9},{9,1},{17,25},{25,17},{2,10},{10... | collective-permute-start | bytes 1572872 | tf_op jit(solution)/shard_map/ppermute | solution.py:181
  69.1 18.4 %copy-start.15 = (bf16[1024,256]{1,0:T(8,128)(2,1)S(1)}, bf16[1024,256]{1,0:T(8,128)(2,1)}, u32[]{:S(2)}) copy-start(bf16[1024,256]{1,0:T(8,128)(2,1)} %partial_product.5) | copy-start | bytes 1572868
  69.1 16.3 %collective-permute-start.23 = (bf16[1024,256]{1,0:T(8,128)(2,1)}, bf16[1024,256]{1,0:T(8,128)(2,1)S(1)}, u32[]{:S(2)}, u32[]{:S(2)}) collective-permute-start(bf16[1024,256]{1,0:T(8,128)(2,1)} %partial_product.5), channel_id=1, source_target_pairs={{0,2},{1,3},{6,4},{7,5},{8,10},{9,11},{14,12},{15,13},{16,18},{17,... | collective-permute-start | bytes 1572872 | tf_op jit(solution)/shard_map/ppermute | solution.py:191
  77.0 28.8 %collective-permute-start.25 = (bf16[1024,256]{1,0:T(8,128)(2,1)}, bf16[1024,256]{1,0:T(8,128)(2,1)}, u32[]{:S(2)}, u32[]{:S(2)}) collective-permute-start(bf16[1024,256]{1,0:T(8,128)(2,1)} %partial_product.6), channel_id=1, source_target_pairs={{0,2},{1,3},{6,4},{7,5},{8,10},{9,11},{14,12},{15,13},{16,18},{17,... | collective-permute-start | bytes 1572872 | tf_op jit(solution)/shard_map/ppermute | solution.py:191
  81.1 11.5 %collective-permute-start.21 = (bf16[256,512]{1,0:T(8,128)(2,1)S(1)}, bf16[256,512]{1,0:T(8,128)(2,1)S(1)}, u32[]{:S(2)}, u32[]{:S(2)}) collective-permute-start(bf16[256,512]{1,0:T(8,128)(2,1)S(1)} %slice.170), channel_id=1, source_target_pairs={{0,8},{8,0},{16,24},{24,16},{1,9},{9,1},{17,25},{25,17},{2,10},{10... | collective-permute-start | bytes 786440 | tf_op jit(solution)/shard_map/ppermute | solution.py:181
  86.2 6.4 %collective-permute-start.22 = (bf16[256,512]{1,0:T(8,128)(2,1)S(1)}, bf16[256,512]{1,0:T(8,128)(2,1)S(1)}, u32[]{:S(2)}, u32[]{:S(2)}) collective-permute-start(bf16[256,512]{1,0:T(8,128)(2,1)S(1)} %slice.171), channel_id=1, source_target_pairs={{0,16},{8,24},{16,0},{24,8},{1,17},{9,25},{17,1},{25,9},{2,18},{10... | collective-permute-start | bytes 786440 | tf_op jit(solution)/shard_map/ppermute | solution.py:181
  88.6 19.1 %collective-permute-start.24 = (bf16[1024,256]{1,0:T(8,128)(2,1)S(1)}, bf16[1024,256]{1,0:T(8,128)(2,1)S(1)}, u32[]{:S(2)}, u32[]{:S(2)}) collective-permute-start(bf16[1024,256]{1,0:T(8,128)(2,1)S(1)} %add_convert_fusion.15), channel_id=1, source_target_pairs={{2,4},{3,5},{4,2},{5,3},{10,12},{11,13},{12,10},{13,11},{18,20},{1... | collective-permute-start | bytes 1572872 | tf_op jit(solution)/shard_map/ppermute | solution.py:191
  92.6 17.3 %collective-permute-start.27 = (bf16[512,512]{1,0:T(8,128)(2,1)}, bf16[512,512]{1,0:T(8,128)(2,1)S(1)}, u32[]{:S(2)}, u32[]{:S(2)}) collective-permute-start(bf16[512,512]{1,0:T(8,128)(2,1)} %get-tuple-element.213.refs_8_), channel_id=1, source_target_pairs={{0,8},{8,0},{16,24},{24,16},{1,9},{9,1},{17,25},{25,17},{2,10},{10... | collective-permute-start | bytes 1572872 | tf_op jit(solution)/shard_map/ppermute | solution.py:181
  94.7 15.2 %collective-permute-start.26 = (bf16[512,512]{1,0:T(8,128)(2,1)}, bf16[512,512]{1,0:T(8,128)(2,1)S(1)}, u32[]{:S(2)}, u32[]{:S(2)}) collective-permute-start(bf16[512,512]{1,0:T(8,128)(2,1)} %get-tuple-element.213.refs_8_), channel_id=1, source_target_pairs={{0,16},{8,24},{16,0},{24,8},{1,17},{9,25},{17,1},{25,9},{2,18},{10... | collective-permute-start | bytes 1572872 | tf_op jit(solution)/shard_map/ppermute | solution.py:181
  100.7 17.8 %copy-start.27 = (bf16[1024,256]{1,0:T(8,128)(2,1)S(1)}, bf16[1024,256]{1,0:T(8,128)(2,1)}, u32[]{:S(2)}) copy-start(bf16[1024,256]{1,0:T(8,128)(2,1)} %get-tuple-element.204) | copy-start | bytes 1572868
  100.7 17.8 %collective-permute-start.32 = (bf16[1024,256]{1,0:T(8,128)(2,1)}, bf16[1024,256]{1,0:T(8,128)(2,1)S(1)}, u32[]{:S(2)}, u32[]{:S(2)}) collective-permute-start(bf16[1024,256]{1,0:T(8,128)(2,1)} %get-tuple-element.204), channel_id=1, source_target_pairs={{0,2},{1,3},{6,4},{7,5},{8,10},{9,11},{14,12},{15,13},{16,18},{17,... | collective-permute-start | bytes 1572872 | tf_op jit(solution)/shard_map/ppermute | solution.py:191
  107.0 12.3 %collective-permute-start.31 = (bf16[1024,256]{1,0:T(8,128)(2,1)S(1)}, bf16[1024,256]{1,0:T(8,128)(2,1)S(1)}, u32[]{:S(2)}, u32[]{:S(2)}) collective-permute-start(bf16[1024,256]{1,0:T(8,128)(2,1)S(1)} %add_convert_fusion.14), channel_id=1, source_target_pairs={{2,4},{3,5},{4,2},{5,3},{10,12},{11,13},{12,10},{13,11},{18,20},{1... | collective-permute-start | bytes 1572872 | tf_op jit(solution)/shard_map/ppermute | solution.py:191
  109.9 11.9 %copy-start.37 = (bf16[512,512]{1,0:T(8,128)(2,1)}, bf16[512,512]{1,0:T(8,128)(2,1)S(1)}, u32[]{:S(2)}) copy-start(bf16[512,512]{1,0:T(8,128)(2,1)S(1)} %collective-permute-done.27.refs_9_) | copy-start | bytes 1572868
  110.0 11.8 %copy-start.38 = (bf16[512,512]{1,0:T(8,128)(2,1)}, bf16[512,512]{1,0:T(8,128)(2,1)S(1)}, u32[]{:S(2)}) copy-start(bf16[512,512]{1,0:T(8,128)(2,1)S(1)} %collective-permute-done.26.refs_10_) | copy-start | bytes 1572868
  110.0 9.3 %collective-permute-start.30 = (bf16[256,512]{1,0:T(8,128)(2,1)S(1)}, bf16[256,512]{1,0:T(8,128)(2,1)S(1)}, u32[]{:S(2)}, u32[]{:S(2)}) collective-permute-start(bf16[256,512]{1,0:T(8,128)(2,1)S(1)} %slice.173), channel_id=1, source_target_pairs={{0,16},{8,24},{16,0},{24,8},{1,17},{9,25},{17,1},{25,9},{2,18},{10... | collective-permute-start | bytes 786440 | tf_op jit(solution)/shard_map/ppermute | solution.py:181
  110.8 9.2 %collective-permute-start.29 = (bf16[256,512]{1,0:T(8,128)(2,1)S(1)}, bf16[256,512]{1,0:T(8,128)(2,1)S(1)}, u32[]{:S(2)}, u32[]{:S(2)}) collective-permute-start(bf16[256,512]{1,0:T(8,128)(2,1)S(1)} %slice.172), channel_id=1, source_target_pairs={{0,8},{8,0},{16,24},{24,16},{1,9},{9,1},{17,25},{25,17},{2,10},{10... | collective-permute-start | bytes 786440 | tf_op jit(solution)/shard_map/ppermute | solution.py:181
  111.8 20.2 %collective-permute-start.28 = (bf16[1024,256]{1,0:T(8,128)(2,1)}, bf16[1024,256]{1,0:T(8,128)(2,1)}, u32[]{:S(2)}, u32[]{:S(2)}) collective-permute-start(bf16[1024,256]{1,0:T(8,128)(2,1)} %broadcast_select_fusion.13), channel_id=1, source_target_pairs={{0,2},{1,3},{2,0},{3,1},{4,6},{5,7},{6,4},{7,5},{8,10},{9,11},{10,... | collective-permute-start | bytes 1572872 | tf_op jit(solution)/shard_map/ppermute | solution.py:191
  118.6 17.0 %collective-permute-start.34 = (bf16[1024,256]{1,0:T(8,128)(2,1)S(1)}, bf16[1024,256]{1,0:T(8,128)(2,1)S(1)}, u32[]{:S(2)}, u32[]{:S(2)}) collective-permute-start(bf16[1024,256]{1,0:T(8,128)(2,1)S(1)} %add_convert_fusion.12), channel_id=1, source_target_pairs={{2,4},{3,5},{4,2},{5,3},{10,12},{11,13},{12,10},{13,11},{18,20},{1... | collective-permute-start | bytes 1572872 | tf_op jit(solution)/shard_map/ppermute | solution.py:191
  120.0 17.4 %collective-permute-start.36 = (bf16[512,512]{1,0:T(8,128)(2,1)}, bf16[512,512]{1,0:T(8,128)(2,1)}, u32[]{:S(2)}, u32[]{:S(2)}) collective-permute-start(bf16[512,512]{1,0:T(8,128)(2,1)} %pad_maximum_fusion.2.refs_8_), channel_id=1, source_target_pairs={{0,8},{8,0},{16,24},{24,16},{1,9},{9,1},{17,25},{25,17},{2,10},{10... | collective-permute-start | bytes 1572872 | tf_op jit(solution)/shard_map/ppermute | solution.py:181
  121.0 17.4 %collective-permute-start.35 = (bf16[512,512]{1,0:T(8,128)(2,1)}, bf16[512,512]{1,0:T(8,128)(2,1)}, u32[]{:S(2)}, u32[]{:S(2)}) collective-permute-start(bf16[512,512]{1,0:T(8,128)(2,1)} %pad_maximum_fusion.2.refs_8_), channel_id=1, source_target_pairs={{0,16},{8,24},{16,0},{24,8},{1,17},{9,25},{17,1},{25,9},{2,18},{10... | collective-permute-start | bytes 1572872 | tf_op jit(solution)/shard_map/ppermute | solution.py:181
  129.1 15.5 %collective-permute-start.33 = (bf16[1024,256]{1,0:T(8,128)(2,1)S(1)}, bf16[1024,256]{1,0:T(8,128)(2,1)S(1)}, u32[]{:S(2)}, u32[]{:S(2)}) collective-permute-start(bf16[1024,256]{1,0:T(8,128)(2,1)S(1)} %broadcast_select_fusion.12), channel_id=1, source_target_pairs={{0,2},{1,3},{2,0},{3,1},{4,6},{5,7},{6,4},{7,5},{8,10},{9,11},{10,... | collective-permute-start | bytes 1572872 | tf_op jit(solution)/shard_map/ppermute | solution.py:191
  134.8 12.2 %collective-permute-start.40 = (bf16[1024,256]{1,0:T(8,128)(2,1)S(1)}, bf16[1024,256]{1,0:T(8,128)(2,1)S(1)}, u32[]{:S(2)}, u32[]{:S(2)}) collective-permute-start(bf16[1024,256]{1,0:T(8,128)(2,1)S(1)} %add_convert_fusion.10), channel_id=1, source_target_pairs={{2,4},{3,5},{4,2},{5,3},{10,12},{11,13},{12,10},{13,11},{18,20},{1... | collective-permute-start | bytes 1572872 | tf_op jit(solution)/shard_map/ppermute | solution.py:191
  139.4 7.6 %collective-permute-start.39 = (bf16[256,512]{1,0:T(8,128)(2,1)S(1)}, bf16[256,512]{1,0:T(8,128)(2,1)S(1)}, u32[]{:S(2)}, u32[]{:S(2)}) collective-permute-start(bf16[256,512]{1,0:T(8,128)(2,1)S(1)} %slice.176), channel_id=1, source_target_pairs={{0,16},{8,24},{16,0},{24,8},{1,17},{9,25},{17,1},{25,9},{2,18},{10... | collective-permute-start | bytes 786440 | tf_op jit(solution)/shard_map/ppermute | solution.py:181
  140.8 6.4 %collective-permute-start.38 = (bf16[256,512]{1,0:T(8,128)(2,1)S(1)}, bf16[256,512]{1,0:T(8,128)(2,1)S(1)}, u32[]{:S(2)}, u32[]{:S(2)}) collective-permute-start(bf16[256,512]{1,0:T(8,128)(2,1)S(1)} %slice.175), channel_id=1, source_target_pairs={{0,8},{8,0},{16,24},{24,16},{1,9},{9,1},{17,25},{25,17},{2,10},{10... | collective-permute-start | bytes 786440 | tf_op jit(solution)/shard_map/ppermute | solution.py:181
  141.6 16.6 %collective-permute-start.37 = (bf16[1024,256]{1,0:T(8,128)(2,1)}, bf16[1024,256]{1,0:T(8,128)(2,1)}, u32[]{:S(2)}, u32[]{:S(2)}) collective-permute-start(bf16[1024,256]{1,0:T(8,128)(2,1)} %broadcast_select_fusion.10), channel_id=1, source_target_pairs={{0,2},{1,3},{2,0},{3,1},{4,6},{5,7},{6,4},{7,5},{8,10},{9,11},{10,... | collective-permute-start | bytes 1572872 | tf_op jit(solution)/shard_map/ppermute | solution.py:191
  145.3 16.5 %collective-permute-start.42 = (bf16[1024,256]{1,0:T(8,128)(2,1)S(1)}, bf16[1024,256]{1,0:T(8,128)(2,1)S(1)}, u32[]{:S(2)}, u32[]{:S(2)}) collective-permute-start(bf16[1024,256]{1,0:T(8,128)(2,1)S(1)} %add_convert_fusion.8), channel_id=1, source_target_pairs={{2,4},{3,5},{4,2},{5,3},{10,12},{11,13},{12,10},{13,11},{18,20},{1... | collective-permute-start | bytes 1572872 | tf_op jit(solution)/shard_map/ppermute | solution.py:191
  155.6 14.6 %collective-permute-start.41 = (bf16[1024,256]{1,0:T(8,128)(2,1)S(1)}, bf16[1024,256]{1,0:T(8,128)(2,1)S(1)}, u32[]{:S(2)}, u32[]{:S(2)}) collective-permute-start(bf16[1024,256]{1,0:T(8,128)(2,1)S(1)} %broadcast_select_fusion.8), channel_id=1, source_target_pairs={{0,2},{1,3},{2,0},{3,1},{4,6},{5,7},{6,4},{7,5},{8,10},{9,11},{10,... | collective-permute-start | bytes 1572872 | tf_op jit(solution)/shard_map/ppermute | solution.py:191
  159.4 12.2 %collective-permute-start.44 = (bf16[1024,256]{1,0:T(8,128)(2,1)S(1)}, bf16[1024,256]{1,0:T(8,128)(2,1)S(1)}, u32[]{:S(2)}, u32[]{:S(2)}) collective-permute-start(bf16[1024,256]{1,0:T(8,128)(2,1)S(1)} %add_convert_fusion.6), channel_id=1, source_target_pairs={{2,4},{3,5},{4,2},{5,3},{10,12},{11,13},{12,10},{13,11},{18,20},{1... | collective-permute-start | bytes 1572872 | tf_op jit(solution)/shard_map/ppermute | solution.py:191
  162.4 19.0 %collective-permute-start.43 = (bf16[1024,256]{1,0:T(8,128)(2,1)S(1)}, bf16[1024,256]{1,0:T(8,128)(2,1)S(1)}, u32[]{:S(2)}, u32[]{:S(2)}) collective-permute-start(bf16[1024,256]{1,0:T(8,128)(2,1)S(1)} %broadcast_select_fusion.6), channel_id=1, source_target_pairs={{0,2},{1,3},{2,0},{3,1},{4,6},{5,7},{6,4},{7,5},{8,10},{9,11},{10,... | collective-permute-start | bytes 1572872 | tf_op jit(solution)/shard_map/ppermute | solution.py:191
  170.8 12.0 %collective-permute-start.46 = (bf16[1024,256]{1,0:T(8,128)(2,1)S(1)}, bf16[1024,256]{1,0:T(8,128)(2,1)S(1)}, u32[]{:S(2)}, u32[]{:S(2)}) collective-permute-start(bf16[1024,256]{1,0:T(8,128)(2,1)S(1)} %add_convert_fusion.4), channel_id=1, source_target_pairs={{2,4},{3,5},{4,2},{5,3},{10,12},{11,13},{12,10},{13,11},{18,20},{1... | collective-permute-start | bytes 1572872 | tf_op jit(solution)/shard_map/ppermute | solution.py:191
  171.7 20.9 %collective-permute-start.45 = (bf16[1024,256]{1,0:T(8,128)(2,1)S(1)}, bf16[1024,256]{1,0:T(8,128)(2,1)S(1)}, u32[]{:S(2)}, u32[]{:S(2)}) collective-permute-start(bf16[1024,256]{1,0:T(8,128)(2,1)S(1)} %add_convert_fusion.3), channel_id=1, source_target_pairs={{2,0},{3,1},{4,6},{5,7},{10,8},{11,9},{12,14},{13,15},{18,16},{19,... | collective-permute-start | bytes 1572872 | tf_op jit(solution)/shard_map/ppermute | solution.py:191
  182.0 2.2 %collective-permute-start.48 = (bf16[1024,256]{1,0:T(8,128)(2,1)S(1)}, bf16[1024,256]{1,0:T(8,128)(2,1)S(1)}, u32[]{:S(2)}, u32[]{:S(2)}) collective-permute-start(bf16[1024,256]{1,0:T(8,128)(2,1)S(1)} %add_convert_fusion.2), channel_id=1, source_target_pairs={{2,4},{3,5},{4,2},{5,3},{10,12},{11,13},{12,10},{13,11},{18,20},{1... | collective-permute-start | bytes 1572872 | tf_op jit(solution)/shard_map/ppermute | solution.py:191
  183.0 18.5 %collective-permute-start.47 = (bf16[1024,256]{1,0:T(8,128)(2,1)S(1)}, bf16[1024,256]{1,0:T(8,128)(2,1)S(1)}, u32[]{:S(2)}, u32[]{:S(2)}) collective-permute-start(bf16[1024,256]{1,0:T(8,128)(2,1)S(1)} %add_convert_fusion.1), channel_id=1, source_target_pairs={{2,0},{3,1},{4,6},{5,7},{10,8},{11,9},{12,14},{13,15},{18,16},{19,... | collective-permute-start | bytes 1572872 | tf_op jit(solution)/shard_map/ppermute | solution.py:191
  193.0 14.1 %collective-permute-start.49 = (bf16[1024,256]{1,0:T(8,128)(2,1)S(1)}, bf16[1024,256]{1,0:T(8,128)(2,1)S(1)}, u32[]{:S(2)}, u32[]{:S(2)}) collective-permute-start(bf16[1024,256]{1,0:T(8,128)(2,1)S(1)} %add_convert_fusion), channel_id=1, source_target_pairs={{2,0},{3,1},{4,6},{5,7},{10,8},{11,9},{12,14},{13,15},{18,16},{19,... | collective-permute-start | bytes 1572872 | tf_op jit(solution)/shard_map/ppermute | solution.py:191
  194.3 13.3 %collective-permute-start.50 = (bf16[448,1536]{1,0:T(8,128)(2,1)S(1)}, bf16[448,1536]{1,0:T(8,128)(2,1)S(1)}, u32[]{:S(2)}, u32[]{:S(2)}) collective-permute-start(bf16[448,1536]{1,0:T(8,128)(2,1)S(1)} %constant_dynamic-update-slice_fusion), channel_id=1, source_target_pairs={{0,1},{1,0},{2,3},{3,2},{4,5},{5,4},{6,7},{7,6},{8,9},{9,8},{10,11... | collective-permute-start | bytes 4128776 | tf_op jit(solution)/shard_map/ppermute | solution.py:178
  207.6 1.9 collective-permute-start.51
  (37 other events, 182.0 us)

commit v10 on v9

--- a/solution.py
+++ b/solution.py
@@ -8,9 +8,9 @@
 from jax.sharding import PartitionSpec as P
 
 EXP_DEV = 1
-GROUPS = ((1,), (1,), (1, 1), (1, 1), (1, 1))
-FIRST_PHASE = {2: 3, 4: 4}
-SECOND_PHASE = {3: 3, 5: 4}
+GROUPS = ((1, 1), (1, 1), (1, 1), (1, 1))
+FIRST_PHASE = {2: 2, 4: 3}
+SECOND_PHASE = {3: 2, 5: 3}
 UNITS = sum(map(sum, GROUPS))
 DELAY = 3
 SWAPS = (6, 8)
@@ -121,9 +121,13 @@
         at += out.shape[1]
 
 
-def matmul(lefts, rights, resid, place, widths):
+def matmul(lefts, rights, resid, place, widths, only=None):
     tokens, depth = lefts[0].shape
+    block = 0
     width = rights[0].shape[1]
+    if only is not None:
+        block, width = only, widths[only]
+        widths = (width,)
     tile = 2 * resid.shape[0]
     flops = 2 * tokens * depth * len(lefts) * width
     moved = 2 * (tokens * depth * len(lefts) + depth * len(lefts) * width + tokens * width)
@@ -133,8 +137,8 @@
             num_scalar_prefetch=1,
             grid=(tokens // tile,),
             in_specs=[pl.BlockSpec((tile, depth), lambda step, place: (step, 0))] * len(lefts)
-            + [pl.BlockSpec(right.shape, lambda step, place: (0, 0)) for right in rights]
-            + [pl.BlockSpec(resid.shape, lambda step, place: (0, 0))],
+            + [pl.BlockSpec((right.shape[0], width), lambda step, place: (0, block)) for right in rights]
+            + [pl.BlockSpec((resid.shape[0], width), lambda step, place: (0, block))],
             out_specs=[pl.BlockSpec((tile, part), lambda step, place: (step, 0)) for part in widths],
         ),
         out_shape=[jax.ShapeDtypeStruct((tokens, part), jnp.bfloat16) for part in widths],
@@ -264,7 +268,8 @@
     scale = jnp.sum(jnp.where(picks, prob.reshape(2, chips, 1, tile), 0.0), axis=3, keepdims=True)
     picks = picks.astype(jnp.bfloat16)
 
-    rights.append(spread(rest[0]))
+    square = ctx_count == 4
+    rights.append(spread_near(rest[0]) if square else spread(rest[0]))
     received, rest, rights[1], resid, picks, scale = lax.optimization_barrier(
         (received, rest, rights[1], resid, picks, scale)
     )
@@ -282,14 +287,14 @@
         token[0] = arrays[0]
         return arrays
 
-    def products(group_at, right):
+    def products(group_at, right, only=None):
         group, at = widths[group_at], starts[group_at]
         if channels < 128:
             right = [jnp.concatenate(right, axis=0)]
         right = chain(*right)
-        found = matmul(lefts, right, resid[:, at : at + sum(group)], place, group)
+        found = matmul(lefts, right, resid[:, at : at + sum(group)], place, group, only)
         token[0] = found[0]
-        return found
+        return found if only is None else found[0]
 
     middle = chips // 2
     distance = jnp.minimum(chip_at, chips - 1 - chip_at)
@@ -308,16 +313,13 @@
             rows_got.append(to_core(jnp.concatenate(waiting, axis=1)))
             waiting.clear()
 
-    square = ctx_count == 4
     hops = middle - 1
     lag = DELAY - 1
     sums = [[None] * pieces for _ in range(hops + 1)]
     ready = [[None] * pieces for _ in range(hops + 1)]
     outer, across = {}, {}
     first_of = [sum(map(len, GROUPS[:at])) for at in range(len(GROUPS))]
-    lefts, rest[1] = lax.optimization_barrier((lefts, rest[1]))
-    rights.append(spread_near(rest[1]) if square else spread(rest[1]))
-    sums[0][: len(GROUPS[0])] = products(0, rights[0])
+    sums[0][0] = products(0, rights[0], 0)
     rights += [None] * (len(GROUPS) - len(rights))
     for step in range(pieces + 2 * lag * hops + DELAY + 1):
         for hop in range(hops):
@@ -361,8 +363,10 @@
                 continue
             (payload,) = chain(payload)
             outer[step, hop] = (swap_chips(payload, hop, inward is not None, outward is not None), inward, outward)
-        if step == 1 and square:
-            rights[2] = spread_on(rights[2])
+        if step == 0:
+            if square:
+                rights[1] = spread_on(rights[1])
+            sums[0][1] = products(0, rights[0], 1)
     result = jnp.where(
         core_at == 0,
         jnp.concatenate(rows_own + rows_got, axis=1),

time: 213 us -> 217 us (1.019)
  waiting for transfers between devices: 63.3 us -> 73.5 us
  starting transfers between devices: 60.6 us -> 57.6 us
    ppermute x21 -> x18, waiting for transfers between devices: 12.5 us -> 25.3 us  [to_ctx(): lax.ppermute(array, 'ctx', [(place, place ^ offset) for place in range(ct...]
    ppermute x21 -> x18, starting transfers between devices: 24.4 us -> 21 us  [to_ctx(): lax.ppermute(array, 'ctx', [(place, place ^ offset) for place in range(ct...]
    unnamed x122 -> x94, local copies, waits for them, and re-layouts: 6.72 us -> 3.78 us
  transfers between devices with their start and end apart: 52 -> 49, of which waited for: 20 -> 19; matrix products, arithmetic and copies ran while one was open for 19% -> 18% of each run, Pallas kernels for 18% -> 16%
where the time goes in v10:
time: 217 us; the launch traced here: 216 us
  waiting for transfers between devices  73.5 us (34%)
  starting transfers between devices  57.6 us (27%)
  Pallas kernels  39 us (18%)
  other arithmetic  21.9 us (10%)
  local copies, waits for them, and re-layouts  20.4 us (9%)
  matrix products  2.36 us (1%)
    ppermute x19, waiting for transfers between devices, swap_chips(): return lax.ppermute(array, 'exp', sorted(pairs))  43.4 us
    ppermute x19, starting transfers between devices, swap_chips(): return lax.ppermute(array, 'exp', sorted(pairs))  30.6 us
    pallas_call x5, Pallas kernels, matmul(): pl.pallas_call(functools.partial(matmul_kernel, len(lefts), len(rights)),...  26.2 us
    ppermute x18, waiting for transfers between devices, to_ctx(): lax.ppermute(array, 'ctx', [(place, place ^ offset) for place in range(ct...  25.3 us
    ppermute x18, starting transfers between devices, to_ctx(): lax.ppermute(array, 'ctx', [(place, place ^ offset) for place in range(ct...  21 us
    pallas_call x1, Pallas kernels, conv_grad(): pl.pallas_call(functools.partial(conv_kernel, tile), grid_spec=pltpu.Pref...  12.7 us
    slice x6, local copies, waits for them, and re-layouts, spread_on(): low, high = chain(near[2][:cut], near[1][cut:])  6 us
    select_n x5, other arithmetic, on_device(): jnp.where(distance == hop, sums[hop][inward], ready[hop + 1][outward])  5.79 us
  transfers between devices with their start and end apart: 49, of which 19 were waited for; matrix products, arithmetic and copies ran while one was open for 18% of the time, Pallas kernels for 16%

profile of v10, /device:TPU:0, one launch (start us, length us, event | category | flops | bytes accessed | tf_op | source)
XLA Modules:
  0.0 215.9 jit_solution(3862038396895114624)
XLA Ops:
  0.0 1.1 constant_dynamic-slice_fusion.7
  1.6 1.2 collective-permute-done
  2.8 3.9 %collective-permute-start.3 = (bf16[512,512]{1,0:T(8,128)(2,1)S(1)}, bf16[512,512]{1,0:T(8,128)(2,1)S(1)}, u32[]{:S(2)}, u32[]{:S(2)}) collective-permute-start(bf16[512,512]{1,0:T(8,128)(2,1)S(1)} %pad_maximum_fusion.refs_8_), channel_id=1, source_target_pairs={{0,24},{8,16},{16,8},{24,0},{1,25},{9,17},{17,9},{25,1},{2,26},{10... | collective-permute-start | bytes 1572872 | tf_op jit(solution)/shard_map/ppermute | solution.py:185
  7.3 12.7 %conv_grad.1 = (bf16[1024,256]{1,0:T(8,128)(2,1)}, bf16[1024,256]{1,0:T(8,128)(2,1)}, bf16[1024,256]{1,0:T(8,128)(2,1)}, bf16[1024,256]{1,0:T(8,128)(2,1)}) custom-call(s32[1]{0:T(128)} %bitcast.1.at_ctx, bf16[256,4096]{1,0:T(8,128)(2,1)} %out_grad.1, bf16[256,4096]{1,0:T(8,128)(2,1)} %gate_in.1, bf16[256,4096]{1,0:T(8,128)(2,1)} %conv_in.1, ...), custom_call_target="tpu_custom_call" | custom-call | flops 41943040 | bytes 10485760 | tf_op jit(solution)/shard_map/conv_grad/pallas_call | solution.py:84
  20.1 10.0 %collective-permute-done.2.refs_10_ = bf16[512,512]{1,0:T(8,128)(2,1)S(1)} collective-permute-done((bf16[512,512]{1,0:T(8,128)(2,1)S(1)}, bf16[512,512]{1,0:T(8,128)(2,1)S(1)}, u32[]{:S(2)}, u32[]{:S(2)}) %collective-permute-start.2) | collective-permute-done | bytes 524320 | tf_op jit(solution)/shard_map/ppermute | solution.py:185
  31.3 1.6 collective-permute-start.5
  33.6 1.2 collective-permute-start.7
  34.9 2.2 constant_dynamic-slice_fusion.4
  37.5 1.7 collective-permute-start.13
  39.2 2.1 constant_dynamic-slice_fusion.3
  41.3 2.7 %collective-permute-start.14 = (f32[4,4,128]{2,1,0:T(4,128)S(1)}, f32[4,4,128]{2,1,0:T(4,128)S(1)}, u32[]{:S(2)}, u32[]{:S(2)}) collective-permute-start(f32[4,4,128]{2,1,0:T(4,128)S(1)} %pad_maximum_fusion.6), channel_id=1, source_target_pairs={{0,4},{1,5},{2,6},{3,7},{4,0},{5,1},{6,2},{7,3},{8,12},{9,13},{10,... | collective-permute-start | bytes 24584 | tf_op jit(solution)/shard_map/ppermute | solution.py:237
  43.9 2.0 constant_dynamic-slice_fusion.5
  46.9 2.0 fusion.23
  49.7 1.5 collective-permute-start.10
  53.0 1.6 maximum_select_fusion
  54.5 2.2 %pad_maximum_fusion.2 = (bf16[512,512]{1,0:T(8,128)(2,1)}, bf16[512,512]{1,0:T(8,128)(2,1)}) fusion(bf16[256,512]{1,0:T(8,128)(2,1)} %get-tuple-element.253, bf16[256,512]{1,0:T(8,128)(2,1)} %get-tuple-element.240, bf16[256,512]{1,0:T(8,128)(2,1)} %get-tuple-element.252, bf16[256,512]{1,0:T(8,128)(2,1)} %get-tuple-element.239), kind=kLoop, calls=%fused_computation.49 | loop fusion | flops 2097152 | bytes 2097152 | tf_op jit(solution)/shard_map/concatenate | solution.py:247
  56.8 1.6 collective-permute-done.6.refs_4_
  58.7 11.0 %collective-permute-done.10.refs_10_ = bf16[512,512]{1,0:T(8,128)(2,1)} collective-permute-done((bf16[512,512]{1,0:T(8,128)(2,1)}, bf16[512,512]{1,0:T(8,128)(2,1)}, u32[]{:S(2)}, u32[]{:S(2)}) %collective-permute-start.10) | collective-permute-done | bytes 524320 | tf_op jit(solution)/shard_map/ppermute | solution.py:185
  70.3 1.0 fusion.22
  73.5 4.3 %partial_product.5 = bf16[1024,256]{1,0:T(8,128)(2,1)} custom-call(s32[1]{0:T(128)} %bitcast.place, bf16[1024,256]{1,0:T(8,128)(2,1)} %get-tuple-element.126.refs_0_, bf16[1024,256]{1,0:T(8,128)(2,1)} %copy-done.2, bf16[1024,256]{1,0:T(8,128)(2,1)} %copy-done.3, bf16[1024,256]{1,0:T(8,128)(2,1)} %copy-done.8, bf16[1024,256]{1,0:T(8,128)(2,1)} %copy-done.4, ...), custom_call_target="tpu_custom_call" | custom-call | flops 1073741824 | bytes 5767168 | tf_op jit(solution)/shard_map/partial_product/pallas_call | solution.py:134
  77.8 3.5 %collective-permute-start.20 = (bf16[1024,256]{1,0:T(8,128)(2,1)}, bf16[1024,256]{1,0:T(8,128)(2,1)S(1)}, u32[]{:S(2)}, u32[]{:S(2)}) collective-permute-start(bf16[1024,256]{1,0:T(8,128)(2,1)} %partial_product.5), channel_id=1, source_target_pairs={{0,2},{1,3},{6,4},{7,5},{8,10},{9,11},{14,12},{15,13},{16,18},{17,... | collective-permute-start | bytes 1572872 | tf_op jit(solution)/shard_map/ppermute | solution.py:195
  81.3 1.0 slice.128
  82.3 1.0 slice.127
  83.9 4.3 %partial_product.6 = bf16[1024,256]{1,0:T(8,128)(2,1)} custom-call(s32[1]{0:T(128)} %bitcast.place, bf16[1024,256]{1,0:T(8,128)(2,1)} %get-tuple-element.126.refs_0_, bf16[1024,256]{1,0:T(8,128)(2,1)} %copy-done.2, bf16[1024,256]{1,0:T(8,128)(2,1)} %copy-done.3, bf16[1024,256]{1,0:T(8,128)(2,1)} %copy-done.8, bf16[1024,256]{1,0:T(8,128)(2,1)} %copy-done.4, ...), custom_call_target="tpu_custom_call" | custom-call | flops 1073741824 | bytes 5767168 | tf_op jit(solution)/shard_map/partial_product/pallas_call | solution.py:134
  88.2 1.5 collective-permute-start.19
  89.7 1.3 collective-permute-start.22
  91.0 2.9 %collective-permute-done.20 = bf16[1024,256]{1,0:T(8,128)(2,1)S(1)} collective-permute-done((bf16[1024,256]{1,0:T(8,128)(2,1)}, bf16[1024,256]{1,0:T(8,128)(2,1)S(1)}, u32[]{:S(2)}, u32[]{:S(2)}) %collective-permute-start.20) | collective-permute-done | bytes 524320 | tf_op jit(solution)/shard_map/ppermute | solution.py:195
  94.7 1.2 collective-permute-done.19.refs_12_
  96.0 1.6 collective-permute-start.24
  98.3 5.9 %partial_product.7 = (bf16[1024,256]{1,0:T(8,128)(2,1)}, bf16[1024,256]{1,0:T(8,128)(2,1)}) custom-call(s32[1]{0:T(128)} %bitcast.place, bf16[1024,256]{1,0:T(8,128)(2,1)} %get-tuple-element.126.refs_0_, bf16[1024,256]{1,0:T(8,128)(2,1)} %copy-done.2, bf16[1024,256]{1,0:T(8,128)(2,1)} %copy-done.3, bf16[1024,256]{1,0:T(8,128)(2,1)} %copy-done.8, ...), custom_call_target="tpu_custom_call" | custom-call | flops 2147483648 | bytes 7340032 | tf_op jit(solution)/shard_map/partial_product/pallas_call | solution.py:134
  104.3 5.8 %collective-permute-start.29 = (bf16[1024,256]{1,0:T(8,128)(2,1)}, bf16[1024,256]{1,0:T(8,128)(2,1)S(1)}, u32[]{:S(2)}, u32[]{:S(2)}) collective-permute-start(bf16[1024,256]{1,0:T(8,128)(2,1)} %get-tuple-element.182), channel_id=1, source_target_pairs={{0,2},{1,3},{6,4},{7,5},{8,10},{9,11},{14,12},{15,13},{16,18},{17,... | collective-permute-start | bytes 1572872 | tf_op jit(solution)/shard_map/ppermute | solution.py:195
  111.0 1.2 slice.159
  112.1 1.0 slice.158
  113.7 1.5 collective-permute-start.26
  115.2 2.0 broadcast_select_fusion.13
  117.4 5.3 %collective-permute-done.29 = bf16[1024,256]{1,0:T(8,128)(2,1)S(1)} collective-permute-done((bf16[1024,256]{1,0:T(8,128)(2,1)}, bf16[1024,256]{1,0:T(8,128)(2,1)S(1)}, u32[]{:S(2)}, u32[]{:S(2)}) %collective-permute-start.29) | collective-permute-done | bytes 524320 | tf_op jit(solution)/shard_map/ppermute | solution.py:195
  124.5 1.2 collective-permute-start.32
  125.7 5.9 %partial_product.8 = (bf16[1024,256]{1,0:T(8,128)(2,1)}, bf16[1024,256]{1,0:T(8,128)(2,1)}) custom-call(s32[1]{0:T(128)} %bitcast.place, bf16[1024,256]{1,0:T(8,128)(2,1)} %get-tuple-element.126.refs_0_, bf16[1024,256]{1,0:T(8,128)(2,1)} %copy-done.2, bf16[1024,256]{1,0:T(8,128)(2,1)} %copy-done.3, bf16[1024,256]{1,0:T(8,128)(2,1)} %copy-done.8, ...), custom_call_target="tpu_custom_call" | custom-call | flops 2147483648 | bytes 7340032 | tf_op jit(solution)/shard_map/partial_product/pallas_call | solution.py:134
  131.6 1.3 broadcast_select_fusion.12
  132.9 3.0 %collective-permute-start.30 = (bf16[1024,256]{1,0:T(8,128)(2,1)S(1)}, bf16[1024,256]{1,0:T(8,128)(2,1)S(1)}, u32[]{:S(2)}, u32[]{:S(2)}) collective-permute-start(bf16[1024,256]{1,0:T(8,128)(2,1)S(1)} %broadcast_select_fusion.12), channel_id=1, source_target_pairs={{0,2},{1,3},{2,0},{3,1},{4,6},{5,7},{6,4},{7,5},{8,10},{9,11},{10,... | collective-permute-start | bytes 1572872 | tf_op jit(solution)/shard_map/ppermute | solution.py:195
  135.9 1.2 broadcast_select_fusion.11
  137.5 1.2 add_convert_fusion.10
  140.3 1.0 broadcast_select_fusion.10
  141.3 1.0 slice.162
  142.3 1.0 slice.161
  143.2 0.9 collective-permute-start.36
  144.1 1.2 collective-permute-start.35
  145.4 2.0 collective-permute-start.34
  151.2 5.8 %partial_product.9 = (bf16[1024,256]{1,0:T(8,128)(2,1)}, bf16[1024,256]{1,0:T(8,128)(2,1)}) custom-call(s32[1]{0:T(128)} %bitcast.place, bf16[1024,256]{1,0:T(8,128)(2,1)} %get-tuple-element.126.refs_0_, bf16[1024,256]{1,0:T(8,128)(2,1)} %copy-done.2, bf16[1024,256]{1,0:T(8,128)(2,1)} %copy-done.3, bf16[1024,256]{1,0:T(8,128)(2,1)} %copy-done.8, ...), custom_call_target="tpu_custom_call" | custom-call | flops 2147483648 | bytes 7340032 | tf_op jit(solution)/shard_map/partial_product/pallas_call | solution.py:134
  157.1 1.3 broadcast_select_fusion.8
  158.4 3.3 %collective-permute-start.38 = (bf16[1024,256]{1,0:T(8,128)(2,1)S(1)}, bf16[1024,256]{1,0:T(8,128)(2,1)S(1)}, u32[]{:S(2)}, u32[]{:S(2)}) collective-permute-start(bf16[1024,256]{1,0:T(8,128)(2,1)S(1)} %broadcast_select_fusion.8), channel_id=1, source_target_pairs={{0,2},{1,3},{2,0},{3,1},{4,6},{5,7},{6,4},{7,5},{8,10},{9,11},{10,... | collective-permute-start | bytes 1572872 | tf_op jit(solution)/shard_map/ppermute | solution.py:195
  161.7 1.2 add_convert_fusion.6
  163.7 1.7 broadcast_select_fusion.7
  165.9 1.6 collective-permute-start.40
  167.6 6.9 %collective-permute-done.38 = bf16[1024,256]{1,0:T(8,128)(2,1)S(1)} collective-permute-done((bf16[1024,256]{1,0:T(8,128)(2,1)S(1)}, bf16[1024,256]{1,0:T(8,128)(2,1)S(1)}, u32[]{:S(2)}, u32[]{:S(2)}) %collective-permute-start.38) | collective-permute-done | bytes 524320 | tf_op jit(solution)/shard_map/ppermute | solution.py:195
  176.1 1.3 collective-permute-start.42
  177.4 7.9 %collective-permute-done.40 = bf16[1024,256]{1,0:T(8,128)(2,1)S(1)} collective-permute-done((bf16[1024,256]{1,0:T(8,128)(2,1)S(1)}, bf16[1024,256]{1,0:T(8,128)(2,1)S(1)}, u32[]{:S(2)}, u32[]{:S(2)}) %collective-permute-start.40) | collective-permute-done | bytes 524320 | tf_op jit(solution)/shard_map/ppermute | solution.py:195
  186.9 1.3 collective-permute-start.44
  188.4 8.2 %collective-permute-done.42 = bf16[1024,256]{1,0:T(8,128)(2,1)S(1)} collective-permute-done((bf16[1024,256]{1,0:T(8,128)(2,1)S(1)}, bf16[1024,256]{1,0:T(8,128)(2,1)S(1)}, u32[]{:S(2)}, u32[]{:S(2)}) %collective-permute-start.42) | collective-permute-done | bytes 524320 | tf_op jit(solution)/shard_map/ppermute | solution.py:195
  196.9 1.3 collective-permute-start.46
  198.4 6.9 %collective-permute-done.44 = bf16[1024,256]{1,0:T(8,128)(2,1)S(1)} collective-permute-done((bf16[1024,256]{1,0:T(8,128)(2,1)S(1)}, bf16[1024,256]{1,0:T(8,128)(2,1)S(1)}, u32[]{:S(2)}, u32[]{:S(2)}) %collective-permute-start.44) | collective-permute-done | bytes 524320 | tf_op jit(solution)/shard_map/ppermute | solution.py:195
  205.7 5.2 %collective-permute-done.46 = bf16[1024,256]{1,0:T(8,128)(2,1)S(1)} collective-permute-done((bf16[1024,256]{1,0:T(8,128)(2,1)S(1)}, bf16[1024,256]{1,0:T(8,128)(2,1)S(1)}, u32[]{:S(2)}, u32[]{:S(2)}) %collective-permute-start.46) | collective-permute-done | bytes 524320 | tf_op jit(solution)/shard_map/ppermute | solution.py:195
  211.9 1.4 collective-permute-done.48
  213.6 2.2 %broadcast_select_fusion = bf16[1,448,4096]{2,1,0:T(8,128)(2,1)} fusion(bf16[1,448,4096]{2,1,0:T(8,128)(2,1)S(1)} %get-tuple-element.256, bf16[1,448,4096]{2,1,0:T(8,128)(2,1)S(1)} %constant_dynamic-update-slice_fusion.14, pred[]{:T(512)S(6)} %eq.30), kind=kLoop, calls=%fused_computation | loop fusion | flops 1835008 | bytes 11010049 | tf_op jit(solution)/shard_map/jit(_where)/select_n | solution.py:370
  (220 shorter events, 28.0 us)
Async XLA Ops:
  1.1 1.7 collective-permute-start
  2.8 17.3 %copy-start = (bf16[512,512]{1,0:T(8,128)(2,1)}, bf16[512,512]{1,0:T(8,128)(2,1)S(1)}, u32[]{:S(2)}) copy-start(bf16[512,512]{1,0:T(8,128)(2,1)S(1)} %pad_maximum_fusion.refs_8_) | copy-start | bytes 1572868
  2.8 17.3 %collective-permute-start.3 = (bf16[512,512]{1,0:T(8,128)(2,1)S(1)}, bf16[512,512]{1,0:T(8,128)(2,1)S(1)}, u32[]{:S(2)}, u32[]{:S(2)}) collective-permute-start(bf16[512,512]{1,0:T(8,128)(2,1)S(1)} %pad_maximum_fusion.refs_8_), channel_id=1, source_target_pairs={{0,24},{8,16},{16,8},{24,0},{1,25},{9,17},{17,9},{25,1},{2,26},{10... | collective-permute-start | bytes 1572872 | tf_op jit(solution)/shard_map/ppermute | solution.py:185
  6.7 23.5 %collective-permute-start.2 = (bf16[512,512]{1,0:T(8,128)(2,1)S(1)}, bf16[512,512]{1,0:T(8,128)(2,1)S(1)}, u32[]{:S(2)}, u32[]{:S(2)}) collective-permute-start(bf16[512,512]{1,0:T(8,128)(2,1)S(1)} %pad_maximum_fusion.refs_8_), channel_id=1, source_target_pairs={{0,16},{8,24},{16,0},{24,8},{1,17},{9,25},{17,1},{25,9},{2,18},{10... | collective-permute-start | bytes 1572872 | tf_op jit(solution)/shard_map/ppermute | solution.py:185
  7.2 23.2 %collective-permute-start.1 = (bf16[512,512]{1,0:T(8,128)(2,1)S(1)}, bf16[512,512]{1,0:T(8,128)(2,1)S(1)}, u32[]{:S(2)}, u32[]{:S(2)}) collective-permute-start(bf16[512,512]{1,0:T(8,128)(2,1)S(1)} %pad_maximum_fusion.refs_8_), channel_id=1, source_target_pairs={{0,8},{8,0},{16,24},{24,16},{1,9},{9,1},{17,25},{25,17},{2,10},{10... | collective-permute-start | bytes 1572872 | tf_op jit(solution)/shard_map/ppermute | solution.py:185
  7.3 27.5 %copy-start.27 = (s32[128,2]{0,1:T(2,128)S(1)}, s32[128,2]{0,1:T(2,128)}, u32[]{:S(2)}) copy-start(s32[128,2]{0,1:T(2,128)} %param.20) | copy-start | bytes 3076
  7.3 27.5 %copy-start.28 = (f32[128,2]{0,1:T(2,128)S(1)}, f32[128,2]{0,1:T(2,128)}, u32[]{:S(2)}) copy-start(f32[128,2]{0,1:T(2,128)} %param.21) | copy-start | bytes 3076
  20.1 28.8 %copy-start.5 = (bf16[512,512]{1,0:T(8,128)(2,1)}, bf16[512,512]{1,0:T(8,128)(2,1)S(1)}, u32[]{:S(2)}) copy-start(bf16[512,512]{1,0:T(8,128)(2,1)S(1)} %collective-permute-done.3.refs_11_) | copy-start | bytes 1572868
  31.0 3.8 %collective-permute-start.4 = (bf16[1024,256]{1,0:T(8,128)(2,1)}, bf16[1024,256]{1,0:T(8,128)(2,1)S(1)}, u32[]{:S(2)}, u32[]{:S(2)}) collective-permute-start(bf16[1024,256]{1,0:T(8,128)(2,1)} %get-tuple-element.126.refs_0_), channel_id=1, source_target_pairs={{0,1},{1,0},{2,3},{3,2},{4,5},{5,4},{6,7},{7,6},{8,9},{9,8},{10,11... | collective-permute-start | bytes 1572872 | tf_op jit(solution)/shard_map/ppermute | solution.py:182
  31.3 25.5 %collective-permute-start.5 = (bf16[1024,256]{1,0:T(8,128)(2,1)}, bf16[1024,256]{1,0:T(8,128)(2,1)S(1)}, u32[]{:S(2)}, u32[]{:S(2)}) collective-permute-start(bf16[1024,256]{1,0:T(8,128)(2,1)} %get-tuple-element.128), channel_id=1, source_target_pairs={{0,8},{8,0},{16,24},{24,16},{1,9},{9,1},{17,25},{25,17},{2,10},{10... | collective-permute-start | bytes 1572872 | tf_op jit(solution)/shard_map/ppermute | solution.py:185
  32.9 25.5 %collective-permute-start.6 = (bf16[1024,256]{1,0:T(8,128)(2,1)}, bf16[1024,256]{1,0:T(8,128)(2,1)S(1)}, u32[]{:S(2)}, u32[]{:S(2)}) collective-permute-start(bf16[1024,256]{1,0:T(8,128)(2,1)} %get-tuple-element.129), channel_id=1, source_target_pairs={{0,16},{8,24},{16,0},{24,8},{1,17},{9,25},{17,1},{25,9},{2,18},{10... | collective-permute-start | bytes 1572872 | tf_op jit(solution)/shard_map/ppermute | solution.py:185
  33.6 25.1 %collective-permute-start.7 = (bf16[1024,256]{1,0:T(8,128)(2,1)}, bf16[1024,256]{1,0:T(8,128)(2,1)}, u32[]{:S(2)}, u32[]{:S(2)}) collective-permute-start(bf16[1024,256]{1,0:T(8,128)(2,1)} %get-tuple-element.130), channel_id=1, source_target_pairs={{0,24},{8,16},{16,8},{24,0},{1,25},{9,17},{17,9},{25,1},{2,26},{10... | collective-permute-start | bytes 1572872 | tf_op jit(solution)/shard_map/ppermute | solution.py:185
  34.8 14.1 %copy-start.2 = (bf16[1024,256]{1,0:T(8,128)(2,1)}, bf16[1024,256]{1,0:T(8,128)(2,1)S(1)}, u32[]{:S(2)}) copy-start(bf16[1024,256]{1,0:T(8,128)(2,1)S(1)} %collective-permute-done.4.refs_1_) | copy-start | bytes 1572868
  34.8 2.6 %collective-permute-start.12 = (f32[1,4,128]{2,1,0:T(4,128)S(1)}, f32[1,4,128]{2,1,0:T(4,128)S(1)}, u32[]{:S(2)}, u32[]{:S(2)}) collective-permute-start(f32[1,4,128]{2,1,0:T(4,128)S(1)} %maximum_bitcast_fusion), channel_id=1, source_target_pairs={{0,1},{1,0},{2,3},{3,2},{4,5},{5,4},{6,7},{7,6},{8,9},{9,8},{10,11... | collective-permute-start | bytes 6152 | tf_op jit(solution)/shard_map/ppermute | solution.py:237
  37.1 9.9 %collective-permute-start.8 = (bf16[256,1536]{1,0:T(8,128)(2,1)}, bf16[256,1536]{1,0:T(8,128)(2,1)}, u32[]{:S(2)}, u32[]{:S(2)}) collective-permute-start(bf16[256,1536]{1,0:T(8,128)(2,1)} %constant_dynamic-slice_fusion.4), channel_id=1, source_target_pairs={{0,1},{1,0},{2,3},{3,2},{4,5},{5,4},{6,7},{7,6},{8,9},{9,8},{10,11... | collective-permute-start | bytes 2359304 | tf_op jit(solution)/shard_map/ppermute | solution.py:182
  37.5 3.8 %collective-permute-start.13 = (f32[2,4,128]{2,1,0:T(4,128)S(1)}, f32[2,4,128]{2,1,0:T(4,128)S(1)}, u32[]{:S(2)}, u32[]{:S(2)}) collective-permute-start(f32[2,4,128]{2,1,0:T(4,128)S(1)} %pad_maximum_fusion.7), channel_id=1, source_target_pairs={{0,2},{1,3},{2,0},{3,1},{4,6},{5,7},{6,4},{7,5},{8,10},{9,11},{10,... | collective-permute-start | bytes 12296 | tf_op jit(solution)/shard_map/ppermute | solution.py:237
  41.3 4.6 %collective-permute-start.14 = (f32[4,4,128]{2,1,0:T(4,128)S(1)}, f32[4,4,128]{2,1,0:T(4,128)S(1)}, u32[]{:S(2)}, u32[]{:S(2)}) collective-permute-start(f32[4,4,128]{2,1,0:T(4,128)S(1)} %pad_maximum_fusion.6), channel_id=1, source_target_pairs={{0,4},{1,5},{2,6},{3,7},{4,0},{5,1},{6,2},{7,3},{8,12},{9,13},{10,... | collective-permute-start | bytes 24584 | tf_op jit(solution)/shard_map/ppermute | solution.py:237
  45.9 5.4 %collective-permute-start.11 = (bf16[128,2048]{1,0:T(8,128)(2,1)}, bf16[128,2048]{1,0:T(8,128)(2,1)}, u32[]{:S(2)}, u32[]{:S(2)}) collective-permute-start(bf16[128,2048]{1,0:T(8,128)(2,1)} %get-tuple-element.251), channel_id=1, source_target_pairs={{0,1},{1,0},{2,3},{3,2},{4,5},{5,4},{6,7},{7,6},{8,9},{9,8},{10,11... | collective-permute-start | bytes 1572872 | tf_op jit(solution)/shard_map/ppermute | solution.py:182
  49.7 20.0 %collective-permute-start.10 = (bf16[512,512]{1,0:T(8,128)(2,1)}, bf16[512,512]{1,0:T(8,128)(2,1)}, u32[]{:S(2)}, u32[]{:S(2)}) collective-permute-start(bf16[512,512]{1,0:T(8,128)(2,1)} %pad_maximum_fusion.1.refs_8_), channel_id=1, source_target_pairs={{0,16},{8,24},{16,0},{24,8},{1,17},{9,25},{17,1},{25,9},{2,18},{10... | collective-permute-start | bytes 1572872 | tf_op jit(solution)/shard_map/ppermute | solution.py:185
  51.3 18.5 %collective-permute-start.9 = (bf16[512,512]{1,0:T(8,128)(2,1)}, bf16[512,512]{1,0:T(8,128)(2,1)}, u32[]{:S(2)}, u32[]{:S(2)}) collective-permute-start(bf16[512,512]{1,0:T(8,128)(2,1)} %pad_maximum_fusion.1.refs_8_), channel_id=1, source_target_pairs={{0,8},{8,0},{16,24},{24,16},{1,9},{9,1},{17,25},{25,17},{2,10},{10... | collective-permute-start | bytes 1572872 | tf_op jit(solution)/shard_map/ppermute | solution.py:185
  56.8 16.7 %copy-start.3 = (bf16[1024,256]{1,0:T(8,128)(2,1)}, bf16[1024,256]{1,0:T(8,128)(2,1)S(1)}, u32[]{:S(2)}) copy-start(bf16[1024,256]{1,0:T(8,128)(2,1)S(1)} %collective-permute-done.5.refs_2_) | copy-start | bytes 1572868
  58.4 15.1 %copy-start.4 = (bf16[1024,256]{1,0:T(8,128)(2,1)}, bf16[1024,256]{1,0:T(8,128)(2,1)S(1)}, u32[]{:S(2)}) copy-start(bf16[1024,256]{1,0:T(8,128)(2,1)S(1)} %collective-permute-done.6.refs_4_) | copy-start | bytes 1572868
  69.8 2.4 %collective-permute-start.15 = (bf16[1024,256]{1,0:T(8,128)(2,1)S(1)}, bf16[1024,256]{1,0:T(8,128)(2,1)S(1)}, u32[]{:S(2)}, u32[]{:S(2)}) collective-permute-start(bf16[1024,256]{1,0:T(8,128)(2,1)S(1)} %collective-permute-done.5.refs_2_), channel_id=1, source_target_pairs={{0,1},{1,0},{2,3},{3,2},{4,5},{5,4},{6,7},{7,6},{8,9},{9,8},{10,11... | collective-permute-start | bytes 1572872 | tf_op jit(solution)/shard_map/ppermute | solution.py:182
  69.8 3.2 %collective-permute-start.16 = (bf16[1024,256]{1,0:T(8,128)(2,1)S(1)}, bf16[1024,256]{1,0:T(8,128)(2,1)}, u32[]{:S(2)}, u32[]{:S(2)}) collective-permute-start(bf16[1024,256]{1,0:T(8,128)(2,1)S(1)} %collective-permute-done.6.refs_4_), channel_id=1, source_target_pairs={{0,1},{1,0},{2,3},{3,2},{4,5},{5,4},{6,7},{7,6},{8,9},{9,8},{10,11... | collective-permute-start | bytes 1572872 | tf_op jit(solution)/shard_map/ppermute | solution.py:182
  70.3 3.2 %collective-permute-start.17 = (bf16[1024,256]{1,0:T(8,128)(2,1)}, bf16[1024,256]{1,0:T(8,128)(2,1)}, u32[]{:S(2)}, u32[]{:S(2)}) collective-permute-start(bf16[1024,256]{1,0:T(8,128)(2,1)} %collective-permute-done.7.refs_6_), channel_id=1, source_target_pairs={{0,1},{1,0},{2,3},{3,2},{4,5},{5,4},{6,7},{7,6},{8,9},{9,8},{10,11... | collective-permute-start | bytes 1572872 | tf_op jit(solution)/shard_map/ppermute | solution.py:182
  77.8 16.1 %collective-permute-start.20 = (bf16[1024,256]{1,0:T(8,128)(2,1)}, bf16[1024,256]{1,0:T(8,128)(2,1)S(1)}, u32[]{:S(2)}, u32[]{:S(2)}) collective-permute-start(bf16[1024,256]{1,0:T(8,128)(2,1)} %partial_product.5), channel_id=1, source_target_pairs={{0,2},{1,3},{6,4},{7,5},{8,10},{9,11},{14,12},{15,13},{16,18},{17,... | collective-permute-start | bytes 1572872 | tf_op jit(solution)/shard_map/ppermute | solution.py:195
  83.3 10.6 %copy-start.10 = (bf16[1024,256]{1,0:T(8,128)(2,1)S(1)}, bf16[1024,256]{1,0:T(8,128)(2,1)}, u32[]{:S(2)}) copy-start(bf16[1024,256]{1,0:T(8,128)(2,1)} %partial_product.5) | copy-start | bytes 1572868
  83.3 12.7 %collective-permute-start.18 = (bf16[256,512]{1,0:T(8,128)(2,1)S(1)}, bf16[256,512]{1,0:T(8,128)(2,1)S(1)}, u32[]{:S(2)}, u32[]{:S(2)}) collective-permute-start(bf16[256,512]{1,0:T(8,128)(2,1)S(1)} %slice.127), channel_id=1, source_target_pairs={{0,8},{8,0},{16,24},{24,16},{1,9},{9,1},{17,25},{25,17},{2,10},{10... | collective-permute-start | bytes 786440 | tf_op jit(solution)/shard_map/ppermute | solution.py:185
  88.2 7.8 %collective-permute-start.19 = (bf16[256,512]{1,0:T(8,128)(2,1)S(1)}, bf16[256,512]{1,0:T(8,128)(2,1)S(1)}, u32[]{:S(2)}, u32[]{:S(2)}) collective-permute-start(bf16[256,512]{1,0:T(8,128)(2,1)S(1)} %slice.128), channel_id=1, source_target_pairs={{0,16},{8,24},{16,0},{24,8},{1,17},{9,25},{17,1},{25,9},{2,18},{10... | collective-permute-start | bytes 786440 | tf_op jit(solution)/shard_map/ppermute | solution.py:185
  89.7 20.4 %collective-permute-start.22 = (bf16[1024,256]{1,0:T(8,128)(2,1)}, bf16[1024,256]{1,0:T(8,128)(2,1)S(1)}, u32[]{:S(2)}, u32[]{:S(2)}) collective-permute-start(bf16[1024,256]{1,0:T(8,128)(2,1)} %partial_product.6), channel_id=1, source_target_pairs={{0,2},{1,3},{6,4},{7,5},{8,10},{9,11},{14,12},{15,13},{16,18},{17,... | collective-permute-start | bytes 1572872 | tf_op jit(solution)/shard_map/ppermute | solution.py:195
  94.0 16.9 %collective-permute-start.21 = (bf16[1024,256]{1,0:T(8,128)(2,1)S(1)}, bf16[1024,256]{1,0:T(8,128)(2,1)S(1)}, u32[]{:S(2)}, u32[]{:S(2)}) collective-permute-start(bf16[1024,256]{1,0:T(8,128)(2,1)S(1)} %add_convert_fusion.15), channel_id=1, source_target_pairs={{2,4},{3,5},{4,2},{5,3},{10,12},{11,13},{12,10},{13,11},{18,20},{1... | collective-permute-start | bytes 1572872 | tf_op jit(solution)/shard_map/ppermute | solution.py:195
  96.0 15.0 %collective-permute-start.24 = (bf16[512,512]{1,0:T(8,128)(2,1)}, bf16[512,512]{1,0:T(8,128)(2,1)}, u32[]{:S(2)}, u32[]{:S(2)}) collective-permute-start(bf16[512,512]{1,0:T(8,128)(2,1)} %get-tuple-element.191.refs_8_), channel_id=1, source_target_pairs={{0,8},{8,0},{16,24},{24,16},{1,9},{9,1},{17,25},{25,17},{2,10},{10... | collective-permute-start | bytes 1572872 | tf_op jit(solution)/shard_map/ppermute | solution.py:185
  97.5 14.6 %collective-permute-start.23 = (bf16[512,512]{1,0:T(8,128)(2,1)}, bf16[512,512]{1,0:T(8,128)(2,1)}, u32[]{:S(2)}, u32[]{:S(2)}) collective-permute-start(bf16[512,512]{1,0:T(8,128)(2,1)} %get-tuple-element.191.refs_8_), channel_id=1, source_target_pairs={{0,16},{8,24},{16,0},{24,8},{1,17},{9,25},{17,1},{25,9},{2,18},{10... | collective-permute-start | bytes 1572872 | tf_op jit(solution)/shard_map/ppermute | solution.py:185
  98.3 11.7 %copy-start.9 = (bf16[1024,256]{1,0:T(8,128)(2,1)S(1)}, bf16[1024,256]{1,0:T(8,128)(2,1)}, u32[]{:S(2)}) copy-start(bf16[1024,256]{1,0:T(8,128)(2,1)} %partial_product.6) | copy-start | bytes 1572868
  104.3 18.5 %copy-start.22 = (bf16[1024,256]{1,0:T(8,128)(2,1)S(1)}, bf16[1024,256]{1,0:T(8,128)(2,1)}, u32[]{:S(2)}) copy-start(bf16[1024,256]{1,0:T(8,128)(2,1)} %get-tuple-element.182) | copy-start | bytes 1572868
  104.3 18.4 %collective-permute-start.29 = (bf16[1024,256]{1,0:T(8,128)(2,1)}, bf16[1024,256]{1,0:T(8,128)(2,1)S(1)}, u32[]{:S(2)}, u32[]{:S(2)}) collective-permute-start(bf16[1024,256]{1,0:T(8,128)(2,1)} %get-tuple-element.182), channel_id=1, source_target_pairs={{0,2},{1,3},{6,4},{7,5},{8,10},{9,11},{14,12},{15,13},{16,18},{17,... | collective-permute-start | bytes 1572872 | tf_op jit(solution)/shard_map/ppermute | solution.py:195
  110.2 13.3 %collective-permute-start.28 = (bf16[1024,256]{1,0:T(8,128)(2,1)S(1)}, bf16[1024,256]{1,0:T(8,128)(2,1)S(1)}, u32[]{:S(2)}, u32[]{:S(2)}) collective-permute-start(bf16[1024,256]{1,0:T(8,128)(2,1)S(1)} %add_convert_fusion.14), channel_id=1, source_target_pairs={{2,4},{3,5},{4,2},{5,3},{10,12},{11,13},{12,10},{13,11},{18,20},{1... | collective-permute-start | bytes 1572872 | tf_op jit(solution)/shard_map/ppermute | solution.py:195
  110.9 11.8 %copy-start.12 = (bf16[1024,256]{1,0:T(8,128)(2,1)}, bf16[1024,256]{1,0:T(8,128)(2,1)S(1)}, u32[]{:S(2)}) copy-start(bf16[1024,256]{1,0:T(8,128)(2,1)S(1)} %collective-permute-done.21) | copy-start | bytes 1572868
  113.1 10.5 %collective-permute-start.27 = (bf16[256,512]{1,0:T(8,128)(2,1)S(1)}, bf16[256,512]{1,0:T(8,128)(2,1)S(1)}, u32[]{:S(2)}, u32[]{:S(2)}) collective-permute-start(bf16[256,512]{1,0:T(8,128)(2,1)S(1)} %slice.159), channel_id=1, source_target_pairs={{0,16},{8,24},{16,0},{24,8},{1,17},{9,25},{17,1},{25,9},{2,18},{10... | collective-permute-start | bytes 786440 | tf_op jit(solution)/shard_map/ppermute | solution.py:185
  113.7 9.9 %collective-permute-start.26 = (bf16[256,512]{1,0:T(8,128)(2,1)S(1)}, bf16[256,512]{1,0:T(8,128)(2,1)S(1)}, u32[]{:S(2)}, u32[]{:S(2)}) collective-permute-start(bf16[256,512]{1,0:T(8,128)(2,1)S(1)} %slice.158), channel_id=1, source_target_pairs={{0,8},{8,0},{16,24},{24,16},{1,9},{9,1},{17,25},{25,17},{2,10},{10... | collective-permute-start | bytes 786440 | tf_op jit(solution)/shard_map/ppermute | solution.py:185
  117.2 18.7 %collective-permute-start.25 = (bf16[1024,256]{1,0:T(8,128)(2,1)}, bf16[1024,256]{1,0:T(8,128)(2,1)}, u32[]{:S(2)}, u32[]{:S(2)}) collective-permute-start(bf16[1024,256]{1,0:T(8,128)(2,1)} %broadcast_select_fusion.13), channel_id=1, source_target_pairs={{0,2},{1,3},{2,0},{3,1},{4,6},{5,7},{6,4},{7,5},{8,10},{9,11},{10,... | collective-permute-start | bytes 1572872 | tf_op jit(solution)/shard_map/ppermute | solution.py:195
  122.9 16.7 %collective-permute-start.31 = (bf16[1024,256]{1,0:T(8,128)(2,1)S(1)}, bf16[1024,256]{1,0:T(8,128)(2,1)S(1)}, u32[]{:S(2)}, u32[]{:S(2)}) collective-permute-start(bf16[1024,256]{1,0:T(8,128)(2,1)S(1)} %add_convert_fusion.12), channel_id=1, source_target_pairs={{2,4},{3,5},{4,2},{5,3},{10,12},{11,13},{12,10},{13,11},{18,20},{1... | collective-permute-start | bytes 1572872 | tf_op jit(solution)/shard_map/ppermute | solution.py:195
  123.6 17.7 %collective-permute-start.33 = (bf16[512,512]{1,0:T(8,128)(2,1)}, bf16[512,512]{1,0:T(8,128)(2,1)}, u32[]{:S(2)}, u32[]{:S(2)}) collective-permute-start(bf16[512,512]{1,0:T(8,128)(2,1)} %get-tuple-element.212.refs_8_), channel_id=1, source_target_pairs={{0,8},{8,0},{16,24},{24,16},{1,9},{9,1},{17,25},{25,17},{2,10},{10... | collective-permute-start | bytes 1572872 | tf_op jit(solution)/shard_map/ppermute | solution.py:185
  124.5 17.8 %collective-permute-start.32 = (bf16[512,512]{1,0:T(8,128)(2,1)}, bf16[512,512]{1,0:T(8,128)(2,1)}, u32[]{:S(2)}, u32[]{:S(2)}) collective-permute-start(bf16[512,512]{1,0:T(8,128)(2,1)} %get-tuple-element.212.refs_8_), channel_id=1, source_target_pairs={{0,16},{8,24},{16,0},{24,8},{1,17},{9,25},{17,1},{25,9},{2,18},{10... | collective-permute-start | bytes 1572872 | tf_op jit(solution)/shard_map/ppermute | solution.py:185
  125.7 10.2 %copy-start.13 = (bf16[1024,256]{1,0:T(8,128)(2,1)S(1)}, bf16[1024,256]{1,0:T(8,128)(2,1)}, u32[]{:S(2)}) copy-start(bf16[1024,256]{1,0:T(8,128)(2,1)} %copy-done.12) | copy-start | bytes 1572868
  132.9 14.4 %collective-permute-start.30 = (bf16[1024,256]{1,0:T(8,128)(2,1)S(1)}, bf16[1024,256]{1,0:T(8,128)(2,1)S(1)}, u32[]{:S(2)}, u32[]{:S(2)}) collective-permute-start(bf16[1024,256]{1,0:T(8,128)(2,1)S(1)} %broadcast_select_fusion.12), channel_id=1, source_target_pairs={{0,2},{1,3},{2,0},{3,1},{4,6},{5,7},{6,4},{7,5},{8,10},{9,11},{10,... | collective-permute-start | bytes 1572872 | tf_op jit(solution)/shard_map/ppermute | solution.py:195
  138.7 8.9 %copy-start.16 = (bf16[1024,256]{1,0:T(8,128)(2,1)S(1)}, bf16[1024,256]{1,0:T(8,128)(2,1)}, u32[]{:S(2)}) copy-start(bf16[1024,256]{1,0:T(8,128)(2,1)} %get-tuple-element.210) | copy-start | bytes 1572868
  138.7 11.0 %collective-permute-start.37 = (bf16[1024,256]{1,0:T(8,128)(2,1)S(1)}, bf16[1024,256]{1,0:T(8,128)(2,1)S(1)}, u32[]{:S(2)}, u32[]{:S(2)}) collective-permute-start(bf16[1024,256]{1,0:T(8,128)(2,1)S(1)} %add_convert_fusion.10), channel_id=1, source_target_pairs={{2,4},{3,5},{4,2},{5,3},{10,12},{11,13},{12,10},{13,11},{18,20},{1... | collective-permute-start | bytes 1572872 | tf_op jit(solution)/shard_map/ppermute | solution.py:195
  143.2 6.5 %collective-permute-start.36 = (bf16[256,512]{1,0:T(8,128)(2,1)S(1)}, bf16[256,512]{1,0:T(8,128)(2,1)S(1)}, u32[]{:S(2)}, u32[]{:S(2)}) collective-permute-start(bf16[256,512]{1,0:T(8,128)(2,1)S(1)} %slice.162), channel_id=1, source_target_pairs={{0,16},{8,24},{16,0},{24,8},{1,17},{9,25},{17,1},{25,9},{2,18},{10... | collective-permute-start | bytes 786440 | tf_op jit(solution)/shard_map/ppermute | solution.py:185
  144.1 6.4 %collective-permute-start.35 = (bf16[256,512]{1,0:T(8,128)(2,1)S(1)}, bf16[256,512]{1,0:T(8,128)(2,1)S(1)}, u32[]{:S(2)}, u32[]{:S(2)}) collective-permute-start(bf16[256,512]{1,0:T(8,128)(2,1)S(1)} %slice.161), channel_id=1, source_target_pairs={{0,8},{8,0},{16,24},{24,16},{1,9},{9,1},{17,25},{25,17},{2,10},{10... | collective-permute-start | bytes 786440 | tf_op jit(solution)/shard_map/ppermute | solution.py:185
  145.4 16.3 %collective-permute-start.34 = (bf16[1024,256]{1,0:T(8,128)(2,1)}, bf16[1024,256]{1,0:T(8,128)(2,1)}, u32[]{:S(2)}, u32[]{:S(2)}) collective-permute-start(bf16[1024,256]{1,0:T(8,128)(2,1)} %broadcast_select_fusion.10), channel_id=1, source_target_pairs={{0,2},{1,3},{2,0},{3,1},{4,6},{5,7},{6,4},{7,5},{8,10},{9,11},{10,... | collective-permute-start | bytes 1572872 | tf_op jit(solution)/shard_map/ppermute | solution.py:195
  148.0 17.3 %collective-permute-start.39 = (bf16[1024,256]{1,0:T(8,128)(2,1)S(1)}, bf16[1024,256]{1,0:T(8,128)(2,1)S(1)}, u32[]{:S(2)}, u32[]{:S(2)}) collective-permute-start(bf16[1024,256]{1,0:T(8,128)(2,1)S(1)} %add_convert_fusion.8), channel_id=1, source_target_pairs={{2,4},{3,5},{4,2},{5,3},{10,12},{11,13},{12,10},{13,11},{18,20},{1... | collective-permute-start | bytes 1572872 | tf_op jit(solution)/shard_map/ppermute | solution.py:195
  157.1 8.5 %copy-start.24 = (f32[2,4,112]{2,0,1:T(2,128)S(1)}, f32[2,4,112]{2,0,1:T(2,128)}, u32[]{:S(2)}) copy-start(f32[2,4,112]{2,0,1:T(2,128)} %select_reduce_fusion) | copy-start | bytes 10756
  158.4 16.1 %collective-permute-start.38 = (bf16[1024,256]{1,0:T(8,128)(2,1)S(1)}, bf16[1024,256]{1,0:T(8,128)(2,1)S(1)}, u32[]{:S(2)}, u32[]{:S(2)}) collective-permute-start(bf16[1024,256]{1,0:T(8,128)(2,1)S(1)} %broadcast_select_fusion.8), channel_id=1, source_target_pairs={{0,2},{1,3},{2,0},{3,1},{4,6},{5,7},{6,4},{7,5},{8,10},{9,11},{10,... | collective-permute-start | bytes 1572872 | tf_op jit(solution)/shard_map/ppermute | solution.py:195
  162.9 13.1 %collective-permute-start.41 = (bf16[1024,256]{1,0:T(8,128)(2,1)S(1)}, bf16[1024,256]{1,0:T(8,128)(2,1)S(1)}, u32[]{:S(2)}, u32[]{:S(2)}) collective-permute-start(bf16[1024,256]{1,0:T(8,128)(2,1)S(1)} %add_convert_fusion.6), channel_id=1, source_target_pairs={{2,4},{3,5},{4,2},{5,3},{10,12},{11,13},{12,10},{13,11},{18,20},{1... | collective-permute-start | bytes 1572872 | tf_op jit(solution)/shard_map/ppermute | solution.py:195
  165.4 9.3 %copy-start.17 = (bf16[1024,256]{1,0:T(8,128)(2,1)S(1)}, bf16[1024,256]{1,0:T(8,128)(2,1)}, u32[]{:S(2)}) copy-start(bf16[1024,256]{1,0:T(8,128)(2,1)} %get-tuple-element.227) | copy-start | bytes 1572868
  165.9 19.4 %collective-permute-start.40 = (bf16[1024,256]{1,0:T(8,128)(2,1)S(1)}, bf16[1024,256]{1,0:T(8,128)(2,1)S(1)}, u32[]{:S(2)}, u32[]{:S(2)}) collective-permute-start(bf16[1024,256]{1,0:T(8,128)(2,1)S(1)} %broadcast_select_fusion.6), channel_id=1, source_target_pairs={{0,2},{1,3},{2,0},{3,1},{4,6},{5,7},{6,4},{7,5},{8,10},{9,11},{10,... | collective-permute-start | bytes 1572872 | tf_op jit(solution)/shard_map/ppermute | solution.py:195
  175.2 11.6 %collective-permute-start.43 = (bf16[1024,256]{1,0:T(8,128)(2,1)S(1)}, bf16[1024,256]{1,0:T(8,128)(2,1)S(1)}, u32[]{:S(2)}, u32[]{:S(2)}) collective-permute-start(bf16[1024,256]{1,0:T(8,128)(2,1)S(1)} %add_convert_fusion.4), channel_id=1, source_target_pairs={{2,4},{3,5},{4,2},{5,3},{10,12},{11,13},{12,10},{13,11},{18,20},{1... | collective-permute-start | bytes 1572872 | tf_op jit(solution)/shard_map/ppermute | solution.py:195
  176.1 20.5 %collective-permute-start.42 = (bf16[1024,256]{1,0:T(8,128)(2,1)S(1)}, bf16[1024,256]{1,0:T(8,128)(2,1)S(1)}, u32[]{:S(2)}, u32[]{:S(2)}) collective-permute-start(bf16[1024,256]{1,0:T(8,128)(2,1)S(1)} %add_convert_fusion.3), channel_id=1, source_target_pairs={{2,0},{3,1},{4,6},{5,7},{10,8},{11,9},{12,14},{13,15},{18,16},{19,... | collective-permute-start | bytes 1572872 | tf_op jit(solution)/shard_map/ppermute | solution.py:195
  186.0 2.2 %collective-permute-start.45 = (bf16[1024,256]{1,0:T(8,128)(2,1)S(1)}, bf16[1024,256]{1,0:T(8,128)(2,1)S(1)}, u32[]{:S(2)}, u32[]{:S(2)}) collective-permute-start(bf16[1024,256]{1,0:T(8,128)(2,1)S(1)} %add_convert_fusion.2), channel_id=1, source_target_pairs={{2,4},{3,5},{4,2},{5,3},{10,12},{11,13},{12,10},{13,11},{18,20},{1... | collective-permute-start | bytes 1572872 | tf_op jit(solution)/shard_map/ppermute | solution.py:195
  186.9 18.4 %collective-permute-start.44 = (bf16[1024,256]{1,0:T(8,128)(2,1)S(1)}, bf16[1024,256]{1,0:T(8,128)(2,1)S(1)}, u32[]{:S(2)}, u32[]{:S(2)}) collective-permute-start(bf16[1024,256]{1,0:T(8,128)(2,1)S(1)} %add_convert_fusion.1), channel_id=1, source_target_pairs={{2,0},{3,1},{4,6},{5,7},{10,8},{11,9},{12,14},{13,15},{18,16},{19,... | collective-permute-start | bytes 1572872 | tf_op jit(solution)/shard_map/ppermute | solution.py:195
  196.9 14.0 %collective-permute-start.46 = (bf16[1024,256]{1,0:T(8,128)(2,1)S(1)}, bf16[1024,256]{1,0:T(8,128)(2,1)S(1)}, u32[]{:S(2)}, u32[]{:S(2)}) collective-permute-start(bf16[1024,256]{1,0:T(8,128)(2,1)S(1)} %add_convert_fusion), channel_id=1, source_target_pairs={{2,0},{3,1},{4,6},{5,7},{10,8},{11,9},{12,14},{13,15},{18,16},{19,... | collective-permute-start | bytes 1572872 | tf_op jit(solution)/shard_map/ppermute | solution.py:195
  198.3 13.2 %collective-permute-start.47 = (bf16[448,1536]{1,0:T(8,128)(2,1)S(1)}, bf16[448,1536]{1,0:T(8,128)(2,1)S(1)}, u32[]{:S(2)}, u32[]{:S(2)}) collective-permute-start(bf16[448,1536]{1,0:T(8,128)(2,1)S(1)} %constant_dynamic-update-slice_fusion), channel_id=1, source_target_pairs={{0,1},{1,0},{2,3},{3,2},{4,5},{5,4},{6,7},{7,6},{8,9},{9,8},{10,11... | collective-permute-start | bytes 4128776 | tf_op jit(solution)/shard_map/ppermute | solution.py:182
  211.4 1.9 collective-permute-start.48
  (20 other events, 58.3 us)

commit v11 on v9

--- a/solution.py
+++ b/solution.py
@@ -9,8 +9,8 @@
 
 EXP_DEV = 1
 GROUPS = ((1,), (1,), (1, 1), (1, 1), (1, 1))
-FIRST_PHASE = {2: 3, 4: 4}
-SECOND_PHASE = {3: 3, 5: 4}
+GATHERED = (3, 4)
+GATHER_AT = {2: 4}
 UNITS = sum(map(sum, GROUPS))
 DELAY = 3
 SWAPS = (6, 8)
@@ -121,10 +121,18 @@
         at += out.shape[1]
 
 
-def matmul(lefts, rights, resid, place, widths):
+def matmul(lefts, rights, resid, place, widths, gathered=0):
     tokens, depth = lefts[0].shape
     width = rights[0].shape[1]
     tile = 2 * resid.shape[0]
+    right_specs = [pl.BlockSpec(right.shape, lambda step, place: (0, 0)) for right in rights]
+    if gathered:
+        rows = rights[0].shape[0] // gathered
+        rights = rights * gathered
+        right_specs = [
+            pl.BlockSpec((rows, width), functools.partial(lambda offset, step, place: (place[1] ^ offset, 0), offset))
+            for offset in range(gathered)
+        ]
     flops = 2 * tokens * depth * len(lefts) * width
     moved = 2 * (tokens * depth * len(lefts) + depth * len(lefts) * width + tokens * width)
     return pl.pallas_call(
@@ -133,7 +141,7 @@
             num_scalar_prefetch=1,
             grid=(tokens // tile,),
             in_specs=[pl.BlockSpec((tile, depth), lambda step, place: (step, 0))] * len(lefts)
-            + [pl.BlockSpec(right.shape, lambda step, place: (0, 0)) for right in rights]
+            + right_specs
             + [pl.BlockSpec(resid.shape, lambda step, place: (0, 0))],
             out_specs=[pl.BlockSpec((tile, part), lambda step, place: (step, 0)) for part in widths],
         ),
@@ -273,7 +281,7 @@
 
     if channels < 128:
         lefts = [jnp.concatenate(lefts, axis=1)]
-    place = chip_at.astype(jnp.int32).reshape(1)
+    place = jnp.stack([chip_at, ctx_at]).astype(jnp.int32)
     pieces = sum(map(len, GROUPS))
     token = [place]
 
@@ -282,14 +290,21 @@
         token[0] = arrays[0]
         return arrays
 
-    def products(group_at, right):
+    def products(group_at):
         group, at = widths[group_at], starts[group_at]
+        right = chain(*rights[group_at])
+        gathered = ctx_count if group_at in GATHERED else 0
         if channels < 128:
             right = [jnp.concatenate(right, axis=0)]
-        right = chain(*right)
-        found = matmul(lefts, right, resid[:, at : at + sum(group)], place, group)
+            if gathered:
+                right = right[0].reshape(ctx_count, -1, sum(group))[ctx_at ^ jnp.arange(ctx_count)]
+                right, gathered = [right.reshape(-1, sum(group))], 0
+        found = matmul(lefts, right, resid[:, at : at + sum(group)], place, group, gathered)
         token[0] = found[0]
         return found
+
+    def gather(group_at):
+        return [lax.all_gather(rest[group_at - 1], "ctx", axis=0, tiled=True)]
 
     middle = chips // 2
     distance = jnp.minimum(chip_at, chips - 1 - chip_at)
@@ -317,8 +332,9 @@
     first_of = [sum(map(len, GROUPS[:at])) for at in range(len(GROUPS))]
     lefts, rest[1] = lax.optimization_barrier((lefts, rest[1]))
     rights.append(spread_near(rest[1]) if square else spread(rest[1]))
-    sums[0][: len(GROUPS[0])] = products(0, rights[0])
     rights += [None] * (len(GROUPS) - len(rights))
+    rights[3] = gather(3)
+    sums[0][: len(GROUPS[0])] = products(0)
     for step in range(pieces + 2 * lag * hops + DELAY + 1):
         for hop in range(hops):
             if (step - 2, hop) not in outer:
@@ -337,15 +353,12 @@
             got, index = across[step - 1]
             own, got = chain(sums[hops][index], got)
             ready[hops][index] = add(own, got)
-        if step in SECOND_PHASE and square:
-            rights[SECOND_PHASE[step]] = spread_on(rights[SECOND_PHASE[step]])
-        group_at = first_of.index(step) if step and step in first_of else None
-        if step in FIRST_PHASE:
-            coming = FIRST_PHASE[step]
-            piece, *rights[group_at] = chain(rest[coming - 1], *rights[group_at])
-            rights[coming] = spread_near(piece) if square else spread(piece)
-        if group_at:
-            sums[0][step : step + len(GROUPS[group_at])] = products(group_at, rights[group_at])
+        if step in GATHER_AT:
+            (rest[GATHER_AT[step] - 1],) = chain(rest[GATHER_AT[step] - 1])
+            rights[GATHER_AT[step]] = gather(GATHER_AT[step])
+        if step and step in first_of:
+            group_at = first_of.index(step)
+            sums[0][step : step + len(GROUPS[group_at])] = products(group_at)
         for hop in range(hops):
             inward = step - lag * hop
             outward = inward - DELAY - 2 * lag * (hops - 1 - hop)

time: 213 us -> 235 us (1.10)
  between operations: 1.3 us -> 14.4 us
  starting transfers between devices: 60.6 us -> 55.8 us
  Pallas kernels: 39.1 us -> 43.1 us
  other arithmetic: 23.4 us -> 26.8 us
  local copies, waits for them, and re-layouts: 22 us -> 25.4 us
  waiting for transfers between devices: 63.3 us -> 66.6 us
    ppermute x21 -> x13, starting transfers between devices: 24.4 us -> 15.7 us  [to_ctx(): lax.ppermute(array, 'ctx', [(place, place ^ offset) for place in range(ct...]
    ppermute x21 -> x13, waiting for transfers between devices: 12.5 us -> 20.9 us  [to_ctx(): lax.ppermute(array, 'ctx', [(place, place ^ offset) for place in range(ct...]
    pallas_call x5, Pallas kernels: 26.3 us -> 30.4 us  [matmul(): pl.pallas_call(functools.partial(matmul_kernel, len(lefts), len(rights)),...]
    ppermute x19, waiting for transfers between devices: 45.3 us -> 41.6 us  [swap_chips(): return lax.ppermute(array, 'exp', sorted(pairs))]
    ppermute x19, starting transfers between devices: 29.8 us -> 33.5 us  [swap_chips(): return lax.ppermute(array, 'exp', sorted(pairs))]
    unnamed x122 -> x88, local copies, waits for them, and re-layouts: 6.72 us -> 9.48 us
  transfers between devices with their start and end apart: 52 -> 46, of which waited for: 20 -> 17; matrix products, arithmetic and copies ran while one was open for 19% -> 20% of each run, Pallas kernels for 18% -> 18%
where the time goes in v11:
time: 235 us; the launch traced here: 234 us
  waiting for transfers between devices  66.6 us (28%)
  starting transfers between devices  55.8 us (24%)
  Pallas kernels  43.1 us (18%)
  other arithmetic  26.8 us (11%)
  local copies, waits for them, and re-layouts  25.4 us (11%)
  between operations  14.4 us (6%)
  matrix products  2.35 us (1%)
    ppermute x19, waiting for transfers between devices, swap_chips(): return lax.ppermute(array, 'exp', sorted(pairs))  41.6 us
    ppermute x19, starting transfers between devices, swap_chips(): return lax.ppermute(array, 'exp', sorted(pairs))  33.5 us
    pallas_call x5, Pallas kernels, matmul(): pl.pallas_call(functools.partial(matmul_kernel, len(lefts), len(rights)),...  30.4 us
    ppermute x13, waiting for transfers between devices, to_ctx(): lax.ppermute(array, 'ctx', [(place, place ^ offset) for place in range(ct...  20.9 us
    ppermute x13, starting transfers between devices, to_ctx(): lax.ppermute(array, 'ctx', [(place, place ^ offset) for place in range(ct...  15.7 us
    pallas_call x1, Pallas kernels, conv_grad(): pl.pallas_call(functools.partial(conv_kernel, tile), grid_spec=pltpu.Pref...  12.7 us
    unnamed x88, local copies, waits for them, and re-layouts  9.48 us
    select_n x5, other arithmetic, on_device(): jnp.where(distance == hop, sums[hop][inward], ready[hop + 1][outward])  7.14 us
  transfers between devices with their start and end apart: 46, of which 17 were waited for; matrix products, arithmetic and copies ran while one was open for 20% of the time, Pallas kernels for 18%

profile of v11, /device:TPU:0, one launch (start us, length us, event | category | flops | bytes accessed | tf_op | source)
XLA Modules:
  0.0 234.4 jit_solution(13446331141262201857)
XLA Ops:
  6.5 1.0 constant_dynamic-slice_fusion.8
  8.0 1.0 collective-permute-done
  9.1 3.9 %collective-permute-start.3 = (bf16[512,256]{1,0:T(8,128)(2,1)S(1)}, bf16[512,256]{1,0:T(8,128)(2,1)S(1)}, u32[]{:S(2)}, u32[]{:S(2)}) collective-permute-start(bf16[512,256]{1,0:T(8,128)(2,1)S(1)} %pad_maximum_fusion.4.refs_8_), channel_id=1, source_target_pairs={{0,24},{8,16},{16,8},{24,0},{1,25},{9,17},{17,9},{25,1},{2,26},{10... | collective-permute-start | bytes 786440 | tf_op jit(solution)/shard_map/ppermute | solution.py:189
  13.6 12.7 %conv_grad.1 = (bf16[1024,256]{1,0:T(8,128)(2,1)}, bf16[1024,256]{1,0:T(8,128)(2,1)}, bf16[1024,256]{1,0:T(8,128)(2,1)}, bf16[1024,256]{1,0:T(8,128)(2,1)}) custom-call(s32[1]{0:T(128)} %bitcast.1.at_ctx, bf16[256,4096]{1,0:T(8,128)(2,1)} %out_grad.1, bf16[256,4096]{1,0:T(8,128)(2,1)} %gate_in.1, bf16[256,4096]{1,0:T(8,128)(2,1)} %conv_in.1, ...), custom_call_target="tpu_custom_call" | custom-call | flops 41943040 | bytes 10485760 | tf_op jit(solution)/shard_map/conv_grad/pallas_call | solution.py:84
  27.3 1.9 collective-permute-start.5
  29.2 1.5 collective-permute-start.6
  30.9 2.3 constant_dynamic-slice_fusion.5
  33.6 2.1 constant_dynamic-slice_fusion.4
  35.7 2.0 collective-permute-start.14
  37.7 2.0 constant_dynamic-slice_fusion.6
  39.8 2.7 %collective-permute-start.15 = (f32[4,4,128]{2,1,0:T(4,128)S(1)}, f32[4,4,128]{2,1,0:T(4,128)S(1)}, u32[]{:S(2)}, u32[]{:S(2)}) collective-permute-start(f32[4,4,128]{2,1,0:T(4,128)S(1)} %pad_maximum_fusion.7), channel_id=1, source_target_pairs={{0,4},{1,5},{2,6},{3,7},{4,0},{5,1},{6,2},{7,3},{8,12},{9,13},{10,... | collective-permute-start | bytes 24584 | tf_op jit(solution)/shard_map/ppermute | solution.py:241
  42.4 0.9 constant_dynamic-slice_fusion.2
  43.3 1.0 collective-permute-done.15
  46.6 2.5 %maximum_select_fusion = bf16[256,2048]{1,0:T(8,128)(2,1)} fusion(bf16[128,2048]{1,0:T(8,128)(2,1)} %collective-permute-done.12, bf16[128,2048]{1,0:T(8,128)(2,1)S(1)} %get-tuple-element.227, pred[]{:T(512)S(6)} %eq.30), kind=kLoop, calls=%fused_computation.27 | loop fusion | flops 4718592 | bytes 2097153 | tf_op jit(solution)/shard_map/jit(_where)/select_n | solution.py:253
  49.2 0.9 slice.148
  50.1 2.5 %collective-permute-start.11 = (bf16[512,256]{1,0:T(8,128)(2,1)S(1)}, bf16[512,256]{1,0:T(8,128)(2,1)S(1)}, u32[]{:S(2)}, u32[]{:S(2)}) collective-permute-start(bf16[512,256]{1,0:T(8,128)(2,1)S(1)} %pad_maximum_fusion.5.refs_8_), channel_id=1, source_target_pairs={{0,24},{8,16},{16,8},{24,0},{1,25},{9,17},{17,9},{25,1},{2,26},{10... | collective-permute-start | bytes 786440 | tf_op jit(solution)/shard_map/ppermute | solution.py:189
  53.2 1.2 fusion.24
  55.8 2.1 pad_maximum_fusion
  57.8 2.4 %collective-permute-done.6.refs_4_ = bf16[1024,256]{1,0:T(8,128)(2,1)S(1)} collective-permute-done((bf16[1024,256]{1,0:T(8,128)(2,1)}, bf16[1024,256]{1,0:T(8,128)(2,1)S(1)}, u32[]{:S(2)}, u32[]{:S(2)}) %collective-permute-start.6) | collective-permute-done | bytes 524320 | tf_op jit(solution)/shard_map/ppermute | solution.py:189
  60.5 5.5 %collective-permute-done.10.refs_10_ = bf16[512,256]{1,0:T(8,128)(2,1)} collective-permute-done((bf16[512,256]{1,0:T(8,128)(2,1)S(1)}, bf16[512,256]{1,0:T(8,128)(2,1)}, u32[]{:S(2)}, u32[]{:S(2)}) %collective-permute-start.10) | collective-permute-done | bytes 262176 | tf_op jit(solution)/shard_map/ppermute | solution.py:189
  66.7 1.7 fusion.23
  69.5 1.5 collective-permute-start.20
  71.6 5.2 %partial_product.5 = bf16[1024,256]{1,0:T(8,128)(2,1)} custom-call(s32[2]{0:T(128)} %get-tuple-element.252.place, bf16[1024,256]{1,0:T(8,128)(2,1)} %get-tuple-element.126.refs_0_, bf16[1024,256]{1,0:T(8,128)(2,1)} %copy-done, bf16[1024,256]{1,0:T(8,128)(2,1)} %copy-done.1, bf16[1024,256]{1,0:T(8,128)(2,1)} %copy-done.4, bf16[1024,256]{1,0:T(8,128)(2,1)} %copy-done.2, ...), custom_call_target="tpu_custom_call" | custom-call | flops 1073741824 | bytes 5767168 | tf_op jit(solution)/shard_map/partial_product/pallas_call | solution.py:138
  76.9 3.7 %collective-permute-start.23 = (bf16[1024,256]{1,0:T(8,128)(2,1)}, bf16[1024,256]{1,0:T(8,128)(2,1)S(1)}, u32[]{:S(2)}, u32[]{:S(2)}) collective-permute-start(bf16[1024,256]{1,0:T(8,128)(2,1)} %partial_product.5), channel_id=1, source_target_pairs={{0,2},{1,3},{6,4},{7,5},{8,10},{9,11},{14,12},{15,13},{16,18},{17,... | collective-permute-start | bytes 1572872 | tf_op jit(solution)/shard_map/ppermute | solution.py:199
  80.6 5.1 %partial_product.6 = bf16[1024,256]{1,0:T(8,128)(2,1)} custom-call(s32[2]{0:T(128)} %get-tuple-element.252.place, bf16[1024,256]{1,0:T(8,128)(2,1)} %get-tuple-element.126.refs_0_, bf16[1024,256]{1,0:T(8,128)(2,1)} %copy-done, bf16[1024,256]{1,0:T(8,128)(2,1)} %copy-done.1, bf16[1024,256]{1,0:T(8,128)(2,1)} %copy-done.4, bf16[1024,256]{1,0:T(8,128)(2,1)} %copy-done.2, ...), custom_call_target="tpu_custom_call" | custom-call | flops 1073741824 | bytes 5767168 | tf_op jit(solution)/shard_map/partial_product/pallas_call | solution.py:138
  85.7 2.1 collective-permute-start.25
  87.8 1.7 collective-permute-done.20.refs_10_
  89.4 1.0 slice.154
  90.7 1.7 slice.155
  92.3 1.0 collective-permute-start.21
  93.3 1.0 collective-permute-start.22
  95.2 0.9 fusion.22
  96.1 10.8 %collective-permute-done.22.refs_12_ = bf16[256,512]{1,0:T(8,128)(2,1)} collective-permute-done((bf16[256,512]{1,0:T(8,128)(2,1)}, bf16[256,512]{1,0:T(8,128)(2,1)}, u32[]{:S(2)}, u32[]{:S(2)}) %collective-permute-start.22) | collective-permute-done | bytes 262176 | tf_op jit(solution)/shard_map/ppermute | solution.py:189
  106.9 6.6 %partial_product.7 = (bf16[1024,256]{1,0:T(8,128)(2,1)}, bf16[1024,256]{1,0:T(8,128)(2,1)}) custom-call(s32[2]{0:T(128)} %get-tuple-element.252.place, bf16[1024,256]{1,0:T(8,128)(2,1)} %get-tuple-element.126.refs_0_, bf16[1024,256]{1,0:T(8,128)(2,1)} %copy-done, bf16[1024,256]{1,0:T(8,128)(2,1)} %copy-done.1, bf16[1024,256]{1,0:T(8,128)(2,1)} %copy-done.4, ...), custom_call_target="tpu_custom_call" | custom-call | flops 2147483648 | bytes 7340032 | tf_op jit(solution)/shard_map/partial_product/pallas_call | solution.py:138
  113.6 4.4 %collective-permute-start.28 = (bf16[1024,256]{1,0:T(8,128)(2,1)}, bf16[1024,256]{1,0:T(8,128)(2,1)S(1)}, u32[]{:S(2)}, u32[]{:S(2)}) collective-permute-start(bf16[1024,256]{1,0:T(8,128)(2,1)} %get-tuple-element.174), channel_id=1, source_target_pairs={{0,2},{1,3},{6,4},{7,5},{8,10},{9,11},{14,12},{15,13},{16,18},{17,... | collective-permute-start | bytes 1572872 | tf_op jit(solution)/shard_map/ppermute | solution.py:199
  118.0 1.2 add_convert_fusion.14
  119.9 2.3 broadcast_select_fusion.13
  122.2 1.0 collective-permute-start.26
  123.2 7.5 %collective-permute-done.28 = bf16[1024,256]{1,0:T(8,128)(2,1)S(1)} collective-permute-done((bf16[1024,256]{1,0:T(8,128)(2,1)}, bf16[1024,256]{1,0:T(8,128)(2,1)S(1)}, u32[]{:S(2)}, u32[]{:S(2)}) %collective-permute-start.28) | collective-permute-done | bytes 524320 | tf_op jit(solution)/shard_map/ppermute | solution.py:199
  130.8 1.4 collective-permute-start.30
  132.2 6.7 %partial_product.8 = (bf16[1024,256]{1,0:T(8,128)(2,1)}, bf16[1024,256]{1,0:T(8,128)(2,1)}) custom-call(s32[2]{0:T(128)} %get-tuple-element.252.place, bf16[1024,256]{1,0:T(8,128)(2,1)} %get-tuple-element.126.refs_0_, bf16[1024,256]{1,0:T(8,128)(2,1)} %copy-done, bf16[1024,256]{1,0:T(8,128)(2,1)} %copy-done.1, bf16[1024,256]{1,0:T(8,128)(2,1)} %copy-done.4, ...), custom_call_target="tpu_custom_call" | custom-call | flops 2147483648 | bytes 7340032 | tf_op jit(solution)/shard_map/partial_product/pallas_call | solution.py:138
  138.9 1.3 broadcast_select_fusion.12
  140.3 3.8 %collective-permute-start.29 = (bf16[1024,256]{1,0:T(8,128)(2,1)S(1)}, bf16[1024,256]{1,0:T(8,128)(2,1)S(1)}, u32[]{:S(2)}, u32[]{:S(2)}) collective-permute-start(bf16[1024,256]{1,0:T(8,128)(2,1)S(1)} %broadcast_select_fusion.12), channel_id=1, source_target_pairs={{0,2},{1,3},{2,0},{3,1},{4,6},{5,7},{6,4},{7,5},{8,10},{9,11},{10,... | collective-permute-start | bytes 1572872 | tf_op jit(solution)/shard_map/ppermute | solution.py:199
  144.1 1.2 add_convert_fusion.10
  146.0 2.1 broadcast_select_fusion.10
  148.1 2.4 %collective-permute-start.31 = (bf16[1024,256]{1,0:T(8,128)(2,1)}, bf16[1024,256]{1,0:T(8,128)(2,1)}, u32[]{:S(2)}, u32[]{:S(2)}) collective-permute-start(bf16[1024,256]{1,0:T(8,128)(2,1)} %broadcast_select_fusion.10), channel_id=1, source_target_pairs={{0,2},{1,3},{2,0},{3,1},{4,6},{5,7},{6,4},{7,5},{8,10},{9,11},{10,... | collective-permute-start | bytes 1572872 | tf_op jit(solution)/shard_map/ppermute | solution.py:199
  150.4 1.2 broadcast_select_fusion.11
  152.7 1.3 collective-permute-done.29
  155.6 1.1 copy-done.28
  157.4 6.8 %partial_product.9 = (bf16[1024,256]{1,0:T(8,128)(2,1)}, bf16[1024,256]{1,0:T(8,128)(2,1)}) custom-call(s32[2]{0:T(128)} %get-tuple-element.252.place, bf16[1024,256]{1,0:T(8,128)(2,1)} %get-tuple-element.126.refs_0_, bf16[1024,256]{1,0:T(8,128)(2,1)} %copy-done, bf16[1024,256]{1,0:T(8,128)(2,1)} %copy-done.1, bf16[1024,256]{1,0:T(8,128)(2,1)} %copy-done.4, ...), custom_call_target="tpu_custom_call" | custom-call | flops 2147483648 | bytes 7340032 | tf_op jit(solution)/shard_map/partial_product/pallas_call | solution.py:138
  164.2 1.3 broadcast_select_fusion.8
  165.5 4.3 %collective-permute-start.33 = (bf16[1024,256]{1,0:T(8,128)(2,1)S(1)}, bf16[1024,256]{1,0:T(8,128)(2,1)S(1)}, u32[]{:S(2)}, u32[]{:S(2)}) collective-permute-start(bf16[1024,256]{1,0:T(8,128)(2,1)S(1)} %broadcast_select_fusion.8), channel_id=1, source_target_pairs={{0,2},{1,3},{2,0},{3,1},{4,6},{5,7},{6,4},{7,5},{8,10},{9,11},{10,... | collective-permute-start | bytes 1572872 | tf_op jit(solution)/shard_map/ppermute | solution.py:199
  169.8 1.2 add_convert_fusion.6
  171.8 1.4 broadcast_select_fusion.7
  173.8 1.3 collective-permute-start.35
  175.9 6.4 %collective-permute-done.33 = bf16[1024,256]{1,0:T(8,128)(2,1)S(1)} collective-permute-done((bf16[1024,256]{1,0:T(8,128)(2,1)S(1)}, bf16[1024,256]{1,0:T(8,128)(2,1)S(1)}, u32[]{:S(2)}, u32[]{:S(2)}) %collective-permute-start.33) | collective-permute-done | bytes 524320 | tf_op jit(solution)/shard_map/ppermute | solution.py:199
  183.4 1.3 collective-permute-start.37
  185.1 8.4 %collective-permute-done.35 = bf16[1024,256]{1,0:T(8,128)(2,1)S(1)} collective-permute-done((bf16[1024,256]{1,0:T(8,128)(2,1)S(1)}, bf16[1024,256]{1,0:T(8,128)(2,1)S(1)}, u32[]{:S(2)}, u32[]{:S(2)}) %collective-permute-start.35) | collective-permute-done | bytes 524320 | tf_op jit(solution)/shard_map/ppermute | solution.py:199
  196.4 1.3 collective-permute-start.39
  197.9 1.3 collective-permute-start.41
  199.2 5.5 %collective-permute-done.37 = bf16[1024,256]{1,0:T(8,128)(2,1)S(1)} collective-permute-done((bf16[1024,256]{1,0:T(8,128)(2,1)S(1)}, bf16[1024,256]{1,0:T(8,128)(2,1)S(1)}, u32[]{:S(2)}, u32[]{:S(2)}) %collective-permute-start.37) | collective-permute-done | bytes 524320 | tf_op jit(solution)/shard_map/ppermute | solution.py:199
  205.9 12.5 %collective-permute-done.41 = bf16[1024,256]{1,0:T(8,128)(2,1)S(1)} collective-permute-done((bf16[1024,256]{1,0:T(8,128)(2,1)S(1)}, bf16[1024,256]{1,0:T(8,128)(2,1)S(1)}, u32[]{:S(2)}, u32[]{:S(2)}) %collective-permute-start.41) | collective-permute-done | bytes 524320 | tf_op jit(solution)/shard_map/ppermute | solution.py:199
  220.8 1.4 bitcast_dynamic-update-slice_fusion
  223.3 4.3 %broadcast_select_fusion = bf16[1,448,4096]{2,1,0:T(8,128)(2,1)} fusion(bf16[1,448,4096]{2,1,0:T(8,128)(2,1)} %get-tuple-element.233, bf16[1,448,4096]{2,1,0:T(8,128)(2,1)S(1)} %constant_dynamic-update-slice_fusion.14, pred[]{:T(512)S(6)} %eq.30), kind=kLoop, calls=%fused_computation | loop fusion | flops 1835008 | bytes 11010049 | tf_op jit(solution)/shard_map/jit(_where)/select_n | solution.py:379
  (210 shorter events, 26.7 us)
Async XLA Ops:
  6.5 125.7 %all-gather.3.cloned.1.call-start = ((), (), s32[]{:S(2)}) async-start(), calls=%async_computation | async-start | bytes 2621440 | tf_op jit(solution)/shard_map/all_gather | solution.py:307
  7.5 1.5 collective-permute-start
  9.1 17.2 %copy-start.20 = (bf16[512,256]{1,0:T(8,128)(2,1)}, bf16[512,256]{1,0:T(8,128)(2,1)S(1)}, u32[]{:S(2)}) copy-start(bf16[512,256]{1,0:T(8,128)(2,1)S(1)} %pad_maximum_fusion.4.refs_8_) | copy-start | bytes 786436
  9.1 17.3 %collective-permute-start.3 = (bf16[512,256]{1,0:T(8,128)(2,1)S(1)}, bf16[512,256]{1,0:T(8,128)(2,1)S(1)}, u32[]{:S(2)}, u32[]{:S(2)}) collective-permute-start(bf16[512,256]{1,0:T(8,128)(2,1)S(1)} %pad_maximum_fusion.4.refs_8_), channel_id=1, source_target_pairs={{0,24},{8,16},{16,8},{24,0},{1,25},{9,17},{17,9},{25,1},{2,26},{10... | collective-permute-start | bytes 786440 | tf_op jit(solution)/shard_map/ppermute | solution.py:189
  12.9 13.4 %collective-permute-start.2 = (bf16[512,256]{1,0:T(8,128)(2,1)S(1)}, bf16[512,256]{1,0:T(8,128)(2,1)S(1)}, u32[]{:S(2)}, u32[]{:S(2)}) collective-permute-start(bf16[512,256]{1,0:T(8,128)(2,1)S(1)} %pad_maximum_fusion.4.refs_8_), channel_id=1, source_target_pairs={{0,16},{8,24},{16,0},{24,8},{1,17},{9,25},{17,1},{25,9},{2,18},{10... | collective-permute-start | bytes 786440 | tf_op jit(solution)/shard_map/ppermute | solution.py:189
  13.4 12.9 %collective-permute-start.1 = (bf16[512,256]{1,0:T(8,128)(2,1)S(1)}, bf16[512,256]{1,0:T(8,128)(2,1)S(1)}, u32[]{:S(2)}, u32[]{:S(2)}) collective-permute-start(bf16[512,256]{1,0:T(8,128)(2,1)S(1)} %pad_maximum_fusion.4.refs_8_), channel_id=1, source_target_pairs={{0,8},{8,0},{16,24},{24,16},{1,9},{9,1},{17,25},{25,17},{2,10},{10... | collective-permute-start | bytes 786440 | tf_op jit(solution)/shard_map/ppermute | solution.py:189
  13.6 17.2 %copy-start.30 = (s32[128,2]{0,1:T(2,128)S(1)}, s32[128,2]{0,1:T(2,128)}, u32[]{:S(2)}) copy-start(s32[128,2]{0,1:T(2,128)} %param.20) | copy-start | bytes 3076
  13.6 17.2 %copy-start.31 = (f32[128,2]{0,1:T(2,128)S(1)}, f32[128,2]{0,1:T(2,128)}, u32[]{:S(2)}) copy-start(f32[128,2]{0,1:T(2,128)} %param.21) | copy-start | bytes 3076
  26.3 19.1 %copy-start.24 = (bf16[512,256]{1,0:T(8,128)(2,1)}, bf16[512,256]{1,0:T(8,128)(2,1)S(1)}, u32[]{:S(2)}) copy-start(bf16[512,256]{1,0:T(8,128)(2,1)S(1)} %collective-permute-done.3.refs_11_) | copy-start | bytes 786436
  26.4 4.4 %collective-permute-start.4 = (bf16[1024,256]{1,0:T(8,128)(2,1)}, bf16[1024,256]{1,0:T(8,128)(2,1)S(1)}, u32[]{:S(2)}, u32[]{:S(2)}) collective-permute-start(bf16[1024,256]{1,0:T(8,128)(2,1)} %get-tuple-element.126.refs_0_), channel_id=1, source_target_pairs={{0,1},{1,0},{2,3},{3,2},{4,5},{5,4},{6,7},{7,6},{8,9},{9,8},{10,11... | collective-permute-start | bytes 1572872 | tf_op jit(solution)/shard_map/ppermute | solution.py:186
  27.3 27.0 %collective-permute-start.5 = (bf16[1024,256]{1,0:T(8,128)(2,1)}, bf16[1024,256]{1,0:T(8,128)(2,1)S(1)}, u32[]{:S(2)}, u32[]{:S(2)}) collective-permute-start(bf16[1024,256]{1,0:T(8,128)(2,1)} %get-tuple-element.116), channel_id=1, source_target_pairs={{0,8},{8,0},{16,24},{24,16},{1,9},{9,1},{17,25},{25,17},{2,10},{10... | collective-permute-start | bytes 1572872 | tf_op jit(solution)/shard_map/ppermute | solution.py:189
  29.2 31.0 %collective-permute-start.6 = (bf16[1024,256]{1,0:T(8,128)(2,1)}, bf16[1024,256]{1,0:T(8,128)(2,1)S(1)}, u32[]{:S(2)}, u32[]{:S(2)}) collective-permute-start(bf16[1024,256]{1,0:T(8,128)(2,1)} %get-tuple-element.117), channel_id=1, source_target_pairs={{0,16},{8,24},{16,0},{24,8},{1,17},{9,25},{17,1},{25,9},{2,18},{10... | collective-permute-start | bytes 1572872 | tf_op jit(solution)/shard_map/ppermute | solution.py:189
  30.7 29.5 %collective-permute-start.7 = (bf16[1024,256]{1,0:T(8,128)(2,1)}, bf16[1024,256]{1,0:T(8,128)(2,1)S(1)}, u32[]{:S(2)}, u32[]{:S(2)}) collective-permute-start(bf16[1024,256]{1,0:T(8,128)(2,1)} %get-tuple-element.118), channel_id=1, source_target_pairs={{0,24},{8,16},{16,8},{24,0},{1,25},{9,17},{17,9},{25,1},{2,26},{10... | collective-permute-start | bytes 1572872 | tf_op jit(solution)/shard_map/ppermute | solution.py:189
  30.8 18.4 %copy-start = (bf16[1024,256]{1,0:T(8,128)(2,1)}, bf16[1024,256]{1,0:T(8,128)(2,1)S(1)}, u32[]{:S(2)}) copy-start(bf16[1024,256]{1,0:T(8,128)(2,1)S(1)} %collective-permute-done.4.refs_1_) | copy-start | bytes 1572868
  30.8 4.8 %collective-permute-start.13 = (f32[1,4,128]{2,1,0:T(4,128)S(1)}, f32[1,4,128]{2,1,0:T(4,128)S(1)}, u32[]{:S(2)}, u32[]{:S(2)}) collective-permute-start(f32[1,4,128]{2,1,0:T(4,128)S(1)} %maximum_bitcast_fusion), channel_id=1, source_target_pairs={{0,1},{1,0},{2,3},{3,2},{4,5},{5,4},{6,7},{7,6},{8,9},{9,8},{10,11... | collective-permute-start | bytes 6152 | tf_op jit(solution)/shard_map/ppermute | solution.py:241
  33.2 16.0 %collective-permute-start.8 = (bf16[256,1792]{1,0:T(8,128)(2,1)}, bf16[256,1792]{1,0:T(8,128)(2,1)}, u32[]{:S(2)}, u32[]{:S(2)}) collective-permute-start(bf16[256,1792]{1,0:T(8,128)(2,1)} %constant_dynamic-slice_fusion.5), channel_id=1, source_target_pairs={{0,1},{1,0},{2,3},{3,2},{4,5},{5,4},{6,7},{7,6},{8,9},{9,8},{10,11... | collective-permute-start | bytes 2752520 | tf_op jit(solution)/shard_map/ppermute | solution.py:186
  35.7 4.1 %collective-permute-start.14 = (f32[2,4,128]{2,1,0:T(4,128)S(1)}, f32[2,4,128]{2,1,0:T(4,128)S(1)}, u32[]{:S(2)}, u32[]{:S(2)}) collective-permute-start(f32[2,4,128]{2,1,0:T(4,128)S(1)} %pad_maximum_fusion.8), channel_id=1, source_target_pairs={{0,2},{1,3},{2,0},{3,1},{4,6},{5,7},{6,4},{7,5},{8,10},{9,11},{10,... | collective-permute-start | bytes 12296 | tf_op jit(solution)/shard_map/ppermute | solution.py:241
  39.8 4.6 %collective-permute-start.15 = (f32[4,4,128]{2,1,0:T(4,128)S(1)}, f32[4,4,128]{2,1,0:T(4,128)S(1)}, u32[]{:S(2)}, u32[]{:S(2)}) collective-permute-start(f32[4,4,128]{2,1,0:T(4,128)S(1)} %pad_maximum_fusion.7), channel_id=1, source_target_pairs={{0,4},{1,5},{2,6},{3,7},{4,0},{5,1},{6,2},{7,3},{8,12},{9,13},{10,... | collective-permute-start | bytes 24584 | tf_op jit(solution)/shard_map/ppermute | solution.py:241
  44.4 2.3 collective-permute-start.12
  45.4 9.6 %copy-start.22 = (bf16[256,512]{1,0:T(8,128)(2,1)S(1)}, bf16[256,512]{1,0:T(8,128)(2,1)}, u32[]{:S(2)}) copy-start(bf16[256,512]{1,0:T(8,128)(2,1)} %get-tuple-element.215) | copy-start | bytes 786436
  50.1 26.8 %copy-start.21 = (bf16[512,256]{1,0:T(8,128)(2,1)}, bf16[512,256]{1,0:T(8,128)(2,1)S(1)}, u32[]{:S(2)}) copy-start(bf16[512,256]{1,0:T(8,128)(2,1)S(1)} %pad_maximum_fusion.5.refs_8_) | copy-start | bytes 786436
  50.1 10.4 %collective-permute-start.11 = (bf16[512,256]{1,0:T(8,128)(2,1)S(1)}, bf16[512,256]{1,0:T(8,128)(2,1)S(1)}, u32[]{:S(2)}, u32[]{:S(2)}) collective-permute-start(bf16[512,256]{1,0:T(8,128)(2,1)S(1)} %pad_maximum_fusion.5.refs_8_), channel_id=1, source_target_pairs={{0,24},{8,16},{16,8},{24,0},{1,25},{9,17},{17,9},{25,1},{2,26},{10... | collective-permute-start | bytes 786440 | tf_op jit(solution)/shard_map/ppermute | solution.py:189
  52.6 13.3 %collective-permute-start.10 = (bf16[512,256]{1,0:T(8,128)(2,1)S(1)}, bf16[512,256]{1,0:T(8,128)(2,1)}, u32[]{:S(2)}, u32[]{:S(2)}) collective-permute-start(bf16[512,256]{1,0:T(8,128)(2,1)S(1)} %pad_maximum_fusion.5.refs_8_), channel_id=1, source_target_pairs={{0,16},{8,24},{16,0},{24,8},{1,17},{9,25},{17,1},{25,9},{2,18},{10... | collective-permute-start | bytes 786440 | tf_op jit(solution)/shard_map/ppermute | solution.py:189
  54.3 17.3 %copy-start.1 = (bf16[1024,256]{1,0:T(8,128)(2,1)}, bf16[1024,256]{1,0:T(8,128)(2,1)S(1)}, u32[]{:S(2)}) copy-start(bf16[1024,256]{1,0:T(8,128)(2,1)S(1)} %collective-permute-done.5.refs_2_) | copy-start | bytes 1572868
  54.3 11.7 %collective-permute-start.9 = (bf16[512,256]{1,0:T(8,128)(2,1)S(1)}, bf16[512,256]{1,0:T(8,128)(2,1)}, u32[]{:S(2)}, u32[]{:S(2)}) collective-permute-start(bf16[512,256]{1,0:T(8,128)(2,1)S(1)} %pad_maximum_fusion.5.refs_8_), channel_id=1, source_target_pairs={{0,8},{8,0},{16,24},{24,16},{1,9},{9,1},{17,25},{25,17},{2,10},{10... | collective-permute-start | bytes 786440 | tf_op jit(solution)/shard_map/ppermute | solution.py:189
  60.2 11.4 %copy-start.2 = (bf16[1024,256]{1,0:T(8,128)(2,1)}, bf16[1024,256]{1,0:T(8,128)(2,1)S(1)}, u32[]{:S(2)}) copy-start(bf16[1024,256]{1,0:T(8,128)(2,1)S(1)} %collective-permute-done.6.refs_4_) | copy-start | bytes 1572868
  60.2 11.4 %copy-start.3 = (bf16[1024,256]{1,0:T(8,128)(2,1)}, bf16[1024,256]{1,0:T(8,128)(2,1)S(1)}, u32[]{:S(2)}) copy-start(bf16[1024,256]{1,0:T(8,128)(2,1)S(1)} %collective-permute-done.7.refs_6_) | copy-start | bytes 1572868
  66.0 91.4 %all-gather.5.cloned.1.call-start = ((), (), s32[]{:S(2)}) async-start(), calls=%async_computation.1 | async-start | bytes 2621440 | tf_op jit(solution)/shard_map/all_gather | solution.py:307
  66.1 2.4 %collective-permute-start.16 = (bf16[1024,256]{1,0:T(8,128)(2,1)S(1)}, bf16[1024,256]{1,0:T(8,128)(2,1)S(1)}, u32[]{:S(2)}, u32[]{:S(2)}) collective-permute-start(bf16[1024,256]{1,0:T(8,128)(2,1)S(1)} %collective-permute-done.5.refs_2_), channel_id=1, source_target_pairs={{0,1},{1,0},{2,3},{3,2},{4,5},{5,4},{6,7},{7,6},{8,9},{9,8},{10,11... | collective-permute-start | bytes 1572872 | tf_op jit(solution)/shard_map/ppermute | solution.py:186
  66.2 2.6 %collective-permute-start.17 = (bf16[1024,256]{1,0:T(8,128)(2,1)S(1)}, bf16[1024,256]{1,0:T(8,128)(2,1)S(1)}, u32[]{:S(2)}, u32[]{:S(2)}) collective-permute-start(bf16[1024,256]{1,0:T(8,128)(2,1)S(1)} %collective-permute-done.6.refs_4_), channel_id=1, source_target_pairs={{0,1},{1,0},{2,3},{3,2},{4,5},{5,4},{6,7},{7,6},{8,9},{9,8},{10,11... | collective-permute-start | bytes 1572872 | tf_op jit(solution)/shard_map/ppermute | solution.py:186
  66.6 2.9 %collective-permute-start.18 = (bf16[1024,256]{1,0:T(8,128)(2,1)S(1)}, bf16[1024,256]{1,0:T(8,128)(2,1)S(1)}, u32[]{:S(2)}, u32[]{:S(2)}) collective-permute-start(bf16[1024,256]{1,0:T(8,128)(2,1)S(1)} %collective-permute-done.7.refs_6_), channel_id=1, source_target_pairs={{0,1},{1,0},{2,3},{3,2},{4,5},{5,4},{6,7},{7,6},{8,9},{9,8},{10,11... | collective-permute-start | bytes 1572872 | tf_op jit(solution)/shard_map/ppermute | solution.py:186
  69.5 19.9 %collective-permute-start.20 = (bf16[512,512]{1,0:T(8,128)(2,1)}, bf16[512,512]{1,0:T(8,128)(2,1)}, u32[]{:S(2)}, u32[]{:S(2)}) collective-permute-start(bf16[512,512]{1,0:T(8,128)(2,1)} %get-tuple-element.160.refs_8_), channel_id=1, source_target_pairs={{0,16},{8,24},{16,0},{24,8},{1,17},{9,25},{17,1},{25,9},{2,18},{10... | collective-permute-start | bytes 1572872 | tf_op jit(solution)/shard_map/ppermute | solution.py:189
  71.1 19.6 %collective-permute-start.19 = (bf16[512,512]{1,0:T(8,128)(2,1)}, bf16[512,512]{1,0:T(8,128)(2,1)}, u32[]{:S(2)}, u32[]{:S(2)}) collective-permute-start(bf16[512,512]{1,0:T(8,128)(2,1)} %get-tuple-element.160.refs_8_), channel_id=1, source_target_pairs={{0,8},{8,0},{16,24},{24,16},{1,9},{9,1},{17,25},{25,17},{2,10},{10... | collective-permute-start | bytes 1572872 | tf_op jit(solution)/shard_map/ppermute | solution.py:189
  76.9 17.5 %copy-start.18 = (bf16[1024,256]{1,0:T(8,128)(2,1)S(1)}, bf16[1024,256]{1,0:T(8,128)(2,1)}, u32[]{:S(2)}) copy-start(bf16[1024,256]{1,0:T(8,128)(2,1)} %partial_product.5) | copy-start | bytes 1572868
  76.9 16.4 %collective-permute-start.23 = (bf16[1024,256]{1,0:T(8,128)(2,1)}, bf16[1024,256]{1,0:T(8,128)(2,1)S(1)}, u32[]{:S(2)}, u32[]{:S(2)}) collective-permute-start(bf16[1024,256]{1,0:T(8,128)(2,1)} %partial_product.5), channel_id=1, source_target_pairs={{0,2},{1,3},{6,4},{7,5},{8,10},{9,11},{14,12},{15,13},{16,18},{17,... | collective-permute-start | bytes 1572872 | tf_op jit(solution)/shard_map/ppermute | solution.py:199
  80.6 14.6 %copy-start.7 = (bf16[256,2048]{1,0:T(8,128)(2,1)S(1)}, bf16[256,2048]{1,0:T(8,128)(2,1)}, u32[]{:S(2)}) copy-start(bf16[256,2048]{1,0:T(8,128)(2,1)} %maximum_select_fusion) | copy-start | bytes 3145732
  85.7 32.3 %collective-permute-start.25 = (bf16[1024,256]{1,0:T(8,128)(2,1)}, bf16[1024,256]{1,0:T(8,128)(2,1)}, u32[]{:S(2)}, u32[]{:S(2)}) collective-permute-start(bf16[1024,256]{1,0:T(8,128)(2,1)} %partial_product.6), channel_id=1, source_target_pairs={{0,2},{1,3},{6,4},{7,5},{8,10},{9,11},{14,12},{15,13},{16,18},{17,... | collective-permute-start | bytes 1572872 | tf_op jit(solution)/shard_map/ppermute | solution.py:199
  92.3 14.6 %collective-permute-start.21 = (bf16[256,512]{1,0:T(8,128)(2,1)S(1)}, bf16[256,512]{1,0:T(8,128)(2,1)}, u32[]{:S(2)}, u32[]{:S(2)}) collective-permute-start(bf16[256,512]{1,0:T(8,128)(2,1)S(1)} %slice.154), channel_id=1, source_target_pairs={{0,8},{8,0},{16,24},{24,16},{1,9},{9,1},{17,25},{25,17},{2,10},{10... | collective-permute-start | bytes 786440 | tf_op jit(solution)/shard_map/ppermute | solution.py:189
  93.3 13.6 %collective-permute-start.22 = (bf16[256,512]{1,0:T(8,128)(2,1)}, bf16[256,512]{1,0:T(8,128)(2,1)}, u32[]{:S(2)}, u32[]{:S(2)}) collective-permute-start(bf16[256,512]{1,0:T(8,128)(2,1)} %slice.155), channel_id=1, source_target_pairs={{0,16},{8,24},{16,0},{24,8},{1,17},{9,25},{17,1},{25,9},{2,18},{10... | collective-permute-start | bytes 786440 | tf_op jit(solution)/shard_map/ppermute | solution.py:189
  94.5 25.4 %collective-permute-start.24 = (bf16[1024,256]{1,0:T(8,128)(2,1)S(1)}, bf16[1024,256]{1,0:T(8,128)(2,1)S(1)}, u32[]{:S(2)}, u32[]{:S(2)}) collective-permute-start(bf16[1024,256]{1,0:T(8,128)(2,1)S(1)} %add_convert_fusion.15), channel_id=1, source_target_pairs={{2,4},{3,5},{4,2},{5,3},{10,12},{11,13},{12,10},{13,11},{18,20},{1... | collective-permute-start | bytes 1572872 | tf_op jit(solution)/shard_map/ppermute | solution.py:199
  106.9 11.1 %copy-start.15 = (bf16[1024,256]{1,0:T(8,128)(2,1)S(1)}, bf16[1024,256]{1,0:T(8,128)(2,1)}, u32[]{:S(2)}) copy-start(bf16[1024,256]{1,0:T(8,128)(2,1)} %partial_product.6) | copy-start | bytes 1572868
  113.5 17.1 %copy-start.23 = (bf16[1024,256]{1,0:T(8,128)(2,1)S(1)}, bf16[1024,256]{1,0:T(8,128)(2,1)}, u32[]{:S(2)}) copy-start(bf16[1024,256]{1,0:T(8,128)(2,1)} %get-tuple-element.174) | copy-start | bytes 1572868
  113.6 17.1 %collective-permute-start.28 = (bf16[1024,256]{1,0:T(8,128)(2,1)}, bf16[1024,256]{1,0:T(8,128)(2,1)S(1)}, u32[]{:S(2)}, u32[]{:S(2)}) collective-permute-start(bf16[1024,256]{1,0:T(8,128)(2,1)} %get-tuple-element.174), channel_id=1, source_target_pairs={{0,2},{1,3},{6,4},{7,5},{8,10},{9,11},{14,12},{15,13},{16,18},{17,... | collective-permute-start | bytes 1572872 | tf_op jit(solution)/shard_map/ppermute | solution.py:199
  119.2 13.0 %collective-permute-start.27 = (bf16[1024,256]{1,0:T(8,128)(2,1)S(1)}, bf16[1024,256]{1,0:T(8,128)(2,1)S(1)}, u32[]{:S(2)}, u32[]{:S(2)}) collective-permute-start(bf16[1024,256]{1,0:T(8,128)(2,1)S(1)} %add_convert_fusion.14), channel_id=1, source_target_pairs={{2,4},{3,5},{4,2},{5,3},{10,12},{11,13},{12,10},{13,11},{18,20},{1... | collective-permute-start | bytes 1572872 | tf_op jit(solution)/shard_map/ppermute | solution.py:199
  122.2 21.9 %collective-permute-start.26 = (bf16[1024,256]{1,0:T(8,128)(2,1)}, bf16[1024,256]{1,0:T(8,128)(2,1)}, u32[]{:S(2)}, u32[]{:S(2)}) collective-permute-start(bf16[1024,256]{1,0:T(8,128)(2,1)} %broadcast_select_fusion.13), channel_id=1, source_target_pairs={{0,2},{1,3},{2,0},{3,1},{4,6},{5,7},{6,4},{7,5},{8,10},{9,11},{10,... | collective-permute-start | bytes 1572872 | tf_op jit(solution)/shard_map/ppermute | solution.py:199
  130.8 15.2 %collective-permute-start.30 = (bf16[1024,256]{1,0:T(8,128)(2,1)S(1)}, bf16[1024,256]{1,0:T(8,128)(2,1)}, u32[]{:S(2)}, u32[]{:S(2)}) collective-permute-start(bf16[1024,256]{1,0:T(8,128)(2,1)S(1)} %add_convert_fusion.12), channel_id=1, source_target_pairs={{2,4},{3,5},{4,2},{5,3},{10,12},{11,13},{12,10},{13,11},{18,20},{1... | collective-permute-start | bytes 1572872 | tf_op jit(solution)/shard_map/ppermute | solution.py:199
  132.2 11.8 %copy-start.16 = (bf16[1024,256]{1,0:T(8,128)(2,1)S(1)}, bf16[1024,256]{1,0:T(8,128)(2,1)}, u32[]{:S(2)}) copy-start(bf16[1024,256]{1,0:T(8,128)(2,1)} %get-tuple-element.185) | copy-start | bytes 1572868
  138.9 11.5 %copy-start.9 = (bf16[1024,256]{1,0:T(8,128)(2,1)S(1)}, bf16[1024,256]{1,0:T(8,128)(2,1)}, u32[]{:S(2)}) copy-start(bf16[1024,256]{1,0:T(8,128)(2,1)} %copy-done.8) | copy-start | bytes 1572868
  140.3 13.7 %collective-permute-start.29 = (bf16[1024,256]{1,0:T(8,128)(2,1)S(1)}, bf16[1024,256]{1,0:T(8,128)(2,1)S(1)}, u32[]{:S(2)}, u32[]{:S(2)}) collective-permute-start(bf16[1024,256]{1,0:T(8,128)(2,1)S(1)} %broadcast_select_fusion.12), channel_id=1, source_target_pairs={{0,2},{1,3},{2,0},{3,1},{4,6},{5,7},{6,4},{7,5},{8,10},{9,11},{10,... | collective-permute-start | bytes 1572872 | tf_op jit(solution)/shard_map/ppermute | solution.py:199
  145.3 12.2 %collective-permute-start.32 = (bf16[1024,256]{1,0:T(8,128)(2,1)S(1)}, bf16[1024,256]{1,0:T(8,128)(2,1)S(1)}, u32[]{:S(2)}, u32[]{:S(2)}) collective-permute-start(bf16[1024,256]{1,0:T(8,128)(2,1)S(1)} %add_convert_fusion.10), channel_id=1, source_target_pairs={{2,4},{3,5},{4,2},{5,3},{10,12},{11,13},{12,10},{13,11},{18,20},{1... | collective-permute-start | bytes 1572872 | tf_op jit(solution)/shard_map/ppermute | solution.py:199
  148.1 21.7 %collective-permute-start.31 = (bf16[1024,256]{1,0:T(8,128)(2,1)}, bf16[1024,256]{1,0:T(8,128)(2,1)}, u32[]{:S(2)}, u32[]{:S(2)}) collective-permute-start(bf16[1024,256]{1,0:T(8,128)(2,1)} %broadcast_select_fusion.10), channel_id=1, source_target_pairs={{0,2},{1,3},{2,0},{3,1},{4,6},{5,7},{6,4},{7,5},{8,10},{9,11},{10,... | collective-permute-start | bytes 1572872 | tf_op jit(solution)/shard_map/ppermute | solution.py:199
  154.7 18.6 %collective-permute-start.34 = (bf16[1024,256]{1,0:T(8,128)(2,1)S(1)}, bf16[1024,256]{1,0:T(8,128)(2,1)S(1)}, u32[]{:S(2)}, u32[]{:S(2)}) collective-permute-start(bf16[1024,256]{1,0:T(8,128)(2,1)S(1)} %add_convert_fusion.8), channel_id=1, source_target_pairs={{2,4},{3,5},{4,2},{5,3},{10,12},{11,13},{12,10},{13,11},{18,20},{1... | collective-permute-start | bytes 1572872 | tf_op jit(solution)/shard_map/ppermute | solution.py:199
  157.4 12.4 %copy-start.11 = (bf16[1024,256]{1,0:T(8,128)(2,1)S(1)}, bf16[1024,256]{1,0:T(8,128)(2,1)}, u32[]{:S(2)}) copy-start(bf16[1024,256]{1,0:T(8,128)(2,1)} %get-tuple-element.198) | copy-start | bytes 1572868
  165.5 16.7 %collective-permute-start.33 = (bf16[1024,256]{1,0:T(8,128)(2,1)S(1)}, bf16[1024,256]{1,0:T(8,128)(2,1)S(1)}, u32[]{:S(2)}, u32[]{:S(2)}) collective-permute-start(bf16[1024,256]{1,0:T(8,128)(2,1)S(1)} %broadcast_select_fusion.8), channel_id=1, source_target_pairs={{0,2},{1,3},{2,0},{3,1},{4,6},{5,7},{6,4},{7,5},{8,10},{9,11},{10,... | collective-permute-start | bytes 1572872 | tf_op jit(solution)/shard_map/ppermute | solution.py:199
  171.0 11.2 %copy-start.17 = (bf16[1024,256]{1,0:T(8,128)(2,1)S(1)}, bf16[1024,256]{1,0:T(8,128)(2,1)}, u32[]{:S(2)}) copy-start(bf16[1024,256]{1,0:T(8,128)(2,1)} %get-tuple-element.203) | copy-start | bytes 1572868
  171.0 12.3 %collective-permute-start.36 = (bf16[1024,256]{1,0:T(8,128)(2,1)S(1)}, bf16[1024,256]{1,0:T(8,128)(2,1)S(1)}, u32[]{:S(2)}, u32[]{:S(2)}) collective-permute-start(bf16[1024,256]{1,0:T(8,128)(2,1)S(1)} %add_convert_fusion.6), channel_id=1, source_target_pairs={{2,4},{3,5},{4,2},{5,3},{10,12},{11,13},{12,10},{13,11},{18,20},{1... | collective-permute-start | bytes 1572872 | tf_op jit(solution)/shard_map/ppermute | solution.py:199
  173.8 19.7 %collective-permute-start.35 = (bf16[1024,256]{1,0:T(8,128)(2,1)S(1)}, bf16[1024,256]{1,0:T(8,128)(2,1)S(1)}, u32[]{:S(2)}, u32[]{:S(2)}) collective-permute-start(bf16[1024,256]{1,0:T(8,128)(2,1)S(1)} %broadcast_select_fusion.6), channel_id=1, source_target_pairs={{0,2},{1,3},{2,0},{3,1},{4,6},{5,7},{6,4},{7,5},{8,10},{9,11},{10,... | collective-permute-start | bytes 1572872 | tf_op jit(solution)/shard_map/ppermute | solution.py:199
  182.4 13.9 %collective-permute-start.38 = (bf16[1024,256]{1,0:T(8,128)(2,1)S(1)}, bf16[1024,256]{1,0:T(8,128)(2,1)S(1)}, u32[]{:S(2)}, u32[]{:S(2)}) collective-permute-start(bf16[1024,256]{1,0:T(8,128)(2,1)S(1)} %add_convert_fusion.4), channel_id=1, source_target_pairs={{2,4},{3,5},{4,2},{5,3},{10,12},{11,13},{12,10},{13,11},{18,20},{1... | collective-permute-start | bytes 1572872 | tf_op jit(solution)/shard_map/ppermute | solution.py:199
  183.4 21.3 %collective-permute-start.37 = (bf16[1024,256]{1,0:T(8,128)(2,1)S(1)}, bf16[1024,256]{1,0:T(8,128)(2,1)S(1)}, u32[]{:S(2)}, u32[]{:S(2)}) collective-permute-start(bf16[1024,256]{1,0:T(8,128)(2,1)S(1)} %add_convert_fusion.3), channel_id=1, source_target_pairs={{2,0},{3,1},{4,6},{5,7},{10,8},{11,9},{12,14},{13,15},{18,16},{19,... | collective-permute-start | bytes 1572872 | tf_op jit(solution)/shard_map/ppermute | solution.py:199
  194.1 3.6 %collective-permute-start.40 = (bf16[1024,256]{1,0:T(8,128)(2,1)S(1)}, bf16[1024,256]{1,0:T(8,128)(2,1)S(1)}, u32[]{:S(2)}, u32[]{:S(2)}) collective-permute-start(bf16[1024,256]{1,0:T(8,128)(2,1)S(1)} %add_convert_fusion.2), channel_id=1, source_target_pairs={{2,4},{3,5},{4,2},{5,3},{10,12},{11,13},{12,10},{13,11},{18,20},{1... | collective-permute-start | bytes 1572872 | tf_op jit(solution)/shard_map/ppermute | solution.py:199
  196.4 22.4 %collective-permute-start.39 = (bf16[1024,256]{1,0:T(8,128)(2,1)S(1)}, bf16[1024,256]{1,0:T(8,128)(2,1)S(1)}, u32[]{:S(2)}, u32[]{:S(2)}) collective-permute-start(bf16[1024,256]{1,0:T(8,128)(2,1)S(1)} %add_convert_fusion.1), channel_id=1, source_target_pairs={{2,0},{3,1},{4,6},{5,7},{10,8},{11,9},{12,14},{13,15},{18,16},{19,... | collective-permute-start | bytes 1572872 | tf_op jit(solution)/shard_map/ppermute | solution.py:199
  197.9 20.6 %collective-permute-start.41 = (bf16[1024,256]{1,0:T(8,128)(2,1)S(1)}, bf16[1024,256]{1,0:T(8,128)(2,1)S(1)}, u32[]{:S(2)}, u32[]{:S(2)}) collective-permute-start(bf16[1024,256]{1,0:T(8,128)(2,1)S(1)} %add_convert_fusion), channel_id=1, source_target_pairs={{2,0},{3,1},{4,6},{5,7},{10,8},{11,9},{12,14},{13,15},{18,16},{19,... | collective-permute-start | bytes 1572872 | tf_op jit(solution)/shard_map/ppermute | solution.py:199
  205.1 15.7 %collective-permute-start.42 = (bf16[448,1536]{1,0:T(8,128)(2,1)S(1)}, bf16[448,1536]{1,0:T(8,128)(2,1)S(1)}, u32[]{:S(2)}, u32[]{:S(2)}) collective-permute-start(bf16[448,1536]{1,0:T(8,128)(2,1)S(1)} %constant_dynamic-update-slice_fusion), channel_id=1, source_target_pairs={{0,1},{1,0},{2,3},{3,2},{4,5},{5,4},{6,7},{7,6},{8,9},{9,8},{10,11... | collective-permute-start | bytes 4128776 | tf_op jit(solution)/shard_map/ppermute | solution.py:186
  219.3 2.9 %collective-permute-start.43 = (bf16[448,512]{1,0:T(8,128)(2,1)S(1)}, bf16[448,512]{1,0:T(8,128)(2,1)S(1)}, u32[]{:S(2)}, u32[]{:S(2)}) collective-permute-start(bf16[448,512]{1,0:T(8,128)(2,1)S(1)} %pad_maximum_fusion.3), channel_id=1, source_target_pairs={{0,1},{1,0},{2,3},{3,2},{4,5},{5,4},{6,7},{7,6},{8,9},{9,8},{10,11... | collective-permute-start | bytes 1376264 | tf_op jit(solution)/shard_map/ppermute | solution.py:186
  (14 other events, 60.9 us)
Sparse Core Ops, SparseCore 0:
  66.1 46.1 all-gather.2
  114.1 35.8 all-gather.4

commit v12 on v9

--- a/solution.py
+++ b/solution.py
@@ -200,10 +200,9 @@
     def spread_near(piece):
         return [piece, to_ctx(piece, 1), to_ctx(piece, 2)]
 
-    def spread_on(near):
-        cut = near[0].shape[0] // 2
-        low, high = chain(near[2][:cut], near[1][cut:])
-        return near + [to_ctx(low, 1), to_ctx(high, 2)]
+    def spread_far(near):
+        (piece,) = chain(near[0])
+        return near + [to_ctx(piece, 3)]
 
     def spread(piece):
         return [piece] + [to_ctx(piece, offset) for offset in range(1, ctx_count)]
@@ -338,7 +337,7 @@
             own, got = chain(sums[hops][index], got)
             ready[hops][index] = add(own, got)
         if step in SECOND_PHASE and square:
-            rights[SECOND_PHASE[step]] = spread_on(rights[SECOND_PHASE[step]])
+            rights[SECOND_PHASE[step]] = spread_far(rights[SECOND_PHASE[step]])
         group_at = first_of.index(step) if step and step in first_of else None
         if step in FIRST_PHASE:
             coming = FIRST_PHASE[step]
@@ -361,8 +360,8 @@
                 continue
             (payload,) = chain(payload)
             outer[step, hop] = (swap_chips(payload, hop, inward is not None, outward is not None), inward, outward)
-        if step == 1 and square:
-            rights[2] = spread_on(rights[2])
+        if step == 0 and square:
+            rights[2] = spread_far(rights[2])
     result = jnp.where(
         core_at == 0,
         jnp.concatenate(rows_own + rows_got, axis=1),

time: 213 us -> 220 us (1.033)
  waiting for transfers between devices: 63.3 us -> 84 us
  starting transfers between devices: 60.6 us -> 53.9 us
  local copies, waits for them, and re-layouts: 22 us -> 17.5 us
  other arithmetic: 23.4 us -> 20.5 us
    ppermute x21 -> x18, waiting for transfers between devices: 12.5 us -> 24.7 us  [to_ctx(): lax.ppermute(array, 'ctx', [(place, place ^ offset) for place in range(ct...]
    ppermute x19, waiting for transfers between devices: 45.3 us -> 53.8 us  [swap_chips(): return lax.ppermute(array, 'exp', sorted(pairs))]
    ppermute x19, starting transfers between devices: 29.8 us -> 25.3 us  [swap_chips(): return lax.ppermute(array, 'exp', sorted(pairs))]
    slice x6 -> x0, local copies, waits for them, and re-layouts: 3.91 us -> none  [spread_on(): low, high = chain(near[2][:cut], near[1][cut:])]
    convert_element_type x11, other arithmetic: 5.62 us -> 2.49 us  [add(): (one.astype(jnp.float32) + other.astype(jnp.float32)).astype(jnp.bfloat16)]
    ppermute x21 -> x18, starting transfers between devices: 24.4 us -> 22.2 us  [to_ctx(): lax.ppermute(array, 'ctx', [(place, place ^ offset) for place in range(ct...]
    unnamed x122 -> x100, local copies, waits for them, and re-layouts: 6.72 us -> 6.1 us
  transfers between devices with their start and end apart: 52 -> 49, of which waited for: 20 -> 20; matrix products, arithmetic and copies ran while one was open for 19% -> 15% of each run, Pallas kernels for 18% -> 16%
where the time goes in v12:
time: 220 us; the launch traced here: 219 us
  waiting for transfers between devices  84 us (38%)
  starting transfers between devices  53.9 us (24%)
  Pallas kernels  39.1 us (18%)
  other arithmetic  20.5 us (9%)
  local copies, waits for them, and re-layouts  17.5 us (8%)
  matrix products  3.01 us (1%)
    ppermute x19, waiting for transfers between devices, swap_chips(): return lax.ppermute(array, 'exp', sorted(pairs))  53.8 us
    pallas_call x5, Pallas kernels, matmul(): pl.pallas_call(functools.partial(matmul_kernel, len(lefts), len(rights)),...  26.3 us
    ppermute x19, starting transfers between devices, swap_chips(): return lax.ppermute(array, 'exp', sorted(pairs))  25.3 us
    ppermute x18, waiting for transfers between devices, to_ctx(): lax.ppermute(array, 'ctx', [(place, place ^ offset) for place in range(ct...  24.7 us
    ppermute x18, starting transfers between devices, to_ctx(): lax.ppermute(array, 'ctx', [(place, place ^ offset) for place in range(ct...  22.2 us
    pallas_call x1, Pallas kernels, conv_grad(): pl.pallas_call(functools.partial(conv_kernel, tile), grid_spec=pltpu.Pref...  12.9 us
    select_n x5, other arithmetic, on_device(): jnp.where(distance == hop, sums[hop][inward], ready[hop + 1][outward])  6.86 us
    unnamed x100, local copies, waits for them, and re-layouts  6.1 us
  transfers between devices with their start and end apart: 49, of which 20 were waited for; matrix products, arithmetic and copies ran while one was open for 15% of the time, Pallas kernels for 16%

profile of v12, /device:TPU:0, one launch (start us, length us, event | category | flops | bytes accessed | tf_op | source)
XLA Modules:
  0.0 219.3 jit_solution(13740531132917428239)
XLA Ops:
  0.0 1.0 constant_dynamic-slice_fusion.8
  1.5 1.0 collective-permute-done
  2.5 3.9 %collective-permute-start.3 = (bf16[512,256]{1,0:T(8,128)(2,1)S(1)}, bf16[512,256]{1,0:T(8,128)(2,1)S(1)}, u32[]{:S(2)}, u32[]{:S(2)}) collective-permute-start(bf16[512,256]{1,0:T(8,128)(2,1)S(1)} %pad_maximum_fusion.4.refs_8_), channel_id=1, source_target_pairs={{0,24},{8,16},{16,8},{24,0},{1,25},{9,17},{17,9},{25,1},{2,26},{10... | collective-permute-start | bytes 786440 | tf_op jit(solution)/shard_map/ppermute | solution.py:181
  7.0 12.9 %conv_grad.1 = (bf16[1024,256]{1,0:T(8,128)(2,1)}, bf16[1024,256]{1,0:T(8,128)(2,1)}, bf16[1024,256]{1,0:T(8,128)(2,1)}, bf16[1024,256]{1,0:T(8,128)(2,1)}) custom-call(s32[1]{0:T(128)} %bitcast.1.at_ctx, bf16[256,4096]{1,0:T(8,128)(2,1)} %out_grad.1, bf16[256,4096]{1,0:T(8,128)(2,1)} %gate_in.1, bf16[256,4096]{1,0:T(8,128)(2,1)} %conv_in.1, ...), custom_call_target="tpu_custom_call" | custom-call | flops 41943040 | bytes 10485760 | tf_op jit(solution)/shard_map/conv_grad/pallas_call | solution.py:84
  20.9 1.9 collective-permute-start.5
  22.8 1.5 collective-permute-start.6
  24.5 2.2 %constant_dynamic-slice_fusion.5 = bf16[256,1792]{1,0:T(8,128)(2,1)} fusion(bf16[256,4096]{1,0:T(8,128)(2,1)} %param.18, s32[]{:T(128)S(6)} %select_n.141), kind=kLoop, calls=%fused_computation.106 | loop fusion | bytes 1835012 | tf_op jit(solution)/shard_map/dynamic_slice | solution.py:194
  27.2 1.1 constant_dynamic-slice_fusion.4
  28.2 2.0 collective-permute-start.14
  30.3 2.0 constant_dynamic-slice_fusion.6
  32.3 2.7 %collective-permute-start.15 = (f32[4,4,128]{2,1,0:T(4,128)S(1)}, f32[4,4,128]{2,1,0:T(4,128)S(1)}, u32[]{:S(2)}, u32[]{:S(2)}) collective-permute-start(f32[4,4,128]{2,1,0:T(4,128)S(1)} %pad_maximum_fusion.7), channel_id=1, source_target_pairs={{0,4},{1,5},{2,6},{3,7},{4,0},{5,1},{6,2},{7,3},{8,12},{9,13},{10,... | collective-permute-start | bytes 24584 | tf_op jit(solution)/shard_map/ppermute | solution.py:232
  35.9 1.0 collective-permute-done.15
  39.8 2.0 maximum_select_fusion
  41.9 0.9 slice.140
  42.9 2.5 %collective-permute-start.11 = (bf16[512,256]{1,0:T(8,128)(2,1)S(1)}, bf16[512,256]{1,0:T(8,128)(2,1)S(1)}, u32[]{:S(2)}, u32[]{:S(2)}) collective-permute-start(bf16[512,256]{1,0:T(8,128)(2,1)S(1)} %pad_maximum_fusion.5.refs_8_), channel_id=1, source_target_pairs={{0,24},{8,16},{16,8},{24,0},{1,25},{9,17},{17,9},{25,1},{2,26},{10... | collective-permute-start | bytes 786440 | tf_op jit(solution)/shard_map/ppermute | solution.py:181
  45.9 1.2 fusion.24
  48.5 1.1 pad_maximum_fusion
  49.6 3.6 %collective-permute-done.6.refs_4_ = bf16[1024,256]{1,0:T(8,128)(2,1)S(1)} collective-permute-done((bf16[1024,256]{1,0:T(8,128)(2,1)}, bf16[1024,256]{1,0:T(8,128)(2,1)S(1)}, u32[]{:S(2)}, u32[]{:S(2)}) %collective-permute-start.6) | collective-permute-done | bytes 524320 | tf_op jit(solution)/shard_map/ppermute | solution.py:181
  53.7 5.2 %collective-permute-done.10.refs_10_ = bf16[512,256]{1,0:T(8,128)(2,1)S(1)} collective-permute-done((bf16[512,256]{1,0:T(8,128)(2,1)S(1)}, bf16[512,256]{1,0:T(8,128)(2,1)S(1)}, u32[]{:S(2)}, u32[]{:S(2)}) %collective-permute-start.10) | collective-permute-done | bytes 262176 | tf_op jit(solution)/shard_map/ppermute | solution.py:181
  60.9 1.6 collective-permute-done.17.refs_5_
  62.8 4.3 %partial_product.5 = bf16[1024,256]{1,0:T(8,128)(2,1)} custom-call(s32[1]{0:T(128)} %bitcast.place, bf16[1024,256]{1,0:T(8,128)(2,1)} %get-tuple-element.141.refs_0_, bf16[1024,256]{1,0:T(8,128)(2,1)} %copy-done.1, bf16[1024,256]{1,0:T(8,128)(2,1)} %copy-done.2, bf16[1024,256]{1,0:T(8,128)(2,1)} %copy-done.4, bf16[1024,256]{1,0:T(8,128)(2,1)} %copy-done.3, ...), custom_call_target="tpu_custom_call" | custom-call | flops 1073741824 | bytes 5767168 | tf_op jit(solution)/shard_map/partial_product/pallas_call | solution.py:130
  67.1 4.4 %collective-permute-start.22 = (bf16[1024,256]{1,0:T(8,128)(2,1)}, bf16[1024,256]{1,0:T(8,128)(2,1)}, u32[]{:S(2)}, u32[]{:S(2)}) collective-permute-start(bf16[1024,256]{1,0:T(8,128)(2,1)} %partial_product.5), channel_id=1, source_target_pairs={{0,2},{1,3},{6,4},{7,5},{8,10},{9,11},{14,12},{15,13},{16,18},{17,... | collective-permute-start | bytes 1572872 | tf_op jit(solution)/shard_map/ppermute | solution.py:191
  71.5 1.5 collective-permute-start.20
  73.6 1.4 collective-permute-start.21
  75.0 4.3 %partial_product.6 = bf16[1024,256]{1,0:T(8,128)(2,1)} custom-call(s32[1]{0:T(128)} %bitcast.place, bf16[1024,256]{1,0:T(8,128)(2,1)} %get-tuple-element.141.refs_0_, bf16[1024,256]{1,0:T(8,128)(2,1)} %copy-done.1, bf16[1024,256]{1,0:T(8,128)(2,1)} %copy-done.2, bf16[1024,256]{1,0:T(8,128)(2,1)} %copy-done.4, bf16[1024,256]{1,0:T(8,128)(2,1)} %copy-done.3, ...), custom_call_target="tpu_custom_call" | custom-call | flops 1073741824 | bytes 5767168 | tf_op jit(solution)/shard_map/partial_product/pallas_call | solution.py:130
  79.3 1.3 collective-permute-start.24
  80.6 2.7 %collective-permute-done.22 = bf16[1024,256]{1,0:T(8,128)(2,1)} collective-permute-done((bf16[1024,256]{1,0:T(8,128)(2,1)}, bf16[1024,256]{1,0:T(8,128)(2,1)}, u32[]{:S(2)}, u32[]{:S(2)}) %collective-permute-start.22) | collective-permute-done | bytes 524320 | tf_op jit(solution)/shard_map/ppermute | solution.py:191
  83.3 1.2 add_convert_fusion.15
  85.2 0.9 fusion.22
  86.1 11.8 %collective-permute-done.21.refs_11_ = bf16[512,512]{1,0:T(8,128)(2,1)} collective-permute-done((bf16[512,512]{1,0:T(8,128)(2,1)}, bf16[512,512]{1,0:T(8,128)(2,1)}, u32[]{:S(2)}, u32[]{:S(2)}) %collective-permute-start.21) | collective-permute-done | bytes 524320 | tf_op jit(solution)/shard_map/ppermute | solution.py:181
  97.9 1.5 collective-permute-start.27
  100.0 5.9 %partial_product.7 = (bf16[1024,256]{1,0:T(8,128)(2,1)}, bf16[1024,256]{1,0:T(8,128)(2,1)}) custom-call(s32[1]{0:T(128)} %bitcast.place, bf16[1024,256]{1,0:T(8,128)(2,1)} %get-tuple-element.141.refs_0_, bf16[1024,256]{1,0:T(8,128)(2,1)} %copy-done.1, bf16[1024,256]{1,0:T(8,128)(2,1)} %copy-done.2, bf16[1024,256]{1,0:T(8,128)(2,1)} %copy-done.4, ...), custom_call_target="tpu_custom_call" | custom-call | flops 2147483648 | bytes 7340032 | tf_op jit(solution)/shard_map/partial_product/pallas_call | solution.py:130
  105.9 1.5 collective-permute-start.30
  108.2 1.5 collective-permute-start.28
  109.7 2.0 broadcast_select_fusion.13
  111.8 5.6 %collective-permute-done.30 = bf16[1024,256]{1,0:T(8,128)(2,1)S(1)} collective-permute-done((bf16[1024,256]{1,0:T(8,128)(2,1)}, bf16[1024,256]{1,0:T(8,128)(2,1)S(1)}, u32[]{:S(2)}, u32[]{:S(2)}) %collective-permute-start.30) | collective-permute-done | bytes 524320 | tf_op jit(solution)/shard_map/ppermute | solution.py:191
  117.3 2.4 %collective-permute-start.25 = (bf16[1024,256]{1,0:T(8,128)(2,1)}, bf16[1024,256]{1,0:T(8,128)(2,1)S(1)}, u32[]{:S(2)}, u32[]{:S(2)}) collective-permute-start(bf16[1024,256]{1,0:T(8,128)(2,1)} %broadcast_select_fusion.13), channel_id=1, source_target_pairs={{0,2},{1,3},{2,0},{3,1},{4,6},{5,7},{6,4},{7,5},{8,10},{9,11},{10,... | collective-permute-start | bytes 1572872 | tf_op jit(solution)/shard_map/ppermute | solution.py:191
  120.6 2.6 %collective-permute-done.28.refs_11_ = bf16[512,512]{1,0:T(8,128)(2,1)} collective-permute-done((bf16[512,512]{1,0:T(8,128)(2,1)}, bf16[512,512]{1,0:T(8,128)(2,1)}, u32[]{:S(2)}, u32[]{:S(2)}) %collective-permute-start.28) | collective-permute-done | bytes 524320 | tf_op jit(solution)/shard_map/ppermute | solution.py:181
  123.2 1.5 collective-permute-start.35
  125.2 5.9 %partial_product.8 = (bf16[1024,256]{1,0:T(8,128)(2,1)}, bf16[1024,256]{1,0:T(8,128)(2,1)}) custom-call(s32[1]{0:T(128)} %bitcast.place, bf16[1024,256]{1,0:T(8,128)(2,1)} %get-tuple-element.141.refs_0_, bf16[1024,256]{1,0:T(8,128)(2,1)} %copy-done.1, bf16[1024,256]{1,0:T(8,128)(2,1)} %copy-done.2, bf16[1024,256]{1,0:T(8,128)(2,1)} %copy-done.4, ...), custom_call_target="tpu_custom_call" | custom-call | flops 2147483648 | bytes 7340032 | tf_op jit(solution)/shard_map/partial_product/pallas_call | solution.py:130
  131.1 1.3 broadcast_select_fusion.12
  134.0 1.5 collective-permute-start.36
  135.5 1.0 broadcast_select_fusion.10
  137.9 6.5 %collective-permute-done.31 = bf16[1024,256]{1,0:T(8,128)(2,1)S(1)} collective-permute-done((bf16[1024,256]{1,0:T(8,128)(2,1)S(1)}, bf16[1024,256]{1,0:T(8,128)(2,1)S(1)}, u32[]{:S(2)}, u32[]{:S(2)}) %collective-permute-start.31) | collective-permute-done | bytes 524320 | tf_op jit(solution)/shard_map/ppermute | solution.py:191
  144.6 1.5 collective-permute-start.39
  146.1 1.0 broadcast_select_fusion.9
  147.1 1.0 collective-permute-done.36.refs_11_
  148.9 5.9 %partial_product.9 = (bf16[1024,256]{1,0:T(8,128)(2,1)}, bf16[1024,256]{1,0:T(8,128)(2,1)}) custom-call(s32[1]{0:T(128)} %bitcast.place, bf16[1024,256]{1,0:T(8,128)(2,1)} %get-tuple-element.141.refs_0_, bf16[1024,256]{1,0:T(8,128)(2,1)} %copy-done.1, bf16[1024,256]{1,0:T(8,128)(2,1)} %copy-done.2, bf16[1024,256]{1,0:T(8,128)(2,1)} %copy-done.4, ...), custom_call_target="tpu_custom_call" | custom-call | flops 2147483648 | bytes 7340032 | tf_op jit(solution)/shard_map/partial_product/pallas_call | solution.py:130
  154.8 1.3 broadcast_select_fusion.8
  156.1 4.1 %collective-permute-start.38 = (bf16[1024,256]{1,0:T(8,128)(2,1)S(1)}, bf16[1024,256]{1,0:T(8,128)(2,1)S(1)}, u32[]{:S(2)}, u32[]{:S(2)}) collective-permute-start(bf16[1024,256]{1,0:T(8,128)(2,1)S(1)} %broadcast_select_fusion.8), channel_id=1, source_target_pairs={{0,2},{1,3},{2,0},{3,1},{4,6},{5,7},{6,4},{7,5},{8,10},{9,11},{10,... | collective-permute-start | bytes 1572872 | tf_op jit(solution)/shard_map/ppermute | solution.py:191
  160.2 1.0 fusion.9
  163.7 1.2 broadcast_select_fusion.6
  165.0 1.1 collective-permute-start.40
  166.1 7.0 %collective-permute-done.38 = bf16[1024,256]{1,0:T(8,128)(2,1)S(1)} collective-permute-done((bf16[1024,256]{1,0:T(8,128)(2,1)S(1)}, bf16[1024,256]{1,0:T(8,128)(2,1)S(1)}, u32[]{:S(2)}, u32[]{:S(2)}) %collective-permute-start.38) | collective-permute-done | bytes 524320 | tf_op jit(solution)/shard_map/ppermute | solution.py:191
  174.5 1.3 collective-permute-start.42
  175.9 8.4 %collective-permute-done.40 = bf16[1024,256]{1,0:T(8,128)(2,1)S(1)} collective-permute-done((bf16[1024,256]{1,0:T(8,128)(2,1)S(1)}, bf16[1024,256]{1,0:T(8,128)(2,1)S(1)}, u32[]{:S(2)}, u32[]{:S(2)}) %collective-permute-start.40) | collective-permute-done | bytes 524320 | tf_op jit(solution)/shard_map/ppermute | solution.py:191
  184.3 1.2 broadcast_select_fusion.4
  186.7 4.4 %collective-permute-done.42 = bf16[1024,256]{1,0:T(8,128)(2,1)S(1)} collective-permute-done((bf16[1024,256]{1,0:T(8,128)(2,1)S(1)}, bf16[1024,256]{1,0:T(8,128)(2,1)S(1)}, u32[]{:S(2)}, u32[]{:S(2)}) %collective-permute-start.42) | collective-permute-done | bytes 524320 | tf_op jit(solution)/shard_map/ppermute | solution.py:191
  191.7 1.3 collective-permute-start.44
  193.3 1.3 collective-permute-start.46
  194.6 12.9 %collective-permute-done.44 = bf16[1024,256]{1,0:T(8,128)(2,1)S(1)} collective-permute-done((bf16[1024,256]{1,0:T(8,128)(2,1)S(1)}, bf16[1024,256]{1,0:T(8,128)(2,1)S(1)}, u32[]{:S(2)}, u32[]{:S(2)}) %collective-permute-start.44) | collective-permute-done | bytes 524320 | tf_op jit(solution)/shard_map/ppermute | solution.py:191
  208.0 6.4 %collective-permute-done.46 = bf16[1024,256]{1,0:T(8,128)(2,1)S(1)} collective-permute-done((bf16[1024,256]{1,0:T(8,128)(2,1)S(1)}, bf16[1024,256]{1,0:T(8,128)(2,1)S(1)}, u32[]{:S(2)}, u32[]{:S(2)}) %collective-permute-start.46) | collective-permute-done | bytes 524320 | tf_op jit(solution)/shard_map/ppermute | solution.py:191
  215.2 1.4 collective-permute-done.48
  217.0 2.2 %broadcast_select_fusion = bf16[1,448,4096]{2,1,0:T(8,128)(2,1)} fusion(bf16[1,448,4096]{2,1,0:T(8,128)(2,1)S(1)} %get-tuple-element.263, bf16[1,448,4096]{2,1,0:T(8,128)(2,1)S(1)} %constant_dynamic-update-slice_fusion.14, pred[]{:T(512)S(6)} %eq.30), kind=kLoop, calls=%fused_computation | loop fusion | flops 1835008 | bytes 11010049 | tf_op jit(solution)/shard_map/jit(_where)/select_n | solution.py:365
  (224 shorter events, 26.4 us)
Async XLA Ops:
  1.0 1.5 collective-permute-start
  2.5 17.4 %copy-start.18 = (bf16[512,256]{1,0:T(8,128)(2,1)}, bf16[512,256]{1,0:T(8,128)(2,1)S(1)}, u32[]{:S(2)}) copy-start(bf16[512,256]{1,0:T(8,128)(2,1)S(1)} %pad_maximum_fusion.4.refs_8_) | copy-start | bytes 786436
  2.5 17.4 %collective-permute-start.3 = (bf16[512,256]{1,0:T(8,128)(2,1)S(1)}, bf16[512,256]{1,0:T(8,128)(2,1)S(1)}, u32[]{:S(2)}, u32[]{:S(2)}) collective-permute-start(bf16[512,256]{1,0:T(8,128)(2,1)S(1)} %pad_maximum_fusion.4.refs_8_), channel_id=1, source_target_pairs={{0,24},{8,16},{16,8},{24,0},{1,25},{9,17},{17,9},{25,1},{2,26},{10... | collective-permute-start | bytes 786440 | tf_op jit(solution)/shard_map/ppermute | solution.py:181
  6.4 13.6 %collective-permute-start.2 = (bf16[512,256]{1,0:T(8,128)(2,1)S(1)}, bf16[512,256]{1,0:T(8,128)(2,1)S(1)}, u32[]{:S(2)}, u32[]{:S(2)}) collective-permute-start(bf16[512,256]{1,0:T(8,128)(2,1)S(1)} %pad_maximum_fusion.4.refs_8_), channel_id=1, source_target_pairs={{0,16},{8,24},{16,0},{24,8},{1,17},{9,25},{17,1},{25,9},{2,18},{10... | collective-permute-start | bytes 786440 | tf_op jit(solution)/shard_map/ppermute | solution.py:181
  6.9 13.1 %collective-permute-start.1 = (bf16[512,256]{1,0:T(8,128)(2,1)S(1)}, bf16[512,256]{1,0:T(8,128)(2,1)S(1)}, u32[]{:S(2)}, u32[]{:S(2)}) collective-permute-start(bf16[512,256]{1,0:T(8,128)(2,1)S(1)} %pad_maximum_fusion.4.refs_8_), channel_id=1, source_target_pairs={{0,8},{8,0},{16,24},{24,16},{1,9},{9,1},{17,25},{25,17},{2,10},{10... | collective-permute-start | bytes 786440 | tf_op jit(solution)/shard_map/ppermute | solution.py:181
  7.0 17.3 %copy-start.35 = (s32[128,2]{0,1:T(2,128)S(1)}, s32[128,2]{0,1:T(2,128)}, u32[]{:S(2)}) copy-start(s32[128,2]{0,1:T(2,128)} %param.20) | copy-start | bytes 3076
  7.0 17.4 %copy-start.36 = (f32[128,2]{0,1:T(2,128)S(1)}, f32[128,2]{0,1:T(2,128)}, u32[]{:S(2)}) copy-start(f32[128,2]{0,1:T(2,128)} %param.21) | copy-start | bytes 3076
  7.0 20.1 %copy-start.21 = (bf16[128,4096]{1,0:T(8,128)(2,1)S(1)}, bf16[128,4096]{1,0:T(8,128)(2,1)}, u32[]{:S(2)}) copy-start(bf16[128,4096]{1,0:T(8,128)(2,1)} %param.19) | copy-start | bytes 3145732
  20.0 18.0 %copy-start.28 = (bf16[512,256]{1,0:T(8,128)(2,1)}, bf16[512,256]{1,0:T(8,128)(2,1)S(1)}, u32[]{:S(2)}) copy-start(bf16[512,256]{1,0:T(8,128)(2,1)S(1)} %collective-permute-done.3.refs_11_) | copy-start | bytes 786436
  20.0 4.4 %collective-permute-start.4 = (bf16[1024,256]{1,0:T(8,128)(2,1)}, bf16[1024,256]{1,0:T(8,128)(2,1)S(1)}, u32[]{:S(2)}, u32[]{:S(2)}) collective-permute-start(bf16[1024,256]{1,0:T(8,128)(2,1)} %get-tuple-element.141.refs_0_), channel_id=1, source_target_pairs={{0,1},{1,0},{2,3},{3,2},{4,5},{5,4},{6,7},{7,6},{8,9},{9,8},{10,11... | collective-permute-start | bytes 1572872 | tf_op jit(solution)/shard_map/ppermute | solution.py:178
  20.9 26.2 %collective-permute-start.5 = (bf16[1024,256]{1,0:T(8,128)(2,1)}, bf16[1024,256]{1,0:T(8,128)(2,1)S(1)}, u32[]{:S(2)}, u32[]{:S(2)}) collective-permute-start(bf16[1024,256]{1,0:T(8,128)(2,1)} %get-tuple-element.131), channel_id=1, source_target_pairs={{0,8},{8,0},{16,24},{24,16},{1,9},{9,1},{17,25},{25,17},{2,10},{10... | collective-permute-start | bytes 1572872 | tf_op jit(solution)/shard_map/ppermute | solution.py:181
  22.8 30.4 %collective-permute-start.6 = (bf16[1024,256]{1,0:T(8,128)(2,1)}, bf16[1024,256]{1,0:T(8,128)(2,1)S(1)}, u32[]{:S(2)}, u32[]{:S(2)}) collective-permute-start(bf16[1024,256]{1,0:T(8,128)(2,1)} %get-tuple-element.132), channel_id=1, source_target_pairs={{0,16},{8,24},{16,0},{24,8},{1,17},{9,25},{17,1},{25,9},{2,18},{10... | collective-permute-start | bytes 1572872 | tf_op jit(solution)/shard_map/ppermute | solution.py:181
  24.3 28.9 %collective-permute-start.7 = (bf16[1024,256]{1,0:T(8,128)(2,1)}, bf16[1024,256]{1,0:T(8,128)(2,1)}, u32[]{:S(2)}, u32[]{:S(2)}) collective-permute-start(bf16[1024,256]{1,0:T(8,128)(2,1)} %get-tuple-element.133), channel_id=1, source_target_pairs={{0,24},{8,16},{16,8},{24,0},{1,25},{9,17},{17,9},{25,1},{2,26},{10... | collective-permute-start | bytes 1572872 | tf_op jit(solution)/shard_map/ppermute | solution.py:181
  24.4 17.5 %copy-start.1 = (bf16[1024,256]{1,0:T(8,128)(2,1)}, bf16[1024,256]{1,0:T(8,128)(2,1)S(1)}, u32[]{:S(2)}) copy-start(bf16[1024,256]{1,0:T(8,128)(2,1)S(1)} %collective-permute-done.4.refs_1_) | copy-start | bytes 1572868
  24.4 3.8 %collective-permute-start.13 = (f32[1,4,128]{2,1,0:T(4,128)S(1)}, f32[1,4,128]{2,1,0:T(4,128)S(1)}, u32[]{:S(2)}, u32[]{:S(2)}) collective-permute-start(f32[1,4,128]{2,1,0:T(4,128)S(1)} %maximum_bitcast_fusion), channel_id=1, source_target_pairs={{0,1},{1,0},{2,3},{3,2},{4,5},{5,4},{6,7},{7,6},{8,9},{9,8},{10,11... | collective-permute-start | bytes 6152 | tf_op jit(solution)/shard_map/ppermute | solution.py:232
  26.8 15.2 %collective-permute-start.8 = (bf16[256,1792]{1,0:T(8,128)(2,1)}, bf16[256,1792]{1,0:T(8,128)(2,1)}, u32[]{:S(2)}, u32[]{:S(2)}) collective-permute-start(bf16[256,1792]{1,0:T(8,128)(2,1)} %constant_dynamic-slice_fusion.5), channel_id=1, source_target_pairs={{0,1},{1,0},{2,3},{3,2},{4,5},{5,4},{6,7},{7,6},{8,9},{9,8},{10,11... | collective-permute-start | bytes 2752520 | tf_op jit(solution)/shard_map/ppermute | solution.py:178
  28.2 4.1 %collective-permute-start.14 = (f32[2,4,128]{2,1,0:T(4,128)S(1)}, f32[2,4,128]{2,1,0:T(4,128)S(1)}, u32[]{:S(2)}, u32[]{:S(2)}) collective-permute-start(f32[2,4,128]{2,1,0:T(4,128)S(1)} %pad_maximum_fusion.8), channel_id=1, source_target_pairs={{0,2},{1,3},{2,0},{3,1},{4,6},{5,7},{6,4},{7,5},{8,10},{9,11},{10,... | collective-permute-start | bytes 12296 | tf_op jit(solution)/shard_map/ppermute | solution.py:232
  32.3 4.6 %collective-permute-start.15 = (f32[4,4,128]{2,1,0:T(4,128)S(1)}, f32[4,4,128]{2,1,0:T(4,128)S(1)}, u32[]{:S(2)}, u32[]{:S(2)}) collective-permute-start(f32[4,4,128]{2,1,0:T(4,128)S(1)} %pad_maximum_fusion.7), channel_id=1, source_target_pairs={{0,4},{1,5},{2,6},{3,7},{4,0},{5,1},{6,2},{7,3},{8,12},{9,13},{10,... | collective-permute-start | bytes 24584 | tf_op jit(solution)/shard_map/ppermute | solution.py:232
  36.9 2.1 collective-permute-start.12
  42.9 24.2 %copy-start.19 = (bf16[512,256]{1,0:T(8,128)(2,1)}, bf16[512,256]{1,0:T(8,128)(2,1)S(1)}, u32[]{:S(2)}) copy-start(bf16[512,256]{1,0:T(8,128)(2,1)S(1)} %pad_maximum_fusion.5.refs_8_) | copy-start | bytes 786436
  42.9 10.9 %collective-permute-start.11 = (bf16[512,256]{1,0:T(8,128)(2,1)S(1)}, bf16[512,256]{1,0:T(8,128)(2,1)S(1)}, u32[]{:S(2)}, u32[]{:S(2)}) collective-permute-start(bf16[512,256]{1,0:T(8,128)(2,1)S(1)} %pad_maximum_fusion.5.refs_8_), channel_id=1, source_target_pairs={{0,24},{8,16},{16,8},{24,0},{1,25},{9,17},{17,9},{25,1},{2,26},{10... | collective-permute-start | bytes 786440 | tf_op jit(solution)/shard_map/ppermute | solution.py:181
  45.4 13.5 %collective-permute-start.10 = (bf16[512,256]{1,0:T(8,128)(2,1)S(1)}, bf16[512,256]{1,0:T(8,128)(2,1)S(1)}, u32[]{:S(2)}, u32[]{:S(2)}) collective-permute-start(bf16[512,256]{1,0:T(8,128)(2,1)S(1)} %pad_maximum_fusion.5.refs_8_), channel_id=1, source_target_pairs={{0,16},{8,24},{16,0},{24,8},{1,17},{9,25},{17,1},{25,9},{2,18},{10... | collective-permute-start | bytes 786440 | tf_op jit(solution)/shard_map/ppermute | solution.py:181
  47.1 15.7 %copy-start.2 = (bf16[1024,256]{1,0:T(8,128)(2,1)}, bf16[1024,256]{1,0:T(8,128)(2,1)S(1)}, u32[]{:S(2)}) copy-start(bf16[1024,256]{1,0:T(8,128)(2,1)S(1)} %collective-permute-done.5.refs_2_) | copy-start | bytes 1572868
  47.1 11.9 %collective-permute-start.9 = (bf16[512,256]{1,0:T(8,128)(2,1)S(1)}, bf16[512,256]{1,0:T(8,128)(2,1)S(1)}, u32[]{:S(2)}, u32[]{:S(2)}) collective-permute-start(bf16[512,256]{1,0:T(8,128)(2,1)S(1)} %pad_maximum_fusion.5.refs_8_), channel_id=1, source_target_pairs={{0,8},{8,0},{16,24},{24,16},{1,9},{9,1},{17,25},{25,17},{2,10},{10... | collective-permute-start | bytes 786440 | tf_op jit(solution)/shard_map/ppermute | solution.py:181
  59.0 2.0 collective-permute-start.16
  59.7 2.9 %collective-permute-start.17 = (bf16[1024,256]{1,0:T(8,128)(2,1)S(1)}, bf16[1024,256]{1,0:T(8,128)(2,1)}, u32[]{:S(2)}, u32[]{:S(2)}) collective-permute-start(bf16[1024,256]{1,0:T(8,128)(2,1)S(1)} %collective-permute-done.6.refs_4_), channel_id=1, source_target_pairs={{0,1},{1,0},{2,3},{3,2},{4,5},{5,4},{6,7},{7,6},{8,9},{9,8},{10,11... | collective-permute-start | bytes 1572872 | tf_op jit(solution)/shard_map/ppermute | solution.py:178
  59.8 3.0 %collective-permute-start.18 = (bf16[1024,256]{1,0:T(8,128)(2,1)}, bf16[1024,256]{1,0:T(8,128)(2,1)}, u32[]{:S(2)}, u32[]{:S(2)}) collective-permute-start(bf16[1024,256]{1,0:T(8,128)(2,1)} %collective-permute-done.7.refs_6_), channel_id=1, source_target_pairs={{0,1},{1,0},{2,3},{3,2},{4,5},{5,4},{6,7},{7,6},{8,9},{9,8},{10,11... | collective-permute-start | bytes 1572872 | tf_op jit(solution)/shard_map/ppermute | solution.py:178
  67.1 16.2 %copy-start.14 = (bf16[1024,256]{1,0:T(8,128)(2,1)S(1)}, bf16[1024,256]{1,0:T(8,128)(2,1)}, u32[]{:S(2)}) copy-start(bf16[1024,256]{1,0:T(8,128)(2,1)} %partial_product.5) | copy-start | bytes 1572868
  67.1 16.2 %collective-permute-start.22 = (bf16[1024,256]{1,0:T(8,128)(2,1)}, bf16[1024,256]{1,0:T(8,128)(2,1)}, u32[]{:S(2)}, u32[]{:S(2)}) collective-permute-start(bf16[1024,256]{1,0:T(8,128)(2,1)} %partial_product.5), channel_id=1, source_target_pairs={{0,2},{1,3},{6,4},{7,5},{8,10},{9,11},{14,12},{15,13},{16,18},{17,... | collective-permute-start | bytes 1572872 | tf_op jit(solution)/shard_map/ppermute | solution.py:191
  71.5 26.4 %collective-permute-start.20 = (bf16[512,512]{1,0:T(8,128)(2,1)}, bf16[512,512]{1,0:T(8,128)(2,1)}, u32[]{:S(2)}, u32[]{:S(2)}) collective-permute-start(bf16[512,512]{1,0:T(8,128)(2,1)} %get-tuple-element.178.refs_8_), channel_id=1, source_target_pairs={{0,16},{8,24},{16,0},{24,8},{1,17},{9,25},{17,1},{25,9},{2,18},{10... | collective-permute-start | bytes 1572872 | tf_op jit(solution)/shard_map/ppermute | solution.py:181
  73.0 24.9 %collective-permute-start.19 = (bf16[512,512]{1,0:T(8,128)(2,1)}, bf16[512,512]{1,0:T(8,128)(2,1)}, u32[]{:S(2)}, u32[]{:S(2)}) collective-permute-start(bf16[512,512]{1,0:T(8,128)(2,1)} %get-tuple-element.178.refs_8_), channel_id=1, source_target_pairs={{0,8},{8,0},{16,24},{24,16},{1,9},{9,1},{17,25},{25,17},{2,10},{10... | collective-permute-start | bytes 1572872 | tf_op jit(solution)/shard_map/ppermute | solution.py:181
  73.6 24.4 %collective-permute-start.21 = (bf16[512,512]{1,0:T(8,128)(2,1)}, bf16[512,512]{1,0:T(8,128)(2,1)}, u32[]{:S(2)}, u32[]{:S(2)}) collective-permute-start(bf16[512,512]{1,0:T(8,128)(2,1)} %get-tuple-element.178.refs_8_), channel_id=1, source_target_pairs={{0,24},{8,16},{16,8},{24,0},{1,25},{9,17},{17,9},{25,1},{2,26},{10... | collective-permute-start | bytes 1572872 | tf_op jit(solution)/shard_map/ppermute | solution.py:181
  79.3 28.0 %collective-permute-start.24 = (bf16[1024,256]{1,0:T(8,128)(2,1)}, bf16[1024,256]{1,0:T(8,128)(2,1)S(1)}, u32[]{:S(2)}, u32[]{:S(2)}) collective-permute-start(bf16[1024,256]{1,0:T(8,128)(2,1)} %partial_product.6), channel_id=1, source_target_pairs={{0,2},{1,3},{6,4},{7,5},{8,10},{9,11},{14,12},{15,13},{16,18},{17,... | collective-permute-start | bytes 1572872 | tf_op jit(solution)/shard_map/ppermute | solution.py:191
  84.5 23.7 %collective-permute-start.23 = (bf16[1024,256]{1,0:T(8,128)(2,1)S(1)}, bf16[1024,256]{1,0:T(8,128)(2,1)S(1)}, u32[]{:S(2)}, u32[]{:S(2)}) collective-permute-start(bf16[1024,256]{1,0:T(8,128)(2,1)S(1)} %add_convert_fusion.15), channel_id=1, source_target_pairs={{2,4},{3,5},{4,2},{5,3},{10,12},{11,13},{12,10},{13,11},{18,20},{1... | collective-permute-start | bytes 1572872 | tf_op jit(solution)/shard_map/ppermute | solution.py:191
  97.9 22.6 %collective-permute-start.27 = (bf16[512,512]{1,0:T(8,128)(2,1)}, bf16[512,512]{1,0:T(8,128)(2,1)}, u32[]{:S(2)}, u32[]{:S(2)}) collective-permute-start(bf16[512,512]{1,0:T(8,128)(2,1)} %get-tuple-element.200.refs_8_), channel_id=1, source_target_pairs={{0,16},{8,24},{16,0},{24,8},{1,17},{9,25},{17,1},{25,9},{2,18},{10... | collective-permute-start | bytes 1572872 | tf_op jit(solution)/shard_map/ppermute | solution.py:181
  99.5 21.1 %collective-permute-start.26 = (bf16[512,512]{1,0:T(8,128)(2,1)}, bf16[512,512]{1,0:T(8,128)(2,1)}, u32[]{:S(2)}, u32[]{:S(2)}) collective-permute-start(bf16[512,512]{1,0:T(8,128)(2,1)} %get-tuple-element.200.refs_8_), channel_id=1, source_target_pairs={{0,8},{8,0},{16,24},{24,16},{1,9},{9,1},{17,25},{25,17},{2,10},{10... | collective-permute-start | bytes 1572872 | tf_op jit(solution)/shard_map/ppermute | solution.py:181
  105.9 13.8 %copy-start.25 = (bf16[1024,256]{1,0:T(8,128)(2,1)S(1)}, bf16[1024,256]{1,0:T(8,128)(2,1)}, u32[]{:S(2)}) copy-start(bf16[1024,256]{1,0:T(8,128)(2,1)} %get-tuple-element.192) | copy-start | bytes 1572868
  105.9 11.4 %collective-permute-start.30 = (bf16[1024,256]{1,0:T(8,128)(2,1)}, bf16[1024,256]{1,0:T(8,128)(2,1)S(1)}, u32[]{:S(2)}, u32[]{:S(2)}) collective-permute-start(bf16[1024,256]{1,0:T(8,128)(2,1)} %get-tuple-element.192), channel_id=1, source_target_pairs={{0,2},{1,3},{6,4},{7,5},{8,10},{9,11},{14,12},{15,13},{16,18},{17,... | collective-permute-start | bytes 1572872 | tf_op jit(solution)/shard_map/ppermute | solution.py:191
  107.5 12.3 %collective-permute-start.29 = (bf16[1024,256]{1,0:T(8,128)(2,1)S(1)}, bf16[1024,256]{1,0:T(8,128)(2,1)S(1)}, u32[]{:S(2)}, u32[]{:S(2)}) collective-permute-start(bf16[1024,256]{1,0:T(8,128)(2,1)S(1)} %add_convert_fusion.14), channel_id=1, source_target_pairs={{2,4},{3,5},{4,2},{5,3},{10,12},{11,13},{12,10},{13,11},{18,20},{1... | collective-permute-start | bytes 1572872 | tf_op jit(solution)/shard_map/ppermute | solution.py:191
  108.2 14.9 %collective-permute-start.28 = (bf16[512,512]{1,0:T(8,128)(2,1)}, bf16[512,512]{1,0:T(8,128)(2,1)}, u32[]{:S(2)}, u32[]{:S(2)}) collective-permute-start(bf16[512,512]{1,0:T(8,128)(2,1)} %get-tuple-element.200.refs_8_), channel_id=1, source_target_pairs={{0,24},{8,16},{16,8},{24,0},{1,25},{9,17},{17,9},{25,1},{2,26},{10... | collective-permute-start | bytes 1572872 | tf_op jit(solution)/shard_map/ppermute | solution.py:181
  117.3 15.2 %collective-permute-start.25 = (bf16[1024,256]{1,0:T(8,128)(2,1)}, bf16[1024,256]{1,0:T(8,128)(2,1)S(1)}, u32[]{:S(2)}, u32[]{:S(2)}) collective-permute-start(bf16[1024,256]{1,0:T(8,128)(2,1)} %broadcast_select_fusion.13), channel_id=1, source_target_pairs={{0,2},{1,3},{2,0},{3,1},{4,6},{5,7},{6,4},{7,5},{8,10},{9,11},{10,... | collective-permute-start | bytes 1572872 | tf_op jit(solution)/shard_map/ppermute | solution.py:191
  119.9 11.2 %copy-start.8 = (bf16[1024,256]{1,0:T(8,128)(2,1)}, bf16[1024,256]{1,0:T(8,128)(2,1)S(1)}, u32[]{:S(2)}) copy-start(bf16[1024,256]{1,0:T(8,128)(2,1)S(1)} %collective-permute-done.29) | copy-start | bytes 1572868
  119.9 14.1 %collective-permute-start.32 = (bf16[1024,256]{1,0:T(8,128)(2,1)S(1)}, bf16[1024,256]{1,0:T(8,128)(2,1)S(1)}, u32[]{:S(2)}, u32[]{:S(2)}) collective-permute-start(bf16[1024,256]{1,0:T(8,128)(2,1)S(1)} %add_convert_fusion.12), channel_id=1, source_target_pairs={{2,4},{3,5},{4,2},{5,3},{10,12},{11,13},{12,10},{13,11},{18,20},{1... | collective-permute-start | bytes 1572872 | tf_op jit(solution)/shard_map/ppermute | solution.py:191
  123.2 24.9 %collective-permute-start.35 = (bf16[512,512]{1,0:T(8,128)(2,1)}, bf16[512,512]{1,0:T(8,128)(2,1)}, u32[]{:S(2)}, u32[]{:S(2)}) collective-permute-start(bf16[512,512]{1,0:T(8,128)(2,1)} %pad_maximum_fusion.2.refs_8_), channel_id=1, source_target_pairs={{0,16},{8,24},{16,0},{24,8},{1,17},{9,25},{17,1},{25,9},{2,18},{10... | collective-permute-start | bytes 1572872 | tf_op jit(solution)/shard_map/ppermute | solution.py:181
  124.7 23.4 %collective-permute-start.34 = (bf16[512,512]{1,0:T(8,128)(2,1)}, bf16[512,512]{1,0:T(8,128)(2,1)}, u32[]{:S(2)}, u32[]{:S(2)}) collective-permute-start(bf16[512,512]{1,0:T(8,128)(2,1)} %pad_maximum_fusion.2.refs_8_), channel_id=1, source_target_pairs={{0,8},{8,0},{16,24},{24,16},{1,9},{9,1},{17,25},{25,17},{2,10},{10... | collective-permute-start | bytes 1572872 | tf_op jit(solution)/shard_map/ppermute | solution.py:181
  132.4 11.9 %collective-permute-start.31 = (bf16[1024,256]{1,0:T(8,128)(2,1)S(1)}, bf16[1024,256]{1,0:T(8,128)(2,1)S(1)}, u32[]{:S(2)}, u32[]{:S(2)}) collective-permute-start(bf16[1024,256]{1,0:T(8,128)(2,1)S(1)} %broadcast_select_fusion.12), channel_id=1, source_target_pairs={{0,2},{1,3},{2,0},{3,1},{4,6},{5,7},{6,4},{7,5},{8,10},{9,11},{10,... | collective-permute-start | bytes 1572872 | tf_op jit(solution)/shard_map/ppermute | solution.py:191
  132.7 11.7 %copy-start.13 = (bf16[1024,256]{1,0:T(8,128)(2,1)S(1)}, bf16[1024,256]{1,0:T(8,128)(2,1)}, u32[]{:S(2)}) copy-start(bf16[1024,256]{1,0:T(8,128)(2,1)} %get-tuple-element.217) | copy-start | bytes 1572868
  133.1 13.0 %copy-start.9 = (bf16[1024,256]{1,0:T(8,128)(2,1)S(1)}, bf16[1024,256]{1,0:T(8,128)(2,1)}, u32[]{:S(2)}) copy-start(bf16[1024,256]{1,0:T(8,128)(2,1)} %copy-done.8) | copy-start | bytes 1572868
  133.3 11.3 %collective-permute-start.37 = (bf16[1024,256]{1,0:T(8,128)(2,1)S(1)}, bf16[1024,256]{1,0:T(8,128)(2,1)S(1)}, u32[]{:S(2)}, u32[]{:S(2)}) collective-permute-start(bf16[1024,256]{1,0:T(8,128)(2,1)S(1)} %add_convert_fusion.10), channel_id=1, source_target_pairs={{2,4},{3,5},{4,2},{5,3},{10,12},{11,13},{12,10},{13,11},{18,20},{1... | collective-permute-start | bytes 1572872 | tf_op jit(solution)/shard_map/ppermute | solution.py:191
  134.0 14.1 %collective-permute-start.36 = (bf16[512,512]{1,0:T(8,128)(2,1)}, bf16[512,512]{1,0:T(8,128)(2,1)S(1)}, u32[]{:S(2)}, u32[]{:S(2)}) collective-permute-start(bf16[512,512]{1,0:T(8,128)(2,1)} %pad_maximum_fusion.2.refs_8_), channel_id=1, source_target_pairs={{0,24},{8,16},{16,8},{24,0},{1,25},{9,17},{17,9},{25,1},{2,26},{10... | collective-permute-start | bytes 1572872 | tf_op jit(solution)/shard_map/ppermute | solution.py:181
  144.4 16.9 %collective-permute-start.33 = (bf16[1024,256]{1,0:T(8,128)(2,1)}, bf16[1024,256]{1,0:T(8,128)(2,1)S(1)}, u32[]{:S(2)}, u32[]{:S(2)}) collective-permute-start(bf16[1024,256]{1,0:T(8,128)(2,1)} %broadcast_select_fusion.10), channel_id=1, source_target_pairs={{0,2},{1,3},{2,0},{3,1},{4,6},{5,7},{6,4},{7,5},{8,10},{9,11},{10,... | collective-permute-start | bytes 1572872 | tf_op jit(solution)/shard_map/ppermute | solution.py:191
  144.6 19.1 %collective-permute-start.39 = (bf16[1024,256]{1,0:T(8,128)(2,1)S(1)}, bf16[1024,256]{1,0:T(8,128)(2,1)}, u32[]{:S(2)}, u32[]{:S(2)}) collective-permute-start(bf16[1024,256]{1,0:T(8,128)(2,1)S(1)} %add_convert_fusion.8), channel_id=1, source_target_pairs={{2,4},{3,5},{4,2},{5,3},{10,12},{11,13},{12,10},{13,11},{18,20},{1... | collective-permute-start | bytes 1572872 | tf_op jit(solution)/shard_map/ppermute | solution.py:191
  148.9 11.3 %copy-start.15 = (bf16[1024,256]{1,0:T(8,128)(2,1)S(1)}, bf16[1024,256]{1,0:T(8,128)(2,1)}, u32[]{:S(2)}) copy-start(bf16[1024,256]{1,0:T(8,128)(2,1)} %broadcast_select_fusion.9) | copy-start | bytes 1572868
  156.1 16.9 %collective-permute-start.38 = (bf16[1024,256]{1,0:T(8,128)(2,1)S(1)}, bf16[1024,256]{1,0:T(8,128)(2,1)S(1)}, u32[]{:S(2)}, u32[]{:S(2)}) collective-permute-start(bf16[1024,256]{1,0:T(8,128)(2,1)S(1)} %broadcast_select_fusion.8), channel_id=1, source_target_pairs={{0,2},{1,3},{2,0},{3,1},{4,6},{5,7},{6,4},{7,5},{8,10},{9,11},{10,... | collective-permute-start | bytes 1572872 | tf_op jit(solution)/shard_map/ppermute | solution.py:191
  161.5 11.6 %copy-start.11 = (bf16[1024,256]{1,0:T(8,128)(2,1)S(1)}, bf16[1024,256]{1,0:T(8,128)(2,1)}, u32[]{:S(2)}) copy-start(bf16[1024,256]{1,0:T(8,128)(2,1)} %get-tuple-element.233) | copy-start | bytes 1572868
  162.0 12.1 %collective-permute-start.41 = (bf16[1024,256]{1,0:T(8,128)(2,1)S(1)}, bf16[1024,256]{1,0:T(8,128)(2,1)S(1)}, u32[]{:S(2)}, u32[]{:S(2)}) collective-permute-start(bf16[1024,256]{1,0:T(8,128)(2,1)S(1)} %add_convert_fusion.6), channel_id=1, source_target_pairs={{2,4},{3,5},{4,2},{5,3},{10,12},{11,13},{12,10},{13,11},{18,20},{1... | collective-permute-start | bytes 1572872 | tf_op jit(solution)/shard_map/ppermute | solution.py:191
  165.0 19.3 %collective-permute-start.40 = (bf16[1024,256]{1,0:T(8,128)(2,1)S(1)}, bf16[1024,256]{1,0:T(8,128)(2,1)S(1)}, u32[]{:S(2)}, u32[]{:S(2)}) collective-permute-start(bf16[1024,256]{1,0:T(8,128)(2,1)S(1)} %broadcast_select_fusion.6), channel_id=1, source_target_pairs={{0,2},{1,3},{2,0},{3,1},{4,6},{5,7},{6,4},{7,5},{8,10},{9,11},{10,... | collective-permute-start | bytes 1572872 | tf_op jit(solution)/shard_map/ppermute | solution.py:191
  173.2 18.3 %collective-permute-start.43 = (bf16[1024,256]{1,0:T(8,128)(2,1)S(1)}, bf16[1024,256]{1,0:T(8,128)(2,1)S(1)}, u32[]{:S(2)}, u32[]{:S(2)}) collective-permute-start(bf16[1024,256]{1,0:T(8,128)(2,1)S(1)} %add_convert_fusion.4), channel_id=1, source_target_pairs={{2,4},{3,5},{4,2},{5,3},{10,12},{11,13},{12,10},{13,11},{18,20},{1... | collective-permute-start | bytes 1572872 | tf_op jit(solution)/shard_map/ppermute | solution.py:191
  174.5 16.6 %collective-permute-start.42 = (bf16[1024,256]{1,0:T(8,128)(2,1)S(1)}, bf16[1024,256]{1,0:T(8,128)(2,1)S(1)}, u32[]{:S(2)}, u32[]{:S(2)}) collective-permute-start(bf16[1024,256]{1,0:T(8,128)(2,1)S(1)} %add_convert_fusion.3), channel_id=1, source_target_pairs={{2,0},{3,1},{4,6},{5,7},{10,8},{11,9},{12,14},{13,15},{18,16},{19,... | collective-permute-start | bytes 1572872 | tf_op jit(solution)/shard_map/ppermute | solution.py:191
  185.7 7.5 %collective-permute-start.45 = (bf16[1024,256]{1,0:T(8,128)(2,1)S(1)}, bf16[1024,256]{1,0:T(8,128)(2,1)S(1)}, u32[]{:S(2)}, u32[]{:S(2)}) collective-permute-start(bf16[1024,256]{1,0:T(8,128)(2,1)S(1)} %add_convert_fusion.2), channel_id=1, source_target_pairs={{2,4},{3,5},{4,2},{5,3},{10,12},{11,13},{12,10},{13,11},{18,20},{1... | collective-permute-start | bytes 1572872 | tf_op jit(solution)/shard_map/ppermute | solution.py:191
  191.7 15.9 %collective-permute-start.44 = (bf16[1024,256]{1,0:T(8,128)(2,1)S(1)}, bf16[1024,256]{1,0:T(8,128)(2,1)S(1)}, u32[]{:S(2)}, u32[]{:S(2)}) collective-permute-start(bf16[1024,256]{1,0:T(8,128)(2,1)S(1)} %add_convert_fusion.1), channel_id=1, source_target_pairs={{2,0},{3,1},{4,6},{5,7},{10,8},{11,9},{12,14},{13,15},{18,16},{19,... | collective-permute-start | bytes 1572872 | tf_op jit(solution)/shard_map/ppermute | solution.py:191
  193.0 21.9 %collective-permute-start.47 = (bf16[448,1536]{1,0:T(8,128)(2,1)S(1)}, bf16[448,1536]{1,0:T(8,128)(2,1)S(1)}, u32[]{:S(2)}, u32[]{:S(2)}) collective-permute-start(bf16[448,1536]{1,0:T(8,128)(2,1)S(1)} %constant_dynamic-update-slice_fusion), channel_id=1, source_target_pairs={{0,1},{1,0},{2,3},{3,2},{4,5},{5,4},{6,7},{7,6},{8,9},{9,8},{10,11... | collective-permute-start | bytes 4128776 | tf_op jit(solution)/shard_map/ppermute | solution.py:178
  193.3 21.0 %collective-permute-start.46 = (bf16[1024,256]{1,0:T(8,128)(2,1)S(1)}, bf16[1024,256]{1,0:T(8,128)(2,1)S(1)}, u32[]{:S(2)}, u32[]{:S(2)}) collective-permute-start(bf16[1024,256]{1,0:T(8,128)(2,1)S(1)} %add_convert_fusion), channel_id=1, source_target_pairs={{2,0},{3,1},{4,6},{5,7},{10,8},{11,9},{12,14},{13,15},{18,16},{19,... | collective-permute-start | bytes 1572872 | tf_op jit(solution)/shard_map/ppermute | solution.py:191
  214.8 1.9 collective-permute-start.48
  (23 other events, 101.0 us)

commit v13 on v12

--- a/solution.py
+++ b/solution.py
@@ -201,8 +201,8 @@
         return [piece, to_ctx(piece, 1), to_ctx(piece, 2)]
 
     def spread_far(near):
-        (piece,) = chain(near[0])
-        return near + [to_ctx(piece, 3)]
+        near = list(chain(*near))
+        return near + [to_ctx(near[0], 3)]
 
     def spread(piece):
         return [piece] + [to_ctx(piece, offset) for offset in range(1, ctx_count)]
@@ -361,7 +361,10 @@
             (payload,) = chain(payload)
             outer[step, hop] = (swap_chips(payload, hop, inward is not None, outward is not None), inward, outward)
         if step == 0 and square:
-            rights[2] = spread_far(rights[2])
+            (piece,) = chain(rights[2][0])
+            rights[2].append(to_ctx(piece, 3))
+        if step == 1 and square:
+            rights[2][1:3] = chain(*rights[2][1:3])
     result = jnp.where(
         core_at == 0,
         jnp.concatenate(rows_own + rows_got, axis=1),

time: 220 us -> 212 us (0.964)
  waiting for transfers between devices: 84 us -> 68.9 us
  starting transfers between devices: 53.9 us -> 60.6 us
    ppermute x18, waiting for transfers between devices: 24.7 us -> 13.5 us  [to_ctx(): lax.ppermute(array, 'ctx', [(place, place ^ offset) for place in range(ct...]
    ppermute x19, starting transfers between devices: 25.3 us -> 32 us  [swap_chips(): return lax.ppermute(array, 'exp', sorted(pairs))]
    ppermute x19, waiting for transfers between devices: 53.8 us -> 49.9 us  [swap_chips(): return lax.ppermute(array, 'exp', sorted(pairs))]
    unnamed x100 -> x110, local copies, waits for them, and re-layouts: 6.1 us -> 5.43 us
  transfers between devices with their start and end apart: 49 -> 49, of which waited for: 20 -> 20; matrix products, arithmetic and copies ran while one was open for 15% -> 17% of each run, Pallas kernels for 16% -> 18%
where the time goes in v13:
time: 212 us; the launch traced here: 211 us
  waiting for transfers between devices  68.9 us (33%)
  starting transfers between devices  60.6 us (29%)
  Pallas kernels  39.1 us (18%)
  other arithmetic  22.4 us (11%)
  local copies, waits for them, and re-layouts  16.8 us (8%)
  matrix products  2.34 us (1%)
    ppermute x19, waiting for transfers between devices, swap_chips(): return lax.ppermute(array, 'exp', sorted(pairs))  49.9 us
    ppermute x19, starting transfers between devices, swap_chips(): return lax.ppermute(array, 'exp', sorted(pairs))  32 us
    pallas_call x5, Pallas kernels, matmul(): pl.pallas_call(functools.partial(matmul_kernel, len(lefts), len(rights)),...  26.2 us
    ppermute x18, starting transfers between devices, to_ctx(): lax.ppermute(array, 'ctx', [(place, place ^ offset) for place in range(ct...  22.2 us
    ppermute x18, waiting for transfers between devices, to_ctx(): lax.ppermute(array, 'ctx', [(place, place ^ offset) for place in range(ct...  13.5 us
    pallas_call x1, Pallas kernels, conv_grad(): pl.pallas_call(functools.partial(conv_kernel, tile), grid_spec=pltpu.Pref...  12.8 us
    select_n x5, other arithmetic, on_device(): jnp.where(distance == hop, sums[hop][inward], ready[hop + 1][outward])  7.4 us
    unnamed x110, local copies, waits for them, and re-layouts  5.43 us
  transfers between devices with their start and end apart: 49, of which 20 were waited for; matrix products, arithmetic and copies ran while one was open for 17% of the time, Pallas kernels for 18%

profile of v13, /device:TPU:0, one launch (start us, length us, event | category | flops | bytes accessed | tf_op | source)
XLA Modules:
  0.0 211.4 jit_solution(16660780987074016008)
XLA Ops:
  0.0 1.0 constant_dynamic-slice_fusion.8
  1.5 1.0 collective-permute-done
  2.5 3.9 %collective-permute-start.3 = (bf16[512,256]{1,0:T(8,128)(2,1)S(1)}, bf16[512,256]{1,0:T(8,128)(2,1)S(1)}, u32[]{:S(2)}, u32[]{:S(2)}) collective-permute-start(bf16[512,256]{1,0:T(8,128)(2,1)S(1)} %pad_maximum_fusion.4.refs_8_), channel_id=1, source_target_pairs={{0,24},{8,16},{16,8},{24,0},{1,25},{9,17},{17,9},{25,1},{2,26},{10... | collective-permute-start | bytes 786440 | tf_op jit(solution)/shard_map/ppermute | solution.py:181
  7.0 12.8 %conv_grad.1 = (bf16[1024,256]{1,0:T(8,128)(2,1)}, bf16[1024,256]{1,0:T(8,128)(2,1)}, bf16[1024,256]{1,0:T(8,128)(2,1)}, bf16[1024,256]{1,0:T(8,128)(2,1)}) custom-call(s32[1]{0:T(128)} %bitcast.1.at_ctx, bf16[256,4096]{1,0:T(8,128)(2,1)} %out_grad.1, bf16[256,4096]{1,0:T(8,128)(2,1)} %gate_in.1, bf16[256,4096]{1,0:T(8,128)(2,1)} %conv_in.1, ...), custom_call_target="tpu_custom_call" | custom-call | flops 41943040 | bytes 10485760 | tf_op jit(solution)/shard_map/conv_grad/pallas_call | solution.py:84
  20.8 1.9 collective-permute-start.5
  22.7 1.5 collective-permute-start.6
  24.4 2.2 %constant_dynamic-slice_fusion.5 = bf16[256,1792]{1,0:T(8,128)(2,1)} fusion(bf16[256,4096]{1,0:T(8,128)(2,1)} %param.18, s32[]{:T(128)S(6)} %select_n.141), kind=kLoop, calls=%fused_computation.106 | loop fusion | bytes 1835012 | tf_op jit(solution)/shard_map/dynamic_slice | solution.py:194
  27.1 1.1 constant_dynamic-slice_fusion.4
  28.3 2.0 collective-permute-start.14
  30.3 2.0 constant_dynamic-slice_fusion.6
  32.3 2.7 %collective-permute-start.15 = (f32[4,4,128]{2,1,0:T(4,128)S(1)}, f32[4,4,128]{2,1,0:T(4,128)S(1)}, u32[]{:S(2)}, u32[]{:S(2)}) collective-permute-start(f32[4,4,128]{2,1,0:T(4,128)S(1)} %pad_maximum_fusion.7), channel_id=1, source_target_pairs={{0,4},{1,5},{2,6},{3,7},{4,0},{5,1},{6,2},{7,3},{8,12},{9,13},{10,... | collective-permute-start | bytes 24584 | tf_op jit(solution)/shard_map/ppermute | solution.py:232
  35.0 0.9 constant_dynamic-slice_fusion.2
  35.9 1.0 collective-permute-done.15
  39.9 2.1 maximum_select_fusion
  42.0 0.9 slice.140
  43.0 2.5 %collective-permute-start.11 = (bf16[512,256]{1,0:T(8,128)(2,1)S(1)}, bf16[512,256]{1,0:T(8,128)(2,1)S(1)}, u32[]{:S(2)}, u32[]{:S(2)}) collective-permute-start(bf16[512,256]{1,0:T(8,128)(2,1)S(1)} %pad_maximum_fusion.5.refs_8_), channel_id=1, source_target_pairs={{0,24},{8,16},{16,8},{24,0},{1,25},{9,17},{17,9},{25,1},{2,26},{10... | collective-permute-start | bytes 786440 | tf_op jit(solution)/shard_map/ppermute | solution.py:181
  46.0 1.2 fusion.24
  48.6 1.0 pad_maximum_fusion
  49.7 3.5 %collective-permute-done.6.refs_4_ = bf16[1024,256]{1,0:T(8,128)(2,1)S(1)} collective-permute-done((bf16[1024,256]{1,0:T(8,128)(2,1)}, bf16[1024,256]{1,0:T(8,128)(2,1)S(1)}, u32[]{:S(2)}, u32[]{:S(2)}) %collective-permute-start.6) | collective-permute-done | bytes 524320 | tf_op jit(solution)/shard_map/ppermute | solution.py:181
  53.5 5.3 %collective-permute-done.10.refs_10_ = bf16[512,256]{1,0:T(8,128)(2,1)S(1)} collective-permute-done((bf16[512,256]{1,0:T(8,128)(2,1)S(1)}, bf16[512,256]{1,0:T(8,128)(2,1)S(1)}, u32[]{:S(2)}, u32[]{:S(2)}) %collective-permute-start.10) | collective-permute-done | bytes 262176 | tf_op jit(solution)/shard_map/ppermute | solution.py:181
  61.8 1.0 collective-permute-done.18.refs_7_
  62.7 1.5 collective-permute-start.20
  64.8 4.3 %partial_product.5 = bf16[1024,256]{1,0:T(8,128)(2,1)} custom-call(s32[1]{0:T(128)} %bitcast.place, bf16[1024,256]{1,0:T(8,128)(2,1)} %get-tuple-element.147.refs_0_, bf16[1024,256]{1,0:T(8,128)(2,1)} %copy-done.1, bf16[1024,256]{1,0:T(8,128)(2,1)} %copy-done.2, bf16[1024,256]{1,0:T(8,128)(2,1)} %copy-done.4, bf16[1024,256]{1,0:T(8,128)(2,1)} %copy-done.3, ...), custom_call_target="tpu_custom_call" | custom-call | flops 1073741824 | bytes 5767168 | tf_op jit(solution)/shard_map/partial_product/pallas_call | solution.py:130
  69.1 4.4 %collective-permute-start.22 = (bf16[1024,256]{1,0:T(8,128)(2,1)}, bf16[1024,256]{1,0:T(8,128)(2,1)}, u32[]{:S(2)}, u32[]{:S(2)}) collective-permute-start(bf16[1024,256]{1,0:T(8,128)(2,1)} %partial_product.5), channel_id=1, source_target_pairs={{0,2},{1,3},{6,4},{7,5},{8,10},{9,11},{14,12},{15,13},{16,18},{17,... | collective-permute-start | bytes 1572872 | tf_op jit(solution)/shard_map/ppermute | solution.py:191
  73.5 1.4 collective-permute-start.21
  74.9 4.3 %partial_product.6 = bf16[1024,256]{1,0:T(8,128)(2,1)} custom-call(s32[1]{0:T(128)} %bitcast.place, bf16[1024,256]{1,0:T(8,128)(2,1)} %get-tuple-element.147.refs_0_, bf16[1024,256]{1,0:T(8,128)(2,1)} %copy-done.1, bf16[1024,256]{1,0:T(8,128)(2,1)} %copy-done.2, bf16[1024,256]{1,0:T(8,128)(2,1)} %copy-done.4, bf16[1024,256]{1,0:T(8,128)(2,1)} %copy-done.3, ...), custom_call_target="tpu_custom_call" | custom-call | flops 1073741824 | bytes 5767168 | tf_op jit(solution)/shard_map/partial_product/pallas_call | solution.py:130
  79.2 1.3 collective-permute-start.24
  80.6 4.8 %collective-permute-done.22 = bf16[1024,256]{1,0:T(8,128)(2,1)} collective-permute-done((bf16[1024,256]{1,0:T(8,128)(2,1)}, bf16[1024,256]{1,0:T(8,128)(2,1)}, u32[]{:S(2)}, u32[]{:S(2)}) %collective-permute-start.22) | collective-permute-done | bytes 524320 | tf_op jit(solution)/shard_map/ppermute | solution.py:191
  85.4 1.2 add_convert_fusion.15
  86.6 2.8 %collective-permute-done.21.refs_11_ = bf16[512,512]{1,0:T(8,128)(2,1)} collective-permute-done((bf16[512,512]{1,0:T(8,128)(2,1)}, bf16[512,512]{1,0:T(8,128)(2,1)}, u32[]{:S(2)}, u32[]{:S(2)}) %collective-permute-start.21) | collective-permute-done | bytes 524320 | tf_op jit(solution)/shard_map/ppermute | solution.py:181
  89.4 1.5 collective-permute-start.26
  92.2 0.9 fusion.22
  93.1 5.9 %partial_product.7 = (bf16[1024,256]{1,0:T(8,128)(2,1)}, bf16[1024,256]{1,0:T(8,128)(2,1)}) custom-call(s32[1]{0:T(128)} %bitcast.place, bf16[1024,256]{1,0:T(8,128)(2,1)} %get-tuple-element.147.refs_0_, bf16[1024,256]{1,0:T(8,128)(2,1)} %copy-done.1, bf16[1024,256]{1,0:T(8,128)(2,1)} %copy-done.2, bf16[1024,256]{1,0:T(8,128)(2,1)} %copy-done.4, ...), custom_call_target="tpu_custom_call" | custom-call | flops 2147483648 | bytes 7340032 | tf_op jit(solution)/shard_map/partial_product/pallas_call | solution.py:130
  99.0 6.4 %collective-permute-start.30 = (bf16[1024,256]{1,0:T(8,128)(2,1)}, bf16[1024,256]{1,0:T(8,128)(2,1)S(1)}, u32[]{:S(2)}, u32[]{:S(2)}) collective-permute-start(bf16[1024,256]{1,0:T(8,128)(2,1)} %get-tuple-element.202), channel_id=1, source_target_pairs={{0,2},{1,3},{6,4},{7,5},{8,10},{9,11},{14,12},{15,13},{16,18},{17,... | collective-permute-start | bytes 1572872 | tf_op jit(solution)/shard_map/ppermute | solution.py:191
  106.4 1.5 collective-permute-start.28
  107.8 2.0 broadcast_select_fusion.13
  109.9 8.2 %collective-permute-done.30 = bf16[1024,256]{1,0:T(8,128)(2,1)S(1)} collective-permute-done((bf16[1024,256]{1,0:T(8,128)(2,1)}, bf16[1024,256]{1,0:T(8,128)(2,1)S(1)}, u32[]{:S(2)}, u32[]{:S(2)}) %collective-permute-start.30) | collective-permute-done | bytes 524320 | tf_op jit(solution)/shard_map/ppermute | solution.py:191
  119.0 1.2 collective-permute-start.34
  121.0 5.9 %partial_product.8 = (bf16[1024,256]{1,0:T(8,128)(2,1)}, bf16[1024,256]{1,0:T(8,128)(2,1)}) custom-call(s32[1]{0:T(128)} %bitcast.place, bf16[1024,256]{1,0:T(8,128)(2,1)} %get-tuple-element.147.refs_0_, bf16[1024,256]{1,0:T(8,128)(2,1)} %copy-done.1, bf16[1024,256]{1,0:T(8,128)(2,1)} %copy-done.2, bf16[1024,256]{1,0:T(8,128)(2,1)} %copy-done.4, ...), custom_call_target="tpu_custom_call" | custom-call | flops 2147483648 | bytes 7340032 | tf_op jit(solution)/shard_map/partial_product/pallas_call | solution.py:130
  127.0 1.3 broadcast_select_fusion.12
  128.3 3.0 %collective-permute-start.31 = (bf16[1024,256]{1,0:T(8,128)(2,1)S(1)}, bf16[1024,256]{1,0:T(8,128)(2,1)S(1)}, u32[]{:S(2)}, u32[]{:S(2)}) collective-permute-start(bf16[1024,256]{1,0:T(8,128)(2,1)S(1)} %broadcast_select_fusion.12), channel_id=1, source_target_pairs={{0,2},{1,3},{2,0},{3,1},{4,6},{5,7},{6,4},{7,5},{8,10},{9,11},{10,... | collective-permute-start | bytes 1572872 | tf_op jit(solution)/shard_map/ppermute | solution.py:191
  131.3 1.2 broadcast_select_fusion.11
  132.9 1.2 add_convert_fusion.10
  135.6 1.0 broadcast_select_fusion.10
  136.7 1.5 collective-permute-start.36
  138.1 1.9 collective-permute-start.35
  140.1 2.5 %collective-permute-done.31 = bf16[1024,256]{1,0:T(8,128)(2,1)S(1)} collective-permute-done((bf16[1024,256]{1,0:T(8,128)(2,1)S(1)}, bf16[1024,256]{1,0:T(8,128)(2,1)S(1)}, u32[]{:S(2)}, u32[]{:S(2)}) %collective-permute-start.31) | collective-permute-done | bytes 524320 | tf_op jit(solution)/shard_map/ppermute | solution.py:191
  143.2 1.5 collective-permute-start.39
  145.6 1.4 collective-permute-done.36.refs_11_
  147.7 5.8 %partial_product.9 = (bf16[1024,256]{1,0:T(8,128)(2,1)}, bf16[1024,256]{1,0:T(8,128)(2,1)}) custom-call(s32[1]{0:T(128)} %bitcast.place, bf16[1024,256]{1,0:T(8,128)(2,1)} %get-tuple-element.147.refs_0_, bf16[1024,256]{1,0:T(8,128)(2,1)} %copy-done.1, bf16[1024,256]{1,0:T(8,128)(2,1)} %copy-done.2, bf16[1024,256]{1,0:T(8,128)(2,1)} %copy-done.4, ...), custom_call_target="tpu_custom_call" | custom-call | flops 2147483648 | bytes 7340032 | tf_op jit(solution)/shard_map/partial_product/pallas_call | solution.py:130
  153.6 1.3 broadcast_select_fusion.8
  154.9 2.3 %collective-permute-start.38 = (bf16[1024,256]{1,0:T(8,128)(2,1)S(1)}, bf16[1024,256]{1,0:T(8,128)(2,1)S(1)}, u32[]{:S(2)}, u32[]{:S(2)}) collective-permute-start(bf16[1024,256]{1,0:T(8,128)(2,1)S(1)} %broadcast_select_fusion.8), channel_id=1, source_target_pairs={{0,2},{1,3},{2,0},{3,1},{4,6},{5,7},{6,4},{7,5},{8,10},{9,11},{10,... | collective-permute-start | bytes 1572872 | tf_op jit(solution)/shard_map/ppermute | solution.py:191
  158.4 1.8 broadcast_select_fusion.6
  160.5 2.2 %collective-permute-start.40 = (bf16[1024,256]{1,0:T(8,128)(2,1)S(1)}, bf16[1024,256]{1,0:T(8,128)(2,1)S(1)}, u32[]{:S(2)}, u32[]{:S(2)}) collective-permute-start(bf16[1024,256]{1,0:T(8,128)(2,1)S(1)} %broadcast_select_fusion.6), channel_id=1, source_target_pairs={{0,2},{1,3},{2,0},{3,1},{4,6},{5,7},{6,4},{7,5},{8,10},{9,11},{10,... | collective-permute-start | bytes 1572872 | tf_op jit(solution)/shard_map/ppermute | solution.py:191
  162.9 6.1 %collective-permute-done.38 = bf16[1024,256]{1,0:T(8,128)(2,1)S(1)} collective-permute-done((bf16[1024,256]{1,0:T(8,128)(2,1)S(1)}, bf16[1024,256]{1,0:T(8,128)(2,1)S(1)}, u32[]{:S(2)}, u32[]{:S(2)}) %collective-permute-start.38) | collective-permute-done | bytes 524320 | tf_op jit(solution)/shard_map/ppermute | solution.py:191
  170.2 1.3 collective-permute-start.42
  171.8 8.4 %collective-permute-done.40 = bf16[1024,256]{1,0:T(8,128)(2,1)S(1)} collective-permute-done((bf16[1024,256]{1,0:T(8,128)(2,1)S(1)}, bf16[1024,256]{1,0:T(8,128)(2,1)S(1)}, u32[]{:S(2)}, u32[]{:S(2)}) %collective-permute-start.40) | collective-permute-done | bytes 524320 | tf_op jit(solution)/shard_map/ppermute | solution.py:191
  180.2 1.2 broadcast_select_fusion.4
  182.9 1.3 collective-permute-start.44
  184.4 1.3 collective-permute-start.46
  185.7 5.8 %collective-permute-done.42 = bf16[1024,256]{1,0:T(8,128)(2,1)S(1)} collective-permute-done((bf16[1024,256]{1,0:T(8,128)(2,1)S(1)}, bf16[1024,256]{1,0:T(8,128)(2,1)S(1)}, u32[]{:S(2)}, u32[]{:S(2)}) %collective-permute-start.42) | collective-permute-done | bytes 524320 | tf_op jit(solution)/shard_map/ppermute | solution.py:191
  192.0 14.1 %collective-permute-done.46 = bf16[1024,256]{1,0:T(8,128)(2,1)S(1)} collective-permute-done((bf16[1024,256]{1,0:T(8,128)(2,1)S(1)}, bf16[1024,256]{1,0:T(8,128)(2,1)S(1)}, u32[]{:S(2)}, u32[]{:S(2)}) %collective-permute-start.46) | collective-permute-done | bytes 524320 | tf_op jit(solution)/shard_map/ppermute | solution.py:191
  207.4 1.4 collective-permute-done.48
  209.2 2.2 %broadcast_select_fusion = bf16[1,448,4096]{2,1,0:T(8,128)(2,1)} fusion(bf16[1,448,4096]{2,1,0:T(8,128)(2,1)S(1)} %get-tuple-element.275, bf16[1,448,4096]{2,1,0:T(8,128)(2,1)S(1)} %constant_dynamic-update-slice_fusion.14, pred[]{:T(512)S(6)} %eq.30), kind=kLoop, calls=%fused_computation | loop fusion | flops 1835008 | bytes 11010049 | tf_op jit(solution)/shard_map/jit(_where)/select_n | solution.py:368
  (234 shorter events, 25.7 us)
Async XLA Ops:
  1.0 1.5 collective-permute-start
  2.5 17.4 %copy-start.20 = (bf16[512,256]{1,0:T(8,128)(2,1)}, bf16[512,256]{1,0:T(8,128)(2,1)S(1)}, u32[]{:S(2)}) copy-start(bf16[512,256]{1,0:T(8,128)(2,1)S(1)} %pad_maximum_fusion.4.refs_8_) | copy-start | bytes 786436
  2.5 17.4 %collective-permute-start.3 = (bf16[512,256]{1,0:T(8,128)(2,1)S(1)}, bf16[512,256]{1,0:T(8,128)(2,1)S(1)}, u32[]{:S(2)}, u32[]{:S(2)}) collective-permute-start(bf16[512,256]{1,0:T(8,128)(2,1)S(1)} %pad_maximum_fusion.4.refs_8_), channel_id=1, source_target_pairs={{0,24},{8,16},{16,8},{24,0},{1,25},{9,17},{17,9},{25,1},{2,26},{10... | collective-permute-start | bytes 786440 | tf_op jit(solution)/shard_map/ppermute | solution.py:181
  6.4 13.5 %collective-permute-start.2 = (bf16[512,256]{1,0:T(8,128)(2,1)S(1)}, bf16[512,256]{1,0:T(8,128)(2,1)S(1)}, u32[]{:S(2)}, u32[]{:S(2)}) collective-permute-start(bf16[512,256]{1,0:T(8,128)(2,1)S(1)} %pad_maximum_fusion.4.refs_8_), channel_id=1, source_target_pairs={{0,16},{8,24},{16,0},{24,8},{1,17},{9,25},{17,1},{25,9},{2,18},{10... | collective-permute-start | bytes 786440 | tf_op jit(solution)/shard_map/ppermute | solution.py:181
  6.9 13.0 %collective-permute-start.1 = (bf16[512,256]{1,0:T(8,128)(2,1)S(1)}, bf16[512,256]{1,0:T(8,128)(2,1)S(1)}, u32[]{:S(2)}, u32[]{:S(2)}) collective-permute-start(bf16[512,256]{1,0:T(8,128)(2,1)S(1)} %pad_maximum_fusion.4.refs_8_), channel_id=1, source_target_pairs={{0,8},{8,0},{16,24},{24,16},{1,9},{9,1},{17,25},{25,17},{2,10},{10... | collective-permute-start | bytes 786440 | tf_op jit(solution)/shard_map/ppermute | solution.py:181
  7.0 17.3 %copy-start.39 = (s32[128,2]{0,1:T(2,128)S(1)}, s32[128,2]{0,1:T(2,128)}, u32[]{:S(2)}) copy-start(s32[128,2]{0,1:T(2,128)} %param.20) | copy-start | bytes 3076
  7.0 17.3 %copy-start.40 = (f32[128,2]{0,1:T(2,128)S(1)}, f32[128,2]{0,1:T(2,128)}, u32[]{:S(2)}) copy-start(f32[128,2]{0,1:T(2,128)} %param.21) | copy-start | bytes 3076
  7.0 20.1 %copy-start.23 = (bf16[128,4096]{1,0:T(8,128)(2,1)S(1)}, bf16[128,4096]{1,0:T(8,128)(2,1)}, u32[]{:S(2)}) copy-start(bf16[128,4096]{1,0:T(8,128)(2,1)} %param.19) | copy-start | bytes 3145732
  19.9 18.1 %copy-start.31 = (bf16[512,256]{1,0:T(8,128)(2,1)}, bf16[512,256]{1,0:T(8,128)(2,1)S(1)}, u32[]{:S(2)}) copy-start(bf16[512,256]{1,0:T(8,128)(2,1)S(1)} %collective-permute-done.3.refs_11_) | copy-start | bytes 786436
  20.0 4.4 %collective-permute-start.4 = (bf16[1024,256]{1,0:T(8,128)(2,1)}, bf16[1024,256]{1,0:T(8,128)(2,1)S(1)}, u32[]{:S(2)}, u32[]{:S(2)}) collective-permute-start(bf16[1024,256]{1,0:T(8,128)(2,1)} %get-tuple-element.147.refs_0_), channel_id=1, source_target_pairs={{0,1},{1,0},{2,3},{3,2},{4,5},{5,4},{6,7},{7,6},{8,9},{9,8},{10,11... | collective-permute-start | bytes 1572872 | tf_op jit(solution)/shard_map/ppermute | solution.py:178
  20.8 26.3 %collective-permute-start.5 = (bf16[1024,256]{1,0:T(8,128)(2,1)}, bf16[1024,256]{1,0:T(8,128)(2,1)S(1)}, u32[]{:S(2)}, u32[]{:S(2)}) collective-permute-start(bf16[1024,256]{1,0:T(8,128)(2,1)} %get-tuple-element.137), channel_id=1, source_target_pairs={{0,8},{8,0},{16,24},{24,16},{1,9},{9,1},{17,25},{25,17},{2,10},{10... | collective-permute-start | bytes 1572872 | tf_op jit(solution)/shard_map/ppermute | solution.py:181
  22.7 30.5 %collective-permute-start.6 = (bf16[1024,256]{1,0:T(8,128)(2,1)}, bf16[1024,256]{1,0:T(8,128)(2,1)S(1)}, u32[]{:S(2)}, u32[]{:S(2)}) collective-permute-start(bf16[1024,256]{1,0:T(8,128)(2,1)} %get-tuple-element.138), channel_id=1, source_target_pairs={{0,16},{8,24},{16,0},{24,8},{1,17},{9,25},{17,1},{25,9},{2,18},{10... | collective-permute-start | bytes 1572872 | tf_op jit(solution)/shard_map/ppermute | solution.py:181
  24.2 28.9 %collective-permute-start.7 = (bf16[1024,256]{1,0:T(8,128)(2,1)}, bf16[1024,256]{1,0:T(8,128)(2,1)}, u32[]{:S(2)}, u32[]{:S(2)}) collective-permute-start(bf16[1024,256]{1,0:T(8,128)(2,1)} %get-tuple-element.139), channel_id=1, source_target_pairs={{0,24},{8,16},{16,8},{24,0},{1,25},{9,17},{17,9},{25,1},{2,26},{10... | collective-permute-start | bytes 1572872 | tf_op jit(solution)/shard_map/ppermute | solution.py:181
  24.3 17.7 %copy-start.1 = (bf16[1024,256]{1,0:T(8,128)(2,1)}, bf16[1024,256]{1,0:T(8,128)(2,1)S(1)}, u32[]{:S(2)}) copy-start(bf16[1024,256]{1,0:T(8,128)(2,1)S(1)} %collective-permute-done.4.refs_1_) | copy-start | bytes 1572868
  24.4 3.9 %collective-permute-start.13 = (f32[1,4,128]{2,1,0:T(4,128)S(1)}, f32[1,4,128]{2,1,0:T(4,128)S(1)}, u32[]{:S(2)}, u32[]{:S(2)}) collective-permute-start(f32[1,4,128]{2,1,0:T(4,128)S(1)} %maximum_bitcast_fusion), channel_id=1, source_target_pairs={{0,1},{1,0},{2,3},{3,2},{4,5},{5,4},{6,7},{7,6},{8,9},{9,8},{10,11... | collective-permute-start | bytes 6152 | tf_op jit(solution)/shard_map/ppermute | solution.py:232
  26.7 15.3 %collective-permute-start.8 = (bf16[256,1792]{1,0:T(8,128)(2,1)}, bf16[256,1792]{1,0:T(8,128)(2,1)}, u32[]{:S(2)}, u32[]{:S(2)}) collective-permute-start(bf16[256,1792]{1,0:T(8,128)(2,1)} %constant_dynamic-slice_fusion.5), channel_id=1, source_target_pairs={{0,1},{1,0},{2,3},{3,2},{4,5},{5,4},{6,7},{7,6},{8,9},{9,8},{10,11... | collective-permute-start | bytes 2752520 | tf_op jit(solution)/shard_map/ppermute | solution.py:178
  28.3 4.1 %collective-permute-start.14 = (f32[2,4,128]{2,1,0:T(4,128)S(1)}, f32[2,4,128]{2,1,0:T(4,128)S(1)}, u32[]{:S(2)}, u32[]{:S(2)}) collective-permute-start(f32[2,4,128]{2,1,0:T(4,128)S(1)} %pad_maximum_fusion.8), channel_id=1, source_target_pairs={{0,2},{1,3},{2,0},{3,1},{4,6},{5,7},{6,4},{7,5},{8,10},{9,11},{10,... | collective-permute-start | bytes 12296 | tf_op jit(solution)/shard_map/ppermute | solution.py:232
  32.3 4.6 %collective-permute-start.15 = (f32[4,4,128]{2,1,0:T(4,128)S(1)}, f32[4,4,128]{2,1,0:T(4,128)S(1)}, u32[]{:S(2)}, u32[]{:S(2)}) collective-permute-start(f32[4,4,128]{2,1,0:T(4,128)S(1)} %pad_maximum_fusion.7), channel_id=1, source_target_pairs={{0,4},{1,5},{2,6},{3,7},{4,0},{5,1},{6,2},{7,3},{8,12},{9,13},{10,... | collective-permute-start | bytes 24584 | tf_op jit(solution)/shard_map/ppermute | solution.py:232
  37.0 2.1 %collective-permute-start.12 = (bf16[128,2048]{1,0:T(8,128)(2,1)}, bf16[128,2048]{1,0:T(8,128)(2,1)S(1)}, u32[]{:S(2)}, u32[]{:S(2)}) collective-permute-start(bf16[128,2048]{1,0:T(8,128)(2,1)} %get-tuple-element.270), channel_id=1, source_target_pairs={{0,1},{1,0},{2,3},{3,2},{4,5},{5,4},{6,7},{7,6},{8,9},{9,8},{10,11... | collective-permute-start | bytes 1572872 | tf_op jit(solution)/shard_map/ppermute | solution.py:178
  37.9 10.7 %copy-start.25 = (bf16[256,512]{1,0:T(8,128)(2,1)S(1)}, bf16[256,512]{1,0:T(8,128)(2,1)}, u32[]{:S(2)}) copy-start(bf16[256,512]{1,0:T(8,128)(2,1)} %get-tuple-element.259) | copy-start | bytes 786436
  43.0 26.1 %copy-start.21 = (bf16[512,256]{1,0:T(8,128)(2,1)}, bf16[512,256]{1,0:T(8,128)(2,1)S(1)}, u32[]{:S(2)}) copy-start(bf16[512,256]{1,0:T(8,128)(2,1)S(1)} %pad_maximum_fusion.5.refs_8_) | copy-start | bytes 786436
  43.0 10.6 %collective-permute-start.11 = (bf16[512,256]{1,0:T(8,128)(2,1)S(1)}, bf16[512,256]{1,0:T(8,128)(2,1)S(1)}, u32[]{:S(2)}, u32[]{:S(2)}) collective-permute-start(bf16[512,256]{1,0:T(8,128)(2,1)S(1)} %pad_maximum_fusion.5.refs_8_), channel_id=1, source_target_pairs={{0,24},{8,16},{16,8},{24,0},{1,25},{9,17},{17,9},{25,1},{2,26},{10... | collective-permute-start | bytes 786440 | tf_op jit(solution)/shard_map/ppermute | solution.py:181
  45.5 13.4 %collective-permute-start.10 = (bf16[512,256]{1,0:T(8,128)(2,1)S(1)}, bf16[512,256]{1,0:T(8,128)(2,1)S(1)}, u32[]{:S(2)}, u32[]{:S(2)}) collective-permute-start(bf16[512,256]{1,0:T(8,128)(2,1)S(1)} %pad_maximum_fusion.5.refs_8_), channel_id=1, source_target_pairs={{0,16},{8,24},{16,0},{24,8},{1,17},{9,25},{17,1},{25,9},{2,18},{10... | collective-permute-start | bytes 786440 | tf_op jit(solution)/shard_map/ppermute | solution.py:181
  47.2 17.6 %copy-start.2 = (bf16[1024,256]{1,0:T(8,128)(2,1)}, bf16[1024,256]{1,0:T(8,128)(2,1)S(1)}, u32[]{:S(2)}) copy-start(bf16[1024,256]{1,0:T(8,128)(2,1)S(1)} %collective-permute-done.5.refs_2_) | copy-start | bytes 1572868
  47.2 11.7 %collective-permute-start.9 = (bf16[512,256]{1,0:T(8,128)(2,1)S(1)}, bf16[512,256]{1,0:T(8,128)(2,1)S(1)}, u32[]{:S(2)}, u32[]{:S(2)}) collective-permute-start(bf16[512,256]{1,0:T(8,128)(2,1)S(1)} %pad_maximum_fusion.5.refs_8_), channel_id=1, source_target_pairs={{0,8},{8,0},{16,24},{24,16},{1,9},{9,1},{17,25},{25,17},{2,10},{10... | collective-permute-start | bytes 786440 | tf_op jit(solution)/shard_map/ppermute | solution.py:181
  53.2 11.6 %copy-start.3 = (bf16[1024,256]{1,0:T(8,128)(2,1)}, bf16[1024,256]{1,0:T(8,128)(2,1)S(1)}, u32[]{:S(2)}) copy-start(bf16[1024,256]{1,0:T(8,128)(2,1)S(1)} %collective-permute-done.6.refs_4_) | copy-start | bytes 1572868
  58.9 2.0 collective-permute-start.16
  59.6 2.2 %collective-permute-start.17 = (bf16[1024,256]{1,0:T(8,128)(2,1)S(1)}, bf16[1024,256]{1,0:T(8,128)(2,1)}, u32[]{:S(2)}, u32[]{:S(2)}) collective-permute-start(bf16[1024,256]{1,0:T(8,128)(2,1)S(1)} %collective-permute-done.6.refs_4_), channel_id=1, source_target_pairs={{0,1},{1,0},{2,3},{3,2},{4,5},{5,4},{6,7},{7,6},{8,9},{9,8},{10,11... | collective-permute-start | bytes 1572872 | tf_op jit(solution)/shard_map/ppermute | solution.py:178
  59.7 3.0 %collective-permute-start.18 = (bf16[1024,256]{1,0:T(8,128)(2,1)}, bf16[1024,256]{1,0:T(8,128)(2,1)}, u32[]{:S(2)}, u32[]{:S(2)}) collective-permute-start(bf16[1024,256]{1,0:T(8,128)(2,1)} %collective-permute-done.7.refs_6_), channel_id=1, source_target_pairs={{0,1},{1,0},{2,3},{3,2},{4,5},{5,4},{6,7},{7,6},{8,9},{9,8},{10,11... | collective-permute-start | bytes 1572872 | tf_op jit(solution)/shard_map/ppermute | solution.py:178
  62.7 17.8 %collective-permute-start.20 = (bf16[512,512]{1,0:T(8,128)(2,1)}, bf16[512,512]{1,0:T(8,128)(2,1)}, u32[]{:S(2)}, u32[]{:S(2)}) collective-permute-start(bf16[512,512]{1,0:T(8,128)(2,1)} %get-tuple-element.186.refs_8_), channel_id=1, source_target_pairs={{0,16},{8,24},{16,0},{24,8},{1,17},{9,25},{17,1},{25,9},{2,18},{10... | collective-permute-start | bytes 1572872 | tf_op jit(solution)/shard_map/ppermute | solution.py:181
  64.2 16.3 %collective-permute-start.19 = (bf16[512,512]{1,0:T(8,128)(2,1)}, bf16[512,512]{1,0:T(8,128)(2,1)}, u32[]{:S(2)}, u32[]{:S(2)}) collective-permute-start(bf16[512,512]{1,0:T(8,128)(2,1)} %get-tuple-element.186.refs_8_), channel_id=1, source_target_pairs={{0,8},{8,0},{16,24},{24,16},{1,9},{9,1},{17,25},{25,17},{2,10},{10... | collective-permute-start | bytes 1572872 | tf_op jit(solution)/shard_map/ppermute | solution.py:181
  69.1 16.3 %copy-start.15 = (bf16[1024,256]{1,0:T(8,128)(2,1)S(1)}, bf16[1024,256]{1,0:T(8,128)(2,1)}, u32[]{:S(2)}) copy-start(bf16[1024,256]{1,0:T(8,128)(2,1)} %partial_product.5) | copy-start | bytes 1572868
  69.1 16.3 %collective-permute-start.22 = (bf16[1024,256]{1,0:T(8,128)(2,1)}, bf16[1024,256]{1,0:T(8,128)(2,1)}, u32[]{:S(2)}, u32[]{:S(2)}) collective-permute-start(bf16[1024,256]{1,0:T(8,128)(2,1)} %partial_product.5), channel_id=1, source_target_pairs={{0,2},{1,3},{6,4},{7,5},{8,10},{9,11},{14,12},{15,13},{16,18},{17,... | collective-permute-start | bytes 1572872 | tf_op jit(solution)/shard_map/ppermute | solution.py:191
  73.5 15.9 %collective-permute-start.21 = (bf16[512,512]{1,0:T(8,128)(2,1)}, bf16[512,512]{1,0:T(8,128)(2,1)}, u32[]{:S(2)}, u32[]{:S(2)}) collective-permute-start(bf16[512,512]{1,0:T(8,128)(2,1)} %get-tuple-element.186.refs_8_), channel_id=1, source_target_pairs={{0,24},{8,16},{16,8},{24,0},{1,25},{9,17},{17,9},{25,1},{2,26},{10... | collective-permute-start | bytes 1572872 | tf_op jit(solution)/shard_map/ppermute | solution.py:181
  79.2 26.2 %collective-permute-start.24 = (bf16[1024,256]{1,0:T(8,128)(2,1)}, bf16[1024,256]{1,0:T(8,128)(2,1)S(1)}, u32[]{:S(2)}, u32[]{:S(2)}) collective-permute-start(bf16[1024,256]{1,0:T(8,128)(2,1)} %partial_product.6), channel_id=1, source_target_pairs={{0,2},{1,3},{6,4},{7,5},{8,10},{9,11},{14,12},{15,13},{16,18},{17,... | collective-permute-start | bytes 1572872 | tf_op jit(solution)/shard_map/ppermute | solution.py:191
  89.4 16.9 %collective-permute-start.26 = (bf16[512,512]{1,0:T(8,128)(2,1)}, bf16[512,512]{1,0:T(8,128)(2,1)}, u32[]{:S(2)}, u32[]{:S(2)}) collective-permute-start(bf16[512,512]{1,0:T(8,128)(2,1)} %get-tuple-element.210.refs_8_), channel_id=1, source_target_pairs={{0,16},{8,24},{16,0},{24,8},{1,17},{9,25},{17,1},{25,9},{2,18},{10... | collective-permute-start | bytes 1572872 | tf_op jit(solution)/shard_map/ppermute | solution.py:181
  90.9 15.4 %collective-permute-start.25 = (bf16[512,512]{1,0:T(8,128)(2,1)}, bf16[512,512]{1,0:T(8,128)(2,1)}, u32[]{:S(2)}, u32[]{:S(2)}) collective-permute-start(bf16[512,512]{1,0:T(8,128)(2,1)} %get-tuple-element.210.refs_8_), channel_id=1, source_target_pairs={{0,8},{8,0},{16,24},{24,16},{1,9},{9,1},{17,25},{25,17},{2,10},{10... | collective-permute-start | bytes 1572872 | tf_op jit(solution)/shard_map/ppermute | solution.py:181
  91.5 14.8 %collective-permute-start.23 = (bf16[1024,256]{1,0:T(8,128)(2,1)S(1)}, bf16[1024,256]{1,0:T(8,128)(2,1)S(1)}, u32[]{:S(2)}, u32[]{:S(2)}) collective-permute-start(bf16[1024,256]{1,0:T(8,128)(2,1)S(1)} %add_convert_fusion.15), channel_id=1, source_target_pairs={{2,4},{3,5},{4,2},{5,3},{10,12},{11,13},{12,10},{13,11},{18,20},{1... | collective-permute-start | bytes 1572872 | tf_op jit(solution)/shard_map/ppermute | solution.py:191
  93.1 12.4 %copy-start.14 = (bf16[1024,256]{1,0:T(8,128)(2,1)S(1)}, bf16[1024,256]{1,0:T(8,128)(2,1)}, u32[]{:S(2)}) copy-start(bf16[1024,256]{1,0:T(8,128)(2,1)} %partial_product.6) | copy-start | bytes 1572868
  93.1 13.3 %copy-start.28 = (bf16[512,512]{1,0:T(8,128)(2,1)S(1)}, bf16[512,512]{1,0:T(8,128)(2,1)}, u32[]{:S(2)}) copy-start(bf16[512,512]{1,0:T(8,128)(2,1)} %get-tuple-element.210.refs_8_) | copy-start | bytes 1572868
  99.0 19.1 %copy-start.27 = (bf16[1024,256]{1,0:T(8,128)(2,1)S(1)}, bf16[1024,256]{1,0:T(8,128)(2,1)}, u32[]{:S(2)}) copy-start(bf16[1024,256]{1,0:T(8,128)(2,1)} %get-tuple-element.202) | copy-start | bytes 1572868
  99.0 19.1 %collective-permute-start.30 = (bf16[1024,256]{1,0:T(8,128)(2,1)}, bf16[1024,256]{1,0:T(8,128)(2,1)S(1)}, u32[]{:S(2)}, u32[]{:S(2)}) collective-permute-start(bf16[1024,256]{1,0:T(8,128)(2,1)} %get-tuple-element.202), channel_id=1, source_target_pairs={{0,2},{1,3},{6,4},{7,5},{8,10},{9,11},{14,12},{15,13},{16,18},{17,... | collective-permute-start | bytes 1572872 | tf_op jit(solution)/shard_map/ppermute | solution.py:191
  105.6 13.3 %collective-permute-start.29 = (bf16[1024,256]{1,0:T(8,128)(2,1)S(1)}, bf16[1024,256]{1,0:T(8,128)(2,1)S(1)}, u32[]{:S(2)}, u32[]{:S(2)}) collective-permute-start(bf16[1024,256]{1,0:T(8,128)(2,1)S(1)} %add_convert_fusion.14), channel_id=1, source_target_pairs={{2,4},{3,5},{4,2},{5,3},{10,12},{11,13},{12,10},{13,11},{18,20},{1... | collective-permute-start | bytes 1572872 | tf_op jit(solution)/shard_map/ppermute | solution.py:191
  106.4 12.7 %collective-permute-start.28 = (bf16[512,512]{1,0:T(8,128)(2,1)S(1)}, bf16[512,512]{1,0:T(8,128)(2,1)S(1)}, u32[]{:S(2)}, u32[]{:S(2)}) collective-permute-start(bf16[512,512]{1,0:T(8,128)(2,1)S(1)} %copy-done.28), channel_id=1, source_target_pairs={{0,24},{8,16},{16,8},{24,0},{1,25},{9,17},{17,9},{25,1},{2,26},{10... | collective-permute-start | bytes 1572872 | tf_op jit(solution)/shard_map/ppermute | solution.py:181
  109.9 21.4 %collective-permute-start.27 = (bf16[1024,256]{1,0:T(8,128)(2,1)}, bf16[1024,256]{1,0:T(8,128)(2,1)}, u32[]{:S(2)}, u32[]{:S(2)}) collective-permute-start(bf16[1024,256]{1,0:T(8,128)(2,1)} %broadcast_select_fusion.13), channel_id=1, source_target_pairs={{0,2},{1,3},{2,0},{3,1},{4,6},{5,7},{6,4},{7,5},{8,10},{9,11},{10,... | collective-permute-start | bytes 1572872 | tf_op jit(solution)/shard_map/ppermute | solution.py:191
  118.2 16.6 %collective-permute-start.32 = (bf16[1024,256]{1,0:T(8,128)(2,1)S(1)}, bf16[1024,256]{1,0:T(8,128)(2,1)S(1)}, u32[]{:S(2)}, u32[]{:S(2)}) collective-permute-start(bf16[1024,256]{1,0:T(8,128)(2,1)S(1)} %add_convert_fusion.12), channel_id=1, source_target_pairs={{2,4},{3,5},{4,2},{5,3},{10,12},{11,13},{12,10},{13,11},{18,20},{1... | collective-permute-start | bytes 1572872 | tf_op jit(solution)/shard_map/ppermute | solution.py:191
  119.0 17.6 %collective-permute-start.34 = (bf16[512,512]{1,0:T(8,128)(2,1)}, bf16[512,512]{1,0:T(8,128)(2,1)}, u32[]{:S(2)}, u32[]{:S(2)}) collective-permute-start(bf16[512,512]{1,0:T(8,128)(2,1)} %pad_maximum_fusion.2.refs_8_), channel_id=1, source_target_pairs={{0,16},{8,24},{16,0},{24,8},{1,17},{9,25},{17,1},{25,9},{2,18},{10... | collective-permute-start | bytes 1572872 | tf_op jit(solution)/shard_map/ppermute | solution.py:181
  120.2 16.4 %collective-permute-start.33 = (bf16[512,512]{1,0:T(8,128)(2,1)}, bf16[512,512]{1,0:T(8,128)(2,1)}, u32[]{:S(2)}, u32[]{:S(2)}) collective-permute-start(bf16[512,512]{1,0:T(8,128)(2,1)} %pad_maximum_fusion.2.refs_8_), channel_id=1, source_target_pairs={{0,8},{8,0},{16,24},{24,16},{1,9},{9,1},{17,25},{25,17},{2,10},{10... | collective-permute-start | bytes 1572872 | tf_op jit(solution)/shard_map/ppermute | solution.py:181
  128.3 14.3 %collective-permute-start.31 = (bf16[1024,256]{1,0:T(8,128)(2,1)S(1)}, bf16[1024,256]{1,0:T(8,128)(2,1)S(1)}, u32[]{:S(2)}, u32[]{:S(2)}) collective-permute-start(bf16[1024,256]{1,0:T(8,128)(2,1)S(1)} %broadcast_select_fusion.12), channel_id=1, source_target_pairs={{0,2},{1,3},{2,0},{3,1},{4,6},{5,7},{6,4},{7,5},{8,10},{9,11},{10,... | collective-permute-start | bytes 1572872 | tf_op jit(solution)/shard_map/ppermute | solution.py:191
  134.2 11.4 %collective-permute-start.37 = (bf16[1024,256]{1,0:T(8,128)(2,1)S(1)}, bf16[1024,256]{1,0:T(8,128)(2,1)S(1)}, u32[]{:S(2)}, u32[]{:S(2)}) collective-permute-start(bf16[1024,256]{1,0:T(8,128)(2,1)S(1)} %add_convert_fusion.10), channel_id=1, source_target_pairs={{2,4},{3,5},{4,2},{5,3},{10,12},{11,13},{12,10},{13,11},{18,20},{1... | collective-permute-start | bytes 1572872 | tf_op jit(solution)/shard_map/ppermute | solution.py:191
  136.7 10.3 %collective-permute-start.36 = (bf16[512,512]{1,0:T(8,128)(2,1)}, bf16[512,512]{1,0:T(8,128)(2,1)S(1)}, u32[]{:S(2)}, u32[]{:S(2)}) collective-permute-start(bf16[512,512]{1,0:T(8,128)(2,1)} %pad_maximum_fusion.2.refs_8_), channel_id=1, source_target_pairs={{0,24},{8,16},{16,8},{24,0},{1,25},{9,17},{17,9},{25,1},{2,26},{10... | collective-permute-start | bytes 1572872 | tf_op jit(solution)/shard_map/ppermute | solution.py:181
  138.1 19.1 %collective-permute-start.35 = (bf16[1024,256]{1,0:T(8,128)(2,1)}, bf16[1024,256]{1,0:T(8,128)(2,1)S(1)}, u32[]{:S(2)}, u32[]{:S(2)}) collective-permute-start(bf16[1024,256]{1,0:T(8,128)(2,1)} %broadcast_select_fusion.10), channel_id=1, source_target_pairs={{0,2},{1,3},{2,0},{3,1},{4,6},{5,7},{6,4},{7,5},{8,10},{9,11},{10,... | collective-permute-start | bytes 1572872 | tf_op jit(solution)/shard_map/ppermute | solution.py:191
  143.2 15.2 %collective-permute-start.39 = (bf16[1024,256]{1,0:T(8,128)(2,1)S(1)}, bf16[1024,256]{1,0:T(8,128)(2,1)}, u32[]{:S(2)}, u32[]{:S(2)}) collective-permute-start(bf16[1024,256]{1,0:T(8,128)(2,1)S(1)} %add_convert_fusion.8), channel_id=1, source_target_pairs={{2,4},{3,5},{4,2},{5,3},{10,12},{11,13},{12,10},{13,11},{18,20},{1... | collective-permute-start | bytes 1572872 | tf_op jit(solution)/shard_map/ppermute | solution.py:191
  154.9 14.1 %collective-permute-start.38 = (bf16[1024,256]{1,0:T(8,128)(2,1)S(1)}, bf16[1024,256]{1,0:T(8,128)(2,1)S(1)}, u32[]{:S(2)}, u32[]{:S(2)}) collective-permute-start(bf16[1024,256]{1,0:T(8,128)(2,1)S(1)} %broadcast_select_fusion.8), channel_id=1, source_target_pairs={{0,2},{1,3},{2,0},{3,1},{4,6},{5,7},{6,4},{7,5},{8,10},{9,11},{10,... | collective-permute-start | bytes 1572872 | tf_op jit(solution)/shard_map/ppermute | solution.py:191
  157.4 11.6 %copy-start.13 = (bf16[1024,256]{1,0:T(8,128)(2,1)S(1)}, bf16[1024,256]{1,0:T(8,128)(2,1)}, u32[]{:S(2)}) copy-start(bf16[1024,256]{1,0:T(8,128)(2,1)} %get-tuple-element.245) | copy-start | bytes 1572868
  157.4 12.7 %collective-permute-start.41 = (bf16[1024,256]{1,0:T(8,128)(2,1)S(1)}, bf16[1024,256]{1,0:T(8,128)(2,1)S(1)}, u32[]{:S(2)}, u32[]{:S(2)}) collective-permute-start(bf16[1024,256]{1,0:T(8,128)(2,1)S(1)} %add_convert_fusion.6), channel_id=1, source_target_pairs={{2,4},{3,5},{4,2},{5,3},{10,12},{11,13},{12,10},{13,11},{18,20},{1... | collective-permute-start | bytes 1572872 | tf_op jit(solution)/shard_map/ppermute | solution.py:191
  160.5 19.7 %collective-permute-start.40 = (bf16[1024,256]{1,0:T(8,128)(2,1)S(1)}, bf16[1024,256]{1,0:T(8,128)(2,1)S(1)}, u32[]{:S(2)}, u32[]{:S(2)}) collective-permute-start(bf16[1024,256]{1,0:T(8,128)(2,1)S(1)} %broadcast_select_fusion.6), channel_id=1, source_target_pairs={{0,2},{1,3},{2,0},{3,1},{4,6},{5,7},{6,4},{7,5},{8,10},{9,11},{10,... | collective-permute-start | bytes 1572872 | tf_op jit(solution)/shard_map/ppermute | solution.py:191
  169.1 13.6 %collective-permute-start.43 = (bf16[1024,256]{1,0:T(8,128)(2,1)S(1)}, bf16[1024,256]{1,0:T(8,128)(2,1)S(1)}, u32[]{:S(2)}, u32[]{:S(2)}) collective-permute-start(bf16[1024,256]{1,0:T(8,128)(2,1)S(1)} %add_convert_fusion.4), channel_id=1, source_target_pairs={{2,4},{3,5},{4,2},{5,3},{10,12},{11,13},{12,10},{13,11},{18,20},{1... | collective-permute-start | bytes 1572872 | tf_op jit(solution)/shard_map/ppermute | solution.py:191
  170.2 21.3 %collective-permute-start.42 = (bf16[1024,256]{1,0:T(8,128)(2,1)S(1)}, bf16[1024,256]{1,0:T(8,128)(2,1)S(1)}, u32[]{:S(2)}, u32[]{:S(2)}) collective-permute-start(bf16[1024,256]{1,0:T(8,128)(2,1)S(1)} %add_convert_fusion.3), channel_id=1, source_target_pairs={{2,0},{3,1},{4,6},{5,7},{10,8},{11,9},{12,14},{13,15},{18,16},{19,... | collective-permute-start | bytes 1572872 | tf_op jit(solution)/shard_map/ppermute | solution.py:191
  181.9 2.3 %collective-permute-start.45 = (bf16[1024,256]{1,0:T(8,128)(2,1)S(1)}, bf16[1024,256]{1,0:T(8,128)(2,1)S(1)}, u32[]{:S(2)}, u32[]{:S(2)}) collective-permute-start(bf16[1024,256]{1,0:T(8,128)(2,1)S(1)} %add_convert_fusion.2), channel_id=1, source_target_pairs={{2,4},{3,5},{4,2},{5,3},{10,12},{11,13},{12,10},{13,11},{18,20},{1... | collective-permute-start | bytes 1572872 | tf_op jit(solution)/shard_map/ppermute | solution.py:191
  182.9 23.6 %collective-permute-start.44 = (bf16[1024,256]{1,0:T(8,128)(2,1)S(1)}, bf16[1024,256]{1,0:T(8,128)(2,1)S(1)}, u32[]{:S(2)}, u32[]{:S(2)}) collective-permute-start(bf16[1024,256]{1,0:T(8,128)(2,1)S(1)} %add_convert_fusion.1), channel_id=1, source_target_pairs={{2,0},{3,1},{4,6},{5,7},{10,8},{11,9},{12,14},{13,15},{18,16},{19,... | collective-permute-start | bytes 1572872 | tf_op jit(solution)/shard_map/ppermute | solution.py:191
  184.4 21.7 %collective-permute-start.46 = (bf16[1024,256]{1,0:T(8,128)(2,1)S(1)}, bf16[1024,256]{1,0:T(8,128)(2,1)S(1)}, u32[]{:S(2)}, u32[]{:S(2)}) collective-permute-start(bf16[1024,256]{1,0:T(8,128)(2,1)S(1)} %add_convert_fusion), channel_id=1, source_target_pairs={{2,0},{3,1},{4,6},{5,7},{10,8},{11,9},{12,14},{13,15},{18,16},{19,... | collective-permute-start | bytes 1572872 | tf_op jit(solution)/shard_map/ppermute | solution.py:191
  191.9 15.2 %collective-permute-start.47 = (bf16[448,1536]{1,0:T(8,128)(2,1)S(1)}, bf16[448,1536]{1,0:T(8,128)(2,1)S(1)}, u32[]{:S(2)}, u32[]{:S(2)}) collective-permute-start(bf16[448,1536]{1,0:T(8,128)(2,1)S(1)} %constant_dynamic-update-slice_fusion), channel_id=1, source_target_pairs={{0,1},{1,0},{2,3},{3,2},{4,5},{5,4},{6,7},{7,6},{8,9},{9,8},{10,11... | collective-permute-start | bytes 4128776 | tf_op jit(solution)/shard_map/ppermute | solution.py:178
  206.9 1.9 collective-permute-start.48
  (28 other events, 127.3 us)

commit v14 on v13

--- a/solution.py
+++ b/solution.py
@@ -9,8 +9,9 @@
 
 EXP_DEV = 1
 GROUPS = ((1,), (1,), (1, 1), (1, 1), (1, 1))
-FIRST_PHASE = {2: 3, 4: 4}
-SECOND_PHASE = {3: 3, 5: 4}
+NEAR_AFTER = {1: 3, 3: 4}
+FAR_AFTER = {2: 3, 4: 4}
+PRODUCT_AFTER = {3: 3, 5: 4}
 UNITS = sum(map(sum, GROUPS))
 DELAY = 3
 SWAPS = (6, 8)
@@ -336,14 +337,8 @@
             got, index = across[step - 1]
             own, got = chain(sums[hops][index], got)
             ready[hops][index] = add(own, got)
-        if step in SECOND_PHASE and square:
-            rights[SECOND_PHASE[step]] = spread_far(rights[SECOND_PHASE[step]])
         group_at = first_of.index(step) if step and step in first_of else None
-        if step in FIRST_PHASE:
-            coming = FIRST_PHASE[step]
-            piece, *rights[group_at] = chain(rest[coming - 1], *rights[group_at])
-            rights[coming] = spread_near(piece) if square else spread(piece)
-        if group_at:
+        if group_at and group_at not in PRODUCT_AFTER.values():
             sums[0][step : step + len(GROUPS[group_at])] = products(group_at, rights[group_at])
         for hop in range(hops):
             inward = step - lag * hop
@@ -365,6 +360,18 @@
             rights[2].append(to_ctx(piece, 3))
         if step == 1 and square:
             rights[2][1:3] = chain(*rights[2][1:3])
+        group_at = PRODUCT_AFTER.get(step)
+        if step in NEAR_AFTER:
+            coming = NEAR_AFTER[step]
+            piece, *arrived = chain(rest[coming - 1], *(rights[group_at] if group_at else []))
+            rights[coming] = spread_near(piece) if square else spread(piece)
+            if group_at:
+                rights[group_at] = arrived
+        if step in FAR_AFTER and square:
+            rights[FAR_AFTER[step]] = spread_far(rights[FAR_AFTER[step]])
+        if group_at:
+            first_piece = first_of[group_at]
+            sums[0][first_piece : first_piece + len(GROUPS[group_at])] = products(group_at, rights[group_at])
     result = jnp.where(
         core_at == 0,
         jnp.concatenate(rows_own + rows_got, axis=1),

time: 212 us -> 222 us (1.047)
  starting transfers between devices: 60.6 us -> 71.7 us
  waiting for transfers between devices: 68.9 us -> 64.3 us
  other arithmetic: 22.4 us -> 25.4 us
    ppermute x19, waiting for transfers between devices: 49.9 us -> 38.6 us  [swap_chips(): return lax.ppermute(array, 'exp', sorted(pairs))]
    ppermute x19, starting transfers between devices: 32 us -> 43.2 us  [swap_chips(): return lax.ppermute(array, 'exp', sorted(pairs))]
    ppermute x18, waiting for transfers between devices: 13.5 us -> 19.6 us  [to_ctx(): lax.ppermute(array, 'ctx', [(place, place ^ offset) for place in range(ct...]
    convert_element_type x11, other arithmetic: 3.59 us -> 7.47 us  [add(): (one.astype(jnp.float32) + other.astype(jnp.float32)).astype(jnp.bfloat16)]
    unnamed x110 -> x92, local copies, waits for them, and re-layouts: 5.43 us -> 5.54 us
  transfers between devices with their start and end apart: 49 -> 49, of which waited for: 20 -> 15; matrix products, arithmetic and copies ran while one was open for 17% -> 17% of each run, Pallas kernels for 18% -> 18%
where the time goes in v14:
time: 222 us; the launch traced here: 221 us
  starting transfers between devices  71.7 us (32%)
  waiting for transfers between devices  64.3 us (29%)
  Pallas kernels  39.1 us (18%)
  other arithmetic  25.4 us (11%)
  local copies, waits for them, and re-layouts  16.9 us (8%)
  matrix products  2.36 us (1%)
    ppermute x19, starting transfers between devices, swap_chips(): return lax.ppermute(array, 'exp', sorted(pairs))  43.2 us
    ppermute x19, waiting for transfers between devices, swap_chips(): return lax.ppermute(array, 'exp', sorted(pairs))  38.6 us
    pallas_call x5, Pallas kernels, matmul(): pl.pallas_call(functools.partial(matmul_kernel, len(lefts), len(rights)),...  26.3 us
    ppermute x18, starting transfers between devices, to_ctx(): lax.ppermute(array, 'ctx', [(place, place ^ offset) for place in range(ct...  22.2 us
    ppermute x18, waiting for transfers between devices, to_ctx(): lax.ppermute(array, 'ctx', [(place, place ^ offset) for place in range(ct...  19.6 us
    pallas_call x1, Pallas kernels, conv_grad(): pl.pallas_call(functools.partial(conv_kernel, tile), grid_spec=pltpu.Pref...  12.9 us
    convert_element_type x11, other arithmetic, add(): (one.astype(jnp.float32) + other.astype(jnp.float32)).astype(jnp.bfloat16)  7.47 us
    select_n x5, other arithmetic, on_device(): jnp.where(distance == hop, sums[hop][inward], ready[hop + 1][outward])  5.82 us
  transfers between devices with their start and end apart: 49, of which 15 were waited for; matrix products, arithmetic and copies ran while one was open for 17% of the time, Pallas kernels for 18%

profile of v14, /device:TPU:0, one launch (start us, length us, event | category | flops | bytes accessed | tf_op | source)
XLA Modules:
  0.0 221.0 jit_solution(8266556844983790372)
XLA Ops:
  0.0 1.0 constant_dynamic-slice_fusion.8
  1.5 1.0 collective-permute-done
  2.5 3.9 %collective-permute-start.3 = (bf16[512,256]{1,0:T(8,128)(2,1)S(1)}, bf16[512,256]{1,0:T(8,128)(2,1)S(1)}, u32[]{:S(2)}, u32[]{:S(2)}) collective-permute-start(bf16[512,256]{1,0:T(8,128)(2,1)S(1)} %pad_maximum_fusion.4.refs_8_), channel_id=1, source_target_pairs={{0,24},{8,16},{16,8},{24,0},{1,25},{9,17},{17,9},{25,1},{2,26},{10... | collective-permute-start | bytes 786440 | tf_op jit(solution)/shard_map/ppermute | solution.py:182
  7.0 12.9 %conv_grad.1 = (bf16[1024,256]{1,0:T(8,128)(2,1)}, bf16[1024,256]{1,0:T(8,128)(2,1)}, bf16[1024,256]{1,0:T(8,128)(2,1)}, bf16[1024,256]{1,0:T(8,128)(2,1)}) custom-call(s32[1]{0:T(128)} %bitcast.1.at_ctx, bf16[256,4096]{1,0:T(8,128)(2,1)} %out_grad.1, bf16[256,4096]{1,0:T(8,128)(2,1)} %gate_in.1, bf16[256,4096]{1,0:T(8,128)(2,1)} %conv_in.1, ...), custom_call_target="tpu_custom_call" | custom-call | flops 41943040 | bytes 10485760 | tf_op jit(solution)/shard_map/conv_grad/pallas_call | solution.py:85
  21.0 1.9 collective-permute-start.5
  22.9 1.5 collective-permute-start.6
  24.6 2.2 %constant_dynamic-slice_fusion.5 = bf16[256,1792]{1,0:T(8,128)(2,1)} fusion(bf16[256,4096]{1,0:T(8,128)(2,1)} %param.18, s32[]{:T(128)S(6)} %select_n.141), kind=kLoop, calls=%fused_computation.106 | loop fusion | bytes 1835012 | tf_op jit(solution)/shard_map/dynamic_slice | solution.py:195
  27.3 1.1 constant_dynamic-slice_fusion.4
  28.4 2.0 collective-permute-start.14
  30.4 2.0 constant_dynamic-slice_fusion.6
  32.4 2.7 %collective-permute-start.15 = (f32[4,4,128]{2,1,0:T(4,128)S(1)}, f32[4,4,128]{2,1,0:T(4,128)S(1)}, u32[]{:S(2)}, u32[]{:S(2)}) collective-permute-start(f32[4,4,128]{2,1,0:T(4,128)S(1)} %pad_maximum_fusion.7), channel_id=1, source_target_pairs={{0,4},{1,5},{2,6},{3,7},{4,0},{5,1},{6,2},{7,3},{8,12},{9,13},{10,... | collective-permute-start | bytes 24584 | tf_op jit(solution)/shard_map/ppermute | solution.py:233
  35.1 0.9 constant_dynamic-slice_fusion.2
  36.0 1.0 collective-permute-done.15
  40.0 2.1 maximum_select_fusion
  42.1 0.9 slice.140
  43.0 2.5 %collective-permute-start.11 = (bf16[512,256]{1,0:T(8,128)(2,1)S(1)}, bf16[512,256]{1,0:T(8,128)(2,1)S(1)}, u32[]{:S(2)}, u32[]{:S(2)}) collective-permute-start(bf16[512,256]{1,0:T(8,128)(2,1)S(1)} %pad_maximum_fusion.5.refs_8_), channel_id=1, source_target_pairs={{0,24},{8,16},{16,8},{24,0},{1,25},{9,17},{17,9},{25,1},{2,26},{10... | collective-permute-start | bytes 786440 | tf_op jit(solution)/shard_map/ppermute | solution.py:182
  46.0 1.2 fusion.24
  48.7 1.1 pad_maximum_fusion
  49.7 4.3 %collective-permute-done.6.refs_4_ = bf16[1024,256]{1,0:T(8,128)(2,1)S(1)} collective-permute-done((bf16[1024,256]{1,0:T(8,128)(2,1)}, bf16[1024,256]{1,0:T(8,128)(2,1)S(1)}, u32[]{:S(2)}, u32[]{:S(2)}) %collective-permute-start.6) | collective-permute-done | bytes 524320 | tf_op jit(solution)/shard_map/ppermute | solution.py:182
  54.2 5.4 %collective-permute-done.10.refs_10_ = bf16[512,256]{1,0:T(8,128)(2,1)S(1)} collective-permute-done((bf16[512,256]{1,0:T(8,128)(2,1)S(1)}, bf16[512,256]{1,0:T(8,128)(2,1)S(1)}, u32[]{:S(2)}, u32[]{:S(2)}) %collective-permute-start.10) | collective-permute-done | bytes 262176 | tf_op jit(solution)/shard_map/ppermute | solution.py:182
  61.6 1.6 collective-permute-done.17.refs_5_
  63.5 1.5 collective-permute-start.20
  65.5 4.3 %partial_product.5 = bf16[1024,256]{1,0:T(8,128)(2,1)} custom-call(s32[1]{0:T(128)} %bitcast.place, bf16[1024,256]{1,0:T(8,128)(2,1)} %get-tuple-element.143.refs_0_, bf16[1024,256]{1,0:T(8,128)(2,1)} %copy-done.1, bf16[1024,256]{1,0:T(8,128)(2,1)} %copy-done.2, bf16[1024,256]{1,0:T(8,128)(2,1)} %copy-done.4, bf16[1024,256]{1,0:T(8,128)(2,1)} %copy-done.3, ...), custom_call_target="tpu_custom_call" | custom-call | flops 1073741824 | bytes 5767168 | tf_op jit(solution)/shard_map/partial_product/pallas_call | solution.py:131
  69.9 4.4 %collective-permute-start.22 = (bf16[1024,256]{1,0:T(8,128)(2,1)}, bf16[1024,256]{1,0:T(8,128)(2,1)}, u32[]{:S(2)}, u32[]{:S(2)}) collective-permute-start(bf16[1024,256]{1,0:T(8,128)(2,1)} %partial_product.5), channel_id=1, source_target_pairs={{0,2},{1,3},{6,4},{7,5},{8,10},{9,11},{14,12},{15,13},{16,18},{17,... | collective-permute-start | bytes 1572872 | tf_op jit(solution)/shard_map/ppermute | solution.py:192
  74.3 1.4 collective-permute-start.21
  75.7 4.3 %partial_product.6 = bf16[1024,256]{1,0:T(8,128)(2,1)} custom-call(s32[1]{0:T(128)} %bitcast.place, bf16[1024,256]{1,0:T(8,128)(2,1)} %get-tuple-element.143.refs_0_, bf16[1024,256]{1,0:T(8,128)(2,1)} %copy-done.1, bf16[1024,256]{1,0:T(8,128)(2,1)} %copy-done.2, bf16[1024,256]{1,0:T(8,128)(2,1)} %copy-done.4, bf16[1024,256]{1,0:T(8,128)(2,1)} %copy-done.3, ...), custom_call_target="tpu_custom_call" | custom-call | flops 1073741824 | bytes 5767168 | tf_op jit(solution)/shard_map/partial_product/pallas_call | solution.py:131
  80.0 1.3 collective-permute-start.24
  81.4 1.6 collective-permute-start.26
  83.5 2.7 %collective-permute-done.22 = bf16[1024,256]{1,0:T(8,128)(2,1)} collective-permute-done((bf16[1024,256]{1,0:T(8,128)(2,1)}, bf16[1024,256]{1,0:T(8,128)(2,1)}, u32[]{:S(2)}, u32[]{:S(2)}) %collective-permute-start.22) | collective-permute-done | bytes 524320 | tf_op jit(solution)/shard_map/ppermute | solution.py:192
  86.2 1.2 add_convert_fusion.15
  88.0 0.9 fusion.22
  89.0 2.4 %collective-permute-done.21.refs_11_ = bf16[512,512]{1,0:T(8,128)(2,1)} collective-permute-done((bf16[512,512]{1,0:T(8,128)(2,1)}, bf16[512,512]{1,0:T(8,128)(2,1)}, u32[]{:S(2)}, u32[]{:S(2)}) %collective-permute-start.21) | collective-permute-done | bytes 524320 | tf_op jit(solution)/shard_map/ppermute | solution.py:182
  91.3 5.9 %partial_product.7 = (bf16[1024,256]{1,0:T(8,128)(2,1)}, bf16[1024,256]{1,0:T(8,128)(2,1)}) custom-call(s32[1]{0:T(128)} %bitcast.place, bf16[1024,256]{1,0:T(8,128)(2,1)} %get-tuple-element.143.refs_0_, bf16[1024,256]{1,0:T(8,128)(2,1)} %copy-done.1, bf16[1024,256]{1,0:T(8,128)(2,1)} %copy-done.2, bf16[1024,256]{1,0:T(8,128)(2,1)} %copy-done.4, ...), custom_call_target="tpu_custom_call" | custom-call | flops 2147483648 | bytes 7340032 | tf_op jit(solution)/shard_map/partial_product/pallas_call | solution.py:131
  97.2 5.6 %collective-permute-start.32 = (bf16[1024,256]{1,0:T(8,128)(2,1)}, bf16[1024,256]{1,0:T(8,128)(2,1)}, u32[]{:S(2)}, u32[]{:S(2)}) collective-permute-start(bf16[1024,256]{1,0:T(8,128)(2,1)} %get-tuple-element.204), channel_id=1, source_target_pairs={{0,2},{1,3},{6,4},{7,5},{8,10},{9,11},{14,12},{15,13},{16,18},{17,... | collective-permute-start | bytes 1572872 | tf_op jit(solution)/shard_map/ppermute | solution.py:192
  102.9 1.4 collective-permute-start.28
  105.2 2.2 %broadcast_select_fusion.13 = bf16[1024,256]{1,0:T(8,128)(2,1)} fusion(bf16[1024,256]{1,0:T(8,128)(2,1)} %get-tuple-element.216, pred[]{:T(512)S(6)} %eq.31, bf16[1024,256]{1,0:T(8,128)(2,1)S(1)} %collective-permute-done.23, bf16[1024,256]{1,0:T(8,128)(2,1)S(1)} %add_convert_fusion.15), kind=kLoop, calls=%fused_computation.62 | loop fusion | flops 1310720 | bytes 2097153 | tf_op jit(solution)/shard_map/jit(_where)/select_n | solution.py:349
  107.4 1.8 collective-permute-start.27
  109.1 7.3 %collective-permute-done.28.refs_11_ = bf16[512,512]{1,0:T(8,128)(2,1)} collective-permute-done((bf16[512,512]{1,0:T(8,128)(2,1)}, bf16[512,512]{1,0:T(8,128)(2,1)}, u32[]{:S(2)}, u32[]{:S(2)}) %collective-permute-start.28) | collective-permute-done | bytes 524320 | tf_op jit(solution)/shard_map/ppermute | solution.py:182
  116.5 1.5 collective-permute-start.30
  118.5 5.8 %partial_product.8 = (bf16[1024,256]{1,0:T(8,128)(2,1)}, bf16[1024,256]{1,0:T(8,128)(2,1)}) custom-call(s32[1]{0:T(128)} %bitcast.place, bf16[1024,256]{1,0:T(8,128)(2,1)} %get-tuple-element.143.refs_0_, bf16[1024,256]{1,0:T(8,128)(2,1)} %copy-done.1, bf16[1024,256]{1,0:T(8,128)(2,1)} %copy-done.2, bf16[1024,256]{1,0:T(8,128)(2,1)} %copy-done.4, ...), custom_call_target="tpu_custom_call" | custom-call | flops 2147483648 | bytes 7340032 | tf_op jit(solution)/shard_map/partial_product/pallas_call | solution.py:131
  124.4 1.4 add_convert_fusion.12
  126.6 2.2 %broadcast_select_fusion.12 = bf16[1024,256]{1,0:T(8,128)(2,1)} fusion(bf16[1024,256]{1,0:T(8,128)(2,1)} %get-tuple-element.226, pred[]{:T(512)S(6)} %eq.31, bf16[1024,256]{1,0:T(8,128)(2,1)S(1)} %collective-permute-done.31, bf16[1024,256]{1,0:T(8,128)(2,1)S(1)} %add_convert_fusion.14), kind=kLoop, calls=%fused_computation.61 | loop fusion | flops 1310720 | bytes 2097153 | tf_op jit(solution)/shard_map/jit(_where)/select_n | solution.py:349
  128.8 3.1 %collective-permute-start.33 = (bf16[1024,256]{1,0:T(8,128)(2,1)}, bf16[1024,256]{1,0:T(8,128)(2,1)}, u32[]{:S(2)}, u32[]{:S(2)}) collective-permute-start(bf16[1024,256]{1,0:T(8,128)(2,1)} %broadcast_select_fusion.12), channel_id=1, source_target_pairs={{0,2},{1,3},{2,0},{3,1},{4,6},{5,7},{6,4},{7,5},{8,10},{9,11},{10,... | collective-permute-start | bytes 1572872 | tf_op jit(solution)/shard_map/ppermute | solution.py:192
  132.0 1.4 collective-permute-start.34
  133.4 1.2 add_convert_fusion.10
  135.3 1.2 broadcast_select_fusion.11
  136.6 1.0 broadcast_select_fusion.10
  137.9 7.7 %collective-permute-start.36 = (bf16[1024,256]{1,0:T(8,128)(2,1)}, bf16[1024,256]{1,0:T(8,128)(2,1)}, u32[]{:S(2)}, u32[]{:S(2)}) collective-permute-start(bf16[1024,256]{1,0:T(8,128)(2,1)} %broadcast_select_fusion.10), channel_id=1, source_target_pairs={{0,2},{1,3},{2,0},{3,1},{4,6},{5,7},{6,4},{7,5},{8,10},{9,11},{10,... | collective-permute-start | bytes 1572872 | tf_op jit(solution)/shard_map/ppermute | solution.py:192
  147.9 5.9 %partial_product.9 = (bf16[1024,256]{1,0:T(8,128)(2,1)}, bf16[1024,256]{1,0:T(8,128)(2,1)}) custom-call(s32[1]{0:T(128)} %bitcast.place, bf16[1024,256]{1,0:T(8,128)(2,1)} %get-tuple-element.143.refs_0_, bf16[1024,256]{1,0:T(8,128)(2,1)} %copy-done.1, bf16[1024,256]{1,0:T(8,128)(2,1)} %copy-done.2, bf16[1024,256]{1,0:T(8,128)(2,1)} %copy-done.4, ...), custom_call_target="tpu_custom_call" | custom-call | flops 2147483648 | bytes 7340032 | tf_op jit(solution)/shard_map/partial_product/pallas_call | solution.py:131
  153.8 1.4 add_convert_fusion.8
  155.2 1.0 collective-permute-start.39
  156.2 1.2 broadcast_select_fusion.9
  157.7 1.8 collective-permute-start.38
  159.9 1.4 broadcast_select_fusion.7
  161.3 1.5 add_convert_fusion.6
  164.2 7.7 %collective-permute-start.40 = (bf16[1024,256]{1,0:T(8,128)(2,1)S(1)}, bf16[1024,256]{1,0:T(8,128)(2,1)S(1)}, u32[]{:S(2)}, u32[]{:S(2)}) collective-permute-start(bf16[1024,256]{1,0:T(8,128)(2,1)S(1)} %broadcast_select_fusion.6), channel_id=1, source_target_pairs={{0,2},{1,3},{2,0},{3,1},{4,6},{5,7},{6,4},{7,5},{8,10},{9,11},{10,... | collective-permute-start | bytes 1572872 | tf_op jit(solution)/shard_map/ppermute | solution.py:192
  173.1 1.3 collective-permute-start.42
  174.8 16.9 %collective-permute-done.42 = bf16[1024,256]{1,0:T(8,128)(2,1)S(1)} collective-permute-done((bf16[1024,256]{1,0:T(8,128)(2,1)S(1)}, bf16[1024,256]{1,0:T(8,128)(2,1)S(1)}, u32[]{:S(2)}, u32[]{:S(2)}) %collective-permute-start.42) | collective-permute-done | bytes 524320 | tf_op jit(solution)/shard_map/ppermute | solution.py:192
  193.7 1.3 collective-permute-start.44
  195.3 1.3 collective-permute-start.46
  196.6 12.2 %collective-permute-done.44 = bf16[1024,256]{1,0:T(8,128)(2,1)S(1)} collective-permute-done((bf16[1024,256]{1,0:T(8,128)(2,1)S(1)}, bf16[1024,256]{1,0:T(8,128)(2,1)S(1)}, u32[]{:S(2)}, u32[]{:S(2)}) %collective-permute-start.44) | collective-permute-done | bytes 524320 | tf_op jit(solution)/shard_map/ppermute | solution.py:192
  209.3 6.7 %collective-permute-done.46 = bf16[1024,256]{1,0:T(8,128)(2,1)S(1)} collective-permute-done((bf16[1024,256]{1,0:T(8,128)(2,1)S(1)}, bf16[1024,256]{1,0:T(8,128)(2,1)S(1)}, u32[]{:S(2)}, u32[]{:S(2)}) %collective-permute-start.46) | collective-permute-done | bytes 524320 | tf_op jit(solution)/shard_map/ppermute | solution.py:192
  217.0 1.4 collective-permute-done.48
  218.7 2.2 %broadcast_select_fusion = bf16[1,448,4096]{2,1,0:T(8,128)(2,1)} fusion(bf16[1,448,4096]{2,1,0:T(8,128)(2,1)S(1)} %get-tuple-element.267, bf16[1,448,4096]{2,1,0:T(8,128)(2,1)S(1)} %constant_dynamic-update-slice_fusion.14, pred[]{:T(512)S(6)} %eq.30), kind=kLoop, calls=%fused_computation | loop fusion | flops 1835008 | bytes 11010049 | tf_op jit(solution)/shard_map/jit(_where)/select_n | solution.py:375
  (216 shorter events, 24.3 us)
Async XLA Ops:
  1.0 1.5 collective-permute-start
  2.5 17.4 %copy-start.17 = (bf16[512,256]{1,0:T(8,128)(2,1)}, bf16[512,256]{1,0:T(8,128)(2,1)S(1)}, u32[]{:S(2)}) copy-start(bf16[512,256]{1,0:T(8,128)(2,1)S(1)} %pad_maximum_fusion.4.refs_8_) | copy-start | bytes 786436
  2.5 17.4 %collective-permute-start.3 = (bf16[512,256]{1,0:T(8,128)(2,1)S(1)}, bf16[512,256]{1,0:T(8,128)(2,1)S(1)}, u32[]{:S(2)}, u32[]{:S(2)}) collective-permute-start(bf16[512,256]{1,0:T(8,128)(2,1)S(1)} %pad_maximum_fusion.4.refs_8_), channel_id=1, source_target_pairs={{0,24},{8,16},{16,8},{24,0},{1,25},{9,17},{17,9},{25,1},{2,26},{10... | collective-permute-start | bytes 786440 | tf_op jit(solution)/shard_map/ppermute | solution.py:182
  6.4 13.6 %collective-permute-start.2 = (bf16[512,256]{1,0:T(8,128)(2,1)S(1)}, bf16[512,256]{1,0:T(8,128)(2,1)S(1)}, u32[]{:S(2)}, u32[]{:S(2)}) collective-permute-start(bf16[512,256]{1,0:T(8,128)(2,1)S(1)} %pad_maximum_fusion.4.refs_8_), channel_id=1, source_target_pairs={{0,16},{8,24},{16,0},{24,8},{1,17},{9,25},{17,1},{25,9},{2,18},{10... | collective-permute-start | bytes 786440 | tf_op jit(solution)/shard_map/ppermute | solution.py:182
  6.9 13.1 %collective-permute-start.1 = (bf16[512,256]{1,0:T(8,128)(2,1)S(1)}, bf16[512,256]{1,0:T(8,128)(2,1)S(1)}, u32[]{:S(2)}, u32[]{:S(2)}) collective-permute-start(bf16[512,256]{1,0:T(8,128)(2,1)S(1)} %pad_maximum_fusion.4.refs_8_), channel_id=1, source_target_pairs={{0,8},{8,0},{16,24},{24,16},{1,9},{9,1},{17,25},{25,17},{2,10},{10... | collective-permute-start | bytes 786440 | tf_op jit(solution)/shard_map/ppermute | solution.py:182
  7.0 17.5 %copy-start.31 = (s32[128,2]{0,1:T(2,128)S(1)}, s32[128,2]{0,1:T(2,128)}, u32[]{:S(2)}) copy-start(s32[128,2]{0,1:T(2,128)} %param.20) | copy-start | bytes 3076
  7.0 17.5 %copy-start.32 = (f32[128,2]{0,1:T(2,128)S(1)}, f32[128,2]{0,1:T(2,128)}, u32[]{:S(2)}) copy-start(f32[128,2]{0,1:T(2,128)} %param.21) | copy-start | bytes 3076
  7.0 20.3 %copy-start.20 = (bf16[128,4096]{1,0:T(8,128)(2,1)S(1)}, bf16[128,4096]{1,0:T(8,128)(2,1)}, u32[]{:S(2)}) copy-start(bf16[128,4096]{1,0:T(8,128)(2,1)} %param.19) | copy-start | bytes 3145732
  20.0 18.1 %copy-start.26 = (bf16[512,256]{1,0:T(8,128)(2,1)}, bf16[512,256]{1,0:T(8,128)(2,1)S(1)}, u32[]{:S(2)}) copy-start(bf16[512,256]{1,0:T(8,128)(2,1)S(1)} %collective-permute-done.1.refs_9_) | copy-start | bytes 786436
  20.8 3.7 %collective-permute-start.4 = (bf16[1024,256]{1,0:T(8,128)(2,1)}, bf16[1024,256]{1,0:T(8,128)(2,1)S(1)}, u32[]{:S(2)}, u32[]{:S(2)}) collective-permute-start(bf16[1024,256]{1,0:T(8,128)(2,1)} %get-tuple-element.143.refs_0_), channel_id=1, source_target_pairs={{0,1},{1,0},{2,3},{3,2},{4,5},{5,4},{6,7},{7,6},{8,9},{9,8},{10,11... | collective-permute-start | bytes 1572872 | tf_op jit(solution)/shard_map/ppermute | solution.py:179
  21.0 26.2 %collective-permute-start.5 = (bf16[1024,256]{1,0:T(8,128)(2,1)}, bf16[1024,256]{1,0:T(8,128)(2,1)S(1)}, u32[]{:S(2)}, u32[]{:S(2)}) collective-permute-start(bf16[1024,256]{1,0:T(8,128)(2,1)} %get-tuple-element.133), channel_id=1, source_target_pairs={{0,8},{8,0},{16,24},{24,16},{1,9},{9,1},{17,25},{25,17},{2,10},{10... | collective-permute-start | bytes 1572872 | tf_op jit(solution)/shard_map/ppermute | solution.py:182
  22.9 31.1 %collective-permute-start.6 = (bf16[1024,256]{1,0:T(8,128)(2,1)}, bf16[1024,256]{1,0:T(8,128)(2,1)S(1)}, u32[]{:S(2)}, u32[]{:S(2)}) collective-permute-start(bf16[1024,256]{1,0:T(8,128)(2,1)} %get-tuple-element.134), channel_id=1, source_target_pairs={{0,16},{8,24},{16,0},{24,8},{1,17},{9,25},{17,1},{25,9},{2,18},{10... | collective-permute-start | bytes 1572872 | tf_op jit(solution)/shard_map/ppermute | solution.py:182
  24.4 29.6 %collective-permute-start.7 = (bf16[1024,256]{1,0:T(8,128)(2,1)}, bf16[1024,256]{1,0:T(8,128)(2,1)}, u32[]{:S(2)}, u32[]{:S(2)}) collective-permute-start(bf16[1024,256]{1,0:T(8,128)(2,1)} %get-tuple-element.135), channel_id=1, source_target_pairs={{0,24},{8,16},{16,8},{24,0},{1,25},{9,17},{17,9},{25,1},{2,26},{10... | collective-permute-start | bytes 1572872 | tf_op jit(solution)/shard_map/ppermute | solution.py:182
  24.5 17.5 %copy-start.1 = (bf16[1024,256]{1,0:T(8,128)(2,1)}, bf16[1024,256]{1,0:T(8,128)(2,1)S(1)}, u32[]{:S(2)}) copy-start(bf16[1024,256]{1,0:T(8,128)(2,1)S(1)} %collective-permute-done.4.refs_1_) | copy-start | bytes 1572868
  24.6 3.8 %collective-permute-start.13 = (f32[1,4,128]{2,1,0:T(4,128)S(1)}, f32[1,4,128]{2,1,0:T(4,128)S(1)}, u32[]{:S(2)}, u32[]{:S(2)}) collective-permute-start(f32[1,4,128]{2,1,0:T(4,128)S(1)} %maximum_bitcast_fusion), channel_id=1, source_target_pairs={{0,1},{1,0},{2,3},{3,2},{4,5},{5,4},{6,7},{7,6},{8,9},{9,8},{10,11... | collective-permute-start | bytes 6152 | tf_op jit(solution)/shard_map/ppermute | solution.py:233
  26.9 15.2 %collective-permute-start.8 = (bf16[256,1792]{1,0:T(8,128)(2,1)}, bf16[256,1792]{1,0:T(8,128)(2,1)}, u32[]{:S(2)}, u32[]{:S(2)}) collective-permute-start(bf16[256,1792]{1,0:T(8,128)(2,1)} %constant_dynamic-slice_fusion.5), channel_id=1, source_target_pairs={{0,1},{1,0},{2,3},{3,2},{4,5},{5,4},{6,7},{7,6},{8,9},{9,8},{10,11... | collective-permute-start | bytes 2752520 | tf_op jit(solution)/shard_map/ppermute | solution.py:179
  28.4 4.1 %collective-permute-start.14 = (f32[2,4,128]{2,1,0:T(4,128)S(1)}, f32[2,4,128]{2,1,0:T(4,128)S(1)}, u32[]{:S(2)}, u32[]{:S(2)}) collective-permute-start(f32[2,4,128]{2,1,0:T(4,128)S(1)} %pad_maximum_fusion.8), channel_id=1, source_target_pairs={{0,2},{1,3},{2,0},{3,1},{4,6},{5,7},{6,4},{7,5},{8,10},{9,11},{10,... | collective-permute-start | bytes 12296 | tf_op jit(solution)/shard_map/ppermute | solution.py:233
  32.4 4.6 %collective-permute-start.15 = (f32[4,4,128]{2,1,0:T(4,128)S(1)}, f32[4,4,128]{2,1,0:T(4,128)S(1)}, u32[]{:S(2)}, u32[]{:S(2)}) collective-permute-start(f32[4,4,128]{2,1,0:T(4,128)S(1)} %pad_maximum_fusion.7), channel_id=1, source_target_pairs={{0,4},{1,5},{2,6},{3,7},{4,0},{5,1},{6,2},{7,3},{8,12},{9,13},{10,... | collective-permute-start | bytes 24584 | tf_op jit(solution)/shard_map/ppermute | solution.py:233
  37.1 2.1 collective-permute-start.12
  38.0 10.6 %copy-start.22 = (bf16[256,512]{1,0:T(8,128)(2,1)S(1)}, bf16[256,512]{1,0:T(8,128)(2,1)}, u32[]{:S(2)}) copy-start(bf16[256,512]{1,0:T(8,128)(2,1)} %get-tuple-element.251) | copy-start | bytes 786436
  43.0 26.9 %copy-start.18 = (bf16[512,256]{1,0:T(8,128)(2,1)}, bf16[512,256]{1,0:T(8,128)(2,1)S(1)}, u32[]{:S(2)}) copy-start(bf16[512,256]{1,0:T(8,128)(2,1)S(1)} %pad_maximum_fusion.5.refs_8_) | copy-start | bytes 786436
  43.0 11.2 %collective-permute-start.11 = (bf16[512,256]{1,0:T(8,128)(2,1)S(1)}, bf16[512,256]{1,0:T(8,128)(2,1)S(1)}, u32[]{:S(2)}, u32[]{:S(2)}) collective-permute-start(bf16[512,256]{1,0:T(8,128)(2,1)S(1)} %pad_maximum_fusion.5.refs_8_), channel_id=1, source_target_pairs={{0,24},{8,16},{16,8},{24,0},{1,25},{9,17},{17,9},{25,1},{2,26},{10... | collective-permute-start | bytes 786440 | tf_op jit(solution)/shard_map/ppermute | solution.py:182
  45.5 14.1 %collective-permute-start.10 = (bf16[512,256]{1,0:T(8,128)(2,1)S(1)}, bf16[512,256]{1,0:T(8,128)(2,1)S(1)}, u32[]{:S(2)}, u32[]{:S(2)}) collective-permute-start(bf16[512,256]{1,0:T(8,128)(2,1)S(1)} %pad_maximum_fusion.5.refs_8_), channel_id=1, source_target_pairs={{0,16},{8,24},{16,0},{24,8},{1,17},{9,25},{17,1},{25,9},{2,18},{10... | collective-permute-start | bytes 786440 | tf_op jit(solution)/shard_map/ppermute | solution.py:182
  47.2 18.3 %copy-start.2 = (bf16[1024,256]{1,0:T(8,128)(2,1)}, bf16[1024,256]{1,0:T(8,128)(2,1)S(1)}, u32[]{:S(2)}) copy-start(bf16[1024,256]{1,0:T(8,128)(2,1)S(1)} %collective-permute-done.5.refs_2_) | copy-start | bytes 1572868
  47.2 12.4 %collective-permute-start.9 = (bf16[512,256]{1,0:T(8,128)(2,1)S(1)}, bf16[512,256]{1,0:T(8,128)(2,1)S(1)}, u32[]{:S(2)}, u32[]{:S(2)}) collective-permute-start(bf16[512,256]{1,0:T(8,128)(2,1)S(1)} %pad_maximum_fusion.5.refs_8_), channel_id=1, source_target_pairs={{0,8},{8,0},{16,24},{24,16},{1,9},{9,1},{17,25},{25,17},{2,10},{10... | collective-permute-start | bytes 786440 | tf_op jit(solution)/shard_map/ppermute | solution.py:182
  54.0 11.5 %copy-start.3 = (bf16[1024,256]{1,0:T(8,128)(2,1)}, bf16[1024,256]{1,0:T(8,128)(2,1)S(1)}, u32[]{:S(2)}) copy-start(bf16[1024,256]{1,0:T(8,128)(2,1)S(1)} %collective-permute-done.6.refs_4_) | copy-start | bytes 1572868
  59.7 2.0 collective-permute-start.16
  60.4 2.9 %collective-permute-start.17 = (bf16[1024,256]{1,0:T(8,128)(2,1)S(1)}, bf16[1024,256]{1,0:T(8,128)(2,1)}, u32[]{:S(2)}, u32[]{:S(2)}) collective-permute-start(bf16[1024,256]{1,0:T(8,128)(2,1)S(1)} %collective-permute-done.6.refs_4_), channel_id=1, source_target_pairs={{0,1},{1,0},{2,3},{3,2},{4,5},{5,4},{6,7},{7,6},{8,9},{9,8},{10,11... | collective-permute-start | bytes 1572872 | tf_op jit(solution)/shard_map/ppermute | solution.py:179
  60.4 3.0 %collective-permute-start.18 = (bf16[1024,256]{1,0:T(8,128)(2,1)}, bf16[1024,256]{1,0:T(8,128)(2,1)}, u32[]{:S(2)}, u32[]{:S(2)}) collective-permute-start(bf16[1024,256]{1,0:T(8,128)(2,1)} %collective-permute-done.7.refs_6_), channel_id=1, source_target_pairs={{0,1},{1,0},{2,3},{3,2},{4,5},{5,4},{6,7},{7,6},{8,9},{9,8},{10,11... | collective-permute-start | bytes 1572872 | tf_op jit(solution)/shard_map/ppermute | solution.py:179
  63.5 17.9 %collective-permute-start.20 = (bf16[512,512]{1,0:T(8,128)(2,1)}, bf16[512,512]{1,0:T(8,128)(2,1)}, u32[]{:S(2)}, u32[]{:S(2)}) collective-permute-start(bf16[512,512]{1,0:T(8,128)(2,1)} %get-tuple-element.178.refs_8_), channel_id=1, source_target_pairs={{0,16},{8,24},{16,0},{24,8},{1,17},{9,25},{17,1},{25,9},{2,18},{10... | collective-permute-start | bytes 1572872 | tf_op jit(solution)/shard_map/ppermute | solution.py:182
  65.0 16.4 %collective-permute-start.19 = (bf16[512,512]{1,0:T(8,128)(2,1)}, bf16[512,512]{1,0:T(8,128)(2,1)}, u32[]{:S(2)}, u32[]{:S(2)}) collective-permute-start(bf16[512,512]{1,0:T(8,128)(2,1)} %get-tuple-element.178.refs_8_), channel_id=1, source_target_pairs={{0,8},{8,0},{16,24},{24,16},{1,9},{9,1},{17,25},{25,17},{2,10},{10... | collective-permute-start | bytes 1572872 | tf_op jit(solution)/shard_map/ppermute | solution.py:182
  69.9 16.3 %copy-start.16 = (bf16[1024,256]{1,0:T(8,128)(2,1)S(1)}, bf16[1024,256]{1,0:T(8,128)(2,1)}, u32[]{:S(2)}) copy-start(bf16[1024,256]{1,0:T(8,128)(2,1)} %partial_product.5) | copy-start | bytes 1572868
  69.9 16.3 %collective-permute-start.22 = (bf16[1024,256]{1,0:T(8,128)(2,1)}, bf16[1024,256]{1,0:T(8,128)(2,1)}, u32[]{:S(2)}, u32[]{:S(2)}) collective-permute-start(bf16[1024,256]{1,0:T(8,128)(2,1)} %partial_product.5), channel_id=1, source_target_pairs={{0,2},{1,3},{6,4},{7,5},{8,10},{9,11},{14,12},{15,13},{16,18},{17,... | collective-permute-start | bytes 1572872 | tf_op jit(solution)/shard_map/ppermute | solution.py:192
  74.3 17.1 %collective-permute-start.21 = (bf16[512,512]{1,0:T(8,128)(2,1)}, bf16[512,512]{1,0:T(8,128)(2,1)}, u32[]{:S(2)}, u32[]{:S(2)}) collective-permute-start(bf16[512,512]{1,0:T(8,128)(2,1)} %get-tuple-element.178.refs_8_), channel_id=1, source_target_pairs={{0,24},{8,16},{16,8},{24,0},{1,25},{9,17},{17,9},{25,1},{2,26},{10... | collective-permute-start | bytes 1572872 | tf_op jit(solution)/shard_map/ppermute | solution.py:182
  80.0 24.3 %collective-permute-start.24 = (bf16[1024,256]{1,0:T(8,128)(2,1)}, bf16[1024,256]{1,0:T(8,128)(2,1)S(1)}, u32[]{:S(2)}, u32[]{:S(2)}) collective-permute-start(bf16[1024,256]{1,0:T(8,128)(2,1)} %partial_product.6), channel_id=1, source_target_pairs={{0,2},{1,3},{6,4},{7,5},{8,10},{9,11},{14,12},{15,13},{16,18},{17,... | collective-permute-start | bytes 1572872 | tf_op jit(solution)/shard_map/ppermute | solution.py:192
  81.4 21.5 %collective-permute-start.26 = (bf16[512,512]{1,0:T(8,128)(2,1)}, bf16[512,512]{1,0:T(8,128)(2,1)}, u32[]{:S(2)}, u32[]{:S(2)}) collective-permute-start(bf16[512,512]{1,0:T(8,128)(2,1)} %get-tuple-element.199.refs_8_), channel_id=1, source_target_pairs={{0,16},{8,24},{16,0},{24,8},{1,17},{9,25},{17,1},{25,9},{2,18},{10... | collective-permute-start | bytes 1572872 | tf_op jit(solution)/shard_map/ppermute | solution.py:182
  83.0 19.9 %collective-permute-start.25 = (bf16[512,512]{1,0:T(8,128)(2,1)}, bf16[512,512]{1,0:T(8,128)(2,1)}, u32[]{:S(2)}, u32[]{:S(2)}) collective-permute-start(bf16[512,512]{1,0:T(8,128)(2,1)} %get-tuple-element.199.refs_8_), channel_id=1, source_target_pairs={{0,8},{8,0},{16,24},{24,16},{1,9},{9,1},{17,25},{25,17},{2,10},{10... | collective-permute-start | bytes 1572872 | tf_op jit(solution)/shard_map/ppermute | solution.py:182
  87.3 17.8 %collective-permute-start.23 = (bf16[1024,256]{1,0:T(8,128)(2,1)S(1)}, bf16[1024,256]{1,0:T(8,128)(2,1)S(1)}, u32[]{:S(2)}, u32[]{:S(2)}) collective-permute-start(bf16[1024,256]{1,0:T(8,128)(2,1)S(1)} %add_convert_fusion.15), channel_id=1, source_target_pairs={{2,4},{3,5},{4,2},{5,3},{10,12},{11,13},{12,10},{13,11},{18,20},{1... | collective-permute-start | bytes 1572872 | tf_op jit(solution)/shard_map/ppermute | solution.py:192
  91.3 13.0 %copy-start.15 = (bf16[1024,256]{1,0:T(8,128)(2,1)S(1)}, bf16[1024,256]{1,0:T(8,128)(2,1)}, u32[]{:S(2)}) copy-start(bf16[1024,256]{1,0:T(8,128)(2,1)} %partial_product.6) | copy-start | bytes 1572868
  97.2 27.2 %collective-permute-start.32 = (bf16[1024,256]{1,0:T(8,128)(2,1)}, bf16[1024,256]{1,0:T(8,128)(2,1)}, u32[]{:S(2)}, u32[]{:S(2)}) collective-permute-start(bf16[1024,256]{1,0:T(8,128)(2,1)} %get-tuple-element.204), channel_id=1, source_target_pairs={{0,2},{1,3},{6,4},{7,5},{8,10},{9,11},{14,12},{15,13},{16,18},{17,... | collective-permute-start | bytes 1572872 | tf_op jit(solution)/shard_map/ppermute | solution.py:192
  102.9 13.6 %collective-permute-start.28 = (bf16[512,512]{1,0:T(8,128)(2,1)}, bf16[512,512]{1,0:T(8,128)(2,1)}, u32[]{:S(2)}, u32[]{:S(2)}) collective-permute-start(bf16[512,512]{1,0:T(8,128)(2,1)} %get-tuple-element.199.refs_8_), channel_id=1, source_target_pairs={{0,24},{8,16},{16,8},{24,0},{1,25},{9,17},{17,9},{25,1},{2,26},{10... | collective-permute-start | bytes 1572872 | tf_op jit(solution)/shard_map/ppermute | solution.py:182
  104.4 22.1 %collective-permute-start.31 = (bf16[1024,256]{1,0:T(8,128)(2,1)S(1)}, bf16[1024,256]{1,0:T(8,128)(2,1)S(1)}, u32[]{:S(2)}, u32[]{:S(2)}) collective-permute-start(bf16[1024,256]{1,0:T(8,128)(2,1)S(1)} %add_convert_fusion.14), channel_id=1, source_target_pairs={{2,4},{3,5},{4,2},{5,3},{10,12},{11,13},{12,10},{13,11},{18,20},{1... | collective-permute-start | bytes 1572872 | tf_op jit(solution)/shard_map/ppermute | solution.py:192
  105.2 19.2 %copy-start.9 = (bf16[1024,256]{1,0:T(8,128)(2,1)}, bf16[1024,256]{1,0:T(8,128)(2,1)S(1)}, u32[]{:S(2)}) copy-start(bf16[1024,256]{1,0:T(8,128)(2,1)S(1)} %collective-permute-done.23) | copy-start | bytes 1572868
  107.4 26.0 %collective-permute-start.27 = (bf16[1024,256]{1,0:T(8,128)(2,1)}, bf16[1024,256]{1,0:T(8,128)(2,1)}, u32[]{:S(2)}, u32[]{:S(2)}) collective-permute-start(bf16[1024,256]{1,0:T(8,128)(2,1)} %broadcast_select_fusion.13), channel_id=1, source_target_pairs={{0,2},{1,3},{2,0},{3,1},{4,6},{5,7},{6,4},{7,5},{8,10},{9,11},{10,... | collective-permute-start | bytes 1572872 | tf_op jit(solution)/shard_map/ppermute | solution.py:192
  116.5 15.5 %collective-permute-start.30 = (bf16[512,512]{1,0:T(8,128)(2,1)}, bf16[512,512]{1,0:T(8,128)(2,1)}, u32[]{:S(2)}, u32[]{:S(2)}) collective-permute-start(bf16[512,512]{1,0:T(8,128)(2,1)} %pad_maximum_fusion.2.refs_8_), channel_id=1, source_target_pairs={{0,16},{8,24},{16,0},{24,8},{1,17},{9,25},{17,1},{25,9},{2,18},{10... | collective-permute-start | bytes 1572872 | tf_op jit(solution)/shard_map/ppermute | solution.py:182
  118.0 14.0 %collective-permute-start.29 = (bf16[512,512]{1,0:T(8,128)(2,1)}, bf16[512,512]{1,0:T(8,128)(2,1)}, u32[]{:S(2)}, u32[]{:S(2)}) collective-permute-start(bf16[512,512]{1,0:T(8,128)(2,1)} %pad_maximum_fusion.2.refs_8_), channel_id=1, source_target_pairs={{0,8},{8,0},{16,24},{24,16},{1,9},{9,1},{17,25},{25,17},{2,10},{10... | collective-permute-start | bytes 1572872 | tf_op jit(solution)/shard_map/ppermute | solution.py:182
  124.4 10.9 %copy-start.10 = (bf16[1024,256]{1,0:T(8,128)(2,1)S(1)}, bf16[1024,256]{1,0:T(8,128)(2,1)}, u32[]{:S(2)}) copy-start(bf16[1024,256]{1,0:T(8,128)(2,1)} %copy-done.9) | copy-start | bytes 1572868
  124.4 12.2 %copy-start.6 = (bf16[1024,256]{1,0:T(8,128)(2,1)S(1)}, bf16[1024,256]{1,0:T(8,128)(2,1)}, u32[]{:S(2)}) copy-start(bf16[1024,256]{1,0:T(8,128)(2,1)} %get-tuple-element.232) | copy-start | bytes 1572868
  125.9 10.7 %collective-permute-start.35 = (bf16[1024,256]{1,0:T(8,128)(2,1)S(1)}, bf16[1024,256]{1,0:T(8,128)(2,1)S(1)}, u32[]{:S(2)}, u32[]{:S(2)}) collective-permute-start(bf16[1024,256]{1,0:T(8,128)(2,1)S(1)} %add_convert_fusion.12), channel_id=1, source_target_pairs={{2,4},{3,5},{4,2},{5,3},{10,12},{11,13},{12,10},{13,11},{18,20},{1... | collective-permute-start | bytes 1572872 | tf_op jit(solution)/shard_map/ppermute | solution.py:192
  128.8 25.0 %collective-permute-start.33 = (bf16[1024,256]{1,0:T(8,128)(2,1)}, bf16[1024,256]{1,0:T(8,128)(2,1)}, u32[]{:S(2)}, u32[]{:S(2)}) collective-permute-start(bf16[1024,256]{1,0:T(8,128)(2,1)} %broadcast_select_fusion.12), channel_id=1, source_target_pairs={{0,2},{1,3},{2,0},{3,1},{4,6},{5,7},{6,4},{7,5},{8,10},{9,11},{10,... | collective-permute-start | bytes 1572872 | tf_op jit(solution)/shard_map/ppermute | solution.py:192
  132.0 15.1 %collective-permute-start.34 = (bf16[512,512]{1,0:T(8,128)(2,1)}, bf16[512,512]{1,0:T(8,128)(2,1)S(1)}, u32[]{:S(2)}, u32[]{:S(2)}) collective-permute-start(bf16[512,512]{1,0:T(8,128)(2,1)} %pad_maximum_fusion.2.refs_8_), channel_id=1, source_target_pairs={{0,24},{8,16},{16,8},{24,0},{1,25},{9,17},{17,9},{25,1},{2,26},{10... | collective-permute-start | bytes 1572872 | tf_op jit(solution)/shard_map/ppermute | solution.py:182
  134.6 22.9 %collective-permute-start.37 = (bf16[1024,256]{1,0:T(8,128)(2,1)S(1)}, bf16[1024,256]{1,0:T(8,128)(2,1)S(1)}, u32[]{:S(2)}, u32[]{:S(2)}) collective-permute-start(bf16[1024,256]{1,0:T(8,128)(2,1)S(1)} %add_convert_fusion.10), channel_id=1, source_target_pairs={{2,4},{3,5},{4,2},{5,3},{10,12},{11,13},{12,10},{13,11},{18,20},{1... | collective-permute-start | bytes 1572872 | tf_op jit(solution)/shard_map/ppermute | solution.py:192
  137.9 22.0 %collective-permute-start.36 = (bf16[1024,256]{1,0:T(8,128)(2,1)}, bf16[1024,256]{1,0:T(8,128)(2,1)}, u32[]{:S(2)}, u32[]{:S(2)}) collective-permute-start(bf16[1024,256]{1,0:T(8,128)(2,1)} %broadcast_select_fusion.10), channel_id=1, source_target_pairs={{0,2},{1,3},{2,0},{3,1},{4,6},{5,7},{6,4},{7,5},{8,10},{9,11},{10,... | collective-permute-start | bytes 1572872 | tf_op jit(solution)/shard_map/ppermute | solution.py:192
  155.2 8.8 %collective-permute-start.39 = (bf16[1024,256]{1,0:T(8,128)(2,1)S(1)}, bf16[1024,256]{1,0:T(8,128)(2,1)S(1)}, u32[]{:S(2)}, u32[]{:S(2)}) collective-permute-start(bf16[1024,256]{1,0:T(8,128)(2,1)S(1)} %add_convert_fusion.8), channel_id=1, source_target_pairs={{2,4},{3,5},{4,2},{5,3},{10,12},{11,13},{12,10},{13,11},{18,20},{1... | collective-permute-start | bytes 1572872 | tf_op jit(solution)/shard_map/ppermute | solution.py:192
  157.7 14.2 %collective-permute-start.38 = (bf16[1024,256]{1,0:T(8,128)(2,1)S(1)}, bf16[1024,256]{1,0:T(8,128)(2,1)S(1)}, u32[]{:S(2)}, u32[]{:S(2)}) collective-permute-start(bf16[1024,256]{1,0:T(8,128)(2,1)S(1)} %broadcast_select_fusion.8), channel_id=1, source_target_pairs={{0,2},{1,3},{2,0},{3,1},{4,6},{5,7},{6,4},{7,5},{8,10},{9,11},{10,... | collective-permute-start | bytes 1572872 | tf_op jit(solution)/shard_map/ppermute | solution.py:192
  163.2 9.8 %collective-permute-start.41 = (bf16[1024,256]{1,0:T(8,128)(2,1)S(1)}, bf16[1024,256]{1,0:T(8,128)(2,1)S(1)}, u32[]{:S(2)}, u32[]{:S(2)}) collective-permute-start(bf16[1024,256]{1,0:T(8,128)(2,1)S(1)} %add_convert_fusion.6), channel_id=1, source_target_pairs={{2,4},{3,5},{4,2},{5,3},{10,12},{11,13},{12,10},{13,11},{18,20},{1... | collective-permute-start | bytes 1572872 | tf_op jit(solution)/shard_map/ppermute | solution.py:192
  164.2 27.9 %collective-permute-start.40 = (bf16[1024,256]{1,0:T(8,128)(2,1)S(1)}, bf16[1024,256]{1,0:T(8,128)(2,1)S(1)}, u32[]{:S(2)}, u32[]{:S(2)}) collective-permute-start(bf16[1024,256]{1,0:T(8,128)(2,1)S(1)} %broadcast_select_fusion.6), channel_id=1, source_target_pairs={{0,2},{1,3},{2,0},{3,1},{4,6},{5,7},{6,4},{7,5},{8,10},{9,11},{10,... | collective-permute-start | bytes 1572872 | tf_op jit(solution)/shard_map/ppermute | solution.py:192
  172.1 21.5 %collective-permute-start.43 = (bf16[1024,256]{1,0:T(8,128)(2,1)S(1)}, bf16[1024,256]{1,0:T(8,128)(2,1)S(1)}, u32[]{:S(2)}, u32[]{:S(2)}) collective-permute-start(bf16[1024,256]{1,0:T(8,128)(2,1)S(1)} %add_convert_fusion.4), channel_id=1, source_target_pairs={{2,4},{3,5},{4,2},{5,3},{10,12},{11,13},{12,10},{13,11},{18,20},{1... | collective-permute-start | bytes 1572872 | tf_op jit(solution)/shard_map/ppermute | solution.py:192
  173.1 18.6 %collective-permute-start.42 = (bf16[1024,256]{1,0:T(8,128)(2,1)S(1)}, bf16[1024,256]{1,0:T(8,128)(2,1)S(1)}, u32[]{:S(2)}, u32[]{:S(2)}) collective-permute-start(bf16[1024,256]{1,0:T(8,128)(2,1)S(1)} %add_convert_fusion.3), channel_id=1, source_target_pairs={{2,0},{3,1},{4,6},{5,7},{10,8},{11,9},{12,14},{13,15},{18,16},{19,... | collective-permute-start | bytes 1572872 | tf_op jit(solution)/shard_map/ppermute | solution.py:192
  192.3 2.9 %collective-permute-start.45 = (bf16[1024,256]{1,0:T(8,128)(2,1)S(1)}, bf16[1024,256]{1,0:T(8,128)(2,1)S(1)}, u32[]{:S(2)}, u32[]{:S(2)}) collective-permute-start(bf16[1024,256]{1,0:T(8,128)(2,1)S(1)} %add_convert_fusion.2), channel_id=1, source_target_pairs={{2,4},{3,5},{4,2},{5,3},{10,12},{11,13},{12,10},{13,11},{18,20},{1... | collective-permute-start | bytes 1572872 | tf_op jit(solution)/shard_map/ppermute | solution.py:192
  193.7 15.2 %collective-permute-start.44 = (bf16[1024,256]{1,0:T(8,128)(2,1)S(1)}, bf16[1024,256]{1,0:T(8,128)(2,1)S(1)}, u32[]{:S(2)}, u32[]{:S(2)}) collective-permute-start(bf16[1024,256]{1,0:T(8,128)(2,1)S(1)} %add_convert_fusion.1), channel_id=1, source_target_pairs={{2,0},{3,1},{4,6},{5,7},{10,8},{11,9},{12,14},{13,15},{18,16},{19,... | collective-permute-start | bytes 1572872 | tf_op jit(solution)/shard_map/ppermute | solution.py:192
  195.1 21.5 %collective-permute-start.47 = (bf16[448,1536]{1,0:T(8,128)(2,1)S(1)}, bf16[448,1536]{1,0:T(8,128)(2,1)S(1)}, u32[]{:S(2)}, u32[]{:S(2)}) collective-permute-start(bf16[448,1536]{1,0:T(8,128)(2,1)S(1)} %constant_dynamic-update-slice_fusion), channel_id=1, source_target_pairs={{0,1},{1,0},{2,3},{3,2},{4,5},{5,4},{6,7},{7,6},{8,9},{9,8},{10,11... | collective-permute-start | bytes 4128776 | tf_op jit(solution)/shard_map/ppermute | solution.py:179
  195.3 20.7 %collective-permute-start.46 = (bf16[1024,256]{1,0:T(8,128)(2,1)S(1)}, bf16[1024,256]{1,0:T(8,128)(2,1)S(1)}, u32[]{:S(2)}, u32[]{:S(2)}) collective-permute-start(bf16[1024,256]{1,0:T(8,128)(2,1)S(1)} %add_convert_fusion), channel_id=1, source_target_pairs={{2,0},{3,1},{4,6},{5,7},{10,8},{11,9},{12,14},{13,15},{18,16},{19,... | collective-permute-start | bytes 1572872 | tf_op jit(solution)/shard_map/ppermute | solution.py:192
  216.5 1.9 collective-permute-start.48
  (19 other events, 89.8 us)

commit v15 on v13

--- a/solution.py
+++ b/solution.py
@@ -121,9 +121,13 @@
         at += out.shape[1]
 
 
-def matmul(lefts, rights, resid, place, widths):
+def matmul(lefts, rights, resid, place, widths, only=None):
     tokens, depth = lefts[0].shape
+    block = 0
     width = rights[0].shape[1]
+    if only is not None:
+        block, width = only, widths[only]
+        widths = (width,)
     tile = 2 * resid.shape[0]
     flops = 2 * tokens * depth * len(lefts) * width
     moved = 2 * (tokens * depth * len(lefts) + depth * len(lefts) * width + tokens * width)
@@ -133,8 +137,8 @@
             num_scalar_prefetch=1,
             grid=(tokens // tile,),
             in_specs=[pl.BlockSpec((tile, depth), lambda step, place: (step, 0))] * len(lefts)
-            + [pl.BlockSpec(right.shape, lambda step, place: (0, 0)) for right in rights]
-            + [pl.BlockSpec(resid.shape, lambda step, place: (0, 0))],
+            + [pl.BlockSpec((right.shape[0], width), lambda step, place: (0, block)) for right in rights]
+            + [pl.BlockSpec((resid.shape[0], width), lambda step, place: (0, block))],
             out_specs=[pl.BlockSpec((tile, part), lambda step, place: (step, 0)) for part in widths],
         ),
         out_shape=[jax.ShapeDtypeStruct((tokens, part), jnp.bfloat16) for part in widths],
@@ -281,14 +285,14 @@
         token[0] = arrays[0]
         return arrays
 
-    def products(group_at, right):
+    def products(group_at, right, only=None):
         group, at = widths[group_at], starts[group_at]
         if channels < 128:
             right = [jnp.concatenate(right, axis=0)]
         right = chain(*right)
-        found = matmul(lefts, right, resid[:, at : at + sum(group)], place, group)
+        found = matmul(lefts, right, resid[:, at : at + sum(group)], place, group, only)
         token[0] = found[0]
-        return found
+        return found if only is None else found[0]
 
     middle = chips // 2
     distance = jnp.minimum(chip_at, chips - 1 - chip_at)
@@ -316,7 +320,7 @@
     first_of = [sum(map(len, GROUPS[:at])) for at in range(len(GROUPS))]
     lefts, rest[1] = lax.optimization_barrier((lefts, rest[1]))
     rights.append(spread_near(rest[1]) if square else spread(rest[1]))
-    sums[0][: len(GROUPS[0])] = products(0, rights[0])
+    sums[0][0] = products(0, rights[0], 0)
     rights += [None] * (len(GROUPS) - len(rights))
     for step in range(pieces + 2 * lag * hops + DELAY + 1):
         for hop in range(hops):
@@ -343,8 +347,9 @@
             coming = FIRST_PHASE[step]
             piece, *rights[group_at] = chain(rest[coming - 1], *rights[group_at])
             rights[coming] = spread_near(piece) if square else spread(piece)
-        if group_at:
-            sums[0][step : step + len(GROUPS[group_at])] = products(group_at, rights[group_at])
+        if 0 < step < pieces:
+            group_at = max(at for at, begin in enumerate(first_of) if begin <= step)
+            sums[0][step] = products(group_at, rights[group_at], step - first_of[group_at])
         for hop in range(hops):
             inward = step - lag * hop
             outward = inward - DELAY - 2 * lag * (hops - 1 - hop)

time: 212 us -> 220 us (1.038)
  waiting for transfers between devices: 68.9 us -> 53.7 us
  other arithmetic: 22.4 us -> 33.8 us
  Pallas kernels: 39.1 us -> 47.5 us
  local copies, waits for them, and re-layouts: 16.8 us -> 20.1 us
    ppermute x19, waiting for transfers between devices: 49.9 us -> 36 us  [swap_chips(): return lax.ppermute(array, 'exp', sorted(pairs))]
    pallas_call x5 -> x8, Pallas kernels: 26.2 us -> 34.7 us  [matmul(): pl.pallas_call(functools.partial(matmul_kernel, len(lefts), len(rights)),...]
    convert_element_type x11, other arithmetic: 3.59 us -> 8.9 us  [add(): (one.astype(jnp.float32) + other.astype(jnp.float32)).astype(jnp.bfloat16)]
    select_n x5, other arithmetic: 7.4 us -> 10.3 us  [on_device(): jnp.where(distance == hop, sums[hop][inward], ready[hop + 1][outward])]
    select_n x8, other arithmetic: 3.2 us -> 5.76 us  [on_device(): jnp.where(distance == hop, got, ready[hop + 1][outward])]
    unnamed x110 -> x112, local copies, waits for them, and re-layouts: 5.43 us -> 6.79 us
  transfers between devices with their start and end apart: 49 -> 49, of which waited for: 20 -> 15; matrix products, arithmetic and copies ran while one was open for 17% -> 23% of each run, Pallas kernels for 18% -> 22%
where the time goes in v15:
time: 220 us; the launch traced here: 219 us
  starting transfers between devices  60.8 us (28%)
  waiting for transfers between devices  53.7 us (24%)
  Pallas kernels  47.5 us (22%)
  other arithmetic  33.8 us (15%)
  local copies, waits for them, and re-layouts  20.1 us (9%)
  matrix products  2.33 us (1%)
    ppermute x19, waiting for transfers between devices, swap_chips(): return lax.ppermute(array, 'exp', sorted(pairs))  36 us
    pallas_call x8, Pallas kernels, matmul(): pl.pallas_call(functools.partial(matmul_kernel, len(lefts), len(rights)),...  34.7 us
    ppermute x19, starting transfers between devices, swap_chips(): return lax.ppermute(array, 'exp', sorted(pairs))  32.3 us
    ppermute x18, starting transfers between devices, to_ctx(): lax.ppermute(array, 'ctx', [(place, place ^ offset) for place in range(ct...  22.1 us
    ppermute x18, waiting for transfers between devices, to_ctx(): lax.ppermute(array, 'ctx', [(place, place ^ offset) for place in range(ct...  13.3 us
    pallas_call x1, Pallas kernels, conv_grad(): pl.pallas_call(functools.partial(conv_kernel, tile), grid_spec=pltpu.Pref...  12.8 us
    select_n x5, other arithmetic, on_device(): jnp.where(distance == hop, sums[hop][inward], ready[hop + 1][outward])  10.3 us
    convert_element_type x11, other arithmetic, add(): (one.astype(jnp.float32) + other.astype(jnp.float32)).astype(jnp.bfloat16)  8.9 us
  transfers between devices with their start and end apart: 49, of which 15 were waited for; matrix products, arithmetic and copies ran while one was open for 23% of the time, Pallas kernels for 22%

profile of v15, /device:TPU:0, one launch (start us, length us, event | category | flops | bytes accessed | tf_op | source)
XLA Modules:
  0.0 219.2 jit_solution(3043611872415773944)
XLA Ops:
  2.5 3.9 %collective-permute-start.3 = (bf16[512,256]{1,0:T(8,128)(2,1)S(1)}, bf16[512,256]{1,0:T(8,128)(2,1)S(1)}, u32[]{:S(2)}, u32[]{:S(2)}) collective-permute-start(bf16[512,256]{1,0:T(8,128)(2,1)S(1)} %pad_maximum_fusion.4.refs_8_), channel_id=1, source_target_pairs={{0,24},{8,16},{16,8},{24,0},{1,25},{9,17},{17,9},{25,1},{2,26},{10... | collective-permute-start | bytes 786440 | tf_op jit(solution)/shard_map/ppermute | solution.py:185
  7.0 12.8 %conv_grad.1 = (bf16[1024,256]{1,0:T(8,128)(2,1)}, bf16[1024,256]{1,0:T(8,128)(2,1)}, bf16[1024,256]{1,0:T(8,128)(2,1)}, bf16[1024,256]{1,0:T(8,128)(2,1)}) custom-call(s32[1]{0:T(128)} %bitcast.1.at_ctx, bf16[256,4096]{1,0:T(8,128)(2,1)} %out_grad.1, bf16[256,4096]{1,0:T(8,128)(2,1)} %gate_in.1, bf16[256,4096]{1,0:T(8,128)(2,1)} %conv_in.1, ...), custom_call_target="tpu_custom_call" | custom-call | flops 41943040 | bytes 10485760 | tf_op jit(solution)/shard_map/conv_grad/pallas_call | solution.py:84
  20.8 1.9 collective-permute-start.5
  22.7 1.5 collective-permute-start.6
  24.4 2.2 %constant_dynamic-slice_fusion.5 = bf16[256,1792]{1,0:T(8,128)(2,1)} fusion(bf16[256,4096]{1,0:T(8,128)(2,1)} %param.18, s32[]{:T(128)S(6)} %select_n.141), kind=kLoop, calls=%fused_computation.106 | loop fusion | bytes 1835012 | tf_op jit(solution)/shard_map/dynamic_slice | solution.py:198
  27.0 2.1 constant_dynamic-slice_fusion.4
  29.1 2.0 collective-permute-start.14
  31.2 2.0 constant_dynamic-slice_fusion.6
  33.2 2.7 %collective-permute-start.15 = (f32[4,4,128]{2,1,0:T(4,128)S(1)}, f32[4,4,128]{2,1,0:T(4,128)S(1)}, u32[]{:S(2)}, u32[]{:S(2)}) collective-permute-start(f32[4,4,128]{2,1,0:T(4,128)S(1)} %pad_maximum_fusion.7), channel_id=1, source_target_pairs={{0,4},{1,5},{2,6},{3,7},{4,0},{5,1},{6,2},{7,3},{8,12},{9,13},{10,... | collective-permute-start | bytes 24584 | tf_op jit(solution)/shard_map/ppermute | solution.py:236
  40.1 2.5 %maximum_select_fusion = bf16[256,2048]{1,0:T(8,128)(2,1)} fusion(bf16[128,2048]{1,0:T(8,128)(2,1)} %collective-permute-done.12, bf16[128,2048]{1,0:T(8,128)(2,1)S(1)} %get-tuple-element.281, pred[]{:T(512)S(6)} %eq.30), kind=kLoop, calls=%fused_computation.27 | loop fusion | flops 4718592 | bytes 2097153 | tf_op jit(solution)/shard_map/jit(_where)/select_n | solution.py:248
  43.6 2.5 %collective-permute-start.11 = (bf16[512,256]{1,0:T(8,128)(2,1)S(1)}, bf16[512,256]{1,0:T(8,128)(2,1)S(1)}, u32[]{:S(2)}, u32[]{:S(2)}) collective-permute-start(bf16[512,256]{1,0:T(8,128)(2,1)S(1)} %pad_maximum_fusion.5.refs_8_), channel_id=1, source_target_pairs={{0,24},{8,16},{16,8},{24,0},{1,25},{9,17},{17,9},{25,1},{2,26},{10... | collective-permute-start | bytes 786440 | tf_op jit(solution)/shard_map/ppermute | solution.py:185
  50.4 2.5 %collective-permute-done.6.refs_4_ = bf16[1024,256]{1,0:T(8,128)(2,1)S(1)} collective-permute-done((bf16[1024,256]{1,0:T(8,128)(2,1)}, bf16[1024,256]{1,0:T(8,128)(2,1)S(1)}, u32[]{:S(2)}, u32[]{:S(2)}) %collective-permute-start.6) | collective-permute-done | bytes 524320 | tf_op jit(solution)/shard_map/ppermute | solution.py:185
  53.7 5.1 %collective-permute-done.10.refs_10_ = bf16[512,256]{1,0:T(8,128)(2,1)S(1)} collective-permute-done((bf16[512,256]{1,0:T(8,128)(2,1)S(1)}, bf16[512,256]{1,0:T(8,128)(2,1)S(1)}, u32[]{:S(2)}, u32[]{:S(2)}) %collective-permute-start.10) | collective-permute-done | bytes 262176 | tf_op jit(solution)/shard_map/ppermute | solution.py:185
  60.1 1.7 fusion.23
  62.4 1.5 collective-permute-start.20
  64.6 4.3 %partial_product.8 = bf16[1024,256]{1,0:T(8,128)(2,1)} custom-call(s32[1]{0:T(128)} %bitcast.place, bf16[1024,256]{1,0:T(8,128)(2,1)} %get-tuple-element.153.refs_0_, bf16[1024,256]{1,0:T(8,128)(2,1)} %copy-done, bf16[1024,256]{1,0:T(8,128)(2,1)} %copy-done.1, bf16[1024,256]{1,0:T(8,128)(2,1)} %copy-done.4, bf16[1024,256]{1,0:T(8,128)(2,1)} %copy-done.2, ...), custom_call_target="tpu_custom_call" | custom-call | flops 1073741824 | bytes 5767168 | tf_op jit(solution)/shard_map/partial_product/pallas_call | solution.py:134
  68.9 4.4 %collective-permute-start.22 = (bf16[1024,256]{1,0:T(8,128)(2,1)}, bf16[1024,256]{1,0:T(8,128)(2,1)}, u32[]{:S(2)}, u32[]{:S(2)}) collective-permute-start(bf16[1024,256]{1,0:T(8,128)(2,1)} %partial_product.8), channel_id=1, source_target_pairs={{0,2},{1,3},{6,4},{7,5},{8,10},{9,11},{14,12},{15,13},{16,18},{17,... | collective-permute-start | bytes 1572872 | tf_op jit(solution)/shard_map/ppermute | solution.py:195
  73.3 1.4 collective-permute-start.21
  74.7 4.4 %partial_product.9 = bf16[1024,256]{1,0:T(8,128)(2,1)} custom-call(s32[1]{0:T(128)} %bitcast.place, bf16[1024,256]{1,0:T(8,128)(2,1)} %get-tuple-element.153.refs_0_, bf16[1024,256]{1,0:T(8,128)(2,1)} %copy-done, bf16[1024,256]{1,0:T(8,128)(2,1)} %copy-done.1, bf16[1024,256]{1,0:T(8,128)(2,1)} %copy-done.4, bf16[1024,256]{1,0:T(8,128)(2,1)} %copy-done.2, ...), custom_call_target="tpu_custom_call" | custom-call | flops 1073741824 | bytes 5767168 | tf_op jit(solution)/shard_map/partial_product/pallas_call | solution.py:134
  79.1 2.1 collective-permute-start.26
  81.2 3.9 %collective-permute-done.22 = bf16[1024,256]{1,0:T(8,128)(2,1)} collective-permute-done((bf16[1024,256]{1,0:T(8,128)(2,1)}, bf16[1024,256]{1,0:T(8,128)(2,1)}, u32[]{:S(2)}, u32[]{:S(2)}) %collective-permute-start.22) | collective-permute-done | bytes 524320 | tf_op jit(solution)/shard_map/ppermute | solution.py:195
  86.3 2.8 %collective-permute-done.21.refs_11_ = bf16[512,512]{1,0:T(8,128)(2,1)} collective-permute-done((bf16[512,512]{1,0:T(8,128)(2,1)}, bf16[512,512]{1,0:T(8,128)(2,1)}, u32[]{:S(2)}, u32[]{:S(2)}) %collective-permute-start.21) | collective-permute-done | bytes 524320 | tf_op jit(solution)/shard_map/ppermute | solution.py:185
  89.1 1.5 collective-permute-start.24
  91.3 1.5 collective-permute-start.25
  93.7 4.4 %partial_product.10 = bf16[1024,256]{1,0:T(8,128)(2,1)} custom-call(s32[1]{0:T(128)} %bitcast.place, bf16[1024,256]{1,0:T(8,128)(2,1)} %get-tuple-element.153.refs_0_, bf16[1024,256]{1,0:T(8,128)(2,1)} %copy-done, bf16[1024,256]{1,0:T(8,128)(2,1)} %copy-done.1, bf16[1024,256]{1,0:T(8,128)(2,1)} %copy-done.4, bf16[1024,256]{1,0:T(8,128)(2,1)} %copy-done.2, ...), custom_call_target="tpu_custom_call" | custom-call | flops 1073741824 | bytes 5767168 | tf_op jit(solution)/shard_map/partial_product/pallas_call | solution.py:134
  98.0 6.3 %collective-permute-start.30 = (bf16[1024,256]{1,0:T(8,128)(2,1)}, bf16[1024,256]{1,0:T(8,128)(2,1)}, u32[]{:S(2)}, u32[]{:S(2)}) collective-permute-start(bf16[1024,256]{1,0:T(8,128)(2,1)} %partial_product.10), channel_id=1, source_target_pairs={{0,2},{1,3},{6,4},{7,5},{8,10},{9,11},{14,12},{15,13},{16,18},{17,... | collective-permute-start | bytes 1572872 | tf_op jit(solution)/shard_map/ppermute | solution.py:195
  104.3 1.2 add_convert_fusion.14
  105.5 1.6 collective-permute-start.29
  107.2 1.4 collective-permute-start.28
  108.6 4.3 %partial_product.11 = bf16[1024,256]{1,0:T(8,128)(2,1)} custom-call(s32[1]{0:T(128)} %bitcast.place, bf16[1024,256]{1,0:T(8,128)(2,1)} %get-tuple-element.153.refs_0_, bf16[1024,256]{1,0:T(8,128)(2,1)} %copy-done, bf16[1024,256]{1,0:T(8,128)(2,1)} %copy-done.1, bf16[1024,256]{1,0:T(8,128)(2,1)} %copy-done.4, bf16[1024,256]{1,0:T(8,128)(2,1)} %copy-done.2, ...), custom_call_target="tpu_custom_call" | custom-call | flops 1073741824 | bytes 5767168 | tf_op jit(solution)/shard_map/partial_product/pallas_call | solution.py:134
  112.9 2.2 %broadcast_select_fusion.13 = bf16[1024,256]{1,0:T(8,128)(2,1)} fusion(bf16[1024,256]{1,0:T(8,128)(2,1)} %partial_product.11, pred[]{:T(512)S(6)} %eq.31, bf16[1024,256]{1,0:T(8,128)(2,1)} %collective-permute-done.25, bf16[1024,256]{1,0:T(8,128)(2,1)S(1)} %add_convert_fusion.15), kind=kLoop, calls=%fused_computation.62 | loop fusion | flops 1310720 | bytes 2097153 | tf_op jit(solution)/shard_map/jit(_where)/select_n | solution.py:359
  115.1 1.3 add_convert_fusion.12
  116.5 1.5 collective-permute-start.34
  117.9 2.0 collective-permute-done.28.refs_11_
  120.0 1.2 collective-permute-start.33
  121.9 4.3 %partial_product.12 = bf16[1024,256]{1,0:T(8,128)(2,1)} custom-call(s32[1]{0:T(128)} %bitcast.place, bf16[1024,256]{1,0:T(8,128)(2,1)} %get-tuple-element.153.refs_0_, bf16[1024,256]{1,0:T(8,128)(2,1)} %copy-done, bf16[1024,256]{1,0:T(8,128)(2,1)} %copy-done.1, bf16[1024,256]{1,0:T(8,128)(2,1)} %copy-done.4, bf16[1024,256]{1,0:T(8,128)(2,1)} %copy-done.2, ...), custom_call_target="tpu_custom_call" | custom-call | flops 1073741824 | bytes 5767168 | tf_op jit(solution)/shard_map/partial_product/pallas_call | solution.py:134
  126.2 2.2 %broadcast_select_fusion.12 = bf16[1024,256]{1,0:T(8,128)(2,1)} fusion(bf16[1024,256]{1,0:T(8,128)(2,1)} %partial_product.12, pred[]{:T(512)S(6)} %eq.31, bf16[1024,256]{1,0:T(8,128)(2,1)} %collective-permute-done.29, bf16[1024,256]{1,0:T(8,128)(2,1)S(1)} %add_convert_fusion.14), kind=kLoop, calls=%fused_computation.61 | loop fusion | flops 1310720 | bytes 2097153 | tf_op jit(solution)/shard_map/jit(_where)/select_n | solution.py:359
  129.6 1.4 broadcast_select_fusion.11
  131.0 1.2 add_convert_fusion.10
  132.2 1.5 collective-permute-start.37
  135.6 1.4 collective-permute-start.36
  137.0 4.3 %partial_product.13 = bf16[1024,256]{1,0:T(8,128)(2,1)} custom-call(s32[1]{0:T(128)} %bitcast.place, bf16[1024,256]{1,0:T(8,128)(2,1)} %get-tuple-element.153.refs_0_, bf16[1024,256]{1,0:T(8,128)(2,1)} %copy-done, bf16[1024,256]{1,0:T(8,128)(2,1)} %copy-done.1, bf16[1024,256]{1,0:T(8,128)(2,1)} %copy-done.4, bf16[1024,256]{1,0:T(8,128)(2,1)} %copy-done.2, ...), custom_call_target="tpu_custom_call" | custom-call | flops 1073741824 | bytes 5767168 | tf_op jit(solution)/shard_map/partial_product/pallas_call | solution.py:134
  141.3 2.2 %broadcast_select_fusion.10 = bf16[1024,256]{1,0:T(8,128)(2,1)} fusion(bf16[1024,256]{1,0:T(8,128)(2,1)} %partial_product.13, pred[]{:T(512)S(6)} %eq.31, bf16[1024,256]{1,0:T(8,128)(2,1)} %collective-permute-done.34, bf16[1024,256]{1,0:T(8,128)(2,1)S(1)} %add_convert_fusion.12), kind=kLoop, calls=%fused_computation.59 | loop fusion | flops 1310720 | bytes 2097153 | tf_op jit(solution)/shard_map/jit(_where)/select_n | solution.py:359
  143.6 1.8 collective-permute-start.35
  145.4 1.4 broadcast_select_fusion.9
  146.8 1.2 add_convert_fusion.8
  151.5 4.4 %partial_product.14 = bf16[1024,256]{1,0:T(8,128)(2,1)} custom-call(s32[1]{0:T(128)} %bitcast.place, bf16[1024,256]{1,0:T(8,128)(2,1)} %get-tuple-element.153.refs_0_, bf16[1024,256]{1,0:T(8,128)(2,1)} %copy-done, bf16[1024,256]{1,0:T(8,128)(2,1)} %copy-done.1, bf16[1024,256]{1,0:T(8,128)(2,1)} %copy-done.4, bf16[1024,256]{1,0:T(8,128)(2,1)} %copy-done.2, ...), custom_call_target="tpu_custom_call" | custom-call | flops 1073741824 | bytes 5767168 | tf_op jit(solution)/shard_map/partial_product/pallas_call | solution.py:134
  155.9 2.2 %broadcast_select_fusion.8 = bf16[1024,256]{1,0:T(8,128)(2,1)} fusion(bf16[1024,256]{1,0:T(8,128)(2,1)} %partial_product.14, pred[]{:T(512)S(6)} %eq.31, bf16[1024,256]{1,0:T(8,128)(2,1)} %collective-permute-done.37, bf16[1024,256]{1,0:T(8,128)(2,1)S(1)} %add_convert_fusion.10), kind=kLoop, calls=%fused_computation.57 | loop fusion | flops 1310720 | bytes 2097153 | tf_op jit(solution)/shard_map/jit(_where)/select_n | solution.py:359
  158.1 2.6 %collective-permute-start.38 = (bf16[1024,256]{1,0:T(8,128)(2,1)}, bf16[1024,256]{1,0:T(8,128)(2,1)S(1)}, u32[]{:S(2)}, u32[]{:S(2)}) collective-permute-start(bf16[1024,256]{1,0:T(8,128)(2,1)} %broadcast_select_fusion.8), channel_id=1, source_target_pairs={{0,2},{1,3},{2,0},{3,1},{4,6},{5,7},{6,4},{7,5},{8,10},{9,11},{10,... | collective-permute-start | bytes 1572872 | tf_op jit(solution)/shard_map/ppermute | solution.py:195
  160.7 1.2 add_convert_fusion.6
  161.9 1.5 collective-permute-start.41
  163.4 1.4 broadcast_select_fusion.7
  164.8 4.3 %partial_product.15 = bf16[1024,256]{1,0:T(8,128)(2,1)} custom-call(s32[1]{0:T(128)} %bitcast.place, bf16[1024,256]{1,0:T(8,128)(2,1)} %get-tuple-element.153.refs_0_, bf16[1024,256]{1,0:T(8,128)(2,1)} %copy-done, bf16[1024,256]{1,0:T(8,128)(2,1)} %copy-done.1, bf16[1024,256]{1,0:T(8,128)(2,1)} %copy-done.4, bf16[1024,256]{1,0:T(8,128)(2,1)} %copy-done.2, ...), custom_call_target="tpu_custom_call" | custom-call | flops 1073741824 | bytes 5767168 | tf_op jit(solution)/shard_map/partial_product/pallas_call | solution.py:134
  169.1 1.4 broadcast_select_fusion.6
  172.7 1.2 broadcast_select_fusion.5
  174.0 1.2 add_convert_fusion.3
  175.2 1.3 collective-permute-start.42
  176.8 7.9 %collective-permute-done.40 = bf16[1024,256]{1,0:T(8,128)(2,1)S(1)} collective-permute-done((bf16[1024,256]{1,0:T(8,128)(2,1)S(1)}, bf16[1024,256]{1,0:T(8,128)(2,1)S(1)}, u32[]{:S(2)}, u32[]{:S(2)}) %collective-permute-start.40) | collective-permute-done | bytes 524320 | tf_op jit(solution)/shard_map/ppermute | solution.py:195
  186.4 1.3 collective-permute-start.44
  187.8 1.3 collective-permute-start.46
  189.1 6.8 %collective-permute-done.42 = bf16[1024,256]{1,0:T(8,128)(2,1)S(1)} collective-permute-done((bf16[1024,256]{1,0:T(8,128)(2,1)S(1)}, bf16[1024,256]{1,0:T(8,128)(2,1)S(1)}, u32[]{:S(2)}, u32[]{:S(2)}) %collective-permute-start.42) | collective-permute-done | bytes 524320 | tf_op jit(solution)/shard_map/ppermute | solution.py:195
  196.5 17.3 %collective-permute-done.46 = bf16[1024,256]{1,0:T(8,128)(2,1)S(1)} collective-permute-done((bf16[1024,256]{1,0:T(8,128)(2,1)S(1)}, bf16[1024,256]{1,0:T(8,128)(2,1)S(1)}, u32[]{:S(2)}, u32[]{:S(2)}) %collective-permute-start.46) | collective-permute-done | bytes 524320 | tf_op jit(solution)/shard_map/ppermute | solution.py:195
  215.2 1.4 collective-permute-done.48
  216.9 2.2 %broadcast_select_fusion = bf16[1,448,4096]{2,1,0:T(8,128)(2,1)} fusion(bf16[1,448,4096]{2,1,0:T(8,128)(2,1)S(1)} %get-tuple-element.287, bf16[1,448,4096]{2,1,0:T(8,128)(2,1)S(1)} %constant_dynamic-update-slice_fusion.14, pred[]{:T(512)S(6)} %eq.30), kind=kLoop, calls=%fused_computation | loop fusion | flops 1835008 | bytes 11010049 | tf_op jit(solution)/shard_map/jit(_where)/select_n | solution.py:373
  (239 shorter events, 33.4 us)
Async XLA Ops:
  1.0 1.5 collective-permute-start
  2.5 17.3 %copy-start.26 = (bf16[512,256]{1,0:T(8,128)(2,1)}, bf16[512,256]{1,0:T(8,128)(2,1)S(1)}, u32[]{:S(2)}) copy-start(bf16[512,256]{1,0:T(8,128)(2,1)S(1)} %pad_maximum_fusion.4.refs_8_) | copy-start | bytes 786436
  2.5 17.3 %collective-permute-start.3 = (bf16[512,256]{1,0:T(8,128)(2,1)S(1)}, bf16[512,256]{1,0:T(8,128)(2,1)S(1)}, u32[]{:S(2)}, u32[]{:S(2)}) collective-permute-start(bf16[512,256]{1,0:T(8,128)(2,1)S(1)} %pad_maximum_fusion.4.refs_8_), channel_id=1, source_target_pairs={{0,24},{8,16},{16,8},{24,0},{1,25},{9,17},{17,9},{25,1},{2,26},{10... | collective-permute-start | bytes 786440 | tf_op jit(solution)/shard_map/ppermute | solution.py:185
  6.4 13.5 %collective-permute-start.2 = (bf16[512,256]{1,0:T(8,128)(2,1)S(1)}, bf16[512,256]{1,0:T(8,128)(2,1)S(1)}, u32[]{:S(2)}, u32[]{:S(2)}) collective-permute-start(bf16[512,256]{1,0:T(8,128)(2,1)S(1)} %pad_maximum_fusion.4.refs_8_), channel_id=1, source_target_pairs={{0,16},{8,24},{16,0},{24,8},{1,17},{9,25},{17,1},{25,9},{2,18},{10... | collective-permute-start | bytes 786440 | tf_op jit(solution)/shard_map/ppermute | solution.py:185
  6.9 13.0 %collective-permute-start.1 = (bf16[512,256]{1,0:T(8,128)(2,1)S(1)}, bf16[512,256]{1,0:T(8,128)(2,1)S(1)}, u32[]{:S(2)}, u32[]{:S(2)}) collective-permute-start(bf16[512,256]{1,0:T(8,128)(2,1)S(1)} %pad_maximum_fusion.4.refs_8_), channel_id=1, source_target_pairs={{0,8},{8,0},{16,24},{24,16},{1,9},{9,1},{17,25},{25,17},{2,10},{10... | collective-permute-start | bytes 786440 | tf_op jit(solution)/shard_map/ppermute | solution.py:185
  7.0 17.2 %copy-start.42 = (s32[128,2]{0,1:T(2,128)S(1)}, s32[128,2]{0,1:T(2,128)}, u32[]{:S(2)}) copy-start(s32[128,2]{0,1:T(2,128)} %param.20) | copy-start | bytes 3076
  7.0 17.2 %copy-start.43 = (f32[128,2]{0,1:T(2,128)S(1)}, f32[128,2]{0,1:T(2,128)}, u32[]{:S(2)}) copy-start(f32[128,2]{0,1:T(2,128)} %param.21) | copy-start | bytes 3076
  19.8 19.0 %copy-start.35 = (bf16[512,256]{1,0:T(8,128)(2,1)}, bf16[512,256]{1,0:T(8,128)(2,1)S(1)}, u32[]{:S(2)}) copy-start(bf16[512,256]{1,0:T(8,128)(2,1)S(1)} %collective-permute-done.3.refs_11_) | copy-start | bytes 786436
  19.9 4.4 %collective-permute-start.4 = (bf16[1024,256]{1,0:T(8,128)(2,1)}, bf16[1024,256]{1,0:T(8,128)(2,1)S(1)}, u32[]{:S(2)}, u32[]{:S(2)}) collective-permute-start(bf16[1024,256]{1,0:T(8,128)(2,1)} %get-tuple-element.153.refs_0_), channel_id=1, source_target_pairs={{0,1},{1,0},{2,3},{3,2},{4,5},{5,4},{6,7},{7,6},{8,9},{9,8},{10,11... | collective-permute-start | bytes 1572872 | tf_op jit(solution)/shard_map/ppermute | solution.py:182
  20.8 27.0 %collective-permute-start.5 = (bf16[1024,256]{1,0:T(8,128)(2,1)}, bf16[1024,256]{1,0:T(8,128)(2,1)S(1)}, u32[]{:S(2)}, u32[]{:S(2)}) collective-permute-start(bf16[1024,256]{1,0:T(8,128)(2,1)} %get-tuple-element.143), channel_id=1, source_target_pairs={{0,8},{8,0},{16,24},{24,16},{1,9},{9,1},{17,25},{25,17},{2,10},{10... | collective-permute-start | bytes 1572872 | tf_op jit(solution)/shard_map/ppermute | solution.py:185
  22.7 30.2 %collective-permute-start.6 = (bf16[1024,256]{1,0:T(8,128)(2,1)}, bf16[1024,256]{1,0:T(8,128)(2,1)S(1)}, u32[]{:S(2)}, u32[]{:S(2)}) collective-permute-start(bf16[1024,256]{1,0:T(8,128)(2,1)} %get-tuple-element.144), channel_id=1, source_target_pairs={{0,16},{8,24},{16,0},{24,8},{1,17},{9,25},{17,1},{25,9},{2,18},{10... | collective-permute-start | bytes 1572872 | tf_op jit(solution)/shard_map/ppermute | solution.py:185
  24.2 28.7 %collective-permute-start.7 = (bf16[1024,256]{1,0:T(8,128)(2,1)}, bf16[1024,256]{1,0:T(8,128)(2,1)S(1)}, u32[]{:S(2)}, u32[]{:S(2)}) collective-permute-start(bf16[1024,256]{1,0:T(8,128)(2,1)} %get-tuple-element.145), channel_id=1, source_target_pairs={{0,24},{8,16},{16,8},{24,0},{1,25},{9,17},{17,9},{25,1},{2,26},{10... | collective-permute-start | bytes 1572872 | tf_op jit(solution)/shard_map/ppermute | solution.py:185
  24.3 18.4 %copy-start = (bf16[1024,256]{1,0:T(8,128)(2,1)}, bf16[1024,256]{1,0:T(8,128)(2,1)S(1)}, u32[]{:S(2)}) copy-start(bf16[1024,256]{1,0:T(8,128)(2,1)S(1)} %collective-permute-done.4.refs_1_) | copy-start | bytes 1572868
  24.3 4.8 %collective-permute-start.13 = (f32[1,4,128]{2,1,0:T(4,128)S(1)}, f32[1,4,128]{2,1,0:T(4,128)S(1)}, u32[]{:S(2)}, u32[]{:S(2)}) collective-permute-start(f32[1,4,128]{2,1,0:T(4,128)S(1)} %maximum_bitcast_fusion), channel_id=1, source_target_pairs={{0,1},{1,0},{2,3},{3,2},{4,5},{5,4},{6,7},{7,6},{8,9},{9,8},{10,11... | collective-permute-start | bytes 6152 | tf_op jit(solution)/shard_map/ppermute | solution.py:236
  26.6 16.0 %collective-permute-start.8 = (bf16[256,1792]{1,0:T(8,128)(2,1)}, bf16[256,1792]{1,0:T(8,128)(2,1)}, u32[]{:S(2)}, u32[]{:S(2)}) collective-permute-start(bf16[256,1792]{1,0:T(8,128)(2,1)} %constant_dynamic-slice_fusion.5), channel_id=1, source_target_pairs={{0,1},{1,0},{2,3},{3,2},{4,5},{5,4},{6,7},{7,6},{8,9},{9,8},{10,11... | collective-permute-start | bytes 2752520 | tf_op jit(solution)/shard_map/ppermute | solution.py:182
  29.1 4.1 %collective-permute-start.14 = (f32[2,4,128]{2,1,0:T(4,128)S(1)}, f32[2,4,128]{2,1,0:T(4,128)S(1)}, u32[]{:S(2)}, u32[]{:S(2)}) collective-permute-start(f32[2,4,128]{2,1,0:T(4,128)S(1)} %pad_maximum_fusion.8), channel_id=1, source_target_pairs={{0,2},{1,3},{2,0},{3,1},{4,6},{5,7},{6,4},{7,5},{8,10},{9,11},{10,... | collective-permute-start | bytes 12296 | tf_op jit(solution)/shard_map/ppermute | solution.py:236
  33.2 4.6 %collective-permute-start.15 = (f32[4,4,128]{2,1,0:T(4,128)S(1)}, f32[4,4,128]{2,1,0:T(4,128)S(1)}, u32[]{:S(2)}, u32[]{:S(2)}) collective-permute-start(f32[4,4,128]{2,1,0:T(4,128)S(1)} %pad_maximum_fusion.7), channel_id=1, source_target_pairs={{0,4},{1,5},{2,6},{3,7},{4,0},{5,1},{6,2},{7,3},{8,12},{9,13},{10,... | collective-permute-start | bytes 24584 | tf_op jit(solution)/shard_map/ppermute | solution.py:236
  37.8 2.3 %collective-permute-start.12 = (bf16[128,2048]{1,0:T(8,128)(2,1)}, bf16[128,2048]{1,0:T(8,128)(2,1)}, u32[]{:S(2)}, u32[]{:S(2)}) collective-permute-start(bf16[128,2048]{1,0:T(8,128)(2,1)} %get-tuple-element.282), channel_id=1, source_target_pairs={{0,1},{1,0},{2,3},{3,2},{4,5},{5,4},{6,7},{7,6},{8,9},{9,8},{10,11... | collective-permute-start | bytes 1572872 | tf_op jit(solution)/shard_map/ppermute | solution.py:182
  43.6 25.3 %copy-start.27 = (bf16[512,256]{1,0:T(8,128)(2,1)}, bf16[512,256]{1,0:T(8,128)(2,1)S(1)}, u32[]{:S(2)}) copy-start(bf16[512,256]{1,0:T(8,128)(2,1)S(1)} %pad_maximum_fusion.5.refs_8_) | copy-start | bytes 786436
  43.6 10.1 %collective-permute-start.11 = (bf16[512,256]{1,0:T(8,128)(2,1)S(1)}, bf16[512,256]{1,0:T(8,128)(2,1)S(1)}, u32[]{:S(2)}, u32[]{:S(2)}) collective-permute-start(bf16[512,256]{1,0:T(8,128)(2,1)S(1)} %pad_maximum_fusion.5.refs_8_), channel_id=1, source_target_pairs={{0,24},{8,16},{16,8},{24,0},{1,25},{9,17},{17,9},{25,1},{2,26},{10... | collective-permute-start | bytes 786440 | tf_op jit(solution)/shard_map/ppermute | solution.py:185
  46.1 12.7 %collective-permute-start.10 = (bf16[512,256]{1,0:T(8,128)(2,1)S(1)}, bf16[512,256]{1,0:T(8,128)(2,1)S(1)}, u32[]{:S(2)}, u32[]{:S(2)}) collective-permute-start(bf16[512,256]{1,0:T(8,128)(2,1)S(1)} %pad_maximum_fusion.5.refs_8_), channel_id=1, source_target_pairs={{0,16},{8,24},{16,0},{24,8},{1,17},{9,25},{17,1},{25,9},{2,18},{10... | collective-permute-start | bytes 786440 | tf_op jit(solution)/shard_map/ppermute | solution.py:185
  47.8 16.8 %copy-start.1 = (bf16[1024,256]{1,0:T(8,128)(2,1)}, bf16[1024,256]{1,0:T(8,128)(2,1)S(1)}, u32[]{:S(2)}) copy-start(bf16[1024,256]{1,0:T(8,128)(2,1)S(1)} %collective-permute-done.5.refs_2_) | copy-start | bytes 1572868
  47.8 11.0 %collective-permute-start.9 = (bf16[512,256]{1,0:T(8,128)(2,1)S(1)}, bf16[512,256]{1,0:T(8,128)(2,1)S(1)}, u32[]{:S(2)}, u32[]{:S(2)}) collective-permute-start(bf16[512,256]{1,0:T(8,128)(2,1)S(1)} %pad_maximum_fusion.5.refs_8_), channel_id=1, source_target_pairs={{0,8},{8,0},{16,24},{24,16},{1,9},{9,1},{17,25},{25,17},{2,10},{10... | collective-permute-start | bytes 786440 | tf_op jit(solution)/shard_map/ppermute | solution.py:185
  52.9 11.7 %copy-start.2 = (bf16[1024,256]{1,0:T(8,128)(2,1)}, bf16[1024,256]{1,0:T(8,128)(2,1)S(1)}, u32[]{:S(2)}) copy-start(bf16[1024,256]{1,0:T(8,128)(2,1)S(1)} %collective-permute-done.6.refs_4_) | copy-start | bytes 1572868
  52.9 11.7 %copy-start.3 = (bf16[1024,256]{1,0:T(8,128)(2,1)}, bf16[1024,256]{1,0:T(8,128)(2,1)S(1)}, u32[]{:S(2)}) copy-start(bf16[1024,256]{1,0:T(8,128)(2,1)S(1)} %collective-permute-done.7.refs_6_) | copy-start | bytes 1572868
  58.8 2.9 %collective-permute-start.16 = (bf16[1024,256]{1,0:T(8,128)(2,1)S(1)}, bf16[1024,256]{1,0:T(8,128)(2,1)S(1)}, u32[]{:S(2)}, u32[]{:S(2)}) collective-permute-start(bf16[1024,256]{1,0:T(8,128)(2,1)S(1)} %collective-permute-done.5.refs_2_), channel_id=1, source_target_pairs={{0,1},{1,0},{2,3},{3,2},{4,5},{5,4},{6,7},{7,6},{8,9},{9,8},{10,11... | collective-permute-start | bytes 1572872 | tf_op jit(solution)/shard_map/ppermute | solution.py:182
  59.6 2.8 %collective-permute-start.17 = (bf16[1024,256]{1,0:T(8,128)(2,1)S(1)}, bf16[1024,256]{1,0:T(8,128)(2,1)S(1)}, u32[]{:S(2)}, u32[]{:S(2)}) collective-permute-start(bf16[1024,256]{1,0:T(8,128)(2,1)S(1)} %collective-permute-done.6.refs_4_), channel_id=1, source_target_pairs={{0,1},{1,0},{2,3},{3,2},{4,5},{5,4},{6,7},{7,6},{8,9},{9,8},{10,11... | collective-permute-start | bytes 1572872 | tf_op jit(solution)/shard_map/ppermute | solution.py:182
  59.6 2.8 %collective-permute-start.18 = (bf16[1024,256]{1,0:T(8,128)(2,1)S(1)}, bf16[1024,256]{1,0:T(8,128)(2,1)}, u32[]{:S(2)}, u32[]{:S(2)}) collective-permute-start(bf16[1024,256]{1,0:T(8,128)(2,1)S(1)} %collective-permute-done.7.refs_6_), channel_id=1, source_target_pairs={{0,1},{1,0},{2,3},{3,2},{4,5},{5,4},{6,7},{7,6},{8,9},{9,8},{10,11... | collective-permute-start | bytes 1572872 | tf_op jit(solution)/shard_map/ppermute | solution.py:182
  62.4 18.8 %collective-permute-start.20 = (bf16[512,512]{1,0:T(8,128)(2,1)}, bf16[512,512]{1,0:T(8,128)(2,1)}, u32[]{:S(2)}, u32[]{:S(2)}) collective-permute-start(bf16[512,512]{1,0:T(8,128)(2,1)} %get-tuple-element.201.refs_8_), channel_id=1, source_target_pairs={{0,16},{8,24},{16,0},{24,8},{1,17},{9,25},{17,1},{25,9},{2,18},{10... | collective-permute-start | bytes 1572872 | tf_op jit(solution)/shard_map/ppermute | solution.py:185
  64.0 17.3 %collective-permute-start.19 = (bf16[512,512]{1,0:T(8,128)(2,1)}, bf16[512,512]{1,0:T(8,128)(2,1)}, u32[]{:S(2)}, u32[]{:S(2)}) collective-permute-start(bf16[512,512]{1,0:T(8,128)(2,1)} %get-tuple-element.201.refs_8_), channel_id=1, source_target_pairs={{0,8},{8,0},{16,24},{24,16},{1,9},{9,1},{17,25},{25,17},{2,10},{10... | collective-permute-start | bytes 1572872 | tf_op jit(solution)/shard_map/ppermute | solution.py:185
  68.9 16.2 %copy-start.21 = (bf16[1024,256]{1,0:T(8,128)(2,1)S(1)}, bf16[1024,256]{1,0:T(8,128)(2,1)}, u32[]{:S(2)}) copy-start(bf16[1024,256]{1,0:T(8,128)(2,1)} %partial_product.8) | copy-start | bytes 1572868
  68.9 16.2 %collective-permute-start.22 = (bf16[1024,256]{1,0:T(8,128)(2,1)}, bf16[1024,256]{1,0:T(8,128)(2,1)}, u32[]{:S(2)}, u32[]{:S(2)}) collective-permute-start(bf16[1024,256]{1,0:T(8,128)(2,1)} %partial_product.8), channel_id=1, source_target_pairs={{0,2},{1,3},{6,4},{7,5},{8,10},{9,11},{14,12},{15,13},{16,18},{17,... | collective-permute-start | bytes 1572872 | tf_op jit(solution)/shard_map/ppermute | solution.py:195
  73.3 15.8 %collective-permute-start.21 = (bf16[512,512]{1,0:T(8,128)(2,1)}, bf16[512,512]{1,0:T(8,128)(2,1)}, u32[]{:S(2)}, u32[]{:S(2)}) collective-permute-start(bf16[512,512]{1,0:T(8,128)(2,1)} %get-tuple-element.201.refs_8_), channel_id=1, source_target_pairs={{0,24},{8,16},{16,8},{24,0},{1,25},{9,17},{17,9},{25,1},{2,26},{10... | collective-permute-start | bytes 1572872 | tf_op jit(solution)/shard_map/ppermute | solution.py:185
  74.7 14.4 %copy-start.7 = (bf16[512,512]{1,0:T(8,128)(2,1)S(1)}, bf16[512,512]{1,0:T(8,128)(2,1)}, u32[]{:S(2)}) copy-start(bf16[512,512]{1,0:T(8,128)(2,1)} %get-tuple-element.230.refs_8_) | copy-start | bytes 1572868
  74.7 18.0 %copy-start.13 = (bf16[256,2048]{1,0:T(8,128)(2,1)S(1)}, bf16[256,2048]{1,0:T(8,128)(2,1)}, u32[]{:S(2)}) copy-start(bf16[256,2048]{1,0:T(8,128)(2,1)} %maximum_select_fusion) | copy-start | bytes 3145732
  79.1 25.2 %collective-permute-start.26 = (bf16[1024,256]{1,0:T(8,128)(2,1)}, bf16[1024,256]{1,0:T(8,128)(2,1)}, u32[]{:S(2)}, u32[]{:S(2)}) collective-permute-start(bf16[1024,256]{1,0:T(8,128)(2,1)} %partial_product.9), channel_id=1, source_target_pairs={{0,2},{1,3},{6,4},{7,5},{8,10},{9,11},{14,12},{15,13},{16,18},{17,... | collective-permute-start | bytes 1572872 | tf_op jit(solution)/shard_map/ppermute | solution.py:195
  89.1 18.0 %collective-permute-start.24 = (bf16[512,512]{1,0:T(8,128)(2,1)S(1)}, bf16[512,512]{1,0:T(8,128)(2,1)S(1)}, u32[]{:S(2)}, u32[]{:S(2)}) collective-permute-start(bf16[512,512]{1,0:T(8,128)(2,1)S(1)} %copy-done.7), channel_id=1, source_target_pairs={{0,16},{8,24},{16,0},{24,8},{1,17},{9,25},{17,1},{25,9},{2,18},{10... | collective-permute-start | bytes 1572872 | tf_op jit(solution)/shard_map/ppermute | solution.py:185
  90.7 16.5 %collective-permute-start.23 = (bf16[512,512]{1,0:T(8,128)(2,1)S(1)}, bf16[512,512]{1,0:T(8,128)(2,1)S(1)}, u32[]{:S(2)}, u32[]{:S(2)}) collective-permute-start(bf16[512,512]{1,0:T(8,128)(2,1)S(1)} %copy-done.7), channel_id=1, source_target_pairs={{0,8},{8,0},{16,24},{24,16},{1,9},{9,1},{17,25},{25,17},{2,10},{10... | collective-permute-start | bytes 1572872 | tf_op jit(solution)/shard_map/ppermute | solution.py:185
  91.3 15.9 %collective-permute-start.25 = (bf16[1024,256]{1,0:T(8,128)(2,1)S(1)}, bf16[1024,256]{1,0:T(8,128)(2,1)}, u32[]{:S(2)}, u32[]{:S(2)}) collective-permute-start(bf16[1024,256]{1,0:T(8,128)(2,1)S(1)} %add_convert_fusion.15), channel_id=1, source_target_pairs={{2,4},{3,5},{4,2},{5,3},{10,12},{11,13},{12,10},{13,11},{18,20},{1... | collective-permute-start | bytes 1572872 | tf_op jit(solution)/shard_map/ppermute | solution.py:195
  93.7 10.7 %copy-start.20 = (bf16[1024,256]{1,0:T(8,128)(2,1)S(1)}, bf16[1024,256]{1,0:T(8,128)(2,1)}, u32[]{:S(2)}) copy-start(bf16[1024,256]{1,0:T(8,128)(2,1)} %partial_product.9) | copy-start | bytes 1572868
  98.0 17.1 %collective-permute-start.30 = (bf16[1024,256]{1,0:T(8,128)(2,1)}, bf16[1024,256]{1,0:T(8,128)(2,1)}, u32[]{:S(2)}, u32[]{:S(2)}) collective-permute-start(bf16[1024,256]{1,0:T(8,128)(2,1)} %partial_product.10), channel_id=1, source_target_pairs={{0,2},{1,3},{6,4},{7,5},{8,10},{9,11},{14,12},{15,13},{16,18},{17,... | collective-permute-start | bytes 1572872 | tf_op jit(solution)/shard_map/ppermute | solution.py:195
  105.5 14.5 %copy-start.6 = (bf16[512,512]{1,0:T(8,128)(2,1)S(1)}, bf16[512,512]{1,0:T(8,128)(2,1)}, u32[]{:S(2)}) copy-start(bf16[512,512]{1,0:T(8,128)(2,1)} %pad_maximum_fusion.2.refs_8_) | copy-start | bytes 1572868
  105.5 12.4 %collective-permute-start.29 = (bf16[1024,256]{1,0:T(8,128)(2,1)S(1)}, bf16[1024,256]{1,0:T(8,128)(2,1)}, u32[]{:S(2)}, u32[]{:S(2)}) collective-permute-start(bf16[1024,256]{1,0:T(8,128)(2,1)S(1)} %add_convert_fusion.14), channel_id=1, source_target_pairs={{2,4},{3,5},{4,2},{5,3},{10,12},{11,13},{12,10},{13,11},{18,20},{1... | collective-permute-start | bytes 1572872 | tf_op jit(solution)/shard_map/ppermute | solution.py:195
  107.2 12.8 %collective-permute-start.28 = (bf16[512,512]{1,0:T(8,128)(2,1)S(1)}, bf16[512,512]{1,0:T(8,128)(2,1)}, u32[]{:S(2)}, u32[]{:S(2)}) collective-permute-start(bf16[512,512]{1,0:T(8,128)(2,1)S(1)} %copy-done.7), channel_id=1, source_target_pairs={{0,24},{8,16},{16,8},{24,0},{1,25},{9,17},{17,9},{25,1},{2,26},{10... | collective-permute-start | bytes 1572872 | tf_op jit(solution)/shard_map/ppermute | solution.py:185
  115.1 14.5 %collective-permute-start.27 = (bf16[1024,256]{1,0:T(8,128)(2,1)}, bf16[1024,256]{1,0:T(8,128)(2,1)}, u32[]{:S(2)}, u32[]{:S(2)}) collective-permute-start(bf16[1024,256]{1,0:T(8,128)(2,1)} %broadcast_select_fusion.13), channel_id=1, source_target_pairs={{0,2},{1,3},{2,0},{3,1},{4,6},{5,7},{6,4},{7,5},{8,10},{9,11},{10,... | collective-permute-start | bytes 1572872 | tf_op jit(solution)/shard_map/ppermute | solution.py:195
  116.5 18.4 %collective-permute-start.34 = (bf16[1024,256]{1,0:T(8,128)(2,1)S(1)}, bf16[1024,256]{1,0:T(8,128)(2,1)}, u32[]{:S(2)}, u32[]{:S(2)}) collective-permute-start(bf16[1024,256]{1,0:T(8,128)(2,1)S(1)} %add_convert_fusion.12), channel_id=1, source_target_pairs={{2,4},{3,5},{4,2},{5,3},{10,12},{11,13},{12,10},{13,11},{18,20},{1... | collective-permute-start | bytes 1572872 | tf_op jit(solution)/shard_map/ppermute | solution.py:195
  120.0 15.6 %collective-permute-start.33 = (bf16[512,512]{1,0:T(8,128)(2,1)S(1)}, bf16[512,512]{1,0:T(8,128)(2,1)S(1)}, u32[]{:S(2)}, u32[]{:S(2)}) collective-permute-start(bf16[512,512]{1,0:T(8,128)(2,1)S(1)} %copy-done.6), channel_id=1, source_target_pairs={{0,16},{8,24},{16,0},{24,8},{1,17},{9,25},{17,1},{25,9},{2,18},{10... | collective-permute-start | bytes 1572872 | tf_op jit(solution)/shard_map/ppermute | solution.py:185
  121.2 14.4 %collective-permute-start.32 = (bf16[512,512]{1,0:T(8,128)(2,1)S(1)}, bf16[512,512]{1,0:T(8,128)(2,1)S(1)}, u32[]{:S(2)}, u32[]{:S(2)}) collective-permute-start(bf16[512,512]{1,0:T(8,128)(2,1)S(1)} %copy-done.6), channel_id=1, source_target_pairs={{0,8},{8,0},{16,24},{24,16},{1,9},{9,1},{17,25},{25,17},{2,10},{10... | collective-permute-start | bytes 1572872 | tf_op jit(solution)/shard_map/ppermute | solution.py:185
  128.5 16.9 %collective-permute-start.31 = (bf16[1024,256]{1,0:T(8,128)(2,1)}, bf16[1024,256]{1,0:T(8,128)(2,1)}, u32[]{:S(2)}, u32[]{:S(2)}) collective-permute-start(bf16[1024,256]{1,0:T(8,128)(2,1)} %broadcast_select_fusion.12), channel_id=1, source_target_pairs={{0,2},{1,3},{2,0},{3,1},{4,6},{5,7},{6,4},{7,5},{8,10},{9,11},{10,... | collective-permute-start | bytes 1572872 | tf_op jit(solution)/shard_map/ppermute | solution.py:195
  132.2 17.8 %collective-permute-start.37 = (bf16[1024,256]{1,0:T(8,128)(2,1)S(1)}, bf16[1024,256]{1,0:T(8,128)(2,1)}, u32[]{:S(2)}, u32[]{:S(2)}) collective-permute-start(bf16[1024,256]{1,0:T(8,128)(2,1)S(1)} %add_convert_fusion.10), channel_id=1, source_target_pairs={{2,4},{3,5},{4,2},{5,3},{10,12},{11,13},{12,10},{13,11},{18,20},{1... | collective-permute-start | bytes 1572872 | tf_op jit(solution)/shard_map/ppermute | solution.py:195
  135.6 15.1 %collective-permute-start.36 = (bf16[512,512]{1,0:T(8,128)(2,1)S(1)}, bf16[512,512]{1,0:T(8,128)(2,1)S(1)}, u32[]{:S(2)}, u32[]{:S(2)}) collective-permute-start(bf16[512,512]{1,0:T(8,128)(2,1)S(1)} %copy-done.6), channel_id=1, source_target_pairs={{0,24},{8,16},{16,8},{24,0},{1,25},{9,17},{17,9},{25,1},{2,26},{10... | collective-permute-start | bytes 1572872 | tf_op jit(solution)/shard_map/ppermute | solution.py:185
  143.6 17.2 %collective-permute-start.35 = (bf16[1024,256]{1,0:T(8,128)(2,1)}, bf16[1024,256]{1,0:T(8,128)(2,1)}, u32[]{:S(2)}, u32[]{:S(2)}) collective-permute-start(bf16[1024,256]{1,0:T(8,128)(2,1)} %broadcast_select_fusion.10), channel_id=1, source_target_pairs={{0,2},{1,3},{2,0},{3,1},{4,6},{5,7},{6,4},{7,5},{8,10},{9,11},{10,... | collective-permute-start | bytes 1572872 | tf_op jit(solution)/shard_map/ppermute | solution.py:195
  148.2 16.5 %collective-permute-start.39 = (bf16[1024,256]{1,0:T(8,128)(2,1)S(1)}, bf16[1024,256]{1,0:T(8,128)(2,1)S(1)}, u32[]{:S(2)}, u32[]{:S(2)}) collective-permute-start(bf16[1024,256]{1,0:T(8,128)(2,1)S(1)} %add_convert_fusion.8), channel_id=1, source_target_pairs={{2,4},{3,5},{4,2},{5,3},{10,12},{11,13},{12,10},{13,11},{18,20},{1... | collective-permute-start | bytes 1572872 | tf_op jit(solution)/shard_map/ppermute | solution.py:195
  158.1 13.6 %collective-permute-start.38 = (bf16[1024,256]{1,0:T(8,128)(2,1)}, bf16[1024,256]{1,0:T(8,128)(2,1)S(1)}, u32[]{:S(2)}, u32[]{:S(2)}) collective-permute-start(bf16[1024,256]{1,0:T(8,128)(2,1)} %broadcast_select_fusion.8), channel_id=1, source_target_pairs={{0,2},{1,3},{2,0},{3,1},{4,6},{5,7},{6,4},{7,5},{8,10},{9,11},{10,... | collective-permute-start | bytes 1572872 | tf_op jit(solution)/shard_map/ppermute | solution.py:195
  161.9 12.1 %collective-permute-start.41 = (bf16[1024,256]{1,0:T(8,128)(2,1)S(1)}, bf16[1024,256]{1,0:T(8,128)(2,1)}, u32[]{:S(2)}, u32[]{:S(2)}) collective-permute-start(bf16[1024,256]{1,0:T(8,128)(2,1)S(1)} %add_convert_fusion.6), channel_id=1, source_target_pairs={{2,4},{3,5},{4,2},{5,3},{10,12},{11,13},{12,10},{13,11},{18,20},{1... | collective-permute-start | bytes 1572872 | tf_op jit(solution)/shard_map/ppermute | solution.py:195
  170.8 13.9 %collective-permute-start.40 = (bf16[1024,256]{1,0:T(8,128)(2,1)S(1)}, bf16[1024,256]{1,0:T(8,128)(2,1)S(1)}, u32[]{:S(2)}, u32[]{:S(2)}) collective-permute-start(bf16[1024,256]{1,0:T(8,128)(2,1)S(1)} %broadcast_select_fusion.6), channel_id=1, source_target_pairs={{0,2},{1,3},{2,0},{3,1},{4,6},{5,7},{6,4},{7,5},{8,10},{9,11},{10,... | collective-permute-start | bytes 1572872 | tf_op jit(solution)/shard_map/ppermute | solution.py:195
  171.9 13.0 %copy-start.8 = (bf16[1024,256]{1,0:T(8,128)(2,1)S(1)}, bf16[1024,256]{1,0:T(8,128)(2,1)}, u32[]{:S(2)}) copy-start(bf16[1024,256]{1,0:T(8,128)(2,1)} %partial_product.15) | copy-start | bytes 1572868
  171.9 14.3 %collective-permute-start.43 = (bf16[1024,256]{1,0:T(8,128)(2,1)S(1)}, bf16[1024,256]{1,0:T(8,128)(2,1)S(1)}, u32[]{:S(2)}, u32[]{:S(2)}) collective-permute-start(bf16[1024,256]{1,0:T(8,128)(2,1)S(1)} %add_convert_fusion.4), channel_id=1, source_target_pairs={{2,4},{3,5},{4,2},{5,3},{10,12},{11,13},{12,10},{13,11},{18,20},{1... | collective-permute-start | bytes 1572872 | tf_op jit(solution)/shard_map/ppermute | solution.py:195
  175.2 20.8 %collective-permute-start.42 = (bf16[1024,256]{1,0:T(8,128)(2,1)S(1)}, bf16[1024,256]{1,0:T(8,128)(2,1)S(1)}, u32[]{:S(2)}, u32[]{:S(2)}) collective-permute-start(bf16[1024,256]{1,0:T(8,128)(2,1)S(1)} %add_convert_fusion.3), channel_id=1, source_target_pairs={{2,0},{3,1},{4,6},{5,7},{10,8},{11,9},{12,14},{13,15},{18,16},{19,... | collective-permute-start | bytes 1572872 | tf_op jit(solution)/shard_map/ppermute | solution.py:195
  185.4 2.3 %collective-permute-start.45 = (bf16[1024,256]{1,0:T(8,128)(2,1)S(1)}, bf16[1024,256]{1,0:T(8,128)(2,1)S(1)}, u32[]{:S(2)}, u32[]{:S(2)}) collective-permute-start(bf16[1024,256]{1,0:T(8,128)(2,1)S(1)} %add_convert_fusion.2), channel_id=1, source_target_pairs={{2,4},{3,5},{4,2},{5,3},{10,12},{11,13},{12,10},{13,11},{18,20},{1... | collective-permute-start | bytes 1572872 | tf_op jit(solution)/shard_map/ppermute | solution.py:195
  186.4 27.8 %collective-permute-start.44 = (bf16[1024,256]{1,0:T(8,128)(2,1)S(1)}, bf16[1024,256]{1,0:T(8,128)(2,1)S(1)}, u32[]{:S(2)}, u32[]{:S(2)}) collective-permute-start(bf16[1024,256]{1,0:T(8,128)(2,1)S(1)} %add_convert_fusion.1), channel_id=1, source_target_pairs={{2,0},{3,1},{4,6},{5,7},{10,8},{11,9},{12,14},{13,15},{18,16},{19,... | collective-permute-start | bytes 1572872 | tf_op jit(solution)/shard_map/ppermute | solution.py:195
  187.8 26.0 %collective-permute-start.46 = (bf16[1024,256]{1,0:T(8,128)(2,1)S(1)}, bf16[1024,256]{1,0:T(8,128)(2,1)S(1)}, u32[]{:S(2)}, u32[]{:S(2)}) collective-permute-start(bf16[1024,256]{1,0:T(8,128)(2,1)S(1)} %add_convert_fusion), channel_id=1, source_target_pairs={{2,0},{3,1},{4,6},{5,7},{10,8},{11,9},{12,14},{13,15},{18,16},{19,... | collective-permute-start | bytes 1572872 | tf_op jit(solution)/shard_map/ppermute | solution.py:195
  196.4 18.4 %collective-permute-start.47 = (bf16[448,1536]{1,0:T(8,128)(2,1)S(1)}, bf16[448,1536]{1,0:T(8,128)(2,1)S(1)}, u32[]{:S(2)}, u32[]{:S(2)}) collective-permute-start(bf16[448,1536]{1,0:T(8,128)(2,1)S(1)} %constant_dynamic-update-slice_fusion), channel_id=1, source_target_pairs={{0,1},{1,0},{2,3},{3,2},{4,5},{5,4},{6,7},{7,6},{8,9},{9,8},{10,11... | collective-permute-start | bytes 4128776 | tf_op jit(solution)/shard_map/ppermute | solution.py:182
  214.7 1.9 collective-permute-start.48
  (29 other events, 143.1 us)

commit v16 on v13

--- a/solution.py
+++ b/solution.py
@@ -312,7 +312,7 @@
     lag = DELAY - 1
     sums = [[None] * pieces for _ in range(hops + 1)]
     ready = [[None] * pieces for _ in range(hops + 1)]
-    outer, across = {}, {}
+    outer, across, postponed = {}, {}, []
     first_of = [sum(map(len, GROUPS[:at])) for at in range(len(GROUPS))]
     lefts, rest[1] = lax.optimization_barrier((lefts, rest[1]))
     rights.append(spread_near(rest[1]) if square else spread(rest[1]))
@@ -331,7 +331,7 @@
             if outward is not None:
                 ready[hop][outward] = jnp.where(distance == hop, got, ready[hop + 1][outward])
                 if hop == 0:
-                    finish(ready[0][outward])
+                    postponed.append(ready[0][outward])
         if step - 1 in across:
             got, index = across[step - 1]
             own, got = chain(sums[hops][index], got)
@@ -365,6 +365,10 @@
             rights[2].append(to_ctx(piece, 3))
         if step == 1 and square:
             rights[2][1:3] = chain(*rights[2][1:3])
+        if step >= pieces and postponed:
+            for grads in chain(*postponed):
+                finish(grads)
+            postponed.clear()
     result = jnp.where(
         core_at == 0,
         jnp.concatenate(rows_own + rows_got, axis=1),

time: 212 us -> 214 us (level)
  waiting for transfers between devices: 68.9 us -> 73.4 us
  local copies, waits for them, and re-layouts: 16.8 us -> 14.5 us
    ppermute x19, waiting for transfers between devices: 49.9 us -> 53.3 us  [swap_chips(): return lax.ppermute(array, 'exp', sorted(pairs))]
    unnamed x110 -> x96, local copies, waits for them, and re-layouts: 5.43 us -> 3.18 us
  transfers between devices with their start and end apart: 49 -> 49, of which waited for: 20 -> 20; matrix products, arithmetic and copies ran while one was open for 17% -> 16% of each run, Pallas kernels for 18% -> 18%
where the time goes in v16:
time: 214 us; the launch traced here: 213 us
  waiting for transfers between devices  73.4 us (34%)
  starting transfers between devices  59.2 us (28%)
  Pallas kernels  39.2 us (18%)
  other arithmetic  23.5 us (11%)
  local copies, waits for them, and re-layouts  14.5 us (7%)
  matrix products  2.36 us (1%)
    ppermute x19, waiting for transfers between devices, swap_chips(): return lax.ppermute(array, 'exp', sorted(pairs))  53.3 us
    ppermute x19, starting transfers between devices, swap_chips(): return lax.ppermute(array, 'exp', sorted(pairs))  30.3 us
    pallas_call x5, Pallas kernels, matmul(): pl.pallas_call(functools.partial(matmul_kernel, len(lefts), len(rights)),...  26.3 us
    ppermute x18, starting transfers between devices, to_ctx(): lax.ppermute(array, 'ctx', [(place, place ^ offset) for place in range(ct...  22.5 us
    ppermute x18, waiting for transfers between devices, to_ctx(): lax.ppermute(array, 'ctx', [(place, place ^ offset) for place in range(ct...  14.6 us
    pallas_call x1, Pallas kernels, conv_grad(): pl.pallas_call(functools.partial(conv_kernel, tile), grid_spec=pltpu.Pref...  12.9 us
    select_n x5, other arithmetic, on_device(): jnp.where(distance == hop, sums[hop][inward], ready[hop + 1][outward])  5.88 us
    select_n x8, other arithmetic, on_device(): jnp.where(distance == hop, got, ready[hop + 1][outward])  4.83 us
  transfers between devices with their start and end apart: 49, of which 20 were waited for; matrix products, arithmetic and copies ran while one was open for 16% of the time, Pallas kernels for 18%

profile of v16, /device:TPU:0, one launch (start us, length us, event | category | flops | bytes accessed | tf_op | source)
XLA Modules:
  0.0 213.3 jit_solution(15356869233591047291)
XLA Ops:
  0.0 1.0 constant_dynamic-slice_fusion.8
  1.5 1.0 collective-permute-done
  2.5 3.9 %collective-permute-start.3 = (bf16[512,256]{1,0:T(8,128)(2,1)S(1)}, bf16[512,256]{1,0:T(8,128)(2,1)S(1)}, u32[]{:S(2)}, u32[]{:S(2)}) collective-permute-start(bf16[512,256]{1,0:T(8,128)(2,1)S(1)} %pad_maximum_fusion.4.refs_8_), channel_id=1, source_target_pairs={{0,24},{8,16},{16,8},{24,0},{1,25},{9,17},{17,9},{25,1},{2,26},{10... | collective-permute-start | bytes 786440 | tf_op jit(solution)/shard_map/ppermute | solution.py:181
  7.0 12.9 %conv_grad.1 = (bf16[1024,256]{1,0:T(8,128)(2,1)}, bf16[1024,256]{1,0:T(8,128)(2,1)}, bf16[1024,256]{1,0:T(8,128)(2,1)}, bf16[1024,256]{1,0:T(8,128)(2,1)}) custom-call(s32[1]{0:T(128)} %bitcast.1.at_ctx, bf16[256,4096]{1,0:T(8,128)(2,1)} %out_grad.1, bf16[256,4096]{1,0:T(8,128)(2,1)} %gate_in.1, bf16[256,4096]{1,0:T(8,128)(2,1)} %conv_in.1, ...), custom_call_target="tpu_custom_call" | custom-call | flops 41943040 | bytes 10485760 | tf_op jit(solution)/shard_map/conv_grad/pallas_call | solution.py:84
  21.0 1.9 collective-permute-start.5
  22.8 1.5 collective-permute-start.6
  24.6 2.2 %constant_dynamic-slice_fusion.5 = bf16[256,1792]{1,0:T(8,128)(2,1)} fusion(bf16[256,4096]{1,0:T(8,128)(2,1)} %param.18, s32[]{:T(128)S(6)} %select_n.141), kind=kLoop, calls=%fused_computation.106 | loop fusion | bytes 1835012 | tf_op jit(solution)/shard_map/dynamic_slice | solution.py:194
  27.2 1.1 constant_dynamic-slice_fusion.4
  28.3 2.0 collective-permute-start.14
  30.3 2.0 constant_dynamic-slice_fusion.6
  32.4 2.7 %collective-permute-start.15 = (f32[4,4,128]{2,1,0:T(4,128)S(1)}, f32[4,4,128]{2,1,0:T(4,128)S(1)}, u32[]{:S(2)}, u32[]{:S(2)}) collective-permute-start(f32[4,4,128]{2,1,0:T(4,128)S(1)} %pad_maximum_fusion.7), channel_id=1, source_target_pairs={{0,4},{1,5},{2,6},{3,7},{4,0},{5,1},{6,2},{7,3},{8,12},{9,13},{10,... | collective-permute-start | bytes 24584 | tf_op jit(solution)/shard_map/ppermute | solution.py:232
  36.0 1.0 collective-permute-done.15
  39.9 2.0 maximum_select_fusion
  42.0 0.9 slice.140
  42.9 2.5 %collective-permute-start.11 = (bf16[512,256]{1,0:T(8,128)(2,1)S(1)}, bf16[512,256]{1,0:T(8,128)(2,1)S(1)}, u32[]{:S(2)}, u32[]{:S(2)}) collective-permute-start(bf16[512,256]{1,0:T(8,128)(2,1)S(1)} %pad_maximum_fusion.5.refs_8_), channel_id=1, source_target_pairs={{0,24},{8,16},{16,8},{24,0},{1,25},{9,17},{17,9},{25,1},{2,26},{10... | collective-permute-start | bytes 786440 | tf_op jit(solution)/shard_map/ppermute | solution.py:181
  46.0 1.2 fusion.24
  48.6 1.1 pad_maximum_fusion
  49.6 3.5 %collective-permute-done.6.refs_4_ = bf16[1024,256]{1,0:T(8,128)(2,1)S(1)} collective-permute-done((bf16[1024,256]{1,0:T(8,128)(2,1)}, bf16[1024,256]{1,0:T(8,128)(2,1)S(1)}, u32[]{:S(2)}, u32[]{:S(2)}) %collective-permute-start.6) | collective-permute-done | bytes 524320 | tf_op jit(solution)/shard_map/ppermute | solution.py:181
  53.7 5.2 %collective-permute-done.10.refs_10_ = bf16[512,256]{1,0:T(8,128)(2,1)S(1)} collective-permute-done((bf16[512,256]{1,0:T(8,128)(2,1)S(1)}, bf16[512,256]{1,0:T(8,128)(2,1)S(1)}, u32[]{:S(2)}, u32[]{:S(2)}) %collective-permute-start.10) | collective-permute-done | bytes 262176 | tf_op jit(solution)/shard_map/ppermute | solution.py:181
  61.0 1.6 collective-permute-done.17.refs_5_
  62.8 1.5 collective-permute-start.20
  64.9 4.4 %partial_product.5 = bf16[1024,256]{1,0:T(8,128)(2,1)} custom-call(s32[1]{0:T(128)} %bitcast.place, bf16[1024,256]{1,0:T(8,128)(2,1)} %get-tuple-element.155.refs_0_, bf16[1024,256]{1,0:T(8,128)(2,1)} %copy-done, bf16[1024,256]{1,0:T(8,128)(2,1)} %copy-done.1, bf16[1024,256]{1,0:T(8,128)(2,1)} %copy-done.3, bf16[1024,256]{1,0:T(8,128)(2,1)} %copy-done.2, ...), custom_call_target="tpu_custom_call" | custom-call | flops 1073741824 | bytes 5767168 | tf_op jit(solution)/shard_map/partial_product/pallas_call | solution.py:130
  69.3 3.6 %collective-permute-start.22 = (bf16[1024,256]{1,0:T(8,128)(2,1)}, bf16[1024,256]{1,0:T(8,128)(2,1)S(1)}, u32[]{:S(2)}, u32[]{:S(2)}) collective-permute-start(bf16[1024,256]{1,0:T(8,128)(2,1)} %partial_product.5), channel_id=1, source_target_pairs={{0,2},{1,3},{6,4},{7,5},{8,10},{9,11},{14,12},{15,13},{16,18},{17,... | collective-permute-start | bytes 1572872 | tf_op jit(solution)/shard_map/ppermute | solution.py:191
  72.9 1.5 collective-permute-start.21
  74.4 4.3 %partial_product.6 = bf16[1024,256]{1,0:T(8,128)(2,1)} custom-call(s32[1]{0:T(128)} %bitcast.place, bf16[1024,256]{1,0:T(8,128)(2,1)} %get-tuple-element.155.refs_0_, bf16[1024,256]{1,0:T(8,128)(2,1)} %copy-done, bf16[1024,256]{1,0:T(8,128)(2,1)} %copy-done.1, bf16[1024,256]{1,0:T(8,128)(2,1)} %copy-done.3, bf16[1024,256]{1,0:T(8,128)(2,1)} %copy-done.2, ...), custom_call_target="tpu_custom_call" | custom-call | flops 1073741824 | bytes 5767168 | tf_op jit(solution)/shard_map/partial_product/pallas_call | solution.py:130
  78.7 2.1 collective-permute-start.24
  80.9 4.7 %collective-permute-done.22 = bf16[1024,256]{1,0:T(8,128)(2,1)S(1)} collective-permute-done((bf16[1024,256]{1,0:T(8,128)(2,1)}, bf16[1024,256]{1,0:T(8,128)(2,1)S(1)}, u32[]{:S(2)}, u32[]{:S(2)}) %collective-permute-start.22) | collective-permute-done | bytes 524320 | tf_op jit(solution)/shard_map/ppermute | solution.py:191
  85.7 3.7 %collective-permute-done.21.refs_11_ = bf16[512,512]{1,0:T(8,128)(2,1)S(1)} collective-permute-done((bf16[512,512]{1,0:T(8,128)(2,1)}, bf16[512,512]{1,0:T(8,128)(2,1)S(1)}, u32[]{:S(2)}, u32[]{:S(2)}) %collective-permute-start.21) | collective-permute-done | bytes 524320 | tf_op jit(solution)/shard_map/ppermute | solution.py:181
  89.4 1.5 collective-permute-start.26
  92.1 0.9 fusion.22
  93.1 5.9 %partial_product.7 = (bf16[1024,256]{1,0:T(8,128)(2,1)}, bf16[1024,256]{1,0:T(8,128)(2,1)}) custom-call(s32[1]{0:T(128)} %bitcast.place, bf16[1024,256]{1,0:T(8,128)(2,1)} %get-tuple-element.155.refs_0_, bf16[1024,256]{1,0:T(8,128)(2,1)} %copy-done, bf16[1024,256]{1,0:T(8,128)(2,1)} %copy-done.1, bf16[1024,256]{1,0:T(8,128)(2,1)} %copy-done.3, ...), custom_call_target="tpu_custom_call" | custom-call | flops 2147483648 | bytes 7340032 | tf_op jit(solution)/shard_map/partial_product/pallas_call | solution.py:130
  99.0 6.4 %collective-permute-start.30 = (bf16[1024,256]{1,0:T(8,128)(2,1)}, bf16[1024,256]{1,0:T(8,128)(2,1)S(1)}, u32[]{:S(2)}, u32[]{:S(2)}) collective-permute-start(bf16[1024,256]{1,0:T(8,128)(2,1)} %get-tuple-element.210), channel_id=1, source_target_pairs={{0,2},{1,3},{6,4},{7,5},{8,10},{9,11},{14,12},{15,13},{16,18},{17,... | collective-permute-start | bytes 1572872 | tf_op jit(solution)/shard_map/ppermute | solution.py:191
  105.4 1.2 add_convert_fusion.14
  107.4 1.8 collective-permute-start.28
  109.1 2.0 broadcast_select_fusion.13
  111.2 6.9 %collective-permute-done.30 = bf16[1024,256]{1,0:T(8,128)(2,1)S(1)} collective-permute-done((bf16[1024,256]{1,0:T(8,128)(2,1)}, bf16[1024,256]{1,0:T(8,128)(2,1)S(1)}, u32[]{:S(2)}, u32[]{:S(2)}) %collective-permute-start.30) | collective-permute-done | bytes 524320 | tf_op jit(solution)/shard_map/ppermute | solution.py:191
  118.9 1.6 collective-permute-done.28.refs_11_
  120.5 1.0 collective-permute-start.34
  121.5 1.3 collective-permute-start.33
  122.8 5.9 %partial_product.8 = (bf16[1024,256]{1,0:T(8,128)(2,1)}, bf16[1024,256]{1,0:T(8,128)(2,1)}) custom-call(s32[1]{0:T(128)} %bitcast.place, bf16[1024,256]{1,0:T(8,128)(2,1)} %get-tuple-element.155.refs_0_, bf16[1024,256]{1,0:T(8,128)(2,1)} %copy-done, bf16[1024,256]{1,0:T(8,128)(2,1)} %copy-done.1, bf16[1024,256]{1,0:T(8,128)(2,1)} %copy-done.3, ...), custom_call_target="tpu_custom_call" | custom-call | flops 2147483648 | bytes 7340032 | tf_op jit(solution)/shard_map/partial_product/pallas_call | solution.py:130
  128.7 1.3 broadcast_select_fusion.12
  130.0 1.5 collective-permute-start.31
  131.5 1.2 add_convert_fusion.10
  133.4 2.0 broadcast_select_fusion.11
  135.5 1.0 broadcast_select_fusion.10
  136.5 1.2 collective-permute-start.36
  137.7 1.9 collective-permute-start.35
  139.6 5.3 %collective-permute-done.31 = bf16[1024,256]{1,0:T(8,128)(2,1)S(1)} collective-permute-done((bf16[1024,256]{1,0:T(8,128)(2,1)S(1)}, bf16[1024,256]{1,0:T(8,128)(2,1)S(1)}, u32[]{:S(2)}, u32[]{:S(2)}) %collective-permute-start.31) | collective-permute-done | bytes 524320 | tf_op jit(solution)/shard_map/ppermute | solution.py:191
  145.0 1.0 broadcast_select_fusion.9
  146.9 5.9 %partial_product.9 = (bf16[1024,256]{1,0:T(8,128)(2,1)}, bf16[1024,256]{1,0:T(8,128)(2,1)}) custom-call(s32[1]{0:T(128)} %bitcast.place, bf16[1024,256]{1,0:T(8,128)(2,1)} %get-tuple-element.155.refs_0_, bf16[1024,256]{1,0:T(8,128)(2,1)} %copy-done, bf16[1024,256]{1,0:T(8,128)(2,1)} %copy-done.1, bf16[1024,256]{1,0:T(8,128)(2,1)} %copy-done.3, ...), custom_call_target="tpu_custom_call" | custom-call | flops 2147483648 | bytes 7340032 | tf_op jit(solution)/shard_map/partial_product/pallas_call | solution.py:130
  152.8 1.3 broadcast_select_fusion.8
  154.1 1.3 collective-permute-start.38
  155.4 1.2 add_convert_fusion.6
  157.7 3.6 %collective-permute-start.41 = (bf16[1024,256]{1,0:T(8,128)(2,1)S(1)}, bf16[1024,256]{1,0:T(8,128)(2,1)S(1)}, u32[]{:S(2)}, u32[]{:S(2)}) collective-permute-start(bf16[1024,256]{1,0:T(8,128)(2,1)S(1)} %broadcast_select_fusion.6), channel_id=1, source_target_pairs={{0,2},{1,3},{2,0},{3,1},{4,6},{5,7},{6,4},{7,5},{8,10},{9,11},{10,... | collective-permute-start | bytes 1572872 | tf_op jit(solution)/shard_map/ppermute | solution.py:191
  161.3 1.2 broadcast_select_fusion.7
  162.6 6.4 %collective-permute-done.38 = bf16[1024,256]{1,0:T(8,128)(2,1)S(1)} collective-permute-done((bf16[1024,256]{1,0:T(8,128)(2,1)S(1)}, bf16[1024,256]{1,0:T(8,128)(2,1)S(1)}, u32[]{:S(2)}, u32[]{:S(2)}) %collective-permute-start.38) | collective-permute-done | bytes 524320 | tf_op jit(solution)/shard_map/ppermute | solution.py:191
  170.2 1.4 collective-permute-start.43
  172.4 7.9 %collective-permute-done.41 = bf16[1024,256]{1,0:T(8,128)(2,1)S(1)} collective-permute-done((bf16[1024,256]{1,0:T(8,128)(2,1)S(1)}, bf16[1024,256]{1,0:T(8,128)(2,1)S(1)}, u32[]{:S(2)}, u32[]{:S(2)}) %collective-permute-start.41) | collective-permute-done | bytes 524320 | tf_op jit(solution)/shard_map/ppermute | solution.py:191
  182.4 1.3 collective-permute-start.45
  183.8 1.3 collective-permute-start.46
  185.1 6.4 %collective-permute-done.43 = bf16[1024,256]{1,0:T(8,128)(2,1)S(1)} collective-permute-done((bf16[1024,256]{1,0:T(8,128)(2,1)S(1)}, bf16[1024,256]{1,0:T(8,128)(2,1)S(1)}, u32[]{:S(2)}, u32[]{:S(2)}) %collective-permute-start.43) | collective-permute-done | bytes 524320 | tf_op jit(solution)/shard_map/ppermute | solution.py:191
  192.4 15.6 %collective-permute-done.46 = bf16[1024,256]{1,0:T(8,128)(2,1)S(1)} collective-permute-done((bf16[1024,256]{1,0:T(8,128)(2,1)S(1)}, bf16[1024,256]{1,0:T(8,128)(2,1)S(1)}, u32[]{:S(2)}, u32[]{:S(2)}) %collective-permute-start.46) | collective-permute-done | bytes 524320 | tf_op jit(solution)/shard_map/ppermute | solution.py:191
  209.4 1.4 collective-permute-done.48
  211.1 2.2 %broadcast_select_fusion = bf16[1,448,4096]{2,1,0:T(8,128)(2,1)} fusion(bf16[1,448,4096]{2,1,0:T(8,128)(2,1)S(1)} %get-tuple-element.291, bf16[1,448,4096]{2,1,0:T(8,128)(2,1)S(1)} %constant_dynamic-update-slice_fusion.14, pred[]{:T(512)S(6)} %eq.30), kind=kLoop, calls=%fused_computation | loop fusion | flops 1835008 | bytes 11010049 | tf_op jit(solution)/shard_map/jit(_where)/select_n | solution.py:372
  (220 shorter events, 23.7 us)
Async XLA Ops:
  1.0 1.5 collective-permute-start
  2.5 17.4 %copy-start.17 = (bf16[512,256]{1,0:T(8,128)(2,1)}, bf16[512,256]{1,0:T(8,128)(2,1)S(1)}, u32[]{:S(2)}) copy-start(bf16[512,256]{1,0:T(8,128)(2,1)S(1)} %pad_maximum_fusion.4.refs_8_) | copy-start | bytes 786436
  2.5 17.4 %collective-permute-start.3 = (bf16[512,256]{1,0:T(8,128)(2,1)S(1)}, bf16[512,256]{1,0:T(8,128)(2,1)S(1)}, u32[]{:S(2)}, u32[]{:S(2)}) collective-permute-start(bf16[512,256]{1,0:T(8,128)(2,1)S(1)} %pad_maximum_fusion.4.refs_8_), channel_id=1, source_target_pairs={{0,24},{8,16},{16,8},{24,0},{1,25},{9,17},{17,9},{25,1},{2,26},{10... | collective-permute-start | bytes 786440 | tf_op jit(solution)/shard_map/ppermute | solution.py:181
  6.4 13.6 %collective-permute-start.2 = (bf16[512,256]{1,0:T(8,128)(2,1)S(1)}, bf16[512,256]{1,0:T(8,128)(2,1)S(1)}, u32[]{:S(2)}, u32[]{:S(2)}) collective-permute-start(bf16[512,256]{1,0:T(8,128)(2,1)S(1)} %pad_maximum_fusion.4.refs_8_), channel_id=1, source_target_pairs={{0,16},{8,24},{16,0},{24,8},{1,17},{9,25},{17,1},{25,9},{2,18},{10... | collective-permute-start | bytes 786440 | tf_op jit(solution)/shard_map/ppermute | solution.py:181
  6.9 13.1 %collective-permute-start.1 = (bf16[512,256]{1,0:T(8,128)(2,1)S(1)}, bf16[512,256]{1,0:T(8,128)(2,1)S(1)}, u32[]{:S(2)}, u32[]{:S(2)}) collective-permute-start(bf16[512,256]{1,0:T(8,128)(2,1)S(1)} %pad_maximum_fusion.4.refs_8_), channel_id=1, source_target_pairs={{0,8},{8,0},{16,24},{24,16},{1,9},{9,1},{17,25},{25,17},{2,10},{10... | collective-permute-start | bytes 786440 | tf_op jit(solution)/shard_map/ppermute | solution.py:181
  7.0 17.4 %copy-start.32 = (s32[128,2]{0,1:T(2,128)S(1)}, s32[128,2]{0,1:T(2,128)}, u32[]{:S(2)}) copy-start(s32[128,2]{0,1:T(2,128)} %param.20) | copy-start | bytes 3076
  7.0 17.4 %copy-start.33 = (f32[128,2]{0,1:T(2,128)S(1)}, f32[128,2]{0,1:T(2,128)}, u32[]{:S(2)}) copy-start(f32[128,2]{0,1:T(2,128)} %param.21) | copy-start | bytes 3076
  7.0 20.2 %copy-start.20 = (bf16[128,4096]{1,0:T(8,128)(2,1)S(1)}, bf16[128,4096]{1,0:T(8,128)(2,1)}, u32[]{:S(2)}) copy-start(bf16[128,4096]{1,0:T(8,128)(2,1)} %param.19) | copy-start | bytes 3145732
  20.0 18.1 %copy-start.26 = (bf16[512,256]{1,0:T(8,128)(2,1)}, bf16[512,256]{1,0:T(8,128)(2,1)S(1)}, u32[]{:S(2)}) copy-start(bf16[512,256]{1,0:T(8,128)(2,1)S(1)} %collective-permute-done.3.refs_11_) | copy-start | bytes 786436
  20.0 4.4 %collective-permute-start.4 = (bf16[1024,256]{1,0:T(8,128)(2,1)}, bf16[1024,256]{1,0:T(8,128)(2,1)S(1)}, u32[]{:S(2)}, u32[]{:S(2)}) collective-permute-start(bf16[1024,256]{1,0:T(8,128)(2,1)} %get-tuple-element.155.refs_0_), channel_id=1, source_target_pairs={{0,1},{1,0},{2,3},{3,2},{4,5},{5,4},{6,7},{7,6},{8,9},{9,8},{10,11... | collective-permute-start | bytes 1572872 | tf_op jit(solution)/shard_map/ppermute | solution.py:178
  21.0 26.2 %collective-permute-start.5 = (bf16[1024,256]{1,0:T(8,128)(2,1)}, bf16[1024,256]{1,0:T(8,128)(2,1)S(1)}, u32[]{:S(2)}, u32[]{:S(2)}) collective-permute-start(bf16[1024,256]{1,0:T(8,128)(2,1)} %get-tuple-element.145), channel_id=1, source_target_pairs={{0,8},{8,0},{16,24},{24,16},{1,9},{9,1},{17,25},{25,17},{2,10},{10... | collective-permute-start | bytes 1572872 | tf_op jit(solution)/shard_map/ppermute | solution.py:181
  22.8 30.3 %collective-permute-start.6 = (bf16[1024,256]{1,0:T(8,128)(2,1)}, bf16[1024,256]{1,0:T(8,128)(2,1)S(1)}, u32[]{:S(2)}, u32[]{:S(2)}) collective-permute-start(bf16[1024,256]{1,0:T(8,128)(2,1)} %get-tuple-element.146), channel_id=1, source_target_pairs={{0,16},{8,24},{16,0},{24,8},{1,17},{9,25},{17,1},{25,9},{2,18},{10... | collective-permute-start | bytes 1572872 | tf_op jit(solution)/shard_map/ppermute | solution.py:181
  24.4 28.8 %collective-permute-start.7 = (bf16[1024,256]{1,0:T(8,128)(2,1)}, bf16[1024,256]{1,0:T(8,128)(2,1)}, u32[]{:S(2)}, u32[]{:S(2)}) collective-permute-start(bf16[1024,256]{1,0:T(8,128)(2,1)} %get-tuple-element.147), channel_id=1, source_target_pairs={{0,24},{8,16},{16,8},{24,0},{1,25},{9,17},{17,9},{25,1},{2,26},{10... | collective-permute-start | bytes 1572872 | tf_op jit(solution)/shard_map/ppermute | solution.py:181
  24.5 17.5 %copy-start = (bf16[1024,256]{1,0:T(8,128)(2,1)}, bf16[1024,256]{1,0:T(8,128)(2,1)S(1)}, u32[]{:S(2)}) copy-start(bf16[1024,256]{1,0:T(8,128)(2,1)S(1)} %collective-permute-done.4.refs_1_) | copy-start | bytes 1572868
  24.5 3.8 %collective-permute-start.13 = (f32[1,4,128]{2,1,0:T(4,128)S(1)}, f32[1,4,128]{2,1,0:T(4,128)S(1)}, u32[]{:S(2)}, u32[]{:S(2)}) collective-permute-start(f32[1,4,128]{2,1,0:T(4,128)S(1)} %maximum_bitcast_fusion), channel_id=1, source_target_pairs={{0,1},{1,0},{2,3},{3,2},{4,5},{5,4},{6,7},{7,6},{8,9},{9,8},{10,11... | collective-permute-start | bytes 6152 | tf_op jit(solution)/shard_map/ppermute | solution.py:232
  26.8 15.1 %collective-permute-start.8 = (bf16[256,1792]{1,0:T(8,128)(2,1)}, bf16[256,1792]{1,0:T(8,128)(2,1)}, u32[]{:S(2)}, u32[]{:S(2)}) collective-permute-start(bf16[256,1792]{1,0:T(8,128)(2,1)} %constant_dynamic-slice_fusion.5), channel_id=1, source_target_pairs={{0,1},{1,0},{2,3},{3,2},{4,5},{5,4},{6,7},{7,6},{8,9},{9,8},{10,11... | collective-permute-start | bytes 2752520 | tf_op jit(solution)/shard_map/ppermute | solution.py:178
  28.3 4.1 %collective-permute-start.14 = (f32[2,4,128]{2,1,0:T(4,128)S(1)}, f32[2,4,128]{2,1,0:T(4,128)S(1)}, u32[]{:S(2)}, u32[]{:S(2)}) collective-permute-start(f32[2,4,128]{2,1,0:T(4,128)S(1)} %pad_maximum_fusion.8), channel_id=1, source_target_pairs={{0,2},{1,3},{2,0},{3,1},{4,6},{5,7},{6,4},{7,5},{8,10},{9,11},{10,... | collective-permute-start | bytes 12296 | tf_op jit(solution)/shard_map/ppermute | solution.py:232
  32.4 4.6 %collective-permute-start.15 = (f32[4,4,128]{2,1,0:T(4,128)S(1)}, f32[4,4,128]{2,1,0:T(4,128)S(1)}, u32[]{:S(2)}, u32[]{:S(2)}) collective-permute-start(f32[4,4,128]{2,1,0:T(4,128)S(1)} %pad_maximum_fusion.7), channel_id=1, source_target_pairs={{0,4},{1,5},{2,6},{3,7},{4,0},{5,1},{6,2},{7,3},{8,12},{9,13},{10,... | collective-permute-start | bytes 24584 | tf_op jit(solution)/shard_map/ppermute | solution.py:232
  37.0 2.1 collective-permute-start.12
  42.9 26.4 %copy-start.18 = (bf16[512,256]{1,0:T(8,128)(2,1)}, bf16[512,256]{1,0:T(8,128)(2,1)S(1)}, u32[]{:S(2)}) copy-start(bf16[512,256]{1,0:T(8,128)(2,1)S(1)} %pad_maximum_fusion.5.refs_8_) | copy-start | bytes 786436
  42.9 10.8 %collective-permute-start.11 = (bf16[512,256]{1,0:T(8,128)(2,1)S(1)}, bf16[512,256]{1,0:T(8,128)(2,1)S(1)}, u32[]{:S(2)}, u32[]{:S(2)}) collective-permute-start(bf16[512,256]{1,0:T(8,128)(2,1)S(1)} %pad_maximum_fusion.5.refs_8_), channel_id=1, source_target_pairs={{0,24},{8,16},{16,8},{24,0},{1,25},{9,17},{17,9},{25,1},{2,26},{10... | collective-permute-start | bytes 786440 | tf_op jit(solution)/shard_map/ppermute | solution.py:181
  45.4 13.5 %collective-permute-start.10 = (bf16[512,256]{1,0:T(8,128)(2,1)S(1)}, bf16[512,256]{1,0:T(8,128)(2,1)S(1)}, u32[]{:S(2)}, u32[]{:S(2)}) collective-permute-start(bf16[512,256]{1,0:T(8,128)(2,1)S(1)} %pad_maximum_fusion.5.refs_8_), channel_id=1, source_target_pairs={{0,16},{8,24},{16,0},{24,8},{1,17},{9,25},{17,1},{25,9},{2,18},{10... | collective-permute-start | bytes 786440 | tf_op jit(solution)/shard_map/ppermute | solution.py:181
  47.1 17.7 %copy-start.1 = (bf16[1024,256]{1,0:T(8,128)(2,1)}, bf16[1024,256]{1,0:T(8,128)(2,1)S(1)}, u32[]{:S(2)}) copy-start(bf16[1024,256]{1,0:T(8,128)(2,1)S(1)} %collective-permute-done.5.refs_2_) | copy-start | bytes 1572868
  47.1 11.8 %collective-permute-start.9 = (bf16[512,256]{1,0:T(8,128)(2,1)S(1)}, bf16[512,256]{1,0:T(8,128)(2,1)S(1)}, u32[]{:S(2)}, u32[]{:S(2)}) collective-permute-start(bf16[512,256]{1,0:T(8,128)(2,1)S(1)} %pad_maximum_fusion.5.refs_8_), channel_id=1, source_target_pairs={{0,8},{8,0},{16,24},{24,16},{1,9},{9,1},{17,25},{25,17},{2,10},{10... | collective-permute-start | bytes 786440 | tf_op jit(solution)/shard_map/ppermute | solution.py:181
  59.0 2.0 collective-permute-start.16
  59.7 2.9 %collective-permute-start.17 = (bf16[1024,256]{1,0:T(8,128)(2,1)S(1)}, bf16[1024,256]{1,0:T(8,128)(2,1)}, u32[]{:S(2)}, u32[]{:S(2)}) collective-permute-start(bf16[1024,256]{1,0:T(8,128)(2,1)S(1)} %collective-permute-done.6.refs_4_), channel_id=1, source_target_pairs={{0,1},{1,0},{2,3},{3,2},{4,5},{5,4},{6,7},{7,6},{8,9},{9,8},{10,11... | collective-permute-start | bytes 1572872 | tf_op jit(solution)/shard_map/ppermute | solution.py:178
  59.8 3.0 %collective-permute-start.18 = (bf16[1024,256]{1,0:T(8,128)(2,1)}, bf16[1024,256]{1,0:T(8,128)(2,1)}, u32[]{:S(2)}, u32[]{:S(2)}) collective-permute-start(bf16[1024,256]{1,0:T(8,128)(2,1)} %collective-permute-done.7.refs_6_), channel_id=1, source_target_pairs={{0,1},{1,0},{2,3},{3,2},{4,5},{5,4},{6,7},{7,6},{8,9},{9,8},{10,11... | collective-permute-start | bytes 1572872 | tf_op jit(solution)/shard_map/ppermute | solution.py:178
  62.8 18.1 %collective-permute-start.20 = (bf16[512,512]{1,0:T(8,128)(2,1)}, bf16[512,512]{1,0:T(8,128)(2,1)}, u32[]{:S(2)}, u32[]{:S(2)}) collective-permute-start(bf16[512,512]{1,0:T(8,128)(2,1)} %get-tuple-element.194.refs_8_), channel_id=1, source_target_pairs={{0,16},{8,24},{16,0},{24,8},{1,17},{9,25},{17,1},{25,9},{2,18},{10... | collective-permute-start | bytes 1572872 | tf_op jit(solution)/shard_map/ppermute | solution.py:181
  64.3 16.5 %collective-permute-start.19 = (bf16[512,512]{1,0:T(8,128)(2,1)}, bf16[512,512]{1,0:T(8,128)(2,1)}, u32[]{:S(2)}, u32[]{:S(2)}) collective-permute-start(bf16[512,512]{1,0:T(8,128)(2,1)} %get-tuple-element.194.refs_8_), channel_id=1, source_target_pairs={{0,8},{8,0},{16,24},{24,16},{1,9},{9,1},{17,25},{25,17},{2,10},{10... | collective-permute-start | bytes 1572872 | tf_op jit(solution)/shard_map/ppermute | solution.py:181
  69.3 16.3 %copy-start.14 = (bf16[1024,256]{1,0:T(8,128)(2,1)S(1)}, bf16[1024,256]{1,0:T(8,128)(2,1)}, u32[]{:S(2)}) copy-start(bf16[1024,256]{1,0:T(8,128)(2,1)} %partial_product.5) | copy-start | bytes 1572868
  69.3 16.3 %collective-permute-start.22 = (bf16[1024,256]{1,0:T(8,128)(2,1)}, bf16[1024,256]{1,0:T(8,128)(2,1)S(1)}, u32[]{:S(2)}, u32[]{:S(2)}) collective-permute-start(bf16[1024,256]{1,0:T(8,128)(2,1)} %partial_product.5), channel_id=1, source_target_pairs={{0,2},{1,3},{6,4},{7,5},{8,10},{9,11},{14,12},{15,13},{16,18},{17,... | collective-permute-start | bytes 1572872 | tf_op jit(solution)/shard_map/ppermute | solution.py:191
  72.9 16.4 %collective-permute-start.21 = (bf16[512,512]{1,0:T(8,128)(2,1)}, bf16[512,512]{1,0:T(8,128)(2,1)S(1)}, u32[]{:S(2)}, u32[]{:S(2)}) collective-permute-start(bf16[512,512]{1,0:T(8,128)(2,1)} %get-tuple-element.194.refs_8_), channel_id=1, source_target_pairs={{0,24},{8,16},{16,8},{24,0},{1,25},{9,17},{17,9},{25,1},{2,26},{10... | collective-permute-start | bytes 1572872 | tf_op jit(solution)/shard_map/ppermute | solution.py:181
  78.7 26.7 %collective-permute-start.24 = (bf16[1024,256]{1,0:T(8,128)(2,1)}, bf16[1024,256]{1,0:T(8,128)(2,1)}, u32[]{:S(2)}, u32[]{:S(2)}) collective-permute-start(bf16[1024,256]{1,0:T(8,128)(2,1)} %partial_product.6), channel_id=1, source_target_pairs={{0,2},{1,3},{6,4},{7,5},{8,10},{9,11},{14,12},{15,13},{16,18},{17,... | collective-permute-start | bytes 1572872 | tf_op jit(solution)/shard_map/ppermute | solution.py:191
  89.4 17.9 %collective-permute-start.26 = (bf16[512,512]{1,0:T(8,128)(2,1)}, bf16[512,512]{1,0:T(8,128)(2,1)}, u32[]{:S(2)}, u32[]{:S(2)}) collective-permute-start(bf16[512,512]{1,0:T(8,128)(2,1)} %get-tuple-element.218.refs_8_), channel_id=1, source_target_pairs={{0,16},{8,24},{16,0},{24,8},{1,17},{9,25},{17,1},{25,9},{2,18},{10... | collective-permute-start | bytes 1572872 | tf_op jit(solution)/shard_map/ppermute | solution.py:181
  90.9 16.4 %collective-permute-start.25 = (bf16[512,512]{1,0:T(8,128)(2,1)}, bf16[512,512]{1,0:T(8,128)(2,1)}, u32[]{:S(2)}, u32[]{:S(2)}) collective-permute-start(bf16[512,512]{1,0:T(8,128)(2,1)} %get-tuple-element.218.refs_8_), channel_id=1, source_target_pairs={{0,8},{8,0},{16,24},{24,16},{1,9},{9,1},{17,25},{25,17},{2,10},{10... | collective-permute-start | bytes 1572872 | tf_op jit(solution)/shard_map/ppermute | solution.py:181
  91.4 15.9 %collective-permute-start.23 = (bf16[1024,256]{1,0:T(8,128)(2,1)S(1)}, bf16[1024,256]{1,0:T(8,128)(2,1)S(1)}, u32[]{:S(2)}, u32[]{:S(2)}) collective-permute-start(bf16[1024,256]{1,0:T(8,128)(2,1)S(1)} %add_convert_fusion.15), channel_id=1, source_target_pairs={{2,4},{3,5},{4,2},{5,3},{10,12},{11,13},{12,10},{13,11},{18,20},{1... | collective-permute-start | bytes 1572872 | tf_op jit(solution)/shard_map/ppermute | solution.py:191
  93.1 12.4 %copy-start.11 = (bf16[1024,256]{1,0:T(8,128)(2,1)S(1)}, bf16[1024,256]{1,0:T(8,128)(2,1)}, u32[]{:S(2)}) copy-start(bf16[1024,256]{1,0:T(8,128)(2,1)} %partial_product.6) | copy-start | bytes 1572868
  99.0 19.1 %copy-start.24 = (bf16[1024,256]{1,0:T(8,128)(2,1)S(1)}, bf16[1024,256]{1,0:T(8,128)(2,1)}, u32[]{:S(2)}) copy-start(bf16[1024,256]{1,0:T(8,128)(2,1)} %get-tuple-element.210) | copy-start | bytes 1572868
  99.0 19.1 %collective-permute-start.30 = (bf16[1024,256]{1,0:T(8,128)(2,1)}, bf16[1024,256]{1,0:T(8,128)(2,1)S(1)}, u32[]{:S(2)}, u32[]{:S(2)}) collective-permute-start(bf16[1024,256]{1,0:T(8,128)(2,1)} %get-tuple-element.210), channel_id=1, source_target_pairs={{0,2},{1,3},{6,4},{7,5},{8,10},{9,11},{14,12},{15,13},{16,18},{17,... | collective-permute-start | bytes 1572872 | tf_op jit(solution)/shard_map/ppermute | solution.py:191
  106.6 12.3 %collective-permute-start.29 = (bf16[1024,256]{1,0:T(8,128)(2,1)S(1)}, bf16[1024,256]{1,0:T(8,128)(2,1)S(1)}, u32[]{:S(2)}, u32[]{:S(2)}) collective-permute-start(bf16[1024,256]{1,0:T(8,128)(2,1)S(1)} %add_convert_fusion.14), channel_id=1, source_target_pairs={{2,4},{3,5},{4,2},{5,3},{10,12},{11,13},{12,10},{13,11},{18,20},{1... | collective-permute-start | bytes 1572872 | tf_op jit(solution)/shard_map/ppermute | solution.py:191
  107.4 13.1 %collective-permute-start.28 = (bf16[512,512]{1,0:T(8,128)(2,1)}, bf16[512,512]{1,0:T(8,128)(2,1)S(1)}, u32[]{:S(2)}, u32[]{:S(2)}) collective-permute-start(bf16[512,512]{1,0:T(8,128)(2,1)} %get-tuple-element.218.refs_8_), channel_id=1, source_target_pairs={{0,24},{8,16},{16,8},{24,0},{1,25},{9,17},{17,9},{25,1},{2,26},{10... | collective-permute-start | bytes 1572872 | tf_op jit(solution)/shard_map/ppermute | solution.py:181
  111.2 20.4 %collective-permute-start.27 = (bf16[1024,256]{1,0:T(8,128)(2,1)}, bf16[1024,256]{1,0:T(8,128)(2,1)}, u32[]{:S(2)}, u32[]{:S(2)}) collective-permute-start(bf16[1024,256]{1,0:T(8,128)(2,1)} %broadcast_select_fusion.13), channel_id=1, source_target_pairs={{0,2},{1,3},{2,0},{3,1},{4,6},{5,7},{6,4},{7,5},{8,10},{9,11},{10,... | collective-permute-start | bytes 1572872 | tf_op jit(solution)/shard_map/ppermute | solution.py:191
  118.2 15.2 %collective-permute-start.32 = (bf16[1024,256]{1,0:T(8,128)(2,1)S(1)}, bf16[1024,256]{1,0:T(8,128)(2,1)S(1)}, u32[]{:S(2)}, u32[]{:S(2)}) collective-permute-start(bf16[1024,256]{1,0:T(8,128)(2,1)S(1)} %add_convert_fusion.12), channel_id=1, source_target_pairs={{2,4},{3,5},{4,2},{5,3},{10,12},{11,13},{12,10},{13,11},{18,20},{1... | collective-permute-start | bytes 1572872 | tf_op jit(solution)/shard_map/ppermute | solution.py:191
  120.5 16.0 %collective-permute-start.34 = (bf16[512,512]{1,0:T(8,128)(2,1)}, bf16[512,512]{1,0:T(8,128)(2,1)}, u32[]{:S(2)}, u32[]{:S(2)}) collective-permute-start(bf16[512,512]{1,0:T(8,128)(2,1)} %pad_maximum_fusion.2.refs_8_), channel_id=1, source_target_pairs={{0,16},{8,24},{16,0},{24,8},{1,17},{9,25},{17,1},{25,9},{2,18},{10... | collective-permute-start | bytes 1572872 | tf_op jit(solution)/shard_map/ppermute | solution.py:181
  121.5 15.0 %collective-permute-start.33 = (bf16[512,512]{1,0:T(8,128)(2,1)}, bf16[512,512]{1,0:T(8,128)(2,1)}, u32[]{:S(2)}, u32[]{:S(2)}) collective-permute-start(bf16[512,512]{1,0:T(8,128)(2,1)} %pad_maximum_fusion.2.refs_8_), channel_id=1, source_target_pairs={{0,8},{8,0},{16,24},{24,16},{1,9},{9,1},{17,25},{25,17},{2,10},{10... | collective-permute-start | bytes 1572872 | tf_op jit(solution)/shard_map/ppermute | solution.py:181
  130.0 14.9 %copy-start.7 = (bf16[1024,256]{1,0:T(8,128)(2,1)S(1)}, bf16[1024,256]{1,0:T(8,128)(2,1)}, u32[]{:S(2)}) copy-start(bf16[1024,256]{1,0:T(8,128)(2,1)} %copy-done.6) | copy-start | bytes 1572868
  130.0 15.9 %copy-start.12 = (bf16[1024,256]{1,0:T(8,128)(2,1)S(1)}, bf16[1024,256]{1,0:T(8,128)(2,1)}, u32[]{:S(2)}) copy-start(bf16[1024,256]{1,0:T(8,128)(2,1)} %get-tuple-element.235) | copy-start | bytes 1572868
  130.0 14.9 %collective-permute-start.31 = (bf16[1024,256]{1,0:T(8,128)(2,1)S(1)}, bf16[1024,256]{1,0:T(8,128)(2,1)S(1)}, u32[]{:S(2)}, u32[]{:S(2)}) collective-permute-start(bf16[1024,256]{1,0:T(8,128)(2,1)S(1)} %broadcast_select_fusion.12), channel_id=1, source_target_pairs={{0,2},{1,3},{2,0},{3,1},{4,6},{5,7},{6,4},{7,5},{8,10},{9,11},{10,... | collective-permute-start | bytes 1572872 | tf_op jit(solution)/shard_map/ppermute | solution.py:191
  132.7 14.1 %collective-permute-start.37 = (bf16[1024,256]{1,0:T(8,128)(2,1)S(1)}, bf16[1024,256]{1,0:T(8,128)(2,1)S(1)}, u32[]{:S(2)}, u32[]{:S(2)}) collective-permute-start(bf16[1024,256]{1,0:T(8,128)(2,1)S(1)} %add_convert_fusion.10), channel_id=1, source_target_pairs={{2,4},{3,5},{4,2},{5,3},{10,12},{11,13},{12,10},{13,11},{18,20},{1... | collective-permute-start | bytes 1572872 | tf_op jit(solution)/shard_map/ppermute | solution.py:191
  136.5 10.4 %collective-permute-start.36 = (bf16[512,512]{1,0:T(8,128)(2,1)}, bf16[512,512]{1,0:T(8,128)(2,1)}, u32[]{:S(2)}, u32[]{:S(2)}) collective-permute-start(bf16[512,512]{1,0:T(8,128)(2,1)} %pad_maximum_fusion.2.refs_8_), channel_id=1, source_target_pairs={{0,24},{8,16},{16,8},{24,0},{1,25},{9,17},{17,9},{25,1},{2,26},{10... | collective-permute-start | bytes 1572872 | tf_op jit(solution)/shard_map/ppermute | solution.py:181
  137.7 17.7 %collective-permute-start.35 = (bf16[1024,256]{1,0:T(8,128)(2,1)}, bf16[1024,256]{1,0:T(8,128)(2,1)}, u32[]{:S(2)}, u32[]{:S(2)}) collective-permute-start(bf16[1024,256]{1,0:T(8,128)(2,1)} %broadcast_select_fusion.10), channel_id=1, source_target_pairs={{0,2},{1,3},{2,0},{3,1},{4,6},{5,7},{6,4},{7,5},{8,10},{9,11},{10,... | collective-permute-start | bytes 1572872 | tf_op jit(solution)/shard_map/ppermute | solution.py:191
  146.1 11.4 %collective-permute-start.39 = (bf16[1024,256]{1,0:T(8,128)(2,1)S(1)}, bf16[1024,256]{1,0:T(8,128)(2,1)S(1)}, u32[]{:S(2)}, u32[]{:S(2)}) collective-permute-start(bf16[1024,256]{1,0:T(8,128)(2,1)S(1)} %add_convert_fusion.8), channel_id=1, source_target_pairs={{2,4},{3,5},{4,2},{5,3},{10,12},{11,13},{12,10},{13,11},{18,20},{1... | collective-permute-start | bytes 1572872 | tf_op jit(solution)/shard_map/ppermute | solution.py:191
  152.8 16.3 %copy-start.13 = (bf16[1024,256]{1,0:T(8,128)(2,1)S(1)}, bf16[1024,256]{1,0:T(8,128)(2,1)}, u32[]{:S(2)}) copy-start(bf16[1024,256]{1,0:T(8,128)(2,1)} %get-tuple-element.251) | copy-start | bytes 1572868
  154.1 14.9 %collective-permute-start.38 = (bf16[1024,256]{1,0:T(8,128)(2,1)S(1)}, bf16[1024,256]{1,0:T(8,128)(2,1)S(1)}, u32[]{:S(2)}, u32[]{:S(2)}) collective-permute-start(bf16[1024,256]{1,0:T(8,128)(2,1)S(1)} %broadcast_select_fusion.8), channel_id=1, source_target_pairs={{0,2},{1,3},{2,0},{3,1},{4,6},{5,7},{6,4},{7,5},{8,10},{9,11},{10,... | collective-permute-start | bytes 1572872 | tf_op jit(solution)/shard_map/ppermute | solution.py:191
  156.6 13.5 %collective-permute-start.40 = (bf16[1024,256]{1,0:T(8,128)(2,1)S(1)}, bf16[1024,256]{1,0:T(8,128)(2,1)S(1)}, u32[]{:S(2)}, u32[]{:S(2)}) collective-permute-start(bf16[1024,256]{1,0:T(8,128)(2,1)S(1)} %add_convert_fusion.6), channel_id=1, source_target_pairs={{2,4},{3,5},{4,2},{5,3},{10,12},{11,13},{12,10},{13,11},{18,20},{1... | collective-permute-start | bytes 1572872 | tf_op jit(solution)/shard_map/ppermute | solution.py:191
  157.7 14.0 %copy-start.25 = (f32[2,4,112]{2,0,1:T(2,128)S(1)}, f32[2,4,112]{2,0,1:T(2,128)}, u32[]{:S(2)}) copy-start(f32[2,4,112]{2,0,1:T(2,128)} %select_reduce_fusion) | copy-start | bytes 10756
  157.7 22.6 %collective-permute-start.41 = (bf16[1024,256]{1,0:T(8,128)(2,1)S(1)}, bf16[1024,256]{1,0:T(8,128)(2,1)S(1)}, u32[]{:S(2)}, u32[]{:S(2)}) collective-permute-start(bf16[1024,256]{1,0:T(8,128)(2,1)S(1)} %broadcast_select_fusion.6), channel_id=1, source_target_pairs={{0,2},{1,3},{2,0},{3,1},{4,6},{5,7},{6,4},{7,5},{8,10},{9,11},{10,... | collective-permute-start | bytes 1572872 | tf_op jit(solution)/shard_map/ppermute | solution.py:191
  169.2 13.1 %collective-permute-start.42 = (bf16[1024,256]{1,0:T(8,128)(2,1)S(1)}, bf16[1024,256]{1,0:T(8,128)(2,1)S(1)}, u32[]{:S(2)}, u32[]{:S(2)}) collective-permute-start(bf16[1024,256]{1,0:T(8,128)(2,1)S(1)} %add_convert_fusion.4), channel_id=1, source_target_pairs={{2,4},{3,5},{4,2},{5,3},{10,12},{11,13},{12,10},{13,11},{18,20},{1... | collective-permute-start | bytes 1572872 | tf_op jit(solution)/shard_map/ppermute | solution.py:191
  170.2 21.3 %collective-permute-start.43 = (bf16[1024,256]{1,0:T(8,128)(2,1)S(1)}, bf16[1024,256]{1,0:T(8,128)(2,1)S(1)}, u32[]{:S(2)}, u32[]{:S(2)}) collective-permute-start(bf16[1024,256]{1,0:T(8,128)(2,1)S(1)} %add_convert_fusion.3), channel_id=1, source_target_pairs={{2,0},{3,1},{4,6},{5,7},{10,8},{11,9},{12,14},{13,15},{18,16},{19,... | collective-permute-start | bytes 1572872 | tf_op jit(solution)/shard_map/ppermute | solution.py:191
  181.1 2.6 %collective-permute-start.44 = (bf16[1024,256]{1,0:T(8,128)(2,1)S(1)}, bf16[1024,256]{1,0:T(8,128)(2,1)S(1)}, u32[]{:S(2)}, u32[]{:S(2)}) collective-permute-start(bf16[1024,256]{1,0:T(8,128)(2,1)S(1)} %add_convert_fusion.2), channel_id=1, source_target_pairs={{2,4},{3,5},{4,2},{5,3},{10,12},{11,13},{12,10},{13,11},{18,20},{1... | collective-permute-start | bytes 1572872 | tf_op jit(solution)/shard_map/ppermute | solution.py:191
  182.4 25.7 %collective-permute-start.45 = (bf16[1024,256]{1,0:T(8,128)(2,1)S(1)}, bf16[1024,256]{1,0:T(8,128)(2,1)S(1)}, u32[]{:S(2)}, u32[]{:S(2)}) collective-permute-start(bf16[1024,256]{1,0:T(8,128)(2,1)S(1)} %add_convert_fusion.1), channel_id=1, source_target_pairs={{2,0},{3,1},{4,6},{5,7},{10,8},{11,9},{12,14},{13,15},{18,16},{19,... | collective-permute-start | bytes 1572872 | tf_op jit(solution)/shard_map/ppermute | solution.py:191
  183.8 24.2 %collective-permute-start.46 = (bf16[1024,256]{1,0:T(8,128)(2,1)S(1)}, bf16[1024,256]{1,0:T(8,128)(2,1)S(1)}, u32[]{:S(2)}, u32[]{:S(2)}) collective-permute-start(bf16[1024,256]{1,0:T(8,128)(2,1)S(1)} %add_convert_fusion), channel_id=1, source_target_pairs={{2,0},{3,1},{4,6},{5,7},{10,8},{11,9},{12,14},{13,15},{18,16},{19,... | collective-permute-start | bytes 1572872 | tf_op jit(solution)/shard_map/ppermute | solution.py:191
  192.3 16.7 %collective-permute-start.47 = (bf16[448,1536]{1,0:T(8,128)(2,1)S(1)}, bf16[448,1536]{1,0:T(8,128)(2,1)S(1)}, u32[]{:S(2)}, u32[]{:S(2)}) collective-permute-start(bf16[448,1536]{1,0:T(8,128)(2,1)S(1)} %constant_dynamic-update-slice_fusion), channel_id=1, source_target_pairs={{0,1},{1,0},{2,3},{3,2},{4,5},{5,4},{6,7},{7,6},{8,9},{9,8},{10,11... | collective-permute-start | bytes 4128776 | tf_op jit(solution)/shard_map/ppermute | solution.py:178
  208.9 1.9 collective-permute-start.48
  (21 other events, 124.8 us)

commit v17 on v13

--- a/solution.py
+++ b/solution.py
@@ -78,7 +78,7 @@
     channels, length = out_grad.shape
     block = min(128, channels)
     window = length // ctx_count
-    tile = min(512, window)
+    tile = min(1024, window)
     whole = pl.BlockSpec((block, length), lambda step, at_ctx: (step, 0))
     row = pl.BlockSpec((1, block), lambda step, at_ctx: (0, step))
     return pl.pallas_call(
@@ -124,7 +124,7 @@
 def matmul(lefts, rights, resid, place, widths):
     tokens, depth = lefts[0].shape
     width = rights[0].shape[1]
-    tile = 2 * resid.shape[0]
+    tile = min(tokens, 4 * resid.shape[0])
     flops = 2 * tokens * depth * len(lefts) * width
     moved = 2 * (tokens * depth * len(lefts) + depth * len(lefts) * width + tokens * width)
     return pl.pallas_call(

time: 212 us -> 213 us (level)
  transfers between devices with their start and end apart: 49 -> 49, of which waited for: 20 -> 20; matrix products, arithmetic and copies ran while one was open for 17% -> 16% of each run, Pallas kernels for 18% -> 19%
where the time goes in v17:
time: 213 us; the launch traced here: 212 us
  waiting for transfers between devices  68.5 us (32%)
  starting transfers between devices  60.8 us (29%)
  Pallas kernels  40.2 us (19%)
  other arithmetic  22.4 us (11%)
  local copies, waits for them, and re-layouts  16.8 us (8%)
  matrix products  2.33 us (1%)
    ppermute x19, waiting for transfers between devices, swap_chips(): return lax.ppermute(array, 'exp', sorted(pairs))  49.4 us
    ppermute x19, starting transfers between devices, swap_chips(): return lax.ppermute(array, 'exp', sorted(pairs))  32.2 us
    pallas_call x5, Pallas kernels, matmul(): pl.pallas_call(functools.partial(matmul_kernel, len(lefts), len(rights)),...  27.6 us
    ppermute x18, starting transfers between devices, to_ctx(): lax.ppermute(array, 'ctx', [(place, place ^ offset) for place in range(ct...  22.2 us
    ppermute x18, waiting for transfers between devices, to_ctx(): lax.ppermute(array, 'ctx', [(place, place ^ offset) for place in range(ct...  13.7 us
    pallas_call x1, Pallas kernels, conv_grad(): pl.pallas_call(functools.partial(conv_kernel, tile), grid_spec=pltpu.Pref...  12.6 us
    select_n x5, other arithmetic, on_device(): jnp.where(distance == hop, sums[hop][inward], ready[hop + 1][outward])  7.41 us
    unnamed x110, local copies, waits for them, and re-layouts  5.42 us
  transfers between devices with their start and end apart: 49, of which 20 were waited for; matrix products, arithmetic and copies ran while one was open for 16% of the time, Pallas kernels for 19%

profile of v17, /device:TPU:0, one launch (start us, length us, event | category | flops | bytes accessed | tf_op | source)
XLA Modules:
  0.0 212.3 jit_solution(7461801153908438905)
XLA Ops:
  0.0 1.0 constant_dynamic-slice_fusion.8
  1.5 1.0 collective-permute-done
  2.5 3.9 %collective-permute-start.3 = (bf16[512,256]{1,0:T(8,128)(2,1)S(1)}, bf16[512,256]{1,0:T(8,128)(2,1)S(1)}, u32[]{:S(2)}, u32[]{:S(2)}) collective-permute-start(bf16[512,256]{1,0:T(8,128)(2,1)S(1)} %pad_maximum_fusion.4.refs_8_), channel_id=1, source_target_pairs={{0,24},{8,16},{16,8},{24,0},{1,25},{9,17},{17,9},{25,1},{2,26},{10... | collective-permute-start | bytes 786440 | tf_op jit(solution)/shard_map/ppermute | solution.py:181
  7.0 12.6 %conv_grad.1 = (bf16[1024,256]{1,0:T(8,128)(2,1)}, bf16[1024,256]{1,0:T(8,128)(2,1)}, bf16[1024,256]{1,0:T(8,128)(2,1)}, bf16[1024,256]{1,0:T(8,128)(2,1)}) custom-call(s32[1]{0:T(128)} %bitcast.1.at_ctx, bf16[256,4096]{1,0:T(8,128)(2,1)} %out_grad.1, bf16[256,4096]{1,0:T(8,128)(2,1)} %gate_in.1, bf16[256,4096]{1,0:T(8,128)(2,1)} %conv_in.1, ...), custom_call_target="tpu_custom_call" | custom-call | flops 41943040 | bytes 10485760 | tf_op jit(solution)/shard_map/conv_grad/pallas_call | solution.py:84
  20.6 1.9 collective-permute-start.5
  22.5 1.5 collective-permute-start.6
  24.2 2.2 %constant_dynamic-slice_fusion.5 = bf16[256,1792]{1,0:T(8,128)(2,1)} fusion(bf16[256,4096]{1,0:T(8,128)(2,1)} %param.18, s32[]{:T(128)S(6)} %select_n.141), kind=kLoop, calls=%fused_computation.106 | loop fusion | bytes 1835012 | tf_op jit(solution)/shard_map/dynamic_slice | solution.py:194
  26.9 1.1 constant_dynamic-slice_fusion.4
  28.0 2.0 collective-permute-start.14
  30.1 2.0 constant_dynamic-slice_fusion.6
  32.1 2.7 %collective-permute-start.15 = (f32[4,4,128]{2,1,0:T(4,128)S(1)}, f32[4,4,128]{2,1,0:T(4,128)S(1)}, u32[]{:S(2)}, u32[]{:S(2)}) collective-permute-start(f32[4,4,128]{2,1,0:T(4,128)S(1)} %pad_maximum_fusion.7), channel_id=1, source_target_pairs={{0,4},{1,5},{2,6},{3,7},{4,0},{5,1},{6,2},{7,3},{8,12},{9,13},{10,... | collective-permute-start | bytes 24584 | tf_op jit(solution)/shard_map/ppermute | solution.py:232
  34.8 0.9 constant_dynamic-slice_fusion.2
  35.7 1.0 collective-permute-done.15
  39.7 2.1 maximum_select_fusion
  41.8 0.9 slice.140
  42.7 2.5 %collective-permute-start.11 = (bf16[512,256]{1,0:T(8,128)(2,1)S(1)}, bf16[512,256]{1,0:T(8,128)(2,1)S(1)}, u32[]{:S(2)}, u32[]{:S(2)}) collective-permute-start(bf16[512,256]{1,0:T(8,128)(2,1)S(1)} %pad_maximum_fusion.5.refs_8_), channel_id=1, source_target_pairs={{0,24},{8,16},{16,8},{24,0},{1,25},{9,17},{17,9},{25,1},{2,26},{10... | collective-permute-start | bytes 786440 | tf_op jit(solution)/shard_map/ppermute | solution.py:181
  45.8 1.2 fusion.24
  48.4 1.0 pad_maximum_fusion
  49.4 3.5 %collective-permute-done.6.refs_4_ = bf16[1024,256]{1,0:T(8,128)(2,1)S(1)} collective-permute-done((bf16[1024,256]{1,0:T(8,128)(2,1)}, bf16[1024,256]{1,0:T(8,128)(2,1)S(1)}, u32[]{:S(2)}, u32[]{:S(2)}) %collective-permute-start.6) | collective-permute-done | bytes 524320 | tf_op jit(solution)/shard_map/ppermute | solution.py:181
  53.3 5.3 %collective-permute-done.10.refs_10_ = bf16[512,256]{1,0:T(8,128)(2,1)S(1)} collective-permute-done((bf16[512,256]{1,0:T(8,128)(2,1)S(1)}, bf16[512,256]{1,0:T(8,128)(2,1)S(1)}, u32[]{:S(2)}, u32[]{:S(2)}) %collective-permute-start.10) | collective-permute-done | bytes 262176 | tf_op jit(solution)/shard_map/ppermute | solution.py:181
  61.5 1.0 collective-permute-done.18.refs_7_
  62.5 1.5 collective-permute-start.20
  64.6 4.5 %partial_product.5 = bf16[1024,256]{1,0:T(8,128)(2,1)} custom-call(s32[1]{0:T(128)} %bitcast.place, bf16[1024,256]{1,0:T(8,128)(2,1)} %get-tuple-element.147.refs_0_, bf16[1024,256]{1,0:T(8,128)(2,1)} %copy-done.1, bf16[1024,256]{1,0:T(8,128)(2,1)} %copy-done.2, bf16[1024,256]{1,0:T(8,128)(2,1)} %copy-done.4, bf16[1024,256]{1,0:T(8,128)(2,1)} %copy-done.3, ...), custom_call_target="tpu_custom_call" | custom-call | flops 1073741824 | bytes 5767168 | tf_op jit(solution)/shard_map/partial_product/pallas_call | solution.py:130
  69.1 4.4 %collective-permute-start.22 = (bf16[1024,256]{1,0:T(8,128)(2,1)}, bf16[1024,256]{1,0:T(8,128)(2,1)}, u32[]{:S(2)}, u32[]{:S(2)}) collective-permute-start(bf16[1024,256]{1,0:T(8,128)(2,1)} %partial_product.5), channel_id=1, source_target_pairs={{0,2},{1,3},{6,4},{7,5},{8,10},{9,11},{14,12},{15,13},{16,18},{17,... | collective-permute-start | bytes 1572872 | tf_op jit(solution)/shard_map/ppermute | solution.py:191
  73.5 1.4 collective-permute-start.21
  74.9 4.5 %partial_product.6 = bf16[1024,256]{1,0:T(8,128)(2,1)} custom-call(s32[1]{0:T(128)} %bitcast.place, bf16[1024,256]{1,0:T(8,128)(2,1)} %get-tuple-element.147.refs_0_, bf16[1024,256]{1,0:T(8,128)(2,1)} %copy-done.1, bf16[1024,256]{1,0:T(8,128)(2,1)} %copy-done.2, bf16[1024,256]{1,0:T(8,128)(2,1)} %copy-done.4, bf16[1024,256]{1,0:T(8,128)(2,1)} %copy-done.3, ...), custom_call_target="tpu_custom_call" | custom-call | flops 1073741824 | bytes 5767168 | tf_op jit(solution)/shard_map/partial_product/pallas_call | solution.py:130
  79.5 1.3 collective-permute-start.24
  80.8 4.6 %collective-permute-done.22 = bf16[1024,256]{1,0:T(8,128)(2,1)} collective-permute-done((bf16[1024,256]{1,0:T(8,128)(2,1)}, bf16[1024,256]{1,0:T(8,128)(2,1)}, u32[]{:S(2)}, u32[]{:S(2)}) %collective-permute-start.22) | collective-permute-done | bytes 524320 | tf_op jit(solution)/shard_map/ppermute | solution.py:191
  85.4 1.2 add_convert_fusion.15
  86.6 2.6 %collective-permute-done.21.refs_11_ = bf16[512,512]{1,0:T(8,128)(2,1)} collective-permute-done((bf16[512,512]{1,0:T(8,128)(2,1)}, bf16[512,512]{1,0:T(8,128)(2,1)}, u32[]{:S(2)}, u32[]{:S(2)}) %collective-permute-start.21) | collective-permute-done | bytes 524320 | tf_op jit(solution)/shard_map/ppermute | solution.py:181
  89.2 1.5 collective-permute-start.26
  91.9 0.9 fusion.22
  92.9 6.2 %partial_product.7 = (bf16[1024,256]{1,0:T(8,128)(2,1)}, bf16[1024,256]{1,0:T(8,128)(2,1)}) custom-call(s32[1]{0:T(128)} %bitcast.place, bf16[1024,256]{1,0:T(8,128)(2,1)} %get-tuple-element.147.refs_0_, bf16[1024,256]{1,0:T(8,128)(2,1)} %copy-done.1, bf16[1024,256]{1,0:T(8,128)(2,1)} %copy-done.2, bf16[1024,256]{1,0:T(8,128)(2,1)} %copy-done.4, ...), custom_call_target="tpu_custom_call" | custom-call | flops 2147483648 | bytes 7340032 | tf_op jit(solution)/shard_map/partial_product/pallas_call | solution.py:130
  99.1 6.4 %collective-permute-start.30 = (bf16[1024,256]{1,0:T(8,128)(2,1)}, bf16[1024,256]{1,0:T(8,128)(2,1)S(1)}, u32[]{:S(2)}, u32[]{:S(2)}) collective-permute-start(bf16[1024,256]{1,0:T(8,128)(2,1)} %get-tuple-element.202), channel_id=1, source_target_pairs={{0,2},{1,3},{6,4},{7,5},{8,10},{9,11},{14,12},{15,13},{16,18},{17,... | collective-permute-start | bytes 1572872 | tf_op jit(solution)/shard_map/ppermute | solution.py:191
  106.4 1.5 collective-permute-start.28
  107.9 2.0 broadcast_select_fusion.13
  110.0 8.2 %collective-permute-done.30 = bf16[1024,256]{1,0:T(8,128)(2,1)S(1)} collective-permute-done((bf16[1024,256]{1,0:T(8,128)(2,1)}, bf16[1024,256]{1,0:T(8,128)(2,1)S(1)}, u32[]{:S(2)}, u32[]{:S(2)}) %collective-permute-start.30) | collective-permute-done | bytes 524320 | tf_op jit(solution)/shard_map/ppermute | solution.py:191
  119.1 1.2 collective-permute-start.34
  121.1 6.2 %partial_product.8 = (bf16[1024,256]{1,0:T(8,128)(2,1)}, bf16[1024,256]{1,0:T(8,128)(2,1)}) custom-call(s32[1]{0:T(128)} %bitcast.place, bf16[1024,256]{1,0:T(8,128)(2,1)} %get-tuple-element.147.refs_0_, bf16[1024,256]{1,0:T(8,128)(2,1)} %copy-done.1, bf16[1024,256]{1,0:T(8,128)(2,1)} %copy-done.2, bf16[1024,256]{1,0:T(8,128)(2,1)} %copy-done.4, ...), custom_call_target="tpu_custom_call" | custom-call | flops 2147483648 | bytes 7340032 | tf_op jit(solution)/shard_map/partial_product/pallas_call | solution.py:130
  127.3 1.3 broadcast_select_fusion.12
  128.6 3.0 %collective-permute-start.31 = (bf16[1024,256]{1,0:T(8,128)(2,1)S(1)}, bf16[1024,256]{1,0:T(8,128)(2,1)S(1)}, u32[]{:S(2)}, u32[]{:S(2)}) collective-permute-start(bf16[1024,256]{1,0:T(8,128)(2,1)S(1)} %broadcast_select_fusion.12), channel_id=1, source_target_pairs={{0,2},{1,3},{2,0},{3,1},{4,6},{5,7},{6,4},{7,5},{8,10},{9,11},{10,... | collective-permute-start | bytes 1572872 | tf_op jit(solution)/shard_map/ppermute | solution.py:191
  131.7 1.2 broadcast_select_fusion.11
  133.2 1.2 add_convert_fusion.10
  136.2 1.0 broadcast_select_fusion.10
  137.2 1.5 collective-permute-start.36
  138.7 2.0 collective-permute-start.35
  140.7 2.1 collective-permute-done.31
  143.4 1.5 collective-permute-start.39
  145.8 1.7 collective-permute-done.36.refs_11_
  148.3 6.1 %partial_product.9 = (bf16[1024,256]{1,0:T(8,128)(2,1)}, bf16[1024,256]{1,0:T(8,128)(2,1)}) custom-call(s32[1]{0:T(128)} %bitcast.place, bf16[1024,256]{1,0:T(8,128)(2,1)} %get-tuple-element.147.refs_0_, bf16[1024,256]{1,0:T(8,128)(2,1)} %copy-done.1, bf16[1024,256]{1,0:T(8,128)(2,1)} %copy-done.2, bf16[1024,256]{1,0:T(8,128)(2,1)} %copy-done.4, ...), custom_call_target="tpu_custom_call" | custom-call | flops 2147483648 | bytes 7340032 | tf_op jit(solution)/shard_map/partial_product/pallas_call | solution.py:130
  154.4 1.3 broadcast_select_fusion.8
  155.7 1.8 collective-permute-start.38
  158.7 1.8 broadcast_select_fusion.6
  160.8 2.8 %collective-permute-start.40 = (bf16[1024,256]{1,0:T(8,128)(2,1)S(1)}, bf16[1024,256]{1,0:T(8,128)(2,1)S(1)}, u32[]{:S(2)}, u32[]{:S(2)}) collective-permute-start(bf16[1024,256]{1,0:T(8,128)(2,1)S(1)} %broadcast_select_fusion.6), channel_id=1, source_target_pairs={{0,2},{1,3},{2,0},{3,1},{4,6},{5,7},{6,4},{7,5},{8,10},{9,11},{10,... | collective-permute-start | bytes 1572872 | tf_op jit(solution)/shard_map/ppermute | solution.py:191
  163.7 6.8 %collective-permute-done.38 = bf16[1024,256]{1,0:T(8,128)(2,1)S(1)} collective-permute-done((bf16[1024,256]{1,0:T(8,128)(2,1)S(1)}, bf16[1024,256]{1,0:T(8,128)(2,1)S(1)}, u32[]{:S(2)}, u32[]{:S(2)}) %collective-permute-start.38) | collective-permute-done | bytes 524320 | tf_op jit(solution)/shard_map/ppermute | solution.py:191
  171.7 1.3 collective-permute-start.42
  173.3 8.4 %collective-permute-done.40 = bf16[1024,256]{1,0:T(8,128)(2,1)S(1)} collective-permute-done((bf16[1024,256]{1,0:T(8,128)(2,1)S(1)}, bf16[1024,256]{1,0:T(8,128)(2,1)S(1)}, u32[]{:S(2)}, u32[]{:S(2)}) %collective-permute-start.40) | collective-permute-done | bytes 524320 | tf_op jit(solution)/shard_map/ppermute | solution.py:191
  181.8 1.2 broadcast_select_fusion.4
  184.4 1.3 collective-permute-start.44
  185.9 1.3 collective-permute-start.46
  187.2 5.8 %collective-permute-done.42 = bf16[1024,256]{1,0:T(8,128)(2,1)S(1)} collective-permute-done((bf16[1024,256]{1,0:T(8,128)(2,1)S(1)}, bf16[1024,256]{1,0:T(8,128)(2,1)S(1)}, u32[]{:S(2)}, u32[]{:S(2)}) %collective-permute-start.42) | collective-permute-done | bytes 524320 | tf_op jit(solution)/shard_map/ppermute | solution.py:191
  193.5 13.4 %collective-permute-done.46 = bf16[1024,256]{1,0:T(8,128)(2,1)S(1)} collective-permute-done((bf16[1024,256]{1,0:T(8,128)(2,1)S(1)}, bf16[1024,256]{1,0:T(8,128)(2,1)S(1)}, u32[]{:S(2)}, u32[]{:S(2)}) %collective-permute-start.46) | collective-permute-done | bytes 524320 | tf_op jit(solution)/shard_map/ppermute | solution.py:191
  208.3 1.4 collective-permute-done.48
  210.0 2.2 %broadcast_select_fusion = bf16[1,448,4096]{2,1,0:T(8,128)(2,1)} fusion(bf16[1,448,4096]{2,1,0:T(8,128)(2,1)S(1)} %get-tuple-element.275, bf16[1,448,4096]{2,1,0:T(8,128)(2,1)S(1)} %constant_dynamic-update-slice_fusion.14, pred[]{:T(512)S(6)} %eq.30), kind=kLoop, calls=%fused_computation | loop fusion | flops 1835008 | bytes 11010049 | tf_op jit(solution)/shard_map/jit(_where)/select_n | solution.py:368
  (234 shorter events, 25.8 us)
Async XLA Ops:
  1.0 1.5 collective-permute-start
  2.5 17.1 %copy-start.20 = (bf16[512,256]{1,0:T(8,128)(2,1)}, bf16[512,256]{1,0:T(8,128)(2,1)S(1)}, u32[]{:S(2)}) copy-start(bf16[512,256]{1,0:T(8,128)(2,1)S(1)} %pad_maximum_fusion.4.refs_8_) | copy-start | bytes 786436
  2.5 17.1 %collective-permute-start.3 = (bf16[512,256]{1,0:T(8,128)(2,1)S(1)}, bf16[512,256]{1,0:T(8,128)(2,1)S(1)}, u32[]{:S(2)}, u32[]{:S(2)}) collective-permute-start(bf16[512,256]{1,0:T(8,128)(2,1)S(1)} %pad_maximum_fusion.4.refs_8_), channel_id=1, source_target_pairs={{0,24},{8,16},{16,8},{24,0},{1,25},{9,17},{17,9},{25,1},{2,26},{10... | collective-permute-start | bytes 786440 | tf_op jit(solution)/shard_map/ppermute | solution.py:181
  6.4 13.3 %collective-permute-start.2 = (bf16[512,256]{1,0:T(8,128)(2,1)S(1)}, bf16[512,256]{1,0:T(8,128)(2,1)S(1)}, u32[]{:S(2)}, u32[]{:S(2)}) collective-permute-start(bf16[512,256]{1,0:T(8,128)(2,1)S(1)} %pad_maximum_fusion.4.refs_8_), channel_id=1, source_target_pairs={{0,16},{8,24},{16,0},{24,8},{1,17},{9,25},{17,1},{25,9},{2,18},{10... | collective-permute-start | bytes 786440 | tf_op jit(solution)/shard_map/ppermute | solution.py:181
  6.9 12.8 %collective-permute-start.1 = (bf16[512,256]{1,0:T(8,128)(2,1)S(1)}, bf16[512,256]{1,0:T(8,128)(2,1)S(1)}, u32[]{:S(2)}, u32[]{:S(2)}) collective-permute-start(bf16[512,256]{1,0:T(8,128)(2,1)S(1)} %pad_maximum_fusion.4.refs_8_), channel_id=1, source_target_pairs={{0,8},{8,0},{16,24},{24,16},{1,9},{9,1},{17,25},{25,17},{2,10},{10... | collective-permute-start | bytes 786440 | tf_op jit(solution)/shard_map/ppermute | solution.py:181
  7.0 17.1 %copy-start.39 = (s32[128,2]{0,1:T(2,128)S(1)}, s32[128,2]{0,1:T(2,128)}, u32[]{:S(2)}) copy-start(s32[128,2]{0,1:T(2,128)} %param.20) | copy-start | bytes 3076
  7.0 17.1 %copy-start.40 = (f32[128,2]{0,1:T(2,128)S(1)}, f32[128,2]{0,1:T(2,128)}, u32[]{:S(2)}) copy-start(f32[128,2]{0,1:T(2,128)} %param.21) | copy-start | bytes 3076
  7.0 19.8 %copy-start.23 = (bf16[128,4096]{1,0:T(8,128)(2,1)S(1)}, bf16[128,4096]{1,0:T(8,128)(2,1)}, u32[]{:S(2)}) copy-start(bf16[128,4096]{1,0:T(8,128)(2,1)} %param.19) | copy-start | bytes 3145732
  19.7 18.1 %copy-start.31 = (bf16[512,256]{1,0:T(8,128)(2,1)}, bf16[512,256]{1,0:T(8,128)(2,1)S(1)}, u32[]{:S(2)}) copy-start(bf16[512,256]{1,0:T(8,128)(2,1)S(1)} %collective-permute-done.3.refs_11_) | copy-start | bytes 786436
  19.7 4.4 %collective-permute-start.4 = (bf16[1024,256]{1,0:T(8,128)(2,1)}, bf16[1024,256]{1,0:T(8,128)(2,1)S(1)}, u32[]{:S(2)}, u32[]{:S(2)}) collective-permute-start(bf16[1024,256]{1,0:T(8,128)(2,1)} %get-tuple-element.147.refs_0_), channel_id=1, source_target_pairs={{0,1},{1,0},{2,3},{3,2},{4,5},{5,4},{6,7},{7,6},{8,9},{9,8},{10,11... | collective-permute-start | bytes 1572872 | tf_op jit(solution)/shard_map/ppermute | solution.py:178
  20.6 26.3 %collective-permute-start.5 = (bf16[1024,256]{1,0:T(8,128)(2,1)}, bf16[1024,256]{1,0:T(8,128)(2,1)S(1)}, u32[]{:S(2)}, u32[]{:S(2)}) collective-permute-start(bf16[1024,256]{1,0:T(8,128)(2,1)} %get-tuple-element.137), channel_id=1, source_target_pairs={{0,8},{8,0},{16,24},{24,16},{1,9},{9,1},{17,25},{25,17},{2,10},{10... | collective-permute-start | bytes 1572872 | tf_op jit(solution)/shard_map/ppermute | solution.py:181
  22.5 30.4 %collective-permute-start.6 = (bf16[1024,256]{1,0:T(8,128)(2,1)}, bf16[1024,256]{1,0:T(8,128)(2,1)S(1)}, u32[]{:S(2)}, u32[]{:S(2)}) collective-permute-start(bf16[1024,256]{1,0:T(8,128)(2,1)} %get-tuple-element.138), channel_id=1, source_target_pairs={{0,16},{8,24},{16,0},{24,8},{1,17},{9,25},{17,1},{25,9},{2,18},{10... | collective-permute-start | bytes 1572872 | tf_op jit(solution)/shard_map/ppermute | solution.py:181
  24.0 28.9 %collective-permute-start.7 = (bf16[1024,256]{1,0:T(8,128)(2,1)}, bf16[1024,256]{1,0:T(8,128)(2,1)}, u32[]{:S(2)}, u32[]{:S(2)}) collective-permute-start(bf16[1024,256]{1,0:T(8,128)(2,1)} %get-tuple-element.139), channel_id=1, source_target_pairs={{0,24},{8,16},{16,8},{24,0},{1,25},{9,17},{17,9},{25,1},{2,26},{10... | collective-permute-start | bytes 1572872 | tf_op jit(solution)/shard_map/ppermute | solution.py:181
  24.1 17.7 %copy-start.1 = (bf16[1024,256]{1,0:T(8,128)(2,1)}, bf16[1024,256]{1,0:T(8,128)(2,1)S(1)}, u32[]{:S(2)}) copy-start(bf16[1024,256]{1,0:T(8,128)(2,1)S(1)} %collective-permute-done.4.refs_1_) | copy-start | bytes 1572868
  24.1 3.9 %collective-permute-start.13 = (f32[1,4,128]{2,1,0:T(4,128)S(1)}, f32[1,4,128]{2,1,0:T(4,128)S(1)}, u32[]{:S(2)}, u32[]{:S(2)}) collective-permute-start(f32[1,4,128]{2,1,0:T(4,128)S(1)} %maximum_bitcast_fusion), channel_id=1, source_target_pairs={{0,1},{1,0},{2,3},{3,2},{4,5},{5,4},{6,7},{7,6},{8,9},{9,8},{10,11... | collective-permute-start | bytes 6152 | tf_op jit(solution)/shard_map/ppermute | solution.py:232
  26.5 15.3 %collective-permute-start.8 = (bf16[256,1792]{1,0:T(8,128)(2,1)}, bf16[256,1792]{1,0:T(8,128)(2,1)}, u32[]{:S(2)}, u32[]{:S(2)}) collective-permute-start(bf16[256,1792]{1,0:T(8,128)(2,1)} %constant_dynamic-slice_fusion.5), channel_id=1, source_target_pairs={{0,1},{1,0},{2,3},{3,2},{4,5},{5,4},{6,7},{7,6},{8,9},{9,8},{10,11... | collective-permute-start | bytes 2752520 | tf_op jit(solution)/shard_map/ppermute | solution.py:178
  28.0 4.1 %collective-permute-start.14 = (f32[2,4,128]{2,1,0:T(4,128)S(1)}, f32[2,4,128]{2,1,0:T(4,128)S(1)}, u32[]{:S(2)}, u32[]{:S(2)}) collective-permute-start(f32[2,4,128]{2,1,0:T(4,128)S(1)} %pad_maximum_fusion.8), channel_id=1, source_target_pairs={{0,2},{1,3},{2,0},{3,1},{4,6},{5,7},{6,4},{7,5},{8,10},{9,11},{10,... | collective-permute-start | bytes 12296 | tf_op jit(solution)/shard_map/ppermute | solution.py:232
  32.1 4.6 %collective-permute-start.15 = (f32[4,4,128]{2,1,0:T(4,128)S(1)}, f32[4,4,128]{2,1,0:T(4,128)S(1)}, u32[]{:S(2)}, u32[]{:S(2)}) collective-permute-start(f32[4,4,128]{2,1,0:T(4,128)S(1)} %pad_maximum_fusion.7), channel_id=1, source_target_pairs={{0,4},{1,5},{2,6},{3,7},{4,0},{5,1},{6,2},{7,3},{8,12},{9,13},{10,... | collective-permute-start | bytes 24584 | tf_op jit(solution)/shard_map/ppermute | solution.py:232
  36.7 2.1 collective-permute-start.12
  37.7 10.7 %copy-start.25 = (bf16[256,512]{1,0:T(8,128)(2,1)S(1)}, bf16[256,512]{1,0:T(8,128)(2,1)}, u32[]{:S(2)}) copy-start(bf16[256,512]{1,0:T(8,128)(2,1)} %get-tuple-element.259) | copy-start | bytes 786436
  42.7 26.4 %copy-start.21 = (bf16[512,256]{1,0:T(8,128)(2,1)}, bf16[512,256]{1,0:T(8,128)(2,1)S(1)}, u32[]{:S(2)}) copy-start(bf16[512,256]{1,0:T(8,128)(2,1)S(1)} %pad_maximum_fusion.5.refs_8_) | copy-start | bytes 786436
  42.7 10.6 %collective-permute-start.11 = (bf16[512,256]{1,0:T(8,128)(2,1)S(1)}, bf16[512,256]{1,0:T(8,128)(2,1)S(1)}, u32[]{:S(2)}, u32[]{:S(2)}) collective-permute-start(bf16[512,256]{1,0:T(8,128)(2,1)S(1)} %pad_maximum_fusion.5.refs_8_), channel_id=1, source_target_pairs={{0,24},{8,16},{16,8},{24,0},{1,25},{9,17},{17,9},{25,1},{2,26},{10... | collective-permute-start | bytes 786440 | tf_op jit(solution)/shard_map/ppermute | solution.py:181
  45.3 13.4 %collective-permute-start.10 = (bf16[512,256]{1,0:T(8,128)(2,1)S(1)}, bf16[512,256]{1,0:T(8,128)(2,1)S(1)}, u32[]{:S(2)}, u32[]{:S(2)}) collective-permute-start(bf16[512,256]{1,0:T(8,128)(2,1)S(1)} %pad_maximum_fusion.5.refs_8_), channel_id=1, source_target_pairs={{0,16},{8,24},{16,0},{24,8},{1,17},{9,25},{17,1},{25,9},{2,18},{10... | collective-permute-start | bytes 786440 | tf_op jit(solution)/shard_map/ppermute | solution.py:181
  47.0 17.6 %copy-start.2 = (bf16[1024,256]{1,0:T(8,128)(2,1)}, bf16[1024,256]{1,0:T(8,128)(2,1)S(1)}, u32[]{:S(2)}) copy-start(bf16[1024,256]{1,0:T(8,128)(2,1)S(1)} %collective-permute-done.5.refs_2_) | copy-start | bytes 1572868
  47.0 11.7 %collective-permute-start.9 = (bf16[512,256]{1,0:T(8,128)(2,1)S(1)}, bf16[512,256]{1,0:T(8,128)(2,1)S(1)}, u32[]{:S(2)}, u32[]{:S(2)}) collective-permute-start(bf16[512,256]{1,0:T(8,128)(2,1)S(1)} %pad_maximum_fusion.5.refs_8_), channel_id=1, source_target_pairs={{0,8},{8,0},{16,24},{24,16},{1,9},{9,1},{17,25},{25,17},{2,10},{10... | collective-permute-start | bytes 786440 | tf_op jit(solution)/shard_map/ppermute | solution.py:181
  52.9 11.6 %copy-start.3 = (bf16[1024,256]{1,0:T(8,128)(2,1)}, bf16[1024,256]{1,0:T(8,128)(2,1)S(1)}, u32[]{:S(2)}) copy-start(bf16[1024,256]{1,0:T(8,128)(2,1)S(1)} %collective-permute-done.6.refs_4_) | copy-start | bytes 1572868
  58.7 2.0 collective-permute-start.16
  59.4 2.2 %collective-permute-start.17 = (bf16[1024,256]{1,0:T(8,128)(2,1)S(1)}, bf16[1024,256]{1,0:T(8,128)(2,1)}, u32[]{:S(2)}, u32[]{:S(2)}) collective-permute-start(bf16[1024,256]{1,0:T(8,128)(2,1)S(1)} %collective-permute-done.6.refs_4_), channel_id=1, source_target_pairs={{0,1},{1,0},{2,3},{3,2},{4,5},{5,4},{6,7},{7,6},{8,9},{9,8},{10,11... | collective-permute-start | bytes 1572872 | tf_op jit(solution)/shard_map/ppermute | solution.py:178
  59.5 3.0 %collective-permute-start.18 = (bf16[1024,256]{1,0:T(8,128)(2,1)}, bf16[1024,256]{1,0:T(8,128)(2,1)}, u32[]{:S(2)}, u32[]{:S(2)}) collective-permute-start(bf16[1024,256]{1,0:T(8,128)(2,1)} %collective-permute-done.7.refs_6_), channel_id=1, source_target_pairs={{0,1},{1,0},{2,3},{3,2},{4,5},{5,4},{6,7},{7,6},{8,9},{9,8},{10,11... | collective-permute-start | bytes 1572872 | tf_op jit(solution)/shard_map/ppermute | solution.py:178
  62.5 18.3 %collective-permute-start.20 = (bf16[512,512]{1,0:T(8,128)(2,1)}, bf16[512,512]{1,0:T(8,128)(2,1)}, u32[]{:S(2)}, u32[]{:S(2)}) collective-permute-start(bf16[512,512]{1,0:T(8,128)(2,1)} %get-tuple-element.186.refs_8_), channel_id=1, source_target_pairs={{0,16},{8,24},{16,0},{24,8},{1,17},{9,25},{17,1},{25,9},{2,18},{10... | collective-permute-start | bytes 1572872 | tf_op jit(solution)/shard_map/ppermute | solution.py:181
  64.0 16.8 %collective-permute-start.19 = (bf16[512,512]{1,0:T(8,128)(2,1)}, bf16[512,512]{1,0:T(8,128)(2,1)}, u32[]{:S(2)}, u32[]{:S(2)}) collective-permute-start(bf16[512,512]{1,0:T(8,128)(2,1)} %get-tuple-element.186.refs_8_), channel_id=1, source_target_pairs={{0,8},{8,0},{16,24},{24,16},{1,9},{9,1},{17,25},{25,17},{2,10},{10... | collective-permute-start | bytes 1572872 | tf_op jit(solution)/shard_map/ppermute | solution.py:181
  69.1 16.3 %copy-start.15 = (bf16[1024,256]{1,0:T(8,128)(2,1)S(1)}, bf16[1024,256]{1,0:T(8,128)(2,1)}, u32[]{:S(2)}) copy-start(bf16[1024,256]{1,0:T(8,128)(2,1)} %partial_product.5) | copy-start | bytes 1572868
  69.1 16.3 %collective-permute-start.22 = (bf16[1024,256]{1,0:T(8,128)(2,1)}, bf16[1024,256]{1,0:T(8,128)(2,1)}, u32[]{:S(2)}, u32[]{:S(2)}) collective-permute-start(bf16[1024,256]{1,0:T(8,128)(2,1)} %partial_product.5), channel_id=1, source_target_pairs={{0,2},{1,3},{6,4},{7,5},{8,10},{9,11},{14,12},{15,13},{16,18},{17,... | collective-permute-start | bytes 1572872 | tf_op jit(solution)/shard_map/ppermute | solution.py:191
  73.5 15.7 %collective-permute-start.21 = (bf16[512,512]{1,0:T(8,128)(2,1)}, bf16[512,512]{1,0:T(8,128)(2,1)}, u32[]{:S(2)}, u32[]{:S(2)}) collective-permute-start(bf16[512,512]{1,0:T(8,128)(2,1)} %get-tuple-element.186.refs_8_), channel_id=1, source_target_pairs={{0,24},{8,16},{16,8},{24,0},{1,25},{9,17},{17,9},{25,1},{2,26},{10... | collective-permute-start | bytes 1572872 | tf_op jit(solution)/shard_map/ppermute | solution.py:181
  79.5 26.1 %collective-permute-start.24 = (bf16[1024,256]{1,0:T(8,128)(2,1)}, bf16[1024,256]{1,0:T(8,128)(2,1)S(1)}, u32[]{:S(2)}, u32[]{:S(2)}) collective-permute-start(bf16[1024,256]{1,0:T(8,128)(2,1)} %partial_product.6), channel_id=1, source_target_pairs={{0,2},{1,3},{6,4},{7,5},{8,10},{9,11},{14,12},{15,13},{16,18},{17,... | collective-permute-start | bytes 1572872 | tf_op jit(solution)/shard_map/ppermute | solution.py:191
  89.2 17.2 %collective-permute-start.26 = (bf16[512,512]{1,0:T(8,128)(2,1)}, bf16[512,512]{1,0:T(8,128)(2,1)}, u32[]{:S(2)}, u32[]{:S(2)}) collective-permute-start(bf16[512,512]{1,0:T(8,128)(2,1)} %get-tuple-element.210.refs_8_), channel_id=1, source_target_pairs={{0,16},{8,24},{16,0},{24,8},{1,17},{9,25},{17,1},{25,9},{2,18},{10... | collective-permute-start | bytes 1572872 | tf_op jit(solution)/shard_map/ppermute | solution.py:181
  90.7 15.7 %collective-permute-start.25 = (bf16[512,512]{1,0:T(8,128)(2,1)}, bf16[512,512]{1,0:T(8,128)(2,1)}, u32[]{:S(2)}, u32[]{:S(2)}) collective-permute-start(bf16[512,512]{1,0:T(8,128)(2,1)} %get-tuple-element.210.refs_8_), channel_id=1, source_target_pairs={{0,8},{8,0},{16,24},{24,16},{1,9},{9,1},{17,25},{25,17},{2,10},{10... | collective-permute-start | bytes 1572872 | tf_op jit(solution)/shard_map/ppermute | solution.py:181
  91.2 15.1 %collective-permute-start.23 = (bf16[1024,256]{1,0:T(8,128)(2,1)S(1)}, bf16[1024,256]{1,0:T(8,128)(2,1)S(1)}, u32[]{:S(2)}, u32[]{:S(2)}) collective-permute-start(bf16[1024,256]{1,0:T(8,128)(2,1)S(1)} %add_convert_fusion.15), channel_id=1, source_target_pairs={{2,4},{3,5},{4,2},{5,3},{10,12},{11,13},{12,10},{13,11},{18,20},{1... | collective-permute-start | bytes 1572872 | tf_op jit(solution)/shard_map/ppermute | solution.py:191
  92.8 12.7 %copy-start.14 = (bf16[1024,256]{1,0:T(8,128)(2,1)S(1)}, bf16[1024,256]{1,0:T(8,128)(2,1)}, u32[]{:S(2)}) copy-start(bf16[1024,256]{1,0:T(8,128)(2,1)} %partial_product.6) | copy-start | bytes 1572868
  92.9 13.6 %copy-start.28 = (bf16[512,512]{1,0:T(8,128)(2,1)S(1)}, bf16[512,512]{1,0:T(8,128)(2,1)}, u32[]{:S(2)}) copy-start(bf16[512,512]{1,0:T(8,128)(2,1)} %get-tuple-element.210.refs_8_) | copy-start | bytes 1572868
  99.1 19.1 %copy-start.27 = (bf16[1024,256]{1,0:T(8,128)(2,1)S(1)}, bf16[1024,256]{1,0:T(8,128)(2,1)}, u32[]{:S(2)}) copy-start(bf16[1024,256]{1,0:T(8,128)(2,1)} %get-tuple-element.202) | copy-start | bytes 1572868
  99.1 19.1 %collective-permute-start.30 = (bf16[1024,256]{1,0:T(8,128)(2,1)}, bf16[1024,256]{1,0:T(8,128)(2,1)S(1)}, u32[]{:S(2)}, u32[]{:S(2)}) collective-permute-start(bf16[1024,256]{1,0:T(8,128)(2,1)} %get-tuple-element.202), channel_id=1, source_target_pairs={{0,2},{1,3},{6,4},{7,5},{8,10},{9,11},{14,12},{15,13},{16,18},{17,... | collective-permute-start | bytes 1572872 | tf_op jit(solution)/shard_map/ppermute | solution.py:191
  105.7 13.3 %collective-permute-start.29 = (bf16[1024,256]{1,0:T(8,128)(2,1)S(1)}, bf16[1024,256]{1,0:T(8,128)(2,1)S(1)}, u32[]{:S(2)}, u32[]{:S(2)}) collective-permute-start(bf16[1024,256]{1,0:T(8,128)(2,1)S(1)} %add_convert_fusion.14), channel_id=1, source_target_pairs={{2,4},{3,5},{4,2},{5,3},{10,12},{11,13},{12,10},{13,11},{18,20},{1... | collective-permute-start | bytes 1572872 | tf_op jit(solution)/shard_map/ppermute | solution.py:191
  106.4 12.7 %collective-permute-start.28 = (bf16[512,512]{1,0:T(8,128)(2,1)S(1)}, bf16[512,512]{1,0:T(8,128)(2,1)S(1)}, u32[]{:S(2)}, u32[]{:S(2)}) collective-permute-start(bf16[512,512]{1,0:T(8,128)(2,1)S(1)} %copy-done.28), channel_id=1, source_target_pairs={{0,24},{8,16},{16,8},{24,0},{1,25},{9,17},{17,9},{25,1},{2,26},{10... | collective-permute-start | bytes 1572872 | tf_op jit(solution)/shard_map/ppermute | solution.py:181
  109.9 21.7 %collective-permute-start.27 = (bf16[1024,256]{1,0:T(8,128)(2,1)}, bf16[1024,256]{1,0:T(8,128)(2,1)}, u32[]{:S(2)}, u32[]{:S(2)}) collective-permute-start(bf16[1024,256]{1,0:T(8,128)(2,1)} %broadcast_select_fusion.13), channel_id=1, source_target_pairs={{0,2},{1,3},{2,0},{3,1},{4,6},{5,7},{6,4},{7,5},{8,10},{9,11},{10,... | collective-permute-start | bytes 1572872 | tf_op jit(solution)/shard_map/ppermute | solution.py:191
  118.3 17.1 %collective-permute-start.32 = (bf16[1024,256]{1,0:T(8,128)(2,1)S(1)}, bf16[1024,256]{1,0:T(8,128)(2,1)S(1)}, u32[]{:S(2)}, u32[]{:S(2)}) collective-permute-start(bf16[1024,256]{1,0:T(8,128)(2,1)S(1)} %add_convert_fusion.12), channel_id=1, source_target_pairs={{2,4},{3,5},{4,2},{5,3},{10,12},{11,13},{12,10},{13,11},{18,20},{1... | collective-permute-start | bytes 1572872 | tf_op jit(solution)/shard_map/ppermute | solution.py:191
  119.1 18.1 %collective-permute-start.34 = (bf16[512,512]{1,0:T(8,128)(2,1)}, bf16[512,512]{1,0:T(8,128)(2,1)}, u32[]{:S(2)}, u32[]{:S(2)}) collective-permute-start(bf16[512,512]{1,0:T(8,128)(2,1)} %pad_maximum_fusion.2.refs_8_), channel_id=1, source_target_pairs={{0,16},{8,24},{16,0},{24,8},{1,17},{9,25},{17,1},{25,9},{2,18},{10... | collective-permute-start | bytes 1572872 | tf_op jit(solution)/shard_map/ppermute | solution.py:181
  120.3 16.9 %collective-permute-start.33 = (bf16[512,512]{1,0:T(8,128)(2,1)}, bf16[512,512]{1,0:T(8,128)(2,1)}, u32[]{:S(2)}, u32[]{:S(2)}) collective-permute-start(bf16[512,512]{1,0:T(8,128)(2,1)} %pad_maximum_fusion.2.refs_8_), channel_id=1, source_target_pairs={{0,8},{8,0},{16,24},{24,16},{1,9},{9,1},{17,25},{25,17},{2,10},{10... | collective-permute-start | bytes 1572872 | tf_op jit(solution)/shard_map/ppermute | solution.py:181
  128.6 14.1 %collective-permute-start.31 = (bf16[1024,256]{1,0:T(8,128)(2,1)S(1)}, bf16[1024,256]{1,0:T(8,128)(2,1)S(1)}, u32[]{:S(2)}, u32[]{:S(2)}) collective-permute-start(bf16[1024,256]{1,0:T(8,128)(2,1)S(1)} %broadcast_select_fusion.12), channel_id=1, source_target_pairs={{0,2},{1,3},{2,0},{3,1},{4,6},{5,7},{6,4},{7,5},{8,10},{9,11},{10,... | collective-permute-start | bytes 1572872 | tf_op jit(solution)/shard_map/ppermute | solution.py:191
  134.5 11.3 %collective-permute-start.37 = (bf16[1024,256]{1,0:T(8,128)(2,1)S(1)}, bf16[1024,256]{1,0:T(8,128)(2,1)S(1)}, u32[]{:S(2)}, u32[]{:S(2)}) collective-permute-start(bf16[1024,256]{1,0:T(8,128)(2,1)S(1)} %add_convert_fusion.10), channel_id=1, source_target_pairs={{2,4},{3,5},{4,2},{5,3},{10,12},{11,13},{12,10},{13,11},{18,20},{1... | collective-permute-start | bytes 1572872 | tf_op jit(solution)/shard_map/ppermute | solution.py:191
  137.2 10.3 %collective-permute-start.36 = (bf16[512,512]{1,0:T(8,128)(2,1)}, bf16[512,512]{1,0:T(8,128)(2,1)S(1)}, u32[]{:S(2)}, u32[]{:S(2)}) collective-permute-start(bf16[512,512]{1,0:T(8,128)(2,1)} %pad_maximum_fusion.2.refs_8_), channel_id=1, source_target_pairs={{0,24},{8,16},{16,8},{24,0},{1,25},{9,17},{17,9},{25,1},{2,26},{10... | collective-permute-start | bytes 1572872 | tf_op jit(solution)/shard_map/ppermute | solution.py:181
  138.7 18.8 %collective-permute-start.35 = (bf16[1024,256]{1,0:T(8,128)(2,1)}, bf16[1024,256]{1,0:T(8,128)(2,1)S(1)}, u32[]{:S(2)}, u32[]{:S(2)}) collective-permute-start(bf16[1024,256]{1,0:T(8,128)(2,1)} %broadcast_select_fusion.10), channel_id=1, source_target_pairs={{0,2},{1,3},{2,0},{3,1},{4,6},{5,7},{6,4},{7,5},{8,10},{9,11},{10,... | collective-permute-start | bytes 1572872 | tf_op jit(solution)/shard_map/ppermute | solution.py:191
  143.4 15.3 %collective-permute-start.39 = (bf16[1024,256]{1,0:T(8,128)(2,1)S(1)}, bf16[1024,256]{1,0:T(8,128)(2,1)}, u32[]{:S(2)}, u32[]{:S(2)}) collective-permute-start(bf16[1024,256]{1,0:T(8,128)(2,1)S(1)} %add_convert_fusion.8), channel_id=1, source_target_pairs={{2,4},{3,5},{4,2},{5,3},{10,12},{11,13},{12,10},{13,11},{18,20},{1... | collective-permute-start | bytes 1572872 | tf_op jit(solution)/shard_map/ppermute | solution.py:191
  155.7 14.8 %collective-permute-start.38 = (bf16[1024,256]{1,0:T(8,128)(2,1)S(1)}, bf16[1024,256]{1,0:T(8,128)(2,1)S(1)}, u32[]{:S(2)}, u32[]{:S(2)}) collective-permute-start(bf16[1024,256]{1,0:T(8,128)(2,1)S(1)} %broadcast_select_fusion.8), channel_id=1, source_target_pairs={{0,2},{1,3},{2,0},{3,1},{4,6},{5,7},{6,4},{7,5},{8,10},{9,11},{10,... | collective-permute-start | bytes 1572872 | tf_op jit(solution)/shard_map/ppermute | solution.py:191
  157.6 12.9 %copy-start.13 = (bf16[1024,256]{1,0:T(8,128)(2,1)S(1)}, bf16[1024,256]{1,0:T(8,128)(2,1)}, u32[]{:S(2)}) copy-start(bf16[1024,256]{1,0:T(8,128)(2,1)} %get-tuple-element.245) | copy-start | bytes 1572868
  157.6 13.9 %collective-permute-start.41 = (bf16[1024,256]{1,0:T(8,128)(2,1)S(1)}, bf16[1024,256]{1,0:T(8,128)(2,1)S(1)}, u32[]{:S(2)}, u32[]{:S(2)}) collective-permute-start(bf16[1024,256]{1,0:T(8,128)(2,1)S(1)} %add_convert_fusion.6), channel_id=1, source_target_pairs={{2,4},{3,5},{4,2},{5,3},{10,12},{11,13},{12,10},{13,11},{18,20},{1... | collective-permute-start | bytes 1572872 | tf_op jit(solution)/shard_map/ppermute | solution.py:191
  160.8 21.0 %collective-permute-start.40 = (bf16[1024,256]{1,0:T(8,128)(2,1)S(1)}, bf16[1024,256]{1,0:T(8,128)(2,1)S(1)}, u32[]{:S(2)}, u32[]{:S(2)}) collective-permute-start(bf16[1024,256]{1,0:T(8,128)(2,1)S(1)} %broadcast_select_fusion.6), channel_id=1, source_target_pairs={{0,2},{1,3},{2,0},{3,1},{4,6},{5,7},{6,4},{7,5},{8,10},{9,11},{10,... | collective-permute-start | bytes 1572872 | tf_op jit(solution)/shard_map/ppermute | solution.py:191
  170.7 13.6 %collective-permute-start.43 = (bf16[1024,256]{1,0:T(8,128)(2,1)S(1)}, bf16[1024,256]{1,0:T(8,128)(2,1)S(1)}, u32[]{:S(2)}, u32[]{:S(2)}) collective-permute-start(bf16[1024,256]{1,0:T(8,128)(2,1)S(1)} %add_convert_fusion.4), channel_id=1, source_target_pairs={{2,4},{3,5},{4,2},{5,3},{10,12},{11,13},{12,10},{13,11},{18,20},{1... | collective-permute-start | bytes 1572872 | tf_op jit(solution)/shard_map/ppermute | solution.py:191
  171.7 21.3 %collective-permute-start.42 = (bf16[1024,256]{1,0:T(8,128)(2,1)S(1)}, bf16[1024,256]{1,0:T(8,128)(2,1)S(1)}, u32[]{:S(2)}, u32[]{:S(2)}) collective-permute-start(bf16[1024,256]{1,0:T(8,128)(2,1)S(1)} %add_convert_fusion.3), channel_id=1, source_target_pairs={{2,0},{3,1},{4,6},{5,7},{10,8},{11,9},{12,14},{13,15},{18,16},{19,... | collective-permute-start | bytes 1572872 | tf_op jit(solution)/shard_map/ppermute | solution.py:191
  183.5 2.3 %collective-permute-start.45 = (bf16[1024,256]{1,0:T(8,128)(2,1)S(1)}, bf16[1024,256]{1,0:T(8,128)(2,1)S(1)}, u32[]{:S(2)}, u32[]{:S(2)}) collective-permute-start(bf16[1024,256]{1,0:T(8,128)(2,1)S(1)} %add_convert_fusion.2), channel_id=1, source_target_pairs={{2,4},{3,5},{4,2},{5,3},{10,12},{11,13},{12,10},{13,11},{18,20},{1... | collective-permute-start | bytes 1572872 | tf_op jit(solution)/shard_map/ppermute | solution.py:191
  184.4 22.9 %collective-permute-start.44 = (bf16[1024,256]{1,0:T(8,128)(2,1)S(1)}, bf16[1024,256]{1,0:T(8,128)(2,1)S(1)}, u32[]{:S(2)}, u32[]{:S(2)}) collective-permute-start(bf16[1024,256]{1,0:T(8,128)(2,1)S(1)} %add_convert_fusion.1), channel_id=1, source_target_pairs={{2,0},{3,1},{4,6},{5,7},{10,8},{11,9},{12,14},{13,15},{18,16},{19,... | collective-permute-start | bytes 1572872 | tf_op jit(solution)/shard_map/ppermute | solution.py:191
  185.9 21.0 %collective-permute-start.46 = (bf16[1024,256]{1,0:T(8,128)(2,1)S(1)}, bf16[1024,256]{1,0:T(8,128)(2,1)S(1)}, u32[]{:S(2)}, u32[]{:S(2)}) collective-permute-start(bf16[1024,256]{1,0:T(8,128)(2,1)S(1)} %add_convert_fusion), channel_id=1, source_target_pairs={{2,0},{3,1},{4,6},{5,7},{10,8},{11,9},{12,14},{13,15},{18,16},{19,... | collective-permute-start | bytes 1572872 | tf_op jit(solution)/shard_map/ppermute | solution.py:191
  193.4 14.5 %collective-permute-start.47 = (bf16[448,1536]{1,0:T(8,128)(2,1)S(1)}, bf16[448,1536]{1,0:T(8,128)(2,1)S(1)}, u32[]{:S(2)}, u32[]{:S(2)}) collective-permute-start(bf16[448,1536]{1,0:T(8,128)(2,1)S(1)} %constant_dynamic-update-slice_fusion), channel_id=1, source_target_pairs={{0,1},{1,0},{2,3},{3,2},{4,5},{5,4},{6,7},{7,6},{8,9},{9,8},{10,11... | collective-permute-start | bytes 4128776 | tf_op jit(solution)/shard_map/ppermute | solution.py:178
  207.8 1.9 collective-permute-start.48
  (28 other events, 128.2 us)
